TPU v7x, 32 devices: a whole 2x2x4 slice. The times are simulated.
32 devices in a mesh: groups: 2 (over y), cand: 4 (over z), eig: 2 (over x), rep: 2 (over core).
Axes of the slice: x: 2, y: 2, z: 4, core: 2. Of those that a mesh axis runs over, the one named last changes fastest.
Arguments:
- acts: bfloat16 [4096, 5120], P(('groups', 'cand'), ('eig', 'rep')), parts along dimension 0, may hold values from -6 to 6
- grads: bfloat16 [4096, 27648], P(('groups', 'cand'), ('eig', 'rep')), parts along dimension 0, may hold values from -6 to 6
- basis_in: bfloat16 [10240, 512], P(('groups', 'eig', 'rep'), 'cand'), parts along dimension 0, may hold values from -0.078125 to 0.078125
- basis_out: bfloat16 [55296, 512], P(('groups', 'eig', 'rep'), 'cand'), parts along dimension 0, may hold values from -0.0390625 to 0.0390625
- eigval: float32 [1024, 512], P(('groups', 'cand', 'eig', 'rep')), parts along dimension 0, may hold values from 0.5 to 5
- test_grads: bfloat16 [128, 512, 512], P('groups', ('cand', 'eig', 'rep')), parts along dimension 0, may hold values from -0.005859375 to 0.005859375
- pair_tiles: int32 [16], P('groups'), parts along dimension 0, may hold values from 1 to 4, 16 in all
- last_rows: int32 [16], P('groups'), parts along dimension 0, may hold values from 1 to 128
Outputs:
- scores: float32 [16, 64], P(('groups', 'cand'), ('eig', 'rep')), parts along dimension 0
There are 2 independent parts, one for each index of `groups`. A program takes and returns all parts, laid end to end along the dimension named above; each array names one. Nothing has to cross between parts.
Inputs may be any that keep to these rules, and one draw needn't show every extreme that they name: `pair_tiles`: 8 pairs laid end to end over the 16 tiles in order; the counts sum to 16 and some pair has 4 tiles. `last_rows`: rows of a pair's last tile past this count are padding.
All inputs are finite; a program needn't handle non-finite values.
Results may differ from a plain program's by a relative error of at most 0.006.
Values may be sent and summed in bfloat16 or wider, within the bound.
No kernel may reach another device: no remote copies, remote signals or barrier semaphores. Data moves between devices by JAX's collectives and lax.ppermute only.
A program may use at most 64 MiB of HBM per device.

v0:
```python
import jax
import jax.numpy as jnp
from jax import lax
from jax.sharding import PartitionSpec as P

TILE = 128


damping = 0.01


def tile_layout(pair_tiles, last_rows, first_tile, count, tile_rows):
    tiles = first_tile + jnp.arange(count, dtype=jnp.int32)
    ends = jnp.cumsum(pair_tiles)
    owner = jnp.sum((ends[None, :] <= tiles[:, None]).astype(jnp.int32), axis=1)
    onehot = owner[:, None] == jnp.arange(pair_tiles.shape[0], dtype=jnp.int32)[None, :]
    last_of = jnp.sum(jnp.where(onehot, last_rows[None, :], 0), axis=1)
    end_of = jnp.sum(jnp.where(onehot, ends[None, :], 0), axis=1)
    limit = jnp.where(tiles == end_of - 1, last_of, tile_rows)
    rowmask = jnp.arange(tile_rows, dtype=jnp.int32)[None, :] < limit[:, None]
    return (rowmask, onehot)


def per_device(acts, grads, basis_in, basis_out, eigval, test_grads, pair_tiles, last_rows):
    ncand = lax.axis_size("cand")
    nfeat = lax.axis_size(("eig", "rep"))
    tok_rows = acts.shape[0]
    width_in = basis_in.shape[1] * ncand
    width_out = basis_out.shape[1] * ncand
    slim = width_out // (ncand * nfeat)
    part_in = jnp.dot(
        acts,
        lax.all_gather(basis_in, "cand", axis=1, tiled=True),
        preferred_element_type=jnp.float32,
    )
    part_out = jnp.dot(
        grads,
        lax.all_gather(basis_out, "cand", axis=1, tiled=True),
        preferred_element_type=jnp.float32,
    )
    part_out = part_out.reshape(tok_rows, ncand, nfeat, slim).transpose(0, 2, 1, 3)
    part_out = part_out.reshape(tok_rows, nfeat * ncand * slim)
    summed_in, summed_out = lax.psum((part_in, part_out), ("eig", "rep"))
    own = lax.dynamic_slice_in_dim(
        summed_out, lax.axis_index(("eig", "rep")) * (ncand * slim), ncand * slim, 1
    )
    rot_in = summed_in.astype(jnp.bfloat16)
    rot_out = own.astype(jnp.bfloat16)
    tile_rows = TILE
    tiles_here = tok_rows // tile_rows
    rowmask, ignored = tile_layout(
        pair_tiles, last_rows, lax.axis_index("cand") * tiles_here, tiles_here, tile_rows
    )
    masked = rot_out.reshape(tiles_here, tile_rows, ncand * slim) * rowmask[:, :, None].astype(
        jnp.bfloat16
    )
    prods = jnp.einsum(
        "tre,tra->tea",
        masked,
        rot_in.reshape(tiles_here, tile_rows, width_in),
        preferred_element_type=jnp.float32,
    ).astype(jnp.bfloat16)
    prods = prods.reshape(tiles_here, ncand, slim, width_in)
    received = lax.all_to_all(prods, "cand", split_axis=1, concat_axis=0, tiled=True)
    all_tiles = received.shape[0]
    received = received.reshape(all_tiles, slim, width_in)
    precond = (test_grads.astype(jnp.float32) / (eigval + damping)).astype(jnp.bfloat16)
    tile_part = jnp.einsum("tea,jea->tj", received, precond, preferred_element_type=jnp.float32)
    ignored_mask, onehot = tile_layout(pair_tiles, last_rows, 0, all_tiles, tile_rows)
    pair_part = jnp.dot(onehot.astype(jnp.float32).T, tile_part, precision=lax.Precision.HIGHEST)
    npairs = pair_part.shape[0]
    ntest = pair_part.shape[1]
    total = lax.psum(pair_part, ("cand", "eig", "rep"))
    rows = lax.dynamic_slice_in_dim(
        total, lax.axis_index("cand") * (npairs // ncand), npairs // ncand, 0
    )
    return lax.dynamic_slice_in_dim(
        rows, lax.axis_index(("eig", "rep")) * (ntest // nfeat), ntest // nfeat, 1
    )


def solution(mesh):
    in_specs = (
        P(("groups", "cand"), ("eig", "rep")),
        P(("groups", "cand"), ("eig", "rep")),
        P(("groups", "eig", "rep"), "cand"),
        P(("groups", "eig", "rep"), "cand"),
        P(("groups", "cand", "eig", "rep"), None),
        P("groups", ("cand", "eig", "rep"), None),
        P("groups"),
        P("groups"),
    )
    out_specs = P(("groups", "cand"), ("eig", "rep"))
    return jax.shard_map(
        per_device, mesh=mesh, in_specs=in_specs, out_specs=out_specs, check_vma=False
    )
```

profile of v0, /device:TPU:0, one launch (start us, length us, event | category | flops | bytes accessed | tf_op | source)
XLA Modules:
  0.0 289.1 jit_solution(2343039698568536722)
XLA Ops:
  6.5 0.7 all-gather.5.cloned.1.call-update
  7.3 0.7 all-gather.3.cloned.1.call-update
  8.0 0.2 reduce-window.8
  8.2 0.2 convert_reduce_fusion.1
  8.4 0.2 select_reduce_fusion.1
  8.6 0.1 fusion.10
  8.7 36.4 %all-gather.5.cloned.1.call-done = bf16[1280,512]{1,0:T(8,128)(2,1)} async-done(((bf16[1280,128]{1,0:T(8,128)(2,1)}), bf16[1280,512]{1,0:T(8,128)(2,1)}) %all-gather.5.cloned.1.call-update) | async-done | bytes 1310736 | tf_op jit(solution)/shard_map/all_gather | solution.py:33
  45.1 2.2 fusion.12
  47.3 125.7 %all-gather.3.cloned.1.call-done = bf16[6912,512]{1,0:T(8,128)(2,1)} async-done(((bf16[6912,128]{1,0:T(8,128)(2,1)}), bf16[6912,512]{1,0:T(8,128)(2,1)}) %all-gather.3.cloned.1.call-update) | async-done | bytes 7077904 | tf_op jit(solution)/shard_map/all_gather | solution.py:38
  172.9 8.2 %fusion.11 = f32[512,512]{0,1:T(8,128)S(1)} fusion(bf16[512,6912]{1,0:T(8,128)(2,1)} %param.9, bf16[6912,512]{1,0:T(8,128)(2,1)} %all-gather.3.cloned.1.call-done), kind=kOutput, calls=%fused_computation.23 | convolution fusion | flops 3623878656 | bytes 15204352 | tf_op jit(solution)/shard_map/dot_general | solution.py:36
  181.1 0.1 copy.13
  181.2 41.7 %all-reduce.2 = (bf16[512,512]{1,0:T(8,128)(2,1)}, bf16[512,512]{0,1:T(8,128)(2,1)}) all-reduce(f32[512,512]{1,0:T(8,128)S(1)} %fusion.12, f32[512,512]{0,1:T(8,128)S(1)} %bitcast.22), channel_id=1, replica_groups=mesh['groups'=2,'cand'=4,'eig'=2,'rep'=2] {'eig','rep'}, use_global_device_ids=true, to_apply=%region_6.7 | all-reduce | flops 524288 | bytes 3145728 | tf_op jit(solution)/shard_map/psum | solution.py:43
  222.9 1.1 dynamic-slice_convert_fusion
  224.0 0.8 copy.14
  224.8 1.6 convolution_convert_fusion
  226.3 0.9 copy.16
  227.2 4.1 %all-to-all-start = ((bf16[4,4,32,512]{3,2,0,1:T(8,128)(2,1)}), bf16[4,4,32,512]{3,2,0,1:T(8,128)(2,1)}, u32[]{:S(2)}, u32[]{:S(2)}) async-start(bf16[4,4,32,512]{3,2,0,1:T(8,128)(2,1)} %copy.16), calls=%async_computation | async-start | bytes 1048576 | tf_op jit(solution)/shard_map/all_to_all | solution.py:64
  231.4 0.1 convert_reduce_fusion
  231.5 1.9 divide_convert_fusion
  233.4 13.3 %all-to-all-done = bf16[4,4,32,512]{3,2,0,1:T(8,128)(2,1)} async-done(((bf16[4,4,32,512]{3,2,0,1:T(8,128)(2,1)}), bf16[4,4,32,512]{3,2,0,1:T(8,128)(2,1)}, u32[]{:S(2)}, u32[]{:S(2)}) %all-to-all-start) | async-done | bytes 524320 | tf_op jit(solution)/shard_map/all_to_all | solution.py:64
  246.7 4.6 %fusion.2 = f32[16,64]{1,0:T(8,128)S(1)} fusion(bf16[64,32,512]{2,1,0:T(8,128)(2,1)} %divide_convert_fusion, bf16[16,32,512]{2,1,0:T(8,128)(2,1)} %bitcast.10), kind=kOutput, calls=%fused_computation.4 | convolution fusion | flops 33554432 | bytes 2625536 | tf_op jit(solution)/shard_map/tea,jea->tj/dot_general | solution.py:68
  251.3 0.3 fusion.8
  251.5 30.1 %psum.23 = f32[8,64]{1,0:T(8,128)S(1)} all-reduce(f32[8,64]{1,0:T(8,128)S(1)} %fusion.8), channel_id=1, replica_groups=mesh['groups'=2,'cand'=4,'eig'=2,'rep'=2] {'cand','eig','rep'}, use_global_device_ids=true, to_apply=%region_7.8 | all-reduce | flops 512 | bytes 4096 | tf_op jit(solution)/shard_map/psum | solution.py:73
  281.7 0.6 dynamic_slice.8
  (15 shorter events, 0.1 us)
Async XLA Ops:
  6.5 38.6 %copy-start = (bf16[512,1280]{1,0:T(8,128)(2,1)S(1)}, bf16[512,1280]{1,0:T(8,128)(2,1)}, u32[]{:S(2)}) copy-start(bf16[512,1280]{1,0:T(8,128)(2,1)} %param.8) | copy-start | bytes 3932164
  6.5 1.5 copy-start.4
  6.5 1.9 copy-start.3
  6.5 38.6 %all-gather.5.cloned.1.call-start = ((), (), s32[]{:S(2)}) async-start(), calls=%async_computation.2 | async-start | bytes 1638400 | tf_op jit(solution)/shard_map/all_gather | solution.py:33
  7.3 165.7 %all-gather.3.cloned.1.call-start = ((), (), s32[]{:S(2)}) async-start(), calls=%async_computation.1 | async-start | bytes 8847360 | tf_op jit(solution)/shard_map/all_gather | solution.py:38
  222.9 8.5 %copy-start.1 = (bf16[64,32,512]{2,1,0:T(8,128)(2,1)S(1)}, bf16[64,32,512]{2,1,0:T(8,128)(2,1)}, u32[]{:S(2)}) copy-start(bf16[64,32,512]{2,1,0:T(8,128)(2,1)} %param.13) | copy-start | bytes 6291460
  224.8 6.7 %copy-start.2 = (f32[32,512]{1,0:T(8,128)S(1)}, f32[32,512]{1,0:T(8,128)}, u32[]{:S(2)}) copy-start(f32[32,512]{1,0:T(8,128)} %param.12) | copy-start | bytes 196612
  227.2 19.5 %all-to-all-start = ((bf16[4,4,32,512]{3,2,0,1:T(8,128)(2,1)}), bf16[4,4,32,512]{3,2,0,1:T(8,128)(2,1)}, u32[]{:S(2)}, u32[]{:S(2)}) async-start(bf16[4,4,32,512]{3,2,0,1:T(8,128)(2,1)} %copy.16), calls=%async_computation | async-start | bytes 1048576 | tf_op jit(solution)/shard_map/all_to_all | solution.py:64
Sparse Core Ops, SparseCore 0:
  8.9 36.1 all-gather.4
  46.7 126.2 all-gather.2
where the time goes:
time: 289 us
  waiting for transfers between devices  177 us (61%)
  blocking collectives  71.8 us (25%)
  matrix products  16.8 us (6%)
  between operations  13.5 us (5%)
  starting transfers between devices  4.18 us (1%)
  local copies, waits for them, and re-layouts  3.42 us (1%)
    all_gather x1, waiting for transfers between devices, per_device(): lax.all_gather(basis_out, 'cand', axis=1, tiled=True)  126 us
    psum x1, blocking collectives, per_device(): summed_in, summed_out = lax.psum((part_in, part_out), ('eig', 'rep'))  41.7 us
    all_gather x1, waiting for transfers between devices, per_device(): lax.all_gather(basis_in, 'cand', axis=1, tiled=True)  36.4 us
    psum x1, blocking collectives, per_device(): total = lax.psum(pair_part, ('cand', 'eig', 'rep'))  30.1 us
    all_to_all x1, waiting for transfers between devices, per_device(): lax.all_to_all(prods, 'cand', split_axis=1, concat_axis=0, tiled=True)  13.3 us
    dot_general x1, matrix products, per_device(): jnp.dot(grads, lax.all_gather(basis_out, 'cand', axis=1, tiled=True), pre...  8.19 us
  transfers between devices with their start and end apart: 3, of which 3 were waited for; matrix products, arithmetic and copies ran while one was open for 2% of the time, Pallas kernels for 0%

commit v1 on v0

--- a/solution.py
+++ b/solution.py
@@ -4,7 +4,8 @@
 from jax.sharding import PartitionSpec as P
 
 TILE = 128
-
+CHUNKS = 3
+FEAT = ("eig", "rep")
 
 damping = 0.01
 
@@ -21,9 +22,136 @@
     return (rowmask, onehot)
 
 
-def per_device(acts, grads, basis_in, basis_out, eigval, test_grads, pair_tiles, last_rows):
+def hop(x, by):
+    n = lax.axis_size("cand")
+    return lax.ppermute(x, "cand", [(i, i + by) for i in range(n) if 0 <= i + by < n])
+
+
+def swap(x, step):
+    n = lax.axis_size(FEAT)
+    return lax.ppermute(x, FEAT, [(i, i ^ step) for i in range(n)])
+
+
+def scatter_sum(part, axis):
+    n = lax.axis_size(FEAT)
+    me = lax.axis_index(FEAT)
+    width = part.shape[axis] // n
+    total = lax.dynamic_slice_in_dim(part, me * width, width, axis)
+    sent = part.astype(jnp.bfloat16)
+    for step in range(1, n):
+        block = lax.dynamic_slice_in_dim(sent, (me ^ step) * width, width, axis)
+        total = total + swap(block, step).astype(jnp.float32)
+    return total
+
+
+def gather_rows(x):
+    n = lax.axis_size(FEAT)
+    me = lax.axis_index(FEAT)
+    rows = x.shape[0]
+    whole = jnp.zeros((rows * n,) + x.shape[1:], x.dtype)
+    whole = lax.dynamic_update_slice_in_dim(whole, x, me * rows, 0)
+    for step in range(1, n):
+        whole = lax.dynamic_update_slice_in_dim(whole, swap(x, step), (me ^ step) * rows, 0)
+    return whole
+
+
+def spread(x):
+    n = lax.axis_size("cand")
+    found = {}
+    up, down = x, x
+    for k in range(1, n):
+        up, down = hop(up, 1), hop(down, -1)
+        found[k], found[-k] = up, down
+    return found
+
+
+def dot_t(basis, rows):
+    return lax.dot_general(basis, rows, (((0,), (1,)), ((), ())), preferred_element_type=jnp.float32)
+
+
+def line_plan(acts, grads, basis_in, basis_out, eigval, test_grads, pair_tiles, last_rows):
     ncand = lax.axis_size("cand")
-    nfeat = lax.axis_size(("eig", "rep"))
+    nfeat = lax.axis_size(FEAT)
+    plane = lax.axis_index("cand")
+    tok_rows = acts.shape[0]
+    cols = basis_in.shape[1]
+    width_in = cols * ncand
+    tiles_here = tok_rows // TILE
+    slim = basis_out.shape[1] // nfeat
+
+    ins = {0: basis_in, **spread(basis_in)}
+    depth = basis_out.shape[0] // CHUNKS
+    pieces = [basis_out[i * depth : (i + 1) * depth] for i in range(CHUNKS)]
+    outs = [{0: piece, **spread(piece)} for piece in pieces]
+
+    part_in = jnp.zeros((tok_rows, width_in), jnp.float32)
+    for k in range(ncand):
+        part = jnp.dot(acts, ins[k], preferred_element_type=jnp.float32)
+        if k:
+            part = part + jnp.dot(acts, ins[k - ncand], preferred_element_type=jnp.float32)
+        part_in = lax.dynamic_update_slice_in_dim(
+            part_in, part, lax.rem(plane - k + ncand, ncand) * cols, 1
+        )
+    rot_in = gather_rows(scatter_sum(part_in, 0).astype(jnp.bfloat16))
+    rot_in = rot_in.reshape(tiles_here, TILE, width_in)
+
+    rowmask, ignored = tile_layout(pair_tiles, last_rows, plane * tiles_here, tiles_here, TILE)
+    keep = rowmask.reshape(1, tok_rows).astype(jnp.bfloat16)
+    precond = (test_grads.astype(jnp.float32) / (eigval + damping)).astype(jnp.bfloat16)
+
+    def partial_out(at):
+        total = None
+        for i in range(CHUNKS):
+            term = dot_t(outs[i][at], grads[:, i * depth : (i + 1) * depth])
+            total = term if total is None else total + term
+        return total
+
+    def tile_prods(part):
+        rot_out = scatter_sum(part, 0).astype(jnp.bfloat16) * keep
+        return jnp.einsum(
+            "etr,tra->tea",
+            rot_out.reshape(slim, tiles_here, TILE),
+            rot_in,
+            preferred_element_type=jnp.float32,
+        ).astype(jnp.bfloat16)
+
+    def pair_scores(prods, source):
+        scores = jnp.einsum("tea,jea->tj", prods, precond, preferred_element_type=jnp.float32)
+        ignored_mask, onehot = tile_layout(
+            pair_tiles, last_rows, source * tiles_here, tiles_here, TILE
+        )
+        return jnp.sum(jnp.where(onehot[:, :, None], scores[:, None, :], 0.0), axis=0)
+
+    total = pair_scores(tile_prods(partial_out(0)), plane)
+    for k in range(1, ncand):
+        if 2 * k < ncand:
+            total = total + pair_scores(hop(tile_prods(partial_out(k)), -k), plane + k)
+            total = total + pair_scores(hop(tile_prods(partial_out(-k)), k), plane - k)
+        else:
+            prods = tile_prods(partial_out(k) + partial_out(-k))
+            pairs = [(i, i - k) for i in range(k, ncand)] + [(i, i + k) for i in range(ncand - k)]
+            back = lax.ppermute(prods, "cand", pairs)
+            source = jnp.where(plane + k < ncand, plane + k, plane - k)
+            total = total + pair_scores(back, source)
+
+    mine = scatter_sum_small(total, FEAT, 1)
+    return scatter_sum_small(mine, "cand", 0)
+
+
+def scatter_sum_small(part, axis_name, axis):
+    n = lax.axis_size(axis_name)
+    me = lax.axis_index(axis_name)
+    width = part.shape[axis] // n
+    total = lax.dynamic_slice_in_dim(part, me * width, width, axis)
+    for step in range(1, n):
+        block = lax.dynamic_slice_in_dim(part, lax.rem(me + step, n) * width, width, axis)
+        total = total + lax.ppermute(block, axis_name, [(i, (i + step) % n) for i in range(n)])
+    return total
+
+
+def gather_plan(acts, grads, basis_in, basis_out, eigval, test_grads, pair_tiles, last_rows):
+    ncand = lax.axis_size("cand")
+    nfeat = lax.axis_size(FEAT)
     tok_rows = acts.shape[0]
     width_in = basis_in.shape[1] * ncand
     width_out = basis_out.shape[1] * ncand
@@ -40,24 +168,23 @@
     )
     part_out = part_out.reshape(tok_rows, ncand, nfeat, slim).transpose(0, 2, 1, 3)
     part_out = part_out.reshape(tok_rows, nfeat * ncand * slim)
-    summed_in, summed_out = lax.psum((part_in, part_out), ("eig", "rep"))
+    summed_in, summed_out = lax.psum((part_in, part_out), FEAT)
     own = lax.dynamic_slice_in_dim(
-        summed_out, lax.axis_index(("eig", "rep")) * (ncand * slim), ncand * slim, 1
+        summed_out, lax.axis_index(FEAT) * (ncand * slim), ncand * slim, 1
     )
     rot_in = summed_in.astype(jnp.bfloat16)
     rot_out = own.astype(jnp.bfloat16)
-    tile_rows = TILE
-    tiles_here = tok_rows // tile_rows
+    tiles_here = tok_rows // TILE
     rowmask, ignored = tile_layout(
-        pair_tiles, last_rows, lax.axis_index("cand") * tiles_here, tiles_here, tile_rows
-    )
-    masked = rot_out.reshape(tiles_here, tile_rows, ncand * slim) * rowmask[:, :, None].astype(
+        pair_tiles, last_rows, lax.axis_index("cand") * tiles_here, tiles_here, TILE
+    )
+    masked = rot_out.reshape(tiles_here, TILE, ncand * slim) * rowmask[:, :, None].astype(
         jnp.bfloat16
     )
     prods = jnp.einsum(
         "tre,tra->tea",
         masked,
-        rot_in.reshape(tiles_here, tile_rows, width_in),
+        rot_in.reshape(tiles_here, TILE, width_in),
         preferred_element_type=jnp.float32,
     ).astype(jnp.bfloat16)
     prods = prods.reshape(tiles_here, ncand, slim, width_in)
@@ -66,7 +193,7 @@
     received = received.reshape(all_tiles, slim, width_in)
     precond = (test_grads.astype(jnp.float32) / (eigval + damping)).astype(jnp.bfloat16)
     tile_part = jnp.einsum("tea,jea->tj", received, precond, preferred_element_type=jnp.float32)
-    ignored_mask, onehot = tile_layout(pair_tiles, last_rows, 0, all_tiles, tile_rows)
+    ignored_mask, onehot = tile_layout(pair_tiles, last_rows, 0, all_tiles, TILE)
     pair_part = jnp.dot(onehot.astype(jnp.float32).T, tile_part, precision=lax.Precision.HIGHEST)
     npairs = pair_part.shape[0]
     ntest = pair_part.shape[1]
@@ -75,7 +202,7 @@
         total, lax.axis_index("cand") * (npairs // ncand), npairs // ncand, 0
     )
     return lax.dynamic_slice_in_dim(
-        rows, lax.axis_index(("eig", "rep")) * (ntest // nfeat), ntest // nfeat, 1
+        rows, lax.axis_index(FEAT) * (ntest // nfeat), ntest // nfeat, 1
     )
 
 
@@ -91,6 +218,7 @@
         P("groups"),
     )
     out_specs = P(("groups", "cand"), ("eig", "rep"))
+    per_device = line_plan if mesh.shape["cand"] <= 4 else gather_plan
     return jax.shard_map(
         per_device, mesh=mesh, in_specs=in_specs, out_specs=out_specs, check_vma=False
     )

time: 289 us -> 246 us (0.85)
  starting transfers between devices: 4.18 us -> 100 us
  waiting for transfers between devices: 177 us -> 83.4 us
  blocking collectives: 71.8 us -> 0 us
  matrix products: 16.8 us -> 52 us
  between operations: 13.5 us -> 0.89 us
    all_gather x2 -> x0, waiting for transfers between devices: 162 us -> none  [the longest x1 126 us: per_device(): lax.all_gather(basis_out, 'cand', axis=1, tiled=True)]
    ppermute x0 -> x55, starting transfers between devices: none -> 100 us  [the longest x26 70.3 us: hop(): lax.ppermute(x, 'cand', [(i, i + by) for i in range(n) if 0 <= i + by < n])]
    ppermute x0 -> x55, waiting for transfers between devices: none -> 83.4 us  [the longest x26 68.4 us: hop(): lax.ppermute(x, 'cand', [(i, i + by) for i in range(n) if 0 <= i + by < n])]
    psum x2 -> x0, blocking collectives: 71.8 us -> none  [the longest x1 41.7 us: per_device(): summed_in, summed_out = lax.psum((part_in, part_out), ('eig', 'rep'))]
    dot_general x5 -> x38, matrix products: 16.8 us -> 52 us  [the longest x21 32.5 us: dot_t(): lax.dot_general(basis, rows, (((0,), (1,)), ((), ())), preferred_element_...]
    all_to_all x1 -> x0, waiting for transfers between devices: 13.3 us -> none  [per_device(): lax.all_to_all(prods, 'cand', split_axis=1, concat_axis=0, tiled=True)]
    all_to_all x1 -> x0, starting transfers between devices: 4.14 us -> none  [per_device(): lax.all_to_all(prods, 'cand', split_axis=1, concat_axis=0, tiled=True)]
  transfers between devices with their start and end apart: 3 -> 55, of which waited for: 3 -> 26; matrix products, arithmetic and copies ran while one was open for 2% -> 23% of each run, Pallas kernels for 0% -> 0%
where the time goes in v1:
time: 246 us; the launch traced here: 244 us
  starting transfers between devices  100 us (41%)
  waiting for transfers between devices  83.4 us (34%)
  matrix products  52 us (21%)
  other arithmetic  4.13 us (2%)
  local copies, waits for them, and re-layouts  3.77 us (2%)
    ppermute x26, starting transfers between devices, hop(): lax.ppermute(x, 'cand', [(i, i + by) for i in range(n) if 0 <= i + by < n])  70.3 us
    ppermute x26, waiting for transfers between devices, hop(): lax.ppermute(x, 'cand', [(i, i + by) for i in range(n) if 0 <= i + by < n])  68.4 us
    dot_general x21, matrix products, dot_t(): lax.dot_general(basis, rows, (((0,), (1,)), ((), ())), preferred_element_...  32.5 us
    ppermute x21, starting transfers between devices, swap(): return lax.ppermute(x, FEAT, [(i, i ^ step) for i in range(n)])  14.9 us
    dot_general x5, matrix products, pair_scores(): jnp.einsum('tea,jea->tj', prods, precond, preferred_element_type=jnp.floa...  12.1 us
    ppermute x6, starting transfers between devices, scatter_sum_small(): lax.ppermute(block, axis_name, [(i, (i + step) % n) for i in range(n)])  8.94 us
    ppermute x21, waiting for transfers between devices, swap(): return lax.ppermute(x, FEAT, [(i, i ^ step) for i in range(n)])  8.76 us
    ppermute x2, starting transfers between devices, line_plan(): back = lax.ppermute(prods, 'cand', pairs)  6.05 us
  transfers between devices with their start and end apart: 55, of which 26 were waited for; matrix products, arithmetic and copies ran while one was open for 23% of the time, Pallas kernels for 0%

profile of v1, /device:TPU:0, one launch (start us, length us, event | category | flops | bytes accessed | tf_op | source)
XLA Modules:
  0.0 244.4 jit_solution(14859381481473055991)
XLA Ops:
  1.6 6.3 %collective-permute-start.3 = (bf16[1280,128]{1,0:T(8,128)(2,1)}, bf16[1280,128]{1,0:T(8,128)(2,1)}, u32[]{:S(2)}, u32[]{:S(2)}) collective-permute-start(bf16[1280,128]{1,0:T(8,128)(2,1)} %param.10), channel_id=1, source_target_pairs={{0,4},{4,8},{8,12},{1,5},{5,9},{9,13},{2,6},{6,10},{10,14},{3,7},{... | collective-permute-start | bytes 983048 | tf_op jit(solution)/shard_map/ppermute | solution.py:27
  7.9 2.7 %fusion.86 = (bf16[2304,128]{1,0:T(8,128)(2,1)}, bf16[2304,128]{1,0:T(8,128)(2,1)}, bf16[2304,128]{1,0:T(8,128)(2,1)}) fusion(bf16[6912,128]{1,0:T(8,128)(2,1)} %param.11), kind=kLoop, calls=%fused_computation.171 | loop fusion | bytes 3538944 | tf_op jit(solution)/shard_map/slice | solution.py:84
  10.6 4.0 %collective-permute-start.15 = (bf16[2304,128]{1,0:T(8,128)(2,1)}, bf16[2304,128]{1,0:T(8,128)(2,1)}, u32[]{:S(2)}, u32[]{:S(2)}) collective-permute-start(bf16[2304,128]{1,0:T(8,128)(2,1)} %get-tuple-element.13), channel_id=1, source_target_pairs={{0,4},{4,8},{8,12},{1,5},{5,9},{9,13},{2,6},{6,10},{10,14},{3,7},{... | collective-permute-start | bytes 1769480 | tf_op jit(solution)/shard_map/ppermute | solution.py:27
  15.9 5.4 %collective-permute-start.17 = (bf16[2304,128]{1,0:T(8,128)(2,1)}, bf16[2304,128]{1,0:T(8,128)(2,1)}, u32[]{:S(2)}, u32[]{:S(2)}) collective-permute-start(bf16[2304,128]{1,0:T(8,128)(2,1)} %get-tuple-element.14), channel_id=1, source_target_pairs={{0,4},{4,8},{8,12},{1,5},{5,9},{9,13},{2,6},{6,10},{10,14},{3,7},{... | collective-permute-start | bytes 1769480 | tf_op jit(solution)/shard_map/ppermute | solution.py:27
  27.2 3.7 %fusion.91 = (bf16[128,512]{1,0:T(8,128)(2,1)}, f32[128,512]{1,0:T(8,128)}) fusion(f32[128,512]{1,0:T(8,128)S(1)} %convolution_add_fusion.10, bf16[512,6912]{1,0:T(8,128)(2,1)} %param.9, bf16[6912,128]{1,0:T(8,128)(2,1)} %param.11), kind=kOutput, calls=%fused_computation.176 | convolution fusion | flops 302120960 | bytes 3604480 | tf_op jit(solution)/shard_map/dot_general | solution.py:69
  36.9 4.6 %collective-permute-start.16 = (bf16[2304,128]{1,0:T(8,128)(2,1)S(1)}, bf16[2304,128]{1,0:T(8,128)(2,1)S(1)}, u32[]{:S(2)}, u32[]{:S(2)}) collective-permute-start(bf16[2304,128]{1,0:T(8,128)(2,1)S(1)} %copy-done.4), channel_id=1, source_target_pairs={{0,4},{4,8},{8,12},{1,5},{5,9},{9,13},{2,6},{6,10},{10,14},{3,7},{... | collective-permute-start | bytes 1769480 | tf_op jit(solution)/shard_map/ppermute | solution.py:27
  44.5 2.8 %fusion.26 = f32[128,512]{1,0:T(8,128)S(1)} fusion(bf16[2304,128]{1,0:T(8,128)(2,1)} %collective-permute-done.17, bf16[512,6912]{1,0:T(8,128)(2,1)} %param.9), kind=kOutput, calls=%fused_computation.44 | convolution fusion | flops 301989888 | bytes 3211264 | tf_op jit(solution)/shard_map/dot_general | solution.py:69
  47.3 5.0 %collective-permute-done.24 = bf16[2304,128]{1,0:T(8,128)(2,1)S(1)} collective-permute-done((bf16[2304,128]{1,0:T(8,128)(2,1)}, bf16[2304,128]{1,0:T(8,128)(2,1)S(1)}, u32[]{:S(2)}, u32[]{:S(2)}) %collective-permute-start.24) | collective-permute-done | bytes 589856 | tf_op jit(solution)/shard_map/ppermute | solution.py:27
  56.2 4.6 %collective-permute-start.7 = (bf16[1280,128]{1,0:T(8,128)(2,1)}, bf16[1280,128]{1,0:T(8,128)(2,1)S(1)}, u32[]{:S(2)}, u32[]{:S(2)}) collective-permute-start(bf16[1280,128]{1,0:T(8,128)(2,1)} %collective-permute-done.3), channel_id=1, source_target_pairs={{0,4},{4,8},{8,12},{1,5},{5,9},{9,13},{2,6},{6,10},{10,14},{3,7},{... | collective-permute-start | bytes 983048 | tf_op jit(solution)/shard_map/ppermute | solution.py:27
  67.6 4.4 %collective-permute-done.5 = bf16[1280,128]{1,0:T(8,128)(2,1)S(1)} collective-permute-done((bf16[1280,128]{1,0:T(8,128)(2,1)}, bf16[1280,128]{1,0:T(8,128)(2,1)S(1)}, u32[]{:S(2)}, u32[]{:S(2)}) %collective-permute-start.5) | collective-permute-done | bytes 327712 | tf_op jit(solution)/shard_map/ppermute | solution.py:27
  73.2 4.6 %collective-permute-start.31 = (bf16[2304,128]{1,0:T(8,128)(2,1)}, bf16[2304,128]{1,0:T(8,128)(2,1)S(1)}, u32[]{:S(2)}, u32[]{:S(2)}) collective-permute-start(bf16[2304,128]{1,0:T(8,128)(2,1)} %collective-permute-done.17), channel_id=1, source_target_pairs={{0,4},{4,8},{8,12},{1,5},{5,9},{9,13},{2,6},{6,10},{10,14},{3,7},{... | collective-permute-start | bytes 1769480 | tf_op jit(solution)/shard_map/ppermute | solution.py:27
  81.0 8.0 %collective-permute-done.6 = bf16[1280,128]{1,0:T(8,128)(2,1)S(1)} collective-permute-done((bf16[1280,128]{1,0:T(8,128)(2,1)S(1)}, bf16[1280,128]{1,0:T(8,128)(2,1)S(1)}, u32[]{:S(2)}, u32[]{:S(2)}) %collective-permute-start.6) | collective-permute-done | bytes 327712 | tf_op jit(solution)/shard_map/ppermute | solution.py:27
  103.7 4.4 %collective-permute-start.30 = (bf16[2304,128]{1,0:T(8,128)(2,1)S(1)}, bf16[2304,128]{1,0:T(8,128)(2,1)S(1)}, u32[]{:S(2)}, u32[]{:S(2)}) collective-permute-start(bf16[2304,128]{1,0:T(8,128)(2,1)S(1)} %collective-permute-done.16), channel_id=1, source_target_pairs={{0,4},{4,8},{8,12},{1,5},{5,9},{9,13},{2,6},{6,10},{10,14},{3,7},{... | collective-permute-start | bytes 1769480 | tf_op jit(solution)/shard_map/ppermute | solution.py:27
  111.3 8.5 %collective-permute-done.30 = bf16[2304,128]{1,0:T(8,128)(2,1)S(1)} collective-permute-done((bf16[2304,128]{1,0:T(8,128)(2,1)S(1)}, bf16[2304,128]{1,0:T(8,128)(2,1)S(1)}, u32[]{:S(2)}, u32[]{:S(2)}) %collective-permute-start.30) | collective-permute-done | bytes 589856 | tf_op jit(solution)/shard_map/ppermute | solution.py:27
  122.2 4.2 %collective-permute-done.33 = bf16[2304,128]{1,0:T(8,128)(2,1)S(1)} collective-permute-done((bf16[2304,128]{1,0:T(8,128)(2,1)S(1)}, bf16[2304,128]{1,0:T(8,128)(2,1)S(1)}, u32[]{:S(2)}, u32[]{:S(2)}) %collective-permute-start.33) | collective-permute-done | bytes 589856 | tf_op jit(solution)/shard_map/ppermute | solution.py:27
  129.0 8.5 %collective-permute-done.32 = bf16[2304,128]{1,0:T(8,128)(2,1)S(1)} collective-permute-done((bf16[2304,128]{1,0:T(8,128)(2,1)}, bf16[2304,128]{1,0:T(8,128)(2,1)S(1)}, u32[]{:S(2)}, u32[]{:S(2)}) %collective-permute-start.32) | collective-permute-done | bytes 589856 | tf_op jit(solution)/shard_map/ppermute | solution.py:27
  153.0 4.7 %collective-permute-done.41 = bf16[2304,128]{1,0:T(8,128)(2,1)S(1)} collective-permute-done((bf16[2304,128]{1,0:T(8,128)(2,1)S(1)}, bf16[2304,128]{1,0:T(8,128)(2,1)S(1)}, u32[]{:S(2)}, u32[]{:S(2)}) %collective-permute-start.41) | collective-permute-done | bytes 589856 | tf_op jit(solution)/shard_map/ppermute | solution.py:27
  157.6 4.4 %collective-permute-start.40 = (bf16[2304,128]{1,0:T(8,128)(2,1)S(1)}, bf16[2304,128]{1,0:T(8,128)(2,1)S(1)}, u32[]{:S(2)}, u32[]{:S(2)}) collective-permute-start(bf16[2304,128]{1,0:T(8,128)(2,1)S(1)} %collective-permute-done.30), channel_id=1, source_target_pairs={{0,4},{4,8},{8,12},{1,5},{5,9},{9,13},{2,6},{6,10},{10,14},{3,7},{... | collective-permute-start | bytes 1769480 | tf_op jit(solution)/shard_map/ppermute | solution.py:27
  167.3 6.3 %collective-permute-done.40 = bf16[2304,128]{1,0:T(8,128)(2,1)S(1)} collective-permute-done((bf16[2304,128]{1,0:T(8,128)(2,1)S(1)}, bf16[2304,128]{1,0:T(8,128)(2,1)S(1)}, u32[]{:S(2)}, u32[]{:S(2)}) %collective-permute-start.40) | collective-permute-done | bytes 589856 | tf_op jit(solution)/shard_map/ppermute | solution.py:27
  175.9 7.4 %collective-permute-done.43 = bf16[2304,128]{1,0:T(8,128)(2,1)S(1)} collective-permute-done((bf16[2304,128]{1,0:T(8,128)(2,1)S(1)}, bf16[2304,128]{1,0:T(8,128)(2,1)S(1)}, u32[]{:S(2)}, u32[]{:S(2)}) %collective-permute-start.43) | collective-permute-done | bytes 589856 | tf_op jit(solution)/shard_map/ppermute | solution.py:27
  183.3 3.6 %collective-permute-start.39 = (bf16[2304,128]{1,0:T(8,128)(2,1)S(1)}, bf16[2304,128]{1,0:T(8,128)(2,1)S(1)}, u32[]{:S(2)}, u32[]{:S(2)}) collective-permute-start(bf16[2304,128]{1,0:T(8,128)(2,1)S(1)} %collective-permute-done.29), channel_id=1, source_target_pairs={{0,4},{4,8},{8,12},{1,5},{5,9},{9,13},{2,6},{6,10},{10,14},{3,7},{... | collective-permute-start | bytes 1769480 | tf_op jit(solution)/shard_map/ppermute | solution.py:27
  187.8 6.1 %collective-permute-done.42 = bf16[2304,128]{1,0:T(8,128)(2,1)S(1)} collective-permute-done((bf16[2304,128]{1,0:T(8,128)(2,1)S(1)}, bf16[2304,128]{1,0:T(8,128)(2,1)S(1)}, u32[]{:S(2)}, u32[]{:S(2)}) %collective-permute-start.42) | collective-permute-done | bytes 589856 | tf_op jit(solution)/shard_map/ppermute | solution.py:27
  206.8 3.8 %collective-permute-start.28 = (bf16[4,32,512]{2,0,1:T(4,128)(2,1)S(1)}, bf16[4,32,512]{2,0,1:T(4,128)(2,1)S(1)}, u32[]{:S(2)}, u32[]{:S(2)}) collective-permute-start(bf16[4,32,512]{2,0,1:T(4,128)(2,1)S(1)} %copy.72), channel_id=1, source_target_pairs={{0,4},{4,8},{8,12},{1,5},{5,9},{9,13},{2,6},{6,10},{10,14},{3,7},{... | collective-permute-start | bytes 393224 | tf_op jit(solution)/shard_map/ppermute | solution.py:27
  212.5 4.5 %collective-permute-start.48 = (bf16[4,32,512]{2,0,1:T(4,128)(2,1)S(1)}, bf16[4,32,512]{2,0,1:T(4,128)(2,1)S(1)}, u32[]{:S(2)}, u32[]{:S(2)}) collective-permute-start(bf16[4,32,512]{2,0,1:T(4,128)(2,1)S(1)} %copy.70), channel_id=1, source_target_pairs={{12,0},{0,12},{13,1},{1,13},{14,2},{2,14},{15,3},{3,15},{28,16},{1... | collective-permute-start | bytes 393224 | tf_op jit(solution)/shard_map/ppermute | solution.py:133
  (193 shorter events, 121.1 us)
Async XLA Ops:
  0.0 33.9 %collective-permute-start.4 = (bf16[1280,128]{1,0:T(8,128)(2,1)}, bf16[1280,128]{1,0:T(8,128)(2,1)}, u32[]{:S(2)}, u32[]{:S(2)}) collective-permute-start(bf16[1280,128]{1,0:T(8,128)(2,1)} %param.10), channel_id=1, source_target_pairs={{4,0},{8,4},{12,8},{5,1},{9,5},{13,9},{6,2},{10,6},{14,10},{7,3},{... | collective-permute-start | bytes 983048 | tf_op jit(solution)/shard_map/ppermute | solution.py:27
  1.6 35.3 %collective-permute-start.3 = (bf16[1280,128]{1,0:T(8,128)(2,1)}, bf16[1280,128]{1,0:T(8,128)(2,1)}, u32[]{:S(2)}, u32[]{:S(2)}) collective-permute-start(bf16[1280,128]{1,0:T(8,128)(2,1)} %param.10), channel_id=1, source_target_pairs={{0,4},{4,8},{8,12},{1,5},{5,9},{9,13},{2,6},{6,10},{10,14},{3,7},{... | collective-permute-start | bytes 983048 | tf_op jit(solution)/shard_map/ppermute | solution.py:27
  10.6 52.7 %collective-permute-start.15 = (bf16[2304,128]{1,0:T(8,128)(2,1)}, bf16[2304,128]{1,0:T(8,128)(2,1)}, u32[]{:S(2)}, u32[]{:S(2)}) collective-permute-start(bf16[2304,128]{1,0:T(8,128)(2,1)} %get-tuple-element.13), channel_id=1, source_target_pairs={{0,4},{4,8},{8,12},{1,5},{5,9},{9,13},{2,6},{6,10},{10,14},{3,7},{... | collective-permute-start | bytes 1769480 | tf_op jit(solution)/shard_map/ppermute | solution.py:27
  14.6 80.1 %collective-permute-start.22 = (bf16[2304,128]{1,0:T(8,128)(2,1)}, bf16[2304,128]{1,0:T(8,128)(2,1)}, u32[]{:S(2)}, u32[]{:S(2)}) collective-permute-start(bf16[2304,128]{1,0:T(8,128)(2,1)} %get-tuple-element.13), channel_id=1, source_target_pairs={{4,0},{8,4},{12,8},{5,1},{9,5},{13,9},{6,2},{10,6},{14,10},{7,3},{... | collective-permute-start | bytes 1769480 | tf_op jit(solution)/shard_map/ppermute | solution.py:27
  15.9 27.0 %collective-permute-start.17 = (bf16[2304,128]{1,0:T(8,128)(2,1)}, bf16[2304,128]{1,0:T(8,128)(2,1)}, u32[]{:S(2)}, u32[]{:S(2)}) collective-permute-start(bf16[2304,128]{1,0:T(8,128)(2,1)} %get-tuple-element.14), channel_id=1, source_target_pairs={{0,4},{4,8},{8,12},{1,5},{5,9},{9,13},{2,6},{6,10},{10,14},{3,7},{... | collective-permute-start | bytes 1769480 | tf_op jit(solution)/shard_map/ppermute | solution.py:27
  33.9 18.4 %collective-permute-start.24 = (bf16[2304,128]{1,0:T(8,128)(2,1)}, bf16[2304,128]{1,0:T(8,128)(2,1)S(1)}, u32[]{:S(2)}, u32[]{:S(2)}) collective-permute-start(bf16[2304,128]{1,0:T(8,128)(2,1)} %get-tuple-element.14), channel_id=1, source_target_pairs={{4,0},{8,4},{12,8},{5,1},{9,5},{13,9},{6,2},{10,6},{14,10},{7,3},{... | collective-permute-start | bytes 1769480 | tf_op jit(solution)/shard_map/ppermute | solution.py:27
  36.9 19.3 %collective-permute-start.16 = (bf16[2304,128]{1,0:T(8,128)(2,1)S(1)}, bf16[2304,128]{1,0:T(8,128)(2,1)S(1)}, u32[]{:S(2)}, u32[]{:S(2)}) collective-permute-start(bf16[2304,128]{1,0:T(8,128)(2,1)S(1)} %copy-done.4), channel_id=1, source_target_pairs={{0,4},{4,8},{8,12},{1,5},{5,9},{9,13},{2,6},{6,10},{10,14},{3,7},{... | collective-permute-start | bytes 1769480 | tf_op jit(solution)/shard_map/ppermute | solution.py:27
  42.9 23.7 %collective-permute-start.23 = (bf16[2304,128]{1,0:T(8,128)(2,1)S(1)}, bf16[2304,128]{1,0:T(8,128)(2,1)S(1)}, u32[]{:S(2)}, u32[]{:S(2)}) collective-permute-start(bf16[2304,128]{1,0:T(8,128)(2,1)S(1)} %copy-done.4), channel_id=1, source_target_pairs={{4,0},{8,4},{12,8},{5,1},{9,5},{13,9},{6,2},{10,6},{14,10},{7,3},{... | collective-permute-start | bytes 1769480 | tf_op jit(solution)/shard_map/ppermute | solution.py:27
  52.3 19.7 %collective-permute-start.5 = (bf16[1280,128]{1,0:T(8,128)(2,1)}, bf16[1280,128]{1,0:T(8,128)(2,1)S(1)}, u32[]{:S(2)}, u32[]{:S(2)}) collective-permute-start(bf16[1280,128]{1,0:T(8,128)(2,1)} %collective-permute-done.4), channel_id=1, source_target_pairs={{4,0},{8,4},{12,8},{5,1},{9,5},{13,9},{6,2},{10,6},{14,10},{7,3},{... | collective-permute-start | bytes 983048 | tf_op jit(solution)/shard_map/ppermute | solution.py:27
  56.2 21.7 %collective-permute-start.7 = (bf16[1280,128]{1,0:T(8,128)(2,1)}, bf16[1280,128]{1,0:T(8,128)(2,1)S(1)}, u32[]{:S(2)}, u32[]{:S(2)}) collective-permute-start(bf16[1280,128]{1,0:T(8,128)(2,1)} %collective-permute-done.3), channel_id=1, source_target_pairs={{0,4},{4,8},{8,12},{1,5},{5,9},{9,13},{2,6},{6,10},{10,14},{3,7},{... | collective-permute-start | bytes 983048 | tf_op jit(solution)/shard_map/ppermute | solution.py:27
  63.3 45.8 %collective-permute-start.34 = (bf16[2304,128]{1,0:T(8,128)(2,1)S(1)}, bf16[2304,128]{1,0:T(8,128)(2,1)S(1)}, u32[]{:S(2)}, u32[]{:S(2)}) collective-permute-start(bf16[2304,128]{1,0:T(8,128)(2,1)S(1)} %collective-permute-done.24), channel_id=1, source_target_pairs={{4,0},{8,4},{12,8},{5,1},{9,5},{13,9},{6,2},{10,6},{14,10},{7,3},{... | collective-permute-start | bytes 1769480 | tf_op jit(solution)/shard_map/ppermute | solution.py:27
  71.9 17.1 %collective-permute-start.6 = (bf16[1280,128]{1,0:T(8,128)(2,1)S(1)}, bf16[1280,128]{1,0:T(8,128)(2,1)S(1)}, u32[]{:S(2)}, u32[]{:S(2)}) collective-permute-start(bf16[1280,128]{1,0:T(8,128)(2,1)S(1)} %collective-permute-done.5), channel_id=1, source_target_pairs={{4,0},{8,4},{12,8},{5,1},{9,5},{13,9},{6,2},{10,6},{14,10},{7,3},{... | collective-permute-start | bytes 983048 | tf_op jit(solution)/shard_map/ppermute | solution.py:27
  73.2 30.5 %collective-permute-start.31 = (bf16[2304,128]{1,0:T(8,128)(2,1)}, bf16[2304,128]{1,0:T(8,128)(2,1)S(1)}, u32[]{:S(2)}, u32[]{:S(2)}) collective-permute-start(bf16[2304,128]{1,0:T(8,128)(2,1)} %collective-permute-done.17), channel_id=1, source_target_pairs={{0,4},{4,8},{8,12},{1,5},{5,9},{9,13},{2,6},{6,10},{10,14},{3,7},{... | collective-permute-start | bytes 1769480 | tf_op jit(solution)/shard_map/ppermute | solution.py:27
  97.3 48.8 %collective-permute-start = (bf16[32,512]{1,0:T(8,128)(2,1)S(1)}, bf16[32,512]{1,0:T(8,128)(2,1)S(1)}, u32[]{:S(2)}, u32[]{:S(2)}) collective-permute-start(bf16[32,512]{1,0:T(8,128)(2,1)S(1)} %get-tuple-element.22), channel_id=1, source_target_pairs={{0,1},{1,0},{2,3},{3,2},{4,5},{5,4},{6,7},{7,6},{8,9},{9,8},{10,11... | collective-permute-start | bytes 98312 | tf_op jit(solution)/shard_map/ppermute | solution.py:32
  98.6 49.1 %collective-permute-start.2 = (bf16[32,512]{1,0:T(8,128)(2,1)S(1)}, bf16[32,512]{1,0:T(8,128)(2,1)S(1)}, u32[]{:S(2)}, u32[]{:S(2)}) collective-permute-start(bf16[32,512]{1,0:T(8,128)(2,1)S(1)} %get-tuple-element.23), channel_id=1, source_target_pairs={{0,3},{1,2},{2,1},{3,0},{4,7},{5,6},{6,5},{7,4},{8,11},{9,10},{10,... | collective-permute-start | bytes 98312 | tf_op jit(solution)/shard_map/ppermute | solution.py:32
  101.8 46.4 %collective-permute-start.1 = (bf16[32,512]{1,0:T(8,128)(2,1)S(1)}, bf16[32,512]{1,0:T(8,128)(2,1)S(1)}, u32[]{:S(2)}, u32[]{:S(2)}) collective-permute-start(bf16[32,512]{1,0:T(8,128)(2,1)S(1)} %get-tuple-element.24), channel_id=1, source_target_pairs={{0,2},{1,3},{2,0},{3,1},{4,6},{5,7},{6,4},{7,5},{8,10},{9,11},{10,... | collective-permute-start | bytes 98312 | tf_op jit(solution)/shard_map/ppermute | solution.py:32
  109.1 17.3 %collective-permute-start.33 = (bf16[2304,128]{1,0:T(8,128)(2,1)S(1)}, bf16[2304,128]{1,0:T(8,128)(2,1)S(1)}, u32[]{:S(2)}, u32[]{:S(2)}) collective-permute-start(bf16[2304,128]{1,0:T(8,128)(2,1)S(1)} %collective-permute-done.23), channel_id=1, source_target_pairs={{4,0},{8,4},{12,8},{5,1},{9,5},{13,9},{6,2},{10,6},{14,10},{7,3},{... | collective-permute-start | bytes 1769480 | tf_op jit(solution)/shard_map/ppermute | solution.py:27
  119.8 17.7 %collective-permute-start.32 = (bf16[2304,128]{1,0:T(8,128)(2,1)}, bf16[2304,128]{1,0:T(8,128)(2,1)S(1)}, u32[]{:S(2)}, u32[]{:S(2)}) collective-permute-start(bf16[2304,128]{1,0:T(8,128)(2,1)} %collective-permute-done.22), channel_id=1, source_target_pairs={{4,0},{8,4},{12,8},{5,1},{9,5},{13,9},{6,2},{10,6},{14,10},{7,3},{... | collective-permute-start | bytes 1769480 | tf_op jit(solution)/shard_map/ppermute | solution.py:27
  145.9 51.5 %collective-permute-start.18 = (bf16[32,512]{1,0:T(8,128)(2,1)S(1)}, bf16[32,512]{1,0:T(8,128)(2,1)S(1)}, u32[]{:S(2)}, u32[]{:S(2)}) collective-permute-start(bf16[32,512]{1,0:T(8,128)(2,1)S(1)} %get-tuple-element.19), channel_id=1, source_target_pairs={{0,1},{1,0},{2,3},{3,2},{4,5},{5,4},{6,7},{7,6},{8,9},{9,8},{10,11... | collective-permute-start | bytes 98312 | tf_op jit(solution)/shard_map/ppermute | solution.py:32
  146.1 52.0 %collective-permute-start.20 = (bf16[32,512]{1,0:T(8,128)(2,1)S(1)}, bf16[32,512]{1,0:T(8,128)(2,1)S(1)}, u32[]{:S(2)}, u32[]{:S(2)}) collective-permute-start(bf16[32,512]{1,0:T(8,128)(2,1)S(1)} %get-tuple-element.20), channel_id=1, source_target_pairs={{0,3},{1,2},{2,1},{3,0},{4,7},{5,6},{6,5},{7,4},{8,11},{9,10},{10,... | collective-permute-start | bytes 98312 | tf_op jit(solution)/shard_map/ppermute | solution.py:32
  147.6 50.9 %collective-permute-start.19 = (bf16[32,512]{1,0:T(8,128)(2,1)S(1)}, bf16[32,512]{1,0:T(8,128)(2,1)S(1)}, u32[]{:S(2)}, u32[]{:S(2)}) collective-permute-start(bf16[32,512]{1,0:T(8,128)(2,1)S(1)} %get-tuple-element.21), channel_id=1, source_target_pairs={{0,2},{1,3},{2,0},{3,1},{4,6},{5,7},{6,4},{7,5},{8,10},{9,11},{10,... | collective-permute-start | bytes 98312 | tf_op jit(solution)/shard_map/ppermute | solution.py:32
  148.1 17.0 %collective-permute-start.44 = (bf16[2304,128]{1,0:T(8,128)(2,1)S(1)}, bf16[2304,128]{1,0:T(8,128)(2,1)S(1)}, u32[]{:S(2)}, u32[]{:S(2)}) collective-permute-start(bf16[2304,128]{1,0:T(8,128)(2,1)S(1)} %collective-permute-done.34), channel_id=1, source_target_pairs={{4,0},{8,4},{12,8},{5,1},{9,5},{13,9},{6,2},{10,6},{14,10},{7,3},{... | collective-permute-start | bytes 1769480 | tf_op jit(solution)/shard_map/ppermute | solution.py:27
  165.1 18.1 %collective-permute-start.43 = (bf16[2304,128]{1,0:T(8,128)(2,1)S(1)}, bf16[2304,128]{1,0:T(8,128)(2,1)S(1)}, u32[]{:S(2)}, u32[]{:S(2)}) collective-permute-start(bf16[2304,128]{1,0:T(8,128)(2,1)S(1)} %collective-permute-done.33), channel_id=1, source_target_pairs={{4,0},{8,4},{12,8},{5,1},{9,5},{13,9},{6,2},{10,6},{14,10},{7,3},{... | collective-permute-start | bytes 1769480 | tf_op jit(solution)/shard_map/ppermute | solution.py:27
  173.7 20.2 %collective-permute-start.42 = (bf16[2304,128]{1,0:T(8,128)(2,1)S(1)}, bf16[2304,128]{1,0:T(8,128)(2,1)S(1)}, u32[]{:S(2)}, u32[]{:S(2)}) collective-permute-start(bf16[2304,128]{1,0:T(8,128)(2,1)S(1)} %collective-permute-done.32), channel_id=1, source_target_pairs={{4,0},{8,4},{12,8},{5,1},{9,5},{13,9},{6,2},{10,6},{14,10},{7,3},{... | collective-permute-start | bytes 1769480 | tf_op jit(solution)/shard_map/ppermute | solution.py:27
  (43 other events, 415.7 us)

commit v2 on v0

--- a/solution.py
+++ b/solution.py
@@ -4,7 +4,11 @@
 from jax.sharding import PartitionSpec as P
 
 TILE = 128
-
+FEAT = ("eig", "rep")
+SIDE = ((0, 1), (1, 0), (2, 3), (3, 2))
+MIDDLE = ((0, 0), (1, 2), (2, 1), (3, 3))
+FAR = ((0, 3), (3, 0), (1, 1), (2, 2))
+TWO = ((0, 2), (2, 0), (1, 3), (3, 1))
 
 damping = 0.01
 
@@ -21,9 +25,176 @@
     return (rowmask, onehot)
 
 
-def per_device(acts, grads, basis_in, basis_out, eigval, test_grads, pair_tiles, last_rows):
+def after(x, *earlier):
+    return lax.optimization_barrier((x, *earlier))[0]
+
+
+def swap(x, axis_name):
+    return lax.ppermute(x, axis_name, [(0, 1), (1, 0)])
+
+
+def halves(x, axis_name):
+    first = lax.axis_index(axis_name) == 0
+    low, high = x[0], x[1]
+    return jnp.where(first, low, high), jnp.where(first, high, low)
+
+
+def scatter_sum(part):
+    keep, give = halves(part.transpose(2, 1, 0, 3, 4), "rep")
+    keep = keep + swap(give, "rep")
+    keep, give = halves(keep, "eig")
+    return keep + swap(give, "eig")
+
+
+def gather_rows(x):
+    other = swap(x, "eig")
+    first = lax.axis_index("eig") == 0
+    both = jnp.stack([jnp.where(first, x, other), jnp.where(first, other, x)])
+    other = swap(both, "rep")
+    first = lax.axis_index("rep") == 0
+    whole = jnp.stack([jnp.where(first, both, other), jnp.where(first, other, both)], axis=1)
+    return whole.reshape((-1,) + x.shape[1:])
+
+
+def dot_t(basis, rows):
+    return lax.dot_general(basis, rows, (((0,), (1,)), ((), ())), preferred_element_type=jnp.float32)
+
+
+def dot_tt(basis, columns):
+    return lax.dot_general(
+        basis, columns, (((0,), (0,)), ((), ())), preferred_element_type=jnp.float32
+    )
+
+
+def line_plan(acts, grads, basis_in, basis_out, eigval, test_grads, pair_tiles, last_rows):
+    plane = lax.axis_index("cand")
+    end = (plane == 0) | (plane == 3)
+    eig, rep = lax.axis_size("eig"), lax.axis_size("rep")
+    tok_rows = acts.shape[0]
+    cols = basis_in.shape[1]
+    width_in = 4 * cols
+    tiles_here = tok_rows // TILE
+    slim = cols // (eig * rep)
+    depth = basis_out.shape[0] // 3
+    rows_in = basis_in.shape[0]
+
+    def pick(at_end, at_middle):
+        return jnp.where(end, at_end, at_middle)
+
+    def side(at_end, at_middle):
+        return lax.ppermute(pick(at_end, at_middle), "cand", SIDE)
+
+    def middle(x):
+        return lax.ppermute(x, "cand", MIDDLE)
+
+    own = [basis_out[i * depth : (i + 1) * depth] for i in range(3)]
+    grad = [grads[:, i * depth : (i + 1) * depth] for i in range(3)]
+    quarter = tok_rows // 4
+    turned = [grad[0][i * quarter : (i + 1) * quarter].T for i in range(4)]
+
+    s0 = lax.ppermute(basis_in, "cand", SIDE)
+    m0 = middle(basis_in)
+    s1 = lax.ppermute(own[1], "cand", SIDE)
+    m1 = middle(after(s0, m0))
+    s2 = side(after(own[0], s0), own[2])
+    m2 = middle(after(own[1], m0))
+    s3 = side(after(basis_out[3 * depth - 2 * rows_in :], s1), jnp.concatenate([m0, m1]))
+    m3 = middle(after(own[2], m1))
+    s4 = side(after(turned[0], s2), m2)
+    m4 = middle(after(own[0], m2))
+    s5 = side(after(turned[1], s3), m3)
+    m5 = middle(after(s1, m3))
+    s6 = side(after(turned[2], s4), m5)
+    m6 = middle(after(s3[2 * rows_in - depth :], m4))
+    s7 = side(after(turned[3], s5), m6)
+    m7 = middle(after(s2, m5))
+
+    in_b, in_c = pick(s3[:rows_in], m0), pick(s3[rows_in:], m1)
+    at_b = jnp.where(end, plane ^ 2, plane ^ 3)
+    at_c = jnp.where(end, plane ^ 3, plane ^ 2)
+    part_in = jnp.zeros((tok_rows, width_in), jnp.float32)
+    for shard, at in ((basis_in, plane), (s0, plane ^ 1), (in_b, at_b), (in_c, at_c)):
+        part = jnp.dot(acts, shard, preferred_element_type=jnp.float32)
+        part_in = lax.dynamic_update_slice_in_dim(part_in, part, at * cols, 1)
+    part_in = part_in.reshape(1, eig, rep, tok_rows // (eig * rep), width_in)
+    rot_in = gather_rows(scatter_sum(part_in)[0].astype(jnp.bfloat16))
+    rot_in = rot_in.reshape(tiles_here, TILE, width_in)
+
+    only_middle = jnp.where(end, 0.0, 1.0)
+
+    def blocks(*parts):
+        return jnp.stack([part.reshape(eig, rep, slim, part.shape[1]) for part in parts])
+
+    part_own = dot_t(basis_out, grads)
+    part_a = dot_t(s1, grad[1]) + dot_t(pick(s2, s3[2 * rows_in - depth :]), grad[2])
+    part_a = part_a + only_middle * dot_t(s2, grad[0])
+    sum_own, sum_a = scatter_sum(blocks(part_own, part_a))
+
+    part_b = dot_t(pick(s4, m2), grad[1]) + dot_t(pick(s5, m3), grad[2])
+    part_b = part_b + only_middle * dot_t(m4, grad[0])
+    sum_b = scatter_sum(blocks(part_b))[0]
+
+    part_c = dot_t(pick(s6, m5), grad[1]) + dot_t(pick(s7, m6), grad[2])
+    part_c = part_c + only_middle * dot_t(m7, grad[0])
+    theirs = [
+        jnp.concatenate([dot_tt(shard, tokens) for tokens in (s4, s5, s6, s7)], axis=1)
+        for shard in (own[0], m4, m7)
+    ]
+    sums = scatter_sum(blocks(part_c, *theirs))
+    sum_c = sums[0]
+    back = lax.ppermute(sums[1:], "cand", SIDE)
+    back = jnp.where(end, back, 0.0)
+
+    rowmask, ignored = tile_layout(pair_tiles, last_rows, plane * tiles_here, tiles_here, TILE)
+    keep = rowmask.reshape(1, tok_rows).astype(jnp.bfloat16)
+    precond = (test_grads.astype(jnp.float32) / (eigval + damping)).astype(jnp.bfloat16)
+
+    def tile_prods(rot_out):
+        return jnp.einsum(
+            "etr,tra->tea",
+            (rot_out.astype(jnp.bfloat16) * keep).reshape(slim, tiles_here, TILE),
+            rot_in,
+            preferred_element_type=jnp.float32,
+        ).astype(jnp.bfloat16)
+
+    def pair_scores(prods, source):
+        scores = jnp.einsum("tea,jea->tj", prods, precond, preferred_element_type=jnp.float32)
+        ignored_mask, onehot = tile_layout(
+            pair_tiles, last_rows, source * tiles_here, tiles_here, TILE
+        )
+        return jnp.sum(jnp.where(onehot[:, :, None], scores[:, None, :], 0.0), axis=0)
+
+    prods_a = tile_prods(sum_a + back[0])
+    prods_b = tile_prods(sum_b + back[1])
+    prods_c = tile_prods(sum_c + back[2])
+    total = pair_scores(tile_prods(sum_own), plane)
+    total = total + pair_scores(lax.ppermute(prods_a, "cand", SIDE), plane ^ 1)
+    total = total + pair_scores(lax.ppermute(pick(prods_b, prods_c), "cand", TWO), plane ^ 2)
+    three = [(0, 3), (3, 0), (1, 2), (2, 1)]
+    total = total + pair_scores(lax.ppermute(pick(prods_c, prods_b), "cand", three), plane ^ 3)
+
+    return final_sum(total)
+
+
+def final_sum(total):
+    npairs, ntest = total.shape
+    mine = total.reshape(npairs, 2, 2, ntest // 4).transpose(2, 1, 0, 3)
+    keep, give = halves(mine, "rep")
+    keep = keep + swap(give, "rep")
+    keep, give = halves(keep, "eig")
+    keep = keep + swap(give, "eig")
+    plane = lax.axis_index("cand")
+    rows = npairs // 4
+    result = lax.dynamic_slice_in_dim(keep, plane * rows, rows, 0)
+    for step in range(1, 4):
+        block = lax.dynamic_slice_in_dim(keep, (plane ^ step) * rows, rows, 0)
+        result = result + lax.ppermute(block, "cand", [(i, i ^ step) for i in range(4)])
+    return result
+
+
+def gather_plan(acts, grads, basis_in, basis_out, eigval, test_grads, pair_tiles, last_rows):
     ncand = lax.axis_size("cand")
-    nfeat = lax.axis_size(("eig", "rep"))
+    nfeat = lax.axis_size(FEAT)
     tok_rows = acts.shape[0]
     width_in = basis_in.shape[1] * ncand
     width_out = basis_out.shape[1] * ncand
@@ -40,24 +211,23 @@
     )
     part_out = part_out.reshape(tok_rows, ncand, nfeat, slim).transpose(0, 2, 1, 3)
     part_out = part_out.reshape(tok_rows, nfeat * ncand * slim)
-    summed_in, summed_out = lax.psum((part_in, part_out), ("eig", "rep"))
+    summed_in, summed_out = lax.psum((part_in, part_out), FEAT)
     own = lax.dynamic_slice_in_dim(
-        summed_out, lax.axis_index(("eig", "rep")) * (ncand * slim), ncand * slim, 1
+        summed_out, lax.axis_index(FEAT) * (ncand * slim), ncand * slim, 1
     )
     rot_in = summed_in.astype(jnp.bfloat16)
     rot_out = own.astype(jnp.bfloat16)
-    tile_rows = TILE
-    tiles_here = tok_rows // tile_rows
+    tiles_here = tok_rows // TILE
     rowmask, ignored = tile_layout(
-        pair_tiles, last_rows, lax.axis_index("cand") * tiles_here, tiles_here, tile_rows
-    )
-    masked = rot_out.reshape(tiles_here, tile_rows, ncand * slim) * rowmask[:, :, None].astype(
+        pair_tiles, last_rows, lax.axis_index("cand") * tiles_here, tiles_here, TILE
+    )
+    masked = rot_out.reshape(tiles_here, TILE, ncand * slim) * rowmask[:, :, None].astype(
         jnp.bfloat16
     )
     prods = jnp.einsum(
         "tre,tra->tea",
         masked,
-        rot_in.reshape(tiles_here, tile_rows, width_in),
+        rot_in.reshape(tiles_here, TILE, width_in),
         preferred_element_type=jnp.float32,
     ).astype(jnp.bfloat16)
     prods = prods.reshape(tiles_here, ncand, slim, width_in)
@@ -66,7 +236,7 @@
     received = received.reshape(all_tiles, slim, width_in)
     precond = (test_grads.astype(jnp.float32) / (eigval + damping)).astype(jnp.bfloat16)
     tile_part = jnp.einsum("tea,jea->tj", received, precond, preferred_element_type=jnp.float32)
-    ignored_mask, onehot = tile_layout(pair_tiles, last_rows, 0, all_tiles, tile_rows)
+    ignored_mask, onehot = tile_layout(pair_tiles, last_rows, 0, all_tiles, TILE)
     pair_part = jnp.dot(onehot.astype(jnp.float32).T, tile_part, precision=lax.Precision.HIGHEST)
     npairs = pair_part.shape[0]
     ntest = pair_part.shape[1]
@@ -75,7 +245,7 @@
         total, lax.axis_index("cand") * (npairs // ncand), npairs // ncand, 0
     )
     return lax.dynamic_slice_in_dim(
-        rows, lax.axis_index(("eig", "rep")) * (ntest // nfeat), ntest // nfeat, 1
+        rows, lax.axis_index(FEAT) * (ntest // nfeat), ntest // nfeat, 1
     )
 
 
@@ -91,6 +261,8 @@
         P("groups"),
     )
     out_specs = P(("groups", "cand"), ("eig", "rep"))
+    sizes = (mesh.shape["cand"], mesh.shape["eig"], mesh.shape["rep"])
+    per_device = line_plan if sizes == (4, 2, 2) else gather_plan
     return jax.shard_map(
         per_device, mesh=mesh, in_specs=in_specs, out_specs=out_specs, check_vma=False
     )

time: 289 us -> 224 us (0.78); the launches traced: 289 us -> 221 us
  waiting for transfers between devices: 177 us -> 38.3 us
  blocking collectives: 71.8 us -> 0 us
  starting transfers between devices: 4.18 us -> 66.9 us
  matrix products: 16.8 us -> 68.8 us
  other arithmetic: 2.65 us -> 23.7 us
  local copies, waits for them, and re-layouts: 3.42 us -> 22.7 us
  between operations: 13.5 us -> 0.81 us
    all_gather x2 -> x0, waiting for transfers between devices: 162 us -> none  [the longest x1 126 us: per_device(): lax.all_gather(basis_out, 'cand', axis=1, tiled=True)]
    psum x2 -> x0, blocking collectives: 71.8 us -> none  [the longest x1 41.7 us: per_device(): summed_in, summed_out = lax.psum((part_in, part_out), ('eig', 'rep'))]
    ppermute x0 -> x35, starting transfers between devices: none -> 66.9 us  [the longest x8 32.8 us: middle(): return lax.ppermute(x, 'cand', MIDDLE)]
    dot_general x5 -> x34, matrix products: 16.8 us -> 68.8 us  [the longest x10 32.3 us: dot_t(): lax.dot_general(basis, rows, (((0,), (1,)), ((), ())), preferred_element_...]
    ppermute x0 -> x35, waiting for transfers between devices: none -> 38.3 us  [the longest x12 18.1 us: swap(): return lax.ppermute(x, axis_name, [(0, 1), (1, 0)])]
    all_to_all x1 -> x0, waiting for transfers between devices: 13.3 us -> none  [per_device(): lax.all_to_all(prods, 'cand', split_axis=1, concat_axis=0, tiled=True)]
    unnamed x10 -> x69, local copies, waits for them, and re-layouts: 0.02 us -> 9.24 us
    select_n x0 -> x15, other arithmetic: none -> 7.64 us  [the longest x9 4.45 us: halves(): return (jnp.where(first, low, high), jnp.where(first, high, low))]
  transfers between devices with their start and end apart: 3 -> 35, of which waited for: 3 -> 12; matrix products, arithmetic and copies ran while one was open for 2% -> 49% of each run, Pallas kernels for 0% -> 0%
where the time goes in v2:
time: 224 us; the launch traced here: 221 us
  matrix products  68.8 us (31%)
  starting transfers between devices  66.9 us (30%)
  waiting for transfers between devices  38.3 us (17%)
  other arithmetic  23.7 us (11%)
  local copies, waits for them, and re-layouts  22.7 us (10%)
    ppermute x8, starting transfers between devices, middle(): return lax.ppermute(x, 'cand', MIDDLE)  32.8 us
    dot_general x10, matrix products, dot_t(): lax.dot_general(basis, rows, (((0,), (1,)), ((), ())), preferred_element_...  32.3 us
    dot_general x12, matrix products, dot_tt(): lax.dot_general(basis, columns, (((0,), (0,)), ((), ())), preferred_eleme...  18.3 us
    ppermute x12, waiting for transfers between devices, swap(): return lax.ppermute(x, axis_name, [(0, 1), (1, 0)])  18.1 us
    ppermute x6, waiting for transfers between devices, side(): return lax.ppermute(pick(at_end, at_middle), 'cand', SIDE)  11.9 us
    ppermute x6, starting transfers between devices, side(): return lax.ppermute(pick(at_end, at_middle), 'cand', SIDE)  10.4 us
    dot_general x4, matrix products, pair_scores(): jnp.einsum('tea,jea->tj', prods, precond, preferred_element_type=jnp.floa...  10.1 us
    unnamed x69, local copies, waits for them, and re-layouts  9.24 us
  transfers between devices with their start and end apart: 35, of which 12 were waited for; matrix products, arithmetic and copies ran while one was open for 49% of the time, Pallas kernels for 0%

profile of v2, /device:TPU:0, one launch (start us, length us, event | category | flops | bytes accessed | tf_op | source)
XLA Modules:
  0.0 221.2 jit_solution(11200640896161256868)
XLA Ops:
  0.0 3.0 %collective-permute-start.1 = (bf16[1280,128]{1,0:T(8,128)(2,1)}, bf16[1280,128]{1,0:T(8,128)(2,1)}, u32[]{:S(2)}, u32[]{:S(2)}) collective-permute-start(bf16[1280,128]{1,0:T(8,128)(2,1)} %param.10), channel_id=1, source_target_pairs={{0,4},{4,0},{8,12},{12,8},{1,5},{5,1},{9,13},{13,9},{2,6},{6,2},{1... | collective-permute-start | bytes 983048 | tf_op jit(solution)/shard_map/ppermute | solution.py:95
  4.7 3.3 %fusion.106 = (bf16[128,2304]{1,0:T(8,128)(2,1)}, bf16[128,2304]{1,0:T(8,128)(2,1)}, bf16[128,2304]{1,0:T(8,128)(2,1)}, bf16[128,2304]{1,0:T(8,128)(2,1)}) fusion(bf16[512,6912]{1,0:T(8,128)(2,1)} %param.9), kind=kLoop, calls=%fused_computation.174 | loop fusion | bytes 4718592 | tf_op jit(solution)/shard_map/slice | solution.py:93
  8.0 6.2 %fusion.109 = f32[128,512]{1,0:T(8,128)} fusion(bf16[6912,128]{1,0:T(8,128)(2,1)S(1)} %copy-done.1, bf16[512,6912]{1,0:T(8,128)(2,1)} %param.9), kind=kOutput, calls=%fused_computation.177 | convolution fusion | flops 905969664 | bytes 9109504 | tf_op jit(solution)/shard_map/dot_general | solution.py:60
  16.6 3.5 %divide_convert_fusion = bf16[64,32,512]{2,1,0:T(8,128)(2,1)} fusion(bf16[64,32,512]{2,1,0:T(8,128)(2,1)} %param.13, f32[32,512]{1,0:T(8,128)S(1)} %broadcast_add_fusion), kind=kLoop, calls=%fused_computation | loop fusion | flops 3145728 | bytes 4259840 | tf_op jit(solution)/shard_map/convert_element_type | solution.py:150
  29.3 6.0 %collective-permute-start.12 = (bf16[2304,128]{1,0:T(8,128)(2,1)}, bf16[2304,128]{1,0:T(8,128)(2,1)}, u32[]{:S(2)}, u32[]{:S(2)}) collective-permute-start(bf16[2304,128]{1,0:T(8,128)(2,1)} %get-tuple-element.22), channel_id=1, source_target_pairs={{0,0},{4,8},{8,4},{12,12},{1,1},{5,9},{9,5},{13,13},{2,2},{6,10},{... | collective-permute-start | bytes 1769480 | tf_op jit(solution)/shard_map/ppermute | solution.py:88
  35.9 3.9 %collective-permute-start.4 = (bf16[1280,128]{1,0:T(8,128)(2,1)}, bf16[1280,128]{1,0:T(8,128)(2,1)}, u32[]{:S(2)}, u32[]{:S(2)}) collective-permute-start(bf16[1280,128]{1,0:T(8,128)(2,1)} %collective-permute-done.1), channel_id=1, source_target_pairs={{0,0},{4,8},{8,4},{12,12},{1,1},{5,9},{9,5},{13,13},{2,2},{6,10},{... | collective-permute-start | bytes 983048 | tf_op jit(solution)/shard_map/ppermute | solution.py:88
  50.7 4.4 %collective-permute-done.2 = bf16[2304,128]{1,0:T(8,128)(2,1)} collective-permute-done((bf16[2304,128]{1,0:T(8,128)(2,1)}, bf16[2304,128]{1,0:T(8,128)(2,1)}, u32[]{:S(2)}, u32[]{:S(2)}) %collective-permute-start.2) | collective-permute-done | bytes 589856 | tf_op jit(solution)/shard_map/ppermute | solution.py:85
  55.1 2.9 %collective-permute-start.13 = (bf16[2304,128]{1,0:T(8,128)(2,1)S(1)}, bf16[2304,128]{1,0:T(8,128)(2,1)S(1)}, u32[]{:S(2)}, u32[]{:S(2)}) collective-permute-start(bf16[2304,128]{1,0:T(8,128)(2,1)S(1)} %broadcast_select_fusion.3), channel_id=1, source_target_pairs={{0,4},{4,0},{8,12},{12,8},{1,5},{5,1},{9,13},{13,9},{2,6},{6,2},{1... | collective-permute-start | bytes 1769480 | tf_op jit(solution)/shard_map/ppermute | solution.py:85
  65.6 6.0 %collective-permute-start.15 = (bf16[2304,128]{1,0:T(8,128)(2,1)}, bf16[2304,128]{1,0:T(8,128)(2,1)}, u32[]{:S(2)}, u32[]{:S(2)}) collective-permute-start(bf16[2304,128]{1,0:T(8,128)(2,1)} %collective-permute-done), channel_id=1, source_target_pairs={{0,0},{4,8},{8,4},{12,12},{1,1},{5,9},{9,5},{13,13},{2,2},{6,10},{... | collective-permute-start | bytes 1769480 | tf_op jit(solution)/shard_map/ppermute | solution.py:88
  73.6 3.4 %fusion.41 = f32[128,512]{1,0:T(8,128)} fusion(bf16[2304,128]{1,0:T(8,128)(2,1)S(1)} %collective-permute-done.18, bf16[512,6912]{1,0:T(8,128)(2,1)} %param.9, f32[]{:T(128)S(6)} %select_n.424), kind=kOutput, calls=%fused_computation.34 | convolution fusion | flops 302055424 | bytes 3211268 | tf_op jit(solution)/shard_map/dot_general | solution.py:60
  77.0 6.9 %collective-permute-done.5 = bf16[2560,128]{1,0:T(8,128)(2,1)S(1)} collective-permute-done((bf16[2560,128]{1,0:T(8,128)(2,1)S(1)}, bf16[2560,128]{1,0:T(8,128)(2,1)S(1)}, u32[]{:S(2)}, u32[]{:S(2)}) %collective-permute-start.5) | collective-permute-done | bytes 655392 | tf_op jit(solution)/shard_map/ppermute | solution.py:85
  84.8 5.5 %collective-permute-start.17 = (bf16[2304,128]{1,0:T(8,128)(2,1)}, bf16[2304,128]{1,0:T(8,128)(2,1)}, u32[]{:S(2)}, u32[]{:S(2)}) collective-permute-start(bf16[2304,128]{1,0:T(8,128)(2,1)} %broadcast_select_fusion.1), channel_id=1, source_target_pairs={{0,4},{4,0},{8,12},{12,8},{1,5},{5,1},{9,13},{13,9},{2,6},{6,2},{1... | collective-permute-start | bytes 1769480 | tf_op jit(solution)/shard_map/ppermute | solution.py:85
  90.3 2.8 %fusion.10 = f32[128,512]{1,0:T(8,128)S(1)} fusion(bf16[512,6912]{1,0:T(8,128)(2,1)} %param.9, bf16[2304,128]{1,0:T(8,128)(2,1)} %collective-permute-done.2, pred[]{:T(512)S(6)} %or.3, bf16[2560,128]{1,0:T(8,128)(2,1)S(1)} %collective-permute-done.5), kind=kOutput, calls=%fused_computation.11 | convolution fusion | flops 302284800 | bytes 3801089 | tf_op jit(solution)/shard_map/dot_general | solution.py:60
  93.1 2.8 %fusion.50 = f32[128,512]{1,0:T(8,128)S(1)} fusion(f32[128,512]{1,0:T(8,128)S(1)} %fusion.35, f32[128,512]{1,0:T(8,128)S(1)} %fusion.10, bf16[2304,128]{1,0:T(8,128)(2,1)} %collective-permute-done, bf16[512,6912]{1,0:T(8,128)(2,1)} %param.9), kind=kOutput, calls=%fused_computation.37 | convolution fusion | flops 302120960 | bytes 3735552 | tf_op jit(solution)/shard_map/dot_general | solution.py:60
  98.3 6.0 %collective-permute-start.19 = (bf16[2304,128]{1,0:T(8,128)(2,1)}, bf16[2304,128]{1,0:T(8,128)(2,1)}, u32[]{:S(2)}, u32[]{:S(2)}) collective-permute-start(bf16[2304,128]{1,0:T(8,128)(2,1)} %slice.161), channel_id=1, source_target_pairs={{0,0},{4,8},{8,4},{12,12},{1,1},{5,9},{9,5},{13,13},{2,2},{6,10},{... | collective-permute-start | bytes 1769480 | tf_op jit(solution)/shard_map/ppermute | solution.py:88
  119.4 3.0 %collective-permute-done.7 = f32[2,32,512]{2,1,0:T(8,128)S(1)} collective-permute-done((f32[2,32,512]{2,1,0:T(8,128)S(1)}, f32[2,32,512]{2,1,0:T(8,128)S(1)}, u32[]{:S(2)}, u32[]{:S(2)}) %collective-permute-start.7) | collective-permute-done | bytes 131104 | tf_op jit(solution)/shard_map/ppermute | solution.py:33
  122.3 6.0 %collective-permute-start.21 = (bf16[2304,128]{1,0:T(8,128)(2,1)}, bf16[2304,128]{1,0:T(8,128)(2,1)}, u32[]{:S(2)}, u32[]{:S(2)}) collective-permute-start(bf16[2304,128]{1,0:T(8,128)(2,1)} %collective-permute-done.2), channel_id=1, source_target_pairs={{0,0},{4,8},{8,4},{12,12},{1,1},{5,9},{9,5},{13,13},{2,2},{6,10},{... | collective-permute-start | bytes 1769480 | tf_op jit(solution)/shard_map/ppermute | solution.py:88
  133.6 2.8 %fusion.6 = f32[128,512]{1,0:T(8,128)S(1)} fusion(bf16[512,6912]{1,0:T(8,128)(2,1)} %param.9, bf16[2304,128]{1,0:T(8,128)(2,1)} %collective-permute-done.17, bf16[2304,128]{1,0:T(8,128)(2,1)S(1)} %copy-done.21, pred[]{:T(512)S(6)} %or.3), kind=kOutput, calls=%fused_computation.7 | convolution fusion | flops 302284800 | bytes 3801089 | tf_op jit(solution)/shard_map/dot_general | solution.py:60
  153.5 3.5 %fusion.38 = f32[128,512]{1,0:T(8,128)} fusion(bf16[2304,128]{1,0:T(8,128)(2,1)} %collective-permute-done.21, bf16[512,6912]{1,0:T(8,128)(2,1)} %param.9, f32[]{:T(128)S(6)} %select_n.424), kind=kOutput, calls=%fused_computation.33 | convolution fusion | flops 302055424 | bytes 3211268 | tf_op jit(solution)/shard_map/dot_general | solution.py:60
  165.1 2.8 %fusion.47 = f32[128,512]{1,0:T(8,128)S(1)} fusion(f32[128,512]{1,0:T(8,128)S(1)} %copy-done.31, f32[128,512]{1,0:T(8,128)S(1)} %fusion.8, bf16[512,6912]{1,0:T(8,128)(2,1)} %param.9, bf16[2304,128]{1,0:T(8,128)(2,1)} %collective-permute-done.16, bf16[2304,128]{1,0:T(8,128)(2,1)} %collective-permute-done.15, pred[]{:T(512)S(6)} %or.3), kind=kOutput, calls=%fused_computation.36 | convolution fusion | flops 302415872 | bytes 4325377 | tf_op jit(solution)/shard_map/dot_general | solution.py:60
  171.5 4.4 %collective-permute-done.10 = bf16[128,512]{1,0:T(8,128)(2,1)S(1)} collective-permute-done((bf16[128,512]{1,0:T(8,128)(2,1)S(1)}, bf16[128,512]{1,0:T(8,128)(2,1)S(1)}, u32[]{:S(2)}, u32[]{:S(2)}) %collective-permute-start.10) | collective-permute-done | bytes 131104 | tf_op jit(solution)/shard_map/ppermute | solution.py:33
  178.4 6.4 %collective-permute-done.23 = f32[4,32,512]{2,1,0:T(8,128)S(1)} collective-permute-done((f32[4,32,512]{2,1,0:T(8,128)S(1)}, f32[4,32,512]{2,1,0:T(8,128)S(1)}, u32[]{:S(2)}, u32[]{:S(2)}) %collective-permute-start.23) | collective-permute-done | bytes 262176 | tf_op jit(solution)/shard_map/ppermute | solution.py:33
  186.7 3.9 %collective-permute-done.24 = f32[3,32,512]{2,1,0:T(8,128)S(1)} collective-permute-done((f32[3,32,512]{2,1,0:T(8,128)S(1)}, f32[3,32,512]{2,1,0:T(8,128)S(1)}, u32[]{:S(2)}, u32[]{:S(2)}) %collective-permute-start.24) | collective-permute-done | bytes 196640 | tf_op jit(solution)/shard_map/ppermute | solution.py:145
  210.3 3.1 %collective-permute-done.31 = f32[8,16]{1,0:T(8,128)S(1)} collective-permute-done((f32[8,16]{1,0:T(8,128)S(1)}, f32[8,16]{1,0:T(8,128)S(1)}, u32[]{:S(2)}, u32[]{:S(2)}) %collective-permute-start.31) | collective-permute-done | bytes 544 | tf_op jit(solution)/shard_map/ppermute | solution.py:33
  (229 shorter events, 118.1 us)
Async XLA Ops:
  0.0 24.6 %collective-permute-start.1 = (bf16[1280,128]{1,0:T(8,128)(2,1)}, bf16[1280,128]{1,0:T(8,128)(2,1)}, u32[]{:S(2)}, u32[]{:S(2)}) collective-permute-start(bf16[1280,128]{1,0:T(8,128)(2,1)} %param.10), channel_id=1, source_target_pairs={{0,4},{4,0},{8,12},{12,8},{1,5},{5,1},{9,13},{13,9},{2,6},{6,2},{1... | collective-permute-start | bytes 983048 | tf_op jit(solution)/shard_map/ppermute | solution.py:95
  3.0 26.3 %collective-permute-start.3 = (bf16[1280,128]{1,0:T(8,128)(2,1)}, bf16[1280,128]{1,0:T(8,128)(2,1)S(1)}, u32[]{:S(2)}, u32[]{:S(2)}) collective-permute-start(bf16[1280,128]{1,0:T(8,128)(2,1)} %param.10), channel_id=1, source_target_pairs={{0,0},{4,8},{8,4},{12,12},{1,1},{5,9},{9,5},{13,13},{2,2},{6,10},{... | collective-permute-start | bytes 983048 | tf_op jit(solution)/shard_map/ppermute | solution.py:88
  26.9 23.8 %collective-permute-start = (bf16[2304,128]{1,0:T(8,128)(2,1)}, bf16[2304,128]{1,0:T(8,128)(2,1)}, u32[]{:S(2)}, u32[]{:S(2)}) collective-permute-start(bf16[2304,128]{1,0:T(8,128)(2,1)} %get-tuple-element.22), channel_id=1, source_target_pairs={{0,4},{4,0},{8,12},{12,8},{1,5},{5,1},{9,13},{13,9},{2,6},{6,2},{1... | collective-permute-start | bytes 1769480 | tf_op jit(solution)/shard_map/ppermute | solution.py:97
  29.3 25.7 %collective-permute-start.2 = (bf16[2304,128]{1,0:T(8,128)(2,1)}, bf16[2304,128]{1,0:T(8,128)(2,1)}, u32[]{:S(2)}, u32[]{:S(2)}) collective-permute-start(bf16[2304,128]{1,0:T(8,128)(2,1)} %get-tuple-element.41), channel_id=1, source_target_pairs={{0,4},{4,0},{8,12},{12,8},{1,5},{5,1},{9,13},{13,9},{2,6},{6,2},{1... | collective-permute-start | bytes 1769480 | tf_op jit(solution)/shard_map/ppermute | solution.py:85
  29.3 25.7 %collective-permute-start.12 = (bf16[2304,128]{1,0:T(8,128)(2,1)}, bf16[2304,128]{1,0:T(8,128)(2,1)}, u32[]{:S(2)}, u32[]{:S(2)}) collective-permute-start(bf16[2304,128]{1,0:T(8,128)(2,1)} %get-tuple-element.22), channel_id=1, source_target_pairs={{0,0},{4,8},{8,4},{12,12},{1,1},{5,9},{9,5},{13,13},{2,2},{6,10},{... | collective-permute-start | bytes 1769480 | tf_op jit(solution)/shard_map/ppermute | solution.py:88
  35.9 13.1 %collective-permute-start.4 = (bf16[1280,128]{1,0:T(8,128)(2,1)}, bf16[1280,128]{1,0:T(8,128)(2,1)}, u32[]{:S(2)}, u32[]{:S(2)}) collective-permute-start(bf16[1280,128]{1,0:T(8,128)(2,1)} %collective-permute-done.1), channel_id=1, source_target_pairs={{0,0},{4,8},{8,4},{12,12},{1,1},{5,9},{9,5},{13,13},{2,2},{6,10},{... | collective-permute-start | bytes 983048 | tf_op jit(solution)/shard_map/ppermute | solution.py:88
  49.0 16.7 %collective-permute-start.14 = (bf16[2304,128]{1,0:T(8,128)(2,1)}, bf16[2304,128]{1,0:T(8,128)(2,1)S(1)}, u32[]{:S(2)}, u32[]{:S(2)}) collective-permute-start(bf16[2304,128]{1,0:T(8,128)(2,1)} %get-tuple-element.24), channel_id=1, source_target_pairs={{0,0},{4,8},{8,4},{12,12},{1,1},{5,9},{9,5},{13,13},{2,2},{6,10},{... | collective-permute-start | bytes 1769480 | tf_op jit(solution)/shard_map/ppermute | solution.py:88
  55.1 17.1 %collective-permute-start.13 = (bf16[2304,128]{1,0:T(8,128)(2,1)S(1)}, bf16[2304,128]{1,0:T(8,128)(2,1)S(1)}, u32[]{:S(2)}, u32[]{:S(2)}) collective-permute-start(bf16[2304,128]{1,0:T(8,128)(2,1)S(1)} %broadcast_select_fusion.3), channel_id=1, source_target_pairs={{0,4},{4,0},{8,12},{12,8},{1,5},{5,1},{9,13},{13,9},{2,6},{6,2},{1... | collective-permute-start | bytes 1769480 | tf_op jit(solution)/shard_map/ppermute | solution.py:85
  58.0 15.2 %collective-permute-start.18 = (bf16[2304,128]{1,0:T(8,128)(2,1)}, bf16[2304,128]{1,0:T(8,128)(2,1)S(1)}, u32[]{:S(2)}, u32[]{:S(2)}) collective-permute-start(bf16[2304,128]{1,0:T(8,128)(2,1)} %slice.124), channel_id=1, source_target_pairs={{0,0},{4,8},{8,4},{12,12},{1,1},{5,9},{9,5},{13,13},{2,2},{6,10},{... | collective-permute-start | bytes 1769480 | tf_op jit(solution)/shard_map/ppermute | solution.py:88
  60.9 23.0 %collective-permute-start.5 = (bf16[2560,128]{1,0:T(8,128)(2,1)S(1)}, bf16[2560,128]{1,0:T(8,128)(2,1)S(1)}, u32[]{:S(2)}, u32[]{:S(2)}) collective-permute-start(bf16[2560,128]{1,0:T(8,128)(2,1)S(1)} %maximum_select_fusion), channel_id=1, source_target_pairs={{0,4},{4,0},{8,12},{12,8},{1,5},{5,1},{9,13},{13,9},{2,6},{6,2},{1... | collective-permute-start | bytes 1966088 | tf_op jit(solution)/shard_map/ppermute | solution.py:85
  65.6 52.8 %collective-permute-start.15 = (bf16[2304,128]{1,0:T(8,128)(2,1)}, bf16[2304,128]{1,0:T(8,128)(2,1)}, u32[]{:S(2)}, u32[]{:S(2)}) collective-permute-start(bf16[2304,128]{1,0:T(8,128)(2,1)} %collective-permute-done), channel_id=1, source_target_pairs={{0,0},{4,8},{8,4},{12,12},{1,1},{5,9},{9,5},{13,13},{2,2},{6,10},{... | collective-permute-start | bytes 1769480 | tf_op jit(solution)/shard_map/ppermute | solution.py:88
  84.8 48.8 %collective-permute-start.17 = (bf16[2304,128]{1,0:T(8,128)(2,1)}, bf16[2304,128]{1,0:T(8,128)(2,1)}, u32[]{:S(2)}, u32[]{:S(2)}) collective-permute-start(bf16[2304,128]{1,0:T(8,128)(2,1)} %broadcast_select_fusion.1), channel_id=1, source_target_pairs={{0,4},{4,0},{8,12},{12,8},{1,5},{5,1},{9,13},{13,9},{2,6},{6,2},{1... | collective-permute-start | bytes 1769480 | tf_op jit(solution)/shard_map/ppermute | solution.py:85
  97.5 18.3 %collective-permute-start.6 = (f32[2,2,32,512]{3,2,1,0:T(8,128)}, f32[2,2,32,512]{3,2,1,0:T(8,128)}, u32[]{:S(2)}, u32[]{:S(2)}) collective-permute-start(f32[2,2,32,512]{3,2,1,0:T(8,128)} %select_bitcast_fusion.5), channel_id=1, source_target_pairs={{0,1},{1,0},{2,3},{3,2},{4,5},{5,4},{6,7},{7,6},{8,9},{9,8},{10,11... | collective-permute-start | bytes 786440 | tf_op jit(solution)/shard_map/ppermute | solution.py:33
  98.3 41.5 %collective-permute-start.19 = (bf16[2304,128]{1,0:T(8,128)(2,1)}, bf16[2304,128]{1,0:T(8,128)(2,1)}, u32[]{:S(2)}, u32[]{:S(2)}) collective-permute-start(bf16[2304,128]{1,0:T(8,128)(2,1)} %slice.161), channel_id=1, source_target_pairs={{0,0},{4,8},{8,4},{12,12},{1,1},{5,9},{9,5},{13,13},{2,2},{6,10},{... | collective-permute-start | bytes 1769480 | tf_op jit(solution)/shard_map/ppermute | solution.py:88
  115.3 13.7 %collective-permute-start.8 = (f32[2,1,128,512]{3,2,0,1:T(8,128)}, f32[2,1,128,512]{3,2,0,1:T(8,128)}, u32[]{:S(2)}, u32[]{:S(2)}) collective-permute-start(f32[2,1,128,512]{3,2,0,1:T(8,128)} %select_bitcast_fusion.1), channel_id=1, source_target_pairs={{0,1},{1,0},{2,3},{3,2},{4,5},{5,4},{6,7},{7,6},{8,9},{9,8},{10,11... | collective-permute-start | bytes 1572872 | tf_op jit(solution)/shard_map/ppermute | solution.py:33
  119.4 24.2 %collective-permute-start.16 = (bf16[2304,128]{1,0:T(8,128)(2,1)}, bf16[2304,128]{1,0:T(8,128)(2,1)}, u32[]{:S(2)}, u32[]{:S(2)}) collective-permute-start(bf16[2304,128]{1,0:T(8,128)(2,1)} %broadcast_select_fusion.2), channel_id=1, source_target_pairs={{0,4},{4,0},{8,12},{12,8},{1,5},{5,1},{9,13},{13,9},{2,6},{6,2},{1... | collective-permute-start | bytes 1769480 | tf_op jit(solution)/shard_map/ppermute | solution.py:85
  122.3 24.7 %collective-permute-start.21 = (bf16[2304,128]{1,0:T(8,128)(2,1)}, bf16[2304,128]{1,0:T(8,128)(2,1)}, u32[]{:S(2)}, u32[]{:S(2)}) collective-permute-start(bf16[2304,128]{1,0:T(8,128)(2,1)} %collective-permute-done.2), channel_id=1, source_target_pairs={{0,0},{4,8},{8,4},{12,12},{1,1},{5,9},{9,5},{13,13},{2,2},{6,10},{... | collective-permute-start | bytes 1769480 | tf_op jit(solution)/shard_map/ppermute | solution.py:88
  132.1 36.5 %collective-permute-start.9 = (f32[1,128,512]{2,1,0:T(8,128)}, f32[1,128,512]{2,1,0:T(8,128)}, u32[]{:S(2)}, u32[]{:S(2)}) collective-permute-start(f32[1,128,512]{2,1,0:T(8,128)} %fusion.83), channel_id=1, source_target_pairs={{0,2},{2,0},{1,3},{3,1},{4,6},{6,4},{5,7},{7,5},{8,10},{10,8},{9,1... | collective-permute-start | bytes 786440 | tf_op jit(solution)/shard_map/ppermute | solution.py:33
  139.9 30.7 %collective-permute-start.26 = (f32[2,1,32,512]{3,2,1,0:T(8,128)}, f32[2,1,32,512]{3,2,1,0:T(8,128)}, u32[]{:S(2)}, u32[]{:S(2)}) collective-permute-start(f32[2,1,32,512]{3,2,1,0:T(8,128)} %select_bitcast_fusion.6), channel_id=1, source_target_pairs={{0,1},{1,0},{2,3},{3,2},{4,5},{5,4},{6,7},{7,6},{8,9},{9,8},{10,11... | collective-permute-start | bytes 393224 | tf_op jit(solution)/shard_map/ppermute | solution.py:33
  140.0 17.1 %collective-permute-start.20 = (bf16[2304,128]{1,0:T(8,128)(2,1)S(1)}, bf16[2304,128]{1,0:T(8,128)(2,1)S(1)}, u32[]{:S(2)}, u32[]{:S(2)}) collective-permute-start(bf16[2304,128]{1,0:T(8,128)(2,1)S(1)} %broadcast_select_fusion), channel_id=1, source_target_pairs={{0,4},{4,0},{8,12},{12,8},{1,5},{5,1},{9,13},{13,9},{2,6},{6,2},{1... | collective-permute-start | bytes 1769480 | tf_op jit(solution)/shard_map/ppermute | solution.py:85
  176.8 9.8 %collective-permute-start.11 = (bf16[2,128,512]{2,1,0:T(8,128)(2,1)S(1)}, bf16[2,128,512]{2,1,0:T(8,128)(2,1)S(1)}, u32[]{:S(2)}, u32[]{:S(2)}) collective-permute-start(bf16[2,128,512]{2,1,0:T(8,128)(2,1)S(1)} %pad_maximum_fusion.2), channel_id=1, source_target_pairs={{0,1},{1,0},{2,3},{3,2},{4,5},{5,4},{6,7},{7,6},{8,9},{9,8},{10,11... | collective-permute-start | bytes 786440 | tf_op jit(solution)/shard_map/ppermute | solution.py:33
  176.9 13.8 %collective-permute-start.27 = (f32[1,32,512]{2,1,0:T(8,128)S(1)}, f32[1,32,512]{2,1,0:T(8,128)S(1)}, u32[]{:S(2)}, u32[]{:S(2)}) collective-permute-start(f32[1,32,512]{2,1,0:T(8,128)S(1)} %select_bitcast_fusion.10), channel_id=1, source_target_pairs={{0,2},{2,0},{1,3},{3,1},{4,6},{6,4},{5,7},{7,5},{8,10},{10,8},{9,1... | collective-permute-start | bytes 196616 | tf_op jit(solution)/shard_map/ppermute | solution.py:33
  193.6 9.5 %collective-permute-start.28 = (bf16[4,32,512]{2,1,0:T(8,128)(2,1)S(1)}, bf16[4,32,512]{2,1,0:T(8,128)(2,1)S(1)}, u32[]{:S(2)}, u32[]{:S(2)}) collective-permute-start(bf16[4,32,512]{2,1,0:T(8,128)(2,1)S(1)} %get-tuple-element.45), channel_id=1, source_target_pairs={{0,8},{8,0},{4,12},{12,4},{1,9},{9,1},{5,13},{13,5},{2,10},{10,2},... | collective-permute-start | bytes 393224 | tf_op jit(solution)/shard_map/ppermute | solution.py:172
  193.7 12.1 %collective-permute-start.29 = (bf16[4,32,512]{2,1,0:T(8,128)(2,1)S(1)}, bf16[4,32,512]{2,1,0:T(8,128)(2,1)S(1)}, u32[]{:S(2)}, u32[]{:S(2)}) collective-permute-start(bf16[4,32,512]{2,1,0:T(8,128)(2,1)S(1)} %get-tuple-element.46), channel_id=1, source_target_pairs={{0,12},{12,0},{4,8},{8,4},{1,13},{13,1},{5,9},{9,5},{2,14},{14,2},... | collective-permute-start | bytes 393224 | tf_op jit(solution)/shard_map/ppermute | solution.py:174
  (44 other events, 268.7 us)

commit v3 on v2

--- a/solution.py
+++ b/solution.py
@@ -1,14 +1,17 @@
 import jax
 import jax.numpy as jnp
 from jax import lax
+from jax.experimental import pallas as pl
+from jax.experimental.pallas import tpu as pltpu
 from jax.sharding import PartitionSpec as P
 
 TILE = 128
 FEAT = ("eig", "rep")
+ALL = ("cand", "eig", "rep")
+STEPS = 3
 SIDE = ((0, 1), (1, 0), (2, 3), (3, 2))
-MIDDLE = ((0, 0), (1, 2), (2, 1), (3, 3))
-FAR = ((0, 3), (3, 0), (1, 1), (2, 2))
 TWO = ((0, 2), (2, 0), (1, 3), (3, 1))
+THREE = ((0, 3), (3, 0), (1, 2), (2, 1))
 
 damping = 0.01
 
@@ -35,14 +38,12 @@
 
 def halves(x, axis_name):
     first = lax.axis_index(axis_name) == 0
-    low, high = x[0], x[1]
+    low, high = jnp.split(x, 2)
     return jnp.where(first, low, high), jnp.where(first, high, low)
 
 
-def scatter_sum(part):
-    keep, give = halves(part.transpose(2, 1, 0, 3, 4), "rep")
-    keep = keep + swap(give, "rep")
-    keep, give = halves(keep, "eig")
+def scatter_sum(keep, give):
+    keep, give = halves(keep + swap(give, "rep"), "eig")
     return keep + swap(give, "eig")
 
 
@@ -56,25 +57,261 @@
     return whole.reshape((-1,) + x.shape[1:])
 
 
-def dot_t(basis, rows):
-    return lax.dot_general(basis, rows, (((0,), (1,)), ((), ())), preferred_element_type=jnp.float32)
-
-
-def dot_tt(basis, columns):
-    return lax.dot_general(
-        basis, columns, (((0,), (0,)), ((), ())), preferred_element_type=jnp.float32
-    )
+def split_rows(full_ref, keep_ref, give_ref, rep, columns=None):
+    rows = full_ref.shape[0] // 4
+    columns = slice(None) if columns is None else columns
+    for e in range(2):
+        here = pl.ds(e * rows, rows)
+        mine = pl.ds(pl.multiple_of((2 * e + rep) * rows, rows), rows)
+        theirs = pl.ds(pl.multiple_of((2 * e + 1 - rep) * rows, rows), rows)
+        keep_ref[here, columns] = full_ref[mine, :]
+        give_ref[here, columns] = full_ref[theirs, :]
+
+
+def feature_dots(flags, grads, segments, start=None, split=True):
+    tok = grads.shape[0]
+    cols = segments[0][0][0][0].shape[1]
+    depth = grads.shape[1] // (3 * STEPS)
+    firsts = [sum(s[3] for s in segments[:at]) for at in range(len(segments))]
+    total = sum(s[3] for s in segments)
+
+    def grads_at(i, flags_ref):
+        at = 0
+        for first, (choices, at_end, at_middle, steps, only) in zip(firsts, segments):
+            base = at_end + flags_ref[0] * 0 if at_end == at_middle else (
+                flags_ref[0] * at_end + (1 - flags_ref[0]) * at_middle
+            )
+            at = jnp.where(i >= first, base + i - first, at)
+        return (0, at)
+
+    def rows_at(first, steps, row, wanted):
+        def index(i, flags_ref):
+            step = jnp.clip(i - first, 0, steps - 1)
+            if wanted is not None:
+                step = step * (flags_ref[0] if wanted else 1 - flags_ref[0])
+            return (row + step, 0)
+
+        return index
+
+    operands, specs = [grads], [pl.BlockSpec((tok, depth), grads_at)]
+    for first, (choices, at_end, at_middle, steps, only) in zip(firsts, segments):
+        for which, (array, row) in enumerate(choices):
+            wanted = None if len(choices) == 1 else which == 0
+            operands.append(array)
+            specs.append(pl.BlockSpec((depth, cols), rows_at(first, steps, row, wanted)))
+    if start is not None:
+        operands.append(start)
+        specs.append(pl.BlockSpec((tok, cols), lambda i, flags_ref: (0, 0)))
+
+    def kernel(flags_ref, grads_ref, *refs):
+        i = pl.program_id(0)
+        end = flags_ref[0] == 1
+        inputs, rest = list(refs[: len(operands) - 1]), refs[len(operands) - 1 :]
+        if split:
+            keep_ref, give_ref, total_ref, turned_ref = rest
+        else:
+            (total_ref,) = rest
+
+        @pl.when(i == 0)
+        def begin():
+            total_ref[...] = jnp.zeros_like(total_ref) if start is None else inputs[-1][...]
+
+        at = 0
+        for first, (choices, at_end, at_middle, steps, only) in zip(firsts, segments):
+            here = inputs[at : at + len(choices)]
+            at += len(choices)
+            active = (i >= first) & (i < first + steps)
+            if only:
+                active = active & (flags_ref[0] == 0)
+
+            @pl.when(active)
+            def add(here=here):
+                shard = here[0][...]
+                if len(here) == 2:
+                    shard = jnp.where(end, shard, here[1][...])
+                total_ref[...] += jnp.dot(
+                    grads_ref[...], shard, preferred_element_type=jnp.float32
+                )
+
+        if split:
+
+            @pl.when(i == total - 1)
+            def finish():
+                turned_ref[...] = total_ref[...].T
+                split_rows(turned_ref, keep_ref, give_ref, flags_ref[1])
+
+    whole = lambda i, flags_ref: (0, 0)
+    if split:
+        out_shape = [jax.ShapeDtypeStruct((cols // 2, tok), jnp.float32)] * 2
+        out_specs = [pl.BlockSpec((cols // 2, tok), whole)] * 2
+        scratch = [pltpu.VMEM((tok, cols), jnp.float32), pltpu.VMEM((cols, tok), jnp.float32)]
+    else:
+        out_shape = jax.ShapeDtypeStruct((tok, cols), jnp.float32)
+        out_specs = pl.BlockSpec((tok, cols), whole)
+        scratch = []
+    return pl.pallas_call(
+        kernel,
+        out_shape=out_shape,
+        grid_spec=pltpu.PrefetchScalarGridSpec(
+            num_scalar_prefetch=1,
+            grid=(total,),
+            in_specs=specs,
+            out_specs=out_specs,
+            scratch_shapes=scratch,
+        ),
+        compiler_params=pltpu.CompilerParams(vmem_limit_bytes=16 << 20),
+        cost_estimate=pl.CostEstimate(
+            flops=2 * tok * cols * depth * total,
+            bytes_accessed=2 * total * depth * (tok + cols),
+            transcendentals=0,
+        ),
+    )(flags, *operands)
+
+
+def partner_dots(flags, pieces, shards, tail=None):
+    blocks = pieces[0][2]
+    cols = shards[0][0].shape[1]
+    depth = blocks // STEPS
+    count = len(pieces)
+    width = len(shards) * count * TILE
+    tok = 0 if tail is None else tail[0].shape[0]
+
+    def at(row):
+        return lambda i, flags_ref: (row + i, 0)
+
+    operands, specs = [], []
+    for array, row, _ in pieces:
+        operands.append(array)
+        specs.append(pl.BlockSpec((depth, cols), at(row)))
+    for array, row in shards:
+        operands.append(array)
+        specs.append(pl.BlockSpec((depth, cols), at(row)))
+    whole = lambda i, flags_ref: (0, 0)
+    if tail is not None:
+        operands += list(tail)
+        specs.append(pl.BlockSpec((tok, depth), lambda i, flags_ref: (0, 2 * STEPS + i)))
+        specs.append(pl.BlockSpec((depth, cols), lambda i, flags_ref: (i * flags_ref[0], 0)))
+        specs.append(pl.BlockSpec((depth, cols), lambda i, flags_ref: (i * (1 - flags_ref[0]), 0)))
+        specs.append(pl.BlockSpec((tok, cols), whole))
+
+    def kernel(flags_ref, *refs):
+        i = pl.program_id(0)
+        piece_refs, shard_refs = refs[:count], refs[count : count + len(shards)]
+        refs = refs[count + len(shards) :]
+        if tail is not None:
+            grads_ref, end_ref, middle_ref, start_ref = refs[:4]
+            refs = refs[4:]
+            keep_ref, give_ref, sums_ref, turned_ref, total_ref, wide_ref = refs
+        else:
+            keep_ref, give_ref, sums_ref, turned_ref = refs
+
+        @pl.when(i == 0)
+        def begin():
+            sums_ref[...] = jnp.zeros_like(sums_ref)
+            if tail is not None:
+                total_ref[...] = start_ref[...]
+
+        for t, piece_ref in enumerate(piece_refs):
+            tokens = jnp.concatenate(
+                [piece_ref[q * TILE : (q + 1) * TILE, :] for q in range(depth // TILE)], axis=1
+            )
+            for j, shard_ref in enumerate(shard_refs):
+                sums_ref[j * count + t] += jnp.dot(
+                    tokens, shard_ref[...], preferred_element_type=jnp.float32
+                )
+        if tail is not None:
+            shard = jnp.where(flags_ref[0] == 1, end_ref[...], middle_ref[...])
+            total_ref[...] += jnp.dot(grads_ref[...], shard, preferred_element_type=jnp.float32)
+
+        @pl.when(i == STEPS - 1)
+        def finish():
+            if tail is not None:
+                wide_ref[...] = total_ref[...].T
+                split_rows(wide_ref, keep_ref, give_ref, flags_ref[1], pl.ds(0, tok))
+            for at_block in range(len(shards) * count):
+                turned_ref[...] = sums_ref[at_block].T
+                columns = pl.ds(tok + at_block * TILE, TILE)
+                split_rows(turned_ref, keep_ref, give_ref, flags_ref[1], columns)
+
+    scratch = [
+        pltpu.VMEM((len(shards) * count, TILE, cols), jnp.float32),
+        pltpu.VMEM((cols, TILE), jnp.float32),
+    ]
+    if tail is not None:
+        scratch += [pltpu.VMEM((tok, cols), jnp.float32), pltpu.VMEM((cols, tok), jnp.float32)]
+    return pl.pallas_call(
+        kernel,
+        out_shape=[jax.ShapeDtypeStruct((cols // 2, tok + width), jnp.float32)] * 2,
+        grid_spec=pltpu.PrefetchScalarGridSpec(
+            num_scalar_prefetch=1,
+            grid=(STEPS,),
+            in_specs=specs,
+            out_specs=[pl.BlockSpec((cols // 2, tok + width), whole)] * 2,
+            scratch_shapes=scratch,
+        ),
+        compiler_params=pltpu.CompilerParams(vmem_limit_bytes=16 << 20),
+        cost_estimate=pl.CostEstimate(
+            flops=2 * blocks * cols * (width + tok),
+            bytes_accessed=2 * blocks * (cols * (count + len(shards)) + tok),
+            transcendentals=0,
+        ),
+    )(flags, *operands)
+
+
+def input_dots(flags, acts, shards):
+    tok, depth = acts.shape
+    cols = shards[0][0][0].shape[1]
+    operands, specs = [acts], [pl.BlockSpec((tok, depth), lambda i, flags_ref: (0, 0))]
+    for choices in shards:
+        for array, row in choices:
+            operands.append(array)
+            specs.append(pl.BlockSpec((depth, cols), lambda i, flags_ref, row=row: (row, 0)))
+
+    def kernel(flags_ref, acts_ref, *refs):
+        i = pl.program_id(0)
+        inputs = list(refs[: len(operands) - 1])
+        keep_ref, give_ref, part_ref = refs[len(operands) - 1 :]
+        at = 0
+        for slot, choices in enumerate(shards):
+            here = inputs[at : at + len(choices)]
+            at += len(choices)
+
+            @pl.when(i == slot)
+            def add(here=here):
+                shard = here[0][...]
+                if len(here) == 2:
+                    shard = jnp.where(flags_ref[0] == 1, shard, here[1][...])
+                part_ref[...] = jnp.dot(acts_ref[...], shard, preferred_element_type=jnp.float32)
+
+        split_rows(part_ref, keep_ref, give_ref, flags_ref[1])
+
+    place = pl.BlockSpec((tok // 2, cols), lambda i, flags_ref: (0, flags_ref[2 + i]))
+    return pl.pallas_call(
+        kernel,
+        out_shape=[jax.ShapeDtypeStruct((tok // 2, cols * len(shards)), jnp.float32)] * 2,
+        grid_spec=pltpu.PrefetchScalarGridSpec(
+            num_scalar_prefetch=1,
+            grid=(len(shards),),
+            in_specs=specs,
+            out_specs=[place, place],
+            scratch_shapes=[pltpu.VMEM((tok, cols), jnp.float32)],
+        ),
+        compiler_params=pltpu.CompilerParams(vmem_limit_bytes=16 << 20),
+        cost_estimate=pl.CostEstimate(
+            flops=2 * tok * depth * cols * len(shards),
+            bytes_accessed=2 * depth * (tok + 7 * cols) + 4 * tok * cols * len(shards),
+            transcendentals=0,
+        ),
+    )(flags, *operands)
 
 
 def line_plan(acts, grads, basis_in, basis_out, eigval, test_grads, pair_tiles, last_rows):
     plane = lax.axis_index("cand")
     end = (plane == 0) | (plane == 3)
-    eig, rep = lax.axis_size("eig"), lax.axis_size("rep")
     tok_rows = acts.shape[0]
     cols = basis_in.shape[1]
-    width_in = 4 * cols
     tiles_here = tok_rows // TILE
-    slim = cols // (eig * rep)
+    slim = cols // 4
     depth = basis_out.shape[0] // 3
     rows_in = basis_in.shape[0]
 
@@ -84,66 +321,78 @@
     def side(at_end, at_middle):
         return lax.ppermute(pick(at_end, at_middle), "cand", SIDE)
 
+    among = []
+    for at in range(16):
+        mid = 4 <= at < 12
+        among.append((at, (12 - at + 2 * (at % 4)) if mid else at ^ 1))
+
     def middle(x):
-        return lax.ppermute(x, "cand", MIDDLE)
-
-    own = [basis_out[i * depth : (i + 1) * depth] for i in range(3)]
-    grad = [grads[:, i * depth : (i + 1) * depth] for i in range(3)]
-    quarter = tok_rows // 4
-    turned = [grad[0][i * quarter : (i + 1) * quarter].T for i in range(4)]
-
+        return lax.ppermute(x, ALL, among)
+
+    at_b = jnp.where(end, plane ^ 2, plane ^ 3)
+    at_c = jnp.where(end, plane ^ 3, plane ^ 2)
+    rep = lax.axis_index("rep")
+    flags = jnp.stack([end.astype(jnp.int32), rep, plane, plane ^ 1, at_b, at_c])
+
+    rows = lax.dynamic_slice_in_dim(basis_out, jnp.where(end, 0, depth), 2 * depth, 0)
     s0 = lax.ppermute(basis_in, "cand", SIDE)
     m0 = middle(basis_in)
-    s1 = lax.ppermute(own[1], "cand", SIDE)
+    s12 = lax.ppermute(rows, "cand", SIDE)
+    late_rows = basis_out[depth:]
+    m23 = middle(late_rows)
+    started = after(flags, rows, late_rows)
     m1 = middle(after(s0, m0))
-    s2 = side(after(own[0], s0), own[2])
-    m2 = middle(after(own[1], m0))
-    s3 = side(after(basis_out[3 * depth - 2 * rows_in :], s1), jnp.concatenate([m0, m1]))
-    m3 = middle(after(own[2], m1))
-    s4 = side(after(turned[0], s2), m2)
-    m4 = middle(after(own[0], m2))
-    s5 = side(after(turned[1], s3), m3)
-    m5 = middle(after(s1, m3))
-    s6 = side(after(turned[2], s4), m5)
-    m6 = middle(after(s3[2 * rows_in - depth :], m4))
-    s7 = side(after(turned[3], s5), m6)
-    m7 = middle(after(s2, m5))
-
-    in_b, in_c = pick(s3[:rows_in], m0), pick(s3[rows_in:], m1)
-    at_b = jnp.where(end, plane ^ 2, plane ^ 3)
-    at_c = jnp.where(end, plane ^ 3, plane ^ 2)
-    part_in = jnp.zeros((tok_rows, width_in), jnp.float32)
-    for shard, at in ((basis_in, plane), (s0, plane ^ 1), (in_b, at_b), (in_c, at_c)):
-        part = jnp.dot(acts, shard, preferred_element_type=jnp.float32)
-        part_in = lax.dynamic_update_slice_in_dim(part_in, part, at * cols, 1)
-    part_in = part_in.reshape(1, eig, rep, tok_rows // (eig * rep), width_in)
-    rot_in = gather_rows(scatter_sum(part_in)[0].astype(jnp.bfloat16))
-    rot_in = rot_in.reshape(tiles_here, TILE, width_in)
-
-    only_middle = jnp.where(end, 0.0, 1.0)
-
-    def blocks(*parts):
-        return jnp.stack([part.reshape(eig, rep, slim, part.shape[1]) for part in parts])
-
-    part_own = dot_t(basis_out, grads)
-    part_a = dot_t(s1, grad[1]) + dot_t(pick(s2, s3[2 * rows_in - depth :]), grad[2])
-    part_a = part_a + only_middle * dot_t(s2, grad[0])
-    sum_own, sum_a = scatter_sum(blocks(part_own, part_a))
-
-    part_b = dot_t(pick(s4, m2), grad[1]) + dot_t(pick(s5, m3), grad[2])
-    part_b = part_b + only_middle * dot_t(m4, grad[0])
-    sum_b = scatter_sum(blocks(part_b))[0]
-
-    part_c = dot_t(pick(s6, m5), grad[1]) + dot_t(pick(s7, m6), grad[2])
-    part_c = part_c + only_middle * dot_t(m7, grad[0])
-    theirs = [
-        jnp.concatenate([dot_tt(shard, tokens) for tokens in (s4, s5, s6, s7)], axis=1)
-        for shard in (own[0], m4, m7)
+    stacked = grads[:, :depth].reshape(tiles_here, TILE, depth // TILE, TILE)
+    stacked = after(stacked, s0).transpose(0, 2, 1, 3).reshape(tiles_here * depth, TILE)
+    third = jnp.concatenate([basis_out[2 * depth :], basis_out[: 2 * rows_in - depth]])
+    s3 = side(third, jnp.concatenate([m0, m1]))
+    m5 = middle(s12[depth:])
+    s45 = side(stacked[: 2 * depth], after(m23, s12))
+    m6 = middle(s3[:depth])
+    m47 = middle(after(jnp.concatenate([basis_out[:depth], s12[:depth]]), m5))
+    s6 = side(after(stacked[2 * depth : 3 * depth], s3), m5)
+    s7 = side(after(stacked[3 * depth :], s45), m6)
+
+    early = after(flags, s3)
+    keep, give = input_dots(
+        early, acts, [[(basis_in, 0)], [(s0, 0)], [(s3, 0), (m0, 0)], [(s3, 1), (m1, 0)]]
+    )
+    rot_in = gather_rows(scatter_sum(keep, give).astype(jnp.bfloat16))
+    rot_in = rot_in.reshape(tiles_here, TILE, 4 * cols)
+
+    sum_own = scatter_sum(
+        *feature_dots(started, grads, [([(basis_out, 0)], 0, 0, 3 * STEPS, False)])
+    )
+    sum_a = scatter_sum(
+        *feature_dots(
+            flags,
+            grads,
+            [
+                ([(s12, 0)], STEPS, 0, 2 * STEPS, False),
+                ([(s3, 0)], 2 * STEPS, 2 * STEPS, STEPS, True),
+            ],
+        )
+    )
+    part_b = feature_dots(
+        flags, grads, [([(s45, 0), (m23, 0)], STEPS, STEPS, 2 * STEPS, False),
+                       ([(m47, 0)], 0, 0, STEPS, True)]
+    )
+    sum_b = scatter_sum(*part_b)
+    part_c = feature_dots(
+        flags, grads, [([(s6, 0), (m5, 0)], STEPS, STEPS, STEPS, False),
+                       ([(m47, STEPS)], 0, 0, STEPS, True)], split=False
+    )
+    shards = [(basis_out, 0), (m47, 0), (m47, STEPS)]
+    first = partner_dots(flags, [(s45, 0, depth), (s45, STEPS, depth), (s6, 0, depth)], shards)
+    sum_first = scatter_sum(*first)
+    last = partner_dots(flags, [(s7, 0, depth)], shards, (grads, s7, m6, part_c))
+    sum_last = scatter_sum(*last)
+    sum_c, sum_last = sum_last[:, :tok_rows], sum_last[:, tok_rows:]
+    back = [
+        jnp.where(end, lax.ppermute(x, "cand", SIDE), 0.0).reshape(slim, 3, -1)
+        for x in (sum_first, sum_last)
     ]
-    sums = scatter_sum(blocks(part_c, *theirs))
-    sum_c = sums[0]
-    back = lax.ppermute(sums[1:], "cand", SIDE)
-    back = jnp.where(end, back, 0.0)
+    back = jnp.concatenate(back, axis=2)
 
     rowmask, ignored = tile_layout(pair_tiles, last_rows, plane * tiles_here, tiles_here, TILE)
     keep = rowmask.reshape(1, tok_rows).astype(jnp.bfloat16)
@@ -164,15 +413,13 @@
         )
         return jnp.sum(jnp.where(onehot[:, :, None], scores[:, None, :], 0.0), axis=0)
 
-    prods_a = tile_prods(sum_a + back[0])
-    prods_b = tile_prods(sum_b + back[1])
-    prods_c = tile_prods(sum_c + back[2])
+    prods_a = tile_prods(sum_a + back[:, 0])
+    prods_b = tile_prods(sum_b + back[:, 1])
+    prods_c = tile_prods(sum_c + back[:, 2])
     total = pair_scores(tile_prods(sum_own), plane)
     total = total + pair_scores(lax.ppermute(prods_a, "cand", SIDE), plane ^ 1)
     total = total + pair_scores(lax.ppermute(pick(prods_b, prods_c), "cand", TWO), plane ^ 2)
-    three = [(0, 3), (3, 0), (1, 2), (2, 1)]
-    total = total + pair_scores(lax.ppermute(pick(prods_c, prods_b), "cand", three), plane ^ 3)
-
+    total = total + pair_scores(lax.ppermute(pick(prods_c, prods_b), "cand", THREE), plane ^ 3)
     return final_sum(total)
 
 
@@ -180,9 +427,8 @@
     npairs, ntest = total.shape
     mine = total.reshape(npairs, 2, 2, ntest // 4).transpose(2, 1, 0, 3)
     keep, give = halves(mine, "rep")
-    keep = keep + swap(give, "rep")
-    keep, give = halves(keep, "eig")
-    keep = keep + swap(give, "eig")
+    keep, give = halves((keep + swap(give, "rep"))[0], "eig")
+    keep = (keep + swap(give, "eig"))[0]
     plane = lax.axis_index("cand")
     rows = npairs // 4
     result = lax.dynamic_slice_in_dim(keep, plane * rows, rows, 0)

time: 224 us -> 194 us (0.87)
  matrix products: 68.8 us -> 10.7 us
  Pallas kernels: 0 us -> 27 us
  waiting for transfers between devices: 38.3 us -> 53 us
  other arithmetic: 23.7 us -> 10.2 us
  local copies, waits for them, and re-layouts: 22.7 us -> 34.1 us
  starting transfers between devices: 66.9 us -> 57.6 us
    dot_general x26 -> x0, matrix products: 57.9 us -> none  [the longest x10 32.3 us: dot_t(): lax.dot_general(basis, rows, (((0,), (1,)), ((), ())), preferred_element_...]
    pallas_call x0 -> x7, Pallas kernels: none -> 27 us  [the longest x4 17.7 us: feature_dots(): pl.pallas_call(kernel, out_shape=out_shape, grid_spec=pltpu.PrefetchScala...]
    slice x6 -> x14, local copies, waits for them, and re-layouts: 5.03 us -> 22.9 us  [the longest x2 7.77 us: line_plan(): s7 = side(after(stacked[3 * depth:], s45), m6)]
    ppermute x11 -> x10, starting transfers between devices: 39.4 us -> 27.2 us  [the longest x2 20.5 us: line_plan(): lax.ppermute(x, 'cand', SIDE)]
    ppermute x6 -> x4, waiting for transfers between devices: 11.9 us -> 22.5 us  [side(): return lax.ppermute(pick(at_end, at_middle), 'cand', SIDE)]
    unnamed x69 -> x35, local copies, waits for them, and re-layouts: 9.24 us -> 3.34 us
    select_n x9 -> x8, other arithmetic: 4.45 us -> 0.12 us  [halves(): return (jnp.where(first, low, high), jnp.where(first, high, low))]
    reshape x0 -> x1, local copies, waits for them, and re-layouts: none -> 4.18 us  [line_plan(): stacked = grads[:, :depth].reshape(tiles_here, TILE, depth // TILE, TILE)]
  transfers between devices with their start and end apart: 35 -> 36, of which waited for: 12 -> 15; matrix products, arithmetic and copies ran while one was open for 49% -> 24% of each run, Pallas kernels for 0% -> 14%
where the time goes in v3:
time: 194 us; the launch traced here: 193 us
  starting transfers between devices  57.6 us (30%)
  waiting for transfers between devices  53 us (27%)
  local copies, waits for them, and re-layouts  34.1 us (18%)
  Pallas kernels  27 us (14%)
  matrix products  10.7 us (6%)
  other arithmetic  10.2 us (5%)
    ppermute x4, waiting for transfers between devices, side(): return lax.ppermute(pick(at_end, at_middle), 'cand', SIDE)  22.5 us
    ppermute x16, waiting for transfers between devices, swap(): return lax.ppermute(x, axis_name, [(0, 1), (1, 0)])  21 us
    ppermute x2, starting transfers between devices, line_plan(): lax.ppermute(x, 'cand', SIDE)  20.5 us
    pallas_call x4, Pallas kernels, feature_dots(): pl.pallas_call(kernel, out_shape=out_shape, grid_spec=pltpu.PrefetchScala...  17.7 us
    ppermute x4, starting transfers between devices, side(): return lax.ppermute(pick(at_end, at_middle), 'cand', SIDE)  12.6 us
    dot_general x4, matrix products, pair_scores(): jnp.einsum('tea,jea->tj', prods, precond, preferred_element_type=jnp.floa...  9.87 us
    ppermute x16, starting transfers between devices, swap(): return lax.ppermute(x, axis_name, [(0, 1), (1, 0)])  8.15 us
    slice x2, local copies, waits for them, and re-layouts, line_plan(): s7 = side(after(stacked[3 * depth:], s45), m6)  7.77 us
  transfers between devices with their start and end apart: 36, of which 15 were waited for; matrix products, arithmetic and copies ran while one was open for 24% of the time, Pallas kernels for 14%

profile of v3, /device:TPU:0, one launch (start us, length us, event | category | flops | bytes accessed | tf_op | source)
XLA Modules:
  0.0 193.2 jit_solution(8487300365395232392)
XLA Ops:
  0.0 3.0 %collective-permute-start.3 = (bf16[1280,128]{1,0:T(8,128)(2,1)}, bf16[1280,128]{1,0:T(8,128)(2,1)}, u32[]{:S(2)}, u32[]{:S(2)}) collective-permute-start(bf16[1280,128]{1,0:T(8,128)(2,1)} %refs_0_.3), channel_id=1, source_target_pairs={{0,4},{4,0},{8,12},{12,8},{1,5},{5,1},{9,13},{13,9},{2,6},{6,2},{1... | collective-permute-start | bytes 983048 | tf_op jit(solution)/shard_map/ppermute | solution.py:338
  3.0 3.4 %constant_dynamic-slice_fusion.4 = (bf16[4608,128]{1,0:T(8,128)(2,1)}, bf16[4608,128]{1,0:T(8,128)(2,1)}) fusion(bf16[6912,128]{1,0:T(8,128)(2,1)} %refs_1_.1, s32[]{:T(128)S(6)} %select_n.245), kind=kLoop, calls=%fused_computation.101 | loop fusion | bytes 4718596 | tf_op jit(solution)/shard_map/dynamic_slice | solution.py:337
  6.4 3.3 %collective-permute-start.10 = (bf16[4608,128]{1,0:T(8,128)(2,1)}, bf16[4608,128]{1,0:T(8,128)(2,1)}, u32[]{:S(2)}, u32[]{:S(2)}) collective-permute-start(bf16[4608,128]{1,0:T(8,128)(2,1)} %get-tuple-element.54), channel_id=1, source_target_pairs={{0,4},{4,0},{8,12},{12,8},{1,5},{5,1},{9,13},{13,9},{2,6},{6,2},{1... | collective-permute-start | bytes 3538952 | tf_op jit(solution)/shard_map/ppermute | solution.py:340
  9.8 3.0 %copy-done = bf16[512,6912]{1,0:T(8,128)(2,1)S(1)} copy-done((bf16[512,6912]{1,0:T(8,128)(2,1)S(1)}, bf16[512,6912]{1,0:T(8,128)(2,1)}, u32[]{:S(2)}) %copy-start) | copy-done | bytes 7077912
  12.8 4.8 %shard_map.82 = (f32[64,512]{1,0:T(8,128)S(1)}, f32[64,512]{1,0:T(8,128)S(1)}) custom-call(s32[6]{0:T(128)S(1)} %stack.49.flags_ref, bf16[512,6912]{1,0:T(8,128)(2,1)S(1)} %copy-done, bf16[6912,128]{1,0:T(8,128)(2,1)S(1)} %copy-done.1), custom_call_target="tpu_custom_call" | custom-call | flops 905969664 | bytes 8847360 | tf_op jit(solution)/shard_map/pallas_call | solution.py:152
  20.6 3.6 %divide_convert_fusion = bf16[64,32,512]{2,1,0:T(8,128)(2,1)} fusion(bf16[64,32,512]{2,1,0:T(8,128)(2,1)} %param.13, f32[32,512]{1,0:T(8,128)S(1)} %broadcast_add_fusion), kind=kLoop, calls=%fused_computation | loop fusion | flops 3145728 | bytes 4259840 | tf_op jit(solution)/shard_map/convert_element_type | solution.py:399
  29.0 4.2 %reshape.243 = bf16[4,128,18,128]{1,0,3,2:T(4,128)(2,1)S(1)} reshape(bf16[512,2304]{0,1:T(8,128)(2,1)} %copy.37) | data formatting | bytes 4718592 | tf_op jit(solution)/shard_map/reshape | solution.py:345
  34.8 4.0 %fusion.56 = (bf16[1,18,128,128]{2,0,3,1:T(2,128)(2,1)}, bf16[1,18,128,128]{2,0,3,1:T(2,128)(2,1)}) fusion(bf16[4,18,128,128]{2,0,3,1:T(4,128)(2,1)S(1)} %bitcast.117), kind=kLoop, calls=%fused_computation.114 | loop fusion | bytes 2359296 | tf_op jit(solution)/shard_map/slice | solution.py:354
  40.8 4.3 %copy.38 = bf16[2,18,128,128]{3,2,1,0:T(8,128)(2,1)} copy(bf16[2,18,128,128]{2,0,3,1:T(2,128)(2,1)} %slice.78) | data formatting | bytes 2359296 | tf_op jit(solution)/shard_map/slice | solution.py:350
  47.4 3.7 %copy.40 = bf16[1,18,128,128]{3,2,1,0:T(8,128)(2,1)} copy(bf16[1,18,128,128]{2,0,3,1:T(2,128)(2,1)} %get-tuple-element.50) | data formatting | bytes 1179648 | tf_op jit(solution)/shard_map/slice | solution.py:354
  56.8 13.4 %collective-permute-done.5.refs_2_.refs_4_.refs_1_ = bf16[2560,128]{1,0:T(8,128)(2,1)S(1)} collective-permute-done((bf16[2560,128]{1,0:T(8,128)(2,1)S(1)}, bf16[2560,128]{1,0:T(8,128)(2,1)S(1)}, u32[]{:S(2)}, u32[]{:S(2)}) %collective-permute-start.5) | collective-permute-done | bytes 655392 | tf_op jit(solution)/shard_map/ppermute | solution.py:322
  70.2 4.0 %shard_map.83 = (f32[256,512]{1,0:T(8,128)S(1)}, f32[256,512]{1,0:T(8,128)S(1)}) custom-call(s32[6]{0:T(128)S(1)} %stack.49.flags_ref, bf16[512,1280]{1,0:T(8,128)(2,1)S(1)} %copy-done.3, bf16[1280,128]{1,0:T(8,128)(2,1)S(1)} %copy-done.4, bf16[1280,128]{1,0:T(8,128)(2,1)} %collective-permute-done.3.refs_1_, ...), custom_call_target="tpu_custom_call" | custom-call | flops 671088640 | bytes 4653056 | tf_op jit(solution)/shard_map/pallas_call | solution.py:289
  76.2 5.7 %shard_map.84 = (f32[64,512]{1,0:T(8,128)S(1)}, f32[64,512]{1,0:T(8,128)S(1)}) custom-call(s32[6]{0:T(128)S(1)} %stack.49.flags_ref, bf16[512,6912]{1,0:T(8,128)(2,1)S(1)} %bitcast.116, bf16[4608,128]{1,0:T(8,128)(2,1)} %collective-permute-done.10.refs_0_, bf16[2560,128]{1,0:T(8,128)(2,1)S(1)} %collective-permute-done.5.refs_2_.refs_4_.refs_1_), custom_call_target="tpu_custom_call" | custom-call | flops 905969664 | bytes 8847360 | tf_op jit(solution)/shard_map/pallas_call | solution.py:152
  84.0 7.0 %collective-permute-done.7 = f32[128,512]{1,0:T(8,128)S(1)} collective-permute-done((f32[128,512]{1,0:T(8,128)S(1)}, f32[128,512]{1,0:T(8,128)S(1)}, u32[]{:S(2)}, u32[]{:S(2)}) %collective-permute-start.7) | collective-permute-done | bytes 262176 | tf_op jit(solution)/shard_map/ppermute | solution.py:36
  91.6 4.5 %collective-permute-done.8 = bf16[128,512]{1,0:T(8,128)(2,1)S(1)} collective-permute-done((bf16[128,512]{1,0:T(8,128)(2,1)S(1)}, bf16[128,512]{1,0:T(8,128)(2,1)S(1)}, u32[]{:S(2)}, u32[]{:S(2)}) %collective-permute-start.8) | collective-permute-done | bytes 131104 | tf_op jit(solution)/shard_map/ppermute | solution.py:36
  99.1 7.1 %collective-permute-start.22 = (bf16[2304,128]{1,0:T(8,128)(2,1)S(1)}, bf16[2304,128]{1,0:T(8,128)(2,1)S(1)}, u32[]{:S(2)}, u32[]{:S(2)}) collective-permute-start(bf16[2304,128]{1,0:T(8,128)(2,1)S(1)} %broadcast_select_fusion), channel_id=1, source_target_pairs={{0,4},{4,0},{8,12},{12,8},{1,5},{5,1},{9,13},{13,9},{2,6},{6,2},{1... | collective-permute-start | bytes 1769480 | tf_op jit(solution)/shard_map/ppermute | solution.py:322
  106.9 4.8 %shard_map.88 = (f32[64,512]{1,0:T(8,128)S(1)}, f32[64,512]{1,0:T(8,128)S(1)}) custom-call(s32[6]{0:T(128)S(1)} %stack.49.flags_ref, bf16[512,6912]{1,0:T(8,128)(2,1)S(1)} %bitcast.116, bf16[4608,128]{1,0:T(8,128)(2,1)S(1)} %collective-permute-done.14.refs_0_.refs_1_, bf16[4608,128]{1,0:T(8,128)(2,1)} %collective-permute-done.13.refs_1_, ...), custom_call_target="tpu_custom_call" | custom-call | flops 905969664 | bytes 8847360 | tf_op jit(solution)/shard_map/pallas_call | solution.py:152
  115.6 7.8 %collective-permute-done.22.refs_0_.refs_5_ = bf16[2304,128]{1,0:T(8,128)(2,1)S(1)} collective-permute-done((bf16[2304,128]{1,0:T(8,128)(2,1)S(1)}, bf16[2304,128]{1,0:T(8,128)(2,1)S(1)}, u32[]{:S(2)}, u32[]{:S(2)}) %collective-permute-start.22) | collective-permute-done | bytes 589856 | tf_op jit(solution)/shard_map/ppermute | solution.py:322
  126.0 2.8 %shard_map.85 = (f32[64,1152]{1,0:T(8,128)S(1)}, f32[64,1152]{1,0:T(8,128)S(1)}) custom-call(s32[6]{0:T(128)S(1)} %stack.49.flags_ref, bf16[4608,128]{1,0:T(8,128)(2,1)S(1)} %collective-permute-done.14.refs_0_.refs_1_, bf16[4608,128]{1,0:T(8,128)(2,1)S(1)} %collective-permute-done.14.refs_0_.refs_1_, ...), custom_call_target="tpu_custom_call" | custom-call | flops 679477248 | bytes 3538944 | tf_op jit(solution)/shard_map/pallas_call | solution.py:242
  132.7 4.6 %collective-permute-done.19 = f32[32,1152]{1,0:T(8,128)S(1)} collective-permute-done((f32[32,1152]{1,0:T(8,128)S(1)}, f32[32,1152]{1,0:T(8,128)S(1)}, u32[]{:S(2)}, u32[]{:S(2)}) %collective-permute-start.19) | collective-permute-done | bytes 147488 | tf_op jit(solution)/shard_map/ppermute | solution.py:36
  137.3 18.6 %collective-permute-start.20 = (f32[32,1152]{1,0:T(8,128)S(1)}, f32[32,1152]{1,0:T(8,128)S(1)}, u32[]{:S(2)}, u32[]{:S(2)}) collective-permute-start(f32[32,1152]{1,0:T(8,128)S(1)} %select_add_fusion), channel_id=1, source_target_pairs={{0,4},{4,0},{8,12},{12,8},{1,5},{5,1},{9,13},{13,9},{2,6},{6,2},{1... | collective-permute-start | bytes 442376 | tf_op jit(solution)/shard_map/ppermute | solution.py:392
  170.6 4.3 %collective-permute-done.29 = bf16[4,32,512]{2,1,0:T(8,128)(2,1)S(1)} collective-permute-done((bf16[4,32,512]{2,1,0:T(8,128)(2,1)S(1)}, bf16[4,32,512]{2,1,0:T(8,128)(2,1)S(1)}, u32[]{:S(2)}, u32[]{:S(2)}) %collective-permute-start.29) | collective-permute-done | bytes 131104 | tf_op jit(solution)/shard_map/ppermute | solution.py:421
  182.0 3.2 %collective-permute-done.32 = f32[1,8,16]{2,1,0:T(8,128)S(1)} collective-permute-done((f32[1,8,16]{2,1,0:T(8,128)S(1)}, f32[1,8,16]{2,1,0:T(8,128)S(1)}, u32[]{:S(2)}, u32[]{:S(2)}) %collective-permute-start.32) | collective-permute-done | bytes 544 | tf_op jit(solution)/shard_map/ppermute | solution.py:36
  189.8 2.8 %collective-permute-done.35 = f32[2,16]{1,0:T(2,128)S(1)} collective-permute-done((f32[2,16]{1,0:T(2,128)S(1)}, f32[2,16]{1,0:T(2,128)S(1)}, u32[]{:S(2)}, u32[]{:S(2)}) %collective-permute-start.35) | collective-permute-done | bytes 160 | tf_op jit(solution)/shard_map/ppermute | solution.py:437
  (170 shorter events, 64.9 us)
Async XLA Ops:
  0.0 34.8 %collective-permute-start.3 = (bf16[1280,128]{1,0:T(8,128)(2,1)}, bf16[1280,128]{1,0:T(8,128)(2,1)}, u32[]{:S(2)}, u32[]{:S(2)}) collective-permute-start(bf16[1280,128]{1,0:T(8,128)(2,1)} %refs_0_.3), channel_id=1, source_target_pairs={{0,4},{4,0},{8,12},{12,8},{1,5},{5,1},{9,13},{13,9},{2,6},{6,2},{1... | collective-permute-start | bytes 983048 | tf_op jit(solution)/shard_map/ppermute | solution.py:338
  3.0 31.8 %collective-permute-start.2 = (bf16[1280,128]{1,0:T(8,128)(2,1)}, bf16[1280,128]{1,0:T(8,128)(2,1)S(1)}, u32[]{:S(2)}, u32[]{:S(2)}) collective-permute-start(bf16[1280,128]{1,0:T(8,128)(2,1)} %refs_0_.3), channel_id=1, source_target_pairs={{0,1},{1,0},{2,3},{3,2},{4,8},{5,9},{6,10},{7,11},{8,4},{9,5},{10,... | collective-permute-start | bytes 983048 | tf_op jit(solution)/shard_map/ppermute | solution.py:330
  6.4 47.8 %collective-permute-start.10 = (bf16[4608,128]{1,0:T(8,128)(2,1)}, bf16[4608,128]{1,0:T(8,128)(2,1)}, u32[]{:S(2)}, u32[]{:S(2)}) collective-permute-start(bf16[4608,128]{1,0:T(8,128)(2,1)} %get-tuple-element.54), channel_id=1, source_target_pairs={{0,4},{4,0},{8,12},{12,8},{1,5},{5,1},{9,13},{13,9},{2,6},{6,2},{1... | collective-permute-start | bytes 3538952 | tf_op jit(solution)/shard_map/ppermute | solution.py:340
  9.7 44.5 %collective-permute-start.13 = (bf16[4608,128]{1,0:T(8,128)(2,1)}, bf16[4608,128]{1,0:T(8,128)(2,1)}, u32[]{:S(2)}, u32[]{:S(2)}) collective-permute-start(bf16[4608,128]{1,0:T(8,128)(2,1)} %get-tuple-element.55), channel_id=1, source_target_pairs={{0,1},{1,0},{2,3},{3,2},{4,8},{5,9},{6,10},{7,11},{8,4},{9,5},{10,... | collective-permute-start | bytes 3538952 | tf_op jit(solution)/shard_map/ppermute | solution.py:330
  17.6 15.6 %collective-permute-start = (f32[64,512]{1,0:T(8,128)S(1)}, f32[64,512]{1,0:T(8,128)S(1)}, u32[]{:S(2)}, u32[]{:S(2)}) collective-permute-start(f32[64,512]{1,0:T(8,128)S(1)} %get-tuple-element.27), channel_id=1, source_target_pairs={{0,1},{1,0},{2,3},{3,2},{4,5},{5,4},{6,7},{7,6},{8,9},{9,8},{10,11... | collective-permute-start | bytes 393224 | tf_op jit(solution)/shard_map/ppermute | solution.py:36
  33.2 126.9 %collective-permute-start.1 = (f32[32,512]{1,0:T(8,128)S(1)}, f32[32,512]{1,0:T(8,128)S(1)}, u32[]{:S(2)}, u32[]{:S(2)}) collective-permute-start(f32[32,512]{1,0:T(8,128)S(1)} %slice_select_fusion.5), channel_id=1, source_target_pairs={{0,2},{2,0},{1,3},{3,1},{4,6},{6,4},{5,7},{7,5},{8,10},{10,8},{9,1... | collective-permute-start | bytes 196616 | tf_op jit(solution)/shard_map/ppermute | solution.py:36
  34.8 16.3 %collective-permute-start.4 = (bf16[1280,128]{1,0:T(8,128)(2,1)}, bf16[1280,128]{1,0:T(8,128)(2,1)}, u32[]{:S(2)}, u32[]{:S(2)}) collective-permute-start(bf16[1280,128]{1,0:T(8,128)(2,1)} %collective-permute-done.3.refs_1_), channel_id=1, source_target_pairs={{0,1},{1,0},{2,3},{3,2},{4,8},{5,9},{6,10},{7,11},{8,4},{9,5},{10,... | collective-permute-start | bytes 983048 | tf_op jit(solution)/shard_map/ppermute | solution.py:330
  52.6 17.6 %collective-permute-start.5 = (bf16[2560,128]{1,0:T(8,128)(2,1)S(1)}, bf16[2560,128]{1,0:T(8,128)(2,1)S(1)}, u32[]{:S(2)}, u32[]{:S(2)}) collective-permute-start(bf16[2560,128]{1,0:T(8,128)(2,1)S(1)} %maximum_select_fusion), channel_id=1, source_target_pairs={{0,4},{4,0},{8,12},{12,8},{1,5},{5,1},{9,13},{13,9},{2,6},{6,2},{1... | collective-permute-start | bytes 1966088 | tf_op jit(solution)/shard_map/ppermute | solution.py:322
  55.6 43.3 %collective-permute-start.14 = (bf16[4608,128]{1,0:T(8,128)(2,1)S(1)}, bf16[4608,128]{1,0:T(8,128)(2,1)S(1)}, u32[]{:S(2)}, u32[]{:S(2)}) collective-permute-start(bf16[4608,128]{1,0:T(8,128)(2,1)S(1)} %bitcast_select_fusion), channel_id=1, source_target_pairs={{0,4},{4,0},{8,12},{12,8},{1,5},{5,1},{9,13},{13,9},{2,6},{6,2},{1... | collective-permute-start | bytes 3538952 | tf_op jit(solution)/shard_map/ppermute | solution.py:322
  74.3 7.8 %collective-permute-start.6 = (f32[256,512]{1,0:T(8,128)S(1)}, f32[256,512]{1,0:T(8,128)S(1)}, u32[]{:S(2)}, u32[]{:S(2)}) collective-permute-start(f32[256,512]{1,0:T(8,128)S(1)} %get-tuple-element.31), channel_id=1, source_target_pairs={{0,1},{1,0},{2,3},{3,2},{4,5},{5,4},{6,7},{7,6},{8,9},{9,8},{10,11... | collective-permute-start | bytes 1572872 | tf_op jit(solution)/shard_map/ppermute | solution.py:36
  75.7 7.9 %collective-permute-start.15 = (bf16[2304,128]{1,0:T(8,128)(2,1)S(1)}, bf16[2304,128]{1,0:T(8,128)(2,1)S(1)}, u32[]{:S(2)}, u32[]{:S(2)}) collective-permute-start(bf16[2304,128]{1,0:T(8,128)(2,1)S(1)} %get-tuple-element.57), channel_id=1, source_target_pairs={{0,1},{1,0},{2,3},{3,2},{4,8},{5,9},{6,10},{7,11},{8,4},{9,5},{10,... | collective-permute-start | bytes 1769480 | tf_op jit(solution)/shard_map/ppermute | solution.py:330
  82.2 8.8 %collective-permute-start.7 = (f32[128,512]{1,0:T(8,128)S(1)}, f32[128,512]{1,0:T(8,128)S(1)}, u32[]{:S(2)}, u32[]{:S(2)}) collective-permute-start(f32[128,512]{1,0:T(8,128)S(1)} %slice_select_fusion), channel_id=1, source_target_pairs={{0,2},{2,0},{1,3},{3,1},{4,6},{6,4},{5,7},{7,5},{8,10},{10,8},{9,1... | collective-permute-start | bytes 786440 | tf_op jit(solution)/shard_map/ppermute | solution.py:36
  83.3 15.7 %collective-permute-start.21 = (bf16[2304,128]{1,0:T(8,128)(2,1)S(1)}, bf16[2304,128]{1,0:T(8,128)(2,1)S(1)}, u32[]{:S(2)}, u32[]{:S(2)}) collective-permute-start(bf16[2304,128]{1,0:T(8,128)(2,1)S(1)} %slice.83), channel_id=1, source_target_pairs={{0,1},{1,0},{2,3},{3,2},{4,8},{5,9},{6,10},{7,11},{8,4},{9,5},{10,... | collective-permute-start | bytes 1769480 | tf_op jit(solution)/shard_map/ppermute | solution.py:330
  83.5 23.4 %collective-permute-start.17 = (bf16[4608,128]{1,0:T(8,128)(2,1)S(1)}, bf16[4608,128]{1,0:T(8,128)(2,1)S(1)}, u32[]{:S(2)}, u32[]{:S(2)}) collective-permute-start(bf16[4608,128]{1,0:T(8,128)(2,1)S(1)} %pad_maximum_fusion), channel_id=1, source_target_pairs={{0,1},{1,0},{2,3},{3,2},{4,8},{5,9},{6,10},{7,11},{8,4},{9,5},{10,... | collective-permute-start | bytes 3538952 | tf_op jit(solution)/shard_map/ppermute | solution.py:330
  96.1 17.0 %collective-permute-start.16 = (bf16[2304,128]{1,0:T(8,128)(2,1)S(1)}, bf16[2304,128]{1,0:T(8,128)(2,1)S(1)}, u32[]{:S(2)}, u32[]{:S(2)}) collective-permute-start(bf16[2304,128]{1,0:T(8,128)(2,1)S(1)} %broadcast_select_fusion.1), channel_id=1, source_target_pairs={{0,4},{4,0},{8,12},{12,8},{1,5},{5,1},{9,13},{13,9},{2,6},{6,2},{1... | collective-permute-start | bytes 1769480 | tf_op jit(solution)/shard_map/ppermute | solution.py:322
  99.1 24.2 %collective-permute-start.22 = (bf16[2304,128]{1,0:T(8,128)(2,1)S(1)}, bf16[2304,128]{1,0:T(8,128)(2,1)S(1)}, u32[]{:S(2)}, u32[]{:S(2)}) collective-permute-start(bf16[2304,128]{1,0:T(8,128)(2,1)S(1)} %broadcast_select_fusion), channel_id=1, source_target_pairs={{0,4},{4,0},{8,12},{12,8},{1,5},{5,1},{9,13},{13,9},{2,6},{6,2},{1... | collective-permute-start | bytes 1769480 | tf_op jit(solution)/shard_map/ppermute | solution.py:322
  106.2 53.9 %collective-permute-start.12 = (f32[32,512]{1,0:T(8,128)S(1)}, f32[32,512]{1,0:T(8,128)S(1)}, u32[]{:S(2)}, u32[]{:S(2)}) collective-permute-start(f32[32,512]{1,0:T(8,128)S(1)} %slice_select_fusion.4), channel_id=1, source_target_pairs={{0,2},{2,0},{1,3},{3,1},{4,6},{6,4},{5,7},{7,5},{8,10},{10,8},{9,1... | collective-permute-start | bytes 196616 | tf_op jit(solution)/shard_map/ppermute | solution.py:36
  111.7 17.7 %collective-permute-start.27 = (f32[64,512]{1,0:T(8,128)S(1)}, f32[64,512]{1,0:T(8,128)S(1)}, u32[]{:S(2)}, u32[]{:S(2)}) collective-permute-start(f32[64,512]{1,0:T(8,128)S(1)} %get-tuple-element.44), channel_id=1, source_target_pairs={{0,1},{1,0},{2,3},{3,2},{4,5},{5,4},{6,7},{7,6},{8,9},{9,8},{10,11... | collective-permute-start | bytes 393224 | tf_op jit(solution)/shard_map/ppermute | solution.py:36
  129.4 30.7 %collective-permute-start.28 = (f32[32,512]{1,0:T(8,128)S(1)}, f32[32,512]{1,0:T(8,128)S(1)}, u32[]{:S(2)}, u32[]{:S(2)}) collective-permute-start(f32[32,512]{1,0:T(8,128)S(1)} %slice_select_fusion.3), channel_id=1, source_target_pairs={{0,2},{2,0},{1,3},{3,1},{4,6},{6,4},{5,7},{7,5},{8,10},{10,8},{9,1... | collective-permute-start | bytes 196616 | tf_op jit(solution)/shard_map/ppermute | solution.py:36
  131.7 24.2 %collective-permute-start.24 = (f32[32,896]{1,0:T(8,128)S(1)}, f32[32,896]{1,0:T(8,128)S(1)}, u32[]{:S(2)}, u32[]{:S(2)}) collective-permute-start(f32[32,896]{1,0:T(8,128)S(1)} %slice_select_fusion.2), channel_id=1, source_target_pairs={{0,2},{2,0},{1,3},{3,1},{4,6},{6,4},{5,7},{7,5},{8,10},{10,8},{9,1... | collective-permute-start | bytes 344072 | tf_op jit(solution)/shard_map/ppermute | solution.py:36
  137.3 22.2 %collective-permute-start.20 = (f32[32,1152]{1,0:T(8,128)S(1)}, f32[32,1152]{1,0:T(8,128)S(1)}, u32[]{:S(2)}, u32[]{:S(2)}) collective-permute-start(f32[32,1152]{1,0:T(8,128)S(1)} %select_add_fusion), channel_id=1, source_target_pairs={{0,4},{4,0},{8,12},{12,8},{1,5},{5,1},{9,13},{13,9},{2,6},{6,2},{1... | collective-permute-start | bytes 442376 | tf_op jit(solution)/shard_map/ppermute | solution.py:392
  160.4 7.7 %collective-permute-start.26 = (bf16[4,32,512]{2,1,0:T(8,128)(2,1)S(1)}, bf16[4,32,512]{2,1,0:T(8,128)(2,1)S(1)}, u32[]{:S(2)}, u32[]{:S(2)}) collective-permute-start(bf16[4,32,512]{2,1,0:T(8,128)(2,1)S(1)} %convolution_convert_fusion.2), channel_id=1, source_target_pairs={{0,4},{4,0},{8,12},{12,8},{1,5},{5,1},{9,13},{13,9},{2,6},{6,2},{1... | collective-permute-start | bytes 393224 | tf_op jit(solution)/shard_map/ppermute | solution.py:420
  163.1 11.8 %collective-permute-start.29 = (bf16[4,32,512]{2,1,0:T(8,128)(2,1)S(1)}, bf16[4,32,512]{2,1,0:T(8,128)(2,1)S(1)}, u32[]{:S(2)}, u32[]{:S(2)}) collective-permute-start(bf16[4,32,512]{2,1,0:T(8,128)(2,1)S(1)} %get-tuple-element.60), channel_id=1, source_target_pairs={{0,8},{8,0},{4,12},{12,4},{1,9},{9,1},{5,13},{13,5},{2,10},{10,2},... | collective-permute-start | bytes 393224 | tf_op jit(solution)/shard_map/ppermute | solution.py:421
  163.2 14.3 %collective-permute-start.30 = (bf16[4,32,512]{2,1,0:T(8,128)(2,1)S(1)}, bf16[4,32,512]{2,1,0:T(8,128)(2,1)S(1)}, u32[]{:S(2)}, u32[]{:S(2)}) collective-permute-start(bf16[4,32,512]{2,1,0:T(8,128)(2,1)S(1)} %get-tuple-element.61), channel_id=1, source_target_pairs={{0,12},{12,0},{4,8},{8,4},{1,13},{13,1},{5,9},{9,5},{2,14},{14,2},... | collective-permute-start | bytes 393224 | tf_op jit(solution)/shard_map/ppermute | solution.py:422
  (31 other events, 226.3 us)

commit v4 on v3

--- a/solution.py
+++ b/solution.py
@@ -9,6 +9,7 @@
 FEAT = ("eig", "rep")
 ALL = ("cand", "eig", "rep")
 STEPS = 3
+SHORT = pl.CostEstimate(flops=1, bytes_accessed=1, transcendentals=0)
 SIDE = ((0, 1), (1, 0), (2, 3), (3, 2))
 TWO = ((0, 2), (2, 0), (1, 3), (3, 1))
 THREE = ((0, 3), (3, 0), (1, 2), (2, 1))
@@ -160,38 +161,33 @@
             scratch_shapes=scratch,
         ),
         compiler_params=pltpu.CompilerParams(vmem_limit_bytes=16 << 20),
-        cost_estimate=pl.CostEstimate(
-            flops=2 * tok * cols * depth * total,
-            bytes_accessed=2 * total * depth * (tok + cols),
-            transcendentals=0,
-        ),
+        cost_estimate=SHORT,
     )(flags, *operands)
 
 
-def partner_dots(flags, pieces, shards, tail=None):
-    blocks = pieces[0][2]
+def partner_dots(flags, pieces, shards, wanted, depth, tail=None):
     cols = shards[0][0].shape[1]
-    depth = blocks // STEPS
+    step = depth // STEPS
     count = len(pieces)
-    width = len(shards) * count * TILE
+    width = len(wanted) * TILE
     tok = 0 if tail is None else tail[0].shape[0]
 
     def at(row):
         return lambda i, flags_ref: (row + i, 0)
 
     operands, specs = [], []
-    for array, row, _ in pieces:
+    for array, row in list(pieces) + list(shards):
         operands.append(array)
-        specs.append(pl.BlockSpec((depth, cols), at(row)))
-    for array, row in shards:
-        operands.append(array)
-        specs.append(pl.BlockSpec((depth, cols), at(row)))
+        specs.append(pl.BlockSpec((step, cols), at(row)))
     whole = lambda i, flags_ref: (0, 0)
     if tail is not None:
-        operands += list(tail)
-        specs.append(pl.BlockSpec((tok, depth), lambda i, flags_ref: (0, 2 * STEPS + i)))
-        specs.append(pl.BlockSpec((depth, cols), lambda i, flags_ref: (i * flags_ref[0], 0)))
-        specs.append(pl.BlockSpec((depth, cols), lambda i, flags_ref: (i * (1 - flags_ref[0]), 0)))
+        grads, at_end, at_middle, first, start = tail
+        operands += [grads, grads, at_end, at_middle, first[0], start]
+        specs.append(pl.BlockSpec((tok, step), lambda i, flags_ref: (0, 2 * STEPS + i)))
+        specs.append(pl.BlockSpec((tok, step), lambda i, flags_ref: (0, i * (1 - flags_ref[0]))))
+        specs.append(pl.BlockSpec((step, cols), lambda i, flags_ref: (i * flags_ref[0], 0)))
+        specs.append(pl.BlockSpec((step, cols), lambda i, flags_ref: (i * (1 - flags_ref[0]), 0)))
+        specs.append(pl.BlockSpec((step, cols), at(first[1])))
         specs.append(pl.BlockSpec((tok, cols), whole))
 
     def kernel(flags_ref, *refs):
@@ -199,9 +195,8 @@
         piece_refs, shard_refs = refs[:count], refs[count : count + len(shards)]
         refs = refs[count + len(shards) :]
         if tail is not None:
-            grads_ref, end_ref, middle_ref, start_ref = refs[:4]
-            refs = refs[4:]
-            keep_ref, give_ref, sums_ref, turned_ref, total_ref, wide_ref = refs
+            grads_ref, first_grads_ref, end_ref, middle_ref, first_ref, start_ref = refs[:6]
+            keep_ref, give_ref, sums_ref, turned_ref, total_ref, wide_ref = refs[6:]
         else:
             keep_ref, give_ref, sums_ref, turned_ref = refs
 
@@ -211,14 +206,22 @@
             if tail is not None:
                 total_ref[...] = start_ref[...]
 
-        for t, piece_ref in enumerate(piece_refs):
-            tokens = jnp.concatenate(
-                [piece_ref[q * TILE : (q + 1) * TILE, :] for q in range(depth // TILE)], axis=1
-            )
-            for j, shard_ref in enumerate(shard_refs):
-                sums_ref[j * count + t] += jnp.dot(
-                    tokens, shard_ref[...], preferred_element_type=jnp.float32
+        @pl.when(flags_ref[0] == 0)
+        def at_a_middle_plane():
+            for t, piece_ref in enumerate(piece_refs):
+                tokens = jnp.concatenate(
+                    [piece_ref[q * TILE : (q + 1) * TILE, :] for q in range(step // TILE)], axis=1
                 )
+                for block, (shard, piece) in enumerate(wanted):
+                    if piece == t:
+                        sums_ref[block] += jnp.dot(
+                            tokens, shard_refs[shard][...], preferred_element_type=jnp.float32
+                        )
+            if tail is not None:
+                total_ref[...] += jnp.dot(
+                    first_grads_ref[...], first_ref[...], preferred_element_type=jnp.float32
+                )
+
         if tail is not None:
             shard = jnp.where(flags_ref[0] == 1, end_ref[...], middle_ref[...])
             total_ref[...] += jnp.dot(grads_ref[...], shard, preferred_element_type=jnp.float32)
@@ -228,13 +231,13 @@
             if tail is not None:
                 wide_ref[...] = total_ref[...].T
                 split_rows(wide_ref, keep_ref, give_ref, flags_ref[1], pl.ds(0, tok))
-            for at_block in range(len(shards) * count):
-                turned_ref[...] = sums_ref[at_block].T
-                columns = pl.ds(tok + at_block * TILE, TILE)
+            for block in range(len(wanted)):
+                turned_ref[...] = sums_ref[block].T
+                columns = pl.ds(tok + block * TILE, TILE)
                 split_rows(turned_ref, keep_ref, give_ref, flags_ref[1], columns)
 
     scratch = [
-        pltpu.VMEM((len(shards) * count, TILE, cols), jnp.float32),
+        pltpu.VMEM((len(wanted), TILE, cols), jnp.float32),
         pltpu.VMEM((cols, TILE), jnp.float32),
     ]
     if tail is not None:
@@ -249,13 +252,30 @@
             out_specs=[pl.BlockSpec((cols // 2, tok + width), whole)] * 2,
             scratch_shapes=scratch,
         ),
+        compiler_params=pltpu.CompilerParams(vmem_limit_bytes=24 << 20),
+        cost_estimate=SHORT,
+    )(flags, *operands)
+
+
+def stack_blocks(flags, grads, depth):
+    tiles = grads.shape[0] // TILE
+
+    def kernel(flags_ref, grads_ref, out_ref):
+        for q in range(depth // TILE):
+            out_ref[q * TILE : (q + 1) * TILE, :] = grads_ref[:, q * TILE : (q + 1) * TILE]
+
+    return pl.pallas_call(
+        kernel,
+        out_shape=jax.ShapeDtypeStruct((tiles * depth, TILE), grads.dtype),
+        grid_spec=pltpu.PrefetchScalarGridSpec(
+            num_scalar_prefetch=1,
+            grid=(tiles,),
+            in_specs=[pl.BlockSpec((TILE, depth), lambda t, flags_ref: (t, 0))],
+            out_specs=pl.BlockSpec((depth, TILE), lambda t, flags_ref: (t, 0)),
+        ),
         compiler_params=pltpu.CompilerParams(vmem_limit_bytes=16 << 20),
-        cost_estimate=pl.CostEstimate(
-            flops=2 * blocks * cols * (width + tok),
-            bytes_accessed=2 * blocks * (cols * (count + len(shards)) + tok),
-            transcendentals=0,
-        ),
-    )(flags, *operands)
+        cost_estimate=SHORT,
+    )(flags, grads)
 
 
 def input_dots(flags, acts, shards):
@@ -297,11 +317,7 @@
             scratch_shapes=[pltpu.VMEM((tok, cols), jnp.float32)],
         ),
         compiler_params=pltpu.CompilerParams(vmem_limit_bytes=16 << 20),
-        cost_estimate=pl.CostEstimate(
-            flops=2 * tok * depth * cols * len(shards),
-            bytes_accessed=2 * depth * (tok + 7 * cols) + 4 * tok * cols * len(shards),
-            transcendentals=0,
-        ),
+        cost_estimate=SHORT,
     )(flags, *operands)
 
 
@@ -341,62 +357,74 @@
     late_rows = basis_out[depth:]
     m23 = middle(late_rows)
     started = after(flags, rows, late_rows)
-    m1 = middle(after(s0, m0))
-    stacked = grads[:, :depth].reshape(tiles_here, TILE, depth // TILE, TILE)
-    stacked = after(stacked, s0).transpose(0, 2, 1, 3).reshape(tiles_here * depth, TILE)
+    stacked = stack_blocks(started, grads, depth)
+    part_own = feature_dots(started, grads, [([(basis_out, 0)], 0, 0, 3 * STEPS, False)])
+    precond = (test_grads.astype(jnp.float32) / (eigval + damping)).astype(jnp.bfloat16)
+    m1 = middle(after(s0, m0, precond, stacked, *part_own))
     third = jnp.concatenate([basis_out[2 * depth :], basis_out[: 2 * rows_in - depth]])
     s3 = side(third, jnp.concatenate([m0, m1]))
     m5 = middle(s12[depth:])
     s45 = side(stacked[: 2 * depth], after(m23, s12))
-    m6 = middle(s3[:depth])
-    m47 = middle(after(jnp.concatenate([basis_out[:depth], s12[:depth]]), m5))
+    to_m6 = s3[:depth]
+    m6 = middle(to_m6)
+    m4 = middle(after(basis_out[:depth], m5))
     s6 = side(after(stacked[2 * depth : 3 * depth], s3), m5)
+    m7 = middle(after(s12[:depth], m6))
     s7 = side(after(stacked[3 * depth :], s45), m6)
 
-    early = after(flags, s3)
-    keep, give = input_dots(
-        early, acts, [[(basis_in, 0)], [(s0, 0)], [(s3, 0), (m0, 0)], [(s3, 1), (m1, 0)]]
-    )
-    rot_in = gather_rows(scatter_sum(keep, give).astype(jnp.bfloat16))
+    part_in = input_dots(
+        after(flags, to_m6),
+        acts,
+        [[(basis_in, 0)], [(s0, 0)], [(s3, 0), (m0, 0)], [(s3, 1), (m1, 0)]],
+    )
+    part_a = feature_dots(
+        after(flags, *part_in),
+        grads,
+        [
+            ([(s12, 0)], STEPS, 0, 2 * STEPS, False),
+            ([(s3, 0)], 2 * STEPS, 2 * STEPS, STEPS, True),
+        ],
+    )
+    rot_in = gather_rows(scatter_sum(*after(part_in, s45)).astype(jnp.bfloat16))
     rot_in = rot_in.reshape(tiles_here, TILE, 4 * cols)
-
-    sum_own = scatter_sum(
-        *feature_dots(started, grads, [([(basis_out, 0)], 0, 0, 3 * STEPS, False)])
-    )
-    sum_a = scatter_sum(
-        *feature_dots(
-            flags,
-            grads,
-            [
-                ([(s12, 0)], STEPS, 0, 2 * STEPS, False),
-                ([(s3, 0)], 2 * STEPS, 2 * STEPS, STEPS, True),
-            ],
-        )
-    )
+    sums = [jnp.concatenate(parts, axis=1) for parts in zip(part_own, part_a)]
+    sums = scatter_sum(*after(sums, s45))
+    sum_own, sum_a = sums[:, :tok_rows], sums[:, tok_rows:]
     part_b = feature_dots(
-        flags, grads, [([(s45, 0), (m23, 0)], STEPS, STEPS, 2 * STEPS, False),
-                       ([(m47, 0)], 0, 0, STEPS, True)]
-    )
-    sum_b = scatter_sum(*part_b)
+        after(flags, rot_in, sums),
+        grads,
+        [
+            ([(s45, 0), (m23, 0)], STEPS, STEPS, 2 * STEPS, False),
+            ([(m4, 0)], 0, 0, STEPS, True),
+        ],
+    )
     part_c = feature_dots(
-        flags, grads, [([(s6, 0), (m5, 0)], STEPS, STEPS, STEPS, False),
-                       ([(m47, STEPS)], 0, 0, STEPS, True)], split=False
-    )
-    shards = [(basis_out, 0), (m47, 0), (m47, STEPS)]
-    first = partner_dots(flags, [(s45, 0, depth), (s45, STEPS, depth), (s6, 0, depth)], shards)
-    sum_first = scatter_sum(*first)
-    last = partner_dots(flags, [(s7, 0, depth)], shards, (grads, s7, m6, part_c))
-    sum_last = scatter_sum(*last)
-    sum_c, sum_last = sum_last[:, :tok_rows], sum_last[:, tok_rows:]
-    back = [
-        jnp.where(end, lax.ppermute(x, "cand", SIDE), 0.0).reshape(slim, 3, -1)
-        for x in (sum_first, sum_last)
-    ]
-    back = jnp.concatenate(back, axis=2)
+        after(flags, *part_b),
+        grads,
+        [([(s6, 0), (m5, 0)], STEPS, STEPS, STEPS, False)],
+        split=False,
+    )
+    shards = [(basis_out, 0), (m4, 0), (m7, 0)]
+    pieces = [(s45, 0), (s45, STEPS), (s6, 0), (s7, 0)]
+    early = [(shard, piece) for shard in range(2) for piece in range(3)]
+    part_early = partner_dots(after(flags, part_c), pieces[:3], shards[:2], early, depth)
+    late = [(2, 0), (2, 1), (2, 2), (0, 3), (1, 3), (2, 3)]
+    part_late = partner_dots(
+        after(flags, *part_early), pieces, shards, late, depth, (grads, s7, m6, (m7, 0), part_c)
+    )
+    sums = scatter_sum(*[jnp.concatenate(parts, axis=1) for parts in zip(part_b, part_early)])
+    sum_b = sums[:, :tok_rows]
+    sum_late = scatter_sum(*part_late)
+    sum_c = sum_late[:, :tok_rows]
+    back_early = jnp.where(end, lax.ppermute(sums[:, tok_rows:], "cand", SIDE), 0.0)
+    back_late = jnp.where(end, lax.ppermute(sum_late[:, tok_rows:], "cand", SIDE), 0.0)
+    few = 3 * TILE
+    back_a = jnp.concatenate([back_early[:, :few], back_late[:, few : few + TILE]], axis=1)
+    back_b = jnp.concatenate([back_early[:, few:], back_late[:, few + TILE : few + 2 * TILE]], axis=1)
+    back_c = jnp.concatenate([back_late[:, :few], back_late[:, few + 2 * TILE :]], axis=1)
 
     rowmask, ignored = tile_layout(pair_tiles, last_rows, plane * tiles_here, tiles_here, TILE)
     keep = rowmask.reshape(1, tok_rows).astype(jnp.bfloat16)
-    precond = (test_grads.astype(jnp.float32) / (eigval + damping)).astype(jnp.bfloat16)
 
     def tile_prods(rot_out):
         return jnp.einsum(
@@ -413,9 +441,9 @@
         )
         return jnp.sum(jnp.where(onehot[:, :, None], scores[:, None, :], 0.0), axis=0)
 
-    prods_a = tile_prods(sum_a + back[:, 0])
-    prods_b = tile_prods(sum_b + back[:, 1])
-    prods_c = tile_prods(sum_c + back[:, 2])
+    prods_a = tile_prods(sum_a + back_a)
+    prods_b = tile_prods(sum_b + back_b)
+    prods_c = tile_prods(sum_c + back_c)
     total = pair_scores(tile_prods(sum_own), plane)
     total = total + pair_scores(lax.ppermute(prods_a, "cand", SIDE), plane ^ 1)
     total = total + pair_scores(lax.ppermute(pick(prods_b, prods_c), "cand", TWO), plane ^ 2)
@@ -425,17 +453,9 @@
 
 def final_sum(total):
     npairs, ntest = total.shape
-    mine = total.reshape(npairs, 2, 2, ntest // 4).transpose(2, 1, 0, 3)
-    keep, give = halves(mine, "rep")
-    keep, give = halves((keep + swap(give, "rep"))[0], "eig")
-    keep = (keep + swap(give, "eig"))[0]
-    plane = lax.axis_index("cand")
-    rows = npairs // 4
-    result = lax.dynamic_slice_in_dim(keep, plane * rows, rows, 0)
-    for step in range(1, 4):
-        block = lax.dynamic_slice_in_dim(keep, (plane ^ step) * rows, rows, 0)
-        result = result + lax.ppermute(block, "cand", [(i, i ^ step) for i in range(4)])
-    return result
+    blocks = total.reshape(4, npairs // 4, 4, ntest // 4).transpose(0, 2, 1, 3)
+    blocks = blocks.reshape(16, npairs // 4, ntest // 4)
+    return jnp.sum(lax.all_to_all(blocks, ALL, 0, 0, tiled=True), axis=0)
 
 
 def gather_plan(acts, grads, basis_in, basis_out, eigval, test_grads, pair_tiles, last_rows):

time: 194 us -> 182 us (0.938)
  local copies, waits for them, and re-layouts: 34.1 us -> 18.5 us
  starting transfers between devices: 57.6 us -> 43.5 us
  blocking collectives: 0 us -> 10.9 us
  waiting for transfers between devices: 53 us -> 63.3 us
  Pallas kernels: 27 us -> 24.8 us
    ppermute x5 -> x2, starting transfers between devices: 24.9 us -> 6.59 us  [the longest x1 3.93 us: line_plan(): lax.ppermute(sum_late[:, tok_rows:], 'cand', SIDE)]
    ppermute x4, waiting for transfers between devices: 22.5 us -> 35.9 us  [side(): return lax.ppermute(pick(at_end, at_middle), 'cand', SIDE)]
    all_to_all x0 -> x1, blocking collectives: none -> 10.9 us  [final_sum(): return jnp.sum(lax.all_to_all(blocks, ALL, 0, 0, tiled=True), axis=0)]
    slice x10 -> x9, local copies, waits for them, and re-layouts: 15.2 us -> 5.64 us  [the longest x1 3.33 us: line_plan(): late_rows = basis_out[depth:]]
    ppermute x1, waiting for transfers between devices: 0.01 us -> 8.52 us  [line_plan(): s12 = lax.ppermute(rows, 'cand', SIDE)]
    ppermute x16 -> x10, waiting for transfers between devices: 21 us -> 12.6 us  [swap(): return lax.ppermute(x, axis_name, [(0, 1), (1, 0)])]
    unnamed x35 -> x48, local copies, waits for them, and re-layouts: 3.34 us -> 11.5 us
    slice x2 -> x1, local copies, waits for them, and re-layouts: 7.77 us -> 1.09 us  [line_plan(): s7 = side(after(stacked[3 * depth:], s45), m6)]
  transfers between devices with their start and end apart: 36 -> 28, of which waited for: 15 -> 10; matrix products, arithmetic and copies ran while one was open for 24% -> 13% of each run, Pallas kernels for 14% -> 12%
where the time goes in v4:
time: 182 us
  waiting for transfers between devices  63.3 us (35%)
  starting transfers between devices  43.5 us (24%)
  Pallas kernels  24.8 us (14%)
  local copies, waits for them, and re-layouts  18.5 us (10%)
  blocking collectives  10.9 us (6%)
  matrix products  10.7 us (6%)
  other arithmetic  9.52 us (5%)
    ppermute x4, waiting for transfers between devices, side(): return lax.ppermute(pick(at_end, at_middle), 'cand', SIDE)  35.9 us
    ppermute x4, starting transfers between devices, side(): return lax.ppermute(pick(at_end, at_middle), 'cand', SIDE)  18.5 us
    pallas_call x4, Pallas kernels, feature_dots(): pl.pallas_call(kernel, out_shape=out_shape, grid_spec=pltpu.PrefetchScala...  16.3 us
    ppermute x10, waiting for transfers between devices, swap(): return lax.ppermute(x, axis_name, [(0, 1), (1, 0)])  12.6 us
    unnamed x48, local copies, waits for them, and re-layouts  11.5 us
    all_to_all x1, blocking collectives, final_sum(): return jnp.sum(lax.all_to_all(blocks, ALL, 0, 0, tiled=True), axis=0)  10.9 us
    dot_general x4, matrix products, pair_scores(): jnp.einsum('tea,jea->tj', prods, precond, preferred_element_type=jnp.floa...  9.9 us
    ppermute x1, waiting for transfers between devices, line_plan(): s12 = lax.ppermute(rows, 'cand', SIDE)  8.52 us
  transfers between devices with their start and end apart: 28, of which 10 were waited for; matrix products, arithmetic and copies ran while one was open for 13% of the time, Pallas kernels for 12%

profile of v4, /device:TPU:0, one launch (start us, length us, event | category | flops | bytes accessed | tf_op | source)
XLA Modules:
  0.0 181.8 jit_solution(501319010639530198)
XLA Ops:
  0.0 3.0 %collective-permute-start.1 = (bf16[1280,128]{1,0:T(8,128)(2,1)}, bf16[1280,128]{1,0:T(8,128)(2,1)}, u32[]{:S(2)}, u32[]{:S(2)}) collective-permute-start(bf16[1280,128]{1,0:T(8,128)(2,1)} %refs_0_.3), channel_id=1, source_target_pairs={{0,4},{4,0},{8,12},{12,8},{1,5},{5,1},{9,13},{13,9},{2,6},{6,2},{1... | collective-permute-start | bytes 983048 | tf_op jit(solution)/shard_map/ppermute | solution.py:354
  3.0 3.3 %fusion.47 = (bf16[4608,128]{1,0:T(8,128)(2,1)}, bf16[4608,128]{1,0:T(8,128)(2,1)}) fusion(bf16[6912,128]{1,0:T(8,128)(2,1)} %refs_4_.1, s32[]{:T(128)S(6)} %select_n.161), kind=kLoop, calls=%fused_computation.97 | loop fusion | bytes 4718596 | tf_op jit(solution)/shard_map/slice | solution.py:357
  6.9 2.6 %collective-permute-start.4 = (bf16[4608,128]{1,0:T(8,128)(2,1)}, bf16[4608,128]{1,0:T(8,128)(2,1)S(1)}, u32[]{:S(2)}, u32[]{:S(2)}) collective-permute-start(bf16[4608,128]{1,0:T(8,128)(2,1)} %get-tuple-element.73), channel_id=1, source_target_pairs={{0,4},{4,0},{8,12},{12,8},{1,5},{5,1},{9,13},{13,9},{2,6},{6,2},{1... | collective-permute-start | bytes 3538952 | tf_op jit(solution)/shard_map/ppermute | solution.py:356
  10.7 3.0 %copy-done = bf16[512,6912]{1,0:T(8,128)(2,1)S(1)} copy-done((bf16[512,6912]{1,0:T(8,128)(2,1)S(1)}, bf16[512,6912]{1,0:T(8,128)(2,1)}, u32[]{:S(2)}) %copy-start) | copy-done | bytes 7077912
  16.4 4.8 %shard_map.82 = (f32[64,512]{1,0:T(8,128)S(1)}, f32[64,512]{1,0:T(8,128)S(1)}) custom-call(s32[6]{0:T(128)S(1)} %stack.49.flags_ref, bf16[512,6912]{1,0:T(8,128)(2,1)S(1)} %copy-done, bf16[6912,128]{1,0:T(8,128)(2,1)S(1)} %copy-done.2), custom_call_target="tpu_custom_call" | custom-call | flops 1 | bytes 1 | tf_op jit(solution)/shard_map/pallas_call | solution.py:153
  22.3 3.7 %divide_convert_fusion = bf16[64,32,512]{2,1,0:T(8,128)(2,1)} fusion(bf16[64,32,512]{2,1,0:T(8,128)(2,1)} %param.13, f32[32,512]{1,0:T(8,128)S(1)} %broadcast_add_fusion), kind=kLoop, calls=%fused_computation | loop fusion | flops 3145728 | bytes 4259840 | tf_op jit(solution)/shard_map/convert_element_type | solution.py:362
  27.7 8.5 %collective-permute-done.4.refs_0_ = bf16[4608,128]{1,0:T(8,128)(2,1)S(1)} collective-permute-done((bf16[4608,128]{1,0:T(8,128)(2,1)}, bf16[4608,128]{1,0:T(8,128)(2,1)S(1)}, u32[]{:S(2)}, u32[]{:S(2)}) %collective-permute-start.4) | collective-permute-done | bytes 1179680 | tf_op jit(solution)/shard_map/ppermute | solution.py:356
  37.4 5.4 %collective-permute-start.6 = (bf16[4608,128]{1,0:T(8,128)(2,1)}, bf16[4608,128]{1,0:T(8,128)(2,1)S(1)}, u32[]{:S(2)}, u32[]{:S(2)}) collective-permute-start(bf16[4608,128]{1,0:T(8,128)(2,1)} %slice_select_fusion), channel_id=1, source_target_pairs={{0,4},{4,0},{8,12},{12,8},{1,5},{5,1},{9,13},{13,9},{2,6},{6,2},{1... | collective-permute-start | bytes 3538952 | tf_op jit(solution)/shard_map/ppermute | solution.py:338
  44.6 3.3 %collective-permute-start.3 = (bf16[2560,128]{1,0:T(8,128)(2,1)}, bf16[2560,128]{1,0:T(8,128)(2,1)S(1)}, u32[]{:S(2)}, u32[]{:S(2)}) collective-permute-start(bf16[2560,128]{1,0:T(8,128)(2,1)} %maximum_select_fusion), channel_id=1, source_target_pairs={{0,4},{4,0},{8,12},{12,8},{1,5},{5,1},{9,13},{13,9},{2,6},{6,2},{1... | collective-permute-start | bytes 1966088 | tf_op jit(solution)/shard_map/ppermute | solution.py:338
  49.1 31.9 %collective-permute-done.3.refs_2_.refs_4_.refs_1_ = bf16[2560,128]{1,0:T(8,128)(2,1)S(1)} collective-permute-done((bf16[2560,128]{1,0:T(8,128)(2,1)}, bf16[2560,128]{1,0:T(8,128)(2,1)S(1)}, u32[]{:S(2)}, u32[]{:S(2)}) %collective-permute-start.3) | collective-permute-done | bytes 655392 | tf_op jit(solution)/shard_map/ppermute | solution.py:338
  84.3 3.9 %shard_map.84 = (f32[256,512]{1,0:T(8,128)S(1)}, f32[256,512]{1,0:T(8,128)S(1)}) custom-call(s32[6]{0:T(128)S(1)} %stack.49.flags_ref, bf16[512,1280]{1,0:T(8,128)(2,1)S(1)} %copy-done.8, bf16[1280,128]{1,0:T(8,128)(2,1)S(1)} %copy-done.9, bf16[1280,128]{1,0:T(8,128)(2,1)} %collective-permute-done.1.refs_1_, ...), custom_call_target="tpu_custom_call" | custom-call | flops 1 | bytes 1 | tf_op jit(solution)/shard_map/pallas_call | solution.py:309
  89.0 3.0 %copy-done.1 = bf16[512,6912]{1,0:T(8,128)(2,1)S(1)} copy-done((bf16[512,6912]{1,0:T(8,128)(2,1)S(1)}, bf16[512,6912]{1,0:T(8,128)(2,1)}, u32[]{:S(2)}) %copy-start.1) | copy-done | bytes 7077912
  92.1 3.8 %shard_map.85 = (f32[64,512]{1,0:T(8,128)S(1)}, f32[64,512]{1,0:T(8,128)S(1)}) custom-call(s32[6]{0:T(128)S(1)} %stack.49.flags_ref, bf16[512,6912]{1,0:T(8,128)(2,1)S(1)} %copy-done.1, bf16[4608,128]{1,0:T(8,128)(2,1)S(1)} %collective-permute-done.4.refs_0_, bf16[2560,128]{1,0:T(8,128)(2,1)S(1)} %collective-permute-done.3.refs_2_.refs_4_.refs_1_), custom_call_target="tpu_custom_call" | custom-call | flops 1 | bytes 1 | tf_op jit(solution)/shard_map/pallas_call | solution.py:153
  98.3 5.0 %collective-permute-start.15 = (bf16[2304,128]{1,0:T(8,128)(2,1)S(1)}, bf16[2304,128]{1,0:T(8,128)(2,1)S(1)}, u32[]{:S(2)}, u32[]{:S(2)}) collective-permute-start(bf16[2304,128]{1,0:T(8,128)(2,1)S(1)} %broadcast_select_fusion.1), channel_id=1, source_target_pairs={{0,4},{4,0},{8,12},{12,8},{1,5},{5,1},{9,13},{13,9},{2,6},{6,2},{1... | collective-permute-start | bytes 1769480 | tf_op jit(solution)/shard_map/ppermute | solution.py:338
  107.3 3.9 %collective-permute-done.11 = bf16[128,512]{1,0:T(8,128)(2,1)S(1)} collective-permute-done((bf16[128,512]{1,0:T(8,128)(2,1)S(1)}, bf16[128,512]{1,0:T(8,128)(2,1)S(1)}, u32[]{:S(2)}, u32[]{:S(2)}) %collective-permute-start.11) | collective-permute-done | bytes 131104 | tf_op jit(solution)/shard_map/ppermute | solution.py:37
  112.7 4.8 %collective-permute-start.20 = (bf16[2304,128]{1,0:T(8,128)(2,1)S(1)}, bf16[2304,128]{1,0:T(8,128)(2,1)S(1)}, u32[]{:S(2)}, u32[]{:S(2)}) collective-permute-start(bf16[2304,128]{1,0:T(8,128)(2,1)S(1)} %broadcast_select_fusion), channel_id=1, source_target_pairs={{0,4},{4,0},{8,12},{12,8},{1,5},{5,1},{9,13},{13,9},{2,6},{6,2},{1... | collective-permute-start | bytes 1769480 | tf_op jit(solution)/shard_map/ppermute | solution.py:338
  117.7 4.8 %shard_map.86 = (f32[64,512]{1,0:T(8,128)S(1)}, f32[64,512]{1,0:T(8,128)S(1)}) custom-call(s32[6]{0:T(128)S(1)} %stack.49.flags_ref, bf16[512,6912]{1,0:T(8,128)(2,1)S(1)} %bitcast.56, bf16[4608,128]{1,0:T(8,128)(2,1)S(1)} %collective-permute-done.6.refs_0_.refs_1_, bf16[4608,128]{1,0:T(8,128)(2,1)} %collective-permute-done.5.refs_1_, ...), custom_call_target="tpu_custom_call" | custom-call | flops 1 | bytes 1 | tf_op jit(solution)/shard_map/pallas_call | solution.py:153
  122.5 2.8 %shard_map.87.refs_12_ = f32[512,128]{1,0:T(8,128)S(1)} custom-call(s32[6]{0:T(128)S(1)} %stack.49.flags_ref, bf16[512,6912]{1,0:T(8,128)(2,1)S(1)} %bitcast.56, bf16[2304,128]{1,0:T(8,128)(2,1)S(1)} %collective-permute-done.15.refs_0_.refs_2_, bf16[2304,128]{1,0:T(8,128)(2,1)} %collective-permute-done.13.refs_1_), custom_call_target="tpu_custom_call" | custom-call | flops 1 | bytes 1 | tf_op jit(solution)/shard_map/pallas_call | solution.py:153
  126.3 4.0 %collective-permute-done.20.refs_3_.refs_9_ = bf16[2304,128]{1,0:T(8,128)(2,1)S(1)} collective-permute-done((bf16[2304,128]{1,0:T(8,128)(2,1)S(1)}, bf16[2304,128]{1,0:T(8,128)(2,1)S(1)}, u32[]{:S(2)}, u32[]{:S(2)}) %collective-permute-start.20) | collective-permute-done | bytes 589856 | tf_op jit(solution)/shard_map/ppermute | solution.py:338
  136.8 4.9 %collective-permute-done.23 = f32[32,1280]{1,0:T(8,128)S(1)} collective-permute-done((f32[32,1280]{1,0:T(8,128)S(1)}, f32[32,1280]{1,0:T(8,128)S(1)}, u32[]{:S(2)}, u32[]{:S(2)}) %collective-permute-start.23) | collective-permute-done | bytes 163872 | tf_op jit(solution)/shard_map/ppermute | solution.py:37
  141.7 3.9 %collective-permute-start.24 = (f32[32,768]{1,0:T(8,128)S(1)}, f32[32,768]{1,0:T(8,128)S(1)}, u32[]{:S(2)}, u32[]{:S(2)}) collective-permute-start(f32[32,768]{1,0:T(8,128)S(1)} %slice.99), channel_id=1, source_target_pairs={{0,4},{4,0},{8,12},{12,8},{1,5},{5,1},{9,13},{13,9},{2,6},{6,2},{1... | collective-permute-start | bytes 294920 | tf_op jit(solution)/shard_map/ppermute | solution.py:420
  145.7 2.7 %collective-permute-start.18 = (f32[32,768]{1,0:T(8,128)S(1)}, f32[32,768]{1,0:T(8,128)S(1)}, u32[]{:S(2)}, u32[]{:S(2)}) collective-permute-start(f32[32,768]{1,0:T(8,128)S(1)} %slice.95), channel_id=1, source_target_pairs={{0,4},{4,0},{8,12},{12,8},{1,5},{5,1},{9,13},{13,9},{2,6},{6,2},{1... | collective-permute-start | bytes 294920 | tf_op jit(solution)/shard_map/ppermute | solution.py:419
  161.3 3.7 %collective-permute-done.26 = bf16[4,32,512]{2,1,0:T(8,128)(2,1)S(1)} collective-permute-done((bf16[4,32,512]{2,1,0:T(8,128)(2,1)S(1)}, bf16[4,32,512]{2,1,0:T(8,128)(2,1)S(1)}, u32[]{:S(2)}, u32[]{:S(2)}) %collective-permute-start.26) | collective-permute-done | bytes 131104 | tf_op jit(solution)/shard_map/ppermute | solution.py:449
  170.4 10.9 %all_to_all.5 = f32[16,2,16]{2,1,0:T(2,128)S(1)} all-to-all(f32[16,2,16]{2,1,0:T(2,128)S(1)} %copy.69), channel_id=1, replica_groups=mesh['groups'=2,'cand'=4,'eig'=2,'rep'=2] {'cand','eig','rep'}, dimensions={0} | all-to-all | bytes 4096 | tf_op jit(solution)/shard_map/all_to_all | solution.py:458
  (160 shorter events, 49.3 us)
Async XLA Ops:
  0.0 27.6 %collective-permute-start.1 = (bf16[1280,128]{1,0:T(8,128)(2,1)}, bf16[1280,128]{1,0:T(8,128)(2,1)}, u32[]{:S(2)}, u32[]{:S(2)}) collective-permute-start(bf16[1280,128]{1,0:T(8,128)(2,1)} %refs_0_.3), channel_id=1, source_target_pairs={{0,4},{4,0},{8,12},{12,8},{1,5},{5,1},{9,13},{13,9},{2,6},{6,2},{1... | collective-permute-start | bytes 983048 | tf_op jit(solution)/shard_map/ppermute | solution.py:354
  3.0 24.6 %collective-permute-start = (bf16[1280,128]{1,0:T(8,128)(2,1)}, bf16[1280,128]{1,0:T(8,128)(2,1)S(1)}, u32[]{:S(2)}, u32[]{:S(2)}) collective-permute-start(bf16[1280,128]{1,0:T(8,128)(2,1)} %refs_0_.3), channel_id=1, source_target_pairs={{0,1},{1,0},{2,3},{3,2},{4,8},{5,9},{6,10},{7,11},{8,4},{9,5},{10,... | collective-permute-start | bytes 983048 | tf_op jit(solution)/shard_map/ppermute | solution.py:346
  6.4 21.3 %collective-permute-start.5 = (bf16[4608,128]{1,0:T(8,128)(2,1)}, bf16[4608,128]{1,0:T(8,128)(2,1)}, u32[]{:S(2)}, u32[]{:S(2)}) collective-permute-start(bf16[4608,128]{1,0:T(8,128)(2,1)} %get-tuple-element.72), channel_id=1, source_target_pairs={{0,1},{1,0},{2,3},{3,2},{4,8},{5,9},{6,10},{7,11},{8,4},{9,5},{10,... | collective-permute-start | bytes 3538952 | tf_op jit(solution)/shard_map/ppermute | solution.py:346
  6.9 29.4 %collective-permute-start.4 = (bf16[4608,128]{1,0:T(8,128)(2,1)}, bf16[4608,128]{1,0:T(8,128)(2,1)S(1)}, u32[]{:S(2)}, u32[]{:S(2)}) collective-permute-start(bf16[4608,128]{1,0:T(8,128)(2,1)} %get-tuple-element.73), channel_id=1, source_target_pairs={{0,4},{4,0},{8,12},{12,8},{1,5},{5,1},{9,13},{13,9},{2,6},{6,2},{1... | collective-permute-start | bytes 3538952 | tf_op jit(solution)/shard_map/ppermute | solution.py:356
  27.6 15.2 %collective-permute-start.2 = (bf16[1280,128]{1,0:T(8,128)(2,1)}, bf16[1280,128]{1,0:T(8,128)(2,1)S(1)}, u32[]{:S(2)}, u32[]{:S(2)}) collective-permute-start(bf16[1280,128]{1,0:T(8,128)(2,1)} %collective-permute-done.1.refs_1_), channel_id=1, source_target_pairs={{0,1},{1,0},{2,3},{3,2},{4,8},{5,9},{6,10},{7,11},{8,4},{9,5},{10,... | collective-permute-start | bytes 983048 | tf_op jit(solution)/shard_map/ppermute | solution.py:346
  37.4 50.9 %collective-permute-start.6 = (bf16[4608,128]{1,0:T(8,128)(2,1)}, bf16[4608,128]{1,0:T(8,128)(2,1)S(1)}, u32[]{:S(2)}, u32[]{:S(2)}) collective-permute-start(bf16[4608,128]{1,0:T(8,128)(2,1)} %slice_select_fusion), channel_id=1, source_target_pairs={{0,4},{4,0},{8,12},{12,8},{1,5},{5,1},{9,13},{13,9},{2,6},{6,2},{1... | collective-permute-start | bytes 3538952 | tf_op jit(solution)/shard_map/ppermute | solution.py:338
  44.6 36.4 %collective-permute-start.3 = (bf16[2560,128]{1,0:T(8,128)(2,1)}, bf16[2560,128]{1,0:T(8,128)(2,1)S(1)}, u32[]{:S(2)}, u32[]{:S(2)}) collective-permute-start(bf16[2560,128]{1,0:T(8,128)(2,1)} %maximum_select_fusion), channel_id=1, source_target_pairs={{0,4},{4,0},{8,12},{12,8},{1,5},{5,1},{9,13},{13,9},{2,6},{6,2},{1... | collective-permute-start | bytes 1966088 | tf_op jit(solution)/shard_map/ppermute | solution.py:338
  49.0 47.0 %collective-permute-start.13 = (bf16[2304,128]{1,0:T(8,128)(2,1)}, bf16[2304,128]{1,0:T(8,128)(2,1)}, u32[]{:S(2)}, u32[]{:S(2)}) collective-permute-start(bf16[2304,128]{1,0:T(8,128)(2,1)} %get-tuple-element.75), channel_id=1, source_target_pairs={{0,1},{1,0},{2,3},{3,2},{4,8},{5,9},{6,10},{7,11},{8,4},{9,5},{10,... | collective-permute-start | bytes 1769480 | tf_op jit(solution)/shard_map/ppermute | solution.py:346
  88.3 8.3 %collective-permute-start.9 = (f32[256,512]{1,0:T(8,128)S(1)}, f32[256,512]{1,0:T(8,128)S(1)}, u32[]{:S(2)}, u32[]{:S(2)}) collective-permute-start(f32[256,512]{1,0:T(8,128)S(1)} %get-tuple-element.48), channel_id=1, source_target_pairs={{0,1},{1,0},{2,3},{3,2},{4,5},{5,4},{6,7},{7,6},{8,9},{9,8},{10,11... | collective-permute-start | bytes 1572872 | tf_op jit(solution)/shard_map/ppermute | solution.py:37
  88.5 14.8 %collective-permute-start.19 = (bf16[2304,128]{1,0:T(8,128)(2,1)S(1)}, bf16[2304,128]{1,0:T(8,128)(2,1)S(1)}, u32[]{:S(2)}, u32[]{:S(2)}) collective-permute-start(bf16[2304,128]{1,0:T(8,128)(2,1)S(1)} %slice.89), channel_id=1, source_target_pairs={{0,1},{1,0},{2,3},{3,2},{4,8},{5,9},{6,10},{7,11},{8,4},{9,5},{10,... | collective-permute-start | bytes 1769480 | tf_op jit(solution)/shard_map/ppermute | solution.py:346
  96.0 21.6 %collective-permute-start.14 = (bf16[2304,128]{1,0:T(8,128)(2,1)S(1)}, bf16[2304,128]{1,0:T(8,128)(2,1)S(1)}, u32[]{:S(2)}, u32[]{:S(2)}) collective-permute-start(bf16[2304,128]{1,0:T(8,128)(2,1)S(1)} %copy-done.16), channel_id=1, source_target_pairs={{0,1},{1,0},{2,3},{3,2},{4,8},{5,9},{6,10},{7,11},{8,4},{9,5},{10,... | collective-permute-start | bytes 1769480 | tf_op jit(solution)/shard_map/ppermute | solution.py:346
  96.1 7.3 %collective-permute-start.7 = (f32[64,1024]{1,0:T(8,128)S(1)}, f32[64,1024]{1,0:T(8,128)S(1)}, u32[]{:S(2)}, u32[]{:S(2)}) collective-permute-start(f32[64,1024]{1,0:T(8,128)S(1)} %get-tuple-element.46), channel_id=1, source_target_pairs={{0,1},{1,0},{2,3},{3,2},{4,5},{5,4},{6,7},{7,6},{8,9},{9,8},{10,11... | collective-permute-start | bytes 786440 | tf_op jit(solution)/shard_map/ppermute | solution.py:37
  96.7 8.4 %collective-permute-start.10 = (f32[128,512]{1,0:T(8,128)S(1)}, f32[128,512]{1,0:T(8,128)S(1)}, u32[]{:S(2)}, u32[]{:S(2)}) collective-permute-start(f32[128,512]{1,0:T(8,128)S(1)} %slice_select_fusion.1), channel_id=1, source_target_pairs={{0,2},{2,0},{1,3},{3,1},{4,6},{6,4},{5,7},{7,5},{8,10},{10,8},{9,1... | collective-permute-start | bytes 786440 | tf_op jit(solution)/shard_map/ppermute | solution.py:37
  98.3 24.2 %collective-permute-start.15 = (bf16[2304,128]{1,0:T(8,128)(2,1)S(1)}, bf16[2304,128]{1,0:T(8,128)(2,1)S(1)}, u32[]{:S(2)}, u32[]{:S(2)}) collective-permute-start(bf16[2304,128]{1,0:T(8,128)(2,1)S(1)} %broadcast_select_fusion.1), channel_id=1, source_target_pairs={{0,4},{4,0},{8,12},{12,8},{1,5},{5,1},{9,13},{13,9},{2,6},{6,2},{1... | collective-permute-start | bytes 1769480 | tf_op jit(solution)/shard_map/ppermute | solution.py:338
  103.4 22.9 %collective-permute-start.21 = (bf16[2304,128]{1,0:T(8,128)(2,1)S(1)}, bf16[2304,128]{1,0:T(8,128)(2,1)S(1)}, u32[]{:S(2)}, u32[]{:S(2)}) collective-permute-start(bf16[2304,128]{1,0:T(8,128)(2,1)S(1)} %copy-done.17), channel_id=1, source_target_pairs={{0,1},{1,0},{2,3},{3,2},{4,8},{5,9},{6,10},{7,11},{8,4},{9,5},{10,... | collective-permute-start | bytes 1769480 | tf_op jit(solution)/shard_map/ppermute | solution.py:346
  105.2 6.1 %collective-permute-start.11 = (bf16[128,512]{1,0:T(8,128)(2,1)S(1)}, bf16[128,512]{1,0:T(8,128)(2,1)S(1)}, u32[]{:S(2)}, u32[]{:S(2)}) collective-permute-start(bf16[128,512]{1,0:T(8,128)(2,1)S(1)} %add_convert_fusion), channel_id=1, source_target_pairs={{0,2},{2,0},{1,3},{3,1},{4,6},{6,4},{5,7},{7,5},{8,10},{10,8},{9,1... | collective-permute-start | bytes 393224 | tf_op jit(solution)/shard_map/ppermute | solution.py:37
  111.3 6.1 %collective-permute-start.12 = (bf16[2,128,512]{2,1,0:T(8,128)(2,1)S(1)}, bf16[2,128,512]{2,1,0:T(8,128)(2,1)S(1)}, u32[]{:S(2)}, u32[]{:S(2)}) collective-permute-start(bf16[2,128,512]{2,1,0:T(8,128)(2,1)S(1)} %pad_maximum_fusion.4), channel_id=1, source_target_pairs={{0,1},{1,0},{2,3},{3,2},{4,5},{5,4},{6,7},{7,6},{8,9},{9,8},{10,11... | collective-permute-start | bytes 786440 | tf_op jit(solution)/shard_map/ppermute | solution.py:37
  112.7 17.5 %collective-permute-start.20 = (bf16[2304,128]{1,0:T(8,128)(2,1)S(1)}, bf16[2304,128]{1,0:T(8,128)(2,1)S(1)}, u32[]{:S(2)}, u32[]{:S(2)}) collective-permute-start(bf16[2304,128]{1,0:T(8,128)(2,1)S(1)} %broadcast_select_fusion), channel_id=1, source_target_pairs={{0,4},{4,0},{8,12},{12,8},{1,5},{5,1},{9,13},{13,9},{2,6},{6,2},{1... | collective-permute-start | bytes 1769480 | tf_op jit(solution)/shard_map/ppermute | solution.py:338
  134.5 7.1 %collective-permute-start.23 = (f32[32,1280]{1,0:T(8,128)S(1)}, f32[32,1280]{1,0:T(8,128)S(1)}, u32[]{:S(2)}, u32[]{:S(2)}) collective-permute-start(f32[32,1280]{1,0:T(8,128)S(1)} %slice_select_fusion.2), channel_id=1, source_target_pairs={{0,2},{2,0},{1,3},{3,1},{4,6},{6,4},{5,7},{7,5},{8,10},{10,8},{9,1... | collective-permute-start | bytes 491528 | tf_op jit(solution)/shard_map/ppermute | solution.py:37
  136.1 9.5 %collective-permute-start.17 = (f32[32,1280]{1,0:T(8,128)S(1)}, f32[32,1280]{1,0:T(8,128)S(1)}, u32[]{:S(2)}, u32[]{:S(2)}) collective-permute-start(f32[32,1280]{1,0:T(8,128)S(1)} %slice_select_fusion.3), channel_id=1, source_target_pairs={{0,2},{2,0},{1,3},{3,1},{4,6},{6,4},{5,7},{7,5},{8,10},{10,8},{9,1... | collective-permute-start | bytes 491528 | tf_op jit(solution)/shard_map/ppermute | solution.py:37
  141.7 6.6 %collective-permute-start.24 = (f32[32,768]{1,0:T(8,128)S(1)}, f32[32,768]{1,0:T(8,128)S(1)}, u32[]{:S(2)}, u32[]{:S(2)}) collective-permute-start(f32[32,768]{1,0:T(8,128)S(1)} %slice.99), channel_id=1, source_target_pairs={{0,4},{4,0},{8,12},{12,8},{1,5},{5,1},{9,13},{13,9},{2,6},{6,2},{1... | collective-permute-start | bytes 294920 | tf_op jit(solution)/shard_map/ppermute | solution.py:420
  151.4 7.4 %collective-permute-start.27 = (bf16[4,32,512]{2,1,0:T(8,128)(2,1)S(1)}, bf16[4,32,512]{2,1,0:T(8,128)(2,1)S(1)}, u32[]{:S(2)}, u32[]{:S(2)}) collective-permute-start(bf16[4,32,512]{2,1,0:T(8,128)(2,1)S(1)} %get-tuple-element.79), channel_id=1, source_target_pairs={{0,12},{12,0},{4,8},{8,4},{1,13},{13,1},{5,9},{9,5},{2,14},{14,2},... | collective-permute-start | bytes 393224 | tf_op jit(solution)/shard_map/ppermute | solution.py:450
  153.8 11.3 %collective-permute-start.26 = (bf16[4,32,512]{2,1,0:T(8,128)(2,1)S(1)}, bf16[4,32,512]{2,1,0:T(8,128)(2,1)S(1)}, u32[]{:S(2)}, u32[]{:S(2)}) collective-permute-start(bf16[4,32,512]{2,1,0:T(8,128)(2,1)S(1)} %get-tuple-element.78), channel_id=1, source_target_pairs={{0,8},{8,0},{4,12},{12,4},{1,9},{9,1},{5,13},{13,5},{2,10},{10,2},... | collective-permute-start | bytes 393224 | tf_op jit(solution)/shard_map/ppermute | solution.py:449
  157.9 9.8 %collective-permute-start.25 = (bf16[4,32,512]{2,1,0:T(8,128)(2,1)S(1)}, bf16[4,32,512]{2,1,0:T(8,128)(2,1)S(1)}, u32[]{:S(2)}, u32[]{:S(2)}) collective-permute-start(bf16[4,32,512]{2,1,0:T(8,128)(2,1)S(1)} %convolution_convert_fusion.2), channel_id=1, source_target_pairs={{0,4},{4,0},{8,12},{12,8},{1,5},{5,1},{9,13},{13,9},{2,6},{6,2},{1... | collective-permute-start | bytes 393224 | tf_op jit(solution)/shard_map/ppermute | solution.py:448
  (29 other events, 184.2 us)

commit v5 on v4

--- a/solution.py
+++ b/solution.py
@@ -69,6 +69,14 @@
         give_ref[here, columns] = full_ref[theirs, :]
 
 
+def add_dot(total_ref, rows_ref, shard):
+    half = total_ref.shape[0] // 2
+    for here in (pl.ds(0, half), pl.ds(half, half)):
+        total_ref[here, :] += jnp.dot(
+            rows_ref[here, :], shard, preferred_element_type=jnp.float32
+        )
+
+
 def feature_dots(flags, grads, segments, start=None, split=True):
     tok = grads.shape[0]
     cols = segments[0][0][0][0].shape[1]
@@ -130,9 +138,7 @@
                 shard = here[0][...]
                 if len(here) == 2:
                     shard = jnp.where(end, shard, here[1][...])
-                total_ref[...] += jnp.dot(
-                    grads_ref[...], shard, preferred_element_type=jnp.float32
-                )
+                add_dot(total_ref, grads_ref, shard)
 
         if split:
 
@@ -165,46 +171,64 @@
     )(flags, *operands)
 
 
-def partner_dots(flags, pieces, shards, wanted, depth, tail=None):
+def partner_dots(flags, pieces, shards, wanted, depth, tail=(), grads=None):
     cols = shards[0][0].shape[1]
     step = depth // STEPS
     count = len(pieces)
     width = len(wanted) * TILE
-    tok = 0 if tail is None else tail[0].shape[0]
-
-    def at(row):
-        return lambda i, flags_ref: (row + i, 0)
+    tok = grads.shape[0] if tail else 0
+
+    def at(row, wanted_at=None):
+        def index(i, flags_ref):
+            if wanted_at is not None:
+                i = i * (flags_ref[0] if wanted_at else 1 - flags_ref[0])
+            return (row + i, 0)
+
+        return index
 
     operands, specs = [], []
     for array, row in list(pieces) + list(shards):
         operands.append(array)
         specs.append(pl.BlockSpec((step, cols), at(row)))
     whole = lambda i, flags_ref: (0, 0)
-    if tail is not None:
-        grads, at_end, at_middle, first, start = tail
-        operands += [grads, grads, at_end, at_middle, first[0], start]
-        specs.append(pl.BlockSpec((tok, step), lambda i, flags_ref: (0, 2 * STEPS + i)))
-        specs.append(pl.BlockSpec((tok, step), lambda i, flags_ref: (0, i * (1 - flags_ref[0]))))
-        specs.append(pl.BlockSpec((step, cols), lambda i, flags_ref: (i * flags_ref[0], 0)))
-        specs.append(pl.BlockSpec((step, cols), lambda i, flags_ref: (i * (1 - flags_ref[0]), 0)))
-        specs.append(pl.BlockSpec((step, cols), at(first[1])))
-        specs.append(pl.BlockSpec((tok, cols), whole))
+    for choices, column, only in tail:
+        operands.append(grads)
+        specs.append(
+            pl.BlockSpec((tok, step), lambda i, flags_ref, column=column: (0, column + i))
+        )
+        for which, (array, row) in enumerate(choices):
+            operands.append(array)
+            specs.append(
+                pl.BlockSpec((step, cols), at(row, None if len(choices) == 1 else which == 0))
+            )
 
     def kernel(flags_ref, *refs):
         i = pl.program_id(0)
         piece_refs, shard_refs = refs[:count], refs[count : count + len(shards)]
-        refs = refs[count + len(shards) :]
-        if tail is not None:
-            grads_ref, first_grads_ref, end_ref, middle_ref, first_ref, start_ref = refs[:6]
-            keep_ref, give_ref, sums_ref, turned_ref, total_ref, wide_ref = refs[6:]
+        tail_refs = refs[count + len(shards) : len(operands)]
+        refs = refs[len(operands) :]
+        if tail:
+            keep_ref, give_ref, sums_ref, turned_ref, total_ref, wide_ref = refs
         else:
             keep_ref, give_ref, sums_ref, turned_ref = refs
 
         @pl.when(i == 0)
         def begin():
             sums_ref[...] = jnp.zeros_like(sums_ref)
-            if tail is not None:
-                total_ref[...] = start_ref[...]
+            if tail:
+                total_ref[...] = jnp.zeros_like(total_ref)
+
+        at = 0
+        for choices, column, only in tail:
+            grads_ref, here = tail_refs[at], tail_refs[at + 1 : at + 1 + len(choices)]
+            at += 1 + len(choices)
+
+            @pl.when((flags_ref[0] == 0) | (not only))
+            def add(grads_ref=grads_ref, here=here):
+                shard = here[0][...]
+                if len(here) == 2:
+                    shard = jnp.where(flags_ref[0] == 1, shard, here[1][...])
+                add_dot(total_ref, grads_ref, shard)
 
         @pl.when(flags_ref[0] == 0)
         def at_a_middle_plane():
@@ -217,18 +241,10 @@
                         sums_ref[block] += jnp.dot(
                             tokens, shard_refs[shard][...], preferred_element_type=jnp.float32
                         )
-            if tail is not None:
-                total_ref[...] += jnp.dot(
-                    first_grads_ref[...], first_ref[...], preferred_element_type=jnp.float32
-                )
-
-        if tail is not None:
-            shard = jnp.where(flags_ref[0] == 1, end_ref[...], middle_ref[...])
-            total_ref[...] += jnp.dot(grads_ref[...], shard, preferred_element_type=jnp.float32)
 
         @pl.when(i == STEPS - 1)
         def finish():
-            if tail is not None:
+            if tail:
                 wide_ref[...] = total_ref[...].T
                 split_rows(wide_ref, keep_ref, give_ref, flags_ref[1], pl.ds(0, tok))
             for block in range(len(wanted)):
@@ -240,7 +256,7 @@
         pltpu.VMEM((len(wanted), TILE, cols), jnp.float32),
         pltpu.VMEM((cols, TILE), jnp.float32),
     ]
-    if tail is not None:
+    if tail:
         scratch += [pltpu.VMEM((tok, cols), jnp.float32), pltpu.VMEM((cols, tok), jnp.float32)]
     return pl.pallas_call(
         kernel,
@@ -259,19 +275,28 @@
 
 def stack_blocks(flags, grads, depth):
     tiles = grads.shape[0] // TILE
-
-    def kernel(flags_ref, grads_ref, out_ref):
-        for q in range(depth // TILE):
-            out_ref[q * TILE : (q + 1) * TILE, :] = grads_ref[:, q * TILE : (q + 1) * TILE]
+    half = tiles // 2
+
+    def kernel(flags_ref, grads_ref, first_ref, second_ref):
+        for at, out_ref in enumerate((first_ref, second_ref)):
+
+            @pl.when(pl.program_id(0) // half == at)
+            def copy(out_ref=out_ref):
+                for q in range(depth // TILE):
+                    here = slice(q * TILE, (q + 1) * TILE)
+                    out_ref[here, :] = grads_ref[:, here]
 
     return pl.pallas_call(
         kernel,
-        out_shape=jax.ShapeDtypeStruct((tiles * depth, TILE), grads.dtype),
+        out_shape=[jax.ShapeDtypeStruct((half * depth, TILE), grads.dtype)] * 2,
         grid_spec=pltpu.PrefetchScalarGridSpec(
             num_scalar_prefetch=1,
             grid=(tiles,),
             in_specs=[pl.BlockSpec((TILE, depth), lambda t, flags_ref: (t, 0))],
-            out_specs=pl.BlockSpec((depth, TILE), lambda t, flags_ref: (t, 0)),
+            out_specs=[
+                pl.BlockSpec((depth, TILE), lambda t, flags_ref: (jnp.minimum(t, half - 1), 0)),
+                pl.BlockSpec((depth, TILE), lambda t, flags_ref: (jnp.maximum(t - half, 0), 0)),
+            ],
         ),
         compiler_params=pltpu.CompilerParams(vmem_limit_bytes=16 << 20),
         cost_estimate=SHORT,
@@ -354,26 +379,27 @@
     s0 = lax.ppermute(basis_in, "cand", SIDE)
     m0 = middle(basis_in)
     s12 = lax.ppermute(rows, "cand", SIDE)
-    late_rows = basis_out[depth:]
-    m23 = middle(late_rows)
-    started = after(flags, rows, late_rows)
-    stacked = stack_blocks(started, grads, depth)
+    second = basis_out[depth : 2 * depth]
+    m2 = middle(second)
+    started = after(flags, rows, second)
+    stacked, more_stacked = stack_blocks(started, grads, depth)
     part_own = feature_dots(started, grads, [([(basis_out, 0)], 0, 0, 3 * STEPS, False)])
     precond = (test_grads.astype(jnp.float32) / (eigval + damping)).astype(jnp.bfloat16)
-    m1 = middle(after(s0, m0, precond, stacked, *part_own))
+    m1 = middle(after(s0, m0, precond, stacked, more_stacked, *part_own))
     third = jnp.concatenate([basis_out[2 * depth :], basis_out[: 2 * rows_in - depth]])
     s3 = side(third, jnp.concatenate([m0, m1]))
+    m3 = middle(after(basis_out[2 * depth :], m1, m2))
     m5 = middle(s12[depth:])
-    s45 = side(stacked[: 2 * depth], after(m23, s12))
-    to_m6 = s3[:depth]
-    m6 = middle(to_m6)
+    to_s45 = pick(stacked, jnp.concatenate([m2, m3]))
+    s45 = lax.ppermute(after(to_s45, s3), "cand", SIDE)
+    m6 = middle(s3[:depth])
     m4 = middle(after(basis_out[:depth], m5))
-    s6 = side(after(stacked[2 * depth : 3 * depth], s3), m5)
+    to_s67 = pick(more_stacked, jnp.concatenate([m5, m6]))
+    s67 = lax.ppermute(to_s67, "cand", SIDE)
     m7 = middle(after(s12[:depth], m6))
-    s7 = side(after(stacked[3 * depth :], s45), m6)
 
     part_in = input_dots(
-        after(flags, to_m6),
+        after(flags, s3, m5),
         acts,
         [[(basis_in, 0)], [(s0, 0)], [(s3, 0), (m0, 0)], [(s3, 1), (m1, 0)]],
     )
@@ -385,43 +411,46 @@
             ([(s3, 0)], 2 * STEPS, 2 * STEPS, STEPS, True),
         ],
     )
-    rot_in = gather_rows(scatter_sum(*after(part_in, s45)).astype(jnp.bfloat16))
+    rot_in = gather_rows(scatter_sum(*after(part_in, s45, to_s67)).astype(jnp.bfloat16))
     rot_in = rot_in.reshape(tiles_here, TILE, 4 * cols)
-    sums = [jnp.concatenate(parts, axis=1) for parts in zip(part_own, part_a)]
-    sums = scatter_sum(*after(sums, s45))
-    sum_own, sum_a = sums[:, :tok_rows], sums[:, tok_rows:]
     part_b = feature_dots(
-        after(flags, rot_in, sums),
+        after(flags, *part_a, s45, to_s67),
         grads,
         [
-            ([(s45, 0), (m23, 0)], STEPS, STEPS, 2 * STEPS, False),
+            ([(s45, 0), (m2, 0)], STEPS, STEPS, STEPS, False),
+            ([(s45, STEPS), (m3, 0)], 2 * STEPS, 2 * STEPS, STEPS, False),
             ([(m4, 0)], 0, 0, STEPS, True),
         ],
     )
-    part_c = feature_dots(
-        after(flags, *part_b),
+    shards = [(basis_out, 0), (m4, 0), (m7, 0)]
+    pieces = [(s45, 0), (s45, STEPS), (s67, 0), (s67, STEPS)]
+    early = [(shard, piece) for shard in range(2) for piece in range(2)]
+    part_early = partner_dots(after(flags, *part_b), pieces[:2], shards[:2], early, depth)
+    late = [(2, 0), (2, 1)] + [(shard, piece) for shard in range(3) for piece in (2, 3)]
+    parts = [part_own, part_a, part_b, part_early]
+    sums = scatter_sum(*[jnp.concatenate(part, axis=1) for part in zip(*parts)])
+    part_late = partner_dots(
+        after(flags, sums),
+        pieces,
+        shards,
+        late,
+        depth,
+        [
+            ([(s67, 0), (m5, 0)], STEPS, False),
+            ([(s67, STEPS), (m6, 0)], 2 * STEPS, False),
+            ([(m7, 0)], 0, True),
+        ],
         grads,
-        [([(s6, 0), (m5, 0)], STEPS, STEPS, STEPS, False)],
-        split=False,
-    )
-    shards = [(basis_out, 0), (m4, 0), (m7, 0)]
-    pieces = [(s45, 0), (s45, STEPS), (s6, 0), (s7, 0)]
-    early = [(shard, piece) for shard in range(2) for piece in range(3)]
-    part_early = partner_dots(after(flags, part_c), pieces[:3], shards[:2], early, depth)
-    late = [(2, 0), (2, 1), (2, 2), (0, 3), (1, 3), (2, 3)]
-    part_late = partner_dots(
-        after(flags, *part_early), pieces, shards, late, depth, (grads, s7, m6, (m7, 0), part_c)
-    )
-    sums = scatter_sum(*[jnp.concatenate(parts, axis=1) for parts in zip(part_b, part_early)])
-    sum_b = sums[:, :tok_rows]
+    )
+    sum_own, sum_a, sum_b = [sums[:, i * tok_rows : (i + 1) * tok_rows] for i in range(3)]
+    back_early = jnp.where(end, lax.ppermute(sums[:, 3 * tok_rows :], "cand", SIDE), 0.0)
     sum_late = scatter_sum(*part_late)
     sum_c = sum_late[:, :tok_rows]
-    back_early = jnp.where(end, lax.ppermute(sums[:, tok_rows:], "cand", SIDE), 0.0)
     back_late = jnp.where(end, lax.ppermute(sum_late[:, tok_rows:], "cand", SIDE), 0.0)
-    few = 3 * TILE
-    back_a = jnp.concatenate([back_early[:, :few], back_late[:, few : few + TILE]], axis=1)
-    back_b = jnp.concatenate([back_early[:, few:], back_late[:, few + TILE : few + 2 * TILE]], axis=1)
-    back_c = jnp.concatenate([back_late[:, :few], back_late[:, few + 2 * TILE :]], axis=1)
+    two = 2 * TILE
+    back_a = jnp.concatenate([back_early[:, :two], back_late[:, two : 2 * two]], axis=1)
+    back_b = jnp.concatenate([back_early[:, two:], back_late[:, 2 * two : 3 * two]], axis=1)
+    back_c = jnp.concatenate([back_late[:, :two], back_late[:, 3 * two :]], axis=1)
 
     rowmask, ignored = tile_layout(pair_tiles, last_rows, plane * tiles_here, tiles_here, TILE)
     keep = rowmask.reshape(1, tok_rows).astype(jnp.bfloat16)

time: 182 us -> 185 us (1.016)
  other arithmetic: 9.52 us -> 15.6 us
  waiting for transfers between devices: 63.3 us -> 59 us
    ppermute x1 -> x3, waiting for transfers between devices: 2.54 us -> 28.9 us  [the longest x1 14.4 us: line_plan(): s67 = lax.ppermute(to_s67, 'cand', SIDE)]
    ppermute x4 -> x1, waiting for transfers between devices: 35.9 us -> 11 us  [side(): return lax.ppermute(pick(at_end, at_middle), 'cand', SIDE)]
    ppermute x1 -> x3, starting transfers between devices: 2.66 us -> 17.6 us  [the longest x1 10.9 us: line_plan(): s67 = lax.ppermute(to_s67, 'cand', SIDE)]
    ppermute x4 -> x1, starting transfers between devices: 18.5 us -> 8.94 us  [side(): return lax.ppermute(pick(at_end, at_middle), 'cand', SIDE)]
    ppermute x1, waiting for transfers between devices: 8.52 us -> 0.3 us  [line_plan(): s12 = lax.ppermute(rows, 'cand', SIDE)]
    slice x7 -> x4, local copies, waits for them, and re-layouts: 4.48 us -> 0.06 us  [the longest x1 0.04 us: line_plan(): m6 = middle(s3[:depth])]
    ppermute x1, waiting for transfers between devices: 0.01 us -> 3.62 us  [line_plan(): lax.ppermute(sum_late[:, tok_rows:], 'cand', SIDE)]
    ppermute x1, starting transfers between devices: 3.93 us -> 1.25 us  [line_plan(): lax.ppermute(sum_late[:, tok_rows:], 'cand', SIDE)]
  transfers between devices with their start and end apart: 28 -> 26, of which waited for: 10 -> 10; matrix products, arithmetic and copies ran while one was open for 13% -> 16% of each run, Pallas kernels for 12% -> 11%
where the time goes in v5:
time: 185 us; the launch traced here: 184 us
  waiting for transfers between devices  59 us (32%)
  starting transfers between devices  43.3 us (23%)
  Pallas kernels  25.8 us (14%)
  local copies, waits for them, and re-layouts  18.2 us (10%)
  other arithmetic  15.6 us (8%)
  matrix products  10.7 us (6%)
  blocking collectives  10.6 us (6%)
    ppermute x1, waiting for transfers between devices, line_plan(): s67 = lax.ppermute(to_s67, 'cand', SIDE)  14.4 us
    pallas_call x3, Pallas kernels, feature_dots(): pl.pallas_call(kernel, out_shape=out_shape, grid_spec=pltpu.PrefetchScala...  14.2 us
    ppermute x1, waiting for transfers between devices, line_plan(): s45 = lax.ppermute(after(to_s45, s3), 'cand', SIDE)  13.4 us
    unnamed x84, local copies, waits for them, and re-layouts  12.1 us
    ppermute x1, waiting for transfers between devices, side(): return lax.ppermute(pick(at_end, at_middle), 'cand', SIDE)  11 us
    ppermute x1, starting transfers between devices, line_plan(): s67 = lax.ppermute(to_s67, 'cand', SIDE)  10.9 us
    all_to_all x1, blocking collectives, final_sum(): return jnp.sum(lax.all_to_all(blocks, ALL, 0, 0, tiled=True), axis=0)  10.6 us
    ppermute x8, waiting for transfers between devices, swap(): return lax.ppermute(x, axis_name, [(0, 1), (1, 0)])  10.6 us
  transfers between devices with their start and end apart: 26, of which 10 were waited for; matrix products, arithmetic and copies ran while one was open for 16% of the time, Pallas kernels for 11%

profile of v5, /device:TPU:0, one launch (start us, length us, event | category | flops | bytes accessed | tf_op | source)
XLA Modules:
  0.0 183.9 jit_solution(17909960652251720304)
XLA Ops:
  0.5 4.1 %collective-permute-start.1 = (bf16[1280,128]{1,0:T(8,128)(2,1)}, bf16[1280,128]{1,0:T(8,128)(2,1)}, u32[]{:S(2)}, u32[]{:S(2)}) collective-permute-start(bf16[1280,128]{1,0:T(8,128)(2,1)} %refs_0_.3), channel_id=1, source_target_pairs={{0,4},{4,0},{8,12},{12,8},{1,5},{5,1},{9,13},{13,9},{2,6},{6,2},{1... | collective-permute-start | bytes 983048 | tf_op jit(solution)/shard_map/ppermute | solution.py:379
  8.3 3.5 %divide_convert_fusion = bf16[64,32,512]{2,1,0:T(8,128)(2,1)} fusion(bf16[64,32,512]{2,1,0:T(8,128)(2,1)} %param.13, f32[32,512]{1,0:T(8,128)S(1)} %broadcast_add_fusion), kind=kLoop, calls=%fused_computation | loop fusion | flops 3145728 | bytes 4259840 | tf_op jit(solution)/shard_map/convert_element_type | solution.py:387
  11.9 3.0 %copy-done = bf16[512,6912]{1,0:T(8,128)(2,1)S(1)} copy-done((bf16[512,6912]{1,0:T(8,128)(2,1)S(1)}, bf16[512,6912]{1,0:T(8,128)(2,1)}, u32[]{:S(2)}) %copy-start) | copy-done | bytes 7077912
  18.3 4.6 %shard_map.82 = (f32[64,512]{1,0:T(8,128)S(1)}, f32[64,512]{1,0:T(8,128)S(1)}) custom-call(s32[6]{0:T(128)S(1)} %stack.49.flags_ref, bf16[512,6912]{1,0:T(8,128)(2,1)S(1)} %copy-done, bf16[6912,128]{1,0:T(8,128)(2,1)S(1)} %copy-done.5), custom_call_target="tpu_custom_call" | custom-call | flops 1 | bytes 1 | tf_op jit(solution)/shard_map/pallas_call | solution.py:159
  28.9 8.9 %collective-permute-start.3 = (bf16[2560,128]{1,0:T(8,128)(2,1)S(1)}, bf16[2560,128]{1,0:T(8,128)(2,1)S(1)}, u32[]{:S(2)}, u32[]{:S(2)}) collective-permute-start(bf16[2560,128]{1,0:T(8,128)(2,1)S(1)} %maximum_select_fusion.2), channel_id=1, source_target_pairs={{0,4},{4,0},{8,12},{12,8},{1,5},{5,1},{9,13},{13,9},{2,6},{6,2},{1... | collective-permute-start | bytes 1966088 | tf_op jit(solution)/shard_map/ppermute | solution.py:363
  40.6 11.0 %collective-permute-done.3.refs_2_.refs_4_.refs_1_ = bf16[2560,128]{1,0:T(8,128)(2,1)S(1)} collective-permute-done((bf16[2560,128]{1,0:T(8,128)(2,1)S(1)}, bf16[2560,128]{1,0:T(8,128)(2,1)S(1)}, u32[]{:S(2)}, u32[]{:S(2)}) %collective-permute-start.3) | collective-permute-done | bytes 655392 | tf_op jit(solution)/shard_map/ppermute | solution.py:363
  52.1 2.5 %collective-permute-start.8 = (bf16[4608,128]{1,0:T(8,128)(2,1)S(1)}, bf16[4608,128]{1,0:T(8,128)(2,1)S(1)}, u32[]{:S(2)}, u32[]{:S(2)}) collective-permute-start(bf16[4608,128]{1,0:T(8,128)(2,1)S(1)} %maximum_select_fusion), channel_id=1, source_target_pairs={{0,4},{4,0},{8,12},{12,8},{1,5},{5,1},{9,13},{13,9},{2,6},{6,2},{1... | collective-permute-start | bytes 3538952 | tf_op jit(solution)/shard_map/ppermute | solution.py:394
  54.7 4.7 %shard_map.84 = (f32[256,512]{1,0:T(8,128)S(1)}, f32[256,512]{1,0:T(8,128)}) custom-call(s32[6]{0:T(128)S(1)} %stack.49.flags_ref, bf16[512,1280]{1,0:T(8,128)(2,1)S(1)} %copy-done.14, bf16[1280,128]{1,0:T(8,128)(2,1)S(1)} %copy-done.20, bf16[1280,128]{1,0:T(8,128)(2,1)} %collective-permute-done.1.refs_1_, ...), custom_call_target="tpu_custom_call" | custom-call | flops 1 | bytes 1 | tf_op jit(solution)/shard_map/pallas_call | solution.py:334
  60.1 5.6 %shard_map.85 = (f32[64,512]{1,0:T(8,128)S(1)}, f32[64,512]{1,0:T(8,128)S(1)}) custom-call(s32[6]{0:T(128)S(1)} %stack.49.flags_ref, bf16[512,6912]{1,0:T(8,128)(2,1)S(1)} %bitcast.56, bf16[4608,128]{1,0:T(8,128)(2,1)} %collective-permute-done.4.refs_0_, bf16[2560,128]{1,0:T(8,128)(2,1)S(1)} %collective-permute-done.3.refs_2_.refs_4_.refs_1_), custom_call_target="tpu_custom_call" | custom-call | flops 1 | bytes 1 | tf_op jit(solution)/shard_map/pallas_call | solution.py:159
  67.2 13.4 %collective-permute-done.8.refs_0_.refs_2_.refs_1_ = bf16[4608,128]{1,0:T(8,128)(2,1)S(1)} collective-permute-done((bf16[4608,128]{1,0:T(8,128)(2,1)S(1)}, bf16[4608,128]{1,0:T(8,128)(2,1)S(1)}, u32[]{:S(2)}, u32[]{:S(2)}) %collective-permute-start.8) | collective-permute-done | bytes 1179680 | tf_op jit(solution)/shard_map/ppermute | solution.py:394
  80.5 3.9 %shard_map.86 = (f32[64,512]{1,0:T(8,128)S(1)}, f32[64,512]{1,0:T(8,128)S(1)}) custom-call(s32[6]{0:T(128)S(1)} %stack.49.flags_ref, bf16[512,6912]{1,0:T(8,128)(2,1)S(1)} %bitcast.56, bf16[4608,128]{1,0:T(8,128)(2,1)S(1)} %collective-permute-done.8.refs_0_.refs_2_.refs_1_, bf16[2304,128]{1,0:T(8,128)(2,1)S(1)} %copy-done.9, ...), custom_call_target="tpu_custom_call" | custom-call | flops 1 | bytes 1 | tf_op jit(solution)/shard_map/pallas_call | solution.py:159
  87.5 10.9 %collective-permute-start.18 = (bf16[4608,128]{1,0:T(8,128)(2,1)}, bf16[4608,128]{1,0:T(8,128)(2,1)}, u32[]{:S(2)}, u32[]{:S(2)}) collective-permute-start(bf16[4608,128]{1,0:T(8,128)(2,1)} %maximum_select_fusion.1), channel_id=1, source_target_pairs={{0,4},{4,0},{8,12},{12,8},{1,5},{5,1},{9,13},{13,9},{2,6},{6,2},{1... | collective-permute-start | bytes 3538952 | tf_op jit(solution)/shard_map/ppermute | solution.py:398
  104.5 5.2 %collective-permute-done.12 = f32[32,2048]{1,0:T(8,128)} collective-permute-done((f32[32,2048]{1,0:T(8,128)}, f32[32,2048]{1,0:T(8,128)}, u32[]{:S(2)}, u32[]{:S(2)}) %collective-permute-start.12) | collective-permute-done | bytes 262176 | tf_op jit(solution)/shard_map/ppermute | solution.py:37
  110.9 14.4 %collective-permute-done.18.refs_2_.refs_3_.refs_8_.refs_11_ = bf16[4608,128]{1,0:T(8,128)(2,1)} collective-permute-done((bf16[4608,128]{1,0:T(8,128)(2,1)}, bf16[4608,128]{1,0:T(8,128)(2,1)}, u32[]{:S(2)}, u32[]{:S(2)}) %collective-permute-start.18) | collective-permute-done | bytes 1179680 | tf_op jit(solution)/shard_map/ppermute | solution.py:398
  125.3 3.0 %copy-done.1 = bf16[512,6912]{1,0:T(8,128)(2,1)S(1)} copy-done((bf16[512,6912]{1,0:T(8,128)(2,1)S(1)}, bf16[512,6912]{1,0:T(8,128)(2,1)}, u32[]{:S(2)}) %copy-start.1) | copy-done | bytes 7077912
  128.3 4.8 %shard_map.88 = (f32[64,1536]{1,0:T(8,128)S(1)}, f32[64,1536]{1,0:T(8,128)S(1)}) custom-call(s32[6]{0:T(128)S(1)} %stack.49.flags_ref, bf16[4608,128]{1,0:T(8,128)(2,1)S(1)} %copy-done.3, bf16[4608,128]{1,0:T(8,128)(2,1)S(1)} %copy-done.3, bf16[4608,128]{1,0:T(8,128)(2,1)} %collective-permute-done.18.refs_2_.refs_3_.refs_8_.refs_11_, ...), custom_call_target="tpu_custom_call" | custom-call | flops 1 | bytes 1 | tf_op jit(solution)/shard_map/pallas_call | solution.py:261
  133.3 4.1 %collective-permute-start.17 = (f32[32,512]{1,0:T(8,128)S(1)}, f32[32,512]{1,0:T(8,128)S(1)}, u32[]{:S(2)}, u32[]{:S(2)}) collective-permute-start(f32[32,512]{1,0:T(8,128)S(1)} %slice.82), channel_id=1, source_target_pairs={{0,4},{4,0},{8,12},{12,8},{1,5},{5,1},{9,13},{13,9},{2,6},{6,2},{1... | collective-permute-start | bytes 196616 | tf_op jit(solution)/shard_map/ppermute | solution.py:446
  143.6 3.8 %collective-permute-done.21 = f32[32,1536]{1,0:T(8,128)S(1)} collective-permute-done((f32[32,1536]{1,0:T(8,128)S(1)}, f32[32,1536]{1,0:T(8,128)S(1)}, u32[]{:S(2)}, u32[]{:S(2)}) %collective-permute-start.21) | collective-permute-done | bytes 196640 | tf_op jit(solution)/shard_map/ppermute | solution.py:37
  148.8 3.6 %collective-permute-done.22 = f32[32,1024]{1,0:T(8,128)S(1)} collective-permute-done((f32[32,1024]{1,0:T(8,128)S(1)}, f32[32,1024]{1,0:T(8,128)S(1)}, u32[]{:S(2)}, u32[]{:S(2)}) %collective-permute-start.22) | collective-permute-done | bytes 131104 | tf_op jit(solution)/shard_map/ppermute | solution.py:449
  154.6 2.5 %fusion.8 = f32[4,64]{1,0:T(4,128)S(1)} fusion(bf16[64,32,512]{2,1,0:T(8,128)(2,1)S(1)} %copy-done.31, bf16[4,32,512]{2,1,0:T(8,128)(2,1)S(1)} %convolution_convert_fusion.3), kind=kOutput, calls=%fused_computation.15 | convolution fusion | flops 8388608 | bytes 2229248 | tf_op jit(solution)/shard_map/tea,jea->tj/dot_general | solution.py:467
  160.4 2.5 %fusion.11 = f32[4,64]{1,0:T(4,128)S(1)} fusion(bf16[64,32,512]{2,1,0:T(8,128)(2,1)S(1)} %copy-done.31, bf16[4,32,512]{2,1,0:T(8,128)(2,1)S(1)} %collective-permute-done.23), kind=kOutput, calls=%fused_computation.16 | convolution fusion | flops 8388608 | bytes 2229248 | tf_op jit(solution)/shard_map/tea,jea->tj/dot_general | solution.py:467
  162.9 4.5 %collective-permute-done.24 = bf16[4,32,512]{2,1,0:T(8,128)(2,1)S(1)} collective-permute-done((bf16[4,32,512]{2,1,0:T(8,128)(2,1)S(1)}, bf16[4,32,512]{2,1,0:T(8,128)(2,1)S(1)}, u32[]{:S(2)}, u32[]{:S(2)}) %collective-permute-start.24) | collective-permute-done | bytes 131104 | tf_op jit(solution)/shard_map/ppermute | solution.py:478
  170.0 2.5 %fusion.17 = f32[4,64]{1,0:T(4,128)S(1)} fusion(bf16[64,32,512]{2,1,0:T(8,128)(2,1)S(1)} %copy-done.31, bf16[4,32,512]{2,1,0:T(8,128)(2,1)S(1)} %collective-permute-done.25), kind=kOutput, calls=%fused_computation.18 | convolution fusion | flops 8388608 | bytes 2229248 | tf_op jit(solution)/shard_map/tea,jea->tj/dot_general | solution.py:467
  172.7 10.6 %all_to_all.5 = f32[16,2,16]{2,1,0:T(2,128)S(1)} all-to-all(f32[16,2,16]{2,1,0:T(2,128)S(1)} %copy.69), channel_id=1, replica_groups=mesh['groups'=2,'cand'=4,'eig'=2,'rep'=2] {'cand','eig','rep'}, dimensions={0} | all-to-all | bytes 4096 | tf_op jit(solution)/shard_map/all_to_all | solution.py:487
  (184 shorter events, 45.4 us)
Async XLA Ops:
  0.0 24.7 %collective-permute-start = (bf16[1280,128]{1,0:T(8,128)(2,1)}, bf16[1280,128]{1,0:T(8,128)(2,1)}, u32[]{:S(2)}, u32[]{:S(2)}) collective-permute-start(bf16[1280,128]{1,0:T(8,128)(2,1)} %refs_0_.3), channel_id=1, source_target_pairs={{0,1},{1,0},{2,3},{3,2},{4,8},{5,9},{6,10},{7,11},{8,4},{9,5},{10,... | collective-permute-start | bytes 983048 | tf_op jit(solution)/shard_map/ppermute | solution.py:371
  0.5 24.2 %collective-permute-start.1 = (bf16[1280,128]{1,0:T(8,128)(2,1)}, bf16[1280,128]{1,0:T(8,128)(2,1)}, u32[]{:S(2)}, u32[]{:S(2)}) collective-permute-start(bf16[1280,128]{1,0:T(8,128)(2,1)} %refs_0_.3), channel_id=1, source_target_pairs={{0,4},{4,0},{8,12},{12,8},{1,5},{5,1},{9,13},{13,9},{2,6},{6,2},{1... | collective-permute-start | bytes 983048 | tf_op jit(solution)/shard_map/ppermute | solution.py:379
  7.0 31.2 %collective-permute-start.4 = (bf16[4608,128]{1,0:T(8,128)(2,1)}, bf16[4608,128]{1,0:T(8,128)(2,1)}, u32[]{:S(2)}, u32[]{:S(2)}) collective-permute-start(bf16[4608,128]{1,0:T(8,128)(2,1)} %constant_dynamic-slice_fusion), channel_id=1, source_target_pairs={{0,4},{4,0},{8,12},{12,8},{1,5},{5,1},{9,13},{13,9},{2,6},{6,2},{1... | collective-permute-start | bytes 3538952 | tf_op jit(solution)/shard_map/ppermute | solution.py:381
  8.3 29.5 %collective-permute-start.6 = (bf16[2304,128]{1,0:T(8,128)(2,1)}, bf16[2304,128]{1,0:T(8,128)(2,1)S(1)}, u32[]{:S(2)}, u32[]{:S(2)}) collective-permute-start(bf16[2304,128]{1,0:T(8,128)(2,1)} %get-tuple-element.66), channel_id=1, source_target_pairs={{0,1},{1,0},{2,3},{3,2},{4,8},{5,9},{6,10},{7,11},{8,4},{9,5},{10,... | collective-permute-start | bytes 1769480 | tf_op jit(solution)/shard_map/ppermute | solution.py:371
  28.9 22.7 %collective-permute-start.3 = (bf16[2560,128]{1,0:T(8,128)(2,1)S(1)}, bf16[2560,128]{1,0:T(8,128)(2,1)S(1)}, u32[]{:S(2)}, u32[]{:S(2)}) collective-permute-start(bf16[2560,128]{1,0:T(8,128)(2,1)S(1)} %maximum_select_fusion.2), channel_id=1, source_target_pairs={{0,4},{4,0},{8,12},{12,8},{1,5},{5,1},{9,13},{13,9},{2,6},{6,2},{1... | collective-permute-start | bytes 1966088 | tf_op jit(solution)/shard_map/ppermute | solution.py:363
  37.8 13.9 %collective-permute-start.7 = (bf16[2304,128]{1,0:T(8,128)(2,1)S(1)}, bf16[2304,128]{1,0:T(8,128)(2,1)S(1)}, u32[]{:S(2)}, u32[]{:S(2)}) collective-permute-start(bf16[2304,128]{1,0:T(8,128)(2,1)S(1)} %copy-done.30), channel_id=1, source_target_pairs={{0,1},{1,0},{2,3},{3,2},{4,8},{5,9},{6,10},{7,11},{8,4},{9,5},{10,... | collective-permute-start | bytes 1769480 | tf_op jit(solution)/shard_map/ppermute | solution.py:371
  40.4 14.3 %collective-permute-start.5 = (bf16[2304,128]{1,0:T(8,128)(2,1)S(1)}, bf16[2304,128]{1,0:T(8,128)(2,1)S(1)}, u32[]{:S(2)}, u32[]{:S(2)}) collective-permute-start(bf16[2304,128]{1,0:T(8,128)(2,1)S(1)} %get-tuple-element.68), channel_id=1, source_target_pairs={{0,1},{1,0},{2,3},{3,2},{4,8},{5,9},{6,10},{7,11},{8,4},{9,5},{10,... | collective-permute-start | bytes 1769480 | tf_op jit(solution)/shard_map/ppermute | solution.py:371
  51.6 14.2 %collective-permute-start.9 = (bf16[2304,128]{1,0:T(8,128)(2,1)S(1)}, bf16[2304,128]{1,0:T(8,128)(2,1)S(1)}, u32[]{:S(2)}, u32[]{:S(2)}) collective-permute-start(bf16[2304,128]{1,0:T(8,128)(2,1)S(1)} %slice.79), channel_id=1, source_target_pairs={{0,1},{1,0},{2,3},{3,2},{4,8},{5,9},{6,10},{7,11},{8,4},{9,5},{10,... | collective-permute-start | bytes 1769480 | tf_op jit(solution)/shard_map/ppermute | solution.py:371
  52.1 28.4 %collective-permute-start.8 = (bf16[4608,128]{1,0:T(8,128)(2,1)S(1)}, bf16[4608,128]{1,0:T(8,128)(2,1)S(1)}, u32[]{:S(2)}, u32[]{:S(2)}) collective-permute-start(bf16[4608,128]{1,0:T(8,128)(2,1)S(1)} %maximum_select_fusion), channel_id=1, source_target_pairs={{0,4},{4,0},{8,12},{12,8},{1,5},{5,1},{9,13},{13,9},{2,6},{6,2},{1... | collective-permute-start | bytes 3538952 | tf_op jit(solution)/shard_map/ppermute | solution.py:394
  60.1 20.4 %collective-permute-start.10 = (bf16[2304,128]{1,0:T(8,128)(2,1)S(1)}, bf16[2304,128]{1,0:T(8,128)(2,1)S(1)}, u32[]{:S(2)}, u32[]{:S(2)}) collective-permute-start(bf16[2304,128]{1,0:T(8,128)(2,1)S(1)} %copy-done.32), channel_id=1, source_target_pairs={{0,1},{1,0},{2,3},{3,2},{4,8},{5,9},{6,10},{7,11},{8,4},{9,5},{10,... | collective-permute-start | bytes 1769480 | tf_op jit(solution)/shard_map/ppermute | solution.py:371
  86.1 12.5 %collective-permute-start.11 = (f32[64,2048]{1,0:T(8,128)S(1)}, f32[64,2048]{1,0:T(8,128)S(1)}, u32[]{:S(2)}, u32[]{:S(2)}) collective-permute-start(f32[64,2048]{1,0:T(8,128)S(1)} %pad_maximum_fusion), channel_id=1, source_target_pairs={{0,1},{1,0},{2,3},{3,2},{4,5},{5,4},{6,7},{7,6},{8,9},{9,8},{10,11... | collective-permute-start | bytes 1572872 | tf_op jit(solution)/shard_map/ppermute | solution.py:37
  87.5 37.8 %collective-permute-start.18 = (bf16[4608,128]{1,0:T(8,128)(2,1)}, bf16[4608,128]{1,0:T(8,128)(2,1)}, u32[]{:S(2)}, u32[]{:S(2)}) collective-permute-start(bf16[4608,128]{1,0:T(8,128)(2,1)} %maximum_select_fusion.1), channel_id=1, source_target_pairs={{0,4},{4,0},{8,12},{12,8},{1,5},{5,1},{9,13},{13,9},{2,6},{6,2},{1... | collective-permute-start | bytes 3538952 | tf_op jit(solution)/shard_map/ppermute | solution.py:398
  100.3 9.4 %collective-permute-start.12 = (f32[32,2048]{1,0:T(8,128)}, f32[32,2048]{1,0:T(8,128)}, u32[]{:S(2)}, u32[]{:S(2)}) collective-permute-start(f32[32,2048]{1,0:T(8,128)} %slice_select_fusion.1), channel_id=1, source_target_pairs={{0,2},{2,0},{1,3},{3,1},{4,6},{6,4},{5,7},{7,5},{8,10},{10,8},{9,1... | collective-permute-start | bytes 786440 | tf_op jit(solution)/shard_map/ppermute | solution.py:37
  102.5 8.4 %collective-permute-start.19 = (bf16[2304,128]{1,0:T(8,128)(2,1)}, bf16[2304,128]{1,0:T(8,128)(2,1)S(1)}, u32[]{:S(2)}, u32[]{:S(2)}) collective-permute-start(bf16[2304,128]{1,0:T(8,128)(2,1)} %get-tuple-element.56), channel_id=1, source_target_pairs={{0,1},{1,0},{2,3},{3,2},{4,8},{5,9},{6,10},{7,11},{8,4},{9,5},{10,... | collective-permute-start | bytes 1769480 | tf_op jit(solution)/shard_map/ppermute | solution.py:371
  103.9 33.5 %collective-permute-start.14 = (f32[128,512]{1,0:T(8,128)S(1)}, f32[128,512]{1,0:T(8,128)S(1)}, u32[]{:S(2)}, u32[]{:S(2)}) collective-permute-start(f32[128,512]{1,0:T(8,128)S(1)} %slice_select_fusion), channel_id=1, source_target_pairs={{0,2},{2,0},{1,3},{3,1},{4,6},{6,4},{5,7},{7,5},{8,10},{10,8},{9,1... | collective-permute-start | bytes 786440 | tf_op jit(solution)/shard_map/ppermute | solution.py:37
  133.2 6.9 %collective-permute-start.20 = (f32[64,1536]{1,0:T(8,128)S(1)}, f32[64,1536]{1,0:T(8,128)S(1)}, u32[]{:S(2)}, u32[]{:S(2)}) collective-permute-start(f32[64,1536]{1,0:T(8,128)S(1)} %get-tuple-element.58), channel_id=1, source_target_pairs={{0,1},{1,0},{2,3},{3,2},{4,5},{5,4},{6,7},{7,6},{8,9},{9,8},{10,11... | collective-permute-start | bytes 1179656 | tf_op jit(solution)/shard_map/ppermute | solution.py:37
  133.3 6.8 %collective-permute-start.17 = (f32[32,512]{1,0:T(8,128)S(1)}, f32[32,512]{1,0:T(8,128)S(1)}, u32[]{:S(2)}, u32[]{:S(2)}) collective-permute-start(f32[32,512]{1,0:T(8,128)S(1)} %slice.82), channel_id=1, source_target_pairs={{0,4},{4,0},{8,12},{12,8},{1,5},{5,1},{9,13},{13,9},{2,6},{6,2},{1... | collective-permute-start | bytes 196616 | tf_op jit(solution)/shard_map/ppermute | solution.py:446
  137.5 5.9 %collective-permute-start.15 = (bf16[128,512]{1,0:T(8,128)(2,1)S(1)}, bf16[128,512]{1,0:T(8,128)(2,1)S(1)}, u32[]{:S(2)}, u32[]{:S(2)}) collective-permute-start(bf16[128,512]{1,0:T(8,128)(2,1)S(1)} %add_convert_fusion), channel_id=1, source_target_pairs={{0,2},{2,0},{1,3},{3,1},{4,6},{6,4},{5,7},{7,5},{8,10},{10,8},{9,1... | collective-permute-start | bytes 393224 | tf_op jit(solution)/shard_map/ppermute | solution.py:37
  140.2 7.1 %collective-permute-start.21 = (f32[32,1536]{1,0:T(8,128)S(1)}, f32[32,1536]{1,0:T(8,128)S(1)}, u32[]{:S(2)}, u32[]{:S(2)}) collective-permute-start(f32[32,1536]{1,0:T(8,128)S(1)} %slice_select_fusion.2), channel_id=1, source_target_pairs={{0,2},{2,0},{1,3},{3,1},{4,6},{6,4},{5,7},{7,5},{8,10},{10,8},{9,1... | collective-permute-start | bytes 589832 | tf_op jit(solution)/shard_map/ppermute | solution.py:37
  143.5 5.2 %collective-permute-start.16 = (bf16[2,128,512]{2,1,0:T(8,128)(2,1)S(1)}, bf16[2,128,512]{2,1,0:T(8,128)(2,1)S(1)}, u32[]{:S(2)}, u32[]{:S(2)}) collective-permute-start(bf16[2,128,512]{2,1,0:T(8,128)(2,1)S(1)} %pad_maximum_fusion.2), channel_id=1, source_target_pairs={{0,1},{1,0},{2,3},{3,2},{4,5},{5,4},{6,7},{7,6},{8,9},{9,8},{10,11... | collective-permute-start | bytes 786440 | tf_op jit(solution)/shard_map/ppermute | solution.py:37
  147.4 5.0 %collective-permute-start.22 = (f32[32,1024]{1,0:T(8,128)S(1)}, f32[32,1024]{1,0:T(8,128)S(1)}, u32[]{:S(2)}, u32[]{:S(2)}) collective-permute-start(f32[32,1024]{1,0:T(8,128)S(1)} %slice.85), channel_id=1, source_target_pairs={{0,4},{4,0},{8,12},{12,8},{1,5},{5,1},{9,13},{13,9},{2,6},{6,2},{1... | collective-permute-start | bytes 393224 | tf_op jit(solution)/shard_map/ppermute | solution.py:449
  152.7 7.7 %collective-permute-start.23 = (bf16[4,32,512]{2,1,0:T(8,128)(2,1)S(1)}, bf16[4,32,512]{2,1,0:T(8,128)(2,1)S(1)}, u32[]{:S(2)}, u32[]{:S(2)}) collective-permute-start(bf16[4,32,512]{2,1,0:T(8,128)(2,1)S(1)} %convolution_convert_fusion.2), channel_id=1, source_target_pairs={{0,4},{4,0},{8,12},{12,8},{1,5},{5,1},{9,13},{13,9},{2,6},{6,2},{1... | collective-permute-start | bytes 393224 | tf_op jit(solution)/shard_map/ppermute | solution.py:477
  157.1 10.3 %collective-permute-start.24 = (bf16[4,32,512]{2,1,0:T(8,128)(2,1)S(1)}, bf16[4,32,512]{2,1,0:T(8,128)(2,1)S(1)}, u32[]{:S(2)}, u32[]{:S(2)}) collective-permute-start(bf16[4,32,512]{2,1,0:T(8,128)(2,1)S(1)} %get-tuple-element.74), channel_id=1, source_target_pairs={{0,8},{8,0},{4,12},{12,4},{1,9},{9,1},{5,13},{13,5},{2,10},{10,2},... | collective-permute-start | bytes 393224 | tf_op jit(solution)/shard_map/ppermute | solution.py:478
  158.3 11.8 %collective-permute-start.25 = (bf16[4,32,512]{2,1,0:T(8,128)(2,1)S(1)}, bf16[4,32,512]{2,1,0:T(8,128)(2,1)S(1)}, u32[]{:S(2)}, u32[]{:S(2)}) collective-permute-start(bf16[4,32,512]{2,1,0:T(8,128)(2,1)S(1)} %get-tuple-element.75), channel_id=1, source_target_pairs={{0,12},{12,0},{4,8},{8,4},{1,13},{13,1},{5,9},{9,5},{2,14},{14,2},... | collective-permute-start | bytes 393224 | tf_op jit(solution)/shard_map/ppermute | solution.py:479
  (45 other events, 444.7 us)

commit v6 on v5

--- a/solution.py
+++ b/solution.py
@@ -9,6 +9,7 @@
 FEAT = ("eig", "rep")
 ALL = ("cand", "eig", "rep")
 STEPS = 3
+PARAMS = pltpu.CompilerParams(vmem_limit_bytes=56 << 20)
 SHORT = pl.CostEstimate(flops=1, bytes_accessed=1, transcendentals=0)
 SIDE = ((0, 1), (1, 0), (2, 3), (3, 2))
 TWO = ((0, 2), (2, 0), (1, 3), (3, 1))
@@ -43,8 +44,12 @@
     return jnp.where(first, low, high), jnp.where(first, high, low)
 
 
-def scatter_sum(keep, give):
-    keep, give = halves(keep + swap(give, "rep"), "eig")
+def core_sum(keep, give):
+    return keep + swap(give, "rep")
+
+
+def chip_sum(part):
+    keep, give = halves(part, "eig")
     return keep + swap(give, "eig")
 
 
@@ -166,17 +171,18 @@
             out_specs=out_specs,
             scratch_shapes=scratch,
         ),
-        compiler_params=pltpu.CompilerParams(vmem_limit_bytes=16 << 20),
+        compiler_params=PARAMS,
         cost_estimate=SHORT,
     )(flags, *operands)
 
 
-def partner_dots(flags, pieces, shards, wanted, depth, tail=(), grads=None):
+def partner_dots(flags, pieces, shards, wanted, depth, grads=None, tail=(), start=None):
     cols = shards[0][0].shape[1]
     step = depth // STEPS
     count = len(pieces)
-    width = len(wanted) * TILE
     tok = grads.shape[0] if tail else 0
+    ahead = tok if start is not None else 0
+    width = ahead + len(wanted) * TILE
 
     def at(row, wanted_at=None):
         def index(i, flags_ref):
@@ -201,22 +207,27 @@
             specs.append(
                 pl.BlockSpec((step, cols), at(row, None if len(choices) == 1 else which == 0))
             )
+    if start is not None:
+        operands.append(start)
+        specs.append(pl.BlockSpec((tok, cols), whole))
 
     def kernel(flags_ref, *refs):
         i = pl.program_id(0)
         piece_refs, shard_refs = refs[:count], refs[count : count + len(shards)]
         tail_refs = refs[count + len(shards) : len(operands)]
-        refs = refs[len(operands) :]
-        if tail:
-            keep_ref, give_ref, sums_ref, turned_ref, total_ref, wide_ref = refs
+        keep_ref, give_ref, *rest = refs[len(operands) :]
+        if tail and start is None:
+            total_ref, sums_ref, turned_ref = rest
+        elif tail:
+            sums_ref, turned_ref, total_ref, wide_ref = rest
         else:
-            keep_ref, give_ref, sums_ref, turned_ref = refs
+            sums_ref, turned_ref = rest
 
         @pl.when(i == 0)
         def begin():
             sums_ref[...] = jnp.zeros_like(sums_ref)
             if tail:
-                total_ref[...] = jnp.zeros_like(total_ref)
+                total_ref[...] = jnp.zeros_like(total_ref) if start is None else tail_refs[-1][...]
 
         at = 0
         for choices, column, only in tail:
@@ -244,61 +255,71 @@
 
         @pl.when(i == STEPS - 1)
         def finish():
-            if tail:
+            if ahead:
                 wide_ref[...] = total_ref[...].T
                 split_rows(wide_ref, keep_ref, give_ref, flags_ref[1], pl.ds(0, tok))
             for block in range(len(wanted)):
                 turned_ref[...] = sums_ref[block].T
-                columns = pl.ds(tok + block * TILE, TILE)
+                columns = pl.ds(ahead + block * TILE, TILE)
                 split_rows(turned_ref, keep_ref, give_ref, flags_ref[1], columns)
 
+    out_shape = [jax.ShapeDtypeStruct((cols // 2, width), jnp.float32)] * 2
+    out_specs = [pl.BlockSpec((cols // 2, width), whole)] * 2
     scratch = [
         pltpu.VMEM((len(wanted), TILE, cols), jnp.float32),
         pltpu.VMEM((cols, TILE), jnp.float32),
     ]
-    if tail:
+    if tail and start is None:
+        out_shape.append(jax.ShapeDtypeStruct((tok, cols), jnp.float32))
+        out_specs.append(pl.BlockSpec((tok, cols), whole))
+    elif tail:
         scratch += [pltpu.VMEM((tok, cols), jnp.float32), pltpu.VMEM((cols, tok), jnp.float32)]
     return pl.pallas_call(
         kernel,
-        out_shape=[jax.ShapeDtypeStruct((cols // 2, tok + width), jnp.float32)] * 2,
+        out_shape=out_shape,
         grid_spec=pltpu.PrefetchScalarGridSpec(
             num_scalar_prefetch=1,
             grid=(STEPS,),
             in_specs=specs,
-            out_specs=[pl.BlockSpec((cols // 2, tok + width), whole)] * 2,
+            out_specs=out_specs,
             scratch_shapes=scratch,
         ),
-        compiler_params=pltpu.CompilerParams(vmem_limit_bytes=24 << 20),
+        compiler_params=PARAMS,
         cost_estimate=SHORT,
     )(flags, *operands)
 
 
 def stack_blocks(flags, grads, depth):
     tiles = grads.shape[0] // TILE
-    half = tiles // 2
-
-    def kernel(flags_ref, grads_ref, first_ref, second_ref):
-        for at, out_ref in enumerate((first_ref, second_ref)):
-
-            @pl.when(pl.program_id(0) // half == at)
+    firsts = [0] + list(range(tiles // 2, tiles))
+    counts = [tiles // 2] + [1] * (tiles // 2)
+
+    def kernel(flags_ref, grads_ref, *out_refs):
+        t = pl.program_id(0)
+        for first, count, out_ref in zip(firsts, counts, out_refs):
+
+            @pl.when((t >= first) & (t < first + count))
             def copy(out_ref=out_ref):
                 for q in range(depth // TILE):
                     here = slice(q * TILE, (q + 1) * TILE)
                     out_ref[here, :] = grads_ref[:, here]
 
+    def place(first, count):
+        return lambda t, flags_ref: (jnp.clip(t - first, 0, count - 1), 0)
+
     return pl.pallas_call(
         kernel,
-        out_shape=[jax.ShapeDtypeStruct((half * depth, TILE), grads.dtype)] * 2,
+        out_shape=[jax.ShapeDtypeStruct((count * depth, TILE), grads.dtype) for count in counts],
         grid_spec=pltpu.PrefetchScalarGridSpec(
             num_scalar_prefetch=1,
             grid=(tiles,),
             in_specs=[pl.BlockSpec((TILE, depth), lambda t, flags_ref: (t, 0))],
             out_specs=[
-                pl.BlockSpec((depth, TILE), lambda t, flags_ref: (jnp.minimum(t, half - 1), 0)),
-                pl.BlockSpec((depth, TILE), lambda t, flags_ref: (jnp.maximum(t - half, 0), 0)),
+                pl.BlockSpec((depth, TILE), place(first, count))
+                for first, count in zip(firsts, counts)
             ],
         ),
-        compiler_params=pltpu.CompilerParams(vmem_limit_bytes=16 << 20),
+        compiler_params=PARAMS,
         cost_estimate=SHORT,
     )(flags, grads)
 
@@ -341,7 +362,7 @@
             out_specs=[place, place],
             scratch_shapes=[pltpu.VMEM((tok, cols), jnp.float32)],
         ),
-        compiler_params=pltpu.CompilerParams(vmem_limit_bytes=16 << 20),
+        compiler_params=PARAMS,
         cost_estimate=SHORT,
     )(flags, *operands)
 
@@ -382,10 +403,10 @@
     second = basis_out[depth : 2 * depth]
     m2 = middle(second)
     started = after(flags, rows, second)
-    stacked, more_stacked = stack_blocks(started, grads, depth)
+    stacked, *more_stacked = stack_blocks(started, grads, depth)
     part_own = feature_dots(started, grads, [([(basis_out, 0)], 0, 0, 3 * STEPS, False)])
     precond = (test_grads.astype(jnp.float32) / (eigval + damping)).astype(jnp.bfloat16)
-    m1 = middle(after(s0, m0, precond, stacked, more_stacked, *part_own))
+    m1 = middle(after(s0, m0, precond, stacked, *more_stacked, *part_own))
     third = jnp.concatenate([basis_out[2 * depth :], basis_out[: 2 * rows_in - depth]])
     s3 = side(third, jnp.concatenate([m0, m1]))
     m3 = middle(after(basis_out[2 * depth :], m1, m2))
@@ -394,8 +415,8 @@
     s45 = lax.ppermute(after(to_s45, s3), "cand", SIDE)
     m6 = middle(s3[:depth])
     m4 = middle(after(basis_out[:depth], m5))
-    to_s67 = pick(more_stacked, jnp.concatenate([m5, m6]))
-    s67 = lax.ppermute(to_s67, "cand", SIDE)
+    s6 = side(more_stacked[0], m5)
+    s7 = side(after(more_stacked[1], s45), m6)
     m7 = middle(after(s12[:depth], m6))
 
     part_in = input_dots(
@@ -411,10 +432,8 @@
             ([(s3, 0)], 2 * STEPS, 2 * STEPS, STEPS, True),
         ],
     )
-    rot_in = gather_rows(scatter_sum(*after(part_in, s45, to_s67)).astype(jnp.bfloat16))
-    rot_in = rot_in.reshape(tiles_here, TILE, 4 * cols)
     part_b = feature_dots(
-        after(flags, *part_a, s45, to_s67),
+        after(flags, *part_a, s45),
         grads,
         [
             ([(s45, 0), (m2, 0)], STEPS, STEPS, STEPS, False),
@@ -423,34 +442,45 @@
         ],
     )
     shards = [(basis_out, 0), (m4, 0), (m7, 0)]
-    pieces = [(s45, 0), (s45, STEPS), (s67, 0), (s67, STEPS)]
-    early = [(shard, piece) for shard in range(2) for piece in range(2)]
-    part_early = partner_dots(after(flags, *part_b), pieces[:2], shards[:2], early, depth)
-    late = [(2, 0), (2, 1)] + [(shard, piece) for shard in range(3) for piece in (2, 3)]
-    parts = [part_own, part_a, part_b, part_early]
-    sums = scatter_sum(*[jnp.concatenate(part, axis=1) for part in zip(*parts)])
-    part_late = partner_dots(
-        after(flags, sums),
-        pieces,
+    pieces = [(s45, 0), (s45, STEPS), (s6, 0), (s7, 0)]
+    blocks = [(shard, piece) for piece in (0, 1) for shard in (0, 1)]
+    part_first = partner_dots(after(flags, *part_b), pieces[:2], shards[:2], blocks, depth)
+    *part_second, part_c = partner_dots(
+        after(flags, *part_first),
+        pieces[:3],
         shards,
-        late,
+        [(2, 0), (2, 1), (0, 2), (1, 2), (2, 2)],
         depth,
-        [
-            ([(s67, 0), (m5, 0)], STEPS, False),
-            ([(s67, STEPS), (m6, 0)], 2 * STEPS, False),
-            ([(m7, 0)], 0, True),
-        ],
         grads,
-    )
+        [([(s6, 0), (m5, 0)], STEPS, False), ([(m7, 0)], 0, True)],
+    )
+    rot_in = chip_sum(core_sum(*after(part_in, s6, m7)))
+    rot_in = gather_rows(rot_in.astype(jnp.bfloat16))
+    rot_in = rot_in.reshape(tiles_here, TILE, 4 * cols)
+    parts = [part_own, part_a, part_b, part_first]
+    parts = [jnp.concatenate(part, axis=1) for part in zip(*parts)]
+    core_sums = core_sum(*after(parts, s6, m7))
+    sums = chip_sum(jnp.concatenate([core_sums, core_sum(*part_second)], axis=1))
     sum_own, sum_a, sum_b = [sums[:, i * tok_rows : (i + 1) * tok_rows] for i in range(3)]
-    back_early = jnp.where(end, lax.ppermute(sums[:, 3 * tok_rows :], "cand", SIDE), 0.0)
-    sum_late = scatter_sum(*part_late)
-    sum_c = sum_late[:, :tok_rows]
-    back_late = jnp.where(end, lax.ppermute(sum_late[:, tok_rows:], "cand", SIDE), 0.0)
-    two = 2 * TILE
-    back_a = jnp.concatenate([back_early[:, :two], back_late[:, two : 2 * two]], axis=1)
-    back_b = jnp.concatenate([back_early[:, two:], back_late[:, 2 * two : 3 * two]], axis=1)
-    back_c = jnp.concatenate([back_late[:, :two], back_late[:, 3 * two :]], axis=1)
+    part_last = partner_dots(
+        after(flags, part_c, core_sums),
+        pieces[3:],
+        shards,
+        [(0, 0), (1, 0), (2, 0)],
+        depth,
+        grads,
+        [([(s7, 0), (m6, 0)], 2 * STEPS, False)],
+        part_c,
+    )
+    sum_last = chip_sum(core_sum(*part_last))
+    sum_c = sum_last[:, :tok_rows]
+    back = jnp.where(end, lax.ppermute(sums[:, 3 * tok_rows :], "cand", SIDE), 0.0)
+    last = jnp.where(end, lax.ppermute(sum_last[:, tok_rows:], "cand", SIDE), 0.0)
+    back = [back[:, i * TILE : (i + 1) * TILE] for i in range(9)]
+    last = [last[:, i * TILE : (i + 1) * TILE] for i in range(3)]
+    back_a = jnp.concatenate([back[0], back[2], back[6], last[0]], axis=1)
+    back_b = jnp.concatenate([back[1], back[3], back[7], last[1]], axis=1)
+    back_c = jnp.concatenate([back[4], back[5], back[8], last[2]], axis=1)
 
     rowmask, ignored = tile_layout(pair_tiles, last_rows, plane * tiles_here, tiles_here, TILE)
     keep = rowmask.reshape(1, tok_rows).astype(jnp.bfloat16)

time: 185 us -> 188 us (1.016)
  Pallas kernels: 25.8 us -> 55.4 us
  waiting for transfers between devices: 59 us -> 29.8 us
  starting transfers between devices: 43.3 us -> 57.4 us
  local copies, waits for them, and re-layouts: 18.2 us -> 8.34 us
    ppermute x1 -> x3, starting transfers between devices: 8.94 us -> 34 us  [side(): return lax.ppermute(pick(at_end, at_middle), 'cand', SIDE)]
    ppermute x2 -> x1, waiting for transfers between devices: 18 us -> 2.16 us  [line_plan(): lax.ppermute(sum_last[:, tok_rows:], 'cand', SIDE)]
    pallas_call x3 -> x4, Pallas kernels: 6.89 us -> 22.2 us  [the longest x3 17.1 us: partner_dots(): pl.pallas_call(kernel, out_shape=out_shape, grid_spec=pltpu.PrefetchScala...]
    pallas_call x3, Pallas kernels: 14.2 us -> 27.5 us  [feature_dots(): pl.pallas_call(kernel, out_shape=out_shape, grid_spec=pltpu.PrefetchScala...]
    ppermute x1, waiting for transfers between devices: 13.4 us -> 0.73 us  [line_plan(): s45 = lax.ppermute(after(to_s45, s3), 'cand', SIDE)]
    ppermute x2 -> x1, starting transfers between devices: 12.1 us -> 1.89 us  [line_plan(): lax.ppermute(sum_last[:, tok_rows:], 'cand', SIDE)]
    unnamed x84 -> x52, local copies, waits for them, and re-layouts: 12.1 us -> 2.77 us
    ppermute x8 -> x9, waiting for transfers between devices: 10.6 us -> 7.08 us  [swap(): return lax.ppermute(x, axis_name, [(0, 1), (1, 0)])]
  transfers between devices with their start and end apart: 26 -> 28, of which waited for: 10 -> 11; matrix products, arithmetic and copies ran while one was open for 16% -> 15% of each run, Pallas kernels for 11% -> 30%
where the time goes in v6:
time: 188 us; the launch traced here: 187 us
  starting transfers between devices  57.4 us (31%)
  Pallas kernels  55.4 us (29%)
  waiting for transfers between devices  29.8 us (16%)
  other arithmetic  14.5 us (8%)
  matrix products  10.7 us (6%)
  blocking collectives  10.4 us (6%)
  local copies, waits for them, and re-layouts  8.34 us (4%)
    ppermute x3, starting transfers between devices, side(): return lax.ppermute(pick(at_end, at_middle), 'cand', SIDE)  34 us
    pallas_call x3, Pallas kernels, feature_dots(): pl.pallas_call(kernel, out_shape=out_shape, grid_spec=pltpu.PrefetchScala...  27.5 us
    pallas_call x3, Pallas kernels, partner_dots(): pl.pallas_call(kernel, out_shape=out_shape, grid_spec=pltpu.PrefetchScala...  17.1 us
    ppermute x3, waiting for transfers between devices, side(): return lax.ppermute(pick(at_end, at_middle), 'cand', SIDE)  12.1 us
    all_to_all x1, blocking collectives, final_sum(): return jnp.sum(lax.all_to_all(blocks, ALL, 0, 0, tiled=True), axis=0)  10.4 us
    dot_general x4, matrix products, pair_scores(): jnp.einsum('tea,jea->tj', prods, precond, preferred_element_type=jnp.floa...  9.88 us
    ppermute x9, waiting for transfers between devices, swap(): return lax.ppermute(x, axis_name, [(0, 1), (1, 0)])  7.08 us
    ppermute x1, waiting for transfers between devices, line_plan(): lax.ppermute(pick(prods_b, prods_c), 'cand', TWO)  5.93 us
  transfers between devices with their start and end apart: 28, of which 11 were waited for; matrix products, arithmetic and copies ran while one was open for 15% of the time, Pallas kernels for 30%

profile of v6, /device:TPU:0, one launch (start us, length us, event | category | flops | bytes accessed | tf_op | source)
XLA Modules:
  0.0 186.9 jit_solution(13152817778396004316)
XLA Ops:
  0.5 4.1 %collective-permute-start.1 = (bf16[1280,128]{1,0:T(8,128)(2,1)}, bf16[1280,128]{1,0:T(8,128)(2,1)}, u32[]{:S(2)}, u32[]{:S(2)}) collective-permute-start(bf16[1280,128]{1,0:T(8,128)(2,1)} %refs_0_.3), channel_id=1, source_target_pairs={{0,4},{4,0},{8,12},{12,8},{1,5},{5,1},{9,13},{13,9},{2,6},{6,2},{1... | collective-permute-start | bytes 983048 | tf_op jit(solution)/shard_map/ppermute | solution.py:400
  4.6 2.6 %fusion.42 = (bf16[2304,128]{1,0:T(8,128)(2,1)}, bf16[2304,128]{1,0:T(8,128)(2,1)S(1)}, bf16[2304,128]{1,0:T(8,128)(2,1)}) fusion(bf16[6912,128]{1,0:T(8,128)(2,1)} %refs_1_.1), kind=kLoop, calls=%fused_computation.93 | loop fusion | bytes 3538944 | tf_op jit(solution)/shard_map/slice | solution.py:417
  11.0 3.6 %divide_convert_fusion = bf16[64,32,512]{2,1,0:T(8,128)(2,1)} fusion(bf16[64,32,512]{2,1,0:T(8,128)(2,1)} %param.13, f32[32,512]{1,0:T(8,128)S(1)} %broadcast_add_fusion), kind=kLoop, calls=%fused_computation | loop fusion | flops 3145728 | bytes 4259840 | tf_op jit(solution)/shard_map/convert_element_type | solution.py:408
  15.4 5.1 %shard_map.83 = (bf16[4608,128]{1,0:T(8,128)(2,1)}, bf16[2304,128]{1,0:T(8,128)(2,1)}, bf16[2304,128]{1,0:T(8,128)(2,1)}) custom-call(s32[6]{0:T(128)} %stack.49.flags_ref, bf16[512,6912]{1,0:T(8,128)(2,1)} %refs_4_.1), custom_call_target="tpu_custom_call" | custom-call | flops 1 | bytes 1 | tf_op jit(solution)/shard_map/pallas_call | solution.py:310
  20.4 9.4 %shard_map.82 = (f32[64,512]{1,0:T(8,128)}, f32[64,512]{1,0:T(8,128)}) custom-call(s32[6]{0:T(128)} %stack.49.flags_ref, bf16[512,6912]{1,0:T(8,128)(2,1)} %refs_4_.1, bf16[6912,128]{1,0:T(8,128)(2,1)} %refs_1_.1), custom_call_target="tpu_custom_call" | custom-call | flops 1 | bytes 1 | tf_op jit(solution)/shard_map/pallas_call | solution.py:164
  33.6 8.8 %collective-permute-start.3 = (bf16[2560,128]{1,0:T(8,128)(2,1)S(1)}, bf16[2560,128]{1,0:T(8,128)(2,1)S(1)}, u32[]{:S(2)}, u32[]{:S(2)}) collective-permute-start(bf16[2560,128]{1,0:T(8,128)(2,1)S(1)} %maximum_select_fusion.1), channel_id=1, source_target_pairs={{0,4},{4,0},{8,12},{12,8},{1,5},{5,1},{9,13},{13,9},{2,6},{6,2},{1... | collective-permute-start | bytes 1966088 | tf_op jit(solution)/shard_map/ppermute | solution.py:384
  44.8 11.7 %collective-permute-done.3.refs_2_.refs_4_.refs_1_ = bf16[2560,128]{1,0:T(8,128)(2,1)S(1)} collective-permute-done((bf16[2560,128]{1,0:T(8,128)(2,1)S(1)}, bf16[2560,128]{1,0:T(8,128)(2,1)S(1)}, u32[]{:S(2)}, u32[]{:S(2)}) %collective-permute-start.3) | collective-permute-done | bytes 655392 | tf_op jit(solution)/shard_map/ppermute | solution.py:384
  59.1 11.1 %collective-permute-start.10 = (bf16[2304,128]{1,0:T(8,128)(2,1)S(1)}, bf16[2304,128]{1,0:T(8,128)(2,1)S(1)}, u32[]{:S(2)}, u32[]{:S(2)}) collective-permute-start(bf16[2304,128]{1,0:T(8,128)(2,1)S(1)} %broadcast_select_fusion.1), channel_id=1, source_target_pairs={{0,4},{4,0},{8,12},{12,8},{1,5},{5,1},{9,13},{13,9},{2,6},{6,2},{1... | collective-permute-start | bytes 1769480 | tf_op jit(solution)/shard_map/ppermute | solution.py:384
  70.3 5.7 %shard_map.84 = (f32[256,512]{1,0:T(8,128)}, f32[256,512]{1,0:T(8,128)}) custom-call(s32[6]{0:T(128)} %stack.49.flags_ref, bf16[512,1280]{1,0:T(8,128)(2,1)} %acts_ref.1, bf16[1280,128]{1,0:T(8,128)(2,1)} %refs_0_.3, bf16[1280,128]{1,0:T(8,128)(2,1)} %collective-permute-done.1.refs_1_, bf16[2560,128]{1,0:T(8,128)(2,1)} %copy-done.2, ...), custom_call_target="tpu_custom_call" | custom-call | flops 1 | bytes 1 | tf_op jit(solution)/shard_map/pallas_call | solution.py:355
  76.0 8.9 %shard_map.85 = (f32[64,512]{1,0:T(8,128)}, f32[64,512]{1,0:T(8,128)}) custom-call(s32[6]{0:T(128)} %stack.49.flags_ref, bf16[512,6912]{1,0:T(8,128)(2,1)} %refs_4_.1, bf16[4608,128]{1,0:T(8,128)(2,1)} %copy-done.5, bf16[2560,128]{1,0:T(8,128)(2,1)} %copy-done.2), custom_call_target="tpu_custom_call" | custom-call | flops 1 | bytes 1 | tf_op jit(solution)/shard_map/pallas_call | solution.py:164
  87.5 9.2 %shard_map.86 = (f32[64,512]{1,0:T(8,128)}, f32[64,512]{1,0:T(8,128)}) custom-call(s32[6]{0:T(128)} %stack.49.flags_ref, bf16[512,6912]{1,0:T(8,128)(2,1)} %refs_4_.1, bf16[4608,128]{1,0:T(8,128)(2,1)} %copy-done.1, bf16[2304,128]{1,0:T(8,128)(2,1)} %copy-done.10, bf16[4608,128]{1,0:T(8,128)(2,1)} %copy-done.1, bf16[2304,128]{1,0:T(8,128)(2,1)} %copy-done.11, ...), custom_call_target="tpu_custom_call" | custom-call | flops 1 | bytes 1 | tf_op jit(solution)/shard_map/pallas_call | solution.py:164
  96.8 4.1 %shard_map.87 = (f32[64,512]{1,0:T(8,128)}, f32[64,512]{1,0:T(8,128)}) custom-call(s32[6]{0:T(128)} %stack.49.flags_ref, bf16[4608,128]{1,0:T(8,128)(2,1)} %copy-done.1, bf16[4608,128]{1,0:T(8,128)(2,1)} %copy-done.1, bf16[6912,128]{1,0:T(8,128)(2,1)} %refs_1_.1, bf16[2304,128]{1,0:T(8,128)(2,1)} %copy-done.3), custom_call_target="tpu_custom_call" | custom-call | flops 1 | bytes 1 | tf_op jit(solution)/shard_map/pallas_call | solution.py:277
  103.5 14.0 %collective-permute-start.21 = (bf16[2304,128]{1,0:T(8,128)(2,1)S(1)}, bf16[2304,128]{1,0:T(8,128)(2,1)S(1)}, u32[]{:S(2)}, u32[]{:S(2)}) collective-permute-start(bf16[2304,128]{1,0:T(8,128)(2,1)S(1)} %broadcast_select_fusion), channel_id=1, source_target_pairs={{0,4},{4,0},{8,12},{12,8},{1,5},{5,1},{9,13},{13,9},{2,6},{6,2},{1... | collective-permute-start | bytes 1769480 | tf_op jit(solution)/shard_map/ppermute | solution.py:384
  117.5 7.2 %shard_map.88 = (f32[64,640]{1,0:T(8,128)}, f32[64,640]{1,0:T(8,128)}, f32[512,128]{1,0:T(8,128)}) custom-call(s32[6]{0:T(128)} %stack.49.flags_ref, bf16[4608,128]{1,0:T(8,128)(2,1)} %copy-done.1, bf16[4608,128]{1,0:T(8,128)(2,1)} %copy-done.1, bf16[2304,128]{1,0:T(8,128)(2,1)} %copy-done.6, bf16[6912,128]{1,0:T(8,128)(2,1)} %refs_1_.1, ...), custom_call_target="tpu_custom_call" | custom-call | flops 1 | bytes 1 | tf_op jit(solution)/shard_map/pallas_call | solution.py:277
  131.9 5.8 %shard_map.89 = (f32[64,896]{1,0:T(8,128)}, f32[64,896]{1,0:T(8,128)}) custom-call(s32[6]{0:T(128)} %stack.49.flags_ref, bf16[2304,128]{1,0:T(8,128)(2,1)} %copy-done.7, bf16[6912,128]{1,0:T(8,128)(2,1)} %refs_1_.1, bf16[2304,128]{1,0:T(8,128)(2,1)} %copy-done.3, bf16[2304,128]{1,0:T(8,128)(2,1)} %copy-done.4, bf16[512,6912]{1,0:T(8,128)(2,1)} %refs_4_.1, ...), custom_call_target="tpu_custom_call" | custom-call | flops 1 | bytes 1 | tf_op jit(solution)/shard_map/pallas_call | solution.py:277
  142.0 3.0 %collective-permute-done.15 = f32[32,2688]{1,0:T(8,128)S(1)} collective-permute-done((f32[32,2688]{1,0:T(8,128)S(1)}, f32[32,2688]{1,0:T(8,128)S(1)}, u32[]{:S(2)}, u32[]{:S(2)}) %collective-permute-start.15) | collective-permute-done | bytes 344096 | tf_op jit(solution)/shard_map/ppermute | solution.py:38
  145.1 1.9 %collective-permute-start.20 = (f32[32,1152]{1,0:T(8,128)S(1)}, f32[32,1152]{1,0:T(8,128)S(1)}, u32[]{:S(2)}, u32[]{:S(2)}) collective-permute-start(f32[32,1152]{1,0:T(8,128)S(1)} %slice.105), channel_id=1, source_target_pairs={{0,4},{4,0},{8,12},{12,8},{1,5},{5,1},{9,13},{13,9},{2,6},{6,2},{1... | collective-permute-start | bytes 442376 | tf_op jit(solution)/shard_map/ppermute | solution.py:477
  151.5 2.2 %collective-permute-done.24 = f32[32,384]{1,0:T(8,128)S(1)} collective-permute-done((f32[32,384]{1,0:T(8,128)S(1)}, f32[32,384]{1,0:T(8,128)S(1)}, u32[]{:S(2)}, u32[]{:S(2)}) %collective-permute-start.24) | collective-permute-done | bytes 49184 | tf_op jit(solution)/shard_map/ppermute | solution.py:478
  156.7 2.5 %fusion.8 = f32[4,64]{1,0:T(4,128)S(1)} fusion(bf16[64,32,512]{2,1,0:T(8,128)(2,1)S(1)} %copy-done.12, bf16[4,32,512]{2,1,0:T(8,128)(2,1)S(1)} %convolution_convert_fusion.3), kind=kOutput, calls=%fused_computation.14 | convolution fusion | flops 8388608 | bytes 2229248 | tf_op jit(solution)/shard_map/tea,jea->tj/dot_general | solution.py:497
  162.3 2.5 %fusion.11 = f32[4,64]{1,0:T(4,128)S(1)} fusion(bf16[64,32,512]{2,1,0:T(8,128)(2,1)S(1)} %copy-done.12, bf16[4,32,512]{2,1,0:T(8,128)(2,1)S(1)} %collective-permute-done.25), kind=kOutput, calls=%fused_computation.15 | convolution fusion | flops 8388608 | bytes 2229248 | tf_op jit(solution)/shard_map/tea,jea->tj/dot_general | solution.py:497
  164.8 5.9 %collective-permute-done.26 = bf16[4,32,512]{2,1,0:T(8,128)(2,1)S(1)} collective-permute-done((bf16[4,32,512]{2,1,0:T(8,128)(2,1)S(1)}, bf16[4,32,512]{2,1,0:T(8,128)(2,1)S(1)}, u32[]{:S(2)}, u32[]{:S(2)}) %collective-permute-start.26) | collective-permute-done | bytes 131104 | tf_op jit(solution)/shard_map/ppermute | solution.py:508
  170.7 2.5 %fusion.14 = f32[4,64]{1,0:T(4,128)S(1)} fusion(bf16[64,32,512]{2,1,0:T(8,128)(2,1)S(1)} %copy-done.12, bf16[4,32,512]{2,1,0:T(8,128)(2,1)S(1)} %collective-permute-done.26), kind=kOutput, calls=%fused_computation.16 | convolution fusion | flops 8388608 | bytes 2229248 | tf_op jit(solution)/shard_map/tea,jea->tj/dot_general | solution.py:497
  173.3 2.5 %fusion.17 = f32[4,64]{1,0:T(4,128)S(1)} fusion(bf16[64,32,512]{2,1,0:T(8,128)(2,1)S(1)} %copy-done.12, bf16[4,32,512]{2,1,0:T(8,128)(2,1)S(1)} %collective-permute-done.27), kind=kOutput, calls=%fused_computation.17 | convolution fusion | flops 8388608 | bytes 2229248 | tf_op jit(solution)/shard_map/tea,jea->tj/dot_general | solution.py:497
  176.0 10.4 %all_to_all.5 = f32[16,2,16]{2,1,0:T(2,128)S(1)} all-to-all(f32[16,2,16]{2,1,0:T(2,128)S(1)} %copy.69), channel_id=1, replica_groups=mesh['groups'=2,'cand'=4,'eig'=2,'rep'=2] {'cand','eig','rep'}, dimensions={0} | all-to-all | bytes 4096 | tf_op jit(solution)/shard_map/all_to_all | solution.py:517
  (159 shorter events, 41.8 us)
Async XLA Ops:
  0.0 30.1 %collective-permute-start = (bf16[1280,128]{1,0:T(8,128)(2,1)}, bf16[1280,128]{1,0:T(8,128)(2,1)}, u32[]{:S(2)}, u32[]{:S(2)}) collective-permute-start(bf16[1280,128]{1,0:T(8,128)(2,1)} %refs_0_.3), channel_id=1, source_target_pairs={{0,1},{1,0},{2,3},{3,2},{4,8},{5,9},{6,10},{7,11},{8,4},{9,5},{10,... | collective-permute-start | bytes 983048 | tf_op jit(solution)/shard_map/ppermute | solution.py:392
  0.5 29.7 %collective-permute-start.1 = (bf16[1280,128]{1,0:T(8,128)(2,1)}, bf16[1280,128]{1,0:T(8,128)(2,1)}, u32[]{:S(2)}, u32[]{:S(2)}) collective-permute-start(bf16[1280,128]{1,0:T(8,128)(2,1)} %refs_0_.3), channel_id=1, source_target_pairs={{0,4},{4,0},{8,12},{12,8},{1,5},{5,1},{9,13},{13,9},{2,6},{6,2},{1... | collective-permute-start | bytes 983048 | tf_op jit(solution)/shard_map/ppermute | solution.py:400
  7.2 23.2 %collective-permute-start.6 = (bf16[2304,128]{1,0:T(8,128)(2,1)}, bf16[2304,128]{1,0:T(8,128)(2,1)S(1)}, u32[]{:S(2)}, u32[]{:S(2)}) collective-permute-start(bf16[2304,128]{1,0:T(8,128)(2,1)} %get-tuple-element.82), channel_id=1, source_target_pairs={{0,1},{1,0},{2,3},{3,2},{4,8},{5,9},{6,10},{7,11},{8,4},{9,5},{10,... | collective-permute-start | bytes 1769480 | tf_op jit(solution)/shard_map/ppermute | solution.py:392
  8.3 34.1 %collective-permute-start.4 = (bf16[4608,128]{1,0:T(8,128)(2,1)}, bf16[4608,128]{1,0:T(8,128)(2,1)S(1)}, u32[]{:S(2)}, u32[]{:S(2)}) collective-permute-start(bf16[4608,128]{1,0:T(8,128)(2,1)} %constant_dynamic-slice_fusion), channel_id=1, source_target_pairs={{0,4},{4,0},{8,12},{12,8},{1,5},{5,1},{9,13},{13,9},{2,6},{6,2},{1... | collective-permute-start | bytes 3538952 | tf_op jit(solution)/shard_map/ppermute | solution.py:402
  32.1 11.4 %collective-permute-start.7 = (bf16[2304,128]{1,0:T(8,128)(2,1)S(1)}, bf16[2304,128]{1,0:T(8,128)(2,1)S(1)}, u32[]{:S(2)}, u32[]{:S(2)}) collective-permute-start(bf16[2304,128]{1,0:T(8,128)(2,1)S(1)} %get-tuple-element.53), channel_id=1, source_target_pairs={{0,1},{1,0},{2,3},{3,2},{4,8},{5,9},{6,10},{7,11},{8,4},{9,5},{10,... | collective-permute-start | bytes 1769480 | tf_op jit(solution)/shard_map/ppermute | solution.py:392
  33.6 23.0 %collective-permute-start.3 = (bf16[2560,128]{1,0:T(8,128)(2,1)S(1)}, bf16[2560,128]{1,0:T(8,128)(2,1)S(1)}, u32[]{:S(2)}, u32[]{:S(2)}) collective-permute-start(bf16[2560,128]{1,0:T(8,128)(2,1)S(1)} %maximum_select_fusion.1), channel_id=1, source_target_pairs={{0,4},{4,0},{8,12},{12,8},{1,5},{5,1},{9,13},{13,9},{2,6},{6,2},{1... | collective-permute-start | bytes 1966088 | tf_op jit(solution)/shard_map/ppermute | solution.py:384
  43.4 15.0 %collective-permute-start.5 = (bf16[2304,128]{1,0:T(8,128)(2,1)S(1)}, bf16[2304,128]{1,0:T(8,128)(2,1)S(1)}, u32[]{:S(2)}, u32[]{:S(2)}) collective-permute-start(bf16[2304,128]{1,0:T(8,128)(2,1)S(1)} %get-tuple-element.84), channel_id=1, source_target_pairs={{0,1},{1,0},{2,3},{3,2},{4,8},{5,9},{6,10},{7,11},{8,4},{9,5},{10,... | collective-permute-start | bytes 1769480 | tf_op jit(solution)/shard_map/ppermute | solution.py:392
  56.6 29.1 %collective-permute-start.8 = (bf16[4608,128]{1,0:T(8,128)(2,1)}, bf16[4608,128]{1,0:T(8,128)(2,1)S(1)}, u32[]{:S(2)}, u32[]{:S(2)}) collective-permute-start(bf16[4608,128]{1,0:T(8,128)(2,1)} %maximum_select_fusion), channel_id=1, source_target_pairs={{0,4},{4,0},{8,12},{12,8},{1,5},{5,1},{9,13},{13,9},{2,6},{6,2},{1... | collective-permute-start | bytes 3538952 | tf_op jit(solution)/shard_map/ppermute | solution.py:415
  58.4 11.8 %collective-permute-start.11 = (bf16[2304,128]{1,0:T(8,128)(2,1)S(1)}, bf16[2304,128]{1,0:T(8,128)(2,1)S(1)}, u32[]{:S(2)}, u32[]{:S(2)}) collective-permute-start(bf16[2304,128]{1,0:T(8,128)(2,1)S(1)} %slice.102), channel_id=1, source_target_pairs={{0,1},{1,0},{2,3},{3,2},{4,8},{5,9},{6,10},{7,11},{8,4},{9,5},{10,... | collective-permute-start | bytes 1769480 | tf_op jit(solution)/shard_map/ppermute | solution.py:392
  58.5 27.2 %collective-permute-start.9 = (bf16[2304,128]{1,0:T(8,128)(2,1)}, bf16[2304,128]{1,0:T(8,128)(2,1)S(1)}, u32[]{:S(2)}, u32[]{:S(2)}) collective-permute-start(bf16[2304,128]{1,0:T(8,128)(2,1)} %get-tuple-element.56), channel_id=1, source_target_pairs={{0,1},{1,0},{2,3},{3,2},{4,8},{5,9},{6,10},{7,11},{8,4},{9,5},{10,... | collective-permute-start | bytes 1769480 | tf_op jit(solution)/shard_map/ppermute | solution.py:392
  59.1 43.7 %collective-permute-start.10 = (bf16[2304,128]{1,0:T(8,128)(2,1)S(1)}, bf16[2304,128]{1,0:T(8,128)(2,1)S(1)}, u32[]{:S(2)}, u32[]{:S(2)}) collective-permute-start(bf16[2304,128]{1,0:T(8,128)(2,1)S(1)} %broadcast_select_fusion.1), channel_id=1, source_target_pairs={{0,4},{4,0},{8,12},{12,8},{1,5},{5,1},{9,13},{13,9},{2,6},{6,2},{1... | collective-permute-start | bytes 1769480 | tf_op jit(solution)/shard_map/ppermute | solution.py:384
  70.2 32.6 %collective-permute-start.12 = (bf16[2304,128]{1,0:T(8,128)(2,1)}, bf16[2304,128]{1,0:T(8,128)(2,1)S(1)}, u32[]{:S(2)}, u32[]{:S(2)}) collective-permute-start(bf16[2304,128]{1,0:T(8,128)(2,1)} %get-tuple-element.62), channel_id=1, source_target_pairs={{0,1},{1,0},{2,3},{3,2},{4,8},{5,9},{6,10},{7,11},{8,4},{9,5},{10,... | collective-permute-start | bytes 1769480 | tf_op jit(solution)/shard_map/ppermute | solution.py:392
  102.8 27.2 %collective-permute-start.13 = (f32[64,2048]{1,0:T(8,128)}, f32[64,2048]{1,0:T(8,128)S(1)}, u32[]{:S(2)}, u32[]{:S(2)}) collective-permute-start(f32[64,2048]{1,0:T(8,128)} %get-tuple-element.64), channel_id=1, source_target_pairs={{0,1},{1,0},{2,3},{3,2},{4,5},{5,4},{6,7},{7,6},{8,9},{9,8},{10,11... | collective-permute-start | bytes 1572872 | tf_op jit(solution)/shard_map/ppermute | solution.py:38
  102.9 24.3 %collective-permute-start.16 = (f32[256,512]{1,0:T(8,128)}, f32[256,512]{1,0:T(8,128)}, u32[]{:S(2)}, u32[]{:S(2)}) collective-permute-start(f32[256,512]{1,0:T(8,128)} %get-tuple-element.69), channel_id=1, source_target_pairs={{0,1},{1,0},{2,3},{3,2},{4,5},{5,4},{6,7},{7,6},{8,9},{9,8},{10,11... | collective-permute-start | bytes 1572872 | tf_op jit(solution)/shard_map/ppermute | solution.py:38
  103.5 27.6 %collective-permute-start.21 = (bf16[2304,128]{1,0:T(8,128)(2,1)S(1)}, bf16[2304,128]{1,0:T(8,128)(2,1)S(1)}, u32[]{:S(2)}, u32[]{:S(2)}) collective-permute-start(bf16[2304,128]{1,0:T(8,128)(2,1)S(1)} %broadcast_select_fusion), channel_id=1, source_target_pairs={{0,4},{4,0},{8,12},{12,8},{1,5},{5,1},{9,13},{13,9},{2,6},{6,2},{1... | collective-permute-start | bytes 1769480 | tf_op jit(solution)/shard_map/ppermute | solution.py:384
  128.4 9.3 %collective-permute-start.17 = (f32[128,512]{1,0:T(8,128)S(1)}, f32[128,512]{1,0:T(8,128)S(1)}, u32[]{:S(2)}, u32[]{:S(2)}) collective-permute-start(f32[128,512]{1,0:T(8,128)S(1)} %slice_select_fusion), channel_id=1, source_target_pairs={{0,2},{2,0},{1,3},{3,1},{4,6},{6,4},{5,7},{7,5},{8,10},{10,8},{9,1... | collective-permute-start | bytes 786440 | tf_op jit(solution)/shard_map/ppermute | solution.py:38
  130.1 14.9 %collective-permute-start.15 = (f32[32,2688]{1,0:T(8,128)S(1)}, f32[32,2688]{1,0:T(8,128)S(1)}, u32[]{:S(2)}, u32[]{:S(2)}) collective-permute-start(f32[32,2688]{1,0:T(8,128)S(1)} %broadcast_select_fusion.2), channel_id=1, source_target_pairs={{0,2},{2,0},{1,3},{3,1},{4,6},{6,4},{5,7},{7,5},{8,10},{10,8},{9,1... | collective-permute-start | bytes 1032200 | tf_op jit(solution)/shard_map/ppermute | solution.py:38
  137.8 10.0 %collective-permute-start.18 = (bf16[128,512]{1,0:T(8,128)(2,1)S(1)}, bf16[128,512]{1,0:T(8,128)(2,1)S(1)}, u32[]{:S(2)}, u32[]{:S(2)}) collective-permute-start(bf16[128,512]{1,0:T(8,128)(2,1)S(1)} %add_convert_fusion), channel_id=1, source_target_pairs={{0,2},{2,0},{1,3},{3,1},{4,6},{6,4},{5,7},{7,5},{8,10},{10,8},{9,1... | collective-permute-start | bytes 393224 | tf_op jit(solution)/shard_map/ppermute | solution.py:38
  140.5 9.0 %collective-permute-start.23 = (f32[32,896]{1,0:T(8,128)S(1)}, f32[32,896]{1,0:T(8,128)S(1)}, u32[]{:S(2)}, u32[]{:S(2)}) collective-permute-start(f32[32,896]{1,0:T(8,128)S(1)} %slice_select_fusion.1), channel_id=1, source_target_pairs={{0,2},{2,0},{1,3},{3,1},{4,6},{6,4},{5,7},{7,5},{8,10},{10,8},{9,1... | collective-permute-start | bytes 344072 | tf_op jit(solution)/shard_map/ppermute | solution.py:38
  145.1 8.6 %collective-permute-start.20 = (f32[32,1152]{1,0:T(8,128)S(1)}, f32[32,1152]{1,0:T(8,128)S(1)}, u32[]{:S(2)}, u32[]{:S(2)}) collective-permute-start(f32[32,1152]{1,0:T(8,128)S(1)} %slice.105), channel_id=1, source_target_pairs={{0,4},{4,0},{8,12},{12,8},{1,5},{5,1},{9,13},{13,9},{2,6},{6,2},{1... | collective-permute-start | bytes 442376 | tf_op jit(solution)/shard_map/ppermute | solution.py:477
  149.5 4.2 %collective-permute-start.24 = (f32[32,384]{1,0:T(8,128)S(1)}, f32[32,384]{1,0:T(8,128)S(1)}, u32[]{:S(2)}, u32[]{:S(2)}) collective-permute-start(f32[32,384]{1,0:T(8,128)S(1)} %slice.109), channel_id=1, source_target_pairs={{0,4},{4,0},{8,12},{12,8},{1,5},{5,1},{9,13},{13,9},{2,6},{6,2},{1... | collective-permute-start | bytes 147464 | tf_op jit(solution)/shard_map/ppermute | solution.py:478
  154.2 8.1 %collective-permute-start.25 = (bf16[4,32,512]{2,1,0:T(8,128)(2,1)S(1)}, bf16[4,32,512]{2,1,0:T(8,128)(2,1)S(1)}, u32[]{:S(2)}, u32[]{:S(2)}) collective-permute-start(bf16[4,32,512]{2,1,0:T(8,128)(2,1)S(1)} %convolution_convert_fusion.2), channel_id=1, source_target_pairs={{0,4},{4,0},{8,12},{12,8},{1,5},{5,1},{9,13},{13,9},{2,6},{6,2},{1... | collective-permute-start | bytes 393224 | tf_op jit(solution)/shard_map/ppermute | solution.py:507
  159.2 11.5 %collective-permute-start.26 = (bf16[4,32,512]{2,1,0:T(8,128)(2,1)S(1)}, bf16[4,32,512]{2,1,0:T(8,128)(2,1)S(1)}, u32[]{:S(2)}, u32[]{:S(2)}) collective-permute-start(bf16[4,32,512]{2,1,0:T(8,128)(2,1)S(1)} %get-tuple-element.90), channel_id=1, source_target_pairs={{0,8},{8,0},{4,12},{12,4},{1,9},{9,1},{5,13},{13,5},{2,10},{10,2},... | collective-permute-start | bytes 393224 | tf_op jit(solution)/shard_map/ppermute | solution.py:508
  160.8 12.5 %collective-permute-start.27 = (bf16[4,32,512]{2,1,0:T(8,128)(2,1)S(1)}, bf16[4,32,512]{2,1,0:T(8,128)(2,1)S(1)}, u32[]{:S(2)}, u32[]{:S(2)}) collective-permute-start(bf16[4,32,512]{2,1,0:T(8,128)(2,1)S(1)} %get-tuple-element.91), channel_id=1, source_target_pairs={{0,12},{12,0},{4,8},{8,4},{1,13},{13,1},{5,9},{9,5},{2,14},{14,2},... | collective-permute-start | bytes 393224 | tf_op jit(solution)/shard_map/ppermute | solution.py:509
  (31 other events, 259.2 us)

commit v7 on v6

--- a/solution.py
+++ b/solution.py
@@ -9,11 +9,10 @@
 FEAT = ("eig", "rep")
 ALL = ("cand", "eig", "rep")
 STEPS = 3
-PARAMS = pltpu.CompilerParams(vmem_limit_bytes=56 << 20)
+PARAMS = pltpu.CompilerParams(vmem_limit_bytes=20 << 20)
 SHORT = pl.CostEstimate(flops=1, bytes_accessed=1, transcendentals=0)
 SIDE = ((0, 1), (1, 0), (2, 3), (3, 2))
 TWO = ((0, 2), (2, 0), (1, 3), (3, 1))
-THREE = ((0, 3), (3, 0), (1, 2), (2, 1))
 
 damping = 0.01
 
@@ -383,10 +382,12 @@
     def side(at_end, at_middle):
         return lax.ppermute(pick(at_end, at_middle), "cand", SIDE)
 
-    among = []
+    among, far = [], []
     for at in range(16):
-        mid = 4 <= at < 12
-        among.append((at, (12 - at + 2 * (at % 4)) if mid else at ^ 1))
+        between = 4 <= at < 12
+        across = 12 - 4 * (at // 4) + at % 4
+        among.append((at, across if between else at ^ 1))
+        far.append((at, at ^ 1 if between else across))
 
     def middle(x):
         return lax.ppermute(x, ALL, among)
@@ -406,10 +407,10 @@
     stacked, *more_stacked = stack_blocks(started, grads, depth)
     part_own = feature_dots(started, grads, [([(basis_out, 0)], 0, 0, 3 * STEPS, False)])
     precond = (test_grads.astype(jnp.float32) / (eigval + damping)).astype(jnp.bfloat16)
-    m1 = middle(after(s0, m0, precond, stacked, *more_stacked, *part_own))
+    m1 = middle(after(s0, m0))
     third = jnp.concatenate([basis_out[2 * depth :], basis_out[: 2 * rows_in - depth]])
     s3 = side(third, jnp.concatenate([m0, m1]))
-    m3 = middle(after(basis_out[2 * depth :], m1, m2))
+    m3 = middle(after(basis_out[2 * depth :], m1, m2, precond, stacked, *more_stacked, *part_own))
     m5 = middle(s12[depth:])
     to_s45 = pick(stacked, jnp.concatenate([m2, m3]))
     s45 = lax.ppermute(after(to_s45, s3), "cand", SIDE)
@@ -474,13 +475,6 @@
     )
     sum_last = chip_sum(core_sum(*part_last))
     sum_c = sum_last[:, :tok_rows]
-    back = jnp.where(end, lax.ppermute(sums[:, 3 * tok_rows :], "cand", SIDE), 0.0)
-    last = jnp.where(end, lax.ppermute(sum_last[:, tok_rows:], "cand", SIDE), 0.0)
-    back = [back[:, i * TILE : (i + 1) * TILE] for i in range(9)]
-    last = [last[:, i * TILE : (i + 1) * TILE] for i in range(3)]
-    back_a = jnp.concatenate([back[0], back[2], back[6], last[0]], axis=1)
-    back_b = jnp.concatenate([back[1], back[3], back[7], last[1]], axis=1)
-    back_c = jnp.concatenate([back[4], back[5], back[8], last[2]], axis=1)
 
     rowmask, ignored = tile_layout(pair_tiles, last_rows, plane * tiles_here, tiles_here, TILE)
     keep = rowmask.reshape(1, tok_rows).astype(jnp.bfloat16)
@@ -500,13 +494,24 @@
         )
         return jnp.sum(jnp.where(onehot[:, :, None], scores[:, None, :], 0.0), axis=0)
 
-    prods_a = tile_prods(sum_a + back_a)
-    prods_b = tile_prods(sum_b + back_b)
-    prods_c = tile_prods(sum_c + back_c)
+    def columns(x, *which):
+        return jnp.concatenate([x[:, i * TILE : (i + 1) * TILE] for i in which], axis=1)
+
     total = pair_scores(tile_prods(sum_own), plane)
-    total = total + pair_scores(lax.ppermute(prods_a, "cand", SIDE), plane ^ 1)
-    total = total + pair_scores(lax.ppermute(pick(prods_b, prods_c), "cand", TWO), plane ^ 2)
-    total = total + pair_scores(lax.ppermute(pick(prods_c, prods_b), "cand", THREE), plane ^ 3)
+    prods_middle = tile_prods(sum_b)
+    from_middle = middle(prods_middle)
+    last = lax.ppermute(after(sum_last[:, tok_rows:], total, prods_middle), "cand", SIDE)
+    back = lax.ppermute(sums[:, 3 * tok_rows :], "cand", SIDE)
+    both = jnp.where(end, jnp.concatenate([back, last], axis=1), 0.0)
+    prods_a = tile_prods(sum_a + columns(both, 0, 2, 6, 9))
+    prods_b = tile_prods(sum_b + columns(both, 1, 3, 7, 10))
+    prods_c = tile_prods(sum_c + columns(both, 4, 5, 8, 11))
+    from_far = lax.ppermute(prods_c, ALL, far)
+    from_two = lax.ppermute(pick(prods_b, prods_c), "cand", TWO)
+    from_side = lax.ppermute(prods_a, "cand", SIDE)
+    total = total + pair_scores(from_side, plane ^ 1)
+    total = total + pair_scores(from_two, plane ^ 2)
+    total = total + pair_scores(pick(from_far, from_middle), plane ^ 3)
     return final_sum(total)
 
 

time: 188 us -> 169 us (0.90)
  Pallas kernels: 55.4 us -> 25.4 us
  waiting for transfers between devices: 29.8 us -> 45.7 us
  starting transfers between devices: 57.4 us -> 46.6 us
  local copies, waits for them, and re-layouts: 8.34 us -> 12.5 us
    pallas_call x3, Pallas kernels: 27.5 us -> 13.3 us  [feature_dots(): pl.pallas_call(kernel, out_shape=out_shape, grid_spec=pltpu.PrefetchScala...]
    pallas_call x3, Pallas kernels: 17.1 us -> 6.13 us  [partner_dots(): pl.pallas_call(kernel, out_shape=out_shape, grid_spec=pltpu.PrefetchScala...]
    ppermute x3, starting transfers between devices: 34 us -> 25.3 us  [side(): return lax.ppermute(pick(at_end, at_middle), 'cand', SIDE)]
    ppermute x1, waiting for transfers between devices: 0.73 us -> 7.78 us  [line_plan(): s45 = lax.ppermute(after(to_s45, s3), 'cand', SIDE)]
    unnamed x52, local copies, waits for them, and re-layouts: 2.77 us -> 8.52 us
    ppermute x3, waiting for transfers between devices: 12.1 us -> 17.6 us  [side(): return lax.ppermute(pick(at_end, at_middle), 'cand', SIDE)]
    ppermute x1, waiting for transfers between devices: 0.01 us -> 4.87 us  [line_plan(): s12 = lax.ppermute(rows, 'cand', SIDE)]
    pallas_call x1, Pallas kernels: 5.07 us -> 1.25 us  [stack_blocks(): pl.pallas_call(kernel, out_shape=[jax.ShapeDtypeStruct((count * depth, TI...]
  transfers between devices with their start and end apart: 28 -> 29, of which waited for: 11 -> 12; matrix products, arithmetic and copies ran while one was open for 15% -> 16% of each run, Pallas kernels for 30% -> 15%
where the time goes in v7:
time: 169 us; the launch traced here: 168 us
  starting transfers between devices  46.6 us (28%)
  waiting for transfers between devices  45.7 us (27%)
  Pallas kernels  25.4 us (15%)
  other arithmetic  15.4 us (9%)
  local copies, waits for them, and re-layouts  12.5 us (7%)
  matrix products  10.9 us (6%)
  blocking collectives  10.9 us (6%)
    ppermute x3, starting transfers between devices, side(): return lax.ppermute(pick(at_end, at_middle), 'cand', SIDE)  25.3 us
    ppermute x3, waiting for transfers between devices, side(): return lax.ppermute(pick(at_end, at_middle), 'cand', SIDE)  17.6 us
    pallas_call x3, Pallas kernels, feature_dots(): pl.pallas_call(kernel, out_shape=out_shape, grid_spec=pltpu.PrefetchScala...  13.3 us
    all_to_all x1, blocking collectives, final_sum(): return jnp.sum(lax.all_to_all(blocks, ALL, 0, 0, tiled=True), axis=0)  10.9 us
    dot_general x4, matrix products, pair_scores(): jnp.einsum('tea,jea->tj', prods, precond, preferred_element_type=jnp.floa...  9.87 us
    unnamed x52, local copies, waits for them, and re-layouts  8.52 us
    ppermute x1, waiting for transfers between devices, line_plan(): s45 = lax.ppermute(after(to_s45, s3), 'cand', SIDE)  7.78 us
    ppermute x9, waiting for transfers between devices, swap(): return lax.ppermute(x, axis_name, [(0, 1), (1, 0)])  6.79 us
  transfers between devices with their start and end apart: 29, of which 12 were waited for; matrix products, arithmetic and copies ran while one was open for 16% of the time, Pallas kernels for 15%

profile of v7, /device:TPU:0, one launch (start us, length us, event | category | flops | bytes accessed | tf_op | source)
XLA Modules:
  0.0 168.1 jit_solution(14737480507597848332)
XLA Ops:
  0.5 4.1 %collective-permute-start.1 = (bf16[1280,128]{1,0:T(8,128)(2,1)}, bf16[1280,128]{1,0:T(8,128)(2,1)}, u32[]{:S(2)}, u32[]{:S(2)}) collective-permute-start(bf16[1280,128]{1,0:T(8,128)(2,1)} %refs_0_.3), channel_id=1, source_target_pairs={{0,4},{4,0},{8,12},{12,8},{1,5},{5,1},{9,13},{13,9},{2,6},{6,2},{1... | collective-permute-start | bytes 983048 | tf_op jit(solution)/shard_map/ppermute | solution.py:401
  8.3 3.6 %divide_convert_fusion = bf16[64,32,512]{2,1,0:T(8,128)(2,1)} fusion(bf16[64,32,512]{2,1,0:T(8,128)(2,1)} %param.13, f32[32,512]{1,0:T(8,128)S(1)} %broadcast_add_fusion), kind=kLoop, calls=%fused_computation | loop fusion | flops 3145728 | bytes 4259840 | tf_op jit(solution)/shard_map/convert_element_type | solution.py:409
  14.3 3.0 %copy-done = bf16[512,6912]{1,0:T(8,128)(2,1)S(1)} copy-done((bf16[512,6912]{1,0:T(8,128)(2,1)S(1)}, bf16[512,6912]{1,0:T(8,128)(2,1)}, u32[]{:S(2)}) %copy-start) | copy-done | bytes 7077912
  17.3 4.6 %shard_map.82 = (f32[64,512]{1,0:T(8,128)S(1)}, f32[64,512]{1,0:T(8,128)S(1)}) custom-call(s32[6]{0:T(128)S(1)} %stack.49.flags_ref, bf16[512,6912]{1,0:T(8,128)(2,1)S(1)} %copy-done, bf16[6912,128]{1,0:T(8,128)(2,1)S(1)} %copy-done.2), custom_call_target="tpu_custom_call" | custom-call | flops 1 | bytes 1 | tf_op jit(solution)/shard_map/pallas_call | solution.py:163
  24.6 9.3 %collective-permute-start.3 = (bf16[2560,128]{1,0:T(8,128)(2,1)S(1)}, bf16[2560,128]{1,0:T(8,128)(2,1)S(1)}, u32[]{:S(2)}, u32[]{:S(2)}) collective-permute-start(bf16[2560,128]{1,0:T(8,128)(2,1)S(1)} %maximum_select_fusion.1), channel_id=1, source_target_pairs={{0,4},{4,0},{8,12},{12,8},{1,5},{5,1},{9,13},{13,9},{2,6},{6,2},{1... | collective-permute-start | bytes 1966088 | tf_op jit(solution)/shard_map/ppermute | solution.py:383
  33.8 4.9 %collective-permute-done.4.refs_0_ = bf16[4608,128]{1,0:T(8,128)(2,1)S(1)} collective-permute-done((bf16[4608,128]{1,0:T(8,128)(2,1)}, bf16[4608,128]{1,0:T(8,128)(2,1)S(1)}, u32[]{:S(2)}, u32[]{:S(2)}) %collective-permute-start.4) | collective-permute-done | bytes 1179680 | tf_op jit(solution)/shard_map/ppermute | solution.py:403
  40.8 10.8 %collective-permute-done.3.refs_2_.refs_4_.refs_1_ = bf16[2560,128]{1,0:T(8,128)(2,1)S(1)} collective-permute-done((bf16[2560,128]{1,0:T(8,128)(2,1)S(1)}, bf16[2560,128]{1,0:T(8,128)(2,1)S(1)}, u32[]{:S(2)}, u32[]{:S(2)}) %collective-permute-start.3) | collective-permute-done | bytes 655392 | tf_op jit(solution)/shard_map/ppermute | solution.py:383
  51.7 2.5 %collective-permute-start.8 = (bf16[4608,128]{1,0:T(8,128)(2,1)S(1)}, bf16[4608,128]{1,0:T(8,128)(2,1)S(1)}, u32[]{:S(2)}, u32[]{:S(2)}) collective-permute-start(bf16[4608,128]{1,0:T(8,128)(2,1)S(1)} %maximum_select_fusion), channel_id=1, source_target_pairs={{0,4},{4,0},{8,12},{12,8},{1,5},{5,1},{9,13},{13,9},{2,6},{6,2},{1... | collective-permute-start | bytes 3538952 | tf_op jit(solution)/shard_map/ppermute | solution.py:416
  54.3 10.2 %collective-permute-start.10 = (bf16[2304,128]{1,0:T(8,128)(2,1)S(1)}, bf16[2304,128]{1,0:T(8,128)(2,1)S(1)}, u32[]{:S(2)}, u32[]{:S(2)}) collective-permute-start(bf16[2304,128]{1,0:T(8,128)(2,1)S(1)} %broadcast_select_fusion.1), channel_id=1, source_target_pairs={{0,4},{4,0},{8,12},{12,8},{1,5},{5,1},{9,13},{13,9},{2,6},{6,2},{1... | collective-permute-start | bytes 1769480 | tf_op jit(solution)/shard_map/ppermute | solution.py:383
  64.7 4.7 %shard_map.83 = (f32[256,512]{1,0:T(8,128)S(1)}, f32[256,512]{1,0:T(8,128)}) custom-call(s32[6]{0:T(128)S(1)} %stack.49.flags_ref, bf16[512,1280]{1,0:T(8,128)(2,1)S(1)} %copy-done.7, bf16[1280,128]{1,0:T(8,128)(2,1)S(1)} %copy-done.9, bf16[1280,128]{1,0:T(8,128)(2,1)} %collective-permute-done.1.refs_1_, ...), custom_call_target="tpu_custom_call" | custom-call | flops 1 | bytes 1 | tf_op jit(solution)/shard_map/pallas_call | solution.py:354
  69.4 3.8 %shard_map.84 = (f32[64,512]{1,0:T(8,128)S(1)}, f32[64,512]{1,0:T(8,128)S(1)}) custom-call(s32[6]{0:T(128)S(1)} %stack.49.flags_ref, bf16[512,6912]{1,0:T(8,128)(2,1)S(1)} %bitcast.60, bf16[4608,128]{1,0:T(8,128)(2,1)S(1)} %copy-done.4, bf16[2560,128]{1,0:T(8,128)(2,1)S(1)} %collective-permute-done.3.refs_2_.refs_4_.refs_1_), custom_call_target="tpu_custom_call" | custom-call | flops 1 | bytes 1 | tf_op jit(solution)/shard_map/pallas_call | solution.py:163
  73.2 7.8 %collective-permute-done.8.refs_0_.refs_2_.refs_1_ = bf16[4608,128]{1,0:T(8,128)(2,1)S(1)} collective-permute-done((bf16[4608,128]{1,0:T(8,128)(2,1)S(1)}, bf16[4608,128]{1,0:T(8,128)(2,1)S(1)}, u32[]{:S(2)}, u32[]{:S(2)}) %collective-permute-start.8) | collective-permute-done | bytes 1179680 | tf_op jit(solution)/shard_map/ppermute | solution.py:416
  81.0 4.9 %shard_map.86 = (f32[64,512]{1,0:T(8,128)S(1)}, f32[64,512]{1,0:T(8,128)S(1)}) custom-call(s32[6]{0:T(128)S(1)} %stack.49.flags_ref, bf16[512,6912]{1,0:T(8,128)(2,1)S(1)} %bitcast.60, bf16[4608,128]{1,0:T(8,128)(2,1)S(1)} %collective-permute-done.8.refs_0_.refs_2_.refs_1_, bf16[2304,128]{1,0:T(8,128)(2,1)} %collective-permute-done.6.refs_1_, ...), custom_call_target="tpu_custom_call" | custom-call | flops 1 | bytes 1 | tf_op jit(solution)/shard_map/pallas_call | solution.py:163
  87.8 4.9 %collective-permute-done.10.refs_2_.refs_7_ = bf16[2304,128]{1,0:T(8,128)(2,1)S(1)} collective-permute-done((bf16[2304,128]{1,0:T(8,128)(2,1)S(1)}, bf16[2304,128]{1,0:T(8,128)(2,1)S(1)}, u32[]{:S(2)}, u32[]{:S(2)}) %collective-permute-start.10) | collective-permute-done | bytes 589856 | tf_op jit(solution)/shard_map/ppermute | solution.py:383
  94.2 5.8 %collective-permute-start.21 = (bf16[2304,128]{1,0:T(8,128)(2,1)}, bf16[2304,128]{1,0:T(8,128)(2,1)S(1)}, u32[]{:S(2)}, u32[]{:S(2)}) collective-permute-start(bf16[2304,128]{1,0:T(8,128)(2,1)} %broadcast_select_fusion), channel_id=1, source_target_pairs={{0,4},{4,0},{8,12},{12,8},{1,5},{5,1},{9,13},{13,9},{2,6},{6,2},{1... | collective-permute-start | bytes 1769480 | tf_op jit(solution)/shard_map/ppermute | solution.py:383
  99.9 3.0 %shard_map.88 = (f32[64,640]{1,0:T(8,128)S(1)}, f32[64,640]{1,0:T(8,128)}, f32[512,128]{1,0:T(8,128)S(1)}) custom-call(s32[6]{0:T(128)S(1)} %stack.49.flags_ref, bf16[4608,128]{1,0:T(8,128)(2,1)S(1)} %collective-permute-done.8.refs_0_.refs_2_.refs_1_, bf16[4608,128]{1,0:T(8,128)(2,1)S(1)} %collective-permute-done.8.refs_0_.refs_2_.refs_1_, ...), custom_call_target="tpu_custom_call" | custom-call | flops 1 | bytes 1 | tf_op jit(solution)/shard_map/pallas_call | solution.py:276
  113.6 3.0 %copy-done.1 = bf16[512,6912]{1,0:T(8,128)(2,1)S(1)} copy-done((bf16[512,6912]{1,0:T(8,128)(2,1)S(1)}, bf16[512,6912]{1,0:T(8,128)(2,1)}, u32[]{:S(2)}) %copy-start.1) | copy-done | bytes 7077912
  122.2 2.9 %collective-permute-done.15 = f32[32,2688]{1,0:T(8,128)S(1)} collective-permute-done((f32[32,2688]{1,0:T(8,128)S(1)}, f32[32,2688]{1,0:T(8,128)S(1)}, u32[]{:S(2)}, u32[]{:S(2)}) %collective-permute-start.15) | collective-permute-done | bytes 344096 | tf_op jit(solution)/shard_map/ppermute | solution.py:37
  125.1 2.8 %collective-permute-done.18 = bf16[128,512]{1,0:T(8,128)(2,1)S(1)} collective-permute-done((bf16[128,512]{1,0:T(8,128)(2,1)S(1)}, bf16[128,512]{1,0:T(8,128)(2,1)S(1)}, u32[]{:S(2)}, u32[]{:S(2)}) %collective-permute-start.18) | collective-permute-done | bytes 131104 | tf_op jit(solution)/shard_map/ppermute | solution.py:37
  136.1 2.6 %collective-permute-done.24 = f32[32,384]{1,0:T(8,128)S(1)} collective-permute-done((f32[32,384]{1,0:T(8,128)S(1)}, f32[32,384]{1,0:T(8,128)S(1)}, u32[]{:S(2)}, u32[]{:S(2)}) %collective-permute-start.24) | collective-permute-done | bytes 49184 | tf_op jit(solution)/shard_map/ppermute | solution.py:503
  139.0 2.7 %collective-permute-start.27 = (bf16[4,32,512]{2,1,0:T(8,128)(2,1)S(1)}, bf16[4,32,512]{2,1,0:T(8,128)(2,1)S(1)}, u32[]{:S(2)}, u32[]{:S(2)}) collective-permute-start(bf16[4,32,512]{2,1,0:T(8,128)(2,1)S(1)} %convolution_convert_fusion), channel_id=1, source_target_pairs={{0,12},{1,13},{2,14},{3,15},{4,5},{5,4},{6,7},{7,6},{8,9},{9,8},{1... | collective-permute-start | bytes 393224 | tf_op jit(solution)/shard_map/ppermute | solution.py:509
  144.0 3.3 %collective-permute-done.27 = bf16[4,32,512]{2,1,0:T(8,128)(2,1)S(1)} collective-permute-done((bf16[4,32,512]{2,1,0:T(8,128)(2,1)S(1)}, bf16[4,32,512]{2,1,0:T(8,128)(2,1)S(1)}, u32[]{:S(2)}, u32[]{:S(2)}) %collective-permute-start.27) | collective-permute-done | bytes 131104 | tf_op jit(solution)/shard_map/ppermute | solution.py:509
  153.9 2.5 %fusion.12 = f32[4,64]{1,0:T(4,128)S(1)} fusion(bf16[64,32,512]{2,1,0:T(8,128)(2,1)S(1)} %copy-done.14, bf16[4,32,512]{2,1,0:T(8,128)(2,1)S(1)} %collective-permute-done.25), kind=kOutput, calls=%fused_computation.17 | convolution fusion | flops 8388608 | bytes 2229248 | tf_op jit(solution)/shard_map/tea,jea->tj/dot_general | solution.py:491
  156.6 10.9 %all_to_all.5 = f32[16,2,16]{2,1,0:T(2,128)S(1)} all-to-all(f32[16,2,16]{2,1,0:T(2,128)S(1)} %copy.72), channel_id=1, replica_groups=mesh['groups'=2,'cand'=4,'eig'=2,'rep'=2] {'cand','eig','rep'}, dimensions={0} | all-to-all | bytes 4096 | tf_op jit(solution)/shard_map/all_to_all | solution.py:522
  (163 shorter events, 48.9 us)
Async XLA Ops:
  0.0 12.2 %collective-permute-start = (bf16[1280,128]{1,0:T(8,128)(2,1)}, bf16[1280,128]{1,0:T(8,128)(2,1)S(1)}, u32[]{:S(2)}, u32[]{:S(2)}) collective-permute-start(bf16[1280,128]{1,0:T(8,128)(2,1)} %refs_0_.3), channel_id=1, source_target_pairs={{0,1},{1,0},{2,3},{3,2},{4,8},{5,9},{6,10},{7,11},{8,4},{9,5},{10,... | collective-permute-start | bytes 983048 | tf_op jit(solution)/shard_map/ppermute | solution.py:393
  0.5 13.1 %collective-permute-start.1 = (bf16[1280,128]{1,0:T(8,128)(2,1)}, bf16[1280,128]{1,0:T(8,128)(2,1)}, u32[]{:S(2)}, u32[]{:S(2)}) collective-permute-start(bf16[1280,128]{1,0:T(8,128)(2,1)} %refs_0_.3), channel_id=1, source_target_pairs={{0,4},{4,0},{8,12},{12,8},{1,5},{5,1},{9,13},{13,9},{2,6},{6,2},{1... | collective-permute-start | bytes 983048 | tf_op jit(solution)/shard_map/ppermute | solution.py:401
  7.0 31.7 %collective-permute-start.4 = (bf16[4608,128]{1,0:T(8,128)(2,1)}, bf16[4608,128]{1,0:T(8,128)(2,1)S(1)}, u32[]{:S(2)}, u32[]{:S(2)}) collective-permute-start(bf16[4608,128]{1,0:T(8,128)(2,1)} %constant_dynamic-slice_fusion), channel_id=1, source_target_pairs={{0,4},{4,0},{8,12},{12,8},{1,5},{5,1},{9,13},{13,9},{2,6},{6,2},{1... | collective-permute-start | bytes 3538952 | tf_op jit(solution)/shard_map/ppermute | solution.py:403
  8.2 25.6 %collective-permute-start.6 = (bf16[2304,128]{1,0:T(8,128)(2,1)}, bf16[2304,128]{1,0:T(8,128)(2,1)}, u32[]{:S(2)}, u32[]{:S(2)}) collective-permute-start(bf16[2304,128]{1,0:T(8,128)(2,1)} %get-tuple-element.84), channel_id=1, source_target_pairs={{0,1},{1,0},{2,3},{3,2},{4,8},{5,9},{6,10},{7,11},{8,4},{9,5},{10,... | collective-permute-start | bytes 1769480 | tf_op jit(solution)/shard_map/ppermute | solution.py:393
  13.5 9.7 %collective-permute-start.2 = (bf16[1280,128]{1,0:T(8,128)(2,1)}, bf16[1280,128]{1,0:T(8,128)(2,1)}, u32[]{:S(2)}, u32[]{:S(2)}) collective-permute-start(bf16[1280,128]{1,0:T(8,128)(2,1)} %collective-permute-done.1.refs_1_), channel_id=1, source_target_pairs={{0,1},{1,0},{2,3},{3,2},{4,8},{5,9},{6,10},{7,11},{8,4},{9,5},{10,... | collective-permute-start | bytes 983048 | tf_op jit(solution)/shard_map/ppermute | solution.py:393
  24.6 27.0 %collective-permute-start.3 = (bf16[2560,128]{1,0:T(8,128)(2,1)S(1)}, bf16[2560,128]{1,0:T(8,128)(2,1)S(1)}, u32[]{:S(2)}, u32[]{:S(2)}) collective-permute-start(bf16[2560,128]{1,0:T(8,128)(2,1)S(1)} %maximum_select_fusion.1), channel_id=1, source_target_pairs={{0,4},{4,0},{8,12},{12,8},{1,5},{5,1},{9,13},{13,9},{2,6},{6,2},{1... | collective-permute-start | bytes 1966088 | tf_op jit(solution)/shard_map/ppermute | solution.py:383
  38.8 15.4 %collective-permute-start.5 = (bf16[2304,128]{1,0:T(8,128)(2,1)S(1)}, bf16[2304,128]{1,0:T(8,128)(2,1)S(1)}, u32[]{:S(2)}, u32[]{:S(2)}) collective-permute-start(bf16[2304,128]{1,0:T(8,128)(2,1)S(1)} %get-tuple-element.86), channel_id=1, source_target_pairs={{0,1},{1,0},{2,3},{3,2},{4,8},{5,9},{6,10},{7,11},{8,4},{9,5},{10,... | collective-permute-start | bytes 1769480 | tf_op jit(solution)/shard_map/ppermute | solution.py:393
  51.6 12.9 %collective-permute-start.11 = (bf16[2304,128]{1,0:T(8,128)(2,1)S(1)}, bf16[2304,128]{1,0:T(8,128)(2,1)S(1)}, u32[]{:S(2)}, u32[]{:S(2)}) collective-permute-start(bf16[2304,128]{1,0:T(8,128)(2,1)S(1)} %slice.102), channel_id=1, source_target_pairs={{0,1},{1,0},{2,3},{3,2},{4,8},{5,9},{6,10},{7,11},{8,4},{9,5},{10,... | collective-permute-start | bytes 1769480 | tf_op jit(solution)/shard_map/ppermute | solution.py:393
  51.7 29.3 %collective-permute-start.8 = (bf16[4608,128]{1,0:T(8,128)(2,1)S(1)}, bf16[4608,128]{1,0:T(8,128)(2,1)S(1)}, u32[]{:S(2)}, u32[]{:S(2)}) collective-permute-start(bf16[4608,128]{1,0:T(8,128)(2,1)S(1)} %maximum_select_fusion), channel_id=1, source_target_pairs={{0,4},{4,0},{8,12},{12,8},{1,5},{5,1},{9,13},{13,9},{2,6},{6,2},{1... | collective-permute-start | bytes 3538952 | tf_op jit(solution)/shard_map/ppermute | solution.py:416
  54.2 26.8 %collective-permute-start.9 = (bf16[2304,128]{1,0:T(8,128)(2,1)S(1)}, bf16[2304,128]{1,0:T(8,128)(2,1)S(1)}, u32[]{:S(2)}, u32[]{:S(2)}) collective-permute-start(bf16[2304,128]{1,0:T(8,128)(2,1)S(1)} %copy-done.16), channel_id=1, source_target_pairs={{0,1},{1,0},{2,3},{3,2},{4,8},{5,9},{6,10},{7,11},{8,4},{9,5},{10,... | collective-permute-start | bytes 1769480 | tf_op jit(solution)/shard_map/ppermute | solution.py:393
  54.3 38.4 %collective-permute-start.10 = (bf16[2304,128]{1,0:T(8,128)(2,1)S(1)}, bf16[2304,128]{1,0:T(8,128)(2,1)S(1)}, u32[]{:S(2)}, u32[]{:S(2)}) collective-permute-start(bf16[2304,128]{1,0:T(8,128)(2,1)S(1)} %broadcast_select_fusion.1), channel_id=1, source_target_pairs={{0,4},{4,0},{8,12},{12,8},{1,5},{5,1},{9,13},{13,9},{2,6},{6,2},{1... | collective-permute-start | bytes 1769480 | tf_op jit(solution)/shard_map/ppermute | solution.py:383
  64.5 28.2 %collective-permute-start.12 = (bf16[2304,128]{1,0:T(8,128)(2,1)S(1)}, bf16[2304,128]{1,0:T(8,128)(2,1)S(1)}, u32[]{:S(2)}, u32[]{:S(2)}) collective-permute-start(bf16[2304,128]{1,0:T(8,128)(2,1)S(1)} %get-tuple-element.63), channel_id=1, source_target_pairs={{0,1},{1,0},{2,3},{3,2},{4,8},{5,9},{6,10},{7,11},{8,4},{9,5},{10,... | collective-permute-start | bytes 1769480 | tf_op jit(solution)/shard_map/ppermute | solution.py:393
  92.7 14.3 %collective-permute-start.16 = (f32[256,512]{1,0:T(8,128)}, f32[256,512]{1,0:T(8,128)}, u32[]{:S(2)}, u32[]{:S(2)}) collective-permute-start(f32[256,512]{1,0:T(8,128)} %get-tuple-element.70), channel_id=1, source_target_pairs={{0,1},{1,0},{2,3},{3,2},{4,5},{5,4},{6,7},{7,6},{8,9},{9,8},{10,11... | collective-permute-start | bytes 1572872 | tf_op jit(solution)/shard_map/ppermute | solution.py:37
  92.8 17.3 %collective-permute-start.13 = (f32[64,2048]{1,0:T(8,128)}, f32[64,2048]{1,0:T(8,128)}, u32[]{:S(2)}, u32[]{:S(2)}) collective-permute-start(f32[64,2048]{1,0:T(8,128)} %get-tuple-element.65), channel_id=1, source_target_pairs={{0,1},{1,0},{2,3},{3,2},{4,5},{5,4},{6,7},{7,6},{8,9},{9,8},{10,11... | collective-permute-start | bytes 1572872 | tf_op jit(solution)/shard_map/ppermute | solution.py:37
  94.2 19.5 %collective-permute-start.21 = (bf16[2304,128]{1,0:T(8,128)(2,1)}, bf16[2304,128]{1,0:T(8,128)(2,1)S(1)}, u32[]{:S(2)}, u32[]{:S(2)}) collective-permute-start(bf16[2304,128]{1,0:T(8,128)(2,1)} %broadcast_select_fusion), channel_id=1, source_target_pairs={{0,4},{4,0},{8,12},{12,8},{1,5},{5,1},{9,13},{13,9},{2,6},{6,2},{1... | collective-permute-start | bytes 1769480 | tf_op jit(solution)/shard_map/ppermute | solution.py:383
  108.5 10.6 %collective-permute-start.17 = (f32[128,512]{1,0:T(8,128)S(1)}, f32[128,512]{1,0:T(8,128)S(1)}, u32[]{:S(2)}, u32[]{:S(2)}) collective-permute-start(f32[128,512]{1,0:T(8,128)S(1)} %slice_select_fusion), channel_id=1, source_target_pairs={{0,2},{2,0},{1,3},{3,1},{4,6},{6,4},{5,7},{7,5},{8,10},{10,8},{9,1... | collective-permute-start | bytes 786440 | tf_op jit(solution)/shard_map/ppermute | solution.py:37
  111.2 13.9 %collective-permute-start.15 = (f32[32,2688]{1,0:T(8,128)S(1)}, f32[32,2688]{1,0:T(8,128)S(1)}, u32[]{:S(2)}, u32[]{:S(2)}) collective-permute-start(f32[32,2688]{1,0:T(8,128)S(1)} %broadcast_select_fusion.2), channel_id=1, source_target_pairs={{0,2},{2,0},{1,3},{3,1},{4,6},{6,4},{5,7},{7,5},{8,10},{10,8},{9,1... | collective-permute-start | bytes 1032200 | tf_op jit(solution)/shard_map/ppermute | solution.py:37
  119.2 8.7 %collective-permute-start.18 = (bf16[128,512]{1,0:T(8,128)(2,1)S(1)}, bf16[128,512]{1,0:T(8,128)(2,1)S(1)}, u32[]{:S(2)}, u32[]{:S(2)}) collective-permute-start(bf16[128,512]{1,0:T(8,128)(2,1)S(1)} %add_convert_fusion), channel_id=1, source_target_pairs={{0,2},{2,0},{1,3},{3,1},{4,6},{6,4},{5,7},{7,5},{8,10},{10,8},{9,1... | collective-permute-start | bytes 393224 | tf_op jit(solution)/shard_map/ppermute | solution.py:37
  120.8 9.6 %collective-permute-start.23 = (f32[32,896]{1,0:T(8,128)S(1)}, f32[32,896]{1,0:T(8,128)S(1)}, u32[]{:S(2)}, u32[]{:S(2)}) collective-permute-start(f32[32,896]{1,0:T(8,128)S(1)} %slice_select_fusion.1), channel_id=1, source_target_pairs={{0,2},{2,0},{1,3},{3,1},{4,6},{6,4},{5,7},{7,5},{8,10},{10,8},{9,1... | collective-permute-start | bytes 344072 | tf_op jit(solution)/shard_map/ppermute | solution.py:37
  128.0 8.1 %collective-permute-start.20 = (f32[32,1152]{1,0:T(8,128)S(1)}, f32[32,1152]{1,0:T(8,128)S(1)}, u32[]{:S(2)}, u32[]{:S(2)}) collective-permute-start(f32[32,1152]{1,0:T(8,128)S(1)} %slice.105), channel_id=1, source_target_pairs={{0,4},{4,0},{8,12},{12,8},{1,5},{5,1},{9,13},{13,9},{2,6},{6,2},{1... | collective-permute-start | bytes 442376 | tf_op jit(solution)/shard_map/ppermute | solution.py:504
  136.1 7.9 %collective-permute-start.28 = (bf16[4,32,512]{2,1,0:T(8,128)(2,1)S(1)}, bf16[4,32,512]{2,1,0:T(8,128)(2,1)S(1)}, u32[]{:S(2)}, u32[]{:S(2)}) collective-permute-start(bf16[4,32,512]{2,1,0:T(8,128)(2,1)S(1)} %convolution_convert_fusion.3), channel_id=1, source_target_pairs={{0,1},{1,0},{2,3},{3,2},{4,8},{5,9},{6,10},{7,11},{8,4},{9,5},{10,... | collective-permute-start | bytes 393224 | tf_op jit(solution)/shard_map/ppermute | solution.py:393
  139.0 8.3 %collective-permute-start.27 = (bf16[4,32,512]{2,1,0:T(8,128)(2,1)S(1)}, bf16[4,32,512]{2,1,0:T(8,128)(2,1)S(1)}, u32[]{:S(2)}, u32[]{:S(2)}) collective-permute-start(bf16[4,32,512]{2,1,0:T(8,128)(2,1)S(1)} %convolution_convert_fusion), channel_id=1, source_target_pairs={{0,12},{1,13},{2,14},{3,15},{4,5},{5,4},{6,7},{7,6},{8,9},{9,8},{1... | collective-permute-start | bytes 393224 | tf_op jit(solution)/shard_map/ppermute | solution.py:509
  141.9 9.4 %collective-permute-start.26 = (bf16[4,32,512]{2,1,0:T(8,128)(2,1)S(1)}, bf16[4,32,512]{2,1,0:T(8,128)(2,1)S(1)}, u32[]{:S(2)}, u32[]{:S(2)}) collective-permute-start(bf16[4,32,512]{2,1,0:T(8,128)(2,1)S(1)} %fusion.8), channel_id=1, source_target_pairs={{0,8},{8,0},{4,12},{12,4},{1,9},{9,1},{5,13},{13,5},{2,10},{10,2},... | collective-permute-start | bytes 393224 | tf_op jit(solution)/shard_map/ppermute | solution.py:510
  142.2 11.7 %collective-permute-start.25 = (bf16[4,32,512]{2,1,0:T(8,128)(2,1)S(1)}, bf16[4,32,512]{2,1,0:T(8,128)(2,1)S(1)}, u32[]{:S(2)}, u32[]{:S(2)}) collective-permute-start(bf16[4,32,512]{2,1,0:T(8,128)(2,1)S(1)} %convolution_convert_fusion.2), channel_id=1, source_target_pairs={{0,4},{4,0},{8,12},{12,8},{1,5},{5,1},{9,13},{13,9},{2,6},{6,2},{1... | collective-permute-start | bytes 393224 | tf_op jit(solution)/shard_map/ppermute | solution.py:511
  (32 other events, 273.5 us)

commit v8 on v7

--- a/solution.py
+++ b/solution.py
@@ -209,6 +209,9 @@
     if start is not None:
         operands.append(start)
         specs.append(pl.BlockSpec((tok, cols), whole))
+    elif tail:
+        operands.append(grads)
+        specs.append(pl.BlockSpec((tok, step), lambda i, flags_ref: (0, 2 * STEPS + i)))
 
     def kernel(flags_ref, *refs):
         i = pl.program_id(0)
@@ -216,7 +219,8 @@
         tail_refs = refs[count + len(shards) : len(operands)]
         keep_ref, give_ref, *rest = refs[len(operands) :]
         if tail and start is None:
-            total_ref, sums_ref, turned_ref = rest
+            total_ref, copied_ref, sums_ref, turned_ref = rest
+            copied_ref[...] = tail_refs[-1][...]
         elif tail:
             sums_ref, turned_ref, total_ref, wide_ref = rest
         else:
@@ -271,6 +275,8 @@
     if tail and start is None:
         out_shape.append(jax.ShapeDtypeStruct((tok, cols), jnp.float32))
         out_specs.append(pl.BlockSpec((tok, cols), whole))
+        out_shape.append(jax.ShapeDtypeStruct((tok, depth), grads.dtype))
+        out_specs.append(pl.BlockSpec((tok, step), lambda i, flags_ref: (0, i)))
     elif tail:
         scratch += [pltpu.VMEM((tok, cols), jnp.float32), pltpu.VMEM((cols, tok), jnp.float32)]
     return pl.pallas_call(
@@ -405,19 +411,22 @@
     m2 = middle(second)
     started = after(flags, rows, second)
     stacked, *more_stacked = stack_blocks(started, grads, depth)
-    part_own = feature_dots(started, grads, [([(basis_out, 0)], 0, 0, 3 * STEPS, False)])
+    part_own = feature_dots(
+        after(started, s0, m0), grads, [([(basis_out, 0)], 0, 0, 3 * STEPS, False)]
+    )
     precond = (test_grads.astype(jnp.float32) / (eigval + damping)).astype(jnp.bfloat16)
     m1 = middle(after(s0, m0))
     third = jnp.concatenate([basis_out[2 * depth :], basis_out[: 2 * rows_in - depth]])
     s3 = side(third, jnp.concatenate([m0, m1]))
-    m3 = middle(after(basis_out[2 * depth :], m1, m2, precond, stacked, *more_stacked, *part_own))
+    m3 = middle(after(basis_out[2 * depth :], precond, stacked, *more_stacked, *part_own))
     m5 = middle(s12[depth:])
     to_s45 = pick(stacked, jnp.concatenate([m2, m3]))
     s45 = lax.ppermute(after(to_s45, s3), "cand", SIDE)
     m6 = middle(s3[:depth])
     m4 = middle(after(basis_out[:depth], m5))
     s6 = side(more_stacked[0], m5)
-    s7 = side(after(more_stacked[1], s45), m6)
+    to_s7 = pick(after(more_stacked[1], s45), m6)
+    s7 = lax.ppermute(to_s7, "cand", SIDE)
     m7 = middle(after(s12[:depth], m6))
 
     part_in = input_dots(
@@ -445,9 +454,12 @@
     shards = [(basis_out, 0), (m4, 0), (m7, 0)]
     pieces = [(s45, 0), (s45, STEPS), (s6, 0), (s7, 0)]
     blocks = [(shard, piece) for piece in (0, 1) for shard in (0, 1)]
-    part_first = partner_dots(after(flags, *part_b), pieces[:2], shards[:2], blocks, depth)
-    *part_second, part_c = partner_dots(
-        after(flags, *part_first),
+    part_first = partner_dots(after(flags, to_s7, *part_b), pieces[:2], shards[:2], blocks, depth)
+    parts = [part_own, part_a, part_b, part_first]
+    parts = [jnp.concatenate(part, axis=1) for part in zip(*parts)]
+    core_sums = core_sum(*after(parts, s6, m7))
+    *part_second, part_c, last_grads = partner_dots(
+        after(flags, core_sums),
         pieces[:3],
         shards,
         [(2, 0), (2, 1), (0, 2), (1, 2), (2, 2)],
@@ -458,19 +470,16 @@
     rot_in = chip_sum(core_sum(*after(part_in, s6, m7)))
     rot_in = gather_rows(rot_in.astype(jnp.bfloat16))
     rot_in = rot_in.reshape(tiles_here, TILE, 4 * cols)
-    parts = [part_own, part_a, part_b, part_first]
-    parts = [jnp.concatenate(part, axis=1) for part in zip(*parts)]
-    core_sums = core_sum(*after(parts, s6, m7))
     sums = chip_sum(jnp.concatenate([core_sums, core_sum(*part_second)], axis=1))
     sum_own, sum_a, sum_b = [sums[:, i * tok_rows : (i + 1) * tok_rows] for i in range(3)]
     part_last = partner_dots(
-        after(flags, part_c, core_sums),
+        after(flags, part_c),
         pieces[3:],
         shards,
         [(0, 0), (1, 0), (2, 0)],
         depth,
-        grads,
-        [([(s7, 0), (m6, 0)], 2 * STEPS, False)],
+        last_grads,
+        [([(s7, 0), (m6, 0)], 0, False)],
         part_c,
     )
     sum_last = chip_sum(core_sum(*part_last))
@@ -487,20 +496,22 @@
             preferred_element_type=jnp.float32,
         ).astype(jnp.bfloat16)
 
-    def pair_scores(prods, source):
+    def pair_scores(*received):
+        prods = jnp.concatenate([x for x, source in received])
         scores = jnp.einsum("tea,jea->tj", prods, precond, preferred_element_type=jnp.float32)
-        ignored_mask, onehot = tile_layout(
-            pair_tiles, last_rows, source * tiles_here, tiles_here, TILE
-        )
+        onehot = jnp.concatenate([
+            tile_layout(pair_tiles, last_rows, source * tiles_here, tiles_here, TILE)[1]
+            for x, source in received
+        ])
         return jnp.sum(jnp.where(onehot[:, :, None], scores[:, None, :], 0.0), axis=0)
 
     def columns(x, *which):
         return jnp.concatenate([x[:, i * TILE : (i + 1) * TILE] for i in which], axis=1)
 
-    total = pair_scores(tile_prods(sum_own), plane)
+    prods_own = tile_prods(sum_own)
     prods_middle = tile_prods(sum_b)
     from_middle = middle(prods_middle)
-    last = lax.ppermute(after(sum_last[:, tok_rows:], total, prods_middle), "cand", SIDE)
+    last = lax.ppermute(after(sum_last[:, tok_rows:], prods_own, prods_middle), "cand", SIDE)
     back = lax.ppermute(sums[:, 3 * tok_rows :], "cand", SIDE)
     both = jnp.where(end, jnp.concatenate([back, last], axis=1), 0.0)
     prods_a = tile_prods(sum_a + columns(both, 0, 2, 6, 9))
@@ -509,9 +520,8 @@
     from_far = lax.ppermute(prods_c, ALL, far)
     from_two = lax.ppermute(pick(prods_b, prods_c), "cand", TWO)
     from_side = lax.ppermute(prods_a, "cand", SIDE)
-    total = total + pair_scores(from_side, plane ^ 1)
-    total = total + pair_scores(from_two, plane ^ 2)
-    total = total + pair_scores(pick(from_far, from_middle), plane ^ 3)
+    total = pair_scores((prods_own, plane), (from_side, plane ^ 1))
+    total = total + pair_scores((from_two, plane ^ 2), (pick(from_far, from_middle), plane ^ 3))
     return final_sum(total)
 
 

time: 169 us -> 168 us (level)
  local copies, waits for them, and re-layouts: 12.5 us -> 20.1 us
  matrix products: 10.9 us -> 6.09 us
  starting transfers between devices: 46.6 us -> 42.9 us
  other arithmetic: 15.4 us -> 11.9 us
  waiting for transfers between devices: 45.7 us -> 48.8 us
    ppermute x3 -> x2, starting transfers between devices: 25.3 us -> 15 us  [side(): return lax.ppermute(pick(at_end, at_middle), 'cand', SIDE)]
    unnamed x52 -> x72, local copies, waits for them, and re-layouts: 8.52 us -> 16.1 us
    ppermute x9, waiting for transfers between devices: 6.79 us -> 14.2 us  [swap(): return lax.ppermute(x, axis_name, [(0, 1), (1, 0)])]
    dot_general x4 -> x2, matrix products: 9.87 us -> 5.09 us  [pair_scores(): jnp.einsum('tea,jea->tj', prods, precond, preferred_element_type=jnp.floa...]
    ppermute x1, starting transfers between devices: 2.35 us -> 6.75 us  [line_plan(): back = lax.ppermute(sums[:, 3 * tok_rows:], 'cand', SIDE)]
    ppermute x1, waiting for transfers between devices: 0.01 us -> 3.43 us  [line_plan(): back = lax.ppermute(sums[:, 3 * tok_rows:], 'cand', SIDE)]
    ppermute x3 -> x2, waiting for transfers between devices: 17.6 us -> 14.2 us  [side(): return lax.ppermute(pick(at_end, at_middle), 'cand', SIDE)]
    ppermute x1, starting transfers between devices: 0.01 us -> 3.15 us  [line_plan(): s12 = lax.ppermute(rows, 'cand', SIDE)]
  transfers between devices with their start and end apart: 29 -> 29, of which waited for: 12 -> 13; matrix products, arithmetic and copies ran while one was open for 16% -> 11% of each run, Pallas kernels for 15% -> 16%
where the time goes in v8:
time: 168 us; the launch traced here: 167 us
  waiting for transfers between devices  48.8 us (29%)
  starting transfers between devices  42.9 us (26%)
  Pallas kernels  26.6 us (16%)
  local copies, waits for them, and re-layouts  20.1 us (12%)
  other arithmetic  11.9 us (7%)
  blocking collectives  10.5 us (6%)
  matrix products  6.09 us (4%)
    unnamed x72, local copies, waits for them, and re-layouts  16.1 us
    ppermute x2, starting transfers between devices, side(): return lax.ppermute(pick(at_end, at_middle), 'cand', SIDE)  15 us
    ppermute x9, waiting for transfers between devices, swap(): return lax.ppermute(x, axis_name, [(0, 1), (1, 0)])  14.2 us
    ppermute x2, waiting for transfers between devices, side(): return lax.ppermute(pick(at_end, at_middle), 'cand', SIDE)  14.2 us
    pallas_call x3, Pallas kernels, feature_dots(): pl.pallas_call(kernel, out_shape=out_shape, grid_spec=pltpu.PrefetchScala...  13.3 us
    all_to_all x1, blocking collectives, final_sum(): return jnp.sum(lax.all_to_all(blocks, ALL, 0, 0, tiled=True), axis=0)  10.5 us
    ppermute x1, waiting for transfers between devices, line_plan(): s45 = lax.ppermute(after(to_s45, s3), 'cand', SIDE)  7.76 us
    pallas_call x3, Pallas kernels, partner_dots(): pl.pallas_call(kernel, out_shape=out_shape, grid_spec=pltpu.PrefetchScala...  7.45 us
  transfers between devices with their start and end apart: 29, of which 13 were waited for; matrix products, arithmetic and copies ran while one was open for 11% of the time, Pallas kernels for 16%

profile of v8, /device:TPU:0, one launch (start us, length us, event | category | flops | bytes accessed | tf_op | source)
XLA Modules:
  0.0 167.4 jit_solution(8800036577753553888)
XLA Ops:
  0.0 3.0 %collective-permute-start = (bf16[1280,128]{1,0:T(8,128)(2,1)}, bf16[1280,128]{1,0:T(8,128)(2,1)}, u32[]{:S(2)}, u32[]{:S(2)}) collective-permute-start(bf16[1280,128]{1,0:T(8,128)(2,1)} %refs_0_.3), channel_id=1, source_target_pairs={{0,4},{4,0},{8,12},{12,8},{1,5},{5,1},{9,13},{13,9},{2,6},{6,2},{1... | collective-permute-start | bytes 983048 | tf_op jit(solution)/shard_map/ppermute | solution.py:407
  5.4 3.1 %collective-permute-start.4 = (bf16[4608,128]{1,0:T(8,128)(2,1)}, bf16[4608,128]{1,0:T(8,128)(2,1)S(1)}, u32[]{:S(2)}, u32[]{:S(2)}) collective-permute-start(bf16[4608,128]{1,0:T(8,128)(2,1)} %constant_dynamic-slice_fusion), channel_id=1, source_target_pairs={{0,4},{4,0},{8,12},{12,8},{1,5},{5,1},{9,13},{13,9},{2,6},{6,2},{1... | collective-permute-start | bytes 3538952 | tf_op jit(solution)/shard_map/ppermute | solution.py:409
  11.9 3.0 %copy-done = bf16[512,6912]{1,0:T(8,128)(2,1)S(1)} copy-done((bf16[512,6912]{1,0:T(8,128)(2,1)S(1)}, bf16[512,6912]{1,0:T(8,128)(2,1)}, u32[]{:S(2)}) %copy-start) | copy-done | bytes 7077912
  21.2 3.0 %copy-done.1 = bf16[512,6912]{1,0:T(8,128)(2,1)S(1)} copy-done((bf16[512,6912]{1,0:T(8,128)(2,1)S(1)}, bf16[512,6912]{1,0:T(8,128)(2,1)}, u32[]{:S(2)}) %copy-start.1) | copy-done | bytes 7077912
  24.2 4.6 %shard_map.82 = (f32[64,512]{1,0:T(8,128)S(1)}, f32[64,512]{1,0:T(8,128)S(1)}) custom-call(s32[6]{0:T(128)S(1)} %stack.49.flags_ref, bf16[512,6912]{1,0:T(8,128)(2,1)S(1)} %copy-done.1, bf16[6912,128]{1,0:T(8,128)(2,1)S(1)} %copy-done.3), custom_call_target="tpu_custom_call" | custom-call | flops 1 | bytes 1 | tf_op jit(solution)/shard_map/pallas_call | solution.py:163
  29.1 5.8 %collective-permute-start.3 = (bf16[2560,128]{1,0:T(8,128)(2,1)S(1)}, bf16[2560,128]{1,0:T(8,128)(2,1)S(1)}, u32[]{:S(2)}, u32[]{:S(2)}) collective-permute-start(bf16[2560,128]{1,0:T(8,128)(2,1)S(1)} %maximum_select_fusion.1), channel_id=1, source_target_pairs={{0,4},{4,0},{8,12},{12,8},{1,5},{5,1},{9,13},{13,9},{2,6},{6,2},{1... | collective-permute-start | bytes 1966088 | tf_op jit(solution)/shard_map/ppermute | solution.py:389
  39.2 11.1 %collective-permute-done.3.refs_2_.refs_4_.refs_1_ = bf16[2560,128]{1,0:T(8,128)(2,1)S(1)} collective-permute-done((bf16[2560,128]{1,0:T(8,128)(2,1)S(1)}, bf16[2560,128]{1,0:T(8,128)(2,1)S(1)}, u32[]{:S(2)}, u32[]{:S(2)}) %collective-permute-start.3) | collective-permute-done | bytes 655392 | tf_op jit(solution)/shard_map/ppermute | solution.py:389
  52.8 4.6 %shard_map.83 = (f32[256,512]{1,0:T(8,128)S(1)}, f32[256,512]{1,0:T(8,128)}) custom-call(s32[6]{0:T(128)S(1)} %stack.49.flags_ref, bf16[512,1280]{1,0:T(8,128)(2,1)S(1)} %copy-done.16, bf16[1280,128]{1,0:T(8,128)(2,1)S(1)} %copy-done.25, bf16[1280,128]{1,0:T(8,128)(2,1)} %collective-permute-done.refs_1_, ...), custom_call_target="tpu_custom_call" | custom-call | flops 1 | bytes 1 | tf_op jit(solution)/shard_map/pallas_call | solution.py:360
  58.3 9.2 %collective-permute-start.11 = (bf16[2304,128]{1,0:T(8,128)(2,1)S(1)}, bf16[2304,128]{1,0:T(8,128)(2,1)S(1)}, u32[]{:S(2)}, u32[]{:S(2)}) collective-permute-start(bf16[2304,128]{1,0:T(8,128)(2,1)S(1)} %broadcast_select_fusion), channel_id=1, source_target_pairs={{0,4},{4,0},{8,12},{12,8},{1,5},{5,1},{9,13},{13,9},{2,6},{6,2},{1... | collective-permute-start | bytes 1769480 | tf_op jit(solution)/shard_map/ppermute | solution.py:389
  67.5 3.8 %shard_map.84 = (f32[64,512]{1,0:T(8,128)S(1)}, f32[64,512]{1,0:T(8,128)S(1)}) custom-call(s32[6]{0:T(128)S(1)} %stack.49.flags_ref, bf16[512,6912]{1,0:T(8,128)(2,1)S(1)} %bitcast.56, bf16[4608,128]{1,0:T(8,128)(2,1)S(1)} %copy-done.7, bf16[2560,128]{1,0:T(8,128)(2,1)S(1)} %collective-permute-done.3.refs_2_.refs_4_.refs_1_), custom_call_target="tpu_custom_call" | custom-call | flops 1 | bytes 1 | tf_op jit(solution)/shard_map/pallas_call | solution.py:163
  71.4 7.8 %collective-permute-done.8.refs_0_.refs_2_.refs_1_ = bf16[4608,128]{1,0:T(8,128)(2,1)S(1)} collective-permute-done((bf16[4608,128]{1,0:T(8,128)(2,1)S(1)}, bf16[4608,128]{1,0:T(8,128)(2,1)S(1)}, u32[]{:S(2)}, u32[]{:S(2)}) %collective-permute-start.8) | collective-permute-done | bytes 1179680 | tf_op jit(solution)/shard_map/ppermute | solution.py:424
  81.8 4.9 %shard_map.86 = (f32[64,512]{1,0:T(8,128)S(1)}, f32[64,512]{1,0:T(8,128)S(1)}) custom-call(s32[6]{0:T(128)S(1)} %stack.49.flags_ref, bf16[512,6912]{1,0:T(8,128)(2,1)S(1)} %bitcast.56, bf16[4608,128]{1,0:T(8,128)(2,1)S(1)} %collective-permute-done.8.refs_0_.refs_2_.refs_1_, bf16[2304,128]{1,0:T(8,128)(2,1)} %collective-permute-done.6.refs_1_, ...), custom_call_target="tpu_custom_call" | custom-call | flops 1 | bytes 1 | tf_op jit(solution)/shard_map/pallas_call | solution.py:163
  88.7 3.1 %collective-permute-done.11.refs_2_.refs_7_ = bf16[2304,128]{1,0:T(8,128)(2,1)S(1)} collective-permute-done((bf16[2304,128]{1,0:T(8,128)(2,1)S(1)}, bf16[2304,128]{1,0:T(8,128)(2,1)S(1)}, u32[]{:S(2)}, u32[]{:S(2)}) %collective-permute-start.11) | collective-permute-done | bytes 589856 | tf_op jit(solution)/shard_map/ppermute | solution.py:389
  97.8 3.0 %copy-done.2 = bf16[512,6912]{1,0:T(8,128)(2,1)S(1)} copy-done((bf16[512,6912]{1,0:T(8,128)(2,1)S(1)}, bf16[512,6912]{1,0:T(8,128)(2,1)}, u32[]{:S(2)}) %copy-start.2) | copy-done | bytes 7077912
  101.9 2.8 %shard_map.88 = (f32[64,640]{1,0:T(8,128)S(1)}, f32[64,640]{1,0:T(8,128)S(1)}, f32[512,128]{1,0:T(8,128)S(1)}, bf16[512,2304]{1,0:T(8,128)(2,1)S(1)}) custom-call(s32[6]{0:T(128)S(1)} %stack.49.flags_ref, bf16[4608,128]{1,0:T(8,128)(2,1)S(1)} %collective-permute-done.8.refs_0_.refs_2_.refs_1_, ...), custom_call_target="tpu_custom_call" | custom-call | flops 1 | bytes 1 | tf_op jit(solution)/shard_map/pallas_call | solution.py:282
  107.8 3.8 %shard_map.89 = (f32[64,896]{1,0:T(8,128)S(1)}, f32[64,896]{1,0:T(8,128)S(1)}) custom-call(s32[6]{0:T(128)S(1)} %stack.49.flags_ref, bf16[2304,128]{1,0:T(8,128)(2,1)} %collective-permute-done.21.refs_0_.refs_5_, bf16[6912,128]{1,0:T(8,128)(2,1)S(1)} %copy-done.3, bf16[2304,128]{1,0:T(8,128)(2,1)S(1)} %collective-permute-done.9.refs_4_.refs_3_.refs_2_, ...), custom_call_target="tpu_custom_call" | custom-call | flops 1 | bytes 1 | tf_op jit(solution)/shard_map/pallas_call | solution.py:282
  117.2 8.4 %collective-permute-done.18 = bf16[128,512]{1,0:T(8,128)(2,1)S(1)} collective-permute-done((bf16[128,512]{1,0:T(8,128)(2,1)S(1)}, bf16[128,512]{1,0:T(8,128)(2,1)S(1)}, u32[]{:S(2)}, u32[]{:S(2)}) %collective-permute-start.18) | collective-permute-done | bytes 131104 | tf_op jit(solution)/shard_map/ppermute | solution.py:37
  127.8 6.7 %collective-permute-start.20 = (f32[32,1152]{1,0:T(8,128)S(1)}, f32[32,1152]{1,0:T(8,128)S(1)}, u32[]{:S(2)}, u32[]{:S(2)}) collective-permute-start(f32[32,1152]{1,0:T(8,128)S(1)} %slice.105), channel_id=1, source_target_pairs={{0,4},{4,0},{8,12},{12,8},{1,5},{5,1},{9,13},{13,9},{2,6},{6,2},{1... | collective-permute-start | bytes 442376 | tf_op jit(solution)/shard_map/ppermute | solution.py:515
  135.3 3.4 %collective-permute-done.20 = f32[32,1152]{1,0:T(8,128)S(1)} collective-permute-done((f32[32,1152]{1,0:T(8,128)S(1)}, f32[32,1152]{1,0:T(8,128)S(1)}, u32[]{:S(2)}, u32[]{:S(2)}) %collective-permute-start.20) | collective-permute-done | bytes 147488 | tf_op jit(solution)/shard_map/ppermute | solution.py:515
  141.6 2.6 %collective-permute-start.27 = (bf16[4,32,512]{2,1,0:T(8,128)(2,1)S(1)}, bf16[4,32,512]{2,1,0:T(8,128)(2,1)S(1)}, u32[]{:S(2)}, u32[]{:S(2)}) collective-permute-start(bf16[4,32,512]{2,1,0:T(8,128)(2,1)S(1)} %convolution_convert_fusion), channel_id=1, source_target_pairs={{0,12},{1,13},{2,14},{3,15},{4,5},{5,4},{6,7},{7,6},{8,9},{9,8},{1... | collective-permute-start | bytes 393224 | tf_op jit(solution)/shard_map/ppermute | solution.py:520
  145.4 5.3 %collective-permute-done.27 = bf16[4,32,512]{2,1,0:T(8,128)(2,1)S(1)} collective-permute-done((bf16[4,32,512]{2,1,0:T(8,128)(2,1)S(1)}, bf16[4,32,512]{2,1,0:T(8,128)(2,1)S(1)}, u32[]{:S(2)}, u32[]{:S(2)}) %collective-permute-start.27) | collective-permute-done | bytes 131104 | tf_op jit(solution)/shard_map/ppermute | solution.py:520
  150.7 2.5 %fusion.5 = f32[8,64]{1,0:T(8,128)S(1)} fusion(bf16[64,32,512]{2,1,0:T(8,128)(2,1)S(1)} %copy-done.26, bf16[8,32,512]{2,1,0:T(8,128)(2,1)S(1)} %pad_maximum_fusion.5), kind=kOutput, calls=%fused_computation.12 | convolution fusion | flops 16777216 | bytes 2361344 | tf_op jit(solution)/shard_map/tea,jea->tj/dot_general | solution.py:501
  153.6 2.5 %fusion.8 = f32[8,64]{1,0:T(8,128)S(1)} fusion(bf16[64,32,512]{2,1,0:T(8,128)(2,1)S(1)} %copy-done.26, bf16[8,32,512]{2,1,0:T(8,128)(2,1)S(1)} %pad_maximum_fusion.6), kind=kOutput, calls=%fused_computation.13 | convolution fusion | flops 16777216 | bytes 2361344 | tf_op jit(solution)/shard_map/tea,jea->tj/dot_general | solution.py:501
  156.4 10.5 %all_to_all.5 = f32[16,2,16]{2,1,0:T(2,128)S(1)} all-to-all(f32[16,2,16]{2,1,0:T(2,128)S(1)} %copy.58), channel_id=1, replica_groups=mesh['groups'=2,'cand'=4,'eig'=2,'rep'=2] {'cand','eig','rep'}, dimensions={0} | all-to-all | bytes 4096 | tf_op jit(solution)/shard_map/all_to_all | solution.py:532
  (182 shorter events, 48.0 us)
Async XLA Ops:
  0.0 19.1 %collective-permute-start = (bf16[1280,128]{1,0:T(8,128)(2,1)}, bf16[1280,128]{1,0:T(8,128)(2,1)}, u32[]{:S(2)}, u32[]{:S(2)}) collective-permute-start(bf16[1280,128]{1,0:T(8,128)(2,1)} %refs_0_.3), channel_id=1, source_target_pairs={{0,4},{4,0},{8,12},{12,8},{1,5},{5,1},{9,13},{13,9},{2,6},{6,2},{1... | collective-permute-start | bytes 983048 | tf_op jit(solution)/shard_map/ppermute | solution.py:407
  3.0 16.1 %collective-permute-start.1 = (bf16[1280,128]{1,0:T(8,128)(2,1)}, bf16[1280,128]{1,0:T(8,128)(2,1)S(1)}, u32[]{:S(2)}, u32[]{:S(2)}) collective-permute-start(bf16[1280,128]{1,0:T(8,128)(2,1)} %refs_0_.3), channel_id=1, source_target_pairs={{0,1},{1,0},{2,3},{3,2},{4,8},{5,9},{6,10},{7,11},{8,4},{9,5},{10,... | collective-permute-start | bytes 983048 | tf_op jit(solution)/shard_map/ppermute | solution.py:399
  5.4 31.6 %collective-permute-start.4 = (bf16[4608,128]{1,0:T(8,128)(2,1)}, bf16[4608,128]{1,0:T(8,128)(2,1)S(1)}, u32[]{:S(2)}, u32[]{:S(2)}) collective-permute-start(bf16[4608,128]{1,0:T(8,128)(2,1)} %constant_dynamic-slice_fusion), channel_id=1, source_target_pairs={{0,4},{4,0},{8,12},{12,8},{1,5},{5,1},{9,13},{13,9},{2,6},{6,2},{1... | collective-permute-start | bytes 3538952 | tf_op jit(solution)/shard_map/ppermute | solution.py:409
  9.8 27.4 %collective-permute-start.6 = (bf16[2304,128]{1,0:T(8,128)(2,1)}, bf16[2304,128]{1,0:T(8,128)(2,1)}, u32[]{:S(2)}, u32[]{:S(2)}) collective-permute-start(bf16[2304,128]{1,0:T(8,128)(2,1)} %get-tuple-element.88), channel_id=1, source_target_pairs={{0,1},{1,0},{2,3},{3,2},{4,8},{5,9},{6,10},{7,11},{8,4},{9,5},{10,... | collective-permute-start | bytes 1769480 | tf_op jit(solution)/shard_map/ppermute | solution.py:399
  19.1 9.8 %collective-permute-start.2 = (bf16[1280,128]{1,0:T(8,128)(2,1)}, bf16[1280,128]{1,0:T(8,128)(2,1)S(1)}, u32[]{:S(2)}, u32[]{:S(2)}) collective-permute-start(bf16[1280,128]{1,0:T(8,128)(2,1)} %collective-permute-done.refs_1_), channel_id=1, source_target_pairs={{0,1},{1,0},{2,3},{3,2},{4,8},{5,9},{6,10},{7,11},{8,4},{9,5},{10,... | collective-permute-start | bytes 983048 | tf_op jit(solution)/shard_map/ppermute | solution.py:399
  28.8 8.4 %collective-permute-start.7 = (bf16[2304,128]{1,0:T(8,128)(2,1)S(1)}, bf16[2304,128]{1,0:T(8,128)(2,1)S(1)}, u32[]{:S(2)}, u32[]{:S(2)}) collective-permute-start(bf16[2304,128]{1,0:T(8,128)(2,1)S(1)} %copy-done.27), channel_id=1, source_target_pairs={{0,1},{1,0},{2,3},{3,2},{4,8},{5,9},{6,10},{7,11},{8,4},{9,5},{10,... | collective-permute-start | bytes 1769480 | tf_op jit(solution)/shard_map/ppermute | solution.py:399
  29.1 21.1 %collective-permute-start.3 = (bf16[2560,128]{1,0:T(8,128)(2,1)S(1)}, bf16[2560,128]{1,0:T(8,128)(2,1)S(1)}, u32[]{:S(2)}, u32[]{:S(2)}) collective-permute-start(bf16[2560,128]{1,0:T(8,128)(2,1)S(1)} %maximum_select_fusion.1), channel_id=1, source_target_pairs={{0,4},{4,0},{8,12},{12,8},{1,5},{5,1},{9,13},{13,9},{2,6},{6,2},{1... | collective-permute-start | bytes 1966088 | tf_op jit(solution)/shard_map/ppermute | solution.py:389
  37.2 15.0 %collective-permute-start.5 = (bf16[2304,128]{1,0:T(8,128)(2,1)S(1)}, bf16[2304,128]{1,0:T(8,128)(2,1)S(1)}, u32[]{:S(2)}, u32[]{:S(2)}) collective-permute-start(bf16[2304,128]{1,0:T(8,128)(2,1)S(1)} %get-tuple-element.90), channel_id=1, source_target_pairs={{0,1},{1,0},{2,3},{3,2},{4,8},{5,9},{6,10},{7,11},{8,4},{9,5},{10,... | collective-permute-start | bytes 1769480 | tf_op jit(solution)/shard_map/ppermute | solution.py:399
  50.3 28.9 %collective-permute-start.8 = (bf16[4608,128]{1,0:T(8,128)(2,1)S(1)}, bf16[4608,128]{1,0:T(8,128)(2,1)S(1)}, u32[]{:S(2)}, u32[]{:S(2)}) collective-permute-start(bf16[4608,128]{1,0:T(8,128)(2,1)S(1)} %maximum_select_fusion), channel_id=1, source_target_pairs={{0,4},{4,0},{8,12},{12,8},{1,5},{5,1},{9,13},{13,9},{2,6},{6,2},{1... | collective-permute-start | bytes 3538952 | tf_op jit(solution)/shard_map/ppermute | solution.py:424
  52.1 19.2 %collective-permute-start.10 = (bf16[2304,128]{1,0:T(8,128)(2,1)S(1)}, bf16[2304,128]{1,0:T(8,128)(2,1)S(1)}, u32[]{:S(2)}, u32[]{:S(2)}) collective-permute-start(bf16[2304,128]{1,0:T(8,128)(2,1)S(1)} %slice.101), channel_id=1, source_target_pairs={{0,1},{1,0},{2,3},{3,2},{4,8},{5,9},{6,10},{7,11},{8,4},{9,5},{10,... | collective-permute-start | bytes 1769480 | tf_op jit(solution)/shard_map/ppermute | solution.py:399
  52.3 29.5 %collective-permute-start.9 = (bf16[2304,128]{1,0:T(8,128)(2,1)S(1)}, bf16[2304,128]{1,0:T(8,128)(2,1)S(1)}, u32[]{:S(2)}, u32[]{:S(2)}) collective-permute-start(bf16[2304,128]{1,0:T(8,128)(2,1)S(1)} %copy-done.29), channel_id=1, source_target_pairs={{0,1},{1,0},{2,3},{3,2},{4,8},{5,9},{6,10},{7,11},{8,4},{9,5},{10,... | collective-permute-start | bytes 1769480 | tf_op jit(solution)/shard_map/ppermute | solution.py:399
  58.3 33.5 %collective-permute-start.11 = (bf16[2304,128]{1,0:T(8,128)(2,1)S(1)}, bf16[2304,128]{1,0:T(8,128)(2,1)S(1)}, u32[]{:S(2)}, u32[]{:S(2)}) collective-permute-start(bf16[2304,128]{1,0:T(8,128)(2,1)S(1)} %broadcast_select_fusion), channel_id=1, source_target_pairs={{0,4},{4,0},{8,12},{12,8},{1,5},{5,1},{9,13},{13,9},{2,6},{6,2},{1... | collective-permute-start | bytes 1769480 | tf_op jit(solution)/shard_map/ppermute | solution.py:389
  71.3 21.3 %collective-permute-start.12 = (bf16[2304,128]{1,0:T(8,128)(2,1)S(1)}, bf16[2304,128]{1,0:T(8,128)(2,1)S(1)}, u32[]{:S(2)}, u32[]{:S(2)}) collective-permute-start(bf16[2304,128]{1,0:T(8,128)(2,1)S(1)} %get-tuple-element.67), channel_id=1, source_target_pairs={{0,1},{1,0},{2,3},{3,2},{4,8},{5,9},{6,10},{7,11},{8,4},{9,5},{10,... | collective-permute-start | bytes 1769480 | tf_op jit(solution)/shard_map/ppermute | solution.py:399
  80.1 27.8 %collective-permute-start.21 = (bf16[2304,128]{1,0:T(8,128)(2,1)}, bf16[2304,128]{1,0:T(8,128)(2,1)}, u32[]{:S(2)}, u32[]{:S(2)}) collective-permute-start(bf16[2304,128]{1,0:T(8,128)(2,1)} %broadcast_select_fusion.1), channel_id=1, source_target_pairs={{0,4},{4,0},{8,12},{12,8},{1,5},{5,1},{9,13},{13,9},{2,6},{6,2},{1... | collective-permute-start | bytes 1769480 | tf_op jit(solution)/shard_map/ppermute | solution.py:429
  93.5 11.4 %collective-permute-start.16 = (f32[256,512]{1,0:T(8,128)}, f32[256,512]{1,0:T(8,128)}, u32[]{:S(2)}, u32[]{:S(2)}) collective-permute-start(f32[256,512]{1,0:T(8,128)} %get-tuple-element.74), channel_id=1, source_target_pairs={{0,1},{1,0},{2,3},{3,2},{4,5},{5,4},{6,7},{7,6},{8,9},{9,8},{10,11... | collective-permute-start | bytes 1572872 | tf_op jit(solution)/shard_map/ppermute | solution.py:37
  106.1 8.6 %collective-permute-start.17 = (f32[128,512]{1,0:T(8,128)S(1)}, f32[128,512]{1,0:T(8,128)S(1)}, u32[]{:S(2)}, u32[]{:S(2)}) collective-permute-start(f32[128,512]{1,0:T(8,128)S(1)} %slice_select_fusion), channel_id=1, source_target_pairs={{0,2},{2,0},{1,3},{3,1},{4,6},{6,4},{5,7},{7,5},{8,10},{10,8},{9,1... | collective-permute-start | bytes 786440 | tf_op jit(solution)/shard_map/ppermute | solution.py:37
  111.9 15.8 %collective-permute-start.15 = (f32[32,2688]{1,0:T(8,128)S(1)}, f32[32,2688]{1,0:T(8,128)S(1)}, u32[]{:S(2)}, u32[]{:S(2)}) collective-permute-start(f32[32,2688]{1,0:T(8,128)S(1)} %broadcast_select_fusion.2), channel_id=1, source_target_pairs={{0,2},{2,0},{1,3},{3,1},{4,6},{6,4},{5,7},{7,5},{8,10},{10,8},{9,1... | collective-permute-start | bytes 1032200 | tf_op jit(solution)/shard_map/ppermute | solution.py:37
  114.8 10.8 %collective-permute-start.18 = (bf16[128,512]{1,0:T(8,128)(2,1)S(1)}, bf16[128,512]{1,0:T(8,128)(2,1)S(1)}, u32[]{:S(2)}, u32[]{:S(2)}) collective-permute-start(bf16[128,512]{1,0:T(8,128)(2,1)S(1)} %add_convert_fusion), channel_id=1, source_target_pairs={{0,2},{2,0},{1,3},{3,1},{4,6},{6,4},{5,7},{7,5},{8,10},{10,8},{9,1... | collective-permute-start | bytes 393224 | tf_op jit(solution)/shard_map/ppermute | solution.py:37
  117.1 10.5 %collective-permute-start.23 = (f32[32,896]{1,0:T(8,128)S(1)}, f32[32,896]{1,0:T(8,128)S(1)}, u32[]{:S(2)}, u32[]{:S(2)}) collective-permute-start(f32[32,896]{1,0:T(8,128)S(1)} %slice_select_fusion.1), channel_id=1, source_target_pairs={{0,2},{2,0},{1,3},{3,1},{4,6},{6,4},{5,7},{7,5},{8,10},{10,8},{9,1... | collective-permute-start | bytes 344072 | tf_op jit(solution)/shard_map/ppermute | solution.py:37
  125.7 8.8 %collective-permute-start.19 = (bf16[2,128,512]{2,1,0:T(8,128)(2,1)S(1)}, bf16[2,128,512]{2,1,0:T(8,128)(2,1)S(1)}, u32[]{:S(2)}, u32[]{:S(2)}) collective-permute-start(bf16[2,128,512]{2,1,0:T(8,128)(2,1)S(1)} %pad_maximum_fusion.4), channel_id=1, source_target_pairs={{0,1},{1,0},{2,3},{3,2},{4,5},{5,4},{6,7},{7,6},{8,9},{9,8},{10,11... | collective-permute-start | bytes 786440 | tf_op jit(solution)/shard_map/ppermute | solution.py:37
  127.8 10.9 %collective-permute-start.20 = (f32[32,1152]{1,0:T(8,128)S(1)}, f32[32,1152]{1,0:T(8,128)S(1)}, u32[]{:S(2)}, u32[]{:S(2)}) collective-permute-start(f32[32,1152]{1,0:T(8,128)S(1)} %slice.105), channel_id=1, source_target_pairs={{0,4},{4,0},{8,12},{12,8},{1,5},{5,1},{9,13},{13,9},{2,6},{6,2},{1... | collective-permute-start | bytes 442376 | tf_op jit(solution)/shard_map/ppermute | solution.py:515
  135.2 10.2 %collective-permute-start.28 = (bf16[4,32,512]{2,1,0:T(8,128)(2,1)S(1)}, bf16[4,32,512]{2,1,0:T(8,128)(2,1)S(1)}, u32[]{:S(2)}, u32[]{:S(2)}) collective-permute-start(bf16[4,32,512]{2,1,0:T(8,128)(2,1)S(1)} %convolution_convert_fusion.3), channel_id=1, source_target_pairs={{0,1},{1,0},{2,3},{3,2},{4,8},{5,9},{6,10},{7,11},{8,4},{9,5},{10,... | collective-permute-start | bytes 393224 | tf_op jit(solution)/shard_map/ppermute | solution.py:399
  141.6 9.1 %collective-permute-start.27 = (bf16[4,32,512]{2,1,0:T(8,128)(2,1)S(1)}, bf16[4,32,512]{2,1,0:T(8,128)(2,1)S(1)}, u32[]{:S(2)}, u32[]{:S(2)}) collective-permute-start(bf16[4,32,512]{2,1,0:T(8,128)(2,1)S(1)} %convolution_convert_fusion), channel_id=1, source_target_pairs={{0,12},{1,13},{2,14},{3,15},{4,5},{5,4},{6,7},{7,6},{8,9},{9,8},{1... | collective-permute-start | bytes 393224 | tf_op jit(solution)/shard_map/ppermute | solution.py:520
  144.4 9.1 %collective-permute-start.26 = (bf16[4,32,512]{2,1,0:T(8,128)(2,1)S(1)}, bf16[4,32,512]{2,1,0:T(8,128)(2,1)S(1)}, u32[]{:S(2)}, u32[]{:S(2)}) collective-permute-start(bf16[4,32,512]{2,1,0:T(8,128)(2,1)S(1)} %fusion.4), channel_id=1, source_target_pairs={{0,8},{8,0},{4,12},{12,4},{1,9},{9,1},{5,13},{13,5},{2,10},{10,2},... | collective-permute-start | bytes 393224 | tf_op jit(solution)/shard_map/ppermute | solution.py:521
  (42 other events, 329.0 us)

commit v9 on v8

--- a/solution.py
+++ b/solution.py
@@ -175,110 +175,146 @@
     )(flags, *operands)
 
 
-def partner_dots(flags, pieces, shards, wanted, depth, grads=None, tail=(), start=None):
+def both_dots(flags, grads, at_end, at_middle):
+    tok = grads.shape[0]
+    cols = at_end[0].shape[1]
+    step = grads.shape[1] // (3 * STEPS)
+
+    def third_at(first):
+        def index(i, flags_ref):
+            return (jnp.clip(i - first, 0, STEPS - 1) * (1 - flags_ref[0]), 0)
+
+        return index
+
+    operands = [grads, at_end[0]] + [array for pair in at_middle for array in pair]
+    specs = [
+        pl.BlockSpec((tok, step), lambda i, flags_ref: (0, STEPS + i)),
+        pl.BlockSpec((step, cols), lambda i, flags_ref: (at_end[1] + i * flags_ref[0], 0)),
+    ]
+    for first in (0, STEPS):
+        specs += [pl.BlockSpec((step, cols), third_at(first))] * 2
+
+    def kernel(flags_ref, grads_ref, end_ref, b1_ref, c1_ref, b2_ref, c2_ref, total_ref):
+        i = pl.program_id(0)
+
+        @pl.when(i == 0)
+        def begin():
+            total_ref[...] = jnp.zeros_like(total_ref)
+
+        @pl.when(flags_ref[0] == 1)
+        def one():
+            total_ref[:, :cols] += jnp.dot(
+                grads_ref[...], end_ref[...], preferred_element_type=jnp.float32
+            )
+
+        for first, b_ref, c_ref in ((0, b1_ref, c1_ref), (STEPS, b2_ref, c2_ref)):
+
+            @pl.when((flags_ref[0] == 0) & (i >= first) & (i < first + STEPS))
+            def two(b_ref=b_ref, c_ref=c_ref):
+                shards = jnp.concatenate([b_ref[...], c_ref[...]], axis=1)
+                total_ref[...] += jnp.dot(
+                    grads_ref[...], shards, preferred_element_type=jnp.float32
+                )
+
+    return pl.pallas_call(
+        kernel,
+        out_shape=jax.ShapeDtypeStruct((tok, 2 * cols), jnp.float32),
+        grid_spec=pltpu.PrefetchScalarGridSpec(
+            num_scalar_prefetch=1,
+            grid=(2 * STEPS,),
+            in_specs=specs,
+            out_specs=pl.BlockSpec((tok, 2 * cols), lambda i, flags_ref: (0, 0)),
+        ),
+        compiler_params=PARAMS,
+        cost_estimate=SHORT,
+    )(flags, *operands)
+
+
+def partner_dots(flags, pieces, shards, grads, column, shard, start):
+    tok = grads.shape[0]
     cols = shards[0][0].shape[1]
-    step = depth // STEPS
+    step = shard[2] // STEPS
     count = len(pieces)
-    tok = grads.shape[0] if tail else 0
-    ahead = tok if start is not None else 0
-    width = ahead + len(wanted) * TILE
-
-    def at(row, wanted_at=None):
-        def index(i, flags_ref):
-            if wanted_at is not None:
-                i = i * (flags_ref[0] if wanted_at else 1 - flags_ref[0])
-            return (row + i, 0)
-
-        return index
-
+    two = start.shape[1] == 2 * cols
+    width = tok + len(shards) * count * TILE
+
+    def at(row):
+        return lambda i, flags_ref: (row + i, 0)
+
+    whole = lambda i, flags_ref: (0, 0)
     operands, specs = [], []
-    for array, row in list(pieces) + list(shards):
+    for array, row in list(pieces) + list(shards) + [shard[:2]]:
         operands.append(array)
         specs.append(pl.BlockSpec((step, cols), at(row)))
-    whole = lambda i, flags_ref: (0, 0)
-    for choices, column, only in tail:
-        operands.append(grads)
-        specs.append(
-            pl.BlockSpec((tok, step), lambda i, flags_ref, column=column: (0, column + i))
+    operands += [grads, start]
+    specs.append(
+        pl.BlockSpec(
+            (tok, step),
+            lambda i, flags_ref: (0, column * (flags_ref[0] if two else 1) + i),
         )
-        for which, (array, row) in enumerate(choices):
-            operands.append(array)
-            specs.append(
-                pl.BlockSpec((step, cols), at(row, None if len(choices) == 1 else which == 0))
-            )
-    if start is not None:
-        operands.append(start)
-        specs.append(pl.BlockSpec((tok, cols), whole))
-    elif tail:
+    )
+    specs.append(pl.BlockSpec(start.shape, whole))
+    if two:
         operands.append(grads)
         specs.append(pl.BlockSpec((tok, step), lambda i, flags_ref: (0, 2 * STEPS + i)))
 
     def kernel(flags_ref, *refs):
         i = pl.program_id(0)
         piece_refs, shard_refs = refs[:count], refs[count : count + len(shards)]
-        tail_refs = refs[count + len(shards) : len(operands)]
+        end_ref, grads_ref, start_ref = refs[count + len(shards) : count + len(shards) + 3]
         keep_ref, give_ref, *rest = refs[len(operands) :]
-        if tail and start is None:
-            total_ref, copied_ref, sums_ref, turned_ref = rest
-            copied_ref[...] = tail_refs[-1][...]
-        elif tail:
-            sums_ref, turned_ref, total_ref, wide_ref = rest
+        if two:
+            second_ref, copied_ref, total_ref, sums_ref, turned_ref, wide_ref = rest
+            copied_ref[...] = refs[len(operands) - 1][...]
         else:
-            sums_ref, turned_ref = rest
+            total_ref, sums_ref, turned_ref, wide_ref = rest
 
         @pl.when(i == 0)
         def begin():
+            total_ref[...] = start_ref[...]
             sums_ref[...] = jnp.zeros_like(sums_ref)
-            if tail:
-                total_ref[...] = jnp.zeros_like(total_ref) if start is None else tail_refs[-1][...]
-
-        at = 0
-        for choices, column, only in tail:
-            grads_ref, here = tail_refs[at], tail_refs[at + 1 : at + 1 + len(choices)]
-            at += 1 + len(choices)
-
-            @pl.when((flags_ref[0] == 0) | (not only))
-            def add(grads_ref=grads_ref, here=here):
-                shard = here[0][...]
-                if len(here) == 2:
-                    shard = jnp.where(flags_ref[0] == 1, shard, here[1][...])
-                add_dot(total_ref, grads_ref, shard)
+
+        @pl.when(flags_ref[0] == 1)
+        def at_an_end_plane():
+            total_ref[:, total_ref.shape[1] - cols :] += jnp.dot(
+                grads_ref[...], end_ref[...], preferred_element_type=jnp.float32
+            )
 
         @pl.when(flags_ref[0] == 0)
         def at_a_middle_plane():
-            for t, piece_ref in enumerate(piece_refs):
-                tokens = jnp.concatenate(
-                    [piece_ref[q * TILE : (q + 1) * TILE, :] for q in range(step // TILE)], axis=1
+            side_by_side = jnp.concatenate([ref[...] for ref in shard_refs], axis=1)
+            tokens = jnp.concatenate(
+                [
+                    jnp.concatenate(
+                        [ref[q * TILE : (q + 1) * TILE, :] for q in range(step // TILE)], axis=1
+                    )
+                    for ref in piece_refs
+                ]
+            )
+            sums_ref[...] += jnp.dot(tokens, side_by_side, preferred_element_type=jnp.float32)
+            if two:
+                total_ref[...] += jnp.dot(
+                    grads_ref[...], side_by_side[:, cols:], preferred_element_type=jnp.float32
                 )
-                for block, (shard, piece) in enumerate(wanted):
-                    if piece == t:
-                        sums_ref[block] += jnp.dot(
-                            tokens, shard_refs[shard][...], preferred_element_type=jnp.float32
-                        )
 
         @pl.when(i == STEPS - 1)
         def finish():
-            if ahead:
-                wide_ref[...] = total_ref[...].T
-                split_rows(wide_ref, keep_ref, give_ref, flags_ref[1], pl.ds(0, tok))
-            for block in range(len(wanted)):
-                turned_ref[...] = sums_ref[block].T
-                columns = pl.ds(ahead + block * TILE, TILE)
+            wide_ref[...] = total_ref[:, :cols].T
+            split_rows(wide_ref, keep_ref, give_ref, flags_ref[1], pl.ds(0, tok))
+            for j in range(len(shards)):
+                turned_ref[...] = sums_ref[:, j * cols : (j + 1) * cols].T
+                columns = pl.ds(tok + j * count * TILE, count * TILE)
                 split_rows(turned_ref, keep_ref, give_ref, flags_ref[1], columns)
+            if two:
+                second_ref[...] = total_ref[:, cols:]
 
     out_shape = [jax.ShapeDtypeStruct((cols // 2, width), jnp.float32)] * 2
     out_specs = [pl.BlockSpec((cols // 2, width), whole)] * 2
-    scratch = [
-        pltpu.VMEM((len(wanted), TILE, cols), jnp.float32),
-        pltpu.VMEM((cols, TILE), jnp.float32),
-    ]
-    if tail and start is None:
+    if two:
         out_shape.append(jax.ShapeDtypeStruct((tok, cols), jnp.float32))
         out_specs.append(pl.BlockSpec((tok, cols), whole))
-        out_shape.append(jax.ShapeDtypeStruct((tok, depth), grads.dtype))
+        out_shape.append(jax.ShapeDtypeStruct((tok, STEPS * step), grads.dtype))
         out_specs.append(pl.BlockSpec((tok, step), lambda i, flags_ref: (0, i)))
-    elif tail:
-        scratch += [pltpu.VMEM((tok, cols), jnp.float32), pltpu.VMEM((cols, tok), jnp.float32)]
     return pl.pallas_call(
         kernel,
         out_shape=out_shape,
@@ -287,7 +323,12 @@
             grid=(STEPS,),
             in_specs=specs,
             out_specs=out_specs,
-            scratch_shapes=scratch,
+            scratch_shapes=[
+                pltpu.VMEM(start.shape, jnp.float32),
+                pltpu.VMEM((count * TILE, len(shards) * cols), jnp.float32),
+                pltpu.VMEM((cols, count * TILE), jnp.float32),
+                pltpu.VMEM((cols, tok), jnp.float32),
+            ],
         ),
         compiler_params=PARAMS,
         cost_estimate=SHORT,
@@ -442,48 +483,34 @@
             ([(s3, 0)], 2 * STEPS, 2 * STEPS, STEPS, True),
         ],
     )
-    part_b = feature_dots(
-        after(flags, *part_a, s45),
-        grads,
-        [
-            ([(s45, 0), (m2, 0)], STEPS, STEPS, STEPS, False),
-            ([(s45, STEPS), (m3, 0)], 2 * STEPS, 2 * STEPS, STEPS, False),
-            ([(m4, 0)], 0, 0, STEPS, True),
-        ],
-    )
-    shards = [(basis_out, 0), (m4, 0), (m7, 0)]
-    pieces = [(s45, 0), (s45, STEPS), (s6, 0), (s7, 0)]
-    blocks = [(shard, piece) for piece in (0, 1) for shard in (0, 1)]
-    part_first = partner_dots(after(flags, to_s7, *part_b), pieces[:2], shards[:2], blocks, depth)
-    parts = [part_own, part_a, part_b, part_first]
-    parts = [jnp.concatenate(part, axis=1) for part in zip(*parts)]
-    core_sums = core_sum(*after(parts, s6, m7))
-    *part_second, part_c, last_grads = partner_dots(
-        after(flags, core_sums),
-        pieces[:3],
-        shards,
-        [(2, 0), (2, 1), (0, 2), (1, 2), (2, 2)],
-        depth,
-        grads,
-        [([(s6, 0), (m5, 0)], STEPS, False), ([(m7, 0)], 0, True)],
-    )
-    rot_in = chip_sum(core_sum(*after(part_in, s6, m7)))
+    totals = both_dots(after(flags, to_s7, s45), grads, (s45, 0), ((m2, m5), (m3, m6)))
+    core_in = core_sum(*after(part_in, s6, m4, m7, totals))
+    rot_in = chip_sum(core_in)
     rot_in = gather_rows(rot_in.astype(jnp.bfloat16))
     rot_in = rot_in.reshape(tiles_here, TILE, 4 * cols)
-    sums = chip_sum(jnp.concatenate([core_sums, core_sum(*part_second)], axis=1))
-    sum_own, sum_a, sum_b = [sums[:, i * tok_rows : (i + 1) * tok_rows] for i in range(3)]
+    parts = [jnp.concatenate(part, axis=1) for part in zip(part_own, part_a)]
+    core_a = core_sum(*after(parts, s6, m4, m7, totals))
+    sums = chip_sum(core_a)
+    sum_own, sum_a = sums[:, :tok_rows], sums[:, tok_rows:]
+
+    shards = [(basis_out, 0), (m4, 0), (m7, 0)]
+    *part_b, part_c, last_grads = partner_dots(
+        after(flags, totals, core_in, core_a),
+        [(s45, 0), (s45, STEPS), (s6, 0)],
+        shards,
+        grads,
+        STEPS,
+        (s6, 0, depth),
+        totals,
+    )
+    core_b = core_sum(*part_b)
+    sums = chip_sum(core_b)
+    sum_b, sums = sums[:, :tok_rows], sums[:, tok_rows:]
     part_last = partner_dots(
-        after(flags, part_c),
-        pieces[3:],
-        shards,
-        [(0, 0), (1, 0), (2, 0)],
-        depth,
-        last_grads,
-        [([(s7, 0), (m6, 0)], 0, False)],
-        part_c,
+        after(flags, part_c), [(s7, 0)], shards, last_grads, 0, (s7, 0, depth), part_c
     )
     sum_last = chip_sum(core_sum(*part_last))
-    sum_c = sum_last[:, :tok_rows]
+    sum_c, sum_last = sum_last[:, :tok_rows], sum_last[:, tok_rows:]
 
     rowmask, ignored = tile_layout(pair_tiles, last_rows, plane * tiles_here, tiles_here, TILE)
     keep = rowmask.reshape(1, tok_rows).astype(jnp.bfloat16)
@@ -505,23 +532,29 @@
         ])
         return jnp.sum(jnp.where(onehot[:, :, None], scores[:, None, :], 0.0), axis=0)
 
-    def columns(x, *which):
-        return jnp.concatenate([x[:, i * TILE : (i + 1) * TILE] for i in which], axis=1)
-
     prods_own = tile_prods(sum_own)
     prods_middle = tile_prods(sum_b)
     from_middle = middle(prods_middle)
-    last = lax.ppermute(after(sum_last[:, tok_rows:], prods_own, prods_middle), "cand", SIDE)
-    back = lax.ppermute(sums[:, 3 * tok_rows :], "cand", SIDE)
-    both = jnp.where(end, jnp.concatenate([back, last], axis=1), 0.0)
-    prods_a = tile_prods(sum_a + columns(both, 0, 2, 6, 9))
-    prods_b = tile_prods(sum_b + columns(both, 1, 3, 7, 10))
-    prods_c = tile_prods(sum_c + columns(both, 4, 5, 8, 11))
+    last = lax.ppermute(after(sum_last, prods_own, prods_middle), "cand", SIDE)
+    back = lax.ppermute(sums, "cand", SIDE)
+    back = jnp.where(end, back, 0.0).reshape(slim, 3, tok_rows - TILE)
+    last = jnp.where(end, last, 0.0).reshape(slim, 3, TILE)
+
+    def with_partner(whole, at):
+        return whole + jnp.concatenate([back[:, at], last[:, at]], axis=1)
+
+    prods_a = tile_prods(with_partner(sum_a, 0))
+    prods_b = tile_prods(with_partner(sum_b, 1))
+    prods_c = tile_prods(with_partner(sum_c, 2))
     from_far = lax.ppermute(prods_c, ALL, far)
     from_two = lax.ppermute(pick(prods_b, prods_c), "cand", TWO)
     from_side = lax.ppermute(prods_a, "cand", SIDE)
-    total = pair_scores((prods_own, plane), (from_side, plane ^ 1))
-    total = total + pair_scores((from_two, plane ^ 2), (pick(from_far, from_middle), plane ^ 3))
+    total = pair_scores(
+        (prods_own, plane),
+        (from_side, plane ^ 1),
+        (from_two, plane ^ 2),
+        (pick(from_far, from_middle), plane ^ 3),
+    )
     return final_sum(total)
 
 

time: 168 us -> 173 us (1.030)
  waiting for transfers between devices: 48.8 us -> 57.1 us
  starting transfers between devices: 42.9 us -> 34.8 us
  other arithmetic: 11.9 us -> 15.9 us
  local copies, waits for them, and re-layouts: 20.1 us -> 23.6 us
  matrix products: 6.09 us -> 3.8 us
    pallas_call x3 -> x2, Pallas kernels: 13.3 us -> 8.38 us  [feature_dots(): pl.pallas_call(kernel, out_shape=out_shape, grid_spec=pltpu.PrefetchScala...]
    ppermute x2, starting transfers between devices: 6.83 us -> 2.16 us  [the longest x1 1.15 us: line_plan(): last = lax.ppermute(after(sum_last, prods_own, prods_middle), 'cand', SIDE)]
    ppermute x1, waiting for transfers between devices: 7.76 us -> 12.3 us  [line_plan(): s45 = lax.ppermute(after(to_s45, s3), 'cand', SIDE)]
    pallas_call x0 -> x1, Pallas kernels: none -> 4.36 us  [both_dots(): pl.pallas_call(kernel, out_shape=jax.ShapeDtypeStruct((tok, 2 * cols), jn...]
    ppermute x2, starting transfers between devices: 15 us -> 10.8 us  [side(): return lax.ppermute(pick(at_end, at_middle), 'cand', SIDE)]
    ppermute x9 -> x10, waiting for transfers between devices: 14.2 us -> 10.8 us  [swap(): return lax.ppermute(x, axis_name, [(0, 1), (1, 0)])]
    unnamed x72 -> x79, local copies, waits for them, and re-layouts: 16.1 us -> 19.3 us
    ppermute x1, starting transfers between devices: 3.15 us -> 0.01 us  [line_plan(): s12 = lax.ppermute(rows, 'cand', SIDE)]
  transfers between devices with their start and end apart: 29 -> 30, of which waited for: 13 -> 11; matrix products, arithmetic and copies ran while one was open for 11% -> 12% of each run, Pallas kernels for 16% -> 15%
where the time goes in v9:
time: 173 us; the launch traced here: 172 us
  waiting for transfers between devices  57.1 us (33%)
  starting transfers between devices  34.8 us (20%)
  Pallas kernels  25.2 us (15%)
  local copies, waits for them, and re-layouts  23.6 us (14%)
  other arithmetic  15.9 us (9%)
  blocking collectives  10.8 us (6%)
  matrix products  3.8 us (2%)
    unnamed x79, local copies, waits for them, and re-layouts  19.3 us
    ppermute x2, waiting for transfers between devices, side(): return lax.ppermute(pick(at_end, at_middle), 'cand', SIDE)  15.3 us
    ppermute x1, waiting for transfers between devices, line_plan(): s45 = lax.ppermute(after(to_s45, s3), 'cand', SIDE)  12.3 us
    ppermute x10, waiting for transfers between devices, swap(): return lax.ppermute(x, axis_name, [(0, 1), (1, 0)])  10.8 us
    ppermute x2, starting transfers between devices, side(): return lax.ppermute(pick(at_end, at_middle), 'cand', SIDE)  10.8 us
    all_to_all x1, blocking collectives, final_sum(): return jnp.sum(lax.all_to_all(blocks, ALL, 0, 0, tiled=True), axis=0)  10.8 us
    pallas_call x2, Pallas kernels, feature_dots(): pl.pallas_call(kernel, out_shape=out_shape, grid_spec=pltpu.PrefetchScala...  8.38 us
    ppermute x10, starting transfers between devices, swap(): return lax.ppermute(x, axis_name, [(0, 1), (1, 0)])  6.93 us
  transfers between devices with their start and end apart: 30, of which 11 were waited for; matrix products, arithmetic and copies ran while one was open for 12% of the time, Pallas kernels for 15%

profile of v9, /device:TPU:0, one launch (start us, length us, event | category | flops | bytes accessed | tf_op | source)
XLA Modules:
  0.0 171.9 jit_solution(16331726156286260422)
XLA Ops:
  0.5 4.1 %collective-permute-start = (bf16[1280,128]{1,0:T(8,128)(2,1)}, bf16[1280,128]{1,0:T(8,128)(2,1)}, u32[]{:S(2)}, u32[]{:S(2)}) collective-permute-start(bf16[1280,128]{1,0:T(8,128)(2,1)} %refs_0_.3), channel_id=1, source_target_pairs={{0,4},{4,0},{8,12},{12,8},{1,5},{5,1},{9,13},{13,9},{2,6},{6,2},{1... | collective-permute-start | bytes 983048 | tf_op jit(solution)/shard_map/ppermute | solution.py:448
  11.3 3.0 %copy-done = bf16[512,6912]{1,0:T(8,128)(2,1)S(1)} copy-done((bf16[512,6912]{1,0:T(8,128)(2,1)S(1)}, bf16[512,6912]{1,0:T(8,128)(2,1)}, u32[]{:S(2)}) %copy-start) | copy-done | bytes 7077912
  18.8 3.0 %copy-done.1 = bf16[512,6912]{1,0:T(8,128)(2,1)S(1)} copy-done((bf16[512,6912]{1,0:T(8,128)(2,1)S(1)}, bf16[512,6912]{1,0:T(8,128)(2,1)}, u32[]{:S(2)}) %copy-start.1) | copy-done | bytes 7077912
  21.8 4.6 %shard_map.82 = (f32[64,512]{1,0:T(8,128)S(1)}, f32[64,512]{1,0:T(8,128)S(1)}) custom-call(s32[6]{0:T(128)S(1)} %stack.49.flags_ref, bf16[512,6912]{1,0:T(8,128)(2,1)S(1)} %copy-done.1, bf16[6912,128]{1,0:T(8,128)(2,1)S(1)} %copy-done.3), custom_call_target="tpu_custom_call" | custom-call | flops 1 | bytes 1 | tf_op jit(solution)/shard_map/pallas_call | solution.py:163
  27.2 6.8 %collective-permute-start.3 = (bf16[2560,128]{1,0:T(8,128)(2,1)S(1)}, bf16[2560,128]{1,0:T(8,128)(2,1)S(1)}, u32[]{:S(2)}, u32[]{:S(2)}) collective-permute-start(bf16[2560,128]{1,0:T(8,128)(2,1)S(1)} %maximum_select_fusion.1), channel_id=1, source_target_pairs={{0,4},{4,0},{8,12},{12,8},{1,5},{5,1},{9,13},{13,9},{2,6},{6,2},{1... | collective-permute-start | bytes 1966088 | tf_op jit(solution)/shard_map/ppermute | solution.py:430
  34.0 4.7 %collective-permute-done.4.refs_0_ = bf16[4608,128]{1,0:T(8,128)(2,1)S(1)} collective-permute-done((bf16[4608,128]{1,0:T(8,128)(2,1)}, bf16[4608,128]{1,0:T(8,128)(2,1)S(1)}, u32[]{:S(2)}, u32[]{:S(2)}) %collective-permute-start.4) | collective-permute-done | bytes 1179680 | tf_op jit(solution)/shard_map/ppermute | solution.py:450
  40.8 10.8 %collective-permute-done.3.refs_2_.refs_4_.refs_1_ = bf16[2560,128]{1,0:T(8,128)(2,1)S(1)} collective-permute-done((bf16[2560,128]{1,0:T(8,128)(2,1)S(1)}, bf16[2560,128]{1,0:T(8,128)(2,1)S(1)}, u32[]{:S(2)}, u32[]{:S(2)}) %collective-permute-start.3) | collective-permute-done | bytes 655392 | tf_op jit(solution)/shard_map/ppermute | solution.py:430
  54.3 4.6 %shard_map.83 = (f32[256,512]{1,0:T(8,128)S(1)}, f32[256,512]{1,0:T(8,128)}) custom-call(s32[6]{0:T(128)S(1)} %stack.49.flags_ref, bf16[512,1280]{1,0:T(8,128)(2,1)S(1)} %copy-done.12, bf16[1280,128]{1,0:T(8,128)(2,1)S(1)} %copy-done.20, bf16[1280,128]{1,0:T(8,128)(2,1)} %collective-permute-done.refs_1_, ...), custom_call_target="tpu_custom_call" | custom-call | flops 1 | bytes 1 | tf_op jit(solution)/shard_map/pallas_call | solution.py:401
  59.0 4.0 %collective-permute-start.6 = (bf16[2304,128]{1,0:T(8,128)(2,1)S(1)}, bf16[2304,128]{1,0:T(8,128)(2,1)S(1)}, u32[]{:S(2)}, u32[]{:S(2)}) collective-permute-start(bf16[2304,128]{1,0:T(8,128)(2,1)S(1)} %broadcast_select_fusion.1), channel_id=1, source_target_pairs={{0,4},{4,0},{8,12},{12,8},{1,5},{5,1},{9,13},{13,9},{2,6},{6,2},{1... | collective-permute-start | bytes 1769480 | tf_op jit(solution)/shard_map/ppermute | solution.py:430
  63.0 3.8 %shard_map.84 = (f32[64,512]{1,0:T(8,128)S(1)}, f32[64,512]{1,0:T(8,128)S(1)}) custom-call(s32[6]{0:T(128)S(1)} %stack.49.flags_ref, bf16[512,6912]{1,0:T(8,128)(2,1)S(1)} %bitcast.72, bf16[4608,128]{1,0:T(8,128)(2,1)S(1)} %copy-done.5, bf16[2560,128]{1,0:T(8,128)(2,1)S(1)} %collective-permute-done.3.refs_2_.refs_4_.refs_1_), custom_call_target="tpu_custom_call" | custom-call | flops 1 | bytes 1 | tf_op jit(solution)/shard_map/pallas_call | solution.py:163
  68.2 12.3 %collective-permute-done.12.end_ref.refs_0_.refs_1_ = bf16[4608,128]{1,0:T(8,128)(2,1)S(1)} collective-permute-done((bf16[4608,128]{1,0:T(8,128)(2,1)S(1)}, bf16[4608,128]{1,0:T(8,128)(2,1)S(1)}, u32[]{:S(2)}, u32[]{:S(2)}) %collective-permute-start.12) | collective-permute-done | bytes 1179680 | tf_op jit(solution)/shard_map/ppermute | solution.py:465
  81.4 4.4 %shard_map.86.refs_8_ = f32[512,256]{1,0:T(8,128)S(1)} custom-call(s32[6]{0:T(128)S(1)} %stack.49.flags_ref, bf16[512,6912]{1,0:T(8,128)(2,1)S(1)} %bitcast.72, bf16[4608,128]{1,0:T(8,128)(2,1)S(1)} %collective-permute-done.12.end_ref.refs_0_.refs_1_, bf16[2304,128]{1,0:T(8,128)(2,1)} %collective-permute-done.10.b1_ref, ...), custom_call_target="tpu_custom_call" | custom-call | flops 1 | bytes 1 | tf_op jit(solution)/shard_map/pallas_call | solution.py:219
  86.6 4.5 %collective-permute-done.6.refs_2_.refs_6_ = bf16[2304,128]{1,0:T(8,128)(2,1)S(1)} collective-permute-done((bf16[2304,128]{1,0:T(8,128)(2,1)S(1)}, bf16[2304,128]{1,0:T(8,128)(2,1)S(1)}, u32[]{:S(2)}, u32[]{:S(2)}) %collective-permute-start.6) | collective-permute-done | bytes 589856 | tf_op jit(solution)/shard_map/ppermute | solution.py:430
  95.1 3.7 %collective-permute-start.22 = (bf16[2304,128]{1,0:T(8,128)(2,1)}, bf16[2304,128]{1,0:T(8,128)(2,1)}, u32[]{:S(2)}, u32[]{:S(2)}) collective-permute-start(bf16[2304,128]{1,0:T(8,128)(2,1)} %broadcast_select_fusion), channel_id=1, source_target_pairs={{0,4},{4,0},{8,12},{12,8},{1,5},{5,1},{9,13},{13,9},{2,6},{6,2},{1... | collective-permute-start | bytes 1769480 | tf_op jit(solution)/shard_map/ppermute | solution.py:470
  107.1 3.0 %copy-done.2 = bf16[512,6912]{1,0:T(8,128)(2,1)S(1)} copy-done((bf16[512,6912]{1,0:T(8,128)(2,1)S(1)}, bf16[512,6912]{1,0:T(8,128)(2,1)}, u32[]{:S(2)}) %copy-start.2) | copy-done | bytes 7077912
  113.3 2.8 %shard_map.87 = (f32[64,1664]{1,0:T(8,128)S(1)}, f32[64,1664]{1,0:T(8,128)S(1)}, f32[512,128]{1,0:T(8,128)S(1)}, bf16[512,2304]{1,0:T(8,128)(2,1)S(1)}) custom-call(s32[6]{0:T(128)S(1)} %stack.49.flags_ref, bf16[4608,128]{1,0:T(8,128)(2,1)S(1)} %collective-permute-done.12.end_ref.refs_0_.refs_1_, ...), custom_call_target="tpu_custom_call" | custom-call | flops 1 | bytes 1 | tf_op jit(solution)/shard_map/pallas_call | solution.py:318
  116.2 3.8 %shard_map.88 = (f32[64,896]{1,0:T(8,128)S(1)}, f32[64,896]{1,0:T(8,128)S(1)}) custom-call(s32[6]{0:T(128)S(1)} %stack.49.flags_ref, bf16[2304,128]{1,0:T(8,128)(2,1)} %collective-permute-done.22.refs_0_.refs_4_, bf16[6912,128]{1,0:T(8,128)(2,1)S(1)} %copy-done.3, bf16[2304,128]{1,0:T(8,128)(2,1)S(1)} %copy-done.7, bf16[2304,128]{1,0:T(8,128)(2,1)S(1)} %copy-done.9, ...), custom_call_target="tpu_custom_call" | custom-call | flops 1 | bytes 1 | tf_op jit(solution)/shard_map/pallas_call | solution.py:318
  123.8 4.2 %collective-permute-done.17 = bf16[128,512]{1,0:T(8,128)(2,1)S(1)} collective-permute-done((bf16[128,512]{1,0:T(8,128)(2,1)S(1)}, bf16[128,512]{1,0:T(8,128)(2,1)S(1)}, u32[]{:S(2)}, u32[]{:S(2)}) %collective-permute-start.17) | collective-permute-done | bytes 131104 | tf_op jit(solution)/shard_map/ppermute | solution.py:37
  129.8 6.1 %collective-permute-done.20 = f32[32,1664]{1,0:T(8,128)S(1)} collective-permute-done((f32[32,1664]{1,0:T(8,128)S(1)}, f32[32,1664]{1,0:T(8,128)S(1)}, u32[]{:S(2)}, u32[]{:S(2)}) %collective-permute-start.20) | collective-permute-done | bytes 213024 | tf_op jit(solution)/shard_map/ppermute | solution.py:37
  145.3 2.5 %collective-permute-start.28 = (bf16[4,32,512]{2,1,0:T(8,128)(2,1)S(1)}, bf16[4,32,512]{2,1,0:T(8,128)(2,1)S(1)}, u32[]{:S(2)}, u32[]{:S(2)}) collective-permute-start(bf16[4,32,512]{2,1,0:T(8,128)(2,1)S(1)} %convolution_convert_fusion), channel_id=1, source_target_pairs={{0,12},{1,13},{2,14},{3,15},{4,5},{5,4},{6,7},{7,6},{8,9},{9,8},{1... | collective-permute-start | bytes 393224 | tf_op jit(solution)/shard_map/ppermute | solution.py:549
  148.1 6.1 %collective-permute-done.28 = bf16[4,32,512]{2,1,0:T(8,128)(2,1)S(1)} collective-permute-done((bf16[4,32,512]{2,1,0:T(8,128)(2,1)S(1)}, bf16[4,32,512]{2,1,0:T(8,128)(2,1)S(1)}, u32[]{:S(2)}, u32[]{:S(2)}) %collective-permute-start.28) | collective-permute-done | bytes 131104 | tf_op jit(solution)/shard_map/ppermute | solution.py:549
  154.3 3.1 %collective-permute-done.27 = bf16[4,32,512]{2,1,0:T(8,128)(2,1)S(1)} collective-permute-done((bf16[4,32,512]{2,1,0:T(8,128)(2,1)S(1)}, bf16[4,32,512]{2,1,0:T(8,128)(2,1)S(1)}, u32[]{:S(2)}, u32[]{:S(2)}) %collective-permute-start.27) | collective-permute-done | bytes 131104 | tf_op jit(solution)/shard_map/ppermute | solution.py:550
  157.5 2.8 %fusion.3 = f32[16,64]{1,0:T(8,128)S(1)} fusion(bf16[64,32,512]{2,1,0:T(8,128)(2,1)S(1)} %copy-done.26, bf16[16,32,512]{2,1,0:T(8,128)(2,1)S(1)} %pad_maximum_fusion.1), kind=kOutput, calls=%fused_computation.10 | convolution fusion | flops 33554432 | bytes 2625536 | tf_op jit(solution)/shard_map/tea,jea->tj/dot_general | solution.py:528
  160.5 10.8 %all_to_all.5 = f32[16,2,16]{2,1,0:T(2,128)S(1)} all-to-all(f32[16,2,16]{2,1,0:T(2,128)S(1)} %copy.72), channel_id=1, replica_groups=mesh['groups'=2,'cand'=4,'eig'=2,'rep'=2] {'cand','eig','rep'}, dimensions={0} | all-to-all | bytes 4096 | tf_op jit(solution)/shard_map/all_to_all | solution.py:565
  (190 shorter events, 51.4 us)
Async XLA Ops:
  0.0 18.5 %collective-permute-start.1 = (bf16[1280,128]{1,0:T(8,128)(2,1)}, bf16[1280,128]{1,0:T(8,128)(2,1)S(1)}, u32[]{:S(2)}, u32[]{:S(2)}) collective-permute-start(bf16[1280,128]{1,0:T(8,128)(2,1)} %refs_0_.3), channel_id=1, source_target_pairs={{0,1},{1,0},{2,3},{3,2},{4,8},{5,9},{6,10},{7,11},{8,4},{9,5},{10,... | collective-permute-start | bytes 983048 | tf_op jit(solution)/shard_map/ppermute | solution.py:440
  0.5 18.0 %collective-permute-start = (bf16[1280,128]{1,0:T(8,128)(2,1)}, bf16[1280,128]{1,0:T(8,128)(2,1)}, u32[]{:S(2)}, u32[]{:S(2)}) collective-permute-start(bf16[1280,128]{1,0:T(8,128)(2,1)} %refs_0_.3), channel_id=1, source_target_pairs={{0,4},{4,0},{8,12},{12,8},{1,5},{5,1},{9,13},{13,9},{2,6},{6,2},{1... | collective-permute-start | bytes 983048 | tf_op jit(solution)/shard_map/ppermute | solution.py:448
  7.0 31.7 %collective-permute-start.4 = (bf16[4608,128]{1,0:T(8,128)(2,1)}, bf16[4608,128]{1,0:T(8,128)(2,1)S(1)}, u32[]{:S(2)}, u32[]{:S(2)}) collective-permute-start(bf16[4608,128]{1,0:T(8,128)(2,1)} %constant_dynamic-slice_fusion), channel_id=1, source_target_pairs={{0,4},{4,0},{8,12},{12,8},{1,5},{5,1},{9,13},{13,9},{2,6},{6,2},{1... | collective-permute-start | bytes 3538952 | tf_op jit(solution)/shard_map/ppermute | solution.py:450
  8.3 30.6 %collective-permute-start.10 = (bf16[2304,128]{1,0:T(8,128)(2,1)}, bf16[2304,128]{1,0:T(8,128)(2,1)}, u32[]{:S(2)}, u32[]{:S(2)}) collective-permute-start(bf16[2304,128]{1,0:T(8,128)(2,1)} %get-tuple-element.78), channel_id=1, source_target_pairs={{0,1},{1,0},{2,3},{3,2},{4,8},{5,9},{6,10},{7,11},{8,4},{9,5},{10,... | collective-permute-start | bytes 1769480 | tf_op jit(solution)/shard_map/ppermute | solution.py:440
  18.5 8.5 %collective-permute-start.2 = (bf16[1280,128]{1,0:T(8,128)(2,1)}, bf16[1280,128]{1,0:T(8,128)(2,1)S(1)}, u32[]{:S(2)}, u32[]{:S(2)}) collective-permute-start(bf16[1280,128]{1,0:T(8,128)(2,1)} %collective-permute-done.refs_1_), channel_id=1, source_target_pairs={{0,1},{1,0},{2,3},{3,2},{4,8},{5,9},{6,10},{7,11},{8,4},{9,5},{10,... | collective-permute-start | bytes 983048 | tf_op jit(solution)/shard_map/ppermute | solution.py:440
  26.5 12.5 %collective-permute-start.11 = (bf16[2304,128]{1,0:T(8,128)(2,1)S(1)}, bf16[2304,128]{1,0:T(8,128)(2,1)S(1)}, u32[]{:S(2)}, u32[]{:S(2)}) collective-permute-start(bf16[2304,128]{1,0:T(8,128)(2,1)S(1)} %copy-done.24), channel_id=1, source_target_pairs={{0,1},{1,0},{2,3},{3,2},{4,8},{5,9},{6,10},{7,11},{8,4},{9,5},{10,... | collective-permute-start | bytes 1769480 | tf_op jit(solution)/shard_map/ppermute | solution.py:440
  27.2 24.4 %collective-permute-start.3 = (bf16[2560,128]{1,0:T(8,128)(2,1)S(1)}, bf16[2560,128]{1,0:T(8,128)(2,1)S(1)}, u32[]{:S(2)}, u32[]{:S(2)}) collective-permute-start(bf16[2560,128]{1,0:T(8,128)(2,1)S(1)} %maximum_select_fusion.1), channel_id=1, source_target_pairs={{0,4},{4,0},{8,12},{12,8},{1,5},{5,1},{9,13},{13,9},{2,6},{6,2},{1... | collective-permute-start | bytes 1966088 | tf_op jit(solution)/shard_map/ppermute | solution.py:430
  38.8 15.4 %collective-permute-start.5 = (bf16[2304,128]{1,0:T(8,128)(2,1)S(1)}, bf16[2304,128]{1,0:T(8,128)(2,1)S(1)}, u32[]{:S(2)}, u32[]{:S(2)}) collective-permute-start(bf16[2304,128]{1,0:T(8,128)(2,1)S(1)} %get-tuple-element.80), channel_id=1, source_target_pairs={{0,1},{1,0},{2,3},{3,2},{4,8},{5,9},{6,10},{7,11},{8,4},{9,5},{10,... | collective-permute-start | bytes 1769480 | tf_op jit(solution)/shard_map/ppermute | solution.py:440
  51.6 28.9 %collective-permute-start.12 = (bf16[4608,128]{1,0:T(8,128)(2,1)S(1)}, bf16[4608,128]{1,0:T(8,128)(2,1)S(1)}, u32[]{:S(2)}, u32[]{:S(2)}) collective-permute-start(bf16[4608,128]{1,0:T(8,128)(2,1)S(1)} %maximum_select_fusion), channel_id=1, source_target_pairs={{0,4},{4,0},{8,12},{12,8},{1,5},{5,1},{9,13},{13,9},{2,6},{6,2},{1... | collective-permute-start | bytes 3538952 | tf_op jit(solution)/shard_map/ppermute | solution.py:465
  54.2 13.5 %collective-permute-start.8 = (bf16[2304,128]{1,0:T(8,128)(2,1)S(1)}, bf16[2304,128]{1,0:T(8,128)(2,1)S(1)}, u32[]{:S(2)}, u32[]{:S(2)}) collective-permute-start(bf16[2304,128]{1,0:T(8,128)(2,1)S(1)} %slice.80), channel_id=1, source_target_pairs={{0,1},{1,0},{2,3},{3,2},{4,8},{5,9},{6,10},{7,11},{8,4},{9,5},{10,... | collective-permute-start | bytes 1769480 | tf_op jit(solution)/shard_map/ppermute | solution.py:440
  59.0 32.1 %collective-permute-start.6 = (bf16[2304,128]{1,0:T(8,128)(2,1)S(1)}, bf16[2304,128]{1,0:T(8,128)(2,1)S(1)}, u32[]{:S(2)}, u32[]{:S(2)}) collective-permute-start(bf16[2304,128]{1,0:T(8,128)(2,1)S(1)} %broadcast_select_fusion.1), channel_id=1, source_target_pairs={{0,4},{4,0},{8,12},{12,8},{1,5},{5,1},{9,13},{13,9},{2,6},{6,2},{1... | collective-permute-start | bytes 1769480 | tf_op jit(solution)/shard_map/ppermute | solution.py:430
  63.0 28.1 %collective-permute-start.7 = (bf16[2304,128]{1,0:T(8,128)(2,1)S(1)}, bf16[2304,128]{1,0:T(8,128)(2,1)S(1)}, u32[]{:S(2)}, u32[]{:S(2)}) collective-permute-start(bf16[2304,128]{1,0:T(8,128)(2,1)S(1)} %copy-done.27), channel_id=1, source_target_pairs={{0,1},{1,0},{2,3},{3,2},{4,8},{5,9},{6,10},{7,11},{8,4},{9,5},{10,... | collective-permute-start | bytes 1769480 | tf_op jit(solution)/shard_map/ppermute | solution.py:440
  67.7 24.2 %collective-permute-start.9 = (bf16[2304,128]{1,0:T(8,128)(2,1)S(1)}, bf16[2304,128]{1,0:T(8,128)(2,1)S(1)}, u32[]{:S(2)}, u32[]{:S(2)}) collective-permute-start(bf16[2304,128]{1,0:T(8,128)(2,1)S(1)} %get-tuple-element.51), channel_id=1, source_target_pairs={{0,1},{1,0},{2,3},{3,2},{4,8},{5,9},{6,10},{7,11},{8,4},{9,5},{10,... | collective-permute-start | bytes 1769480 | tf_op jit(solution)/shard_map/ppermute | solution.py:440
  92.7 9.3 %collective-permute-start.15 = (f32[256,512]{1,0:T(8,128)}, f32[256,512]{1,0:T(8,128)}, u32[]{:S(2)}, u32[]{:S(2)}) collective-permute-start(f32[256,512]{1,0:T(8,128)} %get-tuple-element.61), channel_id=1, source_target_pairs={{0,1},{1,0},{2,3},{3,2},{4,5},{5,4},{6,7},{7,6},{8,9},{9,8},{10,11... | collective-permute-start | bytes 1572872 | tf_op jit(solution)/shard_map/ppermute | solution.py:37
  95.1 21.1 %collective-permute-start.22 = (bf16[2304,128]{1,0:T(8,128)(2,1)}, bf16[2304,128]{1,0:T(8,128)(2,1)}, u32[]{:S(2)}, u32[]{:S(2)}) collective-permute-start(bf16[2304,128]{1,0:T(8,128)(2,1)} %broadcast_select_fusion), channel_id=1, source_target_pairs={{0,4},{4,0},{8,12},{12,8},{1,5},{5,1},{9,13},{13,9},{2,6},{6,2},{1... | collective-permute-start | bytes 1769480 | tf_op jit(solution)/shard_map/ppermute | solution.py:470
  104.9 15.7 %collective-permute-start.16 = (f32[128,512]{1,0:T(8,128)}, f32[128,512]{1,0:T(8,128)}, u32[]{:S(2)}, u32[]{:S(2)}) collective-permute-start(f32[128,512]{1,0:T(8,128)} %slice_select_fusion), channel_id=1, source_target_pairs={{0,2},{2,0},{1,3},{3,1},{4,6},{6,4},{5,7},{7,5},{8,10},{10,8},{9,1... | collective-permute-start | bytes 786440 | tf_op jit(solution)/shard_map/ppermute | solution.py:37
  116.1 12.0 %collective-permute-start.19 = (f32[64,1664]{1,0:T(8,128)S(1)}, f32[64,1664]{1,0:T(8,128)S(1)}, u32[]{:S(2)}, u32[]{:S(2)}) collective-permute-start(f32[64,1664]{1,0:T(8,128)S(1)} %get-tuple-element.64), channel_id=1, source_target_pairs={{0,1},{1,0},{2,3},{3,2},{4,5},{5,4},{6,7},{7,6},{8,9},{9,8},{10,11... | collective-permute-start | bytes 1277960 | tf_op jit(solution)/shard_map/ppermute | solution.py:37
  123.2 6.6 %collective-permute-start.24 = (f32[32,896]{1,0:T(8,128)S(1)}, f32[32,896]{1,0:T(8,128)S(1)}, u32[]{:S(2)}, u32[]{:S(2)}) collective-permute-start(f32[32,896]{1,0:T(8,128)S(1)} %slice_select_fusion.3), channel_id=1, source_target_pairs={{0,2},{2,0},{1,3},{3,1},{4,6},{6,4},{5,7},{7,5},{8,10},{10,8},{9,1... | collective-permute-start | bytes 344072 | tf_op jit(solution)/shard_map/ppermute | solution.py:37
  128.1 8.0 %collective-permute-start.18 = (bf16[2,128,512]{2,1,0:T(8,128)(2,1)S(1)}, bf16[2,128,512]{2,1,0:T(8,128)(2,1)S(1)}, u32[]{:S(2)}, u32[]{:S(2)}) collective-permute-start(bf16[2,128,512]{2,1,0:T(8,128)(2,1)S(1)} %pad_maximum_fusion.4), channel_id=1, source_target_pairs={{0,1},{1,0},{2,3},{3,2},{4,5},{5,4},{6,7},{7,6},{8,9},{9,8},{10,11... | collective-permute-start | bytes 786440 | tf_op jit(solution)/shard_map/ppermute | solution.py:37
  128.3 7.7 %collective-permute-start.20 = (f32[32,1664]{1,0:T(8,128)S(1)}, f32[32,1664]{1,0:T(8,128)S(1)}, u32[]{:S(2)}, u32[]{:S(2)}) collective-permute-start(f32[32,1664]{1,0:T(8,128)S(1)} %slice_select_fusion.1), channel_id=1, source_target_pairs={{0,2},{2,0},{1,3},{3,1},{4,6},{6,4},{5,7},{7,5},{8,10},{10,8},{9,1... | collective-permute-start | bytes 638984 | tf_op jit(solution)/shard_map/ppermute | solution.py:37
  138.8 9.3 %collective-permute-start.29 = (bf16[4,32,512]{2,1,0:T(8,128)(2,1)S(1)}, bf16[4,32,512]{2,1,0:T(8,128)(2,1)S(1)}, u32[]{:S(2)}, u32[]{:S(2)}) collective-permute-start(bf16[4,32,512]{2,1,0:T(8,128)(2,1)S(1)} %convolution_convert_fusion.3), channel_id=1, source_target_pairs={{0,1},{1,0},{2,3},{3,2},{4,8},{5,9},{6,10},{7,11},{8,4},{9,5},{10,... | collective-permute-start | bytes 393224 | tf_op jit(solution)/shard_map/ppermute | solution.py:440
  144.1 10.2 %collective-permute-start.26 = (bf16[4,32,512]{2,1,0:T(8,128)(2,1)S(1)}, bf16[4,32,512]{2,1,0:T(8,128)(2,1)S(1)}, u32[]{:S(2)}, u32[]{:S(2)}) collective-permute-start(bf16[4,32,512]{2,1,0:T(8,128)(2,1)S(1)} %convolution_convert_fusion.2), channel_id=1, source_target_pairs={{0,4},{4,0},{8,12},{12,8},{1,5},{5,1},{9,13},{13,9},{2,6},{6,2},{1... | collective-permute-start | bytes 393224 | tf_op jit(solution)/shard_map/ppermute | solution.py:551
  145.3 9.0 %collective-permute-start.28 = (bf16[4,32,512]{2,1,0:T(8,128)(2,1)S(1)}, bf16[4,32,512]{2,1,0:T(8,128)(2,1)S(1)}, u32[]{:S(2)}, u32[]{:S(2)}) collective-permute-start(bf16[4,32,512]{2,1,0:T(8,128)(2,1)S(1)} %convolution_convert_fusion), channel_id=1, source_target_pairs={{0,12},{1,13},{2,14},{3,15},{4,5},{5,4},{6,7},{7,6},{8,9},{9,8},{1... | collective-permute-start | bytes 393224 | tf_op jit(solution)/shard_map/ppermute | solution.py:549
  148.1 9.4 %collective-permute-start.27 = (bf16[4,32,512]{2,1,0:T(8,128)(2,1)S(1)}, bf16[4,32,512]{2,1,0:T(8,128)(2,1)S(1)}, u32[]{:S(2)}, u32[]{:S(2)}) collective-permute-start(bf16[4,32,512]{2,1,0:T(8,128)(2,1)S(1)} %fusion.2), channel_id=1, source_target_pairs={{0,8},{8,0},{4,12},{12,4},{1,9},{9,1},{5,13},{13,5},{2,10},{10,2},... | collective-permute-start | bytes 393224 | tf_op jit(solution)/shard_map/ppermute | solution.py:550
  (45 other events, 301.4 us)

commit v10 on v9

--- a/solution.py
+++ b/solution.py
@@ -43,13 +43,14 @@
     return jnp.where(first, low, high), jnp.where(first, high, low)
 
 
-def core_sum(keep, give):
-    return keep + swap(give, "rep")
-
-
-def chip_sum(part):
-    keep, give = halves(part, "eig")
-    return keep + swap(give, "eig")
+def chip_parts(keep, received):
+    keep, their_keep = halves(keep, "eig")
+    received, their_received = halves(received, "eig")
+    return keep + received, (their_keep + their_received).astype(jnp.bfloat16)
+
+
+def chip_sum(keep, give):
+    return keep + swap(give, "eig").astype(jnp.float32)
 
 
 def gather_rows(x):
@@ -483,19 +484,14 @@
             ([(s3, 0)], 2 * STEPS, 2 * STEPS, STEPS, True),
         ],
     )
-    totals = both_dots(after(flags, to_s7, s45), grads, (s45, 0), ((m2, m5), (m3, m6)))
-    core_in = core_sum(*after(part_in, s6, m4, m7, totals))
-    rot_in = chip_sum(core_in)
-    rot_in = gather_rows(rot_in.astype(jnp.bfloat16))
-    rot_in = rot_in.reshape(tiles_here, TILE, 4 * cols)
+    totals = both_dots(after(flags, to_s7, s45, *part_a), grads, (s45, 0), ((m2, m5), (m3, m6)))
     parts = [jnp.concatenate(part, axis=1) for part in zip(part_own, part_a)]
-    core_a = core_sum(*after(parts, s6, m4, m7, totals))
-    sums = chip_sum(core_a)
-    sum_own, sum_a = sums[:, :tok_rows], sums[:, tok_rows:]
+    keep_a, give_a = after(parts, s6, m4, totals)
+    core_a = swap(give_a, "rep")
 
     shards = [(basis_out, 0), (m4, 0), (m7, 0)]
     *part_b, part_c, last_grads = partner_dots(
-        after(flags, totals, core_in, core_a),
+        after(flags, totals, core_a),
         [(s45, 0), (s45, STEPS), (s6, 0)],
         shards,
         grads,
@@ -503,14 +499,30 @@
         (s6, 0, depth),
         totals,
     )
-    core_b = core_sum(*part_b)
-    sums = chip_sum(core_b)
-    sum_b, sums = sums[:, :tok_rows], sums[:, tok_rows:]
-    part_last = partner_dots(
-        after(flags, part_c), [(s7, 0)], shards, last_grads, 0, (s7, 0, depth), part_c
-    )
-    sum_last = chip_sum(core_sum(*part_last))
-    sum_c, sum_last = sum_last[:, :tok_rows], sum_last[:, tok_rows:]
+    keep_in, give_in = after(part_in, part_c)
+    core_in = swap(give_in, "rep")
+    rot_in = gather_rows(chip_sum(*chip_parts(keep_in, core_in)).astype(jnp.bfloat16))
+    rot_in = rot_in.reshape(tiles_here, TILE, 4 * cols)
+    keep_b, give_b = part_b
+    keep_b, give_b = chip_parts(
+        jnp.concatenate([keep_a, keep_b], axis=1),
+        jnp.concatenate([core_a, swap(give_b, "rep")], axis=1),
+    )
+    sums = chip_sum(keep_b, give_b)
+    sum_own, sum_a, sum_b = [sums[:, i * tok_rows : (i + 1) * tok_rows] for i in range(3)]
+    sums = sums[:, 3 * tok_rows :].astype(jnp.bfloat16)
+    keep_last, give_last = partner_dots(
+        after(flags, part_c),
+        [(s7, 0)],
+        shards,
+        last_grads,
+        0,
+        (s7, 0, depth),
+        part_c,
+    )
+    keep_last, give_last = after((keep_last, give_last), give_b)
+    sum_last = chip_sum(*chip_parts(keep_last, swap(give_last, "rep")))
+    sum_c, sum_last = sum_last[:, :tok_rows], sum_last[:, tok_rows:].astype(jnp.bfloat16)
 
     rowmask, ignored = tile_layout(pair_tiles, last_rows, plane * tiles_here, tiles_here, TILE)
     keep = rowmask.reshape(1, tok_rows).astype(jnp.bfloat16)
@@ -537,11 +549,11 @@
     from_middle = middle(prods_middle)
     last = lax.ppermute(after(sum_last, prods_own, prods_middle), "cand", SIDE)
     back = lax.ppermute(sums, "cand", SIDE)
-    back = jnp.where(end, back, 0.0).reshape(slim, 3, tok_rows - TILE)
-    last = jnp.where(end, last, 0.0).reshape(slim, 3, TILE)
+    back = jnp.where(end, back, jnp.zeros_like(back)).reshape(slim, 3, tok_rows - TILE)
+    last = jnp.where(end, last, jnp.zeros_like(last)).reshape(slim, 3, TILE)
 
     def with_partner(whole, at):
-        return whole + jnp.concatenate([back[:, at], last[:, at]], axis=1)
+        return whole + jnp.concatenate([back[:, at], last[:, at]], axis=1).astype(jnp.float32)
 
     prods_a = tile_prods(with_partner(sum_a, 0))
     prods_b = tile_prods(with_partner(sum_b, 1))

time: 173 us -> 161 us (0.931)
  other arithmetic: 15.9 us -> 11.2 us
  waiting for transfers between devices: 57.1 us -> 54 us
  starting transfers between devices: 34.8 us -> 32.8 us
  local copies, waits for them, and re-layouts: 23.6 us -> 21.8 us
    add x7 -> x1, other arithmetic: 3.52 us -> 0.03 us  [chip_sum(): return keep + swap(give, 'eig').astype(jnp.float32)]
    unnamed x79 -> x70, local copies, waits for them, and re-layouts: 19.3 us -> 16.6 us
    ppermute x1, waiting for transfers between devices: 2.29 us -> 0.01 us  [line_plan(): back = lax.ppermute(sums, 'cand', SIDE)]
    ppermute x1, starting transfers between devices: 3.66 us -> 1.71 us  [line_plan(): s7 = lax.ppermute(to_s7, 'cand', SIDE)]
    ppermute x10 -> x9, starting transfers between devices: 6.93 us -> 5.32 us  [swap(): return lax.ppermute(x, axis_name, [(0, 1), (1, 0)])]
    ppermute x10 -> x9, waiting for transfers between devices: 10.8 us -> 10.1 us  [swap(): return lax.ppermute(x, axis_name, [(0, 1), (1, 0)])]
  transfers between devices with their start and end apart: 30 -> 29, of which waited for: 11 -> 12; matrix products, arithmetic and copies ran while one was open for 12% -> 11% of each run, Pallas kernels for 15% -> 16%
where the time goes in v10:
time: 161 us; the launch traced here: 160 us
  waiting for transfers between devices  54 us (34%)
  starting transfers between devices  32.8 us (20%)
  Pallas kernels  25.7 us (16%)
  local copies, waits for them, and re-layouts  21.8 us (14%)
  other arithmetic  11.2 us (7%)
  blocking collectives  10.4 us (6%)
  matrix products  3.8 us (2%)
    unnamed x70, local copies, waits for them, and re-layouts  16.6 us
    ppermute x2, waiting for transfers between devices, side(): return lax.ppermute(pick(at_end, at_middle), 'cand', SIDE)  15.1 us
    ppermute x1, waiting for transfers between devices, line_plan(): s45 = lax.ppermute(after(to_s45, s3), 'cand', SIDE)  11.3 us
    all_to_all x1, blocking collectives, final_sum(): return jnp.sum(lax.all_to_all(blocks, ALL, 0, 0, tiled=True), axis=0)  10.4 us
    ppermute x9, waiting for transfers between devices, swap(): return lax.ppermute(x, axis_name, [(0, 1), (1, 0)])  10.1 us
    ppermute x2, starting transfers between devices, side(): return lax.ppermute(pick(at_end, at_middle), 'cand', SIDE)  9.82 us
    pallas_call x2, Pallas kernels, feature_dots(): pl.pallas_call(kernel, out_shape=out_shape, grid_spec=pltpu.PrefetchScala...  8.38 us
    pallas_call x2, Pallas kernels, partner_dots(): pl.pallas_call(kernel, out_shape=out_shape, grid_spec=pltpu.PrefetchScala...  7.81 us
  transfers between devices with their start and end apart: 29, of which 12 were waited for; matrix products, arithmetic and copies ran while one was open for 11% of the time, Pallas kernels for 16%

profile of v10, /device:TPU:0, one launch (start us, length us, event | category | flops | bytes accessed | tf_op | source)
XLA Modules:
  0.0 160.4 jit_solution(11641487213354384692)
XLA Ops:
  0.5 4.1 %collective-permute-start = (bf16[1280,128]{1,0:T(8,128)(2,1)}, bf16[1280,128]{1,0:T(8,128)(2,1)}, u32[]{:S(2)}, u32[]{:S(2)}) collective-permute-start(bf16[1280,128]{1,0:T(8,128)(2,1)} %refs_0_.3), channel_id=1, source_target_pairs={{0,4},{4,0},{8,12},{12,8},{1,5},{5,1},{9,13},{13,9},{2,6},{6,2},{1... | collective-permute-start | bytes 983048 | tf_op jit(solution)/shard_map/ppermute | solution.py:449
  4.6 2.4 %constant_dynamic-slice_fusion = bf16[4608,128]{1,0:T(8,128)(2,1)} fusion(bf16[6912,128]{1,0:T(8,128)(2,1)} %refs_1_.1, s32[]{:T(128)S(6)} %select_n.172), kind=kLoop, calls=%fused_computation.91 | loop fusion | bytes 2359300 | tf_op jit(solution)/shard_map/dynamic_slice | solution.py:448
  8.3 3.6 %divide_convert_fusion = bf16[64,32,512]{2,1,0:T(8,128)(2,1)} fusion(bf16[64,32,512]{2,1,0:T(8,128)(2,1)} %param.13, f32[32,512]{1,0:T(8,128)S(1)} %broadcast_add_fusion), kind=kLoop, calls=%fused_computation | loop fusion | flops 3145728 | bytes 4259840 | tf_op jit(solution)/shard_map/convert_element_type | solution.py:459
  11.9 3.0 %copy-done = bf16[512,6912]{1,0:T(8,128)(2,1)S(1)} copy-done((bf16[512,6912]{1,0:T(8,128)(2,1)S(1)}, bf16[512,6912]{1,0:T(8,128)(2,1)}, u32[]{:S(2)}) %copy-start) | copy-done | bytes 7077912
  20.8 3.0 %copy-done.1 = bf16[512,6912]{1,0:T(8,128)(2,1)S(1)} copy-done((bf16[512,6912]{1,0:T(8,128)(2,1)S(1)}, bf16[512,6912]{1,0:T(8,128)(2,1)}, u32[]{:S(2)}) %copy-start.1) | copy-done | bytes 7077912
  23.8 4.6 %shard_map.82 = (f32[64,512]{1,0:T(8,128)S(1)}, f32[64,512]{1,0:T(8,128)S(1)}) custom-call(s32[6]{0:T(128)S(1)} %stack.49.flags_ref, bf16[512,6912]{1,0:T(8,128)(2,1)S(1)} %copy-done.1, bf16[6912,128]{1,0:T(8,128)(2,1)S(1)} %copy-done.3), custom_call_target="tpu_custom_call" | custom-call | flops 1 | bytes 1 | tf_op jit(solution)/shard_map/pallas_call | solution.py:164
  28.8 4.0 %collective-permute-start.3 = (bf16[2560,128]{1,0:T(8,128)(2,1)S(1)}, bf16[2560,128]{1,0:T(8,128)(2,1)S(1)}, u32[]{:S(2)}, u32[]{:S(2)}) collective-permute-start(bf16[2560,128]{1,0:T(8,128)(2,1)S(1)} %maximum_select_fusion.1), channel_id=1, source_target_pairs={{0,4},{4,0},{8,12},{12,8},{1,5},{5,1},{9,13},{13,9},{2,6},{6,2},{1... | collective-permute-start | bytes 1966088 | tf_op jit(solution)/shard_map/ppermute | solution.py:431
  32.8 5.9 %collective-permute-done.4.refs_0_ = bf16[4608,128]{1,0:T(8,128)(2,1)S(1)} collective-permute-done((bf16[4608,128]{1,0:T(8,128)(2,1)}, bf16[4608,128]{1,0:T(8,128)(2,1)S(1)}, u32[]{:S(2)}, u32[]{:S(2)}) %collective-permute-start.4) | collective-permute-done | bytes 1179680 | tf_op jit(solution)/shard_map/ppermute | solution.py:451
  41.3 10.3 %collective-permute-done.3.refs_2_.refs_4_.refs_1_ = bf16[2560,128]{1,0:T(8,128)(2,1)S(1)} collective-permute-done((bf16[2560,128]{1,0:T(8,128)(2,1)S(1)}, bf16[2560,128]{1,0:T(8,128)(2,1)S(1)}, u32[]{:S(2)}, u32[]{:S(2)}) %collective-permute-start.3) | collective-permute-done | bytes 655392 | tf_op jit(solution)/shard_map/ppermute | solution.py:431
  54.1 3.9 %shard_map.83 = (f32[256,512]{1,0:T(8,128)S(1)}, f32[256,512]{1,0:T(8,128)S(1)}) custom-call(s32[6]{0:T(128)S(1)} %stack.49.flags_ref, bf16[512,1280]{1,0:T(8,128)(2,1)S(1)} %copy-done.12, bf16[1280,128]{1,0:T(8,128)(2,1)S(1)} %copy-done.19, bf16[1280,128]{1,0:T(8,128)(2,1)} %collective-permute-done.refs_1_, ...), custom_call_target="tpu_custom_call" | custom-call | flops 1 | bytes 1 | tf_op jit(solution)/shard_map/pallas_call | solution.py:402
  58.1 5.8 %collective-permute-start.6 = (bf16[2304,128]{1,0:T(8,128)(2,1)S(1)}, bf16[2304,128]{1,0:T(8,128)(2,1)S(1)}, u32[]{:S(2)}, u32[]{:S(2)}) collective-permute-start(bf16[2304,128]{1,0:T(8,128)(2,1)S(1)} %broadcast_select_fusion.1), channel_id=1, source_target_pairs={{0,4},{4,0},{8,12},{12,8},{1,5},{5,1},{9,13},{13,9},{2,6},{6,2},{1... | collective-permute-start | bytes 1769480 | tf_op jit(solution)/shard_map/ppermute | solution.py:431
  64.0 3.8 %shard_map.84 = (f32[64,512]{1,0:T(8,128)S(1)}, f32[64,512]{1,0:T(8,128)S(1)}) custom-call(s32[6]{0:T(128)S(1)} %stack.49.flags_ref, bf16[512,6912]{1,0:T(8,128)(2,1)S(1)} %bitcast.72, bf16[4608,128]{1,0:T(8,128)(2,1)S(1)} %copy-done.5, bf16[2560,128]{1,0:T(8,128)(2,1)S(1)} %collective-permute-done.3.refs_2_.refs_4_.refs_1_), custom_call_target="tpu_custom_call" | custom-call | flops 1 | bytes 1 | tf_op jit(solution)/shard_map/pallas_call | solution.py:164
  69.2 11.3 %collective-permute-done.10.end_ref.refs_0_.refs_1_ = bf16[4608,128]{1,0:T(8,128)(2,1)S(1)} collective-permute-done((bf16[4608,128]{1,0:T(8,128)(2,1)S(1)}, bf16[4608,128]{1,0:T(8,128)(2,1)S(1)}, u32[]{:S(2)}, u32[]{:S(2)}) %collective-permute-start.10) | collective-permute-done | bytes 1179680 | tf_op jit(solution)/shard_map/ppermute | solution.py:466
  83.1 4.4 %shard_map.86.refs_8_ = f32[512,256]{1,0:T(8,128)S(1)} custom-call(s32[6]{0:T(128)S(1)} %stack.49.flags_ref, bf16[512,6912]{1,0:T(8,128)(2,1)S(1)} %bitcast.72, bf16[4608,128]{1,0:T(8,128)(2,1)S(1)} %collective-permute-done.10.end_ref.refs_0_.refs_1_, bf16[2304,128]{1,0:T(8,128)(2,1)} %collective-permute-done.8.b1_ref, ...), custom_call_target="tpu_custom_call" | custom-call | flops 1 | bytes 1 | tf_op jit(solution)/shard_map/pallas_call | solution.py:220
  88.3 4.8 %collective-permute-done.6.refs_2_.refs_6_ = bf16[2304,128]{1,0:T(8,128)(2,1)S(1)} collective-permute-done((bf16[2304,128]{1,0:T(8,128)(2,1)S(1)}, bf16[2304,128]{1,0:T(8,128)(2,1)S(1)}, u32[]{:S(2)}, u32[]{:S(2)}) %collective-permute-start.6) | collective-permute-done | bytes 589856 | tf_op jit(solution)/shard_map/ppermute | solution.py:431
  95.9 3.0 %copy-done.2 = bf16[512,6912]{1,0:T(8,128)(2,1)S(1)} copy-done((bf16[512,6912]{1,0:T(8,128)(2,1)S(1)}, bf16[512,6912]{1,0:T(8,128)(2,1)}, u32[]{:S(2)}) %copy-start.2) | copy-done | bytes 7077912
  101.0 3.8 %shard_map.87 = (f32[64,1664]{1,0:T(8,128)S(1)}, f32[64,1664]{1,0:T(8,128)S(1)}, f32[512,128]{1,0:T(8,128)S(1)}, bf16[512,2304]{1,0:T(8,128)(2,1)S(1)}) custom-call(s32[6]{0:T(128)S(1)} %stack.49.flags_ref, bf16[4608,128]{1,0:T(8,128)(2,1)S(1)} %collective-permute-done.10.end_ref.refs_0_.refs_1_, ...), custom_call_target="tpu_custom_call" | custom-call | flops 1 | bytes 1 | tf_op jit(solution)/shard_map/pallas_call | solution.py:319
  106.5 4.0 %shard_map.88 = (f32[64,896]{1,0:T(8,128)S(1)}, f32[64,896]{1,0:T(8,128)S(1)}) custom-call(s32[6]{0:T(128)S(1)} %stack.49.flags_ref, bf16[2304,128]{1,0:T(8,128)(2,1)} %collective-permute-done.21.refs_0_.refs_4_, bf16[6912,128]{1,0:T(8,128)(2,1)S(1)} %copy-done.3, bf16[2304,128]{1,0:T(8,128)(2,1)S(1)} %copy-done.7, ...), custom_call_target="tpu_custom_call" | custom-call | flops 1 | bytes 1 | tf_op jit(solution)/shard_map/pallas_call | solution.py:319
  113.2 4.7 %collective-permute-done.15 = bf16[32,2688]{1,0:T(8,128)(2,1)S(1)} collective-permute-done((bf16[32,2688]{1,0:T(8,128)(2,1)S(1)}, bf16[32,2688]{1,0:T(8,128)(2,1)S(1)}, u32[]{:S(2)}, u32[]{:S(2)}) %collective-permute-start.15) | collective-permute-done | bytes 172064 | tf_op jit(solution)/shard_map/ppermute | solution.py:37
  122.7 2.8 %collective-permute-done.18 = bf16[128,512]{1,0:T(8,128)(2,1)S(1)} collective-permute-done((bf16[128,512]{1,0:T(8,128)(2,1)S(1)}, bf16[128,512]{1,0:T(8,128)(2,1)S(1)}, u32[]{:S(2)}, u32[]{:S(2)}) %collective-permute-start.18) | collective-permute-done | bytes 131104 | tf_op jit(solution)/shard_map/ppermute | solution.py:37
  136.4 6.5 %collective-permute-done.27 = bf16[4,32,512]{2,1,0:T(8,128)(2,1)S(1)} collective-permute-done((bf16[4,32,512]{2,1,0:T(8,128)(2,1)S(1)}, bf16[4,32,512]{2,1,0:T(8,128)(2,1)S(1)}, u32[]{:S(2)}, u32[]{:S(2)}) %collective-permute-start.27) | collective-permute-done | bytes 131104 | tf_op jit(solution)/shard_map/ppermute | solution.py:561
  143.0 3.4 %collective-permute-done.26 = bf16[4,32,512]{2,1,0:T(8,128)(2,1)S(1)} collective-permute-done((bf16[4,32,512]{2,1,0:T(8,128)(2,1)S(1)}, bf16[4,32,512]{2,1,0:T(8,128)(2,1)S(1)}, u32[]{:S(2)}, u32[]{:S(2)}) %collective-permute-start.26) | collective-permute-done | bytes 131104 | tf_op jit(solution)/shard_map/ppermute | solution.py:562
  146.5 2.8 %fusion.3 = f32[16,64]{1,0:T(8,128)S(1)} fusion(bf16[64,32,512]{2,1,0:T(8,128)(2,1)S(1)} %copy-done.23, bf16[16,32,512]{2,1,0:T(8,128)(2,1)S(1)} %pad_maximum_fusion.1), kind=kOutput, calls=%fused_computation.10 | convolution fusion | flops 33554432 | bytes 2625536 | tf_op jit(solution)/shard_map/tea,jea->tj/dot_general | solution.py:540
  149.5 10.4 %all_to_all.5 = f32[16,2,16]{2,1,0:T(2,128)S(1)} all-to-all(f32[16,2,16]{2,1,0:T(2,128)S(1)} %copy.72), channel_id=1, replica_groups=mesh['groups'=2,'cand'=4,'eig'=2,'rep'=2] {'cand','eig','rep'}, dimensions={0} | all-to-all | bytes 4096 | tf_op jit(solution)/shard_map/all_to_all | solution.py:577
  (175 shorter events, 43.2 us)
Async XLA Ops:
  0.0 19.3 %collective-permute-start.1 = (bf16[1280,128]{1,0:T(8,128)(2,1)}, bf16[1280,128]{1,0:T(8,128)(2,1)S(1)}, u32[]{:S(2)}, u32[]{:S(2)}) collective-permute-start(bf16[1280,128]{1,0:T(8,128)(2,1)} %refs_0_.3), channel_id=1, source_target_pairs={{0,1},{1,0},{2,3},{3,2},{4,8},{5,9},{6,10},{7,11},{8,4},{9,5},{10,... | collective-permute-start | bytes 983048 | tf_op jit(solution)/shard_map/ppermute | solution.py:441
  0.5 18.8 %collective-permute-start = (bf16[1280,128]{1,0:T(8,128)(2,1)}, bf16[1280,128]{1,0:T(8,128)(2,1)}, u32[]{:S(2)}, u32[]{:S(2)}) collective-permute-start(bf16[1280,128]{1,0:T(8,128)(2,1)} %refs_0_.3), channel_id=1, source_target_pairs={{0,4},{4,0},{8,12},{12,8},{1,5},{5,1},{9,13},{13,9},{2,6},{6,2},{1... | collective-permute-start | bytes 983048 | tf_op jit(solution)/shard_map/ppermute | solution.py:449
  7.0 31.7 %collective-permute-start.4 = (bf16[4608,128]{1,0:T(8,128)(2,1)}, bf16[4608,128]{1,0:T(8,128)(2,1)S(1)}, u32[]{:S(2)}, u32[]{:S(2)}) collective-permute-start(bf16[4608,128]{1,0:T(8,128)(2,1)} %constant_dynamic-slice_fusion), channel_id=1, source_target_pairs={{0,4},{4,0},{8,12},{12,8},{1,5},{5,1},{9,13},{13,9},{2,6},{6,2},{1... | collective-permute-start | bytes 3538952 | tf_op jit(solution)/shard_map/ppermute | solution.py:451
  8.3 31.5 %collective-permute-start.8 = (bf16[2304,128]{1,0:T(8,128)(2,1)}, bf16[2304,128]{1,0:T(8,128)(2,1)}, u32[]{:S(2)}, u32[]{:S(2)}) collective-permute-start(bf16[2304,128]{1,0:T(8,128)(2,1)} %get-tuple-element.84), channel_id=1, source_target_pairs={{0,1},{1,0},{2,3},{3,2},{4,8},{5,9},{6,10},{7,11},{8,4},{9,5},{10,... | collective-permute-start | bytes 1769480 | tf_op jit(solution)/shard_map/ppermute | solution.py:441
  19.3 9.2 %collective-permute-start.2 = (bf16[1280,128]{1,0:T(8,128)(2,1)}, bf16[1280,128]{1,0:T(8,128)(2,1)S(1)}, u32[]{:S(2)}, u32[]{:S(2)}) collective-permute-start(bf16[1280,128]{1,0:T(8,128)(2,1)} %collective-permute-done.refs_1_), channel_id=1, source_target_pairs={{0,1},{1,0},{2,3},{3,2},{4,8},{5,9},{6,10},{7,11},{8,4},{9,5},{10,... | collective-permute-start | bytes 983048 | tf_op jit(solution)/shard_map/ppermute | solution.py:441
  28.5 11.3 %collective-permute-start.9 = (bf16[2304,128]{1,0:T(8,128)(2,1)S(1)}, bf16[2304,128]{1,0:T(8,128)(2,1)S(1)}, u32[]{:S(2)}, u32[]{:S(2)}) collective-permute-start(bf16[2304,128]{1,0:T(8,128)(2,1)S(1)} %copy-done.22), channel_id=1, source_target_pairs={{0,1},{1,0},{2,3},{3,2},{4,8},{5,9},{6,10},{7,11},{8,4},{9,5},{10,... | collective-permute-start | bytes 1769480 | tf_op jit(solution)/shard_map/ppermute | solution.py:441
  28.8 22.8 %collective-permute-start.3 = (bf16[2560,128]{1,0:T(8,128)(2,1)S(1)}, bf16[2560,128]{1,0:T(8,128)(2,1)S(1)}, u32[]{:S(2)}, u32[]{:S(2)}) collective-permute-start(bf16[2560,128]{1,0:T(8,128)(2,1)S(1)} %maximum_select_fusion.1), channel_id=1, source_target_pairs={{0,4},{4,0},{8,12},{12,8},{1,5},{5,1},{9,13},{13,9},{2,6},{6,2},{1... | collective-permute-start | bytes 1966088 | tf_op jit(solution)/shard_map/ppermute | solution.py:431
  39.7 14.4 %collective-permute-start.5 = (bf16[2304,128]{1,0:T(8,128)(2,1)S(1)}, bf16[2304,128]{1,0:T(8,128)(2,1)S(1)}, u32[]{:S(2)}, u32[]{:S(2)}) collective-permute-start(bf16[2304,128]{1,0:T(8,128)(2,1)S(1)} %get-tuple-element.86), channel_id=1, source_target_pairs={{0,1},{1,0},{2,3},{3,2},{4,8},{5,9},{6,10},{7,11},{8,4},{9,5},{10,... | collective-permute-start | bytes 1769480 | tf_op jit(solution)/shard_map/ppermute | solution.py:441
  51.6 28.9 %collective-permute-start.10 = (bf16[4608,128]{1,0:T(8,128)(2,1)S(1)}, bf16[4608,128]{1,0:T(8,128)(2,1)S(1)}, u32[]{:S(2)}, u32[]{:S(2)}) collective-permute-start(bf16[4608,128]{1,0:T(8,128)(2,1)S(1)} %maximum_select_fusion), channel_id=1, source_target_pairs={{0,4},{4,0},{8,12},{12,8},{1,5},{5,1},{9,13},{13,9},{2,6},{6,2},{1... | collective-permute-start | bytes 3538952 | tf_op jit(solution)/shard_map/ppermute | solution.py:466
  54.0 14.7 %collective-permute-start.11 = (bf16[2304,128]{1,0:T(8,128)(2,1)S(1)}, bf16[2304,128]{1,0:T(8,128)(2,1)S(1)}, u32[]{:S(2)}, u32[]{:S(2)}) collective-permute-start(bf16[2304,128]{1,0:T(8,128)(2,1)S(1)} %slice.81), channel_id=1, source_target_pairs={{0,1},{1,0},{2,3},{3,2},{4,8},{5,9},{6,10},{7,11},{8,4},{9,5},{10,... | collective-permute-start | bytes 1769480 | tf_op jit(solution)/shard_map/ppermute | solution.py:441
  58.1 35.0 %collective-permute-start.6 = (bf16[2304,128]{1,0:T(8,128)(2,1)S(1)}, bf16[2304,128]{1,0:T(8,128)(2,1)S(1)}, u32[]{:S(2)}, u32[]{:S(2)}) collective-permute-start(bf16[2304,128]{1,0:T(8,128)(2,1)S(1)} %broadcast_select_fusion.1), channel_id=1, source_target_pairs={{0,4},{4,0},{8,12},{12,8},{1,5},{5,1},{9,13},{13,9},{2,6},{6,2},{1... | collective-permute-start | bytes 1769480 | tf_op jit(solution)/shard_map/ppermute | solution.py:431
  63.9 29.2 %collective-permute-start.7 = (bf16[2304,128]{1,0:T(8,128)(2,1)S(1)}, bf16[2304,128]{1,0:T(8,128)(2,1)S(1)}, u32[]{:S(2)}, u32[]{:S(2)}) collective-permute-start(bf16[2304,128]{1,0:T(8,128)(2,1)S(1)} %copy-done.25), channel_id=1, source_target_pairs={{0,1},{1,0},{2,3},{3,2},{4,8},{5,9},{6,10},{7,11},{8,4},{9,5},{10,... | collective-permute-start | bytes 1769480 | tf_op jit(solution)/shard_map/ppermute | solution.py:441
  68.7 27.2 %collective-permute-start.13 = (bf16[2304,128]{1,0:T(8,128)(2,1)}, bf16[2304,128]{1,0:T(8,128)(2,1)}, u32[]{:S(2)}, u32[]{:S(2)}) collective-permute-start(bf16[2304,128]{1,0:T(8,128)(2,1)} %get-tuple-element.62), channel_id=1, source_target_pairs={{0,1},{1,0},{2,3},{3,2},{4,8},{5,9},{6,10},{7,11},{8,4},{9,5},{10,... | collective-permute-start | bytes 1769480 | tf_op jit(solution)/shard_map/ppermute | solution.py:441
  81.4 25.1 %collective-permute-start.21 = (bf16[2304,128]{1,0:T(8,128)(2,1)}, bf16[2304,128]{1,0:T(8,128)(2,1)}, u32[]{:S(2)}, u32[]{:S(2)}) collective-permute-start(bf16[2304,128]{1,0:T(8,128)(2,1)} %broadcast_select_fusion), channel_id=1, source_target_pairs={{0,4},{4,0},{8,12},{12,8},{1,5},{5,1},{9,13},{13,9},{2,6},{6,2},{1... | collective-permute-start | bytes 1769480 | tf_op jit(solution)/shard_map/ppermute | solution.py:471
  104.8 5.7 %collective-permute-start.14 = (f32[64,1664]{1,0:T(8,128)S(1)}, f32[64,1664]{1,0:T(8,128)S(1)}, u32[]{:S(2)}, u32[]{:S(2)}) collective-permute-start(f32[64,1664]{1,0:T(8,128)S(1)} %get-tuple-element.64), channel_id=1, source_target_pairs={{0,1},{1,0},{2,3},{3,2},{4,5},{5,4},{6,7},{7,6},{8,9},{9,8},{10,11... | collective-permute-start | bytes 1277960 | tf_op jit(solution)/shard_map/ppermute | solution.py:37
  105.1 7.2 %collective-permute-start.16 = (f32[256,512]{1,0:T(8,128)S(1)}, f32[256,512]{1,0:T(8,128)S(1)}, u32[]{:S(2)}, u32[]{:S(2)}) collective-permute-start(f32[256,512]{1,0:T(8,128)S(1)} %copy-done.21), channel_id=1, source_target_pairs={{0,1},{1,0},{2,3},{3,2},{4,5},{5,4},{6,7},{7,6},{8,9},{9,8},{10,11... | collective-permute-start | bytes 1572872 | tf_op jit(solution)/shard_map/ppermute | solution.py:37
  110.7 7.3 %collective-permute-start.15 = (bf16[32,2688]{1,0:T(8,128)(2,1)S(1)}, bf16[32,2688]{1,0:T(8,128)(2,1)S(1)}, u32[]{:S(2)}, u32[]{:S(2)}) collective-permute-start(bf16[32,2688]{1,0:T(8,128)(2,1)S(1)} %add_convert_fusion), channel_id=1, source_target_pairs={{0,2},{2,0},{1,3},{3,1},{4,6},{6,4},{5,7},{7,5},{8,10},{10,8},{9,1... | collective-permute-start | bytes 516104 | tf_op jit(solution)/shard_map/ppermute | solution.py:37
  112.2 9.8 %collective-permute-start.22 = (f32[64,896]{1,0:T(8,128)S(1)}, f32[64,896]{1,0:T(8,128)S(1)}, u32[]{:S(2)}, u32[]{:S(2)}) collective-permute-start(f32[64,896]{1,0:T(8,128)S(1)} %get-tuple-element.73), channel_id=1, source_target_pairs={{0,1},{1,0},{2,3},{3,2},{4,5},{5,4},{6,7},{7,6},{8,9},{9,8},{10,11... | collective-permute-start | bytes 688136 | tf_op jit(solution)/shard_map/ppermute | solution.py:37
  112.3 8.0 %collective-permute-start.17 = (bf16[128,512]{1,0:T(8,128)(2,1)S(1)}, bf16[128,512]{1,0:T(8,128)(2,1)S(1)}, u32[]{:S(2)}, u32[]{:S(2)}) collective-permute-start(bf16[128,512]{1,0:T(8,128)(2,1)S(1)} %add_convert_fusion.2), channel_id=1, source_target_pairs={{0,2},{2,0},{1,3},{3,1},{4,6},{6,4},{5,7},{7,5},{8,10},{10,8},{9,1... | collective-permute-start | bytes 393224 | tf_op jit(solution)/shard_map/ppermute | solution.py:37
  118.1 7.6 %collective-permute-start.20 = (bf16[32,1152]{1,0:T(8,128)(2,1)S(1)}, bf16[32,1152]{1,0:T(8,128)(2,1)S(1)}, u32[]{:S(2)}, u32[]{:S(2)}) collective-permute-start(bf16[32,1152]{1,0:T(8,128)(2,1)S(1)} %slice.85), channel_id=1, source_target_pairs={{0,4},{4,0},{8,12},{12,8},{1,5},{5,1},{9,13},{13,9},{2,6},{6,2},{1... | collective-permute-start | bytes 221192 | tf_op jit(solution)/shard_map/ppermute | solution.py:551
  130.1 6.3 %collective-permute-start.28 = (bf16[4,32,512]{2,1,0:T(8,128)(2,1)S(1)}, bf16[4,32,512]{2,1,0:T(8,128)(2,1)S(1)}, u32[]{:S(2)}, u32[]{:S(2)}) collective-permute-start(bf16[4,32,512]{2,1,0:T(8,128)(2,1)S(1)} %convolution_convert_fusion.3), channel_id=1, source_target_pairs={{0,1},{1,0},{2,3},{3,2},{4,8},{5,9},{6,10},{7,11},{8,4},{9,5},{10,... | collective-permute-start | bytes 393224 | tf_op jit(solution)/shard_map/ppermute | solution.py:441
  132.1 10.8 %collective-permute-start.25 = (bf16[4,32,512]{2,1,0:T(8,128)(2,1)S(1)}, bf16[4,32,512]{2,1,0:T(8,128)(2,1)S(1)}, u32[]{:S(2)}, u32[]{:S(2)}) collective-permute-start(bf16[4,32,512]{2,1,0:T(8,128)(2,1)S(1)} %convolution_convert_fusion.2), channel_id=1, source_target_pairs={{0,4},{4,0},{8,12},{12,8},{1,5},{5,1},{9,13},{13,9},{2,6},{6,2},{1... | collective-permute-start | bytes 393224 | tf_op jit(solution)/shard_map/ppermute | solution.py:563
  134.4 8.5 %collective-permute-start.27 = (bf16[4,32,512]{2,1,0:T(8,128)(2,1)S(1)}, bf16[4,32,512]{2,1,0:T(8,128)(2,1)S(1)}, u32[]{:S(2)}, u32[]{:S(2)}) collective-permute-start(bf16[4,32,512]{2,1,0:T(8,128)(2,1)S(1)} %convolution_convert_fusion), channel_id=1, source_target_pairs={{0,12},{1,13},{2,14},{3,15},{4,5},{5,4},{6,7},{7,6},{8,9},{9,8},{1... | collective-permute-start | bytes 393224 | tf_op jit(solution)/shard_map/ppermute | solution.py:561
  136.4 10.0 %collective-permute-start.26 = (bf16[4,32,512]{2,1,0:T(8,128)(2,1)S(1)}, bf16[4,32,512]{2,1,0:T(8,128)(2,1)S(1)}, u32[]{:S(2)}, u32[]{:S(2)}) collective-permute-start(bf16[4,32,512]{2,1,0:T(8,128)(2,1)S(1)} %fusion.2), channel_id=1, source_target_pairs={{0,8},{8,0},{4,12},{12,4},{1,9},{9,1},{5,13},{13,5},{2,10},{10,2},... | collective-permute-start | bytes 393224 | tf_op jit(solution)/shard_map/ppermute | solution.py:562
  (37 other events, 238.3 us)

commit v11 on v10

--- a/solution.py
+++ b/solution.py
@@ -187,20 +187,35 @@
 
         return index
 
-    operands = [grads, at_end[0]] + [array for pair in at_middle for array in pair]
+    operands = [grads, at_end[0]] + [array for pair in at_middle for array in pair] + [grads]
     specs = [
         pl.BlockSpec((tok, step), lambda i, flags_ref: (0, STEPS + i)),
         pl.BlockSpec((step, cols), lambda i, flags_ref: (at_end[1] + i * flags_ref[0], 0)),
     ]
     for first in (0, STEPS):
         specs += [pl.BlockSpec((step, cols), third_at(first))] * 2
-
-    def kernel(flags_ref, grads_ref, end_ref, b1_ref, c1_ref, b2_ref, c2_ref, total_ref):
+    specs.append(
+        pl.BlockSpec(
+            (tok, step),
+            lambda i, flags_ref: (0, flags_ref[0] * STEPS + jnp.minimum(i, STEPS - 1)),
+        )
+    )
+
+    def kernel(flags_ref, grads_ref, end_ref, b1_ref, c1_ref, b2_ref, c2_ref, next_ref, *out_refs):
+        total_ref, handed_ref, last_ref = out_refs
         i = pl.program_id(0)
 
         @pl.when(i == 0)
         def begin():
             total_ref[...] = jnp.zeros_like(total_ref)
+
+        @pl.when(i < STEPS)
+        def hand_on_next():
+            handed_ref[...] = next_ref[...]
+
+        @pl.when(i >= STEPS)
+        def hand_on_last():
+            last_ref[...] = grads_ref[...]
 
         @pl.when(flags_ref[0] == 1)
         def one():
@@ -217,21 +232,26 @@
                     grads_ref[...], shards, preferred_element_type=jnp.float32
                 )
 
+    third = jax.ShapeDtypeStruct((tok, STEPS * step), grads.dtype)
     return pl.pallas_call(
         kernel,
-        out_shape=jax.ShapeDtypeStruct((tok, 2 * cols), jnp.float32),
+        out_shape=[jax.ShapeDtypeStruct((tok, 2 * cols), jnp.float32), third, third],
         grid_spec=pltpu.PrefetchScalarGridSpec(
             num_scalar_prefetch=1,
             grid=(2 * STEPS,),
             in_specs=specs,
-            out_specs=pl.BlockSpec((tok, 2 * cols), lambda i, flags_ref: (0, 0)),
+            out_specs=[
+                pl.BlockSpec((tok, 2 * cols), lambda i, flags_ref: (0, 0)),
+                pl.BlockSpec((tok, step), lambda i, flags_ref: (0, jnp.minimum(i, STEPS - 1))),
+                pl.BlockSpec((tok, step), lambda i, flags_ref: (0, jnp.maximum(i - STEPS, 0))),
+            ],
         ),
         compiler_params=PARAMS,
         cost_estimate=SHORT,
     )(flags, *operands)
 
 
-def partner_dots(flags, pieces, shards, grads, column, shard, start):
+def partner_dots(flags, pieces, shards, grads, shard, start):
     tok = grads.shape[0]
     cols = shards[0][0].shape[1]
     step = shard[2] // STEPS
@@ -248,16 +268,8 @@
         operands.append(array)
         specs.append(pl.BlockSpec((step, cols), at(row)))
     operands += [grads, start]
-    specs.append(
-        pl.BlockSpec(
-            (tok, step),
-            lambda i, flags_ref: (0, column * (flags_ref[0] if two else 1) + i),
-        )
-    )
+    specs.append(pl.BlockSpec((tok, step), lambda i, flags_ref: (0, i)))
     specs.append(pl.BlockSpec(start.shape, whole))
-    if two:
-        operands.append(grads)
-        specs.append(pl.BlockSpec((tok, step), lambda i, flags_ref: (0, 2 * STEPS + i)))
 
     def kernel(flags_ref, *refs):
         i = pl.program_id(0)
@@ -265,8 +277,7 @@
         end_ref, grads_ref, start_ref = refs[count + len(shards) : count + len(shards) + 3]
         keep_ref, give_ref, *rest = refs[len(operands) :]
         if two:
-            second_ref, copied_ref, total_ref, sums_ref, turned_ref, wide_ref = rest
-            copied_ref[...] = refs[len(operands) - 1][...]
+            second_ref, total_ref, sums_ref, turned_ref, wide_ref = rest
         else:
             total_ref, sums_ref, turned_ref, wide_ref = rest
 
@@ -314,8 +325,6 @@
     if two:
         out_shape.append(jax.ShapeDtypeStruct((tok, cols), jnp.float32))
         out_specs.append(pl.BlockSpec((tok, cols), whole))
-        out_shape.append(jax.ShapeDtypeStruct((tok, STEPS * step), grads.dtype))
-        out_specs.append(pl.BlockSpec((tok, step), lambda i, flags_ref: (0, i)))
     return pl.pallas_call(
         kernel,
         out_shape=out_shape,
@@ -484,18 +493,17 @@
             ([(s3, 0)], 2 * STEPS, 2 * STEPS, STEPS, True),
         ],
     )
-    totals = both_dots(after(flags, to_s7, s45, *part_a), grads, (s45, 0), ((m2, m5), (m3, m6)))
+    totals, next_grads, last_grads = both_dots(after(flags, to_s7, s45, *part_a), grads, (s45, 0), ((m2, m5), (m3, m6)))
     parts = [jnp.concatenate(part, axis=1) for part in zip(part_own, part_a)]
     keep_a, give_a = after(parts, s6, m4, totals)
     core_a = swap(give_a, "rep")
 
     shards = [(basis_out, 0), (m4, 0), (m7, 0)]
-    *part_b, part_c, last_grads = partner_dots(
+    *part_b, part_c = partner_dots(
         after(flags, totals, core_a),
         [(s45, 0), (s45, STEPS), (s6, 0)],
         shards,
-        grads,
-        STEPS,
+        next_grads,
         (s6, 0, depth),
         totals,
     )
@@ -516,7 +524,6 @@
         [(s7, 0)],
         shards,
         last_grads,
-        0,
         (s7, 0, depth),
         part_c,
     )

time: 161 us -> 160 us (level)
  waiting for transfers between devices: 54 us -> 50.6 us
    ppermute x2, waiting for transfers between devices: 15.1 us -> 11.4 us  [side(): return lax.ppermute(pick(at_end, at_middle), 'cand', SIDE)]
    unnamed x70 -> x78, local copies, waits for them, and re-layouts: 16.6 us -> 18.1 us
  transfers between devices with their start and end apart: 29 -> 29, of which waited for: 12 -> 12; matrix products, arithmetic and copies ran while one was open for 11% -> 11% of each run, Pallas kernels for 16% -> 17%
where the time goes in v11:
time: 160 us; the launch traced here: 159 us
  waiting for transfers between devices  50.6 us (32%)
  starting transfers between devices  32.6 us (20%)
  Pallas kernels  26.7 us (17%)
  local copies, waits for them, and re-layouts  23.3 us (15%)
  other arithmetic  11.2 us (7%)
  blocking collectives  10.4 us (6%)
  matrix products  3.8 us (2%)
    unnamed x78, local copies, waits for them, and re-layouts  18.1 us
    ppermute x1, waiting for transfers between devices, line_plan(): s45 = lax.ppermute(after(to_s45, s3), 'cand', SIDE)  11.5 us
    ppermute x2, waiting for transfers between devices, side(): return lax.ppermute(pick(at_end, at_middle), 'cand', SIDE)  11.4 us
    all_to_all x1, blocking collectives, final_sum(): return jnp.sum(lax.all_to_all(blocks, ALL, 0, 0, tiled=True), axis=0)  10.4 us
    ppermute x9, waiting for transfers between devices, swap(): return lax.ppermute(x, axis_name, [(0, 1), (1, 0)])  10.1 us
    ppermute x2, starting transfers between devices, side(): return lax.ppermute(pick(at_end, at_middle), 'cand', SIDE)  9.64 us
    pallas_call x2, Pallas kernels, feature_dots(): pl.pallas_call(kernel, out_shape=out_shape, grid_spec=pltpu.PrefetchScala...  8.37 us
    pallas_call x2, Pallas kernels, partner_dots(): pl.pallas_call(kernel, out_shape=out_shape, grid_spec=pltpu.PrefetchScala...  7.91 us
  transfers between devices with their start and end apart: 29, of which 12 were waited for; matrix products, arithmetic and copies ran while one was open for 11% of the time, Pallas kernels for 17%

profile of v11, /device:TPU:0, one launch (start us, length us, event | category | flops | bytes accessed | tf_op | source)
XLA Modules:
  0.0 159.1 jit_solution(15946140298271455561)
XLA Ops:
  0.5 4.1 %collective-permute-start = (bf16[1280,128]{1,0:T(8,128)(2,1)}, bf16[1280,128]{1,0:T(8,128)(2,1)}, u32[]{:S(2)}, u32[]{:S(2)}) collective-permute-start(bf16[1280,128]{1,0:T(8,128)(2,1)} %refs_0_.3), channel_id=1, source_target_pairs={{0,4},{4,0},{8,12},{12,8},{1,5},{5,1},{9,13},{13,9},{2,6},{6,2},{1... | collective-permute-start | bytes 983048 | tf_op jit(solution)/shard_map/ppermute | solution.py:458
  4.6 2.4 %constant_dynamic-slice_fusion = bf16[4608,128]{1,0:T(8,128)(2,1)} fusion(bf16[6912,128]{1,0:T(8,128)(2,1)} %refs_1_.1, s32[]{:T(128)S(6)} %select_n.172), kind=kLoop, calls=%fused_computation.91 | loop fusion | bytes 2359300 | tf_op jit(solution)/shard_map/dynamic_slice | solution.py:457
  8.3 3.5 %divide_convert_fusion = bf16[64,32,512]{2,1,0:T(8,128)(2,1)} fusion(bf16[64,32,512]{2,1,0:T(8,128)(2,1)} %param.13, f32[32,512]{1,0:T(8,128)S(1)} %broadcast_add_fusion), kind=kLoop, calls=%fused_computation | loop fusion | flops 3145728 | bytes 4259840 | tf_op jit(solution)/shard_map/convert_element_type | solution.py:468
  11.9 3.0 %copy-done = bf16[512,6912]{1,0:T(8,128)(2,1)S(1)} copy-done((bf16[512,6912]{1,0:T(8,128)(2,1)S(1)}, bf16[512,6912]{1,0:T(8,128)(2,1)}, u32[]{:S(2)}) %copy-start) | copy-done | bytes 7077912
  20.8 3.0 %copy-done.1 = bf16[512,6912]{1,0:T(8,128)(2,1)S(1)} copy-done((bf16[512,6912]{1,0:T(8,128)(2,1)S(1)}, bf16[512,6912]{1,0:T(8,128)(2,1)}, u32[]{:S(2)}) %copy-start.1) | copy-done | bytes 7077912
  23.8 4.6 %shard_map.82 = (f32[64,512]{1,0:T(8,128)S(1)}, f32[64,512]{1,0:T(8,128)S(1)}) custom-call(s32[6]{0:T(128)S(1)} %stack.49.flags_ref, bf16[512,6912]{1,0:T(8,128)(2,1)S(1)} %copy-done.1, bf16[6912,128]{1,0:T(8,128)(2,1)S(1)} %copy-done.2), custom_call_target="tpu_custom_call" | custom-call | flops 1 | bytes 1 | tf_op jit(solution)/shard_map/pallas_call | solution.py:164
  28.7 4.0 %collective-permute-start.3 = (bf16[2560,128]{1,0:T(8,128)(2,1)S(1)}, bf16[2560,128]{1,0:T(8,128)(2,1)S(1)}, u32[]{:S(2)}, u32[]{:S(2)}) collective-permute-start(bf16[2560,128]{1,0:T(8,128)(2,1)S(1)} %maximum_select_fusion.1), channel_id=1, source_target_pairs={{0,4},{4,0},{8,12},{12,8},{1,5},{5,1},{9,13},{13,9},{2,6},{6,2},{1... | collective-permute-start | bytes 1966088 | tf_op jit(solution)/shard_map/ppermute | solution.py:440
  32.7 6.0 %collective-permute-done.4.refs_0_ = bf16[4608,128]{1,0:T(8,128)(2,1)S(1)} collective-permute-done((bf16[4608,128]{1,0:T(8,128)(2,1)}, bf16[4608,128]{1,0:T(8,128)(2,1)S(1)}, u32[]{:S(2)}, u32[]{:S(2)}) %collective-permute-start.4) | collective-permute-done | bytes 1179680 | tf_op jit(solution)/shard_map/ppermute | solution.py:460
  41.3 10.3 %collective-permute-done.3.refs_2_.refs_4_.refs_1_ = bf16[2560,128]{1,0:T(8,128)(2,1)S(1)} collective-permute-done((bf16[2560,128]{1,0:T(8,128)(2,1)S(1)}, bf16[2560,128]{1,0:T(8,128)(2,1)S(1)}, u32[]{:S(2)}, u32[]{:S(2)}) %collective-permute-start.3) | collective-permute-done | bytes 655392 | tf_op jit(solution)/shard_map/ppermute | solution.py:440
  54.1 3.9 %shard_map.83 = (f32[256,512]{1,0:T(8,128)S(1)}, f32[256,512]{1,0:T(8,128)S(1)}) custom-call(s32[6]{0:T(128)S(1)} %stack.49.flags_ref, bf16[512,1280]{1,0:T(8,128)(2,1)S(1)} %copy-done.14, bf16[1280,128]{1,0:T(8,128)(2,1)S(1)} %copy-done.23, bf16[1280,128]{1,0:T(8,128)(2,1)} %collective-permute-done.refs_1_, ...), custom_call_target="tpu_custom_call" | custom-call | flops 1 | bytes 1 | tf_op jit(solution)/shard_map/pallas_call | solution.py:411
  58.2 5.6 %collective-permute-start.6 = (bf16[2304,128]{1,0:T(8,128)(2,1)S(1)}, bf16[2304,128]{1,0:T(8,128)(2,1)S(1)}, u32[]{:S(2)}, u32[]{:S(2)}) collective-permute-start(bf16[2304,128]{1,0:T(8,128)(2,1)S(1)} %broadcast_select_fusion.1), channel_id=1, source_target_pairs={{0,4},{4,0},{8,12},{12,8},{1,5},{5,1},{9,13},{13,9},{2,6},{6,2},{1... | collective-permute-start | bytes 1769480 | tf_op jit(solution)/shard_map/ppermute | solution.py:440
  63.8 3.8 %shard_map.84 = (f32[64,512]{1,0:T(8,128)S(1)}, f32[64,512]{1,0:T(8,128)S(1)}) custom-call(s32[6]{0:T(128)S(1)} %stack.49.flags_ref, bf16[512,6912]{1,0:T(8,128)(2,1)S(1)} %bitcast.72, bf16[4608,128]{1,0:T(8,128)(2,1)S(1)} %copy-done.4, bf16[2560,128]{1,0:T(8,128)(2,1)S(1)} %collective-permute-done.3.refs_2_.refs_4_.refs_1_), custom_call_target="tpu_custom_call" | custom-call | flops 1 | bytes 1 | tf_op jit(solution)/shard_map/pallas_call | solution.py:164
  69.0 11.5 %collective-permute-done.10.end_ref.refs_0_.refs_1_ = bf16[4608,128]{1,0:T(8,128)(2,1)S(1)} collective-permute-done((bf16[4608,128]{1,0:T(8,128)(2,1)S(1)}, bf16[4608,128]{1,0:T(8,128)(2,1)S(1)}, u32[]{:S(2)}, u32[]{:S(2)}) %collective-permute-start.10) | collective-permute-done | bytes 1179680 | tf_op jit(solution)/shard_map/ppermute | solution.py:475
  83.1 5.2 %shard_map.86 = (f32[512,256]{1,0:T(8,128)S(1)}, bf16[512,2304]{1,0:T(8,128)(2,1)S(1)}, bf16[512,2304]{1,0:T(8,128)(2,1)S(1)}) custom-call(s32[6]{0:T(128)S(1)} %stack.49.flags_ref, bf16[512,6912]{1,0:T(8,128)(2,1)S(1)} %bitcast.72, bf16[4608,128]{1,0:T(8,128)(2,1)S(1)} %collective-permute-done.10.end_ref.refs_0_.refs_1_, ...), custom_call_target="tpu_custom_call" | custom-call | flops 1 | bytes 1 | tf_op jit(solution)/shard_map/pallas_call | solution.py:236
  99.6 3.9 %shard_map.87 = (f32[64,1664]{1,0:T(8,128)S(1)}, f32[64,1664]{1,0:T(8,128)S(1)}, f32[512,128]{1,0:T(8,128)S(1)}) custom-call(s32[6]{0:T(128)S(1)} %stack.49.flags_ref, bf16[4608,128]{1,0:T(8,128)(2,1)S(1)} %collective-permute-done.10.end_ref.refs_0_.refs_1_, bf16[4608,128]{1,0:T(8,128)(2,1)S(1)} %collective-permute-done.10.end_ref.refs_0_.refs_1_, ...), custom_call_target="tpu_custom_call" | custom-call | flops 1 | bytes 1 | tf_op jit(solution)/shard_map/pallas_call | solution.py:328
  105.2 4.0 %shard_map.88 = (f32[64,896]{1,0:T(8,128)S(1)}, f32[64,896]{1,0:T(8,128)S(1)}) custom-call(s32[6]{0:T(128)S(1)} %stack.49.flags_ref, bf16[2304,128]{1,0:T(8,128)(2,1)} %collective-permute-done.21.refs_0_.refs_4_, bf16[6912,128]{1,0:T(8,128)(2,1)S(1)} %copy-done.2, bf16[2304,128]{1,0:T(8,128)(2,1)S(1)} %copy-done.9, ...), custom_call_target="tpu_custom_call" | custom-call | flops 1 | bytes 1 | tf_op jit(solution)/shard_map/pallas_call | solution.py:328
  112.0 4.7 %collective-permute-done.15 = bf16[32,2688]{1,0:T(8,128)(2,1)S(1)} collective-permute-done((bf16[32,2688]{1,0:T(8,128)(2,1)S(1)}, bf16[32,2688]{1,0:T(8,128)(2,1)S(1)}, u32[]{:S(2)}, u32[]{:S(2)}) %collective-permute-start.15) | collective-permute-done | bytes 172064 | tf_op jit(solution)/shard_map/ppermute | solution.py:37
  116.8 2.2 %collective-permute-start.20 = (bf16[32,1152]{1,0:T(8,128)(2,1)S(1)}, bf16[32,1152]{1,0:T(8,128)(2,1)S(1)}, u32[]{:S(2)}, u32[]{:S(2)}) collective-permute-start(bf16[32,1152]{1,0:T(8,128)(2,1)S(1)} %slice.85), channel_id=1, source_target_pairs={{0,4},{4,0},{8,12},{12,8},{1,5},{5,1},{9,13},{13,9},{2,6},{6,2},{1... | collective-permute-start | bytes 221192 | tf_op jit(solution)/shard_map/ppermute | solution.py:558
  121.4 2.8 %collective-permute-done.18 = bf16[128,512]{1,0:T(8,128)(2,1)S(1)} collective-permute-done((bf16[128,512]{1,0:T(8,128)(2,1)S(1)}, bf16[128,512]{1,0:T(8,128)(2,1)S(1)}, u32[]{:S(2)}, u32[]{:S(2)}) %collective-permute-start.18) | collective-permute-done | bytes 131104 | tf_op jit(solution)/shard_map/ppermute | solution.py:37
  126.5 2.2 %collective-permute-start.24 = (bf16[32,384]{1,0:T(8,128)(2,1)S(1)}, bf16[32,384]{1,0:T(8,128)(2,1)S(1)}, u32[]{:S(2)}, u32[]{:S(2)}) collective-permute-start(bf16[32,384]{1,0:T(8,128)(2,1)S(1)} %slice.123), channel_id=1, source_target_pairs={{0,4},{4,0},{8,12},{12,8},{1,5},{5,1},{9,13},{13,9},{2,6},{6,2},{1... | collective-permute-start | bytes 73736 | tf_op jit(solution)/shard_map/ppermute | solution.py:557
  135.2 6.5 %collective-permute-done.27 = bf16[4,32,512]{2,1,0:T(8,128)(2,1)S(1)} collective-permute-done((bf16[4,32,512]{2,1,0:T(8,128)(2,1)S(1)}, bf16[4,32,512]{2,1,0:T(8,128)(2,1)S(1)}, u32[]{:S(2)}, u32[]{:S(2)}) %collective-permute-start.27) | collective-permute-done | bytes 131104 | tf_op jit(solution)/shard_map/ppermute | solution.py:568
  141.7 3.4 %collective-permute-done.26 = bf16[4,32,512]{2,1,0:T(8,128)(2,1)S(1)} collective-permute-done((bf16[4,32,512]{2,1,0:T(8,128)(2,1)S(1)}, bf16[4,32,512]{2,1,0:T(8,128)(2,1)S(1)}, u32[]{:S(2)}, u32[]{:S(2)}) %collective-permute-start.26) | collective-permute-done | bytes 131104 | tf_op jit(solution)/shard_map/ppermute | solution.py:569
  145.2 2.8 %fusion.3 = f32[16,64]{1,0:T(8,128)S(1)} fusion(bf16[64,32,512]{2,1,0:T(8,128)(2,1)S(1)} %copy-done.27, bf16[16,32,512]{2,1,0:T(8,128)(2,1)S(1)} %pad_maximum_fusion.1), kind=kOutput, calls=%fused_computation.10 | convolution fusion | flops 33554432 | bytes 2625536 | tf_op jit(solution)/shard_map/tea,jea->tj/dot_general | solution.py:547
  148.2 10.4 %all_to_all.5 = f32[16,2,16]{2,1,0:T(2,128)S(1)} all-to-all(f32[16,2,16]{2,1,0:T(2,128)S(1)} %copy.72), channel_id=1, replica_groups=mesh['groups'=2,'cand'=4,'eig'=2,'rep'=2] {'cand','eig','rep'}, dimensions={0} | all-to-all | bytes 4096 | tf_op jit(solution)/shard_map/all_to_all | solution.py:584
  (183 shorter events, 44.4 us)
Async XLA Ops:
  0.0 19.3 %collective-permute-start.1 = (bf16[1280,128]{1,0:T(8,128)(2,1)}, bf16[1280,128]{1,0:T(8,128)(2,1)S(1)}, u32[]{:S(2)}, u32[]{:S(2)}) collective-permute-start(bf16[1280,128]{1,0:T(8,128)(2,1)} %refs_0_.3), channel_id=1, source_target_pairs={{0,1},{1,0},{2,3},{3,2},{4,8},{5,9},{6,10},{7,11},{8,4},{9,5},{10,... | collective-permute-start | bytes 983048 | tf_op jit(solution)/shard_map/ppermute | solution.py:450
  0.5 18.8 %collective-permute-start = (bf16[1280,128]{1,0:T(8,128)(2,1)}, bf16[1280,128]{1,0:T(8,128)(2,1)}, u32[]{:S(2)}, u32[]{:S(2)}) collective-permute-start(bf16[1280,128]{1,0:T(8,128)(2,1)} %refs_0_.3), channel_id=1, source_target_pairs={{0,4},{4,0},{8,12},{12,8},{1,5},{5,1},{9,13},{13,9},{2,6},{6,2},{1... | collective-permute-start | bytes 983048 | tf_op jit(solution)/shard_map/ppermute | solution.py:458
  7.0 31.7 %collective-permute-start.4 = (bf16[4608,128]{1,0:T(8,128)(2,1)}, bf16[4608,128]{1,0:T(8,128)(2,1)S(1)}, u32[]{:S(2)}, u32[]{:S(2)}) collective-permute-start(bf16[4608,128]{1,0:T(8,128)(2,1)} %constant_dynamic-slice_fusion), channel_id=1, source_target_pairs={{0,4},{4,0},{8,12},{12,8},{1,5},{5,1},{9,13},{13,9},{2,6},{6,2},{1... | collective-permute-start | bytes 3538952 | tf_op jit(solution)/shard_map/ppermute | solution.py:460
  8.3 31.5 %collective-permute-start.8 = (bf16[2304,128]{1,0:T(8,128)(2,1)}, bf16[2304,128]{1,0:T(8,128)(2,1)}, u32[]{:S(2)}, u32[]{:S(2)}) collective-permute-start(bf16[2304,128]{1,0:T(8,128)(2,1)} %get-tuple-element.88), channel_id=1, source_target_pairs={{0,1},{1,0},{2,3},{3,2},{4,8},{5,9},{6,10},{7,11},{8,4},{9,5},{10,... | collective-permute-start | bytes 1769480 | tf_op jit(solution)/shard_map/ppermute | solution.py:450
  19.3 9.2 %collective-permute-start.2 = (bf16[1280,128]{1,0:T(8,128)(2,1)}, bf16[1280,128]{1,0:T(8,128)(2,1)S(1)}, u32[]{:S(2)}, u32[]{:S(2)}) collective-permute-start(bf16[1280,128]{1,0:T(8,128)(2,1)} %collective-permute-done.refs_1_), channel_id=1, source_target_pairs={{0,1},{1,0},{2,3},{3,2},{4,8},{5,9},{6,10},{7,11},{8,4},{9,5},{10,... | collective-permute-start | bytes 983048 | tf_op jit(solution)/shard_map/ppermute | solution.py:450
  28.4 11.3 %collective-permute-start.9 = (bf16[2304,128]{1,0:T(8,128)(2,1)S(1)}, bf16[2304,128]{1,0:T(8,128)(2,1)S(1)}, u32[]{:S(2)}, u32[]{:S(2)}) collective-permute-start(bf16[2304,128]{1,0:T(8,128)(2,1)S(1)} %copy-done.26), channel_id=1, source_target_pairs={{0,1},{1,0},{2,3},{3,2},{4,8},{5,9},{6,10},{7,11},{8,4},{9,5},{10,... | collective-permute-start | bytes 1769480 | tf_op jit(solution)/shard_map/ppermute | solution.py:450
  28.7 22.9 %collective-permute-start.3 = (bf16[2560,128]{1,0:T(8,128)(2,1)S(1)}, bf16[2560,128]{1,0:T(8,128)(2,1)S(1)}, u32[]{:S(2)}, u32[]{:S(2)}) collective-permute-start(bf16[2560,128]{1,0:T(8,128)(2,1)S(1)} %maximum_select_fusion.1), channel_id=1, source_target_pairs={{0,4},{4,0},{8,12},{12,8},{1,5},{5,1},{9,13},{13,9},{2,6},{6,2},{1... | collective-permute-start | bytes 1966088 | tf_op jit(solution)/shard_map/ppermute | solution.py:440
  39.7 14.4 %collective-permute-start.5 = (bf16[2304,128]{1,0:T(8,128)(2,1)S(1)}, bf16[2304,128]{1,0:T(8,128)(2,1)S(1)}, u32[]{:S(2)}, u32[]{:S(2)}) collective-permute-start(bf16[2304,128]{1,0:T(8,128)(2,1)S(1)} %get-tuple-element.90), channel_id=1, source_target_pairs={{0,1},{1,0},{2,3},{3,2},{4,8},{5,9},{6,10},{7,11},{8,4},{9,5},{10,... | collective-permute-start | bytes 1769480 | tf_op jit(solution)/shard_map/ppermute | solution.py:450
  51.6 28.9 %collective-permute-start.10 = (bf16[4608,128]{1,0:T(8,128)(2,1)S(1)}, bf16[4608,128]{1,0:T(8,128)(2,1)S(1)}, u32[]{:S(2)}, u32[]{:S(2)}) collective-permute-start(bf16[4608,128]{1,0:T(8,128)(2,1)S(1)} %maximum_select_fusion), channel_id=1, source_target_pairs={{0,4},{4,0},{8,12},{12,8},{1,5},{5,1},{9,13},{13,9},{2,6},{6,2},{1... | collective-permute-start | bytes 3538952 | tf_op jit(solution)/shard_map/ppermute | solution.py:475
  54.0 14.4 %collective-permute-start.11 = (bf16[2304,128]{1,0:T(8,128)(2,1)S(1)}, bf16[2304,128]{1,0:T(8,128)(2,1)S(1)}, u32[]{:S(2)}, u32[]{:S(2)}) collective-permute-start(bf16[2304,128]{1,0:T(8,128)(2,1)S(1)} %slice.81), channel_id=1, source_target_pairs={{0,1},{1,0},{2,3},{3,2},{4,8},{5,9},{6,10},{7,11},{8,4},{9,5},{10,... | collective-permute-start | bytes 1769480 | tf_op jit(solution)/shard_map/ppermute | solution.py:450
  58.2 35.0 %collective-permute-start.6 = (bf16[2304,128]{1,0:T(8,128)(2,1)S(1)}, bf16[2304,128]{1,0:T(8,128)(2,1)S(1)}, u32[]{:S(2)}, u32[]{:S(2)}) collective-permute-start(bf16[2304,128]{1,0:T(8,128)(2,1)S(1)} %broadcast_select_fusion.1), channel_id=1, source_target_pairs={{0,4},{4,0},{8,12},{12,8},{1,5},{5,1},{9,13},{13,9},{2,6},{6,2},{1... | collective-permute-start | bytes 1769480 | tf_op jit(solution)/shard_map/ppermute | solution.py:440
  63.8 29.4 %collective-permute-start.7 = (bf16[2304,128]{1,0:T(8,128)(2,1)S(1)}, bf16[2304,128]{1,0:T(8,128)(2,1)S(1)}, u32[]{:S(2)}, u32[]{:S(2)}) collective-permute-start(bf16[2304,128]{1,0:T(8,128)(2,1)S(1)} %copy-done.29), channel_id=1, source_target_pairs={{0,1},{1,0},{2,3},{3,2},{4,8},{5,9},{6,10},{7,11},{8,4},{9,5},{10,... | collective-permute-start | bytes 1769480 | tf_op jit(solution)/shard_map/ppermute | solution.py:450
  68.5 27.4 %collective-permute-start.13 = (bf16[2304,128]{1,0:T(8,128)(2,1)}, bf16[2304,128]{1,0:T(8,128)(2,1)}, u32[]{:S(2)}, u32[]{:S(2)}) collective-permute-start(bf16[2304,128]{1,0:T(8,128)(2,1)} %get-tuple-element.65), channel_id=1, source_target_pairs={{0,1},{1,0},{2,3},{3,2},{4,8},{5,9},{6,10},{7,11},{8,4},{9,5},{10,... | collective-permute-start | bytes 1769480 | tf_op jit(solution)/shard_map/ppermute | solution.py:450
  81.4 23.8 %collective-permute-start.21 = (bf16[2304,128]{1,0:T(8,128)(2,1)}, bf16[2304,128]{1,0:T(8,128)(2,1)}, u32[]{:S(2)}, u32[]{:S(2)}) collective-permute-start(bf16[2304,128]{1,0:T(8,128)(2,1)} %broadcast_select_fusion), channel_id=1, source_target_pairs={{0,4},{4,0},{8,12},{12,8},{1,5},{5,1},{9,13},{13,9},{2,6},{6,2},{1... | collective-permute-start | bytes 1769480 | tf_op jit(solution)/shard_map/ppermute | solution.py:480
  103.5 5.8 %collective-permute-start.14 = (f32[64,1664]{1,0:T(8,128)S(1)}, f32[64,1664]{1,0:T(8,128)S(1)}, u32[]{:S(2)}, u32[]{:S(2)}) collective-permute-start(f32[64,1664]{1,0:T(8,128)S(1)} %get-tuple-element.68), channel_id=1, source_target_pairs={{0,1},{1,0},{2,3},{3,2},{4,5},{5,4},{6,7},{7,6},{8,9},{9,8},{10,11... | collective-permute-start | bytes 1277960 | tf_op jit(solution)/shard_map/ppermute | solution.py:37
  103.8 7.2 %collective-permute-start.16 = (f32[256,512]{1,0:T(8,128)S(1)}, f32[256,512]{1,0:T(8,128)S(1)}, u32[]{:S(2)}, u32[]{:S(2)}) collective-permute-start(f32[256,512]{1,0:T(8,128)S(1)} %copy-done.25), channel_id=1, source_target_pairs={{0,1},{1,0},{2,3},{3,2},{4,5},{5,4},{6,7},{7,6},{8,9},{9,8},{10,11... | collective-permute-start | bytes 1572872 | tf_op jit(solution)/shard_map/ppermute | solution.py:37
  109.4 7.3 %collective-permute-start.15 = (bf16[32,2688]{1,0:T(8,128)(2,1)S(1)}, bf16[32,2688]{1,0:T(8,128)(2,1)S(1)}, u32[]{:S(2)}, u32[]{:S(2)}) collective-permute-start(bf16[32,2688]{1,0:T(8,128)(2,1)S(1)} %add_convert_fusion), channel_id=1, source_target_pairs={{0,2},{2,0},{1,3},{3,1},{4,6},{6,4},{5,7},{7,5},{8,10},{10,8},{9,1... | collective-permute-start | bytes 516104 | tf_op jit(solution)/shard_map/ppermute | solution.py:37
  111.0 9.8 %collective-permute-start.22 = (f32[64,896]{1,0:T(8,128)S(1)}, f32[64,896]{1,0:T(8,128)S(1)}, u32[]{:S(2)}, u32[]{:S(2)}) collective-permute-start(f32[64,896]{1,0:T(8,128)S(1)} %get-tuple-element.77), channel_id=1, source_target_pairs={{0,1},{1,0},{2,3},{3,2},{4,5},{5,4},{6,7},{7,6},{8,9},{9,8},{10,11... | collective-permute-start | bytes 688136 | tf_op jit(solution)/shard_map/ppermute | solution.py:37
  111.1 8.0 %collective-permute-start.17 = (bf16[128,512]{1,0:T(8,128)(2,1)S(1)}, bf16[128,512]{1,0:T(8,128)(2,1)S(1)}, u32[]{:S(2)}, u32[]{:S(2)}) collective-permute-start(bf16[128,512]{1,0:T(8,128)(2,1)S(1)} %add_convert_fusion.2), channel_id=1, source_target_pairs={{0,2},{2,0},{1,3},{3,1},{4,6},{6,4},{5,7},{7,5},{8,10},{10,8},{9,1... | collective-permute-start | bytes 393224 | tf_op jit(solution)/shard_map/ppermute | solution.py:37
  116.8 7.5 %collective-permute-start.20 = (bf16[32,1152]{1,0:T(8,128)(2,1)S(1)}, bf16[32,1152]{1,0:T(8,128)(2,1)S(1)}, u32[]{:S(2)}, u32[]{:S(2)}) collective-permute-start(bf16[32,1152]{1,0:T(8,128)(2,1)S(1)} %slice.85), channel_id=1, source_target_pairs={{0,4},{4,0},{8,12},{12,8},{1,5},{5,1},{9,13},{13,9},{2,6},{6,2},{1... | collective-permute-start | bytes 221192 | tf_op jit(solution)/shard_map/ppermute | solution.py:558
  128.8 6.3 %collective-permute-start.28 = (bf16[4,32,512]{2,1,0:T(8,128)(2,1)S(1)}, bf16[4,32,512]{2,1,0:T(8,128)(2,1)S(1)}, u32[]{:S(2)}, u32[]{:S(2)}) collective-permute-start(bf16[4,32,512]{2,1,0:T(8,128)(2,1)S(1)} %convolution_convert_fusion.3), channel_id=1, source_target_pairs={{0,1},{1,0},{2,3},{3,2},{4,8},{5,9},{6,10},{7,11},{8,4},{9,5},{10,... | collective-permute-start | bytes 393224 | tf_op jit(solution)/shard_map/ppermute | solution.py:450
  130.8 10.8 %collective-permute-start.25 = (bf16[4,32,512]{2,1,0:T(8,128)(2,1)S(1)}, bf16[4,32,512]{2,1,0:T(8,128)(2,1)S(1)}, u32[]{:S(2)}, u32[]{:S(2)}) collective-permute-start(bf16[4,32,512]{2,1,0:T(8,128)(2,1)S(1)} %convolution_convert_fusion.2), channel_id=1, source_target_pairs={{0,4},{4,0},{8,12},{12,8},{1,5},{5,1},{9,13},{13,9},{2,6},{6,2},{1... | collective-permute-start | bytes 393224 | tf_op jit(solution)/shard_map/ppermute | solution.py:570
  133.1 8.5 %collective-permute-start.27 = (bf16[4,32,512]{2,1,0:T(8,128)(2,1)S(1)}, bf16[4,32,512]{2,1,0:T(8,128)(2,1)S(1)}, u32[]{:S(2)}, u32[]{:S(2)}) collective-permute-start(bf16[4,32,512]{2,1,0:T(8,128)(2,1)S(1)} %convolution_convert_fusion), channel_id=1, source_target_pairs={{0,12},{1,13},{2,14},{3,15},{4,5},{5,4},{6,7},{7,6},{8,9},{9,8},{1... | collective-permute-start | bytes 393224 | tf_op jit(solution)/shard_map/ppermute | solution.py:568
  135.1 10.0 %collective-permute-start.26 = (bf16[4,32,512]{2,1,0:T(8,128)(2,1)S(1)}, bf16[4,32,512]{2,1,0:T(8,128)(2,1)S(1)}, u32[]{:S(2)}, u32[]{:S(2)}) collective-permute-start(bf16[4,32,512]{2,1,0:T(8,128)(2,1)S(1)} %fusion.2), channel_id=1, source_target_pairs={{0,8},{8,0},{4,12},{12,4},{1,9},{9,1},{5,13},{13,5},{2,10},{10,2},... | collective-permute-start | bytes 393224 | tf_op jit(solution)/shard_map/ppermute | solution.py:569
  (41 other events, 250.3 us)

commit v12 on v11

--- a/solution.py
+++ b/solution.py
@@ -509,7 +509,8 @@
     )
     keep_in, give_in = after(part_in, part_c)
     core_in = swap(give_in, "rep")
-    rot_in = gather_rows(chip_sum(*chip_parts(keep_in, core_in)).astype(jnp.bfloat16))
+    keep_in, give_in = chip_parts(keep_in, core_in)
+    rot_in = gather_rows(chip_sum(keep_in, give_in).astype(jnp.bfloat16))
     rot_in = rot_in.reshape(tiles_here, TILE, 4 * cols)
     keep_b, give_b = part_b
     keep_b, give_b = chip_parts(
@@ -520,14 +521,13 @@
     sum_own, sum_a, sum_b = [sums[:, i * tok_rows : (i + 1) * tok_rows] for i in range(3)]
     sums = sums[:, 3 * tok_rows :].astype(jnp.bfloat16)
     keep_last, give_last = partner_dots(
-        after(flags, part_c),
+        after(flags, part_c, give_b, give_in),
         [(s7, 0)],
         shards,
         last_grads,
         (s7, 0, depth),
         part_c,
     )
-    keep_last, give_last = after((keep_last, give_last), give_b)
     sum_last = chip_sum(*chip_parts(keep_last, swap(give_last, "rep")))
     sum_c, sum_last = sum_last[:, :tok_rows], sum_last[:, tok_rows:].astype(jnp.bfloat16)
 
@@ -579,9 +579,10 @@
 
 def final_sum(total):
     npairs, ntest = total.shape
-    blocks = total.reshape(4, npairs // 4, 4, ntest // 4).transpose(0, 2, 1, 3)
-    blocks = blocks.reshape(16, npairs // 4, ntest // 4)
-    return jnp.sum(lax.all_to_all(blocks, ALL, 0, 0, tiled=True), axis=0)
+    keep, give = halves(total.reshape(npairs, 2, 2, ntest // 4).transpose(2, 0, 1, 3), "rep")
+    blocks = (keep + swap(give, "rep")).reshape(4, npairs // 4, 2, ntest // 4).transpose(0, 2, 1, 3)
+    blocks = blocks.reshape(8, npairs // 4, ntest // 4)
+    return jnp.sum(lax.all_to_all(blocks, ("cand", "eig"), 0, 0, tiled=True), axis=0)
 
 
 def gather_plan(acts, grads, basis_in, basis_out, eigval, test_grads, pair_tiles, last_rows):

time: 160 us -> 156 us (0.975)
  other arithmetic: 11.2 us -> 9.39 us
    ppermute x9 -> x10, waiting for transfers between devices: 10.1 us -> 6.96 us  [swap(): return lax.ppermute(x, axis_name, [(0, 1), (1, 0)])]
    ppermute x1, waiting for transfers between devices: 0.01 us -> 2.54 us  [line_plan(): s7 = lax.ppermute(to_s7, 'cand', SIDE)]
    ppermute x1, starting transfers between devices: 1.72 us -> 3.59 us  [line_plan(): from_far = lax.ppermute(prods_c, ALL, far)]
    ppermute x9 -> x10, starting transfers between devices: 5.32 us -> 5.21 us  [swap(): return lax.ppermute(x, axis_name, [(0, 1), (1, 0)])]
  transfers between devices with their start and end apart: 29 -> 30, of which waited for: 12 -> 14; matrix products, arithmetic and copies ran while one was open for 11% -> 10% of each run, Pallas kernels for 17% -> 17%
where the time goes in v12:
time: 156 us; the launch traced here: 155 us
  waiting for transfers between devices  50.3 us (32%)
  starting transfers between devices  31.9 us (20%)
  Pallas kernels  26 us (17%)
  local copies, waits for them, and re-layouts  23.3 us (15%)
  blocking collectives  9.95 us (6%)
  other arithmetic  9.39 us (6%)
  matrix products  3.8 us (2%)
    unnamed x78, local copies, waits for them, and re-layouts  18.1 us
    ppermute x1, waiting for transfers between devices, line_plan(): s45 = lax.ppermute(after(to_s45, s3), 'cand', SIDE)  12 us
    ppermute x2, waiting for transfers between devices, side(): return lax.ppermute(pick(at_end, at_middle), 'cand', SIDE)  11 us
    ppermute x2, starting transfers between devices, side(): return lax.ppermute(pick(at_end, at_middle), 'cand', SIDE)  10.2 us
    all_to_all x1, blocking collectives, final_sum(): lax.all_to_all(blocks, ('cand', 'eig'), 0, 0, tiled=True)  9.95 us
    pallas_call x2, Pallas kernels, feature_dots(): pl.pallas_call(kernel, out_shape=out_shape, grid_spec=pltpu.PrefetchScala...  8.37 us
    pallas_call x2, Pallas kernels, partner_dots(): pl.pallas_call(kernel, out_shape=out_shape, grid_spec=pltpu.PrefetchScala...  7.21 us
    ppermute x10, waiting for transfers between devices, swap(): return lax.ppermute(x, axis_name, [(0, 1), (1, 0)])  6.96 us
  transfers between devices with their start and end apart: 30, of which 14 were waited for; matrix products, arithmetic and copies ran while one was open for 10% of the time, Pallas kernels for 17%

profile of v12, /device:TPU:0, one launch (start us, length us, event | category | flops | bytes accessed | tf_op | source)
XLA Modules:
  0.0 155.4 jit_solution(9585596532780906870)
XLA Ops:
  0.5 4.1 %collective-permute-start = (bf16[1280,128]{1,0:T(8,128)(2,1)}, bf16[1280,128]{1,0:T(8,128)(2,1)}, u32[]{:S(2)}, u32[]{:S(2)}) collective-permute-start(bf16[1280,128]{1,0:T(8,128)(2,1)} %refs_0_.3), channel_id=1, source_target_pairs={{0,4},{4,0},{8,12},{12,8},{1,5},{5,1},{9,13},{13,9},{2,6},{6,2},{1... | collective-permute-start | bytes 983048 | tf_op jit(solution)/shard_map/ppermute | solution.py:458
  4.6 2.4 %constant_dynamic-slice_fusion = bf16[4608,128]{1,0:T(8,128)(2,1)} fusion(bf16[6912,128]{1,0:T(8,128)(2,1)} %refs_1_.1, s32[]{:T(128)S(6)} %select_n.185), kind=kLoop, calls=%fused_computation.94 | loop fusion | bytes 2359300 | tf_op jit(solution)/shard_map/dynamic_slice | solution.py:457
  8.3 3.5 %divide_convert_fusion = bf16[64,32,512]{2,1,0:T(8,128)(2,1)} fusion(bf16[64,32,512]{2,1,0:T(8,128)(2,1)} %param.13, f32[32,512]{1,0:T(8,128)S(1)} %broadcast_add_fusion), kind=kLoop, calls=%fused_computation | loop fusion | flops 3145728 | bytes 4259840 | tf_op jit(solution)/shard_map/convert_element_type | solution.py:468
  11.9 3.0 %copy-done = bf16[512,6912]{1,0:T(8,128)(2,1)S(1)} copy-done((bf16[512,6912]{1,0:T(8,128)(2,1)S(1)}, bf16[512,6912]{1,0:T(8,128)(2,1)}, u32[]{:S(2)}) %copy-start) | copy-done | bytes 7077912
  20.2 3.0 %copy-done.1 = bf16[512,6912]{1,0:T(8,128)(2,1)S(1)} copy-done((bf16[512,6912]{1,0:T(8,128)(2,1)S(1)}, bf16[512,6912]{1,0:T(8,128)(2,1)}, u32[]{:S(2)}) %copy-start.1) | copy-done | bytes 7077912
  23.3 4.6 %shard_map.82 = (f32[64,512]{1,0:T(8,128)S(1)}, f32[64,512]{1,0:T(8,128)S(1)}) custom-call(s32[6]{0:T(128)S(1)} %stack.49.flags_ref, bf16[512,6912]{1,0:T(8,128)(2,1)S(1)} %copy-done.1, bf16[6912,128]{1,0:T(8,128)(2,1)S(1)} %copy-done.2), custom_call_target="tpu_custom_call" | custom-call | flops 1 | bytes 1 | tf_op jit(solution)/shard_map/pallas_call | solution.py:164
  28.2 4.4 %collective-permute-start.3 = (bf16[2560,128]{1,0:T(8,128)(2,1)S(1)}, bf16[2560,128]{1,0:T(8,128)(2,1)S(1)}, u32[]{:S(2)}, u32[]{:S(2)}) collective-permute-start(bf16[2560,128]{1,0:T(8,128)(2,1)S(1)} %maximum_select_fusion.1), channel_id=1, source_target_pairs={{0,4},{4,0},{8,12},{12,8},{1,5},{5,1},{9,13},{13,9},{2,6},{6,2},{1... | collective-permute-start | bytes 1966088 | tf_op jit(solution)/shard_map/ppermute | solution.py:440
  32.6 6.1 %collective-permute-done.4.refs_0_ = bf16[4608,128]{1,0:T(8,128)(2,1)S(1)} collective-permute-done((bf16[4608,128]{1,0:T(8,128)(2,1)}, bf16[4608,128]{1,0:T(8,128)(2,1)S(1)}, u32[]{:S(2)}, u32[]{:S(2)}) %collective-permute-start.4) | collective-permute-done | bytes 1179680 | tf_op jit(solution)/shard_map/ppermute | solution.py:460
  41.4 10.2 %collective-permute-done.3.refs_2_.refs_4_.refs_1_ = bf16[2560,128]{1,0:T(8,128)(2,1)S(1)} collective-permute-done((bf16[2560,128]{1,0:T(8,128)(2,1)S(1)}, bf16[2560,128]{1,0:T(8,128)(2,1)S(1)}, u32[]{:S(2)}, u32[]{:S(2)}) %collective-permute-start.3) | collective-permute-done | bytes 655392 | tf_op jit(solution)/shard_map/ppermute | solution.py:440
  53.6 3.9 %shard_map.83 = (f32[256,512]{1,0:T(8,128)S(1)}, f32[256,512]{1,0:T(8,128)S(1)}) custom-call(s32[6]{0:T(128)S(1)} %stack.49.flags_ref, bf16[512,1280]{1,0:T(8,128)(2,1)S(1)} %copy-done.14, bf16[1280,128]{1,0:T(8,128)(2,1)S(1)} %copy-done.23, bf16[1280,128]{1,0:T(8,128)(2,1)} %collective-permute-done.refs_1_, ...), custom_call_target="tpu_custom_call" | custom-call | flops 1 | bytes 1 | tf_op jit(solution)/shard_map/pallas_call | solution.py:411
  57.6 5.8 %collective-permute-start.6 = (bf16[2304,128]{1,0:T(8,128)(2,1)S(1)}, bf16[2304,128]{1,0:T(8,128)(2,1)S(1)}, u32[]{:S(2)}, u32[]{:S(2)}) collective-permute-start(bf16[2304,128]{1,0:T(8,128)(2,1)S(1)} %broadcast_select_fusion.1), channel_id=1, source_target_pairs={{0,4},{4,0},{8,12},{12,8},{1,5},{5,1},{9,13},{13,9},{2,6},{6,2},{1... | collective-permute-start | bytes 1769480 | tf_op jit(solution)/shard_map/ppermute | solution.py:440
  63.4 3.8 %shard_map.84 = (f32[64,512]{1,0:T(8,128)S(1)}, f32[64,512]{1,0:T(8,128)S(1)}) custom-call(s32[6]{0:T(128)S(1)} %stack.49.flags_ref, bf16[512,6912]{1,0:T(8,128)(2,1)S(1)} %bitcast.75, bf16[4608,128]{1,0:T(8,128)(2,1)S(1)} %copy-done.4, bf16[2560,128]{1,0:T(8,128)(2,1)S(1)} %collective-permute-done.3.refs_2_.refs_4_.refs_1_), custom_call_target="tpu_custom_call" | custom-call | flops 1 | bytes 1 | tf_op jit(solution)/shard_map/pallas_call | solution.py:164
  68.5 12.0 %collective-permute-done.10.end_ref.refs_0_.refs_1_ = bf16[4608,128]{1,0:T(8,128)(2,1)S(1)} collective-permute-done((bf16[4608,128]{1,0:T(8,128)(2,1)S(1)}, bf16[4608,128]{1,0:T(8,128)(2,1)S(1)}, u32[]{:S(2)}, u32[]{:S(2)}) %collective-permute-start.10) | collective-permute-done | bytes 1179680 | tf_op jit(solution)/shard_map/ppermute | solution.py:475
  81.4 5.2 %shard_map.86 = (f32[512,256]{1,0:T(8,128)S(1)}, bf16[512,2304]{1,0:T(8,128)(2,1)S(1)}, bf16[512,2304]{1,0:T(8,128)(2,1)S(1)}) custom-call(s32[6]{0:T(128)S(1)} %stack.49.flags_ref, bf16[512,6912]{1,0:T(8,128)(2,1)S(1)} %bitcast.75, bf16[4608,128]{1,0:T(8,128)(2,1)S(1)} %collective-permute-done.10.end_ref.refs_0_.refs_1_, ...), custom_call_target="tpu_custom_call" | custom-call | flops 1 | bytes 1 | tf_op jit(solution)/shard_map/pallas_call | solution.py:236
  97.6 3.6 %shard_map.87 = (f32[64,1664]{1,0:T(8,128)S(1)}, f32[64,1664]{1,0:T(8,128)S(1)}, f32[512,128]{1,0:T(8,128)S(1)}) custom-call(s32[6]{0:T(128)S(1)} %stack.49.flags_ref, bf16[4608,128]{1,0:T(8,128)(2,1)S(1)} %collective-permute-done.10.end_ref.refs_0_.refs_1_, bf16[4608,128]{1,0:T(8,128)(2,1)S(1)} %collective-permute-done.10.end_ref.refs_0_.refs_1_, ...), custom_call_target="tpu_custom_call" | custom-call | flops 1 | bytes 1 | tf_op jit(solution)/shard_map/pallas_call | solution.py:328
  105.4 2.5 %collective-permute-done.21.refs_0_.refs_4_ = bf16[2304,128]{1,0:T(8,128)(2,1)S(1)} collective-permute-done((bf16[2304,128]{1,0:T(8,128)(2,1)}, bf16[2304,128]{1,0:T(8,128)(2,1)S(1)}, u32[]{:S(2)}, u32[]{:S(2)}) %collective-permute-start.21) | collective-permute-done | bytes 589856 | tf_op jit(solution)/shard_map/ppermute | solution.py:480
  108.0 3.6 %shard_map.88 = (f32[64,896]{1,0:T(8,128)S(1)}, f32[64,896]{1,0:T(8,128)S(1)}) custom-call(s32[6]{0:T(128)S(1)} %stack.49.flags_ref, bf16[2304,128]{1,0:T(8,128)(2,1)S(1)} %collective-permute-done.21.refs_0_.refs_4_, bf16[6912,128]{1,0:T(8,128)(2,1)S(1)} %copy-done.2, bf16[2304,128]{1,0:T(8,128)(2,1)S(1)} %copy-done.9, ...), custom_call_target="tpu_custom_call" | custom-call | flops 1 | bytes 1 | tf_op jit(solution)/shard_map/pallas_call | solution.py:328
  115.6 3.9 %collective-permute-done.18 = bf16[128,512]{1,0:T(8,128)(2,1)S(1)} collective-permute-done((bf16[128,512]{1,0:T(8,128)(2,1)S(1)}, bf16[128,512]{1,0:T(8,128)(2,1)S(1)}, u32[]{:S(2)}, u32[]{:S(2)}) %collective-permute-start.18) | collective-permute-done | bytes 131104 | tf_op jit(solution)/shard_map/ppermute | solution.py:37
  123.1 2.4 %collective-permute-done.24 = bf16[32,384]{1,0:T(8,128)(2,1)S(1)} collective-permute-done((bf16[32,384]{1,0:T(8,128)(2,1)S(1)}, bf16[32,384]{1,0:T(8,128)(2,1)S(1)}, u32[]{:S(2)}, u32[]{:S(2)}) %collective-permute-start.24) | collective-permute-done | bytes 24608 | tf_op jit(solution)/shard_map/ppermute | solution.py:557
  127.3 3.6 %collective-permute-start.27 = (bf16[4,32,512]{2,1,0:T(8,128)(2,1)S(1)}, bf16[4,32,512]{2,1,0:T(8,128)(2,1)S(1)}, u32[]{:S(2)}, u32[]{:S(2)}) collective-permute-start(bf16[4,32,512]{2,1,0:T(8,128)(2,1)S(1)} %convolution_convert_fusion), channel_id=1, source_target_pairs={{0,12},{1,13},{2,14},{3,15},{4,5},{5,4},{6,7},{7,6},{8,9},{9,8},{1... | collective-permute-start | bytes 393224 | tf_op jit(solution)/shard_map/ppermute | solution.py:568
  131.2 6.1 %collective-permute-done.27 = bf16[4,32,512]{2,1,0:T(8,128)(2,1)S(1)} collective-permute-done((bf16[4,32,512]{2,1,0:T(8,128)(2,1)S(1)}, bf16[4,32,512]{2,1,0:T(8,128)(2,1)S(1)}, u32[]{:S(2)}, u32[]{:S(2)}) %collective-permute-start.27) | collective-permute-done | bytes 131104 | tf_op jit(solution)/shard_map/ppermute | solution.py:568
  137.4 3.1 %collective-permute-done.26 = bf16[4,32,512]{2,1,0:T(8,128)(2,1)S(1)} collective-permute-done((bf16[4,32,512]{2,1,0:T(8,128)(2,1)S(1)}, bf16[4,32,512]{2,1,0:T(8,128)(2,1)S(1)}, u32[]{:S(2)}, u32[]{:S(2)}) %collective-permute-start.26) | collective-permute-done | bytes 131104 | tf_op jit(solution)/shard_map/ppermute | solution.py:569
  140.6 2.8 %fusion.3 = f32[16,64]{1,0:T(8,128)S(1)} fusion(bf16[64,32,512]{2,1,0:T(8,128)(2,1)S(1)} %copy-done.27, bf16[16,32,512]{2,1,0:T(8,128)(2,1)S(1)} %pad_maximum_fusion.1), kind=kOutput, calls=%fused_computation.10 | convolution fusion | flops 33554432 | bytes 2625536 | tf_op jit(solution)/shard_map/tea,jea->tj/dot_general | solution.py:547
  144.9 9.9 %all_to_all.5 = f32[8,2,16]{2,1,0:T(2,128)S(1)} all-to-all(f32[8,2,16]{2,1,0:T(2,128)S(1)} %copy.58), channel_id=1, replica_groups=mesh['groups'=2,'cand'=4,'eig'=2,'rep'=2] {'cand','eig'}, dimensions={0} | all-to-all | bytes 2048 | tf_op jit(solution)/shard_map/all_to_all | solution.py:585
  (187 shorter events, 40.9 us)
Async XLA Ops:
  0.0 19.3 %collective-permute-start.1 = (bf16[1280,128]{1,0:T(8,128)(2,1)}, bf16[1280,128]{1,0:T(8,128)(2,1)S(1)}, u32[]{:S(2)}, u32[]{:S(2)}) collective-permute-start(bf16[1280,128]{1,0:T(8,128)(2,1)} %refs_0_.3), channel_id=1, source_target_pairs={{0,1},{1,0},{2,3},{3,2},{4,8},{5,9},{6,10},{7,11},{8,4},{9,5},{10,... | collective-permute-start | bytes 983048 | tf_op jit(solution)/shard_map/ppermute | solution.py:450
  0.5 18.9 %collective-permute-start = (bf16[1280,128]{1,0:T(8,128)(2,1)}, bf16[1280,128]{1,0:T(8,128)(2,1)}, u32[]{:S(2)}, u32[]{:S(2)}) collective-permute-start(bf16[1280,128]{1,0:T(8,128)(2,1)} %refs_0_.3), channel_id=1, source_target_pairs={{0,4},{4,0},{8,12},{12,8},{1,5},{5,1},{9,13},{13,9},{2,6},{6,2},{1... | collective-permute-start | bytes 983048 | tf_op jit(solution)/shard_map/ppermute | solution.py:458
  7.0 31.7 %collective-permute-start.4 = (bf16[4608,128]{1,0:T(8,128)(2,1)}, bf16[4608,128]{1,0:T(8,128)(2,1)S(1)}, u32[]{:S(2)}, u32[]{:S(2)}) collective-permute-start(bf16[4608,128]{1,0:T(8,128)(2,1)} %constant_dynamic-slice_fusion), channel_id=1, source_target_pairs={{0,4},{4,0},{8,12},{12,8},{1,5},{5,1},{9,13},{13,9},{2,6},{6,2},{1... | collective-permute-start | bytes 3538952 | tf_op jit(solution)/shard_map/ppermute | solution.py:460
  8.3 31.4 %collective-permute-start.8 = (bf16[2304,128]{1,0:T(8,128)(2,1)}, bf16[2304,128]{1,0:T(8,128)(2,1)}, u32[]{:S(2)}, u32[]{:S(2)}) collective-permute-start(bf16[2304,128]{1,0:T(8,128)(2,1)} %get-tuple-element.84), channel_id=1, source_target_pairs={{0,1},{1,0},{2,3},{3,2},{4,8},{5,9},{6,10},{7,11},{8,4},{9,5},{10,... | collective-permute-start | bytes 1769480 | tf_op jit(solution)/shard_map/ppermute | solution.py:450
  19.3 8.6 %collective-permute-start.2 = (bf16[1280,128]{1,0:T(8,128)(2,1)}, bf16[1280,128]{1,0:T(8,128)(2,1)S(1)}, u32[]{:S(2)}, u32[]{:S(2)}) collective-permute-start(bf16[1280,128]{1,0:T(8,128)(2,1)} %collective-permute-done.refs_1_), channel_id=1, source_target_pairs={{0,1},{1,0},{2,3},{3,2},{4,8},{5,9},{6,10},{7,11},{8,4},{9,5},{10,... | collective-permute-start | bytes 983048 | tf_op jit(solution)/shard_map/ppermute | solution.py:450
  27.9 11.9 %collective-permute-start.9 = (bf16[2304,128]{1,0:T(8,128)(2,1)S(1)}, bf16[2304,128]{1,0:T(8,128)(2,1)S(1)}, u32[]{:S(2)}, u32[]{:S(2)}) collective-permute-start(bf16[2304,128]{1,0:T(8,128)(2,1)S(1)} %copy-done.26), channel_id=1, source_target_pairs={{0,1},{1,0},{2,3},{3,2},{4,8},{5,9},{6,10},{7,11},{8,4},{9,5},{10,... | collective-permute-start | bytes 1769480 | tf_op jit(solution)/shard_map/ppermute | solution.py:450
  28.2 23.4 %collective-permute-start.3 = (bf16[2560,128]{1,0:T(8,128)(2,1)S(1)}, bf16[2560,128]{1,0:T(8,128)(2,1)S(1)}, u32[]{:S(2)}, u32[]{:S(2)}) collective-permute-start(bf16[2560,128]{1,0:T(8,128)(2,1)S(1)} %maximum_select_fusion.1), channel_id=1, source_target_pairs={{0,4},{4,0},{8,12},{12,8},{1,5},{5,1},{9,13},{13,9},{2,6},{6,2},{1... | collective-permute-start | bytes 1966088 | tf_op jit(solution)/shard_map/ppermute | solution.py:440
  39.7 13.8 %collective-permute-start.5 = (bf16[2304,128]{1,0:T(8,128)(2,1)S(1)}, bf16[2304,128]{1,0:T(8,128)(2,1)S(1)}, u32[]{:S(2)}, u32[]{:S(2)}) collective-permute-start(bf16[2304,128]{1,0:T(8,128)(2,1)S(1)} %get-tuple-element.86), channel_id=1, source_target_pairs={{0,1},{1,0},{2,3},{3,2},{4,8},{5,9},{6,10},{7,11},{8,4},{9,5},{10,... | collective-permute-start | bytes 1769480 | tf_op jit(solution)/shard_map/ppermute | solution.py:450
  51.6 28.9 %collective-permute-start.10 = (bf16[4608,128]{1,0:T(8,128)(2,1)S(1)}, bf16[4608,128]{1,0:T(8,128)(2,1)S(1)}, u32[]{:S(2)}, u32[]{:S(2)}) collective-permute-start(bf16[4608,128]{1,0:T(8,128)(2,1)S(1)} %maximum_select_fusion), channel_id=1, source_target_pairs={{0,4},{4,0},{8,12},{12,8},{1,5},{5,1},{9,13},{13,9},{2,6},{6,2},{1... | collective-permute-start | bytes 3538952 | tf_op jit(solution)/shard_map/ppermute | solution.py:475
  53.4 14.6 %collective-permute-start.11 = (bf16[2304,128]{1,0:T(8,128)(2,1)S(1)}, bf16[2304,128]{1,0:T(8,128)(2,1)S(1)}, u32[]{:S(2)}, u32[]{:S(2)}) collective-permute-start(bf16[2304,128]{1,0:T(8,128)(2,1)S(1)} %slice.81), channel_id=1, source_target_pairs={{0,1},{1,0},{2,3},{3,2},{4,8},{5,9},{6,10},{7,11},{8,4},{9,5},{10,... | collective-permute-start | bytes 1769480 | tf_op jit(solution)/shard_map/ppermute | solution.py:450
  57.6 33.5 %collective-permute-start.6 = (bf16[2304,128]{1,0:T(8,128)(2,1)S(1)}, bf16[2304,128]{1,0:T(8,128)(2,1)S(1)}, u32[]{:S(2)}, u32[]{:S(2)}) collective-permute-start(bf16[2304,128]{1,0:T(8,128)(2,1)S(1)} %broadcast_select_fusion.1), channel_id=1, source_target_pairs={{0,4},{4,0},{8,12},{12,8},{1,5},{5,1},{9,13},{13,9},{2,6},{6,2},{1... | collective-permute-start | bytes 1769480 | tf_op jit(solution)/shard_map/ppermute | solution.py:440
  63.3 27.7 %collective-permute-start.7 = (bf16[2304,128]{1,0:T(8,128)(2,1)S(1)}, bf16[2304,128]{1,0:T(8,128)(2,1)S(1)}, u32[]{:S(2)}, u32[]{:S(2)}) collective-permute-start(bf16[2304,128]{1,0:T(8,128)(2,1)S(1)} %copy-done.29), channel_id=1, source_target_pairs={{0,1},{1,0},{2,3},{3,2},{4,8},{5,9},{6,10},{7,11},{8,4},{9,5},{10,... | collective-permute-start | bytes 1769480 | tf_op jit(solution)/shard_map/ppermute | solution.py:450
  68.0 25.8 %collective-permute-start.13 = (bf16[2304,128]{1,0:T(8,128)(2,1)}, bf16[2304,128]{1,0:T(8,128)(2,1)}, u32[]{:S(2)}, u32[]{:S(2)}) collective-permute-start(bf16[2304,128]{1,0:T(8,128)(2,1)} %get-tuple-element.63), channel_id=1, source_target_pairs={{0,1},{1,0},{2,3},{3,2},{4,8},{5,9},{6,10},{7,11},{8,4},{9,5},{10,... | collective-permute-start | bytes 1769480 | tf_op jit(solution)/shard_map/ppermute | solution.py:450
  92.0 16.0 %collective-permute-start.21 = (bf16[2304,128]{1,0:T(8,128)(2,1)}, bf16[2304,128]{1,0:T(8,128)(2,1)S(1)}, u32[]{:S(2)}, u32[]{:S(2)}) collective-permute-start(bf16[2304,128]{1,0:T(8,128)(2,1)} %broadcast_select_fusion), channel_id=1, source_target_pairs={{0,4},{4,0},{8,12},{12,8},{1,5},{5,1},{9,13},{13,9},{2,6},{6,2},{1... | collective-permute-start | bytes 1769480 | tf_op jit(solution)/shard_map/ppermute | solution.py:480
  103.1 8.6 %collective-permute-start.15 = (bf16[32,2688]{1,0:T(8,128)(2,1)S(1)}, bf16[32,2688]{1,0:T(8,128)(2,1)S(1)}, u32[]{:S(2)}, u32[]{:S(2)}) collective-permute-start(bf16[32,2688]{1,0:T(8,128)(2,1)S(1)} %add_convert_fusion), channel_id=1, source_target_pairs={{0,2},{2,0},{1,3},{3,1},{4,6},{6,4},{5,7},{7,5},{8,10},{10,8},{9,1... | collective-permute-start | bytes 516104 | tf_op jit(solution)/shard_map/ppermute | solution.py:37
  104.8 8.5 %collective-permute-start.17 = (bf16[128,512]{1,0:T(8,128)(2,1)S(1)}, bf16[128,512]{1,0:T(8,128)(2,1)S(1)}, u32[]{:S(2)}, u32[]{:S(2)}) collective-permute-start(bf16[128,512]{1,0:T(8,128)(2,1)S(1)} %add_convert_fusion.2), channel_id=1, source_target_pairs={{0,2},{2,0},{1,3},{3,1},{4,6},{6,4},{5,7},{7,5},{8,10},{10,8},{9,1... | collective-permute-start | bytes 393224 | tf_op jit(solution)/shard_map/ppermute | solution.py:37
  111.8 7.8 %collective-permute-start.20 = (bf16[32,1152]{1,0:T(8,128)(2,1)S(1)}, bf16[32,1152]{1,0:T(8,128)(2,1)S(1)}, u32[]{:S(2)}, u32[]{:S(2)}) collective-permute-start(bf16[32,1152]{1,0:T(8,128)(2,1)S(1)} %slice.85), channel_id=1, source_target_pairs={{0,4},{4,0},{8,12},{12,8},{1,5},{5,1},{9,13},{13,9},{2,6},{6,2},{1... | collective-permute-start | bytes 221192 | tf_op jit(solution)/shard_map/ppermute | solution.py:558
  113.4 6.1 %collective-permute-start.18 = (bf16[128,512]{1,0:T(8,128)(2,1)S(1)}, bf16[128,512]{1,0:T(8,128)(2,1)S(1)}, u32[]{:S(2)}, u32[]{:S(2)}) collective-permute-start(bf16[128,512]{1,0:T(8,128)(2,1)S(1)} %add_convert_fusion.1), channel_id=1, source_target_pairs={{0,2},{2,0},{1,3},{3,1},{4,6},{6,4},{5,7},{7,5},{8,10},{10,8},{9,1... | collective-permute-start | bytes 393224 | tf_op jit(solution)/shard_map/ppermute | solution.py:37
  115.0 5.1 %collective-permute-start.23 = (bf16[32,896]{1,0:T(8,128)(2,1)S(1)}, bf16[32,896]{1,0:T(8,128)(2,1)S(1)}, u32[]{:S(2)}, u32[]{:S(2)}) collective-permute-start(bf16[32,896]{1,0:T(8,128)(2,1)S(1)} %add_convert_fusion.3), channel_id=1, source_target_pairs={{0,2},{2,0},{1,3},{3,1},{4,6},{6,4},{5,7},{7,5},{8,10},{10,8},{9,1... | collective-permute-start | bytes 172040 | tf_op jit(solution)/shard_map/ppermute | solution.py:37
  121.7 3.9 %collective-permute-start.24 = (bf16[32,384]{1,0:T(8,128)(2,1)S(1)}, bf16[32,384]{1,0:T(8,128)(2,1)S(1)}, u32[]{:S(2)}, u32[]{:S(2)}) collective-permute-start(bf16[32,384]{1,0:T(8,128)(2,1)S(1)} %slice.123), channel_id=1, source_target_pairs={{0,4},{4,0},{8,12},{12,8},{1,5},{5,1},{9,13},{13,9},{2,6},{6,2},{1... | collective-permute-start | bytes 73736 | tf_op jit(solution)/shard_map/ppermute | solution.py:557
  123.0 8.2 %collective-permute-start.28 = (bf16[4,32,512]{2,1,0:T(8,128)(2,1)S(1)}, bf16[4,32,512]{2,1,0:T(8,128)(2,1)S(1)}, u32[]{:S(2)}, u32[]{:S(2)}) collective-permute-start(bf16[4,32,512]{2,1,0:T(8,128)(2,1)S(1)} %convolution_convert_fusion.3), channel_id=1, source_target_pairs={{0,1},{1,0},{2,3},{3,2},{4,8},{5,9},{6,10},{7,11},{8,4},{9,5},{10,... | collective-permute-start | bytes 393224 | tf_op jit(solution)/shard_map/ppermute | solution.py:450
  125.9 11.4 %collective-permute-start.25 = (bf16[4,32,512]{2,1,0:T(8,128)(2,1)S(1)}, bf16[4,32,512]{2,1,0:T(8,128)(2,1)S(1)}, u32[]{:S(2)}, u32[]{:S(2)}) collective-permute-start(bf16[4,32,512]{2,1,0:T(8,128)(2,1)S(1)} %convolution_convert_fusion.2), channel_id=1, source_target_pairs={{0,4},{4,0},{8,12},{12,8},{1,5},{5,1},{9,13},{13,9},{2,6},{6,2},{1... | collective-permute-start | bytes 393224 | tf_op jit(solution)/shard_map/ppermute | solution.py:570
  127.3 10.0 %collective-permute-start.27 = (bf16[4,32,512]{2,1,0:T(8,128)(2,1)S(1)}, bf16[4,32,512]{2,1,0:T(8,128)(2,1)S(1)}, u32[]{:S(2)}, u32[]{:S(2)}) collective-permute-start(bf16[4,32,512]{2,1,0:T(8,128)(2,1)S(1)} %convolution_convert_fusion), channel_id=1, source_target_pairs={{0,12},{1,13},{2,14},{3,15},{4,5},{5,4},{6,7},{7,6},{8,9},{9,8},{1... | collective-permute-start | bytes 393224 | tf_op jit(solution)/shard_map/ppermute | solution.py:568
  131.1 9.3 %collective-permute-start.26 = (bf16[4,32,512]{2,1,0:T(8,128)(2,1)S(1)}, bf16[4,32,512]{2,1,0:T(8,128)(2,1)S(1)}, u32[]{:S(2)}, u32[]{:S(2)}) collective-permute-start(bf16[4,32,512]{2,1,0:T(8,128)(2,1)S(1)} %fusion.2), channel_id=1, source_target_pairs={{0,8},{8,0},{4,12},{12,4},{1,9},{9,1},{5,13},{13,5},{2,10},{10,2},... | collective-permute-start | bytes 393224 | tf_op jit(solution)/shard_map/ppermute | solution.py:569
  (42 other events, 250.8 us)

commit v13 on v11

--- a/solution.py
+++ b/solution.py
@@ -53,14 +53,13 @@
     return keep + swap(give, "eig").astype(jnp.float32)
 
 
-def gather_rows(x):
-    other = swap(x, "eig")
-    first = lax.axis_index("eig") == 0
-    both = jnp.stack([jnp.where(first, x, other), jnp.where(first, other, x)])
-    other = swap(both, "rep")
+def all_rows(core_sum, give):
+    mine = (core_sum + swap(give, "eig").astype(jnp.float32)).astype(jnp.bfloat16)
+    other = swap(mine, "rep")
     first = lax.axis_index("rep") == 0
-    whole = jnp.stack([jnp.where(first, both, other), jnp.where(first, other, both)], axis=1)
-    return whole.reshape((-1,) + x.shape[1:])
+    mine, other = mine.reshape(2, -1, mine.shape[1]), other.reshape(2, -1, mine.shape[1])
+    whole = jnp.stack([jnp.where(first, mine, other), jnp.where(first, other, mine)], axis=1)
+    return whole.reshape(-1, whole.shape[-1])
 
 
 def split_rows(full_ref, keep_ref, give_ref, rep, columns=None):
@@ -508,8 +507,9 @@
         totals,
     )
     keep_in, give_in = after(part_in, part_c)
-    core_in = swap(give_in, "rep")
-    rot_in = gather_rows(chip_sum(*chip_parts(keep_in, core_in)).astype(jnp.bfloat16))
+    core_in = keep_in + swap(give_in, "rep")
+    give_in = core_in.astype(jnp.bfloat16)
+    rot_in = all_rows(core_in, give_in)
     rot_in = rot_in.reshape(tiles_here, TILE, 4 * cols)
     keep_b, give_b = part_b
     keep_b, give_b = chip_parts(
@@ -520,14 +520,13 @@
     sum_own, sum_a, sum_b = [sums[:, i * tok_rows : (i + 1) * tok_rows] for i in range(3)]
     sums = sums[:, 3 * tok_rows :].astype(jnp.bfloat16)
     keep_last, give_last = partner_dots(
-        after(flags, part_c),
+        after(flags, part_c, give_b, give_in),
         [(s7, 0)],
         shards,
         last_grads,
         (s7, 0, depth),
         part_c,
     )
-    keep_last, give_last = after((keep_last, give_last), give_b)
     sum_last = chip_sum(*chip_parts(keep_last, swap(give_last, "rep")))
     sum_c, sum_last = sum_last[:, :tok_rows], sum_last[:, tok_rows:].astype(jnp.bfloat16)
 
@@ -554,7 +553,7 @@
     prods_own = tile_prods(sum_own)
     prods_middle = tile_prods(sum_b)
     from_middle = middle(prods_middle)
-    last = lax.ppermute(after(sum_last, prods_own, prods_middle), "cand", SIDE)
+    last = lax.ppermute(sum_last, "cand", SIDE)
     back = lax.ppermute(sums, "cand", SIDE)
     back = jnp.where(end, back, jnp.zeros_like(back)).reshape(slim, 3, tok_rows - TILE)
     last = jnp.where(end, last, jnp.zeros_like(last)).reshape(slim, 3, TILE)
@@ -565,9 +564,10 @@
     prods_a = tile_prods(with_partner(sum_a, 0))
     prods_b = tile_prods(with_partner(sum_b, 1))
     prods_c = tile_prods(with_partner(sum_c, 2))
-    from_far = lax.ppermute(prods_c, ALL, far)
-    from_two = lax.ppermute(pick(prods_b, prods_c), "cand", TWO)
-    from_side = lax.ppermute(prods_a, "cand", SIDE)
+    to_two = pick(prods_b, prods_c)
+    from_two = lax.ppermute(to_two, "cand", TWO)
+    from_far = lax.ppermute(after(prods_c, to_two), ALL, far)
+    from_side = lax.ppermute(after(prods_a, to_two), "cand", SIDE)
     total = pair_scores(
         (prods_own, plane),
         (from_side, plane ^ 1),

time: 160 us -> 164 us (1.025)
  waiting for transfers between devices: 50.6 us -> 54.3 us
  other arithmetic: 11.2 us -> 8.68 us
  starting transfers between devices: 32.6 us -> 34.8 us
    ppermute x1, waiting for transfers between devices: 0.01 us -> 7.42 us  [line_plan(): s7 = lax.ppermute(to_s7, 'cand', SIDE)]
    ppermute x4, waiting for transfers between devices: 11.5 us -> 8.95 us  [the longest x1 6.91 us: line_plan(): from_far = lax.ppermute(after(prods_c, to_two), ALL, far)]
    ppermute x2, starting transfers between devices: 9.64 us -> 11.9 us  [side(): return lax.ppermute(pick(at_end, at_middle), 'cand', SIDE)]
    ppermute x9 -> x8, starting transfers between devices: 5.32 us -> 4.06 us  [swap(): return lax.ppermute(x, axis_name, [(0, 1), (1, 0)])]
    unnamed x78 -> x82, local copies, waits for them, and re-layouts: 18.1 us -> 19.2 us
    ppermute x9 -> x8, waiting for transfers between devices: 10.1 us -> 9.7 us  [swap(): return lax.ppermute(x, axis_name, [(0, 1), (1, 0)])]
  transfers between devices with their start and end apart: 29 -> 28, of which waited for: 12 -> 15; matrix products, arithmetic and copies ran while one was open for 11% -> 9% of each run, Pallas kernels for 17% -> 14%
where the time goes in v13:
time: 164 us
  waiting for transfers between devices  54.3 us (33%)
  starting transfers between devices  34.8 us (21%)
  Pallas kernels  26 us (16%)
  local copies, waits for them, and re-layouts  24.3 us (15%)
  blocking collectives  11 us (7%)
  other arithmetic  8.68 us (5%)
  matrix products  3.81 us (2%)
    unnamed x82, local copies, waits for them, and re-layouts  19.2 us
    ppermute x1, waiting for transfers between devices, line_plan(): s45 = lax.ppermute(after(to_s45, s3), 'cand', SIDE)  12.4 us
    ppermute x2, starting transfers between devices, side(): return lax.ppermute(pick(at_end, at_middle), 'cand', SIDE)  11.9 us
    all_to_all x1, blocking collectives, final_sum(): return jnp.sum(lax.all_to_all(blocks, ALL, 0, 0, tiled=True), axis=0)  11 us
    ppermute x2, waiting for transfers between devices, side(): return lax.ppermute(pick(at_end, at_middle), 'cand', SIDE)  11 us
    ppermute x8, waiting for transfers between devices, swap(): return lax.ppermute(x, axis_name, [(0, 1), (1, 0)])  9.7 us
    pallas_call x2, Pallas kernels, feature_dots(): pl.pallas_call(kernel, out_shape=out_shape, grid_spec=pltpu.PrefetchScala...  8.38 us
    ppermute x1, waiting for transfers between devices, line_plan(): s7 = lax.ppermute(to_s7, 'cand', SIDE)  7.42 us
  transfers between devices with their start and end apart: 28, of which 15 were waited for; matrix products, arithmetic and copies ran while one was open for 9% of the time, Pallas kernels for 14%

profile of v13, /device:TPU:0, one launch (start us, length us, event | category | flops | bytes accessed | tf_op | source)
XLA Modules:
  0.0 163.6 jit_solution(11179183595506281623)
XLA Ops:
  0.5 4.1 %collective-permute-start = (bf16[1280,128]{1,0:T(8,128)(2,1)}, bf16[1280,128]{1,0:T(8,128)(2,1)}, u32[]{:S(2)}, u32[]{:S(2)}) collective-permute-start(bf16[1280,128]{1,0:T(8,128)(2,1)} %refs_0_.3), channel_id=1, source_target_pairs={{0,4},{4,0},{8,12},{12,8},{1,5},{5,1},{9,13},{13,9},{2,6},{6,2},{1... | collective-permute-start | bytes 983048 | tf_op jit(solution)/shard_map/ppermute | solution.py:457
  4.6 2.4 %constant_dynamic-slice_fusion = bf16[4608,128]{1,0:T(8,128)(2,1)} fusion(bf16[6912,128]{1,0:T(8,128)(2,1)} %refs_1_.1, s32[]{:T(128)S(6)} %select_n.162), kind=kLoop, calls=%fused_computation.87 | loop fusion | bytes 2359300 | tf_op jit(solution)/shard_map/dynamic_slice | solution.py:456
  11.3 3.0 %copy-done = bf16[512,6912]{1,0:T(8,128)(2,1)S(1)} copy-done((bf16[512,6912]{1,0:T(8,128)(2,1)S(1)}, bf16[512,6912]{1,0:T(8,128)(2,1)}, u32[]{:S(2)}) %copy-start) | copy-done | bytes 7077912
  19.0 3.0 %copy-done.1 = bf16[512,6912]{1,0:T(8,128)(2,1)S(1)} copy-done((bf16[512,6912]{1,0:T(8,128)(2,1)S(1)}, bf16[512,6912]{1,0:T(8,128)(2,1)}, u32[]{:S(2)}) %copy-start.1) | copy-done | bytes 7077912
  22.0 4.6 %shard_map.82 = (f32[64,512]{1,0:T(8,128)S(1)}, f32[64,512]{1,0:T(8,128)S(1)}) custom-call(s32[6]{0:T(128)S(1)} %stack.36.flags_ref, bf16[512,6912]{1,0:T(8,128)(2,1)S(1)} %copy-done.1, bf16[6912,128]{1,0:T(8,128)(2,1)S(1)} %copy-done.2), custom_call_target="tpu_custom_call" | custom-call | flops 1 | bytes 1 | tf_op jit(solution)/shard_map/pallas_call | solution.py:163
  27.4 6.6 %collective-permute-start.3 = (bf16[2560,128]{1,0:T(8,128)(2,1)S(1)}, bf16[2560,128]{1,0:T(8,128)(2,1)S(1)}, u32[]{:S(2)}, u32[]{:S(2)}) collective-permute-start(bf16[2560,128]{1,0:T(8,128)(2,1)S(1)} %maximum_select_fusion.1), channel_id=1, source_target_pairs={{0,4},{4,0},{8,12},{12,8},{1,5},{5,1},{9,13},{13,9},{2,6},{6,2},{1... | collective-permute-start | bytes 1966088 | tf_op jit(solution)/shard_map/ppermute | solution.py:439
  34.0 4.7 %collective-permute-done.4.refs_0_ = bf16[4608,128]{1,0:T(8,128)(2,1)S(1)} collective-permute-done((bf16[4608,128]{1,0:T(8,128)(2,1)}, bf16[4608,128]{1,0:T(8,128)(2,1)S(1)}, u32[]{:S(2)}, u32[]{:S(2)}) %collective-permute-start.4) | collective-permute-done | bytes 1179680 | tf_op jit(solution)/shard_map/ppermute | solution.py:459
  41.3 10.3 %collective-permute-done.3.refs_2_.refs_4_.refs_1_ = bf16[2560,128]{1,0:T(8,128)(2,1)S(1)} collective-permute-done((bf16[2560,128]{1,0:T(8,128)(2,1)S(1)}, bf16[2560,128]{1,0:T(8,128)(2,1)S(1)}, u32[]{:S(2)}, u32[]{:S(2)}) %collective-permute-start.3) | collective-permute-done | bytes 655392 | tf_op jit(solution)/shard_map/ppermute | solution.py:439
  53.6 3.9 %shard_map.83 = (f32[256,512]{1,0:T(8,128)S(1)}, f32[256,512]{1,0:T(8,128)S(1)}) custom-call(s32[6]{0:T(128)S(1)} %stack.36.flags_ref, bf16[512,1280]{1,0:T(8,128)(2,1)S(1)} %copy-done.12, bf16[1280,128]{1,0:T(8,128)(2,1)S(1)} %copy-done.23, bf16[1280,128]{1,0:T(8,128)(2,1)} %collective-permute-done.refs_1_, ...), custom_call_target="tpu_custom_call" | custom-call | flops 1 | bytes 1 | tf_op jit(solution)/shard_map/pallas_call | solution.py:410
  57.7 5.3 %collective-permute-start.6 = (bf16[2304,128]{1,0:T(8,128)(2,1)S(1)}, bf16[2304,128]{1,0:T(8,128)(2,1)S(1)}, u32[]{:S(2)}, u32[]{:S(2)}) collective-permute-start(bf16[2304,128]{1,0:T(8,128)(2,1)S(1)} %broadcast_select_fusion.1), channel_id=1, source_target_pairs={{0,4},{4,0},{8,12},{12,8},{1,5},{5,1},{9,13},{13,9},{2,6},{6,2},{1... | collective-permute-start | bytes 1769480 | tf_op jit(solution)/shard_map/ppermute | solution.py:439
  63.0 3.8 %shard_map.84 = (f32[64,512]{1,0:T(8,128)S(1)}, f32[64,512]{1,0:T(8,128)S(1)}) custom-call(s32[6]{0:T(128)S(1)} %stack.36.flags_ref, bf16[512,6912]{1,0:T(8,128)(2,1)S(1)} %bitcast.66, bf16[4608,128]{1,0:T(8,128)(2,1)S(1)} %copy-done.4, bf16[2560,128]{1,0:T(8,128)(2,1)S(1)} %collective-permute-done.3.refs_2_.refs_4_.refs_1_), custom_call_target="tpu_custom_call" | custom-call | flops 1 | bytes 1 | tf_op jit(solution)/shard_map/pallas_call | solution.py:163
  68.1 12.4 %collective-permute-done.10.end_ref.refs_0_.refs_1_ = bf16[4608,128]{1,0:T(8,128)(2,1)S(1)} collective-permute-done((bf16[4608,128]{1,0:T(8,128)(2,1)S(1)}, bf16[4608,128]{1,0:T(8,128)(2,1)S(1)}, u32[]{:S(2)}, u32[]{:S(2)}) %collective-permute-start.10) | collective-permute-done | bytes 1179680 | tf_op jit(solution)/shard_map/ppermute | solution.py:474
  81.4 5.2 %shard_map.86 = (f32[512,256]{1,0:T(8,128)S(1)}, bf16[512,2304]{1,0:T(8,128)(2,1)S(1)}, bf16[512,2304]{1,0:T(8,128)(2,1)S(1)}) custom-call(s32[6]{0:T(128)S(1)} %stack.36.flags_ref, bf16[512,6912]{1,0:T(8,128)(2,1)S(1)} %bitcast.66, bf16[4608,128]{1,0:T(8,128)(2,1)S(1)} %collective-permute-done.10.end_ref.refs_0_.refs_1_, ...), custom_call_target="tpu_custom_call" | custom-call | flops 1 | bytes 1 | tf_op jit(solution)/shard_map/pallas_call | solution.py:235
  97.6 3.6 %shard_map.87 = (f32[64,1664]{1,0:T(8,128)S(1)}, f32[64,1664]{1,0:T(8,128)S(1)}, f32[512,128]{1,0:T(8,128)S(1)}) custom-call(s32[6]{0:T(128)S(1)} %stack.36.flags_ref, bf16[4608,128]{1,0:T(8,128)(2,1)S(1)} %collective-permute-done.10.end_ref.refs_0_.refs_1_, bf16[4608,128]{1,0:T(8,128)(2,1)S(1)} %collective-permute-done.10.end_ref.refs_0_.refs_1_, ...), custom_call_target="tpu_custom_call" | custom-call | flops 1 | bytes 1 | tf_op jit(solution)/shard_map/pallas_call | solution.py:327
  104.8 2.5 %collective-permute-start.20 = (bf16[2304,128]{1,0:T(8,128)(2,1)S(1)}, bf16[2304,128]{1,0:T(8,128)(2,1)S(1)}, u32[]{:S(2)}, u32[]{:S(2)}) collective-permute-start(bf16[2304,128]{1,0:T(8,128)(2,1)S(1)} %copy-done.31), channel_id=1, source_target_pairs={{0,4},{4,0},{8,12},{12,8},{1,5},{5,1},{9,13},{13,9},{2,6},{6,2},{1... | collective-permute-start | bytes 1769480 | tf_op jit(solution)/shard_map/ppermute | solution.py:479
  107.3 2.3 %collective-permute-done.15 = bf16[32,2688]{1,0:T(8,128)(2,1)S(1)} collective-permute-done((bf16[32,2688]{1,0:T(8,128)(2,1)S(1)}, bf16[32,2688]{1,0:T(8,128)(2,1)S(1)}, u32[]{:S(2)}, u32[]{:S(2)}) %collective-permute-start.15) | collective-permute-done | bytes 172064 | tf_op jit(solution)/shard_map/ppermute | solution.py:37
  109.8 2.6 %collective-permute-start.19 = (bf16[32,1152]{1,0:T(8,128)(2,1)S(1)}, bf16[32,1152]{1,0:T(8,128)(2,1)S(1)}, u32[]{:S(2)}, u32[]{:S(2)}) collective-permute-start(bf16[32,1152]{1,0:T(8,128)(2,1)S(1)} %slice.85), channel_id=1, source_target_pairs={{0,4},{4,0},{8,12},{12,8},{1,5},{5,1},{9,13},{13,9},{2,6},{6,2},{1... | collective-permute-start | bytes 221192 | tf_op jit(solution)/shard_map/ppermute | solution.py:557
  114.0 7.4 %collective-permute-done.20.refs_0_.refs_4_ = bf16[2304,128]{1,0:T(8,128)(2,1)S(1)} collective-permute-done((bf16[2304,128]{1,0:T(8,128)(2,1)S(1)}, bf16[2304,128]{1,0:T(8,128)(2,1)S(1)}, u32[]{:S(2)}, u32[]{:S(2)}) %collective-permute-start.20) | collective-permute-done | bytes 589856 | tf_op jit(solution)/shard_map/ppermute | solution.py:479
  121.4 3.6 %shard_map.88 = (f32[64,896]{1,0:T(8,128)S(1)}, f32[64,896]{1,0:T(8,128)S(1)}) custom-call(s32[6]{0:T(128)S(1)} %stack.36.flags_ref, bf16[2304,128]{1,0:T(8,128)(2,1)S(1)} %collective-permute-done.20.refs_0_.refs_4_, bf16[6912,128]{1,0:T(8,128)(2,1)S(1)} %copy-done.2, bf16[2304,128]{1,0:T(8,128)(2,1)S(1)} %copy-done.9, ...), custom_call_target="tpu_custom_call" | custom-call | flops 1 | bytes 1 | tf_op jit(solution)/shard_map/pallas_call | solution.py:327
  127.4 3.5 %collective-permute-done.22 = bf16[32,896]{1,0:T(8,128)(2,1)S(1)} collective-permute-done((bf16[32,896]{1,0:T(8,128)(2,1)S(1)}, bf16[32,896]{1,0:T(8,128)(2,1)S(1)}, u32[]{:S(2)}, u32[]{:S(2)}) %collective-permute-start.22) | collective-permute-done | bytes 57376 | tf_op jit(solution)/shard_map/ppermute | solution.py:37
  135.7 2.5 %collective-permute-start.25 = (bf16[4,32,512]{2,1,0:T(8,128)(2,1)S(1)}, bf16[4,32,512]{2,1,0:T(8,128)(2,1)S(1)}, u32[]{:S(2)}, u32[]{:S(2)}) collective-permute-start(bf16[4,32,512]{2,1,0:T(8,128)(2,1)S(1)} %fusion.2), channel_id=1, source_target_pairs={{0,8},{8,0},{4,12},{12,4},{1,9},{9,1},{5,13},{13,5},{2,10},{10,2},... | collective-permute-start | bytes 393224 | tf_op jit(solution)/shard_map/ppermute | solution.py:568
  141.1 6.9 %collective-permute-done.26 = bf16[4,32,512]{2,1,0:T(8,128)(2,1)S(1)} collective-permute-done((bf16[4,32,512]{2,1,0:T(8,128)(2,1)S(1)}, bf16[4,32,512]{2,1,0:T(8,128)(2,1)S(1)}, u32[]{:S(2)}, u32[]{:S(2)}) %collective-permute-start.26) | collective-permute-done | bytes 131104 | tf_op jit(solution)/shard_map/ppermute | solution.py:569
  149.0 2.8 %fusion.3 = f32[16,64]{1,0:T(8,128)S(1)} fusion(bf16[64,32,512]{2,1,0:T(8,128)(2,1)S(1)} %copy-done.28, bf16[16,32,512]{2,1,0:T(8,128)(2,1)S(1)} %pad_maximum_fusion.1), kind=kOutput, calls=%fused_computation.10 | convolution fusion | flops 33554432 | bytes 2625536 | tf_op jit(solution)/shard_map/tea,jea->tj/dot_general | solution.py:546
  152.0 11.0 %all_to_all.5 = f32[16,2,16]{2,1,0:T(2,128)S(1)} all-to-all(f32[16,2,16]{2,1,0:T(2,128)S(1)} %copy.71), channel_id=1, replica_groups=mesh['groups'=2,'cand'=4,'eig'=2,'rep'=2] {'cand','eig','rep'}, dimensions={0} | all-to-all | bytes 4096 | tf_op jit(solution)/shard_map/all_to_all | solution.py:584
  (182 shorter events, 44.9 us)
Async XLA Ops:
  0.0 18.5 %collective-permute-start.1 = (bf16[1280,128]{1,0:T(8,128)(2,1)}, bf16[1280,128]{1,0:T(8,128)(2,1)S(1)}, u32[]{:S(2)}, u32[]{:S(2)}) collective-permute-start(bf16[1280,128]{1,0:T(8,128)(2,1)} %refs_0_.3), channel_id=1, source_target_pairs={{0,1},{1,0},{2,3},{3,2},{4,8},{5,9},{6,10},{7,11},{8,4},{9,5},{10,... | collective-permute-start | bytes 983048 | tf_op jit(solution)/shard_map/ppermute | solution.py:449
  0.5 18.0 %collective-permute-start = (bf16[1280,128]{1,0:T(8,128)(2,1)}, bf16[1280,128]{1,0:T(8,128)(2,1)}, u32[]{:S(2)}, u32[]{:S(2)}) collective-permute-start(bf16[1280,128]{1,0:T(8,128)(2,1)} %refs_0_.3), channel_id=1, source_target_pairs={{0,4},{4,0},{8,12},{12,8},{1,5},{5,1},{9,13},{13,9},{2,6},{6,2},{1... | collective-permute-start | bytes 983048 | tf_op jit(solution)/shard_map/ppermute | solution.py:457
  7.0 31.7 %collective-permute-start.4 = (bf16[4608,128]{1,0:T(8,128)(2,1)}, bf16[4608,128]{1,0:T(8,128)(2,1)S(1)}, u32[]{:S(2)}, u32[]{:S(2)}) collective-permute-start(bf16[4608,128]{1,0:T(8,128)(2,1)} %constant_dynamic-slice_fusion), channel_id=1, source_target_pairs={{0,4},{4,0},{8,12},{12,8},{1,5},{5,1},{9,13},{13,9},{2,6},{6,2},{1... | collective-permute-start | bytes 3538952 | tf_op jit(solution)/shard_map/ppermute | solution.py:459
  8.3 31.4 %collective-permute-start.8 = (bf16[2304,128]{1,0:T(8,128)(2,1)}, bf16[2304,128]{1,0:T(8,128)(2,1)}, u32[]{:S(2)}, u32[]{:S(2)}) collective-permute-start(bf16[2304,128]{1,0:T(8,128)(2,1)} %get-tuple-element.88), channel_id=1, source_target_pairs={{0,1},{1,0},{2,3},{3,2},{4,8},{5,9},{6,10},{7,11},{8,4},{9,5},{10,... | collective-permute-start | bytes 1769480 | tf_op jit(solution)/shard_map/ppermute | solution.py:449
  18.5 8.7 %collective-permute-start.2 = (bf16[1280,128]{1,0:T(8,128)(2,1)}, bf16[1280,128]{1,0:T(8,128)(2,1)S(1)}, u32[]{:S(2)}, u32[]{:S(2)}) collective-permute-start(bf16[1280,128]{1,0:T(8,128)(2,1)} %collective-permute-done.refs_1_), channel_id=1, source_target_pairs={{0,1},{1,0},{2,3},{3,2},{4,8},{5,9},{6,10},{7,11},{8,4},{9,5},{10,... | collective-permute-start | bytes 983048 | tf_op jit(solution)/shard_map/ppermute | solution.py:449
  26.7 13.1 %collective-permute-start.9 = (bf16[2304,128]{1,0:T(8,128)(2,1)S(1)}, bf16[2304,128]{1,0:T(8,128)(2,1)S(1)}, u32[]{:S(2)}, u32[]{:S(2)}) collective-permute-start(bf16[2304,128]{1,0:T(8,128)(2,1)S(1)} %copy-done.26), channel_id=1, source_target_pairs={{0,1},{1,0},{2,3},{3,2},{4,8},{5,9},{6,10},{7,11},{8,4},{9,5},{10,... | collective-permute-start | bytes 1769480 | tf_op jit(solution)/shard_map/ppermute | solution.py:449
  27.4 24.2 %collective-permute-start.3 = (bf16[2560,128]{1,0:T(8,128)(2,1)S(1)}, bf16[2560,128]{1,0:T(8,128)(2,1)S(1)}, u32[]{:S(2)}, u32[]{:S(2)}) collective-permute-start(bf16[2560,128]{1,0:T(8,128)(2,1)S(1)} %maximum_select_fusion.1), channel_id=1, source_target_pairs={{0,4},{4,0},{8,12},{12,8},{1,5},{5,1},{9,13},{13,9},{2,6},{6,2},{1... | collective-permute-start | bytes 1966088 | tf_op jit(solution)/shard_map/ppermute | solution.py:439
  39.7 13.9 %collective-permute-start.5 = (bf16[2304,128]{1,0:T(8,128)(2,1)S(1)}, bf16[2304,128]{1,0:T(8,128)(2,1)S(1)}, u32[]{:S(2)}, u32[]{:S(2)}) collective-permute-start(bf16[2304,128]{1,0:T(8,128)(2,1)S(1)} %get-tuple-element.90), channel_id=1, source_target_pairs={{0,1},{1,0},{2,3},{3,2},{4,8},{5,9},{6,10},{7,11},{8,4},{9,5},{10,... | collective-permute-start | bytes 1769480 | tf_op jit(solution)/shard_map/ppermute | solution.py:449
  51.6 28.9 %collective-permute-start.10 = (bf16[4608,128]{1,0:T(8,128)(2,1)S(1)}, bf16[4608,128]{1,0:T(8,128)(2,1)S(1)}, u32[]{:S(2)}, u32[]{:S(2)}) collective-permute-start(bf16[4608,128]{1,0:T(8,128)(2,1)S(1)} %maximum_select_fusion), channel_id=1, source_target_pairs={{0,4},{4,0},{8,12},{12,8},{1,5},{5,1},{9,13},{13,9},{2,6},{6,2},{1... | collective-permute-start | bytes 3538952 | tf_op jit(solution)/shard_map/ppermute | solution.py:474
  53.5 14.1 %collective-permute-start.11 = (bf16[2304,128]{1,0:T(8,128)(2,1)S(1)}, bf16[2304,128]{1,0:T(8,128)(2,1)S(1)}, u32[]{:S(2)}, u32[]{:S(2)}) collective-permute-start(bf16[2304,128]{1,0:T(8,128)(2,1)S(1)} %slice.81), channel_id=1, source_target_pairs={{0,1},{1,0},{2,3},{3,2},{4,8},{5,9},{6,10},{7,11},{8,4},{9,5},{10,... | collective-permute-start | bytes 1769480 | tf_op jit(solution)/shard_map/ppermute | solution.py:449
  57.7 33.4 %collective-permute-start.6 = (bf16[2304,128]{1,0:T(8,128)(2,1)S(1)}, bf16[2304,128]{1,0:T(8,128)(2,1)S(1)}, u32[]{:S(2)}, u32[]{:S(2)}) collective-permute-start(bf16[2304,128]{1,0:T(8,128)(2,1)S(1)} %broadcast_select_fusion.1), channel_id=1, source_target_pairs={{0,4},{4,0},{8,12},{12,8},{1,5},{5,1},{9,13},{13,9},{2,6},{6,2},{1... | collective-permute-start | bytes 1769480 | tf_op jit(solution)/shard_map/ppermute | solution.py:439
  62.9 28.1 %collective-permute-start.7 = (bf16[2304,128]{1,0:T(8,128)(2,1)S(1)}, bf16[2304,128]{1,0:T(8,128)(2,1)S(1)}, u32[]{:S(2)}, u32[]{:S(2)}) collective-permute-start(bf16[2304,128]{1,0:T(8,128)(2,1)S(1)} %copy-done.30), channel_id=1, source_target_pairs={{0,1},{1,0},{2,3},{3,2},{4,8},{5,9},{6,10},{7,11},{8,4},{9,5},{10,... | collective-permute-start | bytes 1769480 | tf_op jit(solution)/shard_map/ppermute | solution.py:449
  67.6 26.1 %collective-permute-start.13 = (bf16[2304,128]{1,0:T(8,128)(2,1)}, bf16[2304,128]{1,0:T(8,128)(2,1)}, u32[]{:S(2)}, u32[]{:S(2)}) collective-permute-start(bf16[2304,128]{1,0:T(8,128)(2,1)} %get-tuple-element.64), channel_id=1, source_target_pairs={{0,1},{1,0},{2,3},{3,2},{4,8},{5,9},{6,10},{7,11},{8,4},{9,5},{10,... | collective-permute-start | bytes 1769480 | tf_op jit(solution)/shard_map/ppermute | solution.py:449
  91.9 1.9 %collective-permute-start.12 = (f32[64,1024]{1,0:T(8,128)}, f32[64,1024]{1,0:T(8,128)}, u32[]{:S(2)}, u32[]{:S(2)}) collective-permute-start(f32[64,1024]{1,0:T(8,128)} %get-tuple-element.62), channel_id=1, source_target_pairs={{0,1},{1,0},{2,3},{3,2},{4,5},{5,4},{6,7},{7,6},{8,9},{9,8},{10,11... | collective-permute-start | bytes 786440 | tf_op jit(solution)/shard_map/ppermute | solution.py:37
  103.1 6.5 %collective-permute-start.15 = (bf16[32,2688]{1,0:T(8,128)(2,1)S(1)}, bf16[32,2688]{1,0:T(8,128)(2,1)S(1)}, u32[]{:S(2)}, u32[]{:S(2)}) collective-permute-start(bf16[32,2688]{1,0:T(8,128)(2,1)S(1)} %add_convert_fusion.1), channel_id=1, source_target_pairs={{0,2},{2,0},{1,3},{3,1},{4,6},{6,4},{5,7},{7,5},{8,10},{10,8},{9,1... | collective-permute-start | bytes 516104 | tf_op jit(solution)/shard_map/ppermute | solution.py:37
  104.8 16.7 %collective-permute-start.20 = (bf16[2304,128]{1,0:T(8,128)(2,1)S(1)}, bf16[2304,128]{1,0:T(8,128)(2,1)S(1)}, u32[]{:S(2)}, u32[]{:S(2)}) collective-permute-start(bf16[2304,128]{1,0:T(8,128)(2,1)S(1)} %copy-done.31), channel_id=1, source_target_pairs={{0,4},{4,0},{8,12},{12,8},{1,5},{5,1},{9,13},{13,9},{2,6},{6,2},{1... | collective-permute-start | bytes 1769480 | tf_op jit(solution)/shard_map/ppermute | solution.py:479
  107.3 5.0 %collective-permute-start.16 = (f32[256,512]{1,0:T(8,128)S(1)}, f32[256,512]{1,0:T(8,128)S(1)}, u32[]{:S(2)}, u32[]{:S(2)}) collective-permute-start(f32[256,512]{1,0:T(8,128)S(1)} %copy-done.25), channel_id=1, source_target_pairs={{0,1},{1,0},{2,3},{3,2},{4,5},{5,4},{6,7},{7,6},{8,9},{9,8},{10,11... | collective-permute-start | bytes 1572872 | tf_op jit(solution)/shard_map/ppermute | solution.py:37
  109.8 15.4 %collective-permute-start.19 = (bf16[32,1152]{1,0:T(8,128)(2,1)S(1)}, bf16[32,1152]{1,0:T(8,128)(2,1)S(1)}, u32[]{:S(2)}, u32[]{:S(2)}) collective-permute-start(bf16[32,1152]{1,0:T(8,128)(2,1)S(1)} %slice.85), channel_id=1, source_target_pairs={{0,4},{4,0},{8,12},{12,8},{1,5},{5,1},{9,13},{13,9},{2,6},{6,2},{1... | collective-permute-start | bytes 221192 | tf_op jit(solution)/shard_map/ppermute | solution.py:557
  112.5 20.1 %collective-permute-start.17 = (bf16[256,512]{1,0:T(8,128)(2,1)S(1)}, bf16[256,512]{1,0:T(8,128)(2,1)}, u32[]{:S(2)}, u32[]{:S(2)}) collective-permute-start(bf16[256,512]{1,0:T(8,128)(2,1)S(1)} %get-tuple-element.84), channel_id=1, source_target_pairs={{0,2},{2,0},{1,3},{3,1},{4,6},{6,4},{5,7},{7,5},{8,10},{10,8},{9,1... | collective-permute-start | bytes 786440 | tf_op jit(solution)/shard_map/ppermute | solution.py:37
  126.7 4.2 %collective-permute-start.22 = (bf16[32,896]{1,0:T(8,128)(2,1)S(1)}, bf16[32,896]{1,0:T(8,128)(2,1)S(1)}, u32[]{:S(2)}, u32[]{:S(2)}) collective-permute-start(bf16[32,896]{1,0:T(8,128)(2,1)S(1)} %add_convert_fusion.2), channel_id=1, source_target_pairs={{0,2},{2,0},{1,3},{3,1},{4,6},{6,4},{5,7},{7,5},{8,10},{10,8},{9,1... | collective-permute-start | bytes 172040 | tf_op jit(solution)/shard_map/ppermute | solution.py:37
  130.9 3.9 %collective-permute-start.23 = (bf16[32,384]{1,0:T(8,128)(2,1)S(1)}, bf16[32,384]{1,0:T(8,128)(2,1)S(1)}, u32[]{:S(2)}, u32[]{:S(2)}) collective-permute-start(bf16[32,384]{1,0:T(8,128)(2,1)S(1)} %slice.123), channel_id=1, source_target_pairs={{0,4},{4,0},{8,12},{12,8},{1,5},{5,1},{9,13},{13,9},{2,6},{6,2},{1... | collective-permute-start | bytes 73736 | tf_op jit(solution)/shard_map/ppermute | solution.py:556
  135.7 13.2 %collective-permute-start.25 = (bf16[4,32,512]{2,1,0:T(8,128)(2,1)S(1)}, bf16[4,32,512]{2,1,0:T(8,128)(2,1)S(1)}, u32[]{:S(2)}, u32[]{:S(2)}) collective-permute-start(bf16[4,32,512]{2,1,0:T(8,128)(2,1)S(1)} %fusion.2), channel_id=1, source_target_pairs={{0,8},{8,0},{4,12},{12,4},{1,9},{9,1},{5,13},{13,5},{2,10},{10,2},... | collective-permute-start | bytes 393224 | tf_op jit(solution)/shard_map/ppermute | solution.py:568
  138.4 10.5 %collective-permute-start.24 = (bf16[4,32,512]{2,1,0:T(8,128)(2,1)S(1)}, bf16[4,32,512]{2,1,0:T(8,128)(2,1)S(1)}, u32[]{:S(2)}, u32[]{:S(2)}) collective-permute-start(bf16[4,32,512]{2,1,0:T(8,128)(2,1)S(1)} %convolution_convert_fusion.3), channel_id=1, source_target_pairs={{0,4},{4,0},{8,12},{12,8},{1,5},{5,1},{9,13},{13,9},{2,6},{6,2},{1... | collective-permute-start | bytes 393224 | tf_op jit(solution)/shard_map/ppermute | solution.py:570
  139.8 8.2 %collective-permute-start.26 = (bf16[4,32,512]{2,1,0:T(8,128)(2,1)S(1)}, bf16[4,32,512]{2,1,0:T(8,128)(2,1)S(1)}, u32[]{:S(2)}, u32[]{:S(2)}) collective-permute-start(bf16[4,32,512]{2,1,0:T(8,128)(2,1)S(1)} %convolution_convert_fusion.1), channel_id=1, source_target_pairs={{0,12},{1,13},{2,14},{3,15},{4,5},{5,4},{6,7},{7,6},{8,9},{9,8},{1... | collective-permute-start | bytes 393224 | tf_op jit(solution)/shard_map/ppermute | solution.py:569
  (42 other events, 270.4 us)

commit v14 on v13

--- a/solution.py
+++ b/solution.py
@@ -553,7 +553,7 @@
     prods_own = tile_prods(sum_own)
     prods_middle = tile_prods(sum_b)
     from_middle = middle(prods_middle)
-    last = lax.ppermute(sum_last, "cand", SIDE)
+    last = lax.ppermute(after(sum_last, rot_in), "cand", SIDE)
     back = lax.ppermute(sums, "cand", SIDE)
     back = jnp.where(end, back, jnp.zeros_like(back)).reshape(slim, 3, tok_rows - TILE)
     last = jnp.where(end, last, jnp.zeros_like(last)).reshape(slim, 3, TILE)

time: 164 us -> 151 us (0.921)
  waiting for transfers between devices: 54.3 us -> 43.8 us
  starting transfers between devices: 34.8 us -> 32.3 us
    ppermute x8, waiting for transfers between devices: 9.7 us -> 1.89 us  [swap(): return lax.ppermute(x, axis_name, [(0, 1), (1, 0)])]
    ppermute x1, waiting for transfers between devices: 7.42 us -> 2.55 us  [line_plan(): s7 = lax.ppermute(to_s7, 'cand', SIDE)]
    ppermute x2, starting transfers between devices: 11.9 us -> 10.1 us  [side(): return lax.ppermute(pick(at_end, at_middle), 'cand', SIDE)]
    unnamed x82 -> x78, local copies, waits for them, and re-layouts: 19.2 us -> 18.1 us
  transfers between devices with their start and end apart: 28 -> 28, of which waited for: 15 -> 13; matrix products, arithmetic and copies ran while one was open for 9% -> 10% of each run, Pallas kernels for 14% -> 17%
where the time goes in v14:
time: 151 us
  waiting for transfers between devices  43.8 us (29%)
  starting transfers between devices  32.3 us (21%)
  Pallas kernels  26 us (17%)
  local copies, waits for them, and re-layouts  23.3 us (15%)
  blocking collectives  11.5 us (8%)
  other arithmetic  9.27 us (6%)
  matrix products  3.8 us (3%)
    unnamed x78, local copies, waits for them, and re-layouts  18.1 us
    ppermute x1, waiting for transfers between devices, line_plan(): s45 = lax.ppermute(after(to_s45, s3), 'cand', SIDE)  12.1 us
    all_to_all x1, blocking collectives, final_sum(): return jnp.sum(lax.all_to_all(blocks, ALL, 0, 0, tiled=True), axis=0)  11.5 us
    ppermute x2, waiting for transfers between devices, side(): return lax.ppermute(pick(at_end, at_middle), 'cand', SIDE)  11 us
    ppermute x2, starting transfers between devices, side(): return lax.ppermute(pick(at_end, at_middle), 'cand', SIDE)  10.1 us
    pallas_call x2, Pallas kernels, feature_dots(): pl.pallas_call(kernel, out_shape=out_shape, grid_spec=pltpu.PrefetchScala...  8.38 us
    pallas_call x2, Pallas kernels, partner_dots(): pl.pallas_call(kernel, out_shape=out_shape, grid_spec=pltpu.PrefetchScala...  7.21 us
    ppermute x1, waiting for transfers between devices, line_plan(): from_far = lax.ppermute(after(prods_c, to_two), ALL, far)  6.9 us
  transfers between devices with their start and end apart: 28, of which 13 were waited for; matrix products, arithmetic and copies ran while one was open for 10% of the time, Pallas kernels for 17%

profile of v14, /device:TPU:0, one launch (start us, length us, event | category | flops | bytes accessed | tf_op | source)
XLA Modules:
  0.0 150.6 jit_solution(15532762803534088764)
XLA Ops:
  0.5 4.1 %collective-permute-start = (bf16[1280,128]{1,0:T(8,128)(2,1)}, bf16[1280,128]{1,0:T(8,128)(2,1)}, u32[]{:S(2)}, u32[]{:S(2)}) collective-permute-start(bf16[1280,128]{1,0:T(8,128)(2,1)} %refs_0_.3), channel_id=1, source_target_pairs={{0,4},{4,0},{8,12},{12,8},{1,5},{5,1},{9,13},{13,9},{2,6},{6,2},{1... | collective-permute-start | bytes 983048 | tf_op jit(solution)/shard_map/ppermute | solution.py:457
  4.6 2.4 %constant_dynamic-slice_fusion = bf16[4608,128]{1,0:T(8,128)(2,1)} fusion(bf16[6912,128]{1,0:T(8,128)(2,1)} %refs_1_.1, s32[]{:T(128)S(6)} %select_n.162), kind=kLoop, calls=%fused_computation.87 | loop fusion | bytes 2359300 | tf_op jit(solution)/shard_map/dynamic_slice | solution.py:456
  8.3 3.5 %divide_convert_fusion = bf16[64,32,512]{2,1,0:T(8,128)(2,1)} fusion(bf16[64,32,512]{2,1,0:T(8,128)(2,1)} %param.13, f32[32,512]{1,0:T(8,128)S(1)} %broadcast_add_fusion), kind=kLoop, calls=%fused_computation | loop fusion | flops 3145728 | bytes 4259840 | tf_op jit(solution)/shard_map/convert_element_type | solution.py:467
  11.9 3.0 %copy-done = bf16[512,6912]{1,0:T(8,128)(2,1)S(1)} copy-done((bf16[512,6912]{1,0:T(8,128)(2,1)S(1)}, bf16[512,6912]{1,0:T(8,128)(2,1)}, u32[]{:S(2)}) %copy-start) | copy-done | bytes 7077912
  20.2 3.0 %copy-done.1 = bf16[512,6912]{1,0:T(8,128)(2,1)S(1)} copy-done((bf16[512,6912]{1,0:T(8,128)(2,1)S(1)}, bf16[512,6912]{1,0:T(8,128)(2,1)}, u32[]{:S(2)}) %copy-start.1) | copy-done | bytes 7077912
  23.2 4.6 %shard_map.82 = (f32[64,512]{1,0:T(8,128)S(1)}, f32[64,512]{1,0:T(8,128)S(1)}) custom-call(s32[6]{0:T(128)S(1)} %stack.36.flags_ref, bf16[512,6912]{1,0:T(8,128)(2,1)S(1)} %copy-done.1, bf16[6912,128]{1,0:T(8,128)(2,1)S(1)} %copy-done.2), custom_call_target="tpu_custom_call" | custom-call | flops 1 | bytes 1 | tf_op jit(solution)/shard_map/pallas_call | solution.py:163
  28.1 4.5 %collective-permute-start.3 = (bf16[2560,128]{1,0:T(8,128)(2,1)S(1)}, bf16[2560,128]{1,0:T(8,128)(2,1)S(1)}, u32[]{:S(2)}, u32[]{:S(2)}) collective-permute-start(bf16[2560,128]{1,0:T(8,128)(2,1)S(1)} %maximum_select_fusion.1), channel_id=1, source_target_pairs={{0,4},{4,0},{8,12},{12,8},{1,5},{5,1},{9,13},{13,9},{2,6},{6,2},{1... | collective-permute-start | bytes 1966088 | tf_op jit(solution)/shard_map/ppermute | solution.py:439
  32.6 6.1 %collective-permute-done.4.refs_0_ = bf16[4608,128]{1,0:T(8,128)(2,1)S(1)} collective-permute-done((bf16[4608,128]{1,0:T(8,128)(2,1)}, bf16[4608,128]{1,0:T(8,128)(2,1)S(1)}, u32[]{:S(2)}, u32[]{:S(2)}) %collective-permute-start.4) | collective-permute-done | bytes 1179680 | tf_op jit(solution)/shard_map/ppermute | solution.py:459
  41.3 10.3 %collective-permute-done.3.refs_2_.refs_4_.refs_1_ = bf16[2560,128]{1,0:T(8,128)(2,1)S(1)} collective-permute-done((bf16[2560,128]{1,0:T(8,128)(2,1)S(1)}, bf16[2560,128]{1,0:T(8,128)(2,1)S(1)}, u32[]{:S(2)}, u32[]{:S(2)}) %collective-permute-start.3) | collective-permute-done | bytes 655392 | tf_op jit(solution)/shard_map/ppermute | solution.py:439
  51.6 1.7 %collective-permute-start.10 = (bf16[4608,128]{1,0:T(8,128)(2,1)S(1)}, bf16[4608,128]{1,0:T(8,128)(2,1)S(1)}, u32[]{:S(2)}, u32[]{:S(2)}) collective-permute-start(bf16[4608,128]{1,0:T(8,128)(2,1)S(1)} %maximum_select_fusion), channel_id=1, source_target_pairs={{0,4},{4,0},{8,12},{12,8},{1,5},{5,1},{9,13},{13,9},{2,6},{6,2},{1... | collective-permute-start | bytes 3538952 | tf_op jit(solution)/shard_map/ppermute | solution.py:474
  53.6 3.9 %shard_map.83 = (f32[256,512]{1,0:T(8,128)S(1)}, f32[256,512]{1,0:T(8,128)S(1)}) custom-call(s32[6]{0:T(128)S(1)} %stack.36.flags_ref, bf16[512,1280]{1,0:T(8,128)(2,1)S(1)} %copy-done.12, bf16[1280,128]{1,0:T(8,128)(2,1)S(1)} %copy-done.23, bf16[1280,128]{1,0:T(8,128)(2,1)} %collective-permute-done.refs_1_, ...), custom_call_target="tpu_custom_call" | custom-call | flops 1 | bytes 1 | tf_op jit(solution)/shard_map/pallas_call | solution.py:410
  57.6 5.7 %collective-permute-start.6 = (bf16[2304,128]{1,0:T(8,128)(2,1)S(1)}, bf16[2304,128]{1,0:T(8,128)(2,1)S(1)}, u32[]{:S(2)}, u32[]{:S(2)}) collective-permute-start(bf16[2304,128]{1,0:T(8,128)(2,1)S(1)} %broadcast_select_fusion.1), channel_id=1, source_target_pairs={{0,4},{4,0},{8,12},{12,8},{1,5},{5,1},{9,13},{13,9},{2,6},{6,2},{1... | collective-permute-start | bytes 1769480 | tf_op jit(solution)/shard_map/ppermute | solution.py:439
  63.3 3.8 %shard_map.84 = (f32[64,512]{1,0:T(8,128)S(1)}, f32[64,512]{1,0:T(8,128)S(1)}) custom-call(s32[6]{0:T(128)S(1)} %stack.36.flags_ref, bf16[512,6912]{1,0:T(8,128)(2,1)S(1)} %bitcast.66, bf16[4608,128]{1,0:T(8,128)(2,1)S(1)} %copy-done.4, bf16[2560,128]{1,0:T(8,128)(2,1)S(1)} %collective-permute-done.3.refs_2_.refs_4_.refs_1_), custom_call_target="tpu_custom_call" | custom-call | flops 1 | bytes 1 | tf_op jit(solution)/shard_map/pallas_call | solution.py:163
  68.4 12.1 %collective-permute-done.10.end_ref.refs_0_.refs_1_ = bf16[4608,128]{1,0:T(8,128)(2,1)S(1)} collective-permute-done((bf16[4608,128]{1,0:T(8,128)(2,1)S(1)}, bf16[4608,128]{1,0:T(8,128)(2,1)S(1)}, u32[]{:S(2)}, u32[]{:S(2)}) %collective-permute-start.10) | collective-permute-done | bytes 1179680 | tf_op jit(solution)/shard_map/ppermute | solution.py:474
  81.4 5.2 %shard_map.86 = (f32[512,256]{1,0:T(8,128)S(1)}, bf16[512,2304]{1,0:T(8,128)(2,1)S(1)}, bf16[512,2304]{1,0:T(8,128)(2,1)S(1)}) custom-call(s32[6]{0:T(128)S(1)} %stack.36.flags_ref, bf16[512,6912]{1,0:T(8,128)(2,1)S(1)} %bitcast.66, bf16[4608,128]{1,0:T(8,128)(2,1)S(1)} %collective-permute-done.10.end_ref.refs_0_.refs_1_, ...), custom_call_target="tpu_custom_call" | custom-call | flops 1 | bytes 1 | tf_op jit(solution)/shard_map/pallas_call | solution.py:235
  93.8 1.7 %copy-done.6 = bf16[512,2304]{1,0:T(8,128)(2,1)S(1)} copy-done((bf16[512,2304]{1,0:T(8,128)(2,1)S(1)}, bf16[512,2304]{1,0:T(8,128)(2,1)}, u32[]{:S(2)}) %copy-start.6) | copy-done | bytes 2359320
  97.6 3.6 %shard_map.87 = (f32[64,1664]{1,0:T(8,128)S(1)}, f32[64,1664]{1,0:T(8,128)S(1)}, f32[512,128]{1,0:T(8,128)S(1)}) custom-call(s32[6]{0:T(128)S(1)} %stack.36.flags_ref, bf16[4608,128]{1,0:T(8,128)(2,1)S(1)} %collective-permute-done.10.end_ref.refs_0_.refs_1_, bf16[4608,128]{1,0:T(8,128)(2,1)S(1)} %collective-permute-done.10.end_ref.refs_0_.refs_1_, ...), custom_call_target="tpu_custom_call" | custom-call | flops 1 | bytes 1 | tf_op jit(solution)/shard_map/pallas_call | solution.py:327
  105.4 2.5 %collective-permute-done.20.refs_0_.refs_4_ = bf16[2304,128]{1,0:T(8,128)(2,1)S(1)} collective-permute-done((bf16[2304,128]{1,0:T(8,128)(2,1)}, bf16[2304,128]{1,0:T(8,128)(2,1)S(1)}, u32[]{:S(2)}, u32[]{:S(2)}) %collective-permute-start.20) | collective-permute-done | bytes 589856 | tf_op jit(solution)/shard_map/ppermute | solution.py:479
  108.0 3.6 %shard_map.88 = (f32[64,896]{1,0:T(8,128)S(1)}, f32[64,896]{1,0:T(8,128)S(1)}) custom-call(s32[6]{0:T(128)S(1)} %stack.36.flags_ref, bf16[2304,128]{1,0:T(8,128)(2,1)S(1)} %collective-permute-done.20.refs_0_.refs_4_, bf16[6912,128]{1,0:T(8,128)(2,1)S(1)} %copy-done.2, bf16[2304,128]{1,0:T(8,128)(2,1)S(1)} %copy-done.9, ...), custom_call_target="tpu_custom_call" | custom-call | flops 1 | bytes 1 | tf_op jit(solution)/shard_map/pallas_call | solution.py:327
  117.7 2.7 %collective-permute-start.23 = (bf16[32,384]{1,0:T(8,128)(2,1)S(1)}, bf16[32,384]{1,0:T(8,128)(2,1)S(1)}, u32[]{:S(2)}, u32[]{:S(2)}) collective-permute-start(bf16[32,384]{1,0:T(8,128)(2,1)S(1)} %slice.123), channel_id=1, source_target_pairs={{0,4},{4,0},{8,12},{12,8},{1,5},{5,1},{9,13},{13,9},{2,6},{6,2},{1... | collective-permute-start | bytes 73736 | tf_op jit(solution)/shard_map/ppermute | solution.py:556
  122.8 2.5 %collective-permute-start.25 = (bf16[4,32,512]{2,1,0:T(8,128)(2,1)S(1)}, bf16[4,32,512]{2,1,0:T(8,128)(2,1)S(1)}, u32[]{:S(2)}, u32[]{:S(2)}) collective-permute-start(bf16[4,32,512]{2,1,0:T(8,128)(2,1)S(1)} %fusion.2), channel_id=1, source_target_pairs={{0,8},{8,0},{4,12},{12,4},{1,9},{9,1},{5,13},{13,5},{2,10},{10,2},... | collective-permute-start | bytes 393224 | tf_op jit(solution)/shard_map/ppermute | solution.py:568
  128.4 6.9 %collective-permute-done.26 = bf16[4,32,512]{2,1,0:T(8,128)(2,1)S(1)} collective-permute-done((bf16[4,32,512]{2,1,0:T(8,128)(2,1)S(1)}, bf16[4,32,512]{2,1,0:T(8,128)(2,1)S(1)}, u32[]{:S(2)}, u32[]{:S(2)}) %collective-permute-start.26) | collective-permute-done | bytes 131104 | tf_op jit(solution)/shard_map/ppermute | solution.py:569
  135.5 2.8 %fusion.3 = f32[16,64]{1,0:T(8,128)S(1)} fusion(bf16[64,32,512]{2,1,0:T(8,128)(2,1)S(1)} %copy-done.27, bf16[16,32,512]{2,1,0:T(8,128)(2,1)S(1)} %pad_maximum_fusion.1), kind=kOutput, calls=%fused_computation.10 | convolution fusion | flops 33554432 | bytes 2625536 | tf_op jit(solution)/shard_map/tea,jea->tj/dot_general | solution.py:546
  138.5 11.5 %all_to_all.5 = f32[16,2,16]{2,1,0:T(2,128)S(1)} all-to-all(f32[16,2,16]{2,1,0:T(2,128)S(1)} %copy.71), channel_id=1, replica_groups=mesh['groups'=2,'cand'=4,'eig'=2,'rep'=2] {'cand','eig','rep'}, dimensions={0} | all-to-all | bytes 4096 | tf_op jit(solution)/shard_map/all_to_all | solution.py:584
  (178 shorter events, 38.2 us)
Async XLA Ops:
  0.0 19.3 %collective-permute-start.1 = (bf16[1280,128]{1,0:T(8,128)(2,1)}, bf16[1280,128]{1,0:T(8,128)(2,1)S(1)}, u32[]{:S(2)}, u32[]{:S(2)}) collective-permute-start(bf16[1280,128]{1,0:T(8,128)(2,1)} %refs_0_.3), channel_id=1, source_target_pairs={{0,1},{1,0},{2,3},{3,2},{4,8},{5,9},{6,10},{7,11},{8,4},{9,5},{10,... | collective-permute-start | bytes 983048 | tf_op jit(solution)/shard_map/ppermute | solution.py:449
  0.5 18.8 %collective-permute-start = (bf16[1280,128]{1,0:T(8,128)(2,1)}, bf16[1280,128]{1,0:T(8,128)(2,1)}, u32[]{:S(2)}, u32[]{:S(2)}) collective-permute-start(bf16[1280,128]{1,0:T(8,128)(2,1)} %refs_0_.3), channel_id=1, source_target_pairs={{0,4},{4,0},{8,12},{12,8},{1,5},{5,1},{9,13},{13,9},{2,6},{6,2},{1... | collective-permute-start | bytes 983048 | tf_op jit(solution)/shard_map/ppermute | solution.py:457
  7.0 31.7 %collective-permute-start.4 = (bf16[4608,128]{1,0:T(8,128)(2,1)}, bf16[4608,128]{1,0:T(8,128)(2,1)S(1)}, u32[]{:S(2)}, u32[]{:S(2)}) collective-permute-start(bf16[4608,128]{1,0:T(8,128)(2,1)} %constant_dynamic-slice_fusion), channel_id=1, source_target_pairs={{0,4},{4,0},{8,12},{12,8},{1,5},{5,1},{9,13},{13,9},{2,6},{6,2},{1... | collective-permute-start | bytes 3538952 | tf_op jit(solution)/shard_map/ppermute | solution.py:459
  8.3 31.4 %collective-permute-start.8 = (bf16[2304,128]{1,0:T(8,128)(2,1)}, bf16[2304,128]{1,0:T(8,128)(2,1)}, u32[]{:S(2)}, u32[]{:S(2)}) collective-permute-start(bf16[2304,128]{1,0:T(8,128)(2,1)} %get-tuple-element.90), channel_id=1, source_target_pairs={{0,1},{1,0},{2,3},{3,2},{4,8},{5,9},{6,10},{7,11},{8,4},{9,5},{10,... | collective-permute-start | bytes 1769480 | tf_op jit(solution)/shard_map/ppermute | solution.py:449
  19.3 8.6 %collective-permute-start.2 = (bf16[1280,128]{1,0:T(8,128)(2,1)}, bf16[1280,128]{1,0:T(8,128)(2,1)S(1)}, u32[]{:S(2)}, u32[]{:S(2)}) collective-permute-start(bf16[1280,128]{1,0:T(8,128)(2,1)} %collective-permute-done.refs_1_), channel_id=1, source_target_pairs={{0,1},{1,0},{2,3},{3,2},{4,8},{5,9},{6,10},{7,11},{8,4},{9,5},{10,... | collective-permute-start | bytes 983048 | tf_op jit(solution)/shard_map/ppermute | solution.py:449
  27.8 11.9 %collective-permute-start.9 = (bf16[2304,128]{1,0:T(8,128)(2,1)S(1)}, bf16[2304,128]{1,0:T(8,128)(2,1)S(1)}, u32[]{:S(2)}, u32[]{:S(2)}) collective-permute-start(bf16[2304,128]{1,0:T(8,128)(2,1)S(1)} %copy-done.26), channel_id=1, source_target_pairs={{0,1},{1,0},{2,3},{3,2},{4,8},{5,9},{6,10},{7,11},{8,4},{9,5},{10,... | collective-permute-start | bytes 1769480 | tf_op jit(solution)/shard_map/ppermute | solution.py:449
  28.1 23.5 %collective-permute-start.3 = (bf16[2560,128]{1,0:T(8,128)(2,1)S(1)}, bf16[2560,128]{1,0:T(8,128)(2,1)S(1)}, u32[]{:S(2)}, u32[]{:S(2)}) collective-permute-start(bf16[2560,128]{1,0:T(8,128)(2,1)S(1)} %maximum_select_fusion.1), channel_id=1, source_target_pairs={{0,4},{4,0},{8,12},{12,8},{1,5},{5,1},{9,13},{13,9},{2,6},{6,2},{1... | collective-permute-start | bytes 1966088 | tf_op jit(solution)/shard_map/ppermute | solution.py:439
  39.7 13.8 %collective-permute-start.5 = (bf16[2304,128]{1,0:T(8,128)(2,1)S(1)}, bf16[2304,128]{1,0:T(8,128)(2,1)S(1)}, u32[]{:S(2)}, u32[]{:S(2)}) collective-permute-start(bf16[2304,128]{1,0:T(8,128)(2,1)S(1)} %get-tuple-element.92), channel_id=1, source_target_pairs={{0,1},{1,0},{2,3},{3,2},{4,8},{5,9},{6,10},{7,11},{8,4},{9,5},{10,... | collective-permute-start | bytes 1769480 | tf_op jit(solution)/shard_map/ppermute | solution.py:449
  51.6 28.9 %collective-permute-start.10 = (bf16[4608,128]{1,0:T(8,128)(2,1)S(1)}, bf16[4608,128]{1,0:T(8,128)(2,1)S(1)}, u32[]{:S(2)}, u32[]{:S(2)}) collective-permute-start(bf16[4608,128]{1,0:T(8,128)(2,1)S(1)} %maximum_select_fusion), channel_id=1, source_target_pairs={{0,4},{4,0},{8,12},{12,8},{1,5},{5,1},{9,13},{13,9},{2,6},{6,2},{1... | collective-permute-start | bytes 3538952 | tf_op jit(solution)/shard_map/ppermute | solution.py:474
  53.4 14.5 %collective-permute-start.11 = (bf16[2304,128]{1,0:T(8,128)(2,1)S(1)}, bf16[2304,128]{1,0:T(8,128)(2,1)S(1)}, u32[]{:S(2)}, u32[]{:S(2)}) collective-permute-start(bf16[2304,128]{1,0:T(8,128)(2,1)S(1)} %slice.81), channel_id=1, source_target_pairs={{0,1},{1,0},{2,3},{3,2},{4,8},{5,9},{6,10},{7,11},{8,4},{9,5},{10,... | collective-permute-start | bytes 1769480 | tf_op jit(solution)/shard_map/ppermute | solution.py:449
  57.6 33.5 %collective-permute-start.6 = (bf16[2304,128]{1,0:T(8,128)(2,1)S(1)}, bf16[2304,128]{1,0:T(8,128)(2,1)S(1)}, u32[]{:S(2)}, u32[]{:S(2)}) collective-permute-start(bf16[2304,128]{1,0:T(8,128)(2,1)S(1)} %broadcast_select_fusion.1), channel_id=1, source_target_pairs={{0,4},{4,0},{8,12},{12,8},{1,5},{5,1},{9,13},{13,9},{2,6},{6,2},{1... | collective-permute-start | bytes 1769480 | tf_op jit(solution)/shard_map/ppermute | solution.py:439
  63.2 27.8 %collective-permute-start.7 = (bf16[2304,128]{1,0:T(8,128)(2,1)S(1)}, bf16[2304,128]{1,0:T(8,128)(2,1)S(1)}, u32[]{:S(2)}, u32[]{:S(2)}) collective-permute-start(bf16[2304,128]{1,0:T(8,128)(2,1)S(1)} %copy-done.29), channel_id=1, source_target_pairs={{0,1},{1,0},{2,3},{3,2},{4,8},{5,9},{6,10},{7,11},{8,4},{9,5},{10,... | collective-permute-start | bytes 1769480 | tf_op jit(solution)/shard_map/ppermute | solution.py:449
  67.9 25.9 %collective-permute-start.13 = (bf16[2304,128]{1,0:T(8,128)(2,1)}, bf16[2304,128]{1,0:T(8,128)(2,1)}, u32[]{:S(2)}, u32[]{:S(2)}) collective-permute-start(bf16[2304,128]{1,0:T(8,128)(2,1)} %get-tuple-element.65), channel_id=1, source_target_pairs={{0,1},{1,0},{2,3},{3,2},{4,8},{5,9},{6,10},{7,11},{8,4},{9,5},{10,... | collective-permute-start | bytes 1769480 | tf_op jit(solution)/shard_map/ppermute | solution.py:449
  92.0 16.0 %collective-permute-start.20 = (bf16[2304,128]{1,0:T(8,128)(2,1)}, bf16[2304,128]{1,0:T(8,128)(2,1)S(1)}, u32[]{:S(2)}, u32[]{:S(2)}) collective-permute-start(bf16[2304,128]{1,0:T(8,128)(2,1)} %broadcast_select_fusion), channel_id=1, source_target_pairs={{0,4},{4,0},{8,12},{12,8},{1,5},{5,1},{9,13},{13,9},{2,6},{6,2},{1... | collective-permute-start | bytes 1769480 | tf_op jit(solution)/shard_map/ppermute | solution.py:479
  101.4 3.3 %collective-permute-start.16 = (f32[256,512]{1,0:T(8,128)S(1)}, f32[256,512]{1,0:T(8,128)S(1)}, u32[]{:S(2)}, u32[]{:S(2)}) collective-permute-start(f32[256,512]{1,0:T(8,128)S(1)} %copy-done.25), channel_id=1, source_target_pairs={{0,1},{1,0},{2,3},{3,2},{4,5},{5,4},{6,7},{7,6},{8,9},{9,8},{10,11... | collective-permute-start | bytes 1572872 | tf_op jit(solution)/shard_map/ppermute | solution.py:37
  103.1 8.5 %collective-permute-start.15 = (bf16[32,2688]{1,0:T(8,128)(2,1)S(1)}, bf16[32,2688]{1,0:T(8,128)(2,1)S(1)}, u32[]{:S(2)}, u32[]{:S(2)}) collective-permute-start(bf16[32,2688]{1,0:T(8,128)(2,1)S(1)} %add_convert_fusion.1), channel_id=1, source_target_pairs={{0,2},{2,0},{1,3},{3,1},{4,6},{6,4},{5,7},{7,5},{8,10},{10,8},{9,1... | collective-permute-start | bytes 516104 | tf_op jit(solution)/shard_map/ppermute | solution.py:37
  104.8 10.4 %collective-permute-start.17 = (bf16[256,512]{1,0:T(8,128)(2,1)S(1)}, bf16[256,512]{1,0:T(8,128)(2,1)S(1)}, u32[]{:S(2)}, u32[]{:S(2)}) collective-permute-start(bf16[256,512]{1,0:T(8,128)(2,1)S(1)} %get-tuple-element.86), channel_id=1, source_target_pairs={{0,2},{2,0},{1,3},{3,1},{4,6},{6,4},{5,7},{7,5},{8,10},{10,8},{9,1... | collective-permute-start | bytes 786440 | tf_op jit(solution)/shard_map/ppermute | solution.py:37
  111.8 4.7 %collective-permute-start.19 = (bf16[32,1152]{1,0:T(8,128)(2,1)S(1)}, bf16[32,1152]{1,0:T(8,128)(2,1)S(1)}, u32[]{:S(2)}, u32[]{:S(2)}) collective-permute-start(bf16[32,1152]{1,0:T(8,128)(2,1)S(1)} %slice.85), channel_id=1, source_target_pairs={{0,4},{4,0},{8,12},{12,8},{1,5},{5,1},{9,13},{13,9},{2,6},{6,2},{1... | collective-permute-start | bytes 221192 | tf_op jit(solution)/shard_map/ppermute | solution.py:557
  113.3 4.2 %collective-permute-start.22 = (bf16[32,896]{1,0:T(8,128)(2,1)S(1)}, bf16[32,896]{1,0:T(8,128)(2,1)S(1)}, u32[]{:S(2)}, u32[]{:S(2)}) collective-permute-start(bf16[32,896]{1,0:T(8,128)(2,1)S(1)} %add_convert_fusion.2), channel_id=1, source_target_pairs={{0,2},{2,0},{1,3},{3,1},{4,6},{6,4},{5,7},{7,5},{8,10},{10,8},{9,1... | collective-permute-start | bytes 172040 | tf_op jit(solution)/shard_map/ppermute | solution.py:37
  115.3 2.2 %collective-permute-start.18 = (bf16[256,512]{1,0:T(8,128)(2,1)S(1)}, bf16[256,512]{1,0:T(8,128)(2,1)S(1)}, u32[]{:S(2)}, u32[]{:S(2)}) collective-permute-start(bf16[256,512]{1,0:T(8,128)(2,1)S(1)} %add_convert_fusion), channel_id=1, source_target_pairs={{0,1},{1,0},{2,3},{3,2},{4,5},{5,4},{6,7},{7,6},{8,9},{9,8},{10,11... | collective-permute-start | bytes 786440 | tf_op jit(solution)/shard_map/ppermute | solution.py:37
  117.7 4.5 %collective-permute-start.23 = (bf16[32,384]{1,0:T(8,128)(2,1)S(1)}, bf16[32,384]{1,0:T(8,128)(2,1)S(1)}, u32[]{:S(2)}, u32[]{:S(2)}) collective-permute-start(bf16[32,384]{1,0:T(8,128)(2,1)S(1)} %slice.123), channel_id=1, source_target_pairs={{0,4},{4,0},{8,12},{12,8},{1,5},{5,1},{9,13},{13,9},{2,6},{6,2},{1... | collective-permute-start | bytes 73736 | tf_op jit(solution)/shard_map/ppermute | solution.py:556
  122.8 12.6 %collective-permute-start.25 = (bf16[4,32,512]{2,1,0:T(8,128)(2,1)S(1)}, bf16[4,32,512]{2,1,0:T(8,128)(2,1)S(1)}, u32[]{:S(2)}, u32[]{:S(2)}) collective-permute-start(bf16[4,32,512]{2,1,0:T(8,128)(2,1)S(1)} %fusion.2), channel_id=1, source_target_pairs={{0,8},{8,0},{4,12},{12,4},{1,9},{9,1},{5,13},{13,5},{2,10},{10,2},... | collective-permute-start | bytes 393224 | tf_op jit(solution)/shard_map/ppermute | solution.py:568
  125.5 9.9 %collective-permute-start.24 = (bf16[4,32,512]{2,1,0:T(8,128)(2,1)S(1)}, bf16[4,32,512]{2,1,0:T(8,128)(2,1)S(1)}, u32[]{:S(2)}, u32[]{:S(2)}) collective-permute-start(bf16[4,32,512]{2,1,0:T(8,128)(2,1)S(1)} %convolution_convert_fusion.3), channel_id=1, source_target_pairs={{0,4},{4,0},{8,12},{12,8},{1,5},{5,1},{9,13},{13,9},{2,6},{6,2},{1... | collective-permute-start | bytes 393224 | tf_op jit(solution)/shard_map/ppermute | solution.py:570
  127.1 8.2 %collective-permute-start.26 = (bf16[4,32,512]{2,1,0:T(8,128)(2,1)S(1)}, bf16[4,32,512]{2,1,0:T(8,128)(2,1)S(1)}, u32[]{:S(2)}, u32[]{:S(2)}) collective-permute-start(bf16[4,32,512]{2,1,0:T(8,128)(2,1)S(1)} %convolution_convert_fusion.1), channel_id=1, source_target_pairs={{0,12},{1,13},{2,14},{3,15},{4,5},{5,4},{6,7},{7,6},{8,9},{9,8},{1... | collective-permute-start | bytes 393224 | tf_op jit(solution)/shard_map/ppermute | solution.py:569
  (40 other events, 237.8 us)

commit v15 on v14

--- a/solution.py
+++ b/solution.py
@@ -471,7 +471,7 @@
     m3 = middle(after(basis_out[2 * depth :], precond, stacked, *more_stacked, *part_own))
     m5 = middle(s12[depth:])
     to_s45 = pick(stacked, jnp.concatenate([m2, m3]))
-    s45 = lax.ppermute(after(to_s45, s3), "cand", SIDE)
+    s45 = lax.ppermute(to_s45, "cand", SIDE)
     m6 = middle(s3[:depth])
     m4 = middle(after(basis_out[:depth], m5))
     s6 = side(more_stacked[0], m5)
@@ -494,7 +494,7 @@
     )
     totals, next_grads, last_grads = both_dots(after(flags, to_s7, s45, *part_a), grads, (s45, 0), ((m2, m5), (m3, m6)))
     parts = [jnp.concatenate(part, axis=1) for part in zip(part_own, part_a)]
-    keep_a, give_a = after(parts, s6, m4, totals)
+    keep_a, give_a = after(parts, m4, totals)
     core_a = swap(give_a, "rep")
 
     shards = [(basis_out, 0), (m4, 0), (m7, 0)]
@@ -553,7 +553,7 @@
     prods_own = tile_prods(sum_own)
     prods_middle = tile_prods(sum_b)
     from_middle = middle(prods_middle)
-    last = lax.ppermute(after(sum_last, rot_in), "cand", SIDE)
+    last = lax.ppermute(after(sum_last, rot_in, prods_middle), "cand", SIDE)
     back = lax.ppermute(sums, "cand", SIDE)
     back = jnp.where(end, back, jnp.zeros_like(back)).reshape(slim, 3, tok_rows - TILE)
     last = jnp.where(end, last, jnp.zeros_like(last)).reshape(slim, 3, TILE)
@@ -566,7 +566,7 @@
     prods_c = tile_prods(with_partner(sum_c, 2))
     to_two = pick(prods_b, prods_c)
     from_two = lax.ppermute(to_two, "cand", TWO)
-    from_far = lax.ppermute(after(prods_c, to_two), ALL, far)
+    from_far = lax.ppermute(after(prods_c, to_two, from_middle), ALL, far)
     from_side = lax.ppermute(after(prods_a, to_two), "cand", SIDE)
     total = pair_scores(
         (prods_own, plane),

time: 151 us -> 153 us (1.013)
  starting transfers between devices: 32.3 us -> 44.3 us
  waiting for transfers between devices: 43.8 us -> 32.9 us
    ppermute x3, starting transfers between devices: 5.1 us -> 13.5 us  [the longest x1 7.66 us: line_plan(): s45 = lax.ppermute(to_s45, 'cand', SIDE)]
    ppermute x2, waiting for transfers between devices: 11 us -> 3.48 us  [side(): return lax.ppermute(pick(at_end, at_middle), 'cand', SIDE)]
    ppermute x3, waiting for transfers between devices: 20.7 us -> 14.6 us  [the longest x1 7.66 us: line_plan(): s45 = lax.ppermute(to_s45, 'cand', SIDE)]
    ppermute x1, starting transfers between devices: 1.43 us -> 4.09 us  [line_plan(): back = lax.ppermute(sums, 'cand', SIDE)]
    ppermute x2, starting transfers between devices: 10.1 us -> 11.9 us  [side(): return lax.ppermute(pick(at_end, at_middle), 'cand', SIDE)]
  transfers between devices with their start and end apart: 28 -> 28, of which waited for: 13 -> 10; matrix products, arithmetic and copies ran while one was open for 10% -> 11% of each run, Pallas kernels for 17% -> 17%
where the time goes in v15:
time: 153 us; the launch traced here: 152 us
  starting transfers between devices  44.3 us (29%)
  waiting for transfers between devices  32.9 us (22%)
  Pallas kernels  26 us (17%)
  local copies, waits for them, and re-layouts  23.5 us (15%)
  blocking collectives  10.7 us (7%)
  other arithmetic  10.1 us (7%)
  matrix products  3.81 us (2%)
    unnamed x78, local copies, waits for them, and re-layouts  18.3 us
    ppermute x2, starting transfers between devices, side(): return lax.ppermute(pick(at_end, at_middle), 'cand', SIDE)  11.9 us
    all_to_all x1, blocking collectives, final_sum(): return jnp.sum(lax.all_to_all(blocks, ALL, 0, 0, tiled=True), axis=0)  10.7 us
    pallas_call x2, Pallas kernels, feature_dots(): pl.pallas_call(kernel, out_shape=out_shape, grid_spec=pltpu.PrefetchScala...  8.38 us
    ppermute x1, waiting for transfers between devices, line_plan(): s45 = lax.ppermute(to_s45, 'cand', SIDE)  7.66 us
    ppermute x1, starting transfers between devices, line_plan(): s45 = lax.ppermute(to_s45, 'cand', SIDE)  7.66 us
    pallas_call x2, Pallas kernels, partner_dots(): pl.pallas_call(kernel, out_shape=out_shape, grid_spec=pltpu.PrefetchScala...  7.21 us
    ppermute x1, waiting for transfers between devices, line_plan(): s12 = lax.ppermute(rows, 'cand', SIDE)  6.1 us
  transfers between devices with their start and end apart: 28, of which 10 were waited for; matrix products, arithmetic and copies ran while one was open for 11% of the time, Pallas kernels for 17%

profile of v15, /device:TPU:0, one launch (start us, length us, event | category | flops | bytes accessed | tf_op | source)
XLA Modules:
  0.0 151.9 jit_solution(8973279860095207619)
XLA Ops:
  0.5 4.1 %collective-permute-start = (bf16[1280,128]{1,0:T(8,128)(2,1)}, bf16[1280,128]{1,0:T(8,128)(2,1)}, u32[]{:S(2)}, u32[]{:S(2)}) collective-permute-start(bf16[1280,128]{1,0:T(8,128)(2,1)} %refs_0_.3), channel_id=1, source_target_pairs={{0,4},{4,0},{8,12},{12,8},{1,5},{5,1},{9,13},{13,9},{2,6},{6,2},{1... | collective-permute-start | bytes 983048 | tf_op jit(solution)/shard_map/ppermute | solution.py:457
  4.6 2.4 %constant_dynamic-slice_fusion = bf16[4608,128]{1,0:T(8,128)(2,1)} fusion(bf16[6912,128]{1,0:T(8,128)(2,1)} %refs_1_.1, s32[]{:T(128)S(6)} %select_n.162), kind=kLoop, calls=%fused_computation.87 | loop fusion | bytes 2359300 | tf_op jit(solution)/shard_map/dynamic_slice | solution.py:456
  8.3 3.5 %divide_convert_fusion = bf16[64,32,512]{2,1,0:T(8,128)(2,1)} fusion(bf16[64,32,512]{2,1,0:T(8,128)(2,1)} %param.13, f32[32,512]{1,0:T(8,128)S(1)} %broadcast_add_fusion), kind=kLoop, calls=%fused_computation | loop fusion | flops 3145728 | bytes 4259840 | tf_op jit(solution)/shard_map/convert_element_type | solution.py:467
  11.9 3.0 %copy-done = bf16[512,6912]{1,0:T(8,128)(2,1)S(1)} copy-done((bf16[512,6912]{1,0:T(8,128)(2,1)S(1)}, bf16[512,6912]{1,0:T(8,128)(2,1)}, u32[]{:S(2)}) %copy-start) | copy-done | bytes 7077912
  20.2 3.0 %copy-done.1 = bf16[512,6912]{1,0:T(8,128)(2,1)S(1)} copy-done((bf16[512,6912]{1,0:T(8,128)(2,1)S(1)}, bf16[512,6912]{1,0:T(8,128)(2,1)}, u32[]{:S(2)}) %copy-start.1) | copy-done | bytes 7077912
  23.2 4.6 %shard_map.82 = (f32[64,512]{1,0:T(8,128)S(1)}, f32[64,512]{1,0:T(8,128)S(1)}) custom-call(s32[6]{0:T(128)S(1)} %stack.36.flags_ref, bf16[512,6912]{1,0:T(8,128)(2,1)S(1)} %copy-done.1, bf16[6912,128]{1,0:T(8,128)(2,1)S(1)} %copy-done.2), custom_call_target="tpu_custom_call" | custom-call | flops 1 | bytes 1 | tf_op jit(solution)/shard_map/pallas_call | solution.py:163
  28.1 4.5 %collective-permute-start.3 = (bf16[2560,128]{1,0:T(8,128)(2,1)S(1)}, bf16[2560,128]{1,0:T(8,128)(2,1)S(1)}, u32[]{:S(2)}, u32[]{:S(2)}) collective-permute-start(bf16[2560,128]{1,0:T(8,128)(2,1)S(1)} %maximum_select_fusion.1), channel_id=1, source_target_pairs={{0,4},{4,0},{8,12},{12,8},{1,5},{5,1},{9,13},{13,9},{2,6},{6,2},{1... | collective-permute-start | bytes 1966088 | tf_op jit(solution)/shard_map/ppermute | solution.py:439
  32.6 6.1 %collective-permute-done.4.refs_0_ = bf16[4608,128]{1,0:T(8,128)(2,1)S(1)} collective-permute-done((bf16[4608,128]{1,0:T(8,128)(2,1)}, bf16[4608,128]{1,0:T(8,128)(2,1)S(1)}, u32[]{:S(2)}, u32[]{:S(2)}) %collective-permute-start.4) | collective-permute-done | bytes 1179680 | tf_op jit(solution)/shard_map/ppermute | solution.py:459
  41.5 7.7 %collective-permute-start.9 = (bf16[4608,128]{1,0:T(8,128)(2,1)S(1)}, bf16[4608,128]{1,0:T(8,128)(2,1)S(1)}, u32[]{:S(2)}, u32[]{:S(2)}) collective-permute-start(bf16[4608,128]{1,0:T(8,128)(2,1)S(1)} %maximum_select_fusion), channel_id=1, source_target_pairs={{0,4},{4,0},{8,12},{12,8},{1,5},{5,1},{9,13},{13,9},{2,6},{6,2},{1... | collective-permute-start | bytes 3538952 | tf_op jit(solution)/shard_map/ppermute | solution.py:474
  49.3 3.5 %collective-permute-done.3.refs_2_.refs_4_.refs_1_ = bf16[2560,128]{1,0:T(8,128)(2,1)S(1)} collective-permute-done((bf16[2560,128]{1,0:T(8,128)(2,1)S(1)}, bf16[2560,128]{1,0:T(8,128)(2,1)S(1)}, u32[]{:S(2)}, u32[]{:S(2)}) %collective-permute-start.3) | collective-permute-done | bytes 655392 | tf_op jit(solution)/shard_map/ppermute | solution.py:439
  52.9 3.9 %shard_map.83 = (f32[256,512]{1,0:T(8,128)S(1)}, f32[256,512]{1,0:T(8,128)S(1)}) custom-call(s32[6]{0:T(128)S(1)} %stack.36.flags_ref, bf16[512,1280]{1,0:T(8,128)(2,1)S(1)} %copy-done.12, bf16[1280,128]{1,0:T(8,128)(2,1)S(1)} %copy-done.23, bf16[1280,128]{1,0:T(8,128)(2,1)} %collective-permute-done.refs_1_, ...), custom_call_target="tpu_custom_call" | custom-call | flops 1 | bytes 1 | tf_op jit(solution)/shard_map/pallas_call | solution.py:410
  58.3 7.4 %collective-permute-start.12 = (bf16[2304,128]{1,0:T(8,128)(2,1)}, bf16[2304,128]{1,0:T(8,128)(2,1)S(1)}, u32[]{:S(2)}, u32[]{:S(2)}) collective-permute-start(bf16[2304,128]{1,0:T(8,128)(2,1)} %broadcast_select_fusion), channel_id=1, source_target_pairs={{0,4},{4,0},{8,12},{12,8},{1,5},{5,1},{9,13},{13,9},{2,6},{6,2},{1... | collective-permute-start | bytes 1769480 | tf_op jit(solution)/shard_map/ppermute | solution.py:439
  65.7 3.8 %shard_map.84 = (f32[64,512]{1,0:T(8,128)S(1)}, f32[64,512]{1,0:T(8,128)S(1)}) custom-call(s32[6]{0:T(128)S(1)} %stack.36.flags_ref, bf16[512,6912]{1,0:T(8,128)(2,1)S(1)} %bitcast.66, bf16[4608,128]{1,0:T(8,128)(2,1)S(1)} %copy-done.4, bf16[2560,128]{1,0:T(8,128)(2,1)S(1)} %collective-permute-done.3.refs_2_.refs_4_.refs_1_), custom_call_target="tpu_custom_call" | custom-call | flops 1 | bytes 1 | tf_op jit(solution)/shard_map/pallas_call | solution.py:163
  70.4 7.7 %collective-permute-done.9.end_ref.refs_0_.refs_1_ = bf16[4608,128]{1,0:T(8,128)(2,1)S(1)} collective-permute-done((bf16[4608,128]{1,0:T(8,128)(2,1)S(1)}, bf16[4608,128]{1,0:T(8,128)(2,1)S(1)}, u32[]{:S(2)}, u32[]{:S(2)}) %collective-permute-start.9) | collective-permute-done | bytes 1179680 | tf_op jit(solution)/shard_map/ppermute | solution.py:474
  79.0 5.2 %shard_map.86 = (f32[512,256]{1,0:T(8,128)S(1)}, bf16[512,2304]{1,0:T(8,128)(2,1)S(1)}, bf16[512,2304]{1,0:T(8,128)(2,1)S(1)}) custom-call(s32[6]{0:T(128)S(1)} %stack.36.flags_ref, bf16[512,6912]{1,0:T(8,128)(2,1)S(1)} %bitcast.66, bf16[4608,128]{1,0:T(8,128)(2,1)S(1)} %collective-permute-done.9.end_ref.refs_0_.refs_1_, ...), custom_call_target="tpu_custom_call" | custom-call | flops 1 | bytes 1 | tf_op jit(solution)/shard_map/pallas_call | solution.py:235
  94.9 3.6 %shard_map.87 = (f32[64,1664]{1,0:T(8,128)S(1)}, f32[64,1664]{1,0:T(8,128)S(1)}, f32[512,128]{1,0:T(8,128)S(1)}) custom-call(s32[6]{0:T(128)S(1)} %stack.36.flags_ref, bf16[4608,128]{1,0:T(8,128)(2,1)S(1)} %collective-permute-done.9.end_ref.refs_0_.refs_1_, bf16[4608,128]{1,0:T(8,128)(2,1)S(1)} %collective-permute-done.9.end_ref.refs_0_.refs_1_, ...), custom_call_target="tpu_custom_call" | custom-call | flops 1 | bytes 1 | tf_op jit(solution)/shard_map/pallas_call | solution.py:327
  102.7 2.6 %collective-permute-done.20.refs_0_.refs_4_ = bf16[2304,128]{1,0:T(8,128)(2,1)S(1)} collective-permute-done((bf16[2304,128]{1,0:T(8,128)(2,1)}, bf16[2304,128]{1,0:T(8,128)(2,1)S(1)}, u32[]{:S(2)}, u32[]{:S(2)}) %collective-permute-start.20) | collective-permute-done | bytes 589856 | tf_op jit(solution)/shard_map/ppermute | solution.py:479
  105.3 3.6 %shard_map.88 = (f32[64,896]{1,0:T(8,128)S(1)}, f32[64,896]{1,0:T(8,128)S(1)}) custom-call(s32[6]{0:T(128)S(1)} %stack.36.flags_ref, bf16[2304,128]{1,0:T(8,128)(2,1)S(1)} %collective-permute-done.20.refs_0_.refs_4_, bf16[6912,128]{1,0:T(8,128)(2,1)S(1)} %copy-done.2, bf16[2304,128]{1,0:T(8,128)(2,1)S(1)} %copy-done.9, ...), custom_call_target="tpu_custom_call" | custom-call | flops 1 | bytes 1 | tf_op jit(solution)/shard_map/pallas_call | solution.py:327
  109.1 4.1 %collective-permute-start.19 = (bf16[32,1152]{1,0:T(8,128)(2,1)S(1)}, bf16[32,1152]{1,0:T(8,128)(2,1)S(1)}, u32[]{:S(2)}, u32[]{:S(2)}) collective-permute-start(bf16[32,1152]{1,0:T(8,128)(2,1)S(1)} %slice.85), channel_id=1, source_target_pairs={{0,4},{4,0},{8,12},{12,8},{1,5},{5,1},{9,13},{13,9},{2,6},{6,2},{1... | collective-permute-start | bytes 221192 | tf_op jit(solution)/shard_map/ppermute | solution.py:557
  117.5 2.4 %collective-permute-done.22 = bf16[32,896]{1,0:T(8,128)(2,1)S(1)} collective-permute-done((bf16[32,896]{1,0:T(8,128)(2,1)S(1)}, bf16[32,896]{1,0:T(8,128)(2,1)S(1)}, u32[]{:S(2)}, u32[]{:S(2)}) %collective-permute-start.22) | collective-permute-done | bytes 57376 | tf_op jit(solution)/shard_map/ppermute | solution.py:37
  120.4 3.5 %collective-permute-start.23 = (bf16[32,384]{1,0:T(8,128)(2,1)S(1)}, bf16[32,384]{1,0:T(8,128)(2,1)S(1)}, u32[]{:S(2)}, u32[]{:S(2)}) collective-permute-start(bf16[32,384]{1,0:T(8,128)(2,1)S(1)} %slice.123), channel_id=1, source_target_pairs={{0,4},{4,0},{8,12},{12,8},{1,5},{5,1},{9,13},{13,9},{2,6},{6,2},{1... | collective-permute-start | bytes 73736 | tf_op jit(solution)/shard_map/ppermute | solution.py:556
  131.0 5.3 %collective-permute-done.27 = bf16[4,32,512]{2,1,0:T(8,128)(2,1)S(1)} collective-permute-done((bf16[4,32,512]{2,1,0:T(8,128)(2,1)S(1)}, bf16[4,32,512]{2,1,0:T(8,128)(2,1)S(1)}, u32[]{:S(2)}, u32[]{:S(2)}) %collective-permute-start.27) | collective-permute-done | bytes 131104 | tf_op jit(solution)/shard_map/ppermute | solution.py:569
  137.6 2.8 %fusion.3 = f32[16,64]{1,0:T(8,128)S(1)} fusion(bf16[64,32,512]{2,1,0:T(8,128)(2,1)S(1)} %copy-done.27, bf16[16,32,512]{2,1,0:T(8,128)(2,1)S(1)} %pad_maximum_fusion.1), kind=kOutput, calls=%fused_computation.10 | convolution fusion | flops 33554432 | bytes 2625536 | tf_op jit(solution)/shard_map/tea,jea->tj/dot_general | solution.py:546
  140.6 10.7 %all_to_all.5 = f32[16,2,16]{2,1,0:T(2,128)S(1)} all-to-all(f32[16,2,16]{2,1,0:T(2,128)S(1)} %copy.73), channel_id=1, replica_groups=mesh['groups'=2,'cand'=4,'eig'=2,'rep'=2] {'cand','eig','rep'}, dimensions={0} | all-to-all | bytes 4096 | tf_op jit(solution)/shard_map/all_to_all | solution.py:584
  (179 shorter events, 42.4 us)
Async XLA Ops:
  0.0 19.3 %collective-permute-start.1 = (bf16[1280,128]{1,0:T(8,128)(2,1)}, bf16[1280,128]{1,0:T(8,128)(2,1)S(1)}, u32[]{:S(2)}, u32[]{:S(2)}) collective-permute-start(bf16[1280,128]{1,0:T(8,128)(2,1)} %refs_0_.3), channel_id=1, source_target_pairs={{0,1},{1,0},{2,3},{3,2},{4,8},{5,9},{6,10},{7,11},{8,4},{9,5},{10,... | collective-permute-start | bytes 983048 | tf_op jit(solution)/shard_map/ppermute | solution.py:449
  0.5 18.8 %collective-permute-start = (bf16[1280,128]{1,0:T(8,128)(2,1)}, bf16[1280,128]{1,0:T(8,128)(2,1)}, u32[]{:S(2)}, u32[]{:S(2)}) collective-permute-start(bf16[1280,128]{1,0:T(8,128)(2,1)} %refs_0_.3), channel_id=1, source_target_pairs={{0,4},{4,0},{8,12},{12,8},{1,5},{5,1},{9,13},{13,9},{2,6},{6,2},{1... | collective-permute-start | bytes 983048 | tf_op jit(solution)/shard_map/ppermute | solution.py:457
  7.0 31.7 %collective-permute-start.4 = (bf16[4608,128]{1,0:T(8,128)(2,1)}, bf16[4608,128]{1,0:T(8,128)(2,1)S(1)}, u32[]{:S(2)}, u32[]{:S(2)}) collective-permute-start(bf16[4608,128]{1,0:T(8,128)(2,1)} %constant_dynamic-slice_fusion), channel_id=1, source_target_pairs={{0,4},{4,0},{8,12},{12,8},{1,5},{5,1},{9,13},{13,9},{2,6},{6,2},{1... | collective-permute-start | bytes 3538952 | tf_op jit(solution)/shard_map/ppermute | solution.py:459
  8.3 31.5 %collective-permute-start.7 = (bf16[2304,128]{1,0:T(8,128)(2,1)}, bf16[2304,128]{1,0:T(8,128)(2,1)}, u32[]{:S(2)}, u32[]{:S(2)}) collective-permute-start(bf16[2304,128]{1,0:T(8,128)(2,1)} %get-tuple-element.88), channel_id=1, source_target_pairs={{0,1},{1,0},{2,3},{3,2},{4,8},{5,9},{6,10},{7,11},{8,4},{9,5},{10,... | collective-permute-start | bytes 1769480 | tf_op jit(solution)/shard_map/ppermute | solution.py:449
  19.3 8.6 %collective-permute-start.2 = (bf16[1280,128]{1,0:T(8,128)(2,1)}, bf16[1280,128]{1,0:T(8,128)(2,1)S(1)}, u32[]{:S(2)}, u32[]{:S(2)}) collective-permute-start(bf16[1280,128]{1,0:T(8,128)(2,1)} %collective-permute-done.refs_1_), channel_id=1, source_target_pairs={{0,1},{1,0},{2,3},{3,2},{4,8},{5,9},{6,10},{7,11},{8,4},{9,5},{10,... | collective-permute-start | bytes 983048 | tf_op jit(solution)/shard_map/ppermute | solution.py:449
  27.8 11.9 %collective-permute-start.8 = (bf16[2304,128]{1,0:T(8,128)(2,1)S(1)}, bf16[2304,128]{1,0:T(8,128)(2,1)S(1)}, u32[]{:S(2)}, u32[]{:S(2)}) collective-permute-start(bf16[2304,128]{1,0:T(8,128)(2,1)S(1)} %copy-done.26), channel_id=1, source_target_pairs={{0,1},{1,0},{2,3},{3,2},{4,8},{5,9},{6,10},{7,11},{8,4},{9,5},{10,... | collective-permute-start | bytes 1769480 | tf_op jit(solution)/shard_map/ppermute | solution.py:449
  28.1 24.6 %collective-permute-start.3 = (bf16[2560,128]{1,0:T(8,128)(2,1)S(1)}, bf16[2560,128]{1,0:T(8,128)(2,1)S(1)}, u32[]{:S(2)}, u32[]{:S(2)}) collective-permute-start(bf16[2560,128]{1,0:T(8,128)(2,1)S(1)} %maximum_select_fusion.1), channel_id=1, source_target_pairs={{0,4},{4,0},{8,12},{12,8},{1,5},{5,1},{9,13},{13,9},{2,6},{6,2},{1... | collective-permute-start | bytes 1966088 | tf_op jit(solution)/shard_map/ppermute | solution.py:439
  39.7 13.2 %collective-permute-start.5 = (bf16[2304,128]{1,0:T(8,128)(2,1)S(1)}, bf16[2304,128]{1,0:T(8,128)(2,1)S(1)}, u32[]{:S(2)}, u32[]{:S(2)}) collective-permute-start(bf16[2304,128]{1,0:T(8,128)(2,1)S(1)} %get-tuple-element.90), channel_id=1, source_target_pairs={{0,1},{1,0},{2,3},{3,2},{4,8},{5,9},{6,10},{7,11},{8,4},{9,5},{10,... | collective-permute-start | bytes 1769480 | tf_op jit(solution)/shard_map/ppermute | solution.py:449
  41.5 36.5 %collective-permute-start.9 = (bf16[4608,128]{1,0:T(8,128)(2,1)S(1)}, bf16[4608,128]{1,0:T(8,128)(2,1)S(1)}, u32[]{:S(2)}, u32[]{:S(2)}) collective-permute-start(bf16[4608,128]{1,0:T(8,128)(2,1)S(1)} %maximum_select_fusion), channel_id=1, source_target_pairs={{0,4},{4,0},{8,12},{12,8},{1,5},{5,1},{9,13},{13,9},{2,6},{6,2},{1... | collective-permute-start | bytes 3538952 | tf_op jit(solution)/shard_map/ppermute | solution.py:474
  52.8 17.6 %collective-permute-start.10 = (bf16[2304,128]{1,0:T(8,128)(2,1)S(1)}, bf16[2304,128]{1,0:T(8,128)(2,1)S(1)}, u32[]{:S(2)}, u32[]{:S(2)}) collective-permute-start(bf16[2304,128]{1,0:T(8,128)(2,1)S(1)} %slice.81), channel_id=1, source_target_pairs={{0,1},{1,0},{2,3},{3,2},{4,8},{5,9},{6,10},{7,11},{8,4},{9,5},{10,... | collective-permute-start | bytes 1769480 | tf_op jit(solution)/shard_map/ppermute | solution.py:449
  56.9 31.0 %collective-permute-start.6 = (bf16[2304,128]{1,0:T(8,128)(2,1)S(1)}, bf16[2304,128]{1,0:T(8,128)(2,1)S(1)}, u32[]{:S(2)}, u32[]{:S(2)}) collective-permute-start(bf16[2304,128]{1,0:T(8,128)(2,1)S(1)} %copy-done.29), channel_id=1, source_target_pairs={{0,1},{1,0},{2,3},{3,2},{4,8},{5,9},{6,10},{7,11},{8,4},{9,5},{10,... | collective-permute-start | bytes 1769480 | tf_op jit(solution)/shard_map/ppermute | solution.py:449
  58.3 32.8 %collective-permute-start.12 = (bf16[2304,128]{1,0:T(8,128)(2,1)}, bf16[2304,128]{1,0:T(8,128)(2,1)S(1)}, u32[]{:S(2)}, u32[]{:S(2)}) collective-permute-start(bf16[2304,128]{1,0:T(8,128)(2,1)} %broadcast_select_fusion), channel_id=1, source_target_pairs={{0,4},{4,0},{8,12},{12,8},{1,5},{5,1},{9,13},{13,9},{2,6},{6,2},{1... | collective-permute-start | bytes 1769480 | tf_op jit(solution)/shard_map/ppermute | solution.py:439
  70.4 20.8 %collective-permute-start.13 = (bf16[2304,128]{1,0:T(8,128)(2,1)}, bf16[2304,128]{1,0:T(8,128)(2,1)}, u32[]{:S(2)}, u32[]{:S(2)}) collective-permute-start(bf16[2304,128]{1,0:T(8,128)(2,1)} %get-tuple-element.63), channel_id=1, source_target_pairs={{0,1},{1,0},{2,3},{3,2},{4,8},{5,9},{6,10},{7,11},{8,4},{9,5},{10,... | collective-permute-start | bytes 1769480 | tf_op jit(solution)/shard_map/ppermute | solution.py:449
  88.8 16.5 %collective-permute-start.20 = (bf16[2304,128]{1,0:T(8,128)(2,1)}, bf16[2304,128]{1,0:T(8,128)(2,1)S(1)}, u32[]{:S(2)}, u32[]{:S(2)}) collective-permute-start(bf16[2304,128]{1,0:T(8,128)(2,1)} %broadcast_select_fusion.1), channel_id=1, source_target_pairs={{0,4},{4,0},{8,12},{12,8},{1,5},{5,1},{9,13},{13,9},{2,6},{6,2},{1... | collective-permute-start | bytes 1769480 | tf_op jit(solution)/shard_map/ppermute | solution.py:479
  100.5 8.6 %collective-permute-start.15 = (bf16[32,2688]{1,0:T(8,128)(2,1)S(1)}, bf16[32,2688]{1,0:T(8,128)(2,1)S(1)}, u32[]{:S(2)}, u32[]{:S(2)}) collective-permute-start(bf16[32,2688]{1,0:T(8,128)(2,1)S(1)} %add_convert_fusion.1), channel_id=1, source_target_pairs={{0,2},{2,0},{1,3},{3,1},{4,6},{6,4},{5,7},{7,5},{8,10},{10,8},{9,1... | collective-permute-start | bytes 516104 | tf_op jit(solution)/shard_map/ppermute | solution.py:37
  102.1 15.1 %collective-permute-start.17 = (bf16[256,512]{1,0:T(8,128)(2,1)S(1)}, bf16[256,512]{1,0:T(8,128)(2,1)S(1)}, u32[]{:S(2)}, u32[]{:S(2)}) collective-permute-start(bf16[256,512]{1,0:T(8,128)(2,1)S(1)} %get-tuple-element.84), channel_id=1, source_target_pairs={{0,2},{2,0},{1,3},{3,1},{4,6},{6,4},{5,7},{7,5},{8,10},{10,8},{9,1... | collective-permute-start | bytes 786440 | tf_op jit(solution)/shard_map/ppermute | solution.py:37
  108.9 6.7 %collective-permute-start.21 = (f32[64,896]{1,0:T(8,128)S(1)}, f32[64,896]{1,0:T(8,128)S(1)}, u32[]{:S(2)}, u32[]{:S(2)}) collective-permute-start(f32[64,896]{1,0:T(8,128)S(1)} %get-tuple-element.73), channel_id=1, source_target_pairs={{0,1},{1,0},{2,3},{3,2},{4,5},{5,4},{6,7},{7,6},{8,9},{9,8},{10,11... | collective-permute-start | bytes 688136 | tf_op jit(solution)/shard_map/ppermute | solution.py:37
  109.1 6.4 %collective-permute-start.19 = (bf16[32,1152]{1,0:T(8,128)(2,1)S(1)}, bf16[32,1152]{1,0:T(8,128)(2,1)S(1)}, u32[]{:S(2)}, u32[]{:S(2)}) collective-permute-start(bf16[32,1152]{1,0:T(8,128)(2,1)S(1)} %slice.85), channel_id=1, source_target_pairs={{0,4},{4,0},{8,12},{12,8},{1,5},{5,1},{9,13},{13,9},{2,6},{6,2},{1... | collective-permute-start | bytes 221192 | tf_op jit(solution)/shard_map/ppermute | solution.py:557
  115.7 4.2 %collective-permute-start.22 = (bf16[32,896]{1,0:T(8,128)(2,1)S(1)}, bf16[32,896]{1,0:T(8,128)(2,1)S(1)}, u32[]{:S(2)}, u32[]{:S(2)}) collective-permute-start(bf16[32,896]{1,0:T(8,128)(2,1)S(1)} %add_convert_fusion.2), channel_id=1, source_target_pairs={{0,2},{2,0},{1,3},{3,1},{4,6},{6,4},{5,7},{7,5},{8,10},{10,8},{9,1... | collective-permute-start | bytes 172040 | tf_op jit(solution)/shard_map/ppermute | solution.py:37
  120.3 8.0 %collective-permute-start.26 = (bf16[4,32,512]{2,1,0:T(8,128)(2,1)S(1)}, bf16[4,32,512]{2,1,0:T(8,128)(2,1)S(1)}, u32[]{:S(2)}, u32[]{:S(2)}) collective-permute-start(bf16[4,32,512]{2,1,0:T(8,128)(2,1)S(1)} %convolution_convert_fusion.3), channel_id=1, source_target_pairs={{0,1},{1,0},{2,3},{3,2},{4,8},{5,9},{6,10},{7,11},{8,4},{9,5},{10,... | collective-permute-start | bytes 393224 | tf_op jit(solution)/shard_map/ppermute | solution.py:449
  120.4 5.3 %collective-permute-start.23 = (bf16[32,384]{1,0:T(8,128)(2,1)S(1)}, bf16[32,384]{1,0:T(8,128)(2,1)S(1)}, u32[]{:S(2)}, u32[]{:S(2)}) collective-permute-start(bf16[32,384]{1,0:T(8,128)(2,1)S(1)} %slice.123), channel_id=1, source_target_pairs={{0,4},{4,0},{8,12},{12,8},{1,5},{5,1},{9,13},{13,9},{2,6},{6,2},{1... | collective-permute-start | bytes 73736 | tf_op jit(solution)/shard_map/ppermute | solution.py:556
  126.2 11.3 %collective-permute-start.25 = (bf16[4,32,512]{2,1,0:T(8,128)(2,1)S(1)}, bf16[4,32,512]{2,1,0:T(8,128)(2,1)S(1)}, u32[]{:S(2)}, u32[]{:S(2)}) collective-permute-start(bf16[4,32,512]{2,1,0:T(8,128)(2,1)S(1)} %fusion.2), channel_id=1, source_target_pairs={{0,8},{8,0},{4,12},{12,4},{1,9},{9,1},{5,13},{13,5},{2,10},{10,2},... | collective-permute-start | bytes 393224 | tf_op jit(solution)/shard_map/ppermute | solution.py:568
  128.3 8.0 %collective-permute-start.27 = (bf16[4,32,512]{2,1,0:T(8,128)(2,1)S(1)}, bf16[4,32,512]{2,1,0:T(8,128)(2,1)S(1)}, u32[]{:S(2)}, u32[]{:S(2)}) collective-permute-start(bf16[4,32,512]{2,1,0:T(8,128)(2,1)S(1)} %convolution_convert_fusion), channel_id=1, source_target_pairs={{0,12},{1,13},{2,14},{3,15},{4,5},{5,4},{6,7},{7,6},{8,9},{9,8},{1... | collective-permute-start | bytes 393224 | tf_op jit(solution)/shard_map/ppermute | solution.py:569
  130.9 6.7 %collective-permute-start.24 = (bf16[4,32,512]{2,1,0:T(8,128)(2,1)S(1)}, bf16[4,32,512]{2,1,0:T(8,128)(2,1)S(1)}, u32[]{:S(2)}, u32[]{:S(2)}) collective-permute-start(bf16[4,32,512]{2,1,0:T(8,128)(2,1)S(1)} %convolution_convert_fusion.2), channel_id=1, source_target_pairs={{0,4},{4,0},{8,12},{12,8},{1,5},{5,1},{9,13},{13,9},{2,6},{6,2},{1... | collective-permute-start | bytes 393224 | tf_op jit(solution)/shard_map/ppermute | solution.py:570
  (40 other events, 257.2 us)

commit v16 on v15

--- a/solution.py
+++ b/solution.py
@@ -53,9 +53,7 @@
     return keep + swap(give, "eig").astype(jnp.float32)
 
 
-def all_rows(core_sum, give):
-    mine = (core_sum + swap(give, "eig").astype(jnp.float32)).astype(jnp.bfloat16)
-    other = swap(mine, "rep")
+def all_rows(mine, other):
     first = lax.axis_index("rep") == 0
     mine, other = mine.reshape(2, -1, mine.shape[1]), other.reshape(2, -1, mine.shape[1])
     whole = jnp.stack([jnp.where(first, mine, other), jnp.where(first, other, mine)], axis=1)
@@ -509,7 +507,9 @@
     keep_in, give_in = after(part_in, part_c)
     core_in = keep_in + swap(give_in, "rep")
     give_in = core_in.astype(jnp.bfloat16)
-    rot_in = all_rows(core_in, give_in)
+    rows_here = chip_sum(core_in, give_in).astype(jnp.bfloat16)
+    rows_there = swap(rows_here, "rep")
+    rot_in = all_rows(rows_here, rows_there)
     rot_in = rot_in.reshape(tiles_here, TILE, 4 * cols)
     keep_b, give_b = part_b
     keep_b, give_b = chip_parts(
@@ -527,7 +527,8 @@
         (s7, 0, depth),
         part_c,
     )
-    sum_last = chip_sum(*chip_parts(keep_last, swap(give_last, "rep")))
+    keep_last, give_last = chip_parts(keep_last, swap(give_last, "rep"))
+    sum_last = chip_sum(keep_last, give_last)
     sum_c, sum_last = sum_last[:, :tok_rows], sum_last[:, tok_rows:].astype(jnp.bfloat16)
 
     rowmask, ignored = tile_layout(pair_tiles, last_rows, plane * tiles_here, tiles_here, TILE)
@@ -553,13 +554,14 @@
     prods_own = tile_prods(sum_own)
     prods_middle = tile_prods(sum_b)
     from_middle = middle(prods_middle)
-    last = lax.ppermute(after(sum_last, rot_in, prods_middle), "cand", SIDE)
-    back = lax.ppermute(sums, "cand", SIDE)
-    back = jnp.where(end, back, jnp.zeros_like(back)).reshape(slim, 3, tok_rows - TILE)
-    last = jnp.where(end, last, jnp.zeros_like(last)).reshape(slim, 3, TILE)
+    last = lax.ppermute(after(sum_last, rows_there), "cand", SIDE)
+    back = after(lax.ppermute(sums, "cand", SIDE), give_last)
+    few = tok_rows - TILE
 
     def with_partner(whole, at):
-        return whole + jnp.concatenate([back[:, at], last[:, at]], axis=1).astype(jnp.float32)
+        parts = [back[:, at * few : (at + 1) * few], last[:, at * TILE : (at + 1) * TILE]]
+        parts = jnp.concatenate(parts, axis=1).astype(jnp.float32)
+        return whole + jnp.where(end, parts, 0.0)
 
     prods_a = tile_prods(with_partner(sum_a, 0))
     prods_b = tile_prods(with_partner(sum_b, 1))

time: 153 us -> 152 us (level)
    ppermute x1, waiting for transfers between devices: 5.34 us -> 7.33 us  [line_plan(): from_far = lax.ppermute(after(prods_c, to_two, from_middle), ALL, far)]
    unnamed x78 -> x72, local copies, waits for them, and re-layouts: 18.3 us -> 18.3 us
  transfers between devices with their start and end apart: 28 -> 28, of which waited for: 10 -> 10; matrix products, arithmetic and copies ran while one was open for 11% -> 10% of each run, Pallas kernels for 17% -> 17%
where the time goes in v16:
time: 152 us; the launch traced here: 151 us
  starting transfers between devices  45 us (30%)
  waiting for transfers between devices  31.8 us (21%)
  Pallas kernels  26 us (17%)
  local copies, waits for them, and re-layouts  23.3 us (15%)
  blocking collectives  11 us (7%)
  other arithmetic  10 us (7%)
  matrix products  3.82 us (3%)
    unnamed x72, local copies, waits for them, and re-layouts  18.3 us
    ppermute x2, starting transfers between devices, side(): return lax.ppermute(pick(at_end, at_middle), 'cand', SIDE)  11.9 us
    all_to_all x1, blocking collectives, final_sum(): return jnp.sum(lax.all_to_all(blocks, ALL, 0, 0, tiled=True), axis=0)  11 us
    pallas_call x2, Pallas kernels, feature_dots(): pl.pallas_call(kernel, out_shape=out_shape, grid_spec=pltpu.PrefetchScala...  8.38 us
    ppermute x1, waiting for transfers between devices, line_plan(): s45 = lax.ppermute(to_s45, 'cand', SIDE)  7.67 us
    ppermute x1, starting transfers between devices, line_plan(): s45 = lax.ppermute(to_s45, 'cand', SIDE)  7.66 us
    ppermute x1, waiting for transfers between devices, line_plan(): from_far = lax.ppermute(after(prods_c, to_two, from_middle), ALL, far)  7.33 us
    pallas_call x2, Pallas kernels, partner_dots(): pl.pallas_call(kernel, out_shape=out_shape, grid_spec=pltpu.PrefetchScala...  7.21 us
  transfers between devices with their start and end apart: 28, of which 10 were waited for; matrix products, arithmetic and copies ran while one was open for 10% of the time, Pallas kernels for 17%

profile of v16, /device:TPU:0, one launch (start us, length us, event | category | flops | bytes accessed | tf_op | source)
XLA Modules:
  0.0 151.4 jit_solution(332864651999482154)
XLA Ops:
  0.5 4.1 %collective-permute-start = (bf16[1280,128]{1,0:T(8,128)(2,1)}, bf16[1280,128]{1,0:T(8,128)(2,1)}, u32[]{:S(2)}, u32[]{:S(2)}) collective-permute-start(bf16[1280,128]{1,0:T(8,128)(2,1)} %refs_0_.3), channel_id=1, source_target_pairs={{0,4},{4,0},{8,12},{12,8},{1,5},{5,1},{9,13},{13,9},{2,6},{6,2},{1... | collective-permute-start | bytes 983048 | tf_op jit(solution)/shard_map/ppermute | solution.py:455
  8.3 3.5 %divide_convert_fusion = bf16[64,32,512]{2,1,0:T(8,128)(2,1)} fusion(bf16[64,32,512]{2,1,0:T(8,128)(2,1)} %param.13, f32[32,512]{1,0:T(8,128)S(1)} %broadcast_add_fusion), kind=kLoop, calls=%fused_computation | loop fusion | flops 3145728 | bytes 4259840 | tf_op jit(solution)/shard_map/convert_element_type | solution.py:465
  11.9 3.0 %copy-done = bf16[512,6912]{1,0:T(8,128)(2,1)S(1)} copy-done((bf16[512,6912]{1,0:T(8,128)(2,1)S(1)}, bf16[512,6912]{1,0:T(8,128)(2,1)}, u32[]{:S(2)}) %copy-start) | copy-done | bytes 7077912
  20.2 3.0 %copy-done.1 = bf16[512,6912]{1,0:T(8,128)(2,1)S(1)} copy-done((bf16[512,6912]{1,0:T(8,128)(2,1)S(1)}, bf16[512,6912]{1,0:T(8,128)(2,1)}, u32[]{:S(2)}) %copy-start.1) | copy-done | bytes 7077912
  23.2 4.6 %shard_map.82 = (f32[64,512]{1,0:T(8,128)S(1)}, f32[64,512]{1,0:T(8,128)S(1)}) custom-call(s32[6]{0:T(128)S(1)} %stack.36.flags_ref, bf16[512,6912]{1,0:T(8,128)(2,1)S(1)} %copy-done.1, bf16[6912,128]{1,0:T(8,128)(2,1)S(1)} %copy-done.2), custom_call_target="tpu_custom_call" | custom-call | flops 1 | bytes 1 | tf_op jit(solution)/shard_map/pallas_call | solution.py:161
  28.1 4.5 %collective-permute-start.3 = (bf16[2560,128]{1,0:T(8,128)(2,1)S(1)}, bf16[2560,128]{1,0:T(8,128)(2,1)S(1)}, u32[]{:S(2)}, u32[]{:S(2)}) collective-permute-start(bf16[2560,128]{1,0:T(8,128)(2,1)S(1)} %maximum_select_fusion.1), channel_id=1, source_target_pairs={{0,4},{4,0},{8,12},{12,8},{1,5},{5,1},{9,13},{13,9},{2,6},{6,2},{1... | collective-permute-start | bytes 1966088 | tf_op jit(solution)/shard_map/ppermute | solution.py:437
  32.6 6.1 %collective-permute-done.4.refs_0_ = bf16[4608,128]{1,0:T(8,128)(2,1)S(1)} collective-permute-done((bf16[4608,128]{1,0:T(8,128)(2,1)}, bf16[4608,128]{1,0:T(8,128)(2,1)S(1)}, u32[]{:S(2)}, u32[]{:S(2)}) %collective-permute-start.4) | collective-permute-done | bytes 1179680 | tf_op jit(solution)/shard_map/ppermute | solution.py:457
  41.5 7.7 %collective-permute-start.9 = (bf16[4608,128]{1,0:T(8,128)(2,1)S(1)}, bf16[4608,128]{1,0:T(8,128)(2,1)S(1)}, u32[]{:S(2)}, u32[]{:S(2)}) collective-permute-start(bf16[4608,128]{1,0:T(8,128)(2,1)S(1)} %maximum_select_fusion), channel_id=1, source_target_pairs={{0,4},{4,0},{8,12},{12,8},{1,5},{5,1},{9,13},{13,9},{2,6},{6,2},{1... | collective-permute-start | bytes 3538952 | tf_op jit(solution)/shard_map/ppermute | solution.py:472
  49.3 3.5 %collective-permute-done.3.refs_2_.refs_4_.refs_1_ = bf16[2560,128]{1,0:T(8,128)(2,1)S(1)} collective-permute-done((bf16[2560,128]{1,0:T(8,128)(2,1)S(1)}, bf16[2560,128]{1,0:T(8,128)(2,1)S(1)}, u32[]{:S(2)}, u32[]{:S(2)}) %collective-permute-start.3) | collective-permute-done | bytes 655392 | tf_op jit(solution)/shard_map/ppermute | solution.py:437
  52.9 3.9 %shard_map.83 = (f32[256,512]{1,0:T(8,128)S(1)}, f32[256,512]{1,0:T(8,128)S(1)}) custom-call(s32[6]{0:T(128)S(1)} %stack.36.flags_ref, bf16[512,1280]{1,0:T(8,128)(2,1)S(1)} %copy-done.12, bf16[1280,128]{1,0:T(8,128)(2,1)S(1)} %copy-done.23, bf16[1280,128]{1,0:T(8,128)(2,1)} %collective-permute-done.refs_1_, ...), custom_call_target="tpu_custom_call" | custom-call | flops 1 | bytes 1 | tf_op jit(solution)/shard_map/pallas_call | solution.py:408
  58.3 7.4 %collective-permute-start.12 = (bf16[2304,128]{1,0:T(8,128)(2,1)}, bf16[2304,128]{1,0:T(8,128)(2,1)S(1)}, u32[]{:S(2)}, u32[]{:S(2)}) collective-permute-start(bf16[2304,128]{1,0:T(8,128)(2,1)} %broadcast_select_fusion), channel_id=1, source_target_pairs={{0,4},{4,0},{8,12},{12,8},{1,5},{5,1},{9,13},{13,9},{2,6},{6,2},{1... | collective-permute-start | bytes 1769480 | tf_op jit(solution)/shard_map/ppermute | solution.py:437
  65.7 3.8 %shard_map.84 = (f32[64,512]{1,0:T(8,128)S(1)}, f32[64,512]{1,0:T(8,128)S(1)}) custom-call(s32[6]{0:T(128)S(1)} %stack.36.flags_ref, bf16[512,6912]{1,0:T(8,128)(2,1)S(1)} %bitcast.48, bf16[4608,128]{1,0:T(8,128)(2,1)S(1)} %copy-done.4, bf16[2560,128]{1,0:T(8,128)(2,1)S(1)} %collective-permute-done.3.refs_2_.refs_4_.refs_1_), custom_call_target="tpu_custom_call" | custom-call | flops 1 | bytes 1 | tf_op jit(solution)/shard_map/pallas_call | solution.py:161
  70.4 7.7 %collective-permute-done.9.end_ref.refs_0_.refs_1_ = bf16[4608,128]{1,0:T(8,128)(2,1)S(1)} collective-permute-done((bf16[4608,128]{1,0:T(8,128)(2,1)S(1)}, bf16[4608,128]{1,0:T(8,128)(2,1)S(1)}, u32[]{:S(2)}, u32[]{:S(2)}) %collective-permute-start.9) | collective-permute-done | bytes 1179680 | tf_op jit(solution)/shard_map/ppermute | solution.py:472
  79.0 5.2 %shard_map.86 = (f32[512,256]{1,0:T(8,128)S(1)}, bf16[512,2304]{1,0:T(8,128)(2,1)S(1)}, bf16[512,2304]{1,0:T(8,128)(2,1)S(1)}) custom-call(s32[6]{0:T(128)S(1)} %stack.36.flags_ref, bf16[512,6912]{1,0:T(8,128)(2,1)S(1)} %bitcast.48, bf16[4608,128]{1,0:T(8,128)(2,1)S(1)} %collective-permute-done.9.end_ref.refs_0_.refs_1_, ...), custom_call_target="tpu_custom_call" | custom-call | flops 1 | bytes 1 | tf_op jit(solution)/shard_map/pallas_call | solution.py:233
  94.9 3.6 %shard_map.87 = (f32[64,1664]{1,0:T(8,128)S(1)}, f32[64,1664]{1,0:T(8,128)S(1)}, f32[512,128]{1,0:T(8,128)S(1)}) custom-call(s32[6]{0:T(128)S(1)} %stack.36.flags_ref, bf16[4608,128]{1,0:T(8,128)(2,1)S(1)} %collective-permute-done.9.end_ref.refs_0_.refs_1_, bf16[4608,128]{1,0:T(8,128)(2,1)S(1)} %collective-permute-done.9.end_ref.refs_0_.refs_1_, ...), custom_call_target="tpu_custom_call" | custom-call | flops 1 | bytes 1 | tf_op jit(solution)/shard_map/pallas_call | solution.py:325
  102.7 2.6 %collective-permute-done.20.refs_0_.refs_4_ = bf16[2304,128]{1,0:T(8,128)(2,1)S(1)} collective-permute-done((bf16[2304,128]{1,0:T(8,128)(2,1)}, bf16[2304,128]{1,0:T(8,128)(2,1)S(1)}, u32[]{:S(2)}, u32[]{:S(2)}) %collective-permute-start.20) | collective-permute-done | bytes 589856 | tf_op jit(solution)/shard_map/ppermute | solution.py:477
  105.3 3.6 %shard_map.88 = (f32[64,896]{1,0:T(8,128)S(1)}, f32[64,896]{1,0:T(8,128)S(1)}) custom-call(s32[6]{0:T(128)S(1)} %stack.36.flags_ref, bf16[2304,128]{1,0:T(8,128)(2,1)S(1)} %collective-permute-done.20.refs_0_.refs_4_, bf16[6912,128]{1,0:T(8,128)(2,1)S(1)} %copy-done.2, bf16[2304,128]{1,0:T(8,128)(2,1)S(1)} %copy-done.9, ...), custom_call_target="tpu_custom_call" | custom-call | flops 1 | bytes 1 | tf_op jit(solution)/shard_map/pallas_call | solution.py:325
  109.1 4.1 %collective-permute-start.19 = (bf16[32,1152]{1,0:T(8,128)(2,1)S(1)}, bf16[32,1152]{1,0:T(8,128)(2,1)S(1)}, u32[]{:S(2)}, u32[]{:S(2)}) collective-permute-start(bf16[32,1152]{1,0:T(8,128)(2,1)S(1)} %slice.85), channel_id=1, source_target_pairs={{0,4},{4,0},{8,12},{12,8},{1,5},{5,1},{9,13},{13,9},{2,6},{6,2},{1... | collective-permute-start | bytes 221192 | tf_op jit(solution)/shard_map/ppermute | solution.py:558
  117.6 2.6 %collective-permute-start.23 = (bf16[32,384]{1,0:T(8,128)(2,1)S(1)}, bf16[32,384]{1,0:T(8,128)(2,1)S(1)}, u32[]{:S(2)}, u32[]{:S(2)}) collective-permute-start(bf16[32,384]{1,0:T(8,128)(2,1)S(1)} %slice.120), channel_id=1, source_target_pairs={{0,4},{4,0},{8,12},{12,8},{1,5},{5,1},{9,13},{13,9},{2,6},{6,2},{1... | collective-permute-start | bytes 73736 | tf_op jit(solution)/shard_map/ppermute | solution.py:557
  122.7 3.5 %collective-permute-start.25 = (bf16[4,32,512]{2,1,0:T(8,128)(2,1)S(1)}, bf16[4,32,512]{2,1,0:T(8,128)(2,1)S(1)}, u32[]{:S(2)}, u32[]{:S(2)}) collective-permute-start(bf16[4,32,512]{2,1,0:T(8,128)(2,1)S(1)} %fusion.2), channel_id=1, source_target_pairs={{0,8},{8,0},{4,12},{12,4},{1,9},{9,1},{5,13},{13,5},{2,10},{10,2},... | collective-permute-start | bytes 393224 | tf_op jit(solution)/shard_map/ppermute | solution.py:570
  126.5 2.4 %collective-permute-start.27 = (bf16[4,32,512]{2,1,0:T(8,128)(2,1)S(1)}, bf16[4,32,512]{2,1,0:T(8,128)(2,1)S(1)}, u32[]{:S(2)}, u32[]{:S(2)}) collective-permute-start(bf16[4,32,512]{2,1,0:T(8,128)(2,1)S(1)} %convolution_convert_fusion.1), channel_id=1, source_target_pairs={{0,12},{1,13},{2,14},{3,15},{4,5},{5,4},{6,7},{7,6},{8,9},{9,8},{1... | collective-permute-start | bytes 393224 | tf_op jit(solution)/shard_map/ppermute | solution.py:571
  129.2 7.3 %collective-permute-done.27 = bf16[4,32,512]{2,1,0:T(8,128)(2,1)S(1)} collective-permute-done((bf16[4,32,512]{2,1,0:T(8,128)(2,1)S(1)}, bf16[4,32,512]{2,1,0:T(8,128)(2,1)S(1)}, u32[]{:S(2)}, u32[]{:S(2)}) %collective-permute-start.27) | collective-permute-done | bytes 131104 | tf_op jit(solution)/shard_map/ppermute | solution.py:571
  136.9 2.8 %fusion.3 = f32[16,64]{1,0:T(8,128)S(1)} fusion(bf16[64,32,512]{2,1,0:T(8,128)(2,1)S(1)} %copy-done.27, bf16[16,32,512]{2,1,0:T(8,128)(2,1)S(1)} %pad_maximum_fusion.1), kind=kOutput, calls=%fused_computation.10 | convolution fusion | flops 33554432 | bytes 2625536 | tf_op jit(solution)/shard_map/tea,jea->tj/dot_general | solution.py:547
  139.9 11.0 %all_to_all.5 = f32[16,2,16]{2,1,0:T(2,128)S(1)} all-to-all(f32[16,2,16]{2,1,0:T(2,128)S(1)} %copy.49), channel_id=1, replica_groups=mesh['groups'=2,'cand'=4,'eig'=2,'rep'=2] {'cand','eig','rep'}, dimensions={0} | all-to-all | bytes 4096 | tf_op jit(solution)/shard_map/all_to_all | solution.py:586
  (168 shorter events, 39.3 us)
Async XLA Ops:
  0.0 19.3 %collective-permute-start.1 = (bf16[1280,128]{1,0:T(8,128)(2,1)}, bf16[1280,128]{1,0:T(8,128)(2,1)S(1)}, u32[]{:S(2)}, u32[]{:S(2)}) collective-permute-start(bf16[1280,128]{1,0:T(8,128)(2,1)} %refs_0_.3), channel_id=1, source_target_pairs={{0,1},{1,0},{2,3},{3,2},{4,8},{5,9},{6,10},{7,11},{8,4},{9,5},{10,... | collective-permute-start | bytes 983048 | tf_op jit(solution)/shard_map/ppermute | solution.py:447
  0.5 18.8 %collective-permute-start = (bf16[1280,128]{1,0:T(8,128)(2,1)}, bf16[1280,128]{1,0:T(8,128)(2,1)}, u32[]{:S(2)}, u32[]{:S(2)}) collective-permute-start(bf16[1280,128]{1,0:T(8,128)(2,1)} %refs_0_.3), channel_id=1, source_target_pairs={{0,4},{4,0},{8,12},{12,8},{1,5},{5,1},{9,13},{13,9},{2,6},{6,2},{1... | collective-permute-start | bytes 983048 | tf_op jit(solution)/shard_map/ppermute | solution.py:455
  7.0 31.7 %collective-permute-start.4 = (bf16[4608,128]{1,0:T(8,128)(2,1)}, bf16[4608,128]{1,0:T(8,128)(2,1)S(1)}, u32[]{:S(2)}, u32[]{:S(2)}) collective-permute-start(bf16[4608,128]{1,0:T(8,128)(2,1)} %constant_dynamic-slice_fusion), channel_id=1, source_target_pairs={{0,4},{4,0},{8,12},{12,8},{1,5},{5,1},{9,13},{13,9},{2,6},{6,2},{1... | collective-permute-start | bytes 3538952 | tf_op jit(solution)/shard_map/ppermute | solution.py:457
  8.3 31.4 %collective-permute-start.7 = (bf16[2304,128]{1,0:T(8,128)(2,1)}, bf16[2304,128]{1,0:T(8,128)(2,1)}, u32[]{:S(2)}, u32[]{:S(2)}) collective-permute-start(bf16[2304,128]{1,0:T(8,128)(2,1)} %get-tuple-element.90), channel_id=1, source_target_pairs={{0,1},{1,0},{2,3},{3,2},{4,8},{5,9},{6,10},{7,11},{8,4},{9,5},{10,... | collective-permute-start | bytes 1769480 | tf_op jit(solution)/shard_map/ppermute | solution.py:447
  19.3 8.6 %collective-permute-start.2 = (bf16[1280,128]{1,0:T(8,128)(2,1)}, bf16[1280,128]{1,0:T(8,128)(2,1)S(1)}, u32[]{:S(2)}, u32[]{:S(2)}) collective-permute-start(bf16[1280,128]{1,0:T(8,128)(2,1)} %collective-permute-done.refs_1_), channel_id=1, source_target_pairs={{0,1},{1,0},{2,3},{3,2},{4,8},{5,9},{6,10},{7,11},{8,4},{9,5},{10,... | collective-permute-start | bytes 983048 | tf_op jit(solution)/shard_map/ppermute | solution.py:447
  27.8 11.9 %collective-permute-start.8 = (bf16[2304,128]{1,0:T(8,128)(2,1)S(1)}, bf16[2304,128]{1,0:T(8,128)(2,1)S(1)}, u32[]{:S(2)}, u32[]{:S(2)}) collective-permute-start(bf16[2304,128]{1,0:T(8,128)(2,1)S(1)} %copy-done.26), channel_id=1, source_target_pairs={{0,1},{1,0},{2,3},{3,2},{4,8},{5,9},{6,10},{7,11},{8,4},{9,5},{10,... | collective-permute-start | bytes 1769480 | tf_op jit(solution)/shard_map/ppermute | solution.py:447
  28.1 24.6 %collective-permute-start.3 = (bf16[2560,128]{1,0:T(8,128)(2,1)S(1)}, bf16[2560,128]{1,0:T(8,128)(2,1)S(1)}, u32[]{:S(2)}, u32[]{:S(2)}) collective-permute-start(bf16[2560,128]{1,0:T(8,128)(2,1)S(1)} %maximum_select_fusion.1), channel_id=1, source_target_pairs={{0,4},{4,0},{8,12},{12,8},{1,5},{5,1},{9,13},{13,9},{2,6},{6,2},{1... | collective-permute-start | bytes 1966088 | tf_op jit(solution)/shard_map/ppermute | solution.py:437
  39.7 13.2 %collective-permute-start.5 = (bf16[2304,128]{1,0:T(8,128)(2,1)S(1)}, bf16[2304,128]{1,0:T(8,128)(2,1)S(1)}, u32[]{:S(2)}, u32[]{:S(2)}) collective-permute-start(bf16[2304,128]{1,0:T(8,128)(2,1)S(1)} %get-tuple-element.92), channel_id=1, source_target_pairs={{0,1},{1,0},{2,3},{3,2},{4,8},{5,9},{6,10},{7,11},{8,4},{9,5},{10,... | collective-permute-start | bytes 1769480 | tf_op jit(solution)/shard_map/ppermute | solution.py:447
  41.5 36.5 %collective-permute-start.9 = (bf16[4608,128]{1,0:T(8,128)(2,1)S(1)}, bf16[4608,128]{1,0:T(8,128)(2,1)S(1)}, u32[]{:S(2)}, u32[]{:S(2)}) collective-permute-start(bf16[4608,128]{1,0:T(8,128)(2,1)S(1)} %maximum_select_fusion), channel_id=1, source_target_pairs={{0,4},{4,0},{8,12},{12,8},{1,5},{5,1},{9,13},{13,9},{2,6},{6,2},{1... | collective-permute-start | bytes 3538952 | tf_op jit(solution)/shard_map/ppermute | solution.py:472
  52.8 17.5 %collective-permute-start.10 = (bf16[2304,128]{1,0:T(8,128)(2,1)S(1)}, bf16[2304,128]{1,0:T(8,128)(2,1)S(1)}, u32[]{:S(2)}, u32[]{:S(2)}) collective-permute-start(bf16[2304,128]{1,0:T(8,128)(2,1)S(1)} %slice.81), channel_id=1, source_target_pairs={{0,1},{1,0},{2,3},{3,2},{4,8},{5,9},{6,10},{7,11},{8,4},{9,5},{10,... | collective-permute-start | bytes 1769480 | tf_op jit(solution)/shard_map/ppermute | solution.py:447
  56.9 31.0 %collective-permute-start.6 = (bf16[2304,128]{1,0:T(8,128)(2,1)S(1)}, bf16[2304,128]{1,0:T(8,128)(2,1)S(1)}, u32[]{:S(2)}, u32[]{:S(2)}) collective-permute-start(bf16[2304,128]{1,0:T(8,128)(2,1)S(1)} %copy-done.29), channel_id=1, source_target_pairs={{0,1},{1,0},{2,3},{3,2},{4,8},{5,9},{6,10},{7,11},{8,4},{9,5},{10,... | collective-permute-start | bytes 1769480 | tf_op jit(solution)/shard_map/ppermute | solution.py:447
  58.3 32.8 %collective-permute-start.12 = (bf16[2304,128]{1,0:T(8,128)(2,1)}, bf16[2304,128]{1,0:T(8,128)(2,1)S(1)}, u32[]{:S(2)}, u32[]{:S(2)}) collective-permute-start(bf16[2304,128]{1,0:T(8,128)(2,1)} %broadcast_select_fusion), channel_id=1, source_target_pairs={{0,4},{4,0},{8,12},{12,8},{1,5},{5,1},{9,13},{13,9},{2,6},{6,2},{1... | collective-permute-start | bytes 1769480 | tf_op jit(solution)/shard_map/ppermute | solution.py:437
  70.4 20.7 %collective-permute-start.13 = (bf16[2304,128]{1,0:T(8,128)(2,1)}, bf16[2304,128]{1,0:T(8,128)(2,1)}, u32[]{:S(2)}, u32[]{:S(2)}) collective-permute-start(bf16[2304,128]{1,0:T(8,128)(2,1)} %get-tuple-element.64), channel_id=1, source_target_pairs={{0,1},{1,0},{2,3},{3,2},{4,8},{5,9},{6,10},{7,11},{8,4},{9,5},{10,... | collective-permute-start | bytes 1769480 | tf_op jit(solution)/shard_map/ppermute | solution.py:447
  88.8 16.5 %collective-permute-start.20 = (bf16[2304,128]{1,0:T(8,128)(2,1)}, bf16[2304,128]{1,0:T(8,128)(2,1)S(1)}, u32[]{:S(2)}, u32[]{:S(2)}) collective-permute-start(bf16[2304,128]{1,0:T(8,128)(2,1)} %broadcast_select_fusion.1), channel_id=1, source_target_pairs={{0,4},{4,0},{8,12},{12,8},{1,5},{5,1},{9,13},{13,9},{2,6},{6,2},{1... | collective-permute-start | bytes 1769480 | tf_op jit(solution)/shard_map/ppermute | solution.py:477
  100.4 8.6 %collective-permute-start.15 = (bf16[32,2688]{1,0:T(8,128)(2,1)S(1)}, bf16[32,2688]{1,0:T(8,128)(2,1)S(1)}, u32[]{:S(2)}, u32[]{:S(2)}) collective-permute-start(bf16[32,2688]{1,0:T(8,128)(2,1)S(1)} %add_convert_fusion.1), channel_id=1, source_target_pairs={{0,2},{2,0},{1,3},{3,1},{4,6},{6,4},{5,7},{7,5},{8,10},{10,8},{9,1... | collective-permute-start | bytes 516104 | tf_op jit(solution)/shard_map/ppermute | solution.py:37
  102.1 13.5 %collective-permute-start.17 = (bf16[256,512]{1,0:T(8,128)(2,1)S(1)}, bf16[256,512]{1,0:T(8,128)(2,1)S(1)}, u32[]{:S(2)}, u32[]{:S(2)}) collective-permute-start(bf16[256,512]{1,0:T(8,128)(2,1)S(1)} %get-tuple-element.86), channel_id=1, source_target_pairs={{0,2},{2,0},{1,3},{3,1},{4,6},{6,4},{5,7},{7,5},{8,10},{10,8},{9,1... | collective-permute-start | bytes 786440 | tf_op jit(solution)/shard_map/ppermute | solution.py:37
  108.9 4.3 %collective-permute-start.21 = (f32[64,896]{1,0:T(8,128)S(1)}, f32[64,896]{1,0:T(8,128)S(1)}, u32[]{:S(2)}, u32[]{:S(2)}) collective-permute-start(f32[64,896]{1,0:T(8,128)S(1)} %get-tuple-element.74), channel_id=1, source_target_pairs={{0,1},{1,0},{2,3},{3,2},{4,5},{5,4},{6,7},{7,6},{8,9},{9,8},{10,11... | collective-permute-start | bytes 688136 | tf_op jit(solution)/shard_map/ppermute | solution.py:37
  109.1 6.4 %collective-permute-start.19 = (bf16[32,1152]{1,0:T(8,128)(2,1)S(1)}, bf16[32,1152]{1,0:T(8,128)(2,1)S(1)}, u32[]{:S(2)}, u32[]{:S(2)}) collective-permute-start(bf16[32,1152]{1,0:T(8,128)(2,1)S(1)} %slice.85), channel_id=1, source_target_pairs={{0,4},{4,0},{8,12},{12,8},{1,5},{5,1},{9,13},{13,9},{2,6},{6,2},{1... | collective-permute-start | bytes 221192 | tf_op jit(solution)/shard_map/ppermute | solution.py:558
  113.3 4.2 %collective-permute-start.22 = (bf16[32,896]{1,0:T(8,128)(2,1)S(1)}, bf16[32,896]{1,0:T(8,128)(2,1)S(1)}, u32[]{:S(2)}, u32[]{:S(2)}) collective-permute-start(bf16[32,896]{1,0:T(8,128)(2,1)S(1)} %add_convert_fusion.2), channel_id=1, source_target_pairs={{0,2},{2,0},{1,3},{3,1},{4,6},{6,4},{5,7},{7,5},{8,10},{10,8},{9,1... | collective-permute-start | bytes 172040 | tf_op jit(solution)/shard_map/ppermute | solution.py:37
  117.6 4.4 %collective-permute-start.23 = (bf16[32,384]{1,0:T(8,128)(2,1)S(1)}, bf16[32,384]{1,0:T(8,128)(2,1)S(1)}, u32[]{:S(2)}, u32[]{:S(2)}) collective-permute-start(bf16[32,384]{1,0:T(8,128)(2,1)S(1)} %slice.120), channel_id=1, source_target_pairs={{0,4},{4,0},{8,12},{12,8},{1,5},{5,1},{9,13},{13,9},{2,6},{6,2},{1... | collective-permute-start | bytes 73736 | tf_op jit(solution)/shard_map/ppermute | solution.py:557
  122.4 4.1 %collective-permute-start.26 = (bf16[4,32,512]{2,1,0:T(8,128)(2,1)S(1)}, bf16[4,32,512]{2,1,0:T(8,128)(2,1)S(1)}, u32[]{:S(2)}, u32[]{:S(2)}) collective-permute-start(bf16[4,32,512]{2,1,0:T(8,128)(2,1)S(1)} %convolution_convert_fusion), channel_id=1, source_target_pairs={{0,1},{1,0},{2,3},{3,2},{4,8},{5,9},{6,10},{7,11},{8,4},{9,5},{10,... | collective-permute-start | bytes 393224 | tf_op jit(solution)/shard_map/ppermute | solution.py:447
  122.7 14.0 %collective-permute-start.25 = (bf16[4,32,512]{2,1,0:T(8,128)(2,1)S(1)}, bf16[4,32,512]{2,1,0:T(8,128)(2,1)S(1)}, u32[]{:S(2)}, u32[]{:S(2)}) collective-permute-start(bf16[4,32,512]{2,1,0:T(8,128)(2,1)S(1)} %fusion.2), channel_id=1, source_target_pairs={{0,8},{8,0},{4,12},{12,4},{1,9},{9,1},{5,13},{13,5},{2,10},{10,2},... | collective-permute-start | bytes 393224 | tf_op jit(solution)/shard_map/ppermute | solution.py:570
  126.5 10.1 %collective-permute-start.24 = (bf16[4,32,512]{2,1,0:T(8,128)(2,1)S(1)}, bf16[4,32,512]{2,1,0:T(8,128)(2,1)S(1)}, u32[]{:S(2)}, u32[]{:S(2)}) collective-permute-start(bf16[4,32,512]{2,1,0:T(8,128)(2,1)S(1)} %convolution_convert_fusion.3), channel_id=1, source_target_pairs={{0,4},{4,0},{8,12},{12,8},{1,5},{5,1},{9,13},{13,9},{2,6},{6,2},{1... | collective-permute-start | bytes 393224 | tf_op jit(solution)/shard_map/ppermute | solution.py:572
  126.5 10.0 %collective-permute-start.27 = (bf16[4,32,512]{2,1,0:T(8,128)(2,1)S(1)}, bf16[4,32,512]{2,1,0:T(8,128)(2,1)S(1)}, u32[]{:S(2)}, u32[]{:S(2)}) collective-permute-start(bf16[4,32,512]{2,1,0:T(8,128)(2,1)S(1)} %convolution_convert_fusion.1), channel_id=1, source_target_pairs={{0,12},{1,13},{2,14},{3,15},{4,5},{5,4},{6,7},{7,6},{8,9},{9,8},{1... | collective-permute-start | bytes 393224 | tf_op jit(solution)/shard_map/ppermute | solution.py:571
  (40 other events, 259.0 us)

commit v17 on v16

--- a/solution.py
+++ b/solution.py
@@ -554,8 +554,8 @@
     prods_own = tile_prods(sum_own)
     prods_middle = tile_prods(sum_b)
     from_middle = middle(prods_middle)
-    last = lax.ppermute(after(sum_last, rows_there), "cand", SIDE)
-    back = after(lax.ppermute(sums, "cand", SIDE), give_last)
+    last = after(lax.ppermute(after(sum_last, rows_there), "cand", SIDE), prods_middle)
+    back = after(lax.ppermute(sums, "cand", SIDE), rows_there)
     few = tok_rows - TILE
 
     def with_partner(whole, at):
@@ -568,7 +568,7 @@
     prods_c = tile_prods(with_partner(sum_c, 2))
     to_two = pick(prods_b, prods_c)
     from_two = lax.ppermute(to_two, "cand", TWO)
-    from_far = lax.ppermute(after(prods_c, to_two, from_middle), ALL, far)
+    from_far = lax.ppermute(after(prods_c, to_two), ALL, far)
     from_side = lax.ppermute(after(prods_a, to_two), "cand", SIDE)
     total = pair_scores(
         (prods_own, plane),

time: 152 us -> 151 us (level)
  transfers between devices with their start and end apart: 28 -> 28, of which waited for: 10 -> 9; matrix products, arithmetic and copies ran while one was open for 10% -> 11% of each run, Pallas kernels for 17% -> 17%
where the time goes in v17:
time: 151 us; the launch traced here: 150 us
  starting transfers between devices  43.5 us (29%)
  waiting for transfers between devices  32.1 us (21%)
  Pallas kernels  26 us (17%)
  local copies, waits for them, and re-layouts  23.3 us (15%)
  blocking collectives  11 us (7%)
  other arithmetic  10.1 us (7%)
  matrix products  3.82 us (3%)
    unnamed x72, local copies, waits for them, and re-layouts  18.3 us
    ppermute x2, starting transfers between devices, side(): return lax.ppermute(pick(at_end, at_middle), 'cand', SIDE)  11.9 us
    all_to_all x1, blocking collectives, final_sum(): return jnp.sum(lax.all_to_all(blocks, ALL, 0, 0, tiled=True), axis=0)  11 us
    pallas_call x2, Pallas kernels, feature_dots(): pl.pallas_call(kernel, out_shape=out_shape, grid_spec=pltpu.PrefetchScala...  8.38 us
    ppermute x1, waiting for transfers between devices, line_plan(): s45 = lax.ppermute(to_s45, 'cand', SIDE)  7.66 us
    ppermute x1, starting transfers between devices, line_plan(): s45 = lax.ppermute(to_s45, 'cand', SIDE)  7.66 us
    pallas_call x2, Pallas kernels, partner_dots(): pl.pallas_call(kernel, out_shape=out_shape, grid_spec=pltpu.PrefetchScala...  7.21 us
    ppermute x1, waiting for transfers between devices, line_plan(): from_far = lax.ppermute(after(prods_c, to_two), ALL, far)  6.82 us
  transfers between devices with their start and end apart: 28, of which 9 were waited for; matrix products, arithmetic and copies ran while one was open for 11% of the time, Pallas kernels for 17%

profile of v17, /device:TPU:0, one launch (start us, length us, event | category | flops | bytes accessed | tf_op | source)
XLA Modules:
  0.0 150.4 jit_solution(9743640914094248596)
XLA Ops:
  0.5 4.1 %collective-permute-start = (bf16[1280,128]{1,0:T(8,128)(2,1)}, bf16[1280,128]{1,0:T(8,128)(2,1)}, u32[]{:S(2)}, u32[]{:S(2)}) collective-permute-start(bf16[1280,128]{1,0:T(8,128)(2,1)} %refs_0_.3), channel_id=1, source_target_pairs={{0,4},{4,0},{8,12},{12,8},{1,5},{5,1},{9,13},{13,9},{2,6},{6,2},{1... | collective-permute-start | bytes 983048 | tf_op jit(solution)/shard_map/ppermute | solution.py:455
  8.3 3.5 %divide_convert_fusion = bf16[64,32,512]{2,1,0:T(8,128)(2,1)} fusion(bf16[64,32,512]{2,1,0:T(8,128)(2,1)} %param.13, f32[32,512]{1,0:T(8,128)S(1)} %broadcast_add_fusion), kind=kLoop, calls=%fused_computation | loop fusion | flops 3145728 | bytes 4259840 | tf_op jit(solution)/shard_map/convert_element_type | solution.py:465
  11.9 3.0 %copy-done = bf16[512,6912]{1,0:T(8,128)(2,1)S(1)} copy-done((bf16[512,6912]{1,0:T(8,128)(2,1)S(1)}, bf16[512,6912]{1,0:T(8,128)(2,1)}, u32[]{:S(2)}) %copy-start) | copy-done | bytes 7077912
  20.2 3.0 %copy-done.1 = bf16[512,6912]{1,0:T(8,128)(2,1)S(1)} copy-done((bf16[512,6912]{1,0:T(8,128)(2,1)S(1)}, bf16[512,6912]{1,0:T(8,128)(2,1)}, u32[]{:S(2)}) %copy-start.1) | copy-done | bytes 7077912
  23.2 4.6 %shard_map.82 = (f32[64,512]{1,0:T(8,128)S(1)}, f32[64,512]{1,0:T(8,128)S(1)}) custom-call(s32[6]{0:T(128)S(1)} %stack.36.flags_ref, bf16[512,6912]{1,0:T(8,128)(2,1)S(1)} %copy-done.1, bf16[6912,128]{1,0:T(8,128)(2,1)S(1)} %copy-done.2), custom_call_target="tpu_custom_call" | custom-call | flops 1 | bytes 1 | tf_op jit(solution)/shard_map/pallas_call | solution.py:161
  28.1 4.5 %collective-permute-start.3 = (bf16[2560,128]{1,0:T(8,128)(2,1)S(1)}, bf16[2560,128]{1,0:T(8,128)(2,1)S(1)}, u32[]{:S(2)}, u32[]{:S(2)}) collective-permute-start(bf16[2560,128]{1,0:T(8,128)(2,1)S(1)} %maximum_select_fusion.1), channel_id=1, source_target_pairs={{0,4},{4,0},{8,12},{12,8},{1,5},{5,1},{9,13},{13,9},{2,6},{6,2},{1... | collective-permute-start | bytes 1966088 | tf_op jit(solution)/shard_map/ppermute | solution.py:437
  32.6 6.1 %collective-permute-done.4.refs_0_ = bf16[4608,128]{1,0:T(8,128)(2,1)S(1)} collective-permute-done((bf16[4608,128]{1,0:T(8,128)(2,1)}, bf16[4608,128]{1,0:T(8,128)(2,1)S(1)}, u32[]{:S(2)}, u32[]{:S(2)}) %collective-permute-start.4) | collective-permute-done | bytes 1179680 | tf_op jit(solution)/shard_map/ppermute | solution.py:457
  41.5 7.7 %collective-permute-start.9 = (bf16[4608,128]{1,0:T(8,128)(2,1)S(1)}, bf16[4608,128]{1,0:T(8,128)(2,1)S(1)}, u32[]{:S(2)}, u32[]{:S(2)}) collective-permute-start(bf16[4608,128]{1,0:T(8,128)(2,1)S(1)} %maximum_select_fusion), channel_id=1, source_target_pairs={{0,4},{4,0},{8,12},{12,8},{1,5},{5,1},{9,13},{13,9},{2,6},{6,2},{1... | collective-permute-start | bytes 3538952 | tf_op jit(solution)/shard_map/ppermute | solution.py:472
  49.3 3.5 %collective-permute-done.3.refs_2_.refs_4_.refs_1_ = bf16[2560,128]{1,0:T(8,128)(2,1)S(1)} collective-permute-done((bf16[2560,128]{1,0:T(8,128)(2,1)S(1)}, bf16[2560,128]{1,0:T(8,128)(2,1)S(1)}, u32[]{:S(2)}, u32[]{:S(2)}) %collective-permute-start.3) | collective-permute-done | bytes 655392 | tf_op jit(solution)/shard_map/ppermute | solution.py:437
  52.9 3.9 %shard_map.83 = (f32[256,512]{1,0:T(8,128)S(1)}, f32[256,512]{1,0:T(8,128)S(1)}) custom-call(s32[6]{0:T(128)S(1)} %stack.36.flags_ref, bf16[512,1280]{1,0:T(8,128)(2,1)S(1)} %copy-done.12, bf16[1280,128]{1,0:T(8,128)(2,1)S(1)} %copy-done.23, bf16[1280,128]{1,0:T(8,128)(2,1)} %collective-permute-done.refs_1_, ...), custom_call_target="tpu_custom_call" | custom-call | flops 1 | bytes 1 | tf_op jit(solution)/shard_map/pallas_call | solution.py:408
  58.3 7.4 %collective-permute-start.12 = (bf16[2304,128]{1,0:T(8,128)(2,1)}, bf16[2304,128]{1,0:T(8,128)(2,1)S(1)}, u32[]{:S(2)}, u32[]{:S(2)}) collective-permute-start(bf16[2304,128]{1,0:T(8,128)(2,1)} %broadcast_select_fusion), channel_id=1, source_target_pairs={{0,4},{4,0},{8,12},{12,8},{1,5},{5,1},{9,13},{13,9},{2,6},{6,2},{1... | collective-permute-start | bytes 1769480 | tf_op jit(solution)/shard_map/ppermute | solution.py:437
  65.7 3.8 %shard_map.84 = (f32[64,512]{1,0:T(8,128)S(1)}, f32[64,512]{1,0:T(8,128)S(1)}) custom-call(s32[6]{0:T(128)S(1)} %stack.36.flags_ref, bf16[512,6912]{1,0:T(8,128)(2,1)S(1)} %bitcast.48, bf16[4608,128]{1,0:T(8,128)(2,1)S(1)} %copy-done.4, bf16[2560,128]{1,0:T(8,128)(2,1)S(1)} %collective-permute-done.3.refs_2_.refs_4_.refs_1_), custom_call_target="tpu_custom_call" | custom-call | flops 1 | bytes 1 | tf_op jit(solution)/shard_map/pallas_call | solution.py:161
  70.4 7.7 %collective-permute-done.9.end_ref.refs_0_.refs_1_ = bf16[4608,128]{1,0:T(8,128)(2,1)S(1)} collective-permute-done((bf16[4608,128]{1,0:T(8,128)(2,1)S(1)}, bf16[4608,128]{1,0:T(8,128)(2,1)S(1)}, u32[]{:S(2)}, u32[]{:S(2)}) %collective-permute-start.9) | collective-permute-done | bytes 1179680 | tf_op jit(solution)/shard_map/ppermute | solution.py:472
  79.0 5.2 %shard_map.86 = (f32[512,256]{1,0:T(8,128)S(1)}, bf16[512,2304]{1,0:T(8,128)(2,1)S(1)}, bf16[512,2304]{1,0:T(8,128)(2,1)S(1)}) custom-call(s32[6]{0:T(128)S(1)} %stack.36.flags_ref, bf16[512,6912]{1,0:T(8,128)(2,1)S(1)} %bitcast.48, bf16[4608,128]{1,0:T(8,128)(2,1)S(1)} %collective-permute-done.9.end_ref.refs_0_.refs_1_, ...), custom_call_target="tpu_custom_call" | custom-call | flops 1 | bytes 1 | tf_op jit(solution)/shard_map/pallas_call | solution.py:233
  94.9 3.6 %shard_map.87 = (f32[64,1664]{1,0:T(8,128)S(1)}, f32[64,1664]{1,0:T(8,128)S(1)}, f32[512,128]{1,0:T(8,128)S(1)}) custom-call(s32[6]{0:T(128)S(1)} %stack.36.flags_ref, bf16[4608,128]{1,0:T(8,128)(2,1)S(1)} %collective-permute-done.9.end_ref.refs_0_.refs_1_, bf16[4608,128]{1,0:T(8,128)(2,1)S(1)} %collective-permute-done.9.end_ref.refs_0_.refs_1_, ...), custom_call_target="tpu_custom_call" | custom-call | flops 1 | bytes 1 | tf_op jit(solution)/shard_map/pallas_call | solution.py:325
  102.7 2.6 %collective-permute-done.20.refs_0_.refs_4_ = bf16[2304,128]{1,0:T(8,128)(2,1)S(1)} collective-permute-done((bf16[2304,128]{1,0:T(8,128)(2,1)}, bf16[2304,128]{1,0:T(8,128)(2,1)S(1)}, u32[]{:S(2)}, u32[]{:S(2)}) %collective-permute-start.20) | collective-permute-done | bytes 589856 | tf_op jit(solution)/shard_map/ppermute | solution.py:477
  105.3 3.6 %shard_map.88 = (f32[64,896]{1,0:T(8,128)S(1)}, f32[64,896]{1,0:T(8,128)S(1)}) custom-call(s32[6]{0:T(128)S(1)} %stack.36.flags_ref, bf16[2304,128]{1,0:T(8,128)(2,1)S(1)} %collective-permute-done.20.refs_0_.refs_4_, bf16[6912,128]{1,0:T(8,128)(2,1)S(1)} %copy-done.2, bf16[2304,128]{1,0:T(8,128)(2,1)S(1)} %copy-done.9, ...), custom_call_target="tpu_custom_call" | custom-call | flops 1 | bytes 1 | tf_op jit(solution)/shard_map/pallas_call | solution.py:325
  109.1 4.1 %collective-permute-start.19 = (bf16[32,1152]{1,0:T(8,128)(2,1)S(1)}, bf16[32,1152]{1,0:T(8,128)(2,1)S(1)}, u32[]{:S(2)}, u32[]{:S(2)}) collective-permute-start(bf16[32,1152]{1,0:T(8,128)(2,1)S(1)} %slice.85), channel_id=1, source_target_pairs={{0,4},{4,0},{8,12},{12,8},{1,5},{5,1},{9,13},{13,9},{2,6},{6,2},{1... | collective-permute-start | bytes 221192 | tf_op jit(solution)/shard_map/ppermute | solution.py:558
  115.0 2.5 %collective-permute-done.22 = bf16[32,896]{1,0:T(8,128)(2,1)S(1)} collective-permute-done((bf16[32,896]{1,0:T(8,128)(2,1)S(1)}, bf16[32,896]{1,0:T(8,128)(2,1)S(1)}, u32[]{:S(2)}, u32[]{:S(2)}) %collective-permute-start.22) | collective-permute-done | bytes 57376 | tf_op jit(solution)/shard_map/ppermute | solution.py:37
  118.1 2.7 %collective-permute-start.23 = (bf16[32,384]{1,0:T(8,128)(2,1)S(1)}, bf16[32,384]{1,0:T(8,128)(2,1)S(1)}, u32[]{:S(2)}, u32[]{:S(2)}) collective-permute-start(bf16[32,384]{1,0:T(8,128)(2,1)S(1)} %slice.117), channel_id=1, source_target_pairs={{0,4},{4,0},{8,12},{12,8},{1,5},{5,1},{9,13},{13,9},{2,6},{6,2},{1... | collective-permute-start | bytes 73736 | tf_op jit(solution)/shard_map/ppermute | solution.py:557
  123.1 3.0 %collective-permute-start.25 = (bf16[4,32,512]{2,1,0:T(8,128)(2,1)S(1)}, bf16[4,32,512]{2,1,0:T(8,128)(2,1)S(1)}, u32[]{:S(2)}, u32[]{:S(2)}) collective-permute-start(bf16[4,32,512]{2,1,0:T(8,128)(2,1)S(1)} %fusion.2), channel_id=1, source_target_pairs={{0,8},{8,0},{4,12},{12,4},{1,9},{9,1},{5,13},{13,5},{2,10},{10,2},... | collective-permute-start | bytes 393224 | tf_op jit(solution)/shard_map/ppermute | solution.py:570
  127.8 6.8 %collective-permute-done.26 = bf16[4,32,512]{2,1,0:T(8,128)(2,1)S(1)} collective-permute-done((bf16[4,32,512]{2,1,0:T(8,128)(2,1)S(1)}, bf16[4,32,512]{2,1,0:T(8,128)(2,1)S(1)}, u32[]{:S(2)}, u32[]{:S(2)}) %collective-permute-start.26) | collective-permute-done | bytes 131104 | tf_op jit(solution)/shard_map/ppermute | solution.py:571
  135.8 2.8 %fusion.3 = f32[16,64]{1,0:T(8,128)S(1)} fusion(bf16[64,32,512]{2,1,0:T(8,128)(2,1)S(1)} %copy-done.27, bf16[16,32,512]{2,1,0:T(8,128)(2,1)S(1)} %pad_maximum_fusion.1), kind=kOutput, calls=%fused_computation.10 | convolution fusion | flops 33554432 | bytes 2625536 | tf_op jit(solution)/shard_map/tea,jea->tj/dot_general | solution.py:547
  138.8 11.0 %all_to_all.5 = f32[16,2,16]{2,1,0:T(2,128)S(1)} all-to-all(f32[16,2,16]{2,1,0:T(2,128)S(1)} %copy.49), channel_id=1, replica_groups=mesh['groups'=2,'cand'=4,'eig'=2,'rep'=2] {'cand','eig','rep'}, dimensions={0} | all-to-all | bytes 4096 | tf_op jit(solution)/shard_map/all_to_all | solution.py:586
  (169 shorter events, 39.2 us)
Async XLA Ops:
  0.0 19.3 %collective-permute-start.1 = (bf16[1280,128]{1,0:T(8,128)(2,1)}, bf16[1280,128]{1,0:T(8,128)(2,1)S(1)}, u32[]{:S(2)}, u32[]{:S(2)}) collective-permute-start(bf16[1280,128]{1,0:T(8,128)(2,1)} %refs_0_.3), channel_id=1, source_target_pairs={{0,1},{1,0},{2,3},{3,2},{4,8},{5,9},{6,10},{7,11},{8,4},{9,5},{10,... | collective-permute-start | bytes 983048 | tf_op jit(solution)/shard_map/ppermute | solution.py:447
  0.5 18.8 %collective-permute-start = (bf16[1280,128]{1,0:T(8,128)(2,1)}, bf16[1280,128]{1,0:T(8,128)(2,1)}, u32[]{:S(2)}, u32[]{:S(2)}) collective-permute-start(bf16[1280,128]{1,0:T(8,128)(2,1)} %refs_0_.3), channel_id=1, source_target_pairs={{0,4},{4,0},{8,12},{12,8},{1,5},{5,1},{9,13},{13,9},{2,6},{6,2},{1... | collective-permute-start | bytes 983048 | tf_op jit(solution)/shard_map/ppermute | solution.py:455
  7.0 31.7 %collective-permute-start.4 = (bf16[4608,128]{1,0:T(8,128)(2,1)}, bf16[4608,128]{1,0:T(8,128)(2,1)S(1)}, u32[]{:S(2)}, u32[]{:S(2)}) collective-permute-start(bf16[4608,128]{1,0:T(8,128)(2,1)} %constant_dynamic-slice_fusion), channel_id=1, source_target_pairs={{0,4},{4,0},{8,12},{12,8},{1,5},{5,1},{9,13},{13,9},{2,6},{6,2},{1... | collective-permute-start | bytes 3538952 | tf_op jit(solution)/shard_map/ppermute | solution.py:457
  8.3 31.5 %collective-permute-start.7 = (bf16[2304,128]{1,0:T(8,128)(2,1)}, bf16[2304,128]{1,0:T(8,128)(2,1)}, u32[]{:S(2)}, u32[]{:S(2)}) collective-permute-start(bf16[2304,128]{1,0:T(8,128)(2,1)} %get-tuple-element.92), channel_id=1, source_target_pairs={{0,1},{1,0},{2,3},{3,2},{4,8},{5,9},{6,10},{7,11},{8,4},{9,5},{10,... | collective-permute-start | bytes 1769480 | tf_op jit(solution)/shard_map/ppermute | solution.py:447
  19.3 8.6 %collective-permute-start.2 = (bf16[1280,128]{1,0:T(8,128)(2,1)}, bf16[1280,128]{1,0:T(8,128)(2,1)S(1)}, u32[]{:S(2)}, u32[]{:S(2)}) collective-permute-start(bf16[1280,128]{1,0:T(8,128)(2,1)} %collective-permute-done.refs_1_), channel_id=1, source_target_pairs={{0,1},{1,0},{2,3},{3,2},{4,8},{5,9},{6,10},{7,11},{8,4},{9,5},{10,... | collective-permute-start | bytes 983048 | tf_op jit(solution)/shard_map/ppermute | solution.py:447
  27.8 11.9 %collective-permute-start.8 = (bf16[2304,128]{1,0:T(8,128)(2,1)S(1)}, bf16[2304,128]{1,0:T(8,128)(2,1)S(1)}, u32[]{:S(2)}, u32[]{:S(2)}) collective-permute-start(bf16[2304,128]{1,0:T(8,128)(2,1)S(1)} %copy-done.26), channel_id=1, source_target_pairs={{0,1},{1,0},{2,3},{3,2},{4,8},{5,9},{6,10},{7,11},{8,4},{9,5},{10,... | collective-permute-start | bytes 1769480 | tf_op jit(solution)/shard_map/ppermute | solution.py:447
  28.1 24.6 %collective-permute-start.3 = (bf16[2560,128]{1,0:T(8,128)(2,1)S(1)}, bf16[2560,128]{1,0:T(8,128)(2,1)S(1)}, u32[]{:S(2)}, u32[]{:S(2)}) collective-permute-start(bf16[2560,128]{1,0:T(8,128)(2,1)S(1)} %maximum_select_fusion.1), channel_id=1, source_target_pairs={{0,4},{4,0},{8,12},{12,8},{1,5},{5,1},{9,13},{13,9},{2,6},{6,2},{1... | collective-permute-start | bytes 1966088 | tf_op jit(solution)/shard_map/ppermute | solution.py:437
  39.7 13.2 %collective-permute-start.5 = (bf16[2304,128]{1,0:T(8,128)(2,1)S(1)}, bf16[2304,128]{1,0:T(8,128)(2,1)S(1)}, u32[]{:S(2)}, u32[]{:S(2)}) collective-permute-start(bf16[2304,128]{1,0:T(8,128)(2,1)S(1)} %get-tuple-element.94), channel_id=1, source_target_pairs={{0,1},{1,0},{2,3},{3,2},{4,8},{5,9},{6,10},{7,11},{8,4},{9,5},{10,... | collective-permute-start | bytes 1769480 | tf_op jit(solution)/shard_map/ppermute | solution.py:447
  41.5 36.5 %collective-permute-start.9 = (bf16[4608,128]{1,0:T(8,128)(2,1)S(1)}, bf16[4608,128]{1,0:T(8,128)(2,1)S(1)}, u32[]{:S(2)}, u32[]{:S(2)}) collective-permute-start(bf16[4608,128]{1,0:T(8,128)(2,1)S(1)} %maximum_select_fusion), channel_id=1, source_target_pairs={{0,4},{4,0},{8,12},{12,8},{1,5},{5,1},{9,13},{13,9},{2,6},{6,2},{1... | collective-permute-start | bytes 3538952 | tf_op jit(solution)/shard_map/ppermute | solution.py:472
  52.8 17.6 %collective-permute-start.10 = (bf16[2304,128]{1,0:T(8,128)(2,1)S(1)}, bf16[2304,128]{1,0:T(8,128)(2,1)S(1)}, u32[]{:S(2)}, u32[]{:S(2)}) collective-permute-start(bf16[2304,128]{1,0:T(8,128)(2,1)S(1)} %slice.81), channel_id=1, source_target_pairs={{0,1},{1,0},{2,3},{3,2},{4,8},{5,9},{6,10},{7,11},{8,4},{9,5},{10,... | collective-permute-start | bytes 1769480 | tf_op jit(solution)/shard_map/ppermute | solution.py:447
  56.9 31.0 %collective-permute-start.6 = (bf16[2304,128]{1,0:T(8,128)(2,1)S(1)}, bf16[2304,128]{1,0:T(8,128)(2,1)S(1)}, u32[]{:S(2)}, u32[]{:S(2)}) collective-permute-start(bf16[2304,128]{1,0:T(8,128)(2,1)S(1)} %copy-done.29), channel_id=1, source_target_pairs={{0,1},{1,0},{2,3},{3,2},{4,8},{5,9},{6,10},{7,11},{8,4},{9,5},{10,... | collective-permute-start | bytes 1769480 | tf_op jit(solution)/shard_map/ppermute | solution.py:447
  58.3 32.8 %collective-permute-start.12 = (bf16[2304,128]{1,0:T(8,128)(2,1)}, bf16[2304,128]{1,0:T(8,128)(2,1)S(1)}, u32[]{:S(2)}, u32[]{:S(2)}) collective-permute-start(bf16[2304,128]{1,0:T(8,128)(2,1)} %broadcast_select_fusion), channel_id=1, source_target_pairs={{0,4},{4,0},{8,12},{12,8},{1,5},{5,1},{9,13},{13,9},{2,6},{6,2},{1... | collective-permute-start | bytes 1769480 | tf_op jit(solution)/shard_map/ppermute | solution.py:437
  70.4 20.8 %collective-permute-start.13 = (bf16[2304,128]{1,0:T(8,128)(2,1)}, bf16[2304,128]{1,0:T(8,128)(2,1)}, u32[]{:S(2)}, u32[]{:S(2)}) collective-permute-start(bf16[2304,128]{1,0:T(8,128)(2,1)} %get-tuple-element.65), channel_id=1, source_target_pairs={{0,1},{1,0},{2,3},{3,2},{4,8},{5,9},{6,10},{7,11},{8,4},{9,5},{10,... | collective-permute-start | bytes 1769480 | tf_op jit(solution)/shard_map/ppermute | solution.py:447
  88.8 16.5 %collective-permute-start.20 = (bf16[2304,128]{1,0:T(8,128)(2,1)}, bf16[2304,128]{1,0:T(8,128)(2,1)S(1)}, u32[]{:S(2)}, u32[]{:S(2)}) collective-permute-start(bf16[2304,128]{1,0:T(8,128)(2,1)} %broadcast_select_fusion.1), channel_id=1, source_target_pairs={{0,4},{4,0},{8,12},{12,8},{1,5},{5,1},{9,13},{13,9},{2,6},{6,2},{1... | collective-permute-start | bytes 1769480 | tf_op jit(solution)/shard_map/ppermute | solution.py:477
  100.5 8.6 %collective-permute-start.15 = (bf16[32,2688]{1,0:T(8,128)(2,1)S(1)}, bf16[32,2688]{1,0:T(8,128)(2,1)S(1)}, u32[]{:S(2)}, u32[]{:S(2)}) collective-permute-start(bf16[32,2688]{1,0:T(8,128)(2,1)S(1)} %add_convert_fusion.1), channel_id=1, source_target_pairs={{0,2},{2,0},{1,3},{3,1},{4,6},{6,4},{5,7},{7,5},{8,10},{10,8},{9,1... | collective-permute-start | bytes 516104 | tf_op jit(solution)/shard_map/ppermute | solution.py:37
  102.1 12.7 %collective-permute-start.17 = (bf16[256,512]{1,0:T(8,128)(2,1)S(1)}, bf16[256,512]{1,0:T(8,128)(2,1)S(1)}, u32[]{:S(2)}, u32[]{:S(2)}) collective-permute-start(bf16[256,512]{1,0:T(8,128)(2,1)S(1)} %get-tuple-element.88), channel_id=1, source_target_pairs={{0,2},{2,0},{1,3},{3,1},{4,6},{6,4},{5,7},{7,5},{8,10},{10,8},{9,1... | collective-permute-start | bytes 786440 | tf_op jit(solution)/shard_map/ppermute | solution.py:37
  108.9 4.3 %collective-permute-start.21 = (f32[64,896]{1,0:T(8,128)S(1)}, f32[64,896]{1,0:T(8,128)S(1)}, u32[]{:S(2)}, u32[]{:S(2)}) collective-permute-start(f32[64,896]{1,0:T(8,128)S(1)} %get-tuple-element.76), channel_id=1, source_target_pairs={{0,1},{1,0},{2,3},{3,2},{4,5},{5,4},{6,7},{7,6},{8,9},{9,8},{10,11... | collective-permute-start | bytes 688136 | tf_op jit(solution)/shard_map/ppermute | solution.py:37
  109.1 8.6 %collective-permute-start.19 = (bf16[32,1152]{1,0:T(8,128)(2,1)S(1)}, bf16[32,1152]{1,0:T(8,128)(2,1)S(1)}, u32[]{:S(2)}, u32[]{:S(2)}) collective-permute-start(bf16[32,1152]{1,0:T(8,128)(2,1)S(1)} %slice.85), channel_id=1, source_target_pairs={{0,4},{4,0},{8,12},{12,8},{1,5},{5,1},{9,13},{13,9},{2,6},{6,2},{1... | collective-permute-start | bytes 221192 | tf_op jit(solution)/shard_map/ppermute | solution.py:558
  113.3 4.2 %collective-permute-start.22 = (bf16[32,896]{1,0:T(8,128)(2,1)S(1)}, bf16[32,896]{1,0:T(8,128)(2,1)S(1)}, u32[]{:S(2)}, u32[]{:S(2)}) collective-permute-start(bf16[32,896]{1,0:T(8,128)(2,1)S(1)} %add_convert_fusion.2), channel_id=1, source_target_pairs={{0,2},{2,0},{1,3},{3,1},{4,6},{6,4},{5,7},{7,5},{8,10},{10,8},{9,1... | collective-permute-start | bytes 172040 | tf_op jit(solution)/shard_map/ppermute | solution.py:37
  118.1 4.5 %collective-permute-start.23 = (bf16[32,384]{1,0:T(8,128)(2,1)S(1)}, bf16[32,384]{1,0:T(8,128)(2,1)S(1)}, u32[]{:S(2)}, u32[]{:S(2)}) collective-permute-start(bf16[32,384]{1,0:T(8,128)(2,1)S(1)} %slice.117), channel_id=1, source_target_pairs={{0,4},{4,0},{8,12},{12,8},{1,5},{5,1},{9,13},{13,9},{2,6},{6,2},{1... | collective-permute-start | bytes 73736 | tf_op jit(solution)/shard_map/ppermute | solution.py:557
  120.8 7.0 %collective-permute-start.27 = (bf16[4,32,512]{2,1,0:T(8,128)(2,1)S(1)}, bf16[4,32,512]{2,1,0:T(8,128)(2,1)S(1)}, u32[]{:S(2)}, u32[]{:S(2)}) collective-permute-start(bf16[4,32,512]{2,1,0:T(8,128)(2,1)S(1)} %convolution_convert_fusion.3), channel_id=1, source_target_pairs={{0,1},{1,0},{2,3},{3,2},{4,8},{5,9},{6,10},{7,11},{8,4},{9,5},{10,... | collective-permute-start | bytes 393224 | tf_op jit(solution)/shard_map/ppermute | solution.py:447
  123.1 12.7 %collective-permute-start.25 = (bf16[4,32,512]{2,1,0:T(8,128)(2,1)S(1)}, bf16[4,32,512]{2,1,0:T(8,128)(2,1)S(1)}, u32[]{:S(2)}, u32[]{:S(2)}) collective-permute-start(bf16[4,32,512]{2,1,0:T(8,128)(2,1)S(1)} %fusion.2), channel_id=1, source_target_pairs={{0,8},{8,0},{4,12},{12,4},{1,9},{9,1},{5,13},{13,5},{2,10},{10,2},... | collective-permute-start | bytes 393224 | tf_op jit(solution)/shard_map/ppermute | solution.py:570
  126.1 8.6 %collective-permute-start.26 = (bf16[4,32,512]{2,1,0:T(8,128)(2,1)S(1)}, bf16[4,32,512]{2,1,0:T(8,128)(2,1)S(1)}, u32[]{:S(2)}, u32[]{:S(2)}) collective-permute-start(bf16[4,32,512]{2,1,0:T(8,128)(2,1)S(1)} %convolution_convert_fusion), channel_id=1, source_target_pairs={{0,12},{1,13},{2,14},{3,15},{4,5},{5,4},{6,7},{7,6},{8,9},{9,8},{1... | collective-permute-start | bytes 393224 | tf_op jit(solution)/shard_map/ppermute | solution.py:571
  127.7 8.0 %collective-permute-start.24 = (bf16[4,32,512]{2,1,0:T(8,128)(2,1)S(1)}, bf16[4,32,512]{2,1,0:T(8,128)(2,1)S(1)}, u32[]{:S(2)}, u32[]{:S(2)}) collective-permute-start(bf16[4,32,512]{2,1,0:T(8,128)(2,1)S(1)} %convolution_convert_fusion.2), channel_id=1, source_target_pairs={{0,4},{4,0},{8,12},{12,8},{1,5},{5,1},{9,13},{13,9},{2,6},{6,2},{1... | collective-permute-start | bytes 393224 | tf_op jit(solution)/shard_map/ppermute | solution.py:572
  (40 other events, 258.5 us)

commit v18 on v17

--- a/solution.py
+++ b/solution.py
@@ -491,26 +491,26 @@
         ],
     )
     totals, next_grads, last_grads = both_dots(after(flags, to_s7, s45, *part_a), grads, (s45, 0), ((m2, m5), (m3, m6)))
-    parts = [jnp.concatenate(part, axis=1) for part in zip(part_own, part_a)]
-    keep_a, give_a = after(parts, m4, totals)
-    core_a = swap(give_a, "rep")
-
-    shards = [(basis_out, 0), (m4, 0), (m7, 0)]
-    *part_b, part_c = partner_dots(
-        after(flags, totals, core_a),
-        [(s45, 0), (s45, STEPS), (s6, 0)],
-        shards,
-        next_grads,
-        (s6, 0, depth),
-        totals,
-    )
-    keep_in, give_in = after(part_in, part_c)
+    keep_in, give_in = after(part_in, s6, m7, totals)
     core_in = keep_in + swap(give_in, "rep")
     give_in = core_in.astype(jnp.bfloat16)
     rows_here = chip_sum(core_in, give_in).astype(jnp.bfloat16)
     rows_there = swap(rows_here, "rep")
     rot_in = all_rows(rows_here, rows_there)
     rot_in = rot_in.reshape(tiles_here, TILE, 4 * cols)
+    parts = [jnp.concatenate(part, axis=1) for part in zip(part_own, part_a)]
+    keep_a, give_a = after(parts, m4, totals)
+    core_a = swap(give_a, "rep")
+
+    shards = [(basis_out, 0), (m4, 0), (m7, 0)]
+    *part_b, part_c = partner_dots(
+        after(flags, totals, core_a, core_in),
+        [(s45, 0), (s45, STEPS), (s6, 0)],
+        shards,
+        next_grads,
+        (s6, 0, depth),
+        totals,
+    )
     keep_b, give_b = part_b
     keep_b, give_b = chip_parts(
         jnp.concatenate([keep_a, keep_b], axis=1),
@@ -520,7 +520,7 @@
     sum_own, sum_a, sum_b = [sums[:, i * tok_rows : (i + 1) * tok_rows] for i in range(3)]
     sums = sums[:, 3 * tok_rows :].astype(jnp.bfloat16)
     keep_last, give_last = partner_dots(
-        after(flags, part_c, give_b, give_in),
+        after(flags, part_c, give_b),
         [(s7, 0)],
         shards,
         last_grads,
@@ -555,7 +555,7 @@
     prods_middle = tile_prods(sum_b)
     from_middle = middle(prods_middle)
     last = after(lax.ppermute(after(sum_last, rows_there), "cand", SIDE), prods_middle)
-    back = after(lax.ppermute(sums, "cand", SIDE), rows_there)
+    back = after(lax.ppermute(sums, "cand", SIDE), sum_last)
     few = tok_rows - TILE
 
     def with_partner(whole, at):

time: 151 us -> 155 us (1.026)
  starting transfers between devices: 43.5 us -> 52.6 us
  waiting for transfers between devices: 32.1 us -> 28.5 us
  local copies, waits for them, and re-layouts: 23.3 us -> 20.1 us
    ppermute x1, starting transfers between devices: 2.29 us -> 8.58 us  [line_plan(): s7 = lax.ppermute(to_s7, 'cand', SIDE)]
    ppermute x1, waiting for transfers between devices: 6.1 us -> 2.14 us  [line_plan(): s12 = lax.ppermute(rows, 'cand', SIDE)]
    ppermute x1, starting transfers between devices: 0.01 us -> 3.15 us  [line_plan(): s12 = lax.ppermute(rows, 'cand', SIDE)]
    ppermute x1, starting transfers between devices: 4.09 us -> 1.59 us  [line_plan(): back = after(lax.ppermute(sums, 'cand', SIDE), sum_last)]
    unnamed x72 -> x74, local copies, waits for them, and re-layouts: 18.3 us -> 16 us
    ppermute x2, starting transfers between devices: 11.9 us -> 13.9 us  [side(): return lax.ppermute(pick(at_end, at_middle), 'cand', SIDE)]
    ppermute x8, waiting for transfers between devices: 2.67 us -> 4.69 us  [swap(): return lax.ppermute(x, axis_name, [(0, 1), (1, 0)])]
  transfers between devices with their start and end apart: 28 -> 28, of which waited for: 9 -> 11; matrix products, arithmetic and copies ran while one was open for 11% -> 10% of each run, Pallas kernels for 17% -> 17%
where the time goes in v18:
time: 155 us; the launch traced here: 154 us
  starting transfers between devices  52.6 us (34%)
  waiting for transfers between devices  28.5 us (18%)
  Pallas kernels  26.7 us (17%)
  local copies, waits for them, and re-layouts  20.1 us (13%)
  blocking collectives  11 us (7%)
  other arithmetic  10.8 us (7%)
  matrix products  3.82 us (2%)
    unnamed x74, local copies, waits for them, and re-layouts  16 us
    ppermute x2, starting transfers between devices, side(): return lax.ppermute(pick(at_end, at_middle), 'cand', SIDE)  13.9 us
    all_to_all x1, blocking collectives, final_sum(): return jnp.sum(lax.all_to_all(blocks, ALL, 0, 0, tiled=True), axis=0)  11 us
    ppermute x1, starting transfers between devices, line_plan(): s45 = lax.ppermute(to_s45, 'cand', SIDE)  9.03 us
    ppermute x1, starting transfers between devices, line_plan(): s7 = lax.ppermute(to_s7, 'cand', SIDE)  8.58 us
    pallas_call x2, Pallas kernels, feature_dots(): pl.pallas_call(kernel, out_shape=out_shape, grid_spec=pltpu.PrefetchScala...  8.38 us
    pallas_call x2, Pallas kernels, partner_dots(): pl.pallas_call(kernel, out_shape=out_shape, grid_spec=pltpu.PrefetchScala...  7.21 us
    ppermute x1, waiting for transfers between devices, line_plan(): s45 = lax.ppermute(to_s45, 'cand', SIDE)  6.47 us
  transfers between devices with their start and end apart: 28, of which 11 were waited for; matrix products, arithmetic and copies ran while one was open for 10% of the time, Pallas kernels for 17%

profile of v18, /device:TPU:0, one launch (start us, length us, event | category | flops | bytes accessed | tf_op | source)
XLA Modules:
  0.0 154.3 jit_solution(9903027998732571624)
XLA Ops:
  0.0 3.0 %collective-permute-start = (bf16[1280,128]{1,0:T(8,128)(2,1)}, bf16[1280,128]{1,0:T(8,128)(2,1)}, u32[]{:S(2)}, u32[]{:S(2)}) collective-permute-start(bf16[1280,128]{1,0:T(8,128)(2,1)} %refs_0_.3), channel_id=1, source_target_pairs={{0,4},{4,0},{8,12},{12,8},{1,5},{5,1},{9,13},{13,9},{2,6},{6,2},{1... | collective-permute-start | bytes 983048 | tf_op jit(solution)/shard_map/ppermute | solution.py:455
  3.0 2.4 %constant_dynamic-slice_fusion = bf16[4608,128]{1,0:T(8,128)(2,1)} fusion(bf16[6912,128]{1,0:T(8,128)(2,1)} %refs_1_.1, s32[]{:T(128)S(6)} %select_n.162), kind=kLoop, calls=%fused_computation.79 | loop fusion | bytes 2359300 | tf_op jit(solution)/shard_map/dynamic_slice | solution.py:454
  5.4 3.1 %collective-permute-start.4 = (bf16[4608,128]{1,0:T(8,128)(2,1)}, bf16[4608,128]{1,0:T(8,128)(2,1)S(1)}, u32[]{:S(2)}, u32[]{:S(2)}) collective-permute-start(bf16[4608,128]{1,0:T(8,128)(2,1)} %constant_dynamic-slice_fusion), channel_id=1, source_target_pairs={{0,4},{4,0},{8,12},{12,8},{1,5},{5,1},{9,13},{13,9},{2,6},{6,2},{1... | collective-permute-start | bytes 3538952 | tf_op jit(solution)/shard_map/ppermute | solution.py:457
  9.9 3.5 %divide_convert_fusion = bf16[64,32,512]{2,1,0:T(8,128)(2,1)} fusion(bf16[64,32,512]{2,1,0:T(8,128)(2,1)} %param.13, f32[32,512]{1,0:T(8,128)S(1)} %broadcast_add_fusion), kind=kLoop, calls=%fused_computation | loop fusion | flops 3145728 | bytes 4259840 | tf_op jit(solution)/shard_map/convert_element_type | solution.py:465
  13.5 3.0 %copy-done = bf16[512,6912]{1,0:T(8,128)(2,1)S(1)} copy-done((bf16[512,6912]{1,0:T(8,128)(2,1)S(1)}, bf16[512,6912]{1,0:T(8,128)(2,1)}, u32[]{:S(2)}) %copy-start) | copy-done | bytes 7077912
  21.8 3.0 %copy-done.1 = bf16[512,6912]{1,0:T(8,128)(2,1)S(1)} copy-done((bf16[512,6912]{1,0:T(8,128)(2,1)S(1)}, bf16[512,6912]{1,0:T(8,128)(2,1)}, u32[]{:S(2)}) %copy-start.1) | copy-done | bytes 7077912
  24.8 4.6 %shard_map.82 = (f32[64,512]{1,0:T(8,128)S(1)}, f32[64,512]{1,0:T(8,128)S(1)}) custom-call(s32[6]{0:T(128)S(1)} %stack.36.flags_ref, bf16[512,6912]{1,0:T(8,128)(2,1)S(1)} %copy-done.1, bf16[6912,128]{1,0:T(8,128)(2,1)S(1)} %copy-done.2), custom_call_target="tpu_custom_call" | custom-call | flops 1 | bytes 1 | tf_op jit(solution)/shard_map/pallas_call | solution.py:161
  29.8 5.2 %collective-permute-start.3 = (bf16[2560,128]{1,0:T(8,128)(2,1)S(1)}, bf16[2560,128]{1,0:T(8,128)(2,1)S(1)}, u32[]{:S(2)}, u32[]{:S(2)}) collective-permute-start(bf16[2560,128]{1,0:T(8,128)(2,1)S(1)} %maximum_select_fusion.1), channel_id=1, source_target_pairs={{0,4},{4,0},{8,12},{12,8},{1,5},{5,1},{9,13},{13,9},{2,6},{6,2},{1... | collective-permute-start | bytes 1966088 | tf_op jit(solution)/shard_map/ppermute | solution.py:437
  39.8 9.0 %collective-permute-start.9 = (bf16[4608,128]{1,0:T(8,128)(2,1)S(1)}, bf16[4608,128]{1,0:T(8,128)(2,1)S(1)}, u32[]{:S(2)}, u32[]{:S(2)}) collective-permute-start(bf16[4608,128]{1,0:T(8,128)(2,1)S(1)} %maximum_select_fusion), channel_id=1, source_target_pairs={{0,4},{4,0},{8,12},{12,8},{1,5},{5,1},{9,13},{13,9},{2,6},{6,2},{1... | collective-permute-start | bytes 3538952 | tf_op jit(solution)/shard_map/ppermute | solution.py:472
  48.9 2.2 %collective-permute-done.3.refs_2_.refs_4_.refs_1_ = bf16[2560,128]{1,0:T(8,128)(2,1)S(1)} collective-permute-done((bf16[2560,128]{1,0:T(8,128)(2,1)S(1)}, bf16[2560,128]{1,0:T(8,128)(2,1)S(1)}, u32[]{:S(2)}, u32[]{:S(2)}) %collective-permute-start.3) | collective-permute-done | bytes 655392 | tf_op jit(solution)/shard_map/ppermute | solution.py:437
  51.3 8.8 %collective-permute-start.12 = (bf16[2304,128]{1,0:T(8,128)(2,1)S(1)}, bf16[2304,128]{1,0:T(8,128)(2,1)S(1)}, u32[]{:S(2)}, u32[]{:S(2)}) collective-permute-start(bf16[2304,128]{1,0:T(8,128)(2,1)S(1)} %broadcast_select_fusion), channel_id=1, source_target_pairs={{0,4},{4,0},{8,12},{12,8},{1,5},{5,1},{9,13},{13,9},{2,6},{6,2},{1... | collective-permute-start | bytes 1769480 | tf_op jit(solution)/shard_map/ppermute | solution.py:437
  60.1 4.6 %shard_map.83 = (f32[256,512]{1,0:T(8,128)S(1)}, f32[256,512]{1,0:T(8,128)}) custom-call(s32[6]{0:T(128)S(1)} %stack.36.flags_ref, bf16[512,1280]{1,0:T(8,128)(2,1)S(1)} %copy-done.13, bf16[1280,128]{1,0:T(8,128)(2,1)S(1)} %copy-done.24, bf16[1280,128]{1,0:T(8,128)(2,1)} %collective-permute-done.refs_1_, ...), custom_call_target="tpu_custom_call" | custom-call | flops 1 | bytes 1 | tf_op jit(solution)/shard_map/pallas_call | solution.py:408
  65.5 3.8 %shard_map.84 = (f32[64,512]{1,0:T(8,128)S(1)}, f32[64,512]{1,0:T(8,128)S(1)}) custom-call(s32[6]{0:T(128)S(1)} %stack.36.flags_ref, bf16[512,6912]{1,0:T(8,128)(2,1)S(1)} %bitcast.48, bf16[4608,128]{1,0:T(8,128)(2,1)S(1)} %copy-done.4, bf16[2560,128]{1,0:T(8,128)(2,1)S(1)} %collective-permute-done.3.refs_2_.refs_4_.refs_1_), custom_call_target="tpu_custom_call" | custom-call | flops 1 | bytes 1 | tf_op jit(solution)/shard_map/pallas_call | solution.py:161
  69.9 6.5 %collective-permute-done.9.end_ref.refs_0_.refs_1_ = bf16[4608,128]{1,0:T(8,128)(2,1)S(1)} collective-permute-done((bf16[4608,128]{1,0:T(8,128)(2,1)S(1)}, bf16[4608,128]{1,0:T(8,128)(2,1)S(1)}, u32[]{:S(2)}, u32[]{:S(2)}) %collective-permute-start.9) | collective-permute-done | bytes 1179680 | tf_op jit(solution)/shard_map/ppermute | solution.py:472
  77.3 5.2 %shard_map.86 = (f32[512,256]{1,0:T(8,128)S(1)}, bf16[512,2304]{1,0:T(8,128)(2,1)S(1)}, bf16[512,2304]{1,0:T(8,128)(2,1)S(1)}) custom-call(s32[6]{0:T(128)S(1)} %stack.36.flags_ref, bf16[512,6912]{1,0:T(8,128)(2,1)S(1)} %bitcast.48, bf16[4608,128]{1,0:T(8,128)(2,1)S(1)} %collective-permute-done.9.end_ref.refs_0_.refs_1_, ...), custom_call_target="tpu_custom_call" | custom-call | flops 1 | bytes 1 | tf_op jit(solution)/shard_map/pallas_call | solution.py:233
  90.4 8.6 %collective-permute-start.20 = (bf16[2304,128]{1,0:T(8,128)(2,1)}, bf16[2304,128]{1,0:T(8,128)(2,1)S(1)}, u32[]{:S(2)}, u32[]{:S(2)}) collective-permute-start(bf16[2304,128]{1,0:T(8,128)(2,1)} %broadcast_select_fusion.1), channel_id=1, source_target_pairs={{0,4},{4,0},{8,12},{12,8},{1,5},{5,1},{9,13},{13,9},{2,6},{6,2},{1... | collective-permute-start | bytes 1769480 | tf_op jit(solution)/shard_map/ppermute | solution.py:477
  103.1 3.6 %shard_map.87 = (f32[64,1664]{1,0:T(8,128)S(1)}, f32[64,1664]{1,0:T(8,128)S(1)}, f32[512,128]{1,0:T(8,128)S(1)}) custom-call(s32[6]{0:T(128)S(1)} %stack.36.flags_ref, bf16[4608,128]{1,0:T(8,128)(2,1)S(1)} %collective-permute-done.9.end_ref.refs_0_.refs_1_, bf16[4608,128]{1,0:T(8,128)(2,1)S(1)} %collective-permute-done.9.end_ref.refs_0_.refs_1_, ...), custom_call_target="tpu_custom_call" | custom-call | flops 1 | bytes 1 | tf_op jit(solution)/shard_map/pallas_call | solution.py:325
  110.8 2.4 %collective-permute-done.20.refs_0_.refs_4_ = bf16[2304,128]{1,0:T(8,128)(2,1)S(1)} collective-permute-done((bf16[2304,128]{1,0:T(8,128)(2,1)}, bf16[2304,128]{1,0:T(8,128)(2,1)S(1)}, u32[]{:S(2)}, u32[]{:S(2)}) %collective-permute-start.20) | collective-permute-done | bytes 589856 | tf_op jit(solution)/shard_map/ppermute | solution.py:477
  113.2 3.6 %shard_map.88 = (f32[64,896]{1,0:T(8,128)S(1)}, f32[64,896]{1,0:T(8,128)S(1)}) custom-call(s32[6]{0:T(128)S(1)} %stack.36.flags_ref, bf16[2304,128]{1,0:T(8,128)(2,1)S(1)} %collective-permute-done.20.refs_0_.refs_4_, bf16[6912,128]{1,0:T(8,128)(2,1)S(1)} %copy-done.2, bf16[2304,128]{1,0:T(8,128)(2,1)} %collective-permute-done.6.refs_4_.refs_2_, ...), custom_call_target="tpu_custom_call" | custom-call | flops 1 | bytes 1 | tf_op jit(solution)/shard_map/pallas_call | solution.py:325
  121.1 2.5 %collective-permute-done.22 = bf16[32,896]{1,0:T(8,128)(2,1)S(1)} collective-permute-done((bf16[32,896]{1,0:T(8,128)(2,1)S(1)}, bf16[32,896]{1,0:T(8,128)(2,1)S(1)}, u32[]{:S(2)}, u32[]{:S(2)}) %collective-permute-start.22) | collective-permute-done | bytes 57376 | tf_op jit(solution)/shard_map/ppermute | solution.py:37
  129.8 2.6 %collective-permute-start.26 = (bf16[4,32,512]{2,1,0:T(8,128)(2,1)S(1)}, bf16[4,32,512]{2,1,0:T(8,128)(2,1)S(1)}, u32[]{:S(2)}, u32[]{:S(2)}) collective-permute-start(bf16[4,32,512]{2,1,0:T(8,128)(2,1)S(1)} %convolution_convert_fusion), channel_id=1, source_target_pairs={{0,12},{1,13},{2,14},{3,15},{4,5},{5,4},{6,7},{7,6},{8,9},{9,8},{1... | collective-permute-start | bytes 393224 | tf_op jit(solution)/shard_map/ppermute | solution.py:571
  132.7 5.3 %collective-permute-done.26 = bf16[4,32,512]{2,1,0:T(8,128)(2,1)S(1)} collective-permute-done((bf16[4,32,512]{2,1,0:T(8,128)(2,1)S(1)}, bf16[4,32,512]{2,1,0:T(8,128)(2,1)S(1)}, u32[]{:S(2)}, u32[]{:S(2)}) %collective-permute-start.26) | collective-permute-done | bytes 131104 | tf_op jit(solution)/shard_map/ppermute | solution.py:571
  139.6 2.8 %fusion.3 = f32[16,64]{1,0:T(8,128)S(1)} fusion(bf16[64,32,512]{2,1,0:T(8,128)(2,1)S(1)} %copy-done.30, bf16[16,32,512]{2,1,0:T(8,128)(2,1)S(1)} %pad_maximum_fusion.1), kind=kOutput, calls=%fused_computation.10 | convolution fusion | flops 33554432 | bytes 2625536 | tf_op jit(solution)/shard_map/tea,jea->tj/dot_general | solution.py:547
  142.6 11.0 %all_to_all.5 = f32[16,2,16]{2,1,0:T(2,128)S(1)} all-to-all(f32[16,2,16]{2,1,0:T(2,128)S(1)} %copy.49), channel_id=1, replica_groups=mesh['groups'=2,'cand'=4,'eig'=2,'rep'=2] {'cand','eig','rep'}, dimensions={0} | all-to-all | bytes 4096 | tf_op jit(solution)/shard_map/all_to_all | solution.py:586
  (171 shorter events, 43.2 us)
Async XLA Ops:
  0.0 20.9 %collective-permute-start = (bf16[1280,128]{1,0:T(8,128)(2,1)}, bf16[1280,128]{1,0:T(8,128)(2,1)}, u32[]{:S(2)}, u32[]{:S(2)}) collective-permute-start(bf16[1280,128]{1,0:T(8,128)(2,1)} %refs_0_.3), channel_id=1, source_target_pairs={{0,4},{4,0},{8,12},{12,8},{1,5},{5,1},{9,13},{13,9},{2,6},{6,2},{1... | collective-permute-start | bytes 983048 | tf_op jit(solution)/shard_map/ppermute | solution.py:455
  3.0 17.8 %collective-permute-start.1 = (bf16[1280,128]{1,0:T(8,128)(2,1)}, bf16[1280,128]{1,0:T(8,128)(2,1)S(1)}, u32[]{:S(2)}, u32[]{:S(2)}) collective-permute-start(bf16[1280,128]{1,0:T(8,128)(2,1)} %refs_0_.3), channel_id=1, source_target_pairs={{0,1},{1,0},{2,3},{3,2},{4,8},{5,9},{6,10},{7,11},{8,4},{9,5},{10,... | collective-permute-start | bytes 983048 | tf_op jit(solution)/shard_map/ppermute | solution.py:447
  5.4 31.6 %collective-permute-start.4 = (bf16[4608,128]{1,0:T(8,128)(2,1)}, bf16[4608,128]{1,0:T(8,128)(2,1)S(1)}, u32[]{:S(2)}, u32[]{:S(2)}) collective-permute-start(bf16[4608,128]{1,0:T(8,128)(2,1)} %constant_dynamic-slice_fusion), channel_id=1, source_target_pairs={{0,4},{4,0},{8,12},{12,8},{1,5},{5,1},{9,13},{13,9},{2,6},{6,2},{1... | collective-permute-start | bytes 3538952 | tf_op jit(solution)/shard_map/ppermute | solution.py:457
  9.8 27.4 %collective-permute-start.7 = (bf16[2304,128]{1,0:T(8,128)(2,1)}, bf16[2304,128]{1,0:T(8,128)(2,1)}, u32[]{:S(2)}, u32[]{:S(2)}) collective-permute-start(bf16[2304,128]{1,0:T(8,128)(2,1)} %get-tuple-element.92), channel_id=1, source_target_pairs={{0,1},{1,0},{2,3},{3,2},{4,8},{5,9},{6,10},{7,11},{8,4},{9,5},{10,... | collective-permute-start | bytes 1769480 | tf_op jit(solution)/shard_map/ppermute | solution.py:447
  20.9 8.7 %collective-permute-start.2 = (bf16[1280,128]{1,0:T(8,128)(2,1)}, bf16[1280,128]{1,0:T(8,128)(2,1)S(1)}, u32[]{:S(2)}, u32[]{:S(2)}) collective-permute-start(bf16[1280,128]{1,0:T(8,128)(2,1)} %collective-permute-done.refs_1_), channel_id=1, source_target_pairs={{0,1},{1,0},{2,3},{3,2},{4,8},{5,9},{6,10},{7,11},{8,4},{9,5},{10,... | collective-permute-start | bytes 983048 | tf_op jit(solution)/shard_map/ppermute | solution.py:447
  29.4 7.8 %collective-permute-start.8 = (bf16[2304,128]{1,0:T(8,128)(2,1)S(1)}, bf16[2304,128]{1,0:T(8,128)(2,1)S(1)}, u32[]{:S(2)}, u32[]{:S(2)}) collective-permute-start(bf16[2304,128]{1,0:T(8,128)(2,1)S(1)} %copy-done.29), channel_id=1, source_target_pairs={{0,1},{1,0},{2,3},{3,2},{4,8},{5,9},{6,10},{7,11},{8,4},{9,5},{10,... | collective-permute-start | bytes 1769480 | tf_op jit(solution)/shard_map/ppermute | solution.py:447
  29.8 21.3 %collective-permute-start.3 = (bf16[2560,128]{1,0:T(8,128)(2,1)S(1)}, bf16[2560,128]{1,0:T(8,128)(2,1)S(1)}, u32[]{:S(2)}, u32[]{:S(2)}) collective-permute-start(bf16[2560,128]{1,0:T(8,128)(2,1)S(1)} %maximum_select_fusion.1), channel_id=1, source_target_pairs={{0,4},{4,0},{8,12},{12,8},{1,5},{5,1},{9,13},{13,9},{2,6},{6,2},{1... | collective-permute-start | bytes 1966088 | tf_op jit(solution)/shard_map/ppermute | solution.py:437
  37.2 14.0 %collective-permute-start.5 = (bf16[2304,128]{1,0:T(8,128)(2,1)S(1)}, bf16[2304,128]{1,0:T(8,128)(2,1)S(1)}, u32[]{:S(2)}, u32[]{:S(2)}) collective-permute-start(bf16[2304,128]{1,0:T(8,128)(2,1)S(1)} %get-tuple-element.94), channel_id=1, source_target_pairs={{0,1},{1,0},{2,3},{3,2},{4,8},{5,9},{6,10},{7,11},{8,4},{9,5},{10,... | collective-permute-start | bytes 1769480 | tf_op jit(solution)/shard_map/ppermute | solution.py:447
  39.8 36.6 %collective-permute-start.9 = (bf16[4608,128]{1,0:T(8,128)(2,1)S(1)}, bf16[4608,128]{1,0:T(8,128)(2,1)S(1)}, u32[]{:S(2)}, u32[]{:S(2)}) collective-permute-start(bf16[4608,128]{1,0:T(8,128)(2,1)S(1)} %maximum_select_fusion), channel_id=1, source_target_pairs={{0,4},{4,0},{8,12},{12,8},{1,5},{5,1},{9,13},{13,9},{2,6},{6,2},{1... | collective-permute-start | bytes 3538952 | tf_op jit(solution)/shard_map/ppermute | solution.py:472
  51.1 18.2 %collective-permute-start.10 = (bf16[2304,128]{1,0:T(8,128)(2,1)S(1)}, bf16[2304,128]{1,0:T(8,128)(2,1)S(1)}, u32[]{:S(2)}, u32[]{:S(2)}) collective-permute-start(bf16[2304,128]{1,0:T(8,128)(2,1)S(1)} %slice.81), channel_id=1, source_target_pairs={{0,1},{1,0},{2,3},{3,2},{4,8},{5,9},{6,10},{7,11},{8,4},{9,5},{10,... | collective-permute-start | bytes 1769480 | tf_op jit(solution)/shard_map/ppermute | solution.py:447
  51.3 36.9 %collective-permute-start.12 = (bf16[2304,128]{1,0:T(8,128)(2,1)S(1)}, bf16[2304,128]{1,0:T(8,128)(2,1)S(1)}, u32[]{:S(2)}, u32[]{:S(2)}) collective-permute-start(bf16[2304,128]{1,0:T(8,128)(2,1)S(1)} %broadcast_select_fusion), channel_id=1, source_target_pairs={{0,4},{4,0},{8,12},{12,8},{1,5},{5,1},{9,13},{13,9},{2,6},{6,2},{1... | collective-permute-start | bytes 1769480 | tf_op jit(solution)/shard_map/ppermute | solution.py:437
  65.5 33.5 %collective-permute-start.6 = (bf16[2304,128]{1,0:T(8,128)(2,1)}, bf16[2304,128]{1,0:T(8,128)(2,1)}, u32[]{:S(2)}, u32[]{:S(2)}) collective-permute-start(bf16[2304,128]{1,0:T(8,128)(2,1)} %get-tuple-element.54), channel_id=1, source_target_pairs={{0,1},{1,0},{2,3},{3,2},{4,8},{5,9},{6,10},{7,11},{8,4},{9,5},{10,... | collective-permute-start | bytes 1769480 | tf_op jit(solution)/shard_map/ppermute | solution.py:447
  69.3 18.8 %collective-permute-start.13 = (bf16[2304,128]{1,0:T(8,128)(2,1)S(1)}, bf16[2304,128]{1,0:T(8,128)(2,1)S(1)}, u32[]{:S(2)}, u32[]{:S(2)}) collective-permute-start(bf16[2304,128]{1,0:T(8,128)(2,1)S(1)} %get-tuple-element.64), channel_id=1, source_target_pairs={{0,1},{1,0},{2,3},{3,2},{4,8},{5,9},{6,10},{7,11},{8,4},{9,5},{10,... | collective-permute-start | bytes 1769480 | tf_op jit(solution)/shard_map/ppermute | solution.py:447
  89.0 10.2 %collective-permute-start.14 = (f32[256,512]{1,0:T(8,128)}, f32[256,512]{1,0:T(8,128)}, u32[]{:S(2)}, u32[]{:S(2)}) collective-permute-start(f32[256,512]{1,0:T(8,128)} %get-tuple-element.66), channel_id=1, source_target_pairs={{0,1},{1,0},{2,3},{3,2},{4,5},{5,4},{6,7},{7,6},{8,9},{9,8},{10,11... | collective-permute-start | bytes 1572872 | tf_op jit(solution)/shard_map/ppermute | solution.py:37
  90.4 22.8 %collective-permute-start.20 = (bf16[2304,128]{1,0:T(8,128)(2,1)}, bf16[2304,128]{1,0:T(8,128)(2,1)S(1)}, u32[]{:S(2)}, u32[]{:S(2)}) collective-permute-start(bf16[2304,128]{1,0:T(8,128)(2,1)} %broadcast_select_fusion.1), channel_id=1, source_target_pairs={{0,4},{4,0},{8,12},{12,8},{1,5},{5,1},{9,13},{13,9},{2,6},{6,2},{1... | collective-permute-start | bytes 1769480 | tf_op jit(solution)/shard_map/ppermute | solution.py:477
  100.4 8.6 %collective-permute-start.17 = (bf16[256,512]{1,0:T(8,128)(2,1)S(1)}, bf16[256,512]{1,0:T(8,128)(2,1)S(1)}, u32[]{:S(2)}, u32[]{:S(2)}) collective-permute-start(bf16[256,512]{1,0:T(8,128)(2,1)S(1)} %get-tuple-element.88), channel_id=1, source_target_pairs={{0,2},{2,0},{1,3},{3,1},{4,6},{6,4},{5,7},{7,5},{8,10},{10,8},{9,1... | collective-permute-start | bytes 786440 | tf_op jit(solution)/shard_map/ppermute | solution.py:37
  109.1 7.9 %collective-permute-start.18 = (bf16[256,512]{1,0:T(8,128)(2,1)S(1)}, bf16[256,512]{1,0:T(8,128)(2,1)S(1)}, u32[]{:S(2)}, u32[]{:S(2)}) collective-permute-start(bf16[256,512]{1,0:T(8,128)(2,1)S(1)} %add_convert_fusion), channel_id=1, source_target_pairs={{0,1},{1,0},{2,3},{3,2},{4,5},{5,4},{6,7},{7,6},{8,9},{9,8},{10,11... | collective-permute-start | bytes 786440 | tf_op jit(solution)/shard_map/ppermute | solution.py:37
  109.3 7.8 %collective-permute-start.16 = (bf16[32,2688]{1,0:T(8,128)(2,1)S(1)}, bf16[32,2688]{1,0:T(8,128)(2,1)S(1)}, u32[]{:S(2)}, u32[]{:S(2)}) collective-permute-start(bf16[32,2688]{1,0:T(8,128)(2,1)S(1)} %add_convert_fusion.1), channel_id=1, source_target_pairs={{0,2},{2,0},{1,3},{3,1},{4,6},{6,4},{5,7},{7,5},{8,10},{10,8},{9,1... | collective-permute-start | bytes 516104 | tf_op jit(solution)/shard_map/ppermute | solution.py:37
  117.2 8.5 %collective-permute-start.19 = (bf16[32,1152]{1,0:T(8,128)(2,1)S(1)}, bf16[32,1152]{1,0:T(8,128)(2,1)S(1)}, u32[]{:S(2)}, u32[]{:S(2)}) collective-permute-start(bf16[32,1152]{1,0:T(8,128)(2,1)S(1)} %slice.85), channel_id=1, source_target_pairs={{0,4},{4,0},{8,12},{12,8},{1,5},{5,1},{9,13},{13,9},{2,6},{6,2},{1... | collective-permute-start | bytes 221192 | tf_op jit(solution)/shard_map/ppermute | solution.py:558
  119.0 13.7 %collective-permute-start.27 = (bf16[4,32,512]{2,1,0:T(8,128)(2,1)S(1)}, bf16[4,32,512]{2,1,0:T(8,128)(2,1)S(1)}, u32[]{:S(2)}, u32[]{:S(2)}) collective-permute-start(bf16[4,32,512]{2,1,0:T(8,128)(2,1)S(1)} %convolution_convert_fusion.3), channel_id=1, source_target_pairs={{0,1},{1,0},{2,3},{3,2},{4,8},{5,9},{6,10},{7,11},{8,4},{9,5},{10,... | collective-permute-start | bytes 393224 | tf_op jit(solution)/shard_map/ppermute | solution.py:447
  119.3 4.2 %collective-permute-start.22 = (bf16[32,896]{1,0:T(8,128)(2,1)S(1)}, bf16[32,896]{1,0:T(8,128)(2,1)S(1)}, u32[]{:S(2)}, u32[]{:S(2)}) collective-permute-start(bf16[32,896]{1,0:T(8,128)(2,1)S(1)} %add_convert_fusion.2), channel_id=1, source_target_pairs={{0,2},{2,0},{1,3},{3,1},{4,6},{6,4},{5,7},{7,5},{8,10},{10,8},{9,1... | collective-permute-start | bytes 172040 | tf_op jit(solution)/shard_map/ppermute | solution.py:37
  128.0 10.2 %collective-permute-start.25 = (bf16[4,32,512]{2,1,0:T(8,128)(2,1)S(1)}, bf16[4,32,512]{2,1,0:T(8,128)(2,1)S(1)}, u32[]{:S(2)}, u32[]{:S(2)}) collective-permute-start(bf16[4,32,512]{2,1,0:T(8,128)(2,1)S(1)} %fusion.2), channel_id=1, source_target_pairs={{0,8},{8,0},{4,12},{12,4},{1,9},{9,1},{5,13},{13,5},{2,10},{10,2},... | collective-permute-start | bytes 393224 | tf_op jit(solution)/shard_map/ppermute | solution.py:570
  129.8 8.2 %collective-permute-start.26 = (bf16[4,32,512]{2,1,0:T(8,128)(2,1)S(1)}, bf16[4,32,512]{2,1,0:T(8,128)(2,1)S(1)}, u32[]{:S(2)}, u32[]{:S(2)}) collective-permute-start(bf16[4,32,512]{2,1,0:T(8,128)(2,1)S(1)} %convolution_convert_fusion), channel_id=1, source_target_pairs={{0,12},{1,13},{2,14},{3,15},{4,5},{5,4},{6,7},{7,6},{8,9},{9,8},{1... | collective-permute-start | bytes 393224 | tf_op jit(solution)/shard_map/ppermute | solution.py:571
  132.6 6.9 %collective-permute-start.24 = (bf16[4,32,512]{2,1,0:T(8,128)(2,1)S(1)}, bf16[4,32,512]{2,1,0:T(8,128)(2,1)S(1)}, u32[]{:S(2)}, u32[]{:S(2)}) collective-permute-start(bf16[4,32,512]{2,1,0:T(8,128)(2,1)S(1)} %convolution_convert_fusion.2), channel_id=1, source_target_pairs={{0,4},{4,0},{8,12},{12,8},{1,5},{5,1},{9,13},{13,9},{2,6},{6,2},{1... | collective-permute-start | bytes 393224 | tf_op jit(solution)/shard_map/ppermute | solution.py:572
  (41 other events, 337.5 us)

commit v19 on v17

--- a/solution.py
+++ b/solution.py
@@ -504,7 +504,7 @@
         (s6, 0, depth),
         totals,
     )
-    keep_in, give_in = after(part_in, part_c)
+    keep_in, give_in = after(part_in, m7, totals, core_a)
     core_in = keep_in + swap(give_in, "rep")
     give_in = core_in.astype(jnp.bfloat16)
     rows_here = chip_sum(core_in, give_in).astype(jnp.bfloat16)
@@ -554,7 +554,7 @@
     prods_own = tile_prods(sum_own)
     prods_middle = tile_prods(sum_b)
     from_middle = middle(prods_middle)
-    last = after(lax.ppermute(after(sum_last, rows_there), "cand", SIDE), prods_middle)
+    last = after(lax.ppermute(after(sum_last, rows_here), "cand", SIDE), prods_middle)
     back = after(lax.ppermute(sums, "cand", SIDE), rows_there)
     few = tok_rows - TILE
 

time: 151 us -> 152 us (level)
  starting transfers between devices: 43.5 us -> 51.2 us
  waiting for transfers between devices: 32.1 us -> 25 us
    ppermute x1, waiting for transfers between devices: 6.1 us -> 2.14 us  [line_plan(): s12 = lax.ppermute(rows, 'cand', SIDE)]
    ppermute x2, starting transfers between devices: 11.9 us -> 15.4 us  [side(): return lax.ppermute(pick(at_end, at_middle), 'cand', SIDE)]
    ppermute x1, starting transfers between devices: 0.01 us -> 3.15 us  [line_plan(): s12 = lax.ppermute(rows, 'cand', SIDE)]
    ppermute x1, waiting for transfers between devices: 7.66 us -> 4.83 us  [line_plan(): s45 = lax.ppermute(to_s45, 'cand', SIDE)]
    ppermute x1, starting transfers between devices: 4.09 us -> 6.74 us  [line_plan(): back = after(lax.ppermute(sums, 'cand', SIDE), rows_there)]
  transfers between devices with their start and end apart: 28 -> 28, of which waited for: 9 -> 10; matrix products, arithmetic and copies ran while one was open for 11% -> 11% of each run, Pallas kernels for 17% -> 17%
where the time goes in v19:
time: 152 us; the launch traced here: 151 us
  starting transfers between devices  51.2 us (34%)
  Pallas kernels  25.9 us (17%)
  waiting for transfers between devices  25 us (16%)
  local copies, waits for them, and re-layouts  23.3 us (15%)
  blocking collectives  11 us (7%)
  other arithmetic  10.1 us (7%)
  matrix products  3.81 us (3%)
    unnamed x72, local copies, waits for them, and re-layouts  18.3 us
    ppermute x2, starting transfers between devices, side(): return lax.ppermute(pick(at_end, at_middle), 'cand', SIDE)  15.4 us
    all_to_all x1, blocking collectives, final_sum(): return jnp.sum(lax.all_to_all(blocks, ALL, 0, 0, tiled=True), axis=0)  11 us
    ppermute x1, starting transfers between devices, line_plan(): s45 = lax.ppermute(to_s45, 'cand', SIDE)  8.9 us
    pallas_call x2, Pallas kernels, feature_dots(): pl.pallas_call(kernel, out_shape=out_shape, grid_spec=pltpu.PrefetchScala...  8.37 us
    pallas_call x2, Pallas kernels, partner_dots(): pl.pallas_call(kernel, out_shape=out_shape, grid_spec=pltpu.PrefetchScala...  7.21 us
    ppermute x1, starting transfers between devices, line_plan(): back = after(lax.ppermute(sums, 'cand', SIDE), rows_there)  6.74 us
    ppermute x1, waiting for transfers between devices, line_plan(): from_far = lax.ppermute(after(prods_c, to_two), ALL, far)  6.58 us
  transfers between devices with their start and end apart: 28, of which 10 were waited for; matrix products, arithmetic and copies ran while one was open for 11% of the time, Pallas kernels for 17%

profile of v19, /device:TPU:0, one launch (start us, length us, event | category | flops | bytes accessed | tf_op | source)
XLA Modules:
  0.0 150.9 jit_solution(399386900202512174)
XLA Ops:
  0.0 3.0 %collective-permute-start = (bf16[1280,128]{1,0:T(8,128)(2,1)}, bf16[1280,128]{1,0:T(8,128)(2,1)}, u32[]{:S(2)}, u32[]{:S(2)}) collective-permute-start(bf16[1280,128]{1,0:T(8,128)(2,1)} %refs_0_.3), channel_id=1, source_target_pairs={{0,4},{4,0},{8,12},{12,8},{1,5},{5,1},{9,13},{13,9},{2,6},{6,2},{1... | collective-permute-start | bytes 983048 | tf_op jit(solution)/shard_map/ppermute | solution.py:455
  3.0 2.4 %constant_dynamic-slice_fusion = bf16[4608,128]{1,0:T(8,128)(2,1)} fusion(bf16[6912,128]{1,0:T(8,128)(2,1)} %refs_1_.1, s32[]{:T(128)S(6)} %select_n.162), kind=kLoop, calls=%fused_computation.79 | loop fusion | bytes 2359300 | tf_op jit(solution)/shard_map/dynamic_slice | solution.py:454
  5.4 3.1 %collective-permute-start.4 = (bf16[4608,128]{1,0:T(8,128)(2,1)}, bf16[4608,128]{1,0:T(8,128)(2,1)S(1)}, u32[]{:S(2)}, u32[]{:S(2)}) collective-permute-start(bf16[4608,128]{1,0:T(8,128)(2,1)} %constant_dynamic-slice_fusion), channel_id=1, source_target_pairs={{0,4},{4,0},{8,12},{12,8},{1,5},{5,1},{9,13},{13,9},{2,6},{6,2},{1... | collective-permute-start | bytes 3538952 | tf_op jit(solution)/shard_map/ppermute | solution.py:457
  9.8 3.5 %divide_convert_fusion = bf16[64,32,512]{2,1,0:T(8,128)(2,1)} fusion(bf16[64,32,512]{2,1,0:T(8,128)(2,1)} %param.13, f32[32,512]{1,0:T(8,128)S(1)} %broadcast_add_fusion), kind=kLoop, calls=%fused_computation | loop fusion | flops 3145728 | bytes 4259840 | tf_op jit(solution)/shard_map/convert_element_type | solution.py:465
  13.5 3.0 %copy-done = bf16[512,6912]{1,0:T(8,128)(2,1)S(1)} copy-done((bf16[512,6912]{1,0:T(8,128)(2,1)S(1)}, bf16[512,6912]{1,0:T(8,128)(2,1)}, u32[]{:S(2)}) %copy-start) | copy-done | bytes 7077912
  21.8 3.0 %copy-done.1 = bf16[512,6912]{1,0:T(8,128)(2,1)S(1)} copy-done((bf16[512,6912]{1,0:T(8,128)(2,1)S(1)}, bf16[512,6912]{1,0:T(8,128)(2,1)}, u32[]{:S(2)}) %copy-start.1) | copy-done | bytes 7077912
  24.8 4.6 %shard_map.82 = (f32[64,512]{1,0:T(8,128)S(1)}, f32[64,512]{1,0:T(8,128)S(1)}) custom-call(s32[6]{0:T(128)S(1)} %stack.36.flags_ref, bf16[512,6912]{1,0:T(8,128)(2,1)S(1)} %copy-done.1, bf16[6912,128]{1,0:T(8,128)(2,1)S(1)} %copy-done.2), custom_call_target="tpu_custom_call" | custom-call | flops 1 | bytes 1 | tf_op jit(solution)/shard_map/pallas_call | solution.py:161
  29.7 5.2 %collective-permute-start.3 = (bf16[2560,128]{1,0:T(8,128)(2,1)S(1)}, bf16[2560,128]{1,0:T(8,128)(2,1)S(1)}, u32[]{:S(2)}, u32[]{:S(2)}) collective-permute-start(bf16[2560,128]{1,0:T(8,128)(2,1)S(1)} %maximum_select_fusion.1), channel_id=1, source_target_pairs={{0,4},{4,0},{8,12},{12,8},{1,5},{5,1},{9,13},{13,9},{2,6},{6,2},{1... | collective-permute-start | bytes 1966088 | tf_op jit(solution)/shard_map/ppermute | solution.py:437
  39.9 8.9 %collective-permute-start.9 = (bf16[4608,128]{1,0:T(8,128)(2,1)S(1)}, bf16[4608,128]{1,0:T(8,128)(2,1)S(1)}, u32[]{:S(2)}, u32[]{:S(2)}) collective-permute-start(bf16[4608,128]{1,0:T(8,128)(2,1)S(1)} %maximum_select_fusion), channel_id=1, source_target_pairs={{0,4},{4,0},{8,12},{12,8},{1,5},{5,1},{9,13},{13,9},{2,6},{6,2},{1... | collective-permute-start | bytes 3538952 | tf_op jit(solution)/shard_map/ppermute | solution.py:472
  51.3 3.9 %shard_map.83 = (f32[256,512]{1,0:T(8,128)S(1)}, f32[256,512]{1,0:T(8,128)S(1)}) custom-call(s32[6]{0:T(128)S(1)} %stack.36.flags_ref, bf16[512,1280]{1,0:T(8,128)(2,1)S(1)} %copy-done.12, bf16[1280,128]{1,0:T(8,128)(2,1)S(1)} %copy-done.23, bf16[1280,128]{1,0:T(8,128)(2,1)} %collective-permute-done.refs_1_, ...), custom_call_target="tpu_custom_call" | custom-call | flops 1 | bytes 1 | tf_op jit(solution)/shard_map/pallas_call | solution.py:408
  56.7 10.2 %collective-permute-start.12 = (bf16[2304,128]{1,0:T(8,128)(2,1)}, bf16[2304,128]{1,0:T(8,128)(2,1)S(1)}, u32[]{:S(2)}, u32[]{:S(2)}) collective-permute-start(bf16[2304,128]{1,0:T(8,128)(2,1)} %broadcast_select_fusion), channel_id=1, source_target_pairs={{0,4},{4,0},{8,12},{12,8},{1,5},{5,1},{9,13},{13,9},{2,6},{6,2},{1... | collective-permute-start | bytes 1769480 | tf_op jit(solution)/shard_map/ppermute | solution.py:437
  66.9 3.8 %shard_map.84 = (f32[64,512]{1,0:T(8,128)S(1)}, f32[64,512]{1,0:T(8,128)S(1)}) custom-call(s32[6]{0:T(128)S(1)} %stack.36.flags_ref, bf16[512,6912]{1,0:T(8,128)(2,1)S(1)} %bitcast.48, bf16[4608,128]{1,0:T(8,128)(2,1)S(1)} %copy-done.4, bf16[2560,128]{1,0:T(8,128)(2,1)S(1)} %collective-permute-done.3.refs_2_.refs_4_.refs_1_), custom_call_target="tpu_custom_call" | custom-call | flops 1 | bytes 1 | tf_op jit(solution)/shard_map/pallas_call | solution.py:161
  71.5 4.8 %collective-permute-done.9.end_ref.refs_0_.refs_1_ = bf16[4608,128]{1,0:T(8,128)(2,1)S(1)} collective-permute-done((bf16[4608,128]{1,0:T(8,128)(2,1)S(1)}, bf16[4608,128]{1,0:T(8,128)(2,1)S(1)}, u32[]{:S(2)}, u32[]{:S(2)}) %collective-permute-start.9) | collective-permute-done | bytes 1179680 | tf_op jit(solution)/shard_map/ppermute | solution.py:472
  77.3 5.2 %shard_map.86 = (f32[512,256]{1,0:T(8,128)S(1)}, bf16[512,2304]{1,0:T(8,128)(2,1)S(1)}, bf16[512,2304]{1,0:T(8,128)(2,1)S(1)}) custom-call(s32[6]{0:T(128)S(1)} %stack.36.flags_ref, bf16[512,6912]{1,0:T(8,128)(2,1)S(1)} %bitcast.48, bf16[4608,128]{1,0:T(8,128)(2,1)S(1)} %collective-permute-done.9.end_ref.refs_0_.refs_1_, ...), custom_call_target="tpu_custom_call" | custom-call | flops 1 | bytes 1 | tf_op jit(solution)/shard_map/pallas_call | solution.py:233
  87.2 2.3 %collective-permute-start.20 = (bf16[2304,128]{1,0:T(8,128)(2,1)}, bf16[2304,128]{1,0:T(8,128)(2,1)S(1)}, u32[]{:S(2)}, u32[]{:S(2)}) collective-permute-start(bf16[2304,128]{1,0:T(8,128)(2,1)} %broadcast_select_fusion.1), channel_id=1, source_target_pairs={{0,4},{4,0},{8,12},{12,8},{1,5},{5,1},{9,13},{13,9},{2,6},{6,2},{1... | collective-permute-start | bytes 1769480 | tf_op jit(solution)/shard_map/ppermute | solution.py:477
  93.3 3.6 %shard_map.87 = (f32[64,1664]{1,0:T(8,128)S(1)}, f32[64,1664]{1,0:T(8,128)S(1)}, f32[512,128]{1,0:T(8,128)S(1)}) custom-call(s32[6]{0:T(128)S(1)} %stack.36.flags_ref, bf16[4608,128]{1,0:T(8,128)(2,1)S(1)} %collective-permute-done.9.end_ref.refs_0_.refs_1_, bf16[4608,128]{1,0:T(8,128)(2,1)S(1)} %collective-permute-done.9.end_ref.refs_0_.refs_1_, ...), custom_call_target="tpu_custom_call" | custom-call | flops 1 | bytes 1 | tf_op jit(solution)/shard_map/pallas_call | solution.py:325
  101.1 2.6 %collective-permute-done.20.refs_0_.refs_4_ = bf16[2304,128]{1,0:T(8,128)(2,1)S(1)} collective-permute-done((bf16[2304,128]{1,0:T(8,128)(2,1)}, bf16[2304,128]{1,0:T(8,128)(2,1)S(1)}, u32[]{:S(2)}, u32[]{:S(2)}) %collective-permute-start.20) | collective-permute-done | bytes 589856 | tf_op jit(solution)/shard_map/ppermute | solution.py:477
  103.7 3.6 %shard_map.88 = (f32[64,896]{1,0:T(8,128)S(1)}, f32[64,896]{1,0:T(8,128)S(1)}) custom-call(s32[6]{0:T(128)S(1)} %stack.36.flags_ref, bf16[2304,128]{1,0:T(8,128)(2,1)S(1)} %collective-permute-done.20.refs_0_.refs_4_, bf16[6912,128]{1,0:T(8,128)(2,1)S(1)} %copy-done.2, bf16[2304,128]{1,0:T(8,128)(2,1)S(1)} %copy-done.9, ...), custom_call_target="tpu_custom_call" | custom-call | flops 1 | bytes 1 | tf_op jit(solution)/shard_map/pallas_call | solution.py:325
  107.5 6.7 %collective-permute-start.19 = (bf16[32,1152]{1,0:T(8,128)(2,1)S(1)}, bf16[32,1152]{1,0:T(8,128)(2,1)S(1)}, u32[]{:S(2)}, u32[]{:S(2)}) collective-permute-start(bf16[32,1152]{1,0:T(8,128)(2,1)S(1)} %slice.85), channel_id=1, source_target_pairs={{0,4},{4,0},{8,12},{12,8},{1,5},{5,1},{9,13},{13,9},{2,6},{6,2},{1... | collective-permute-start | bytes 221192 | tf_op jit(solution)/shard_map/ppermute | solution.py:558
  116.0 2.5 %collective-permute-done.22 = bf16[32,896]{1,0:T(8,128)(2,1)S(1)} collective-permute-done((bf16[32,896]{1,0:T(8,128)(2,1)S(1)}, bf16[32,896]{1,0:T(8,128)(2,1)S(1)}, u32[]{:S(2)}, u32[]{:S(2)}) %collective-permute-start.22) | collective-permute-done | bytes 57376 | tf_op jit(solution)/shard_map/ppermute | solution.py:37
  123.0 2.8 %collective-permute-start.25 = (bf16[4,32,512]{2,1,0:T(8,128)(2,1)S(1)}, bf16[4,32,512]{2,1,0:T(8,128)(2,1)S(1)}, u32[]{:S(2)}, u32[]{:S(2)}) collective-permute-start(bf16[4,32,512]{2,1,0:T(8,128)(2,1)S(1)} %fusion.2), channel_id=1, source_target_pairs={{0,8},{8,0},{4,12},{12,4},{1,9},{9,1},{5,13},{13,5},{2,10},{10,2},... | collective-permute-start | bytes 393224 | tf_op jit(solution)/shard_map/ppermute | solution.py:570
  127.5 6.6 %collective-permute-done.26 = bf16[4,32,512]{2,1,0:T(8,128)(2,1)S(1)} collective-permute-done((bf16[4,32,512]{2,1,0:T(8,128)(2,1)S(1)}, bf16[4,32,512]{2,1,0:T(8,128)(2,1)S(1)}, u32[]{:S(2)}, u32[]{:S(2)}) %collective-permute-start.26) | collective-permute-done | bytes 131104 | tf_op jit(solution)/shard_map/ppermute | solution.py:571
  136.3 2.8 %fusion.3 = f32[16,64]{1,0:T(8,128)S(1)} fusion(bf16[64,32,512]{2,1,0:T(8,128)(2,1)S(1)} %copy-done.27, bf16[16,32,512]{2,1,0:T(8,128)(2,1)S(1)} %pad_maximum_fusion.1), kind=kOutput, calls=%fused_computation.10 | convolution fusion | flops 33554432 | bytes 2625536 | tf_op jit(solution)/shard_map/tea,jea->tj/dot_general | solution.py:547
  139.3 11.0 %all_to_all.5 = f32[16,2,16]{2,1,0:T(2,128)S(1)} all-to-all(f32[16,2,16]{2,1,0:T(2,128)S(1)} %copy.49), channel_id=1, replica_groups=mesh['groups'=2,'cand'=4,'eig'=2,'rep'=2] {'cand','eig','rep'}, dimensions={0} | all-to-all | bytes 4096 | tf_op jit(solution)/shard_map/all_to_all | solution.py:586
  (169 shorter events, 41.0 us)
Async XLA Ops:
  0.0 20.9 %collective-permute-start = (bf16[1280,128]{1,0:T(8,128)(2,1)}, bf16[1280,128]{1,0:T(8,128)(2,1)}, u32[]{:S(2)}, u32[]{:S(2)}) collective-permute-start(bf16[1280,128]{1,0:T(8,128)(2,1)} %refs_0_.3), channel_id=1, source_target_pairs={{0,4},{4,0},{8,12},{12,8},{1,5},{5,1},{9,13},{13,9},{2,6},{6,2},{1... | collective-permute-start | bytes 983048 | tf_op jit(solution)/shard_map/ppermute | solution.py:455
  3.0 17.8 %collective-permute-start.1 = (bf16[1280,128]{1,0:T(8,128)(2,1)}, bf16[1280,128]{1,0:T(8,128)(2,1)S(1)}, u32[]{:S(2)}, u32[]{:S(2)}) collective-permute-start(bf16[1280,128]{1,0:T(8,128)(2,1)} %refs_0_.3), channel_id=1, source_target_pairs={{0,1},{1,0},{2,3},{3,2},{4,8},{5,9},{6,10},{7,11},{8,4},{9,5},{10,... | collective-permute-start | bytes 983048 | tf_op jit(solution)/shard_map/ppermute | solution.py:447
  5.4 31.6 %collective-permute-start.4 = (bf16[4608,128]{1,0:T(8,128)(2,1)}, bf16[4608,128]{1,0:T(8,128)(2,1)S(1)}, u32[]{:S(2)}, u32[]{:S(2)}) collective-permute-start(bf16[4608,128]{1,0:T(8,128)(2,1)} %constant_dynamic-slice_fusion), channel_id=1, source_target_pairs={{0,4},{4,0},{8,12},{12,8},{1,5},{5,1},{9,13},{13,9},{2,6},{6,2},{1... | collective-permute-start | bytes 3538952 | tf_op jit(solution)/shard_map/ppermute | solution.py:457
  9.8 28.3 %collective-permute-start.7 = (bf16[2304,128]{1,0:T(8,128)(2,1)}, bf16[2304,128]{1,0:T(8,128)(2,1)}, u32[]{:S(2)}, u32[]{:S(2)}) collective-permute-start(bf16[2304,128]{1,0:T(8,128)(2,1)} %get-tuple-element.92), channel_id=1, source_target_pairs={{0,1},{1,0},{2,3},{3,2},{4,8},{5,9},{6,10},{7,11},{8,4},{9,5},{10,... | collective-permute-start | bytes 1769480 | tf_op jit(solution)/shard_map/ppermute | solution.py:447
  20.9 8.6 %collective-permute-start.2 = (bf16[1280,128]{1,0:T(8,128)(2,1)}, bf16[1280,128]{1,0:T(8,128)(2,1)S(1)}, u32[]{:S(2)}, u32[]{:S(2)}) collective-permute-start(bf16[1280,128]{1,0:T(8,128)(2,1)} %collective-permute-done.refs_1_), channel_id=1, source_target_pairs={{0,1},{1,0},{2,3},{3,2},{4,8},{5,9},{6,10},{7,11},{8,4},{9,5},{10,... | collective-permute-start | bytes 983048 | tf_op jit(solution)/shard_map/ppermute | solution.py:447
  29.4 8.7 %collective-permute-start.8 = (bf16[2304,128]{1,0:T(8,128)(2,1)S(1)}, bf16[2304,128]{1,0:T(8,128)(2,1)S(1)}, u32[]{:S(2)}, u32[]{:S(2)}) collective-permute-start(bf16[2304,128]{1,0:T(8,128)(2,1)S(1)} %copy-done.26), channel_id=1, source_target_pairs={{0,1},{1,0},{2,3},{3,2},{4,8},{5,9},{6,10},{7,11},{8,4},{9,5},{10,... | collective-permute-start | bytes 1769480 | tf_op jit(solution)/shard_map/ppermute | solution.py:447
  29.7 21.4 %collective-permute-start.3 = (bf16[2560,128]{1,0:T(8,128)(2,1)S(1)}, bf16[2560,128]{1,0:T(8,128)(2,1)S(1)}, u32[]{:S(2)}, u32[]{:S(2)}) collective-permute-start(bf16[2560,128]{1,0:T(8,128)(2,1)S(1)} %maximum_select_fusion.1), channel_id=1, source_target_pairs={{0,4},{4,0},{8,12},{12,8},{1,5},{5,1},{9,13},{13,9},{2,6},{6,2},{1... | collective-permute-start | bytes 1966088 | tf_op jit(solution)/shard_map/ppermute | solution.py:437
  38.1 13.2 %collective-permute-start.5 = (bf16[2304,128]{1,0:T(8,128)(2,1)S(1)}, bf16[2304,128]{1,0:T(8,128)(2,1)S(1)}, u32[]{:S(2)}, u32[]{:S(2)}) collective-permute-start(bf16[2304,128]{1,0:T(8,128)(2,1)S(1)} %get-tuple-element.94), channel_id=1, source_target_pairs={{0,1},{1,0},{2,3},{3,2},{4,8},{5,9},{6,10},{7,11},{8,4},{9,5},{10,... | collective-permute-start | bytes 1769480 | tf_op jit(solution)/shard_map/ppermute | solution.py:447
  39.9 36.5 %collective-permute-start.9 = (bf16[4608,128]{1,0:T(8,128)(2,1)S(1)}, bf16[4608,128]{1,0:T(8,128)(2,1)S(1)}, u32[]{:S(2)}, u32[]{:S(2)}) collective-permute-start(bf16[4608,128]{1,0:T(8,128)(2,1)S(1)} %maximum_select_fusion), channel_id=1, source_target_pairs={{0,4},{4,0},{8,12},{12,8},{1,5},{5,1},{9,13},{13,9},{2,6},{6,2},{1... | collective-permute-start | bytes 3538952 | tf_op jit(solution)/shard_map/ppermute | solution.py:472
  51.2 20.4 %collective-permute-start.10 = (bf16[2304,128]{1,0:T(8,128)(2,1)S(1)}, bf16[2304,128]{1,0:T(8,128)(2,1)S(1)}, u32[]{:S(2)}, u32[]{:S(2)}) collective-permute-start(bf16[2304,128]{1,0:T(8,128)(2,1)S(1)} %slice.81), channel_id=1, source_target_pairs={{0,1},{1,0},{2,3},{3,2},{4,8},{5,9},{6,10},{7,11},{8,4},{9,5},{10,... | collective-permute-start | bytes 1769480 | tf_op jit(solution)/shard_map/ppermute | solution.py:447
  55.2 31.0 %collective-permute-start.6 = (bf16[2304,128]{1,0:T(8,128)(2,1)S(1)}, bf16[2304,128]{1,0:T(8,128)(2,1)S(1)}, u32[]{:S(2)}, u32[]{:S(2)}) collective-permute-start(bf16[2304,128]{1,0:T(8,128)(2,1)S(1)} %copy-done.29), channel_id=1, source_target_pairs={{0,1},{1,0},{2,3},{3,2},{4,8},{5,9},{6,10},{7,11},{8,4},{9,5},{10,... | collective-permute-start | bytes 1769480 | tf_op jit(solution)/shard_map/ppermute | solution.py:447
  56.7 32.8 %collective-permute-start.12 = (bf16[2304,128]{1,0:T(8,128)(2,1)}, bf16[2304,128]{1,0:T(8,128)(2,1)S(1)}, u32[]{:S(2)}, u32[]{:S(2)}) collective-permute-start(bf16[2304,128]{1,0:T(8,128)(2,1)} %broadcast_select_fusion), channel_id=1, source_target_pairs={{0,4},{4,0},{8,12},{12,8},{1,5},{5,1},{9,13},{13,9},{2,6},{6,2},{1... | collective-permute-start | bytes 1769480 | tf_op jit(solution)/shard_map/ppermute | solution.py:437
  71.5 18.0 %collective-permute-start.13 = (bf16[2304,128]{1,0:T(8,128)(2,1)}, bf16[2304,128]{1,0:T(8,128)(2,1)}, u32[]{:S(2)}, u32[]{:S(2)}) collective-permute-start(bf16[2304,128]{1,0:T(8,128)(2,1)} %get-tuple-element.65), channel_id=1, source_target_pairs={{0,1},{1,0},{2,3},{3,2},{4,8},{5,9},{6,10},{7,11},{8,4},{9,5},{10,... | collective-permute-start | bytes 1769480 | tf_op jit(solution)/shard_map/ppermute | solution.py:447
  87.2 16.5 %collective-permute-start.20 = (bf16[2304,128]{1,0:T(8,128)(2,1)}, bf16[2304,128]{1,0:T(8,128)(2,1)S(1)}, u32[]{:S(2)}, u32[]{:S(2)}) collective-permute-start(bf16[2304,128]{1,0:T(8,128)(2,1)} %broadcast_select_fusion.1), channel_id=1, source_target_pairs={{0,4},{4,0},{8,12},{12,8},{1,5},{5,1},{9,13},{13,9},{2,6},{6,2},{1... | collective-permute-start | bytes 1769480 | tf_op jit(solution)/shard_map/ppermute | solution.py:477
  98.8 8.6 %collective-permute-start.15 = (bf16[32,2688]{1,0:T(8,128)(2,1)S(1)}, bf16[32,2688]{1,0:T(8,128)(2,1)S(1)}, u32[]{:S(2)}, u32[]{:S(2)}) collective-permute-start(bf16[32,2688]{1,0:T(8,128)(2,1)S(1)} %add_convert_fusion.1), channel_id=1, source_target_pairs={{0,2},{2,0},{1,3},{3,1},{4,6},{6,4},{5,7},{7,5},{8,10},{10,8},{9,1... | collective-permute-start | bytes 516104 | tf_op jit(solution)/shard_map/ppermute | solution.py:37
  100.5 15.4 %collective-permute-start.17 = (bf16[256,512]{1,0:T(8,128)(2,1)S(1)}, bf16[256,512]{1,0:T(8,128)(2,1)S(1)}, u32[]{:S(2)}, u32[]{:S(2)}) collective-permute-start(bf16[256,512]{1,0:T(8,128)(2,1)S(1)} %get-tuple-element.88), channel_id=1, source_target_pairs={{0,2},{2,0},{1,3},{3,1},{4,6},{6,4},{5,7},{7,5},{8,10},{10,8},{9,1... | collective-permute-start | bytes 786440 | tf_op jit(solution)/shard_map/ppermute | solution.py:37
  107.3 6.9 %collective-permute-start.21 = (f32[64,896]{1,0:T(8,128)S(1)}, f32[64,896]{1,0:T(8,128)S(1)}, u32[]{:S(2)}, u32[]{:S(2)}) collective-permute-start(f32[64,896]{1,0:T(8,128)S(1)} %get-tuple-element.76), channel_id=1, source_target_pairs={{0,1},{1,0},{2,3},{3,2},{4,5},{5,4},{6,7},{7,6},{8,9},{9,8},{10,11... | collective-permute-start | bytes 688136 | tf_op jit(solution)/shard_map/ppermute | solution.py:37
  107.5 15.0 %collective-permute-start.19 = (bf16[32,1152]{1,0:T(8,128)(2,1)S(1)}, bf16[32,1152]{1,0:T(8,128)(2,1)S(1)}, u32[]{:S(2)}, u32[]{:S(2)}) collective-permute-start(bf16[32,1152]{1,0:T(8,128)(2,1)S(1)} %slice.85), channel_id=1, source_target_pairs={{0,4},{4,0},{8,12},{12,8},{1,5},{5,1},{9,13},{13,9},{2,6},{6,2},{1... | collective-permute-start | bytes 221192 | tf_op jit(solution)/shard_map/ppermute | solution.py:558
  114.3 4.2 %collective-permute-start.22 = (bf16[32,896]{1,0:T(8,128)(2,1)S(1)}, bf16[32,896]{1,0:T(8,128)(2,1)S(1)}, u32[]{:S(2)}, u32[]{:S(2)}) collective-permute-start(bf16[32,896]{1,0:T(8,128)(2,1)S(1)} %add_convert_fusion.2), channel_id=1, source_target_pairs={{0,2},{2,0},{1,3},{3,1},{4,6},{6,4},{5,7},{7,5},{8,10},{10,8},{9,1... | collective-permute-start | bytes 172040 | tf_op jit(solution)/shard_map/ppermute | solution.py:37
  115.9 4.3 %collective-permute-start.18 = (bf16[256,512]{1,0:T(8,128)(2,1)S(1)}, bf16[256,512]{1,0:T(8,128)(2,1)S(1)}, u32[]{:S(2)}, u32[]{:S(2)}) collective-permute-start(bf16[256,512]{1,0:T(8,128)(2,1)S(1)} %add_convert_fusion), channel_id=1, source_target_pairs={{0,1},{1,0},{2,3},{3,2},{4,5},{5,4},{6,7},{7,6},{8,9},{9,8},{10,11... | collective-permute-start | bytes 786440 | tf_op jit(solution)/shard_map/ppermute | solution.py:37
  120.6 13.5 %collective-permute-start.27 = (bf16[4,32,512]{2,1,0:T(8,128)(2,1)S(1)}, bf16[4,32,512]{2,1,0:T(8,128)(2,1)S(1)}, u32[]{:S(2)}, u32[]{:S(2)}) collective-permute-start(bf16[4,32,512]{2,1,0:T(8,128)(2,1)S(1)} %convolution_convert_fusion.3), channel_id=1, source_target_pairs={{0,1},{1,0},{2,3},{3,2},{4,8},{5,9},{6,10},{7,11},{8,4},{9,5},{10,... | collective-permute-start | bytes 393224 | tf_op jit(solution)/shard_map/ppermute | solution.py:447
  123.0 12.1 %collective-permute-start.25 = (bf16[4,32,512]{2,1,0:T(8,128)(2,1)S(1)}, bf16[4,32,512]{2,1,0:T(8,128)(2,1)S(1)}, u32[]{:S(2)}, u32[]{:S(2)}) collective-permute-start(bf16[4,32,512]{2,1,0:T(8,128)(2,1)S(1)} %fusion.2), channel_id=1, source_target_pairs={{0,8},{8,0},{4,12},{12,4},{1,9},{9,1},{5,13},{13,5},{2,10},{10,2},... | collective-permute-start | bytes 393224 | tf_op jit(solution)/shard_map/ppermute | solution.py:570
  125.8 8.3 %collective-permute-start.26 = (bf16[4,32,512]{2,1,0:T(8,128)(2,1)S(1)}, bf16[4,32,512]{2,1,0:T(8,128)(2,1)S(1)}, u32[]{:S(2)}, u32[]{:S(2)}) collective-permute-start(bf16[4,32,512]{2,1,0:T(8,128)(2,1)S(1)} %convolution_convert_fusion), channel_id=1, source_target_pairs={{0,12},{1,13},{2,14},{3,15},{4,5},{5,4},{6,7},{7,6},{8,9},{9,8},{1... | collective-permute-start | bytes 393224 | tf_op jit(solution)/shard_map/ppermute | solution.py:571
  127.2 9.0 %collective-permute-start.24 = (bf16[4,32,512]{2,1,0:T(8,128)(2,1)S(1)}, bf16[4,32,512]{2,1,0:T(8,128)(2,1)S(1)}, u32[]{:S(2)}, u32[]{:S(2)}) collective-permute-start(bf16[4,32,512]{2,1,0:T(8,128)(2,1)S(1)} %convolution_convert_fusion.2), channel_id=1, source_target_pairs={{0,4},{4,0},{8,12},{12,8},{1,5},{5,1},{9,13},{13,9},{2,6},{6,2},{1... | collective-permute-start | bytes 393224 | tf_op jit(solution)/shard_map/ppermute | solution.py:572
  (40 other events, 272.6 us)

commit v20 on v19

--- a/solution.py
+++ b/solution.py
@@ -260,19 +260,44 @@
         return lambda i, flags_ref: (row + i, 0)
 
     whole = lambda i, flags_ref: (0, 0)
-    operands, specs = [], []
-    for array, row in list(pieces) + list(shards) + [shard[:2]]:
-        operands.append(array)
-        specs.append(pl.BlockSpec((step, cols), at(row)))
+    fetched = [shards[1][0], shards[2][0], shard[0]] if two else []
+    listed = list(pieces) + list(shards) + [shard[:2]]
+    places = [[array is x for x in fetched].index(True) if any(array is x for x in fetched) else None
+              for array, row in listed]
+    operands, specs = list(fetched), [pl.BlockSpec(memory_space=pltpu.HBM)] * len(fetched)
+    for (array, row), place in zip(listed, places):
+        if place is None:
+            operands.append(array)
+            specs.append(pl.BlockSpec((step, cols), at(row)))
+    blocked = len(operands) - len(fetched)
     operands += [grads, start]
     specs.append(pl.BlockSpec((tok, step), lambda i, flags_ref: (0, i)))
     specs.append(pl.BlockSpec(start.shape, whole))
 
     def kernel(flags_ref, *refs):
         i = pl.program_id(0)
-        piece_refs, shard_refs = refs[:count], refs[count : count + len(shards)]
-        end_ref, grads_ref, start_ref = refs[count + len(shards) : count + len(shards) + 3]
+        far_refs, block_refs = refs[: len(fetched)], list(refs[len(fetched) : len(fetched) + blocked])
+        grads_ref, start_ref = refs[len(fetched) + blocked : len(operands)]
         keep_ref, give_ref, *rest = refs[len(operands) :]
+        if fetched:
+            *rest, held_ref, arrived = rest
+            copies = [
+                pltpu.make_async_copy(far_ref, held_ref.at[k], arrived.at[k])
+                for k, far_ref in enumerate(far_refs)
+            ]
+
+            @pl.when(i == 0)
+            def fetch():
+                for copy in copies:
+                    copy.start()
+                for copy in copies:
+                    copy.wait()
+
+        here = pl.ds(pl.multiple_of(i * step, step), step)
+        all_refs = [
+            block_refs.pop(0) if place is None else held_ref.at[place, here] for place in places
+        ]
+        piece_refs, shard_refs, end_ref = all_refs[:count], all_refs[count:-1], all_refs[-1]
         if two:
             second_ref, total_ref, sums_ref, turned_ref, wide_ref = rest
         else:
@@ -335,7 +360,12 @@
                 pltpu.VMEM((count * TILE, len(shards) * cols), jnp.float32),
                 pltpu.VMEM((cols, count * TILE), jnp.float32),
                 pltpu.VMEM((cols, tok), jnp.float32),
-            ],
+            ]
+            + [
+                pltpu.VMEM((len(fetched), STEPS * step, cols), grads.dtype),
+                pltpu.SemaphoreType.DMA((len(fetched),)),
+            ]
+            * bool(fetched),
         ),
         compiler_params=PARAMS,
         cost_estimate=SHORT,

time: 152 us -> 151 us (level)
    unnamed x72 -> x66, local copies, waits for them, and re-layouts: 18.3 us -> 17.3 us
where the time goes in v20:
time: 151 us; the launch traced here: 150 us
  starting transfers between devices  51.4 us (34%)
  Pallas kernels  26.1 us (17%)
  waiting for transfers between devices  25.2 us (17%)
  local copies, waits for them, and re-layouts  22.3 us (15%)
  blocking collectives  11 us (7%)
  other arithmetic  10 us (7%)
  matrix products  3.81 us (3%)
    unnamed x66, local copies, waits for them, and re-layouts  17.3 us
    ppermute x2, starting transfers between devices, side(): return lax.ppermute(pick(at_end, at_middle), 'cand', SIDE)  15.4 us
    all_to_all x1, blocking collectives, final_sum(): return jnp.sum(lax.all_to_all(blocks, ALL, 0, 0, tiled=True), axis=0)  11 us
    ppermute x1, starting transfers between devices, line_plan(): s45 = lax.ppermute(to_s45, 'cand', SIDE)  8.88 us
    pallas_call x2, Pallas kernels, feature_dots(): pl.pallas_call(kernel, out_shape=out_shape, grid_spec=pltpu.PrefetchScala...  8.38 us
    pallas_call x2, Pallas kernels, partner_dots(): pl.pallas_call(kernel, out_shape=out_shape, grid_spec=pltpu.PrefetchScala...  7.34 us
    ppermute x1, starting transfers between devices, line_plan(): back = after(lax.ppermute(sums, 'cand', SIDE), rows_there)  6.97 us
    ppermute x1, waiting for transfers between devices, line_plan(): from_far = lax.ppermute(after(prods_c, to_two), ALL, far)  6.59 us
  transfers between devices with their start and end apart: 28, of which 10 were waited for; matrix products, arithmetic and copies ran while one was open for 11% of the time, Pallas kernels for 17%

profile of v20, /device:TPU:0, one launch (start us, length us, event | category | flops | bytes accessed | tf_op | source)
XLA Modules:
  0.0 150.3 jit_solution(3404427441332551165)
XLA Ops:
  0.0 3.0 %collective-permute-start = (bf16[1280,128]{1,0:T(8,128)(2,1)}, bf16[1280,128]{1,0:T(8,128)(2,1)}, u32[]{:S(2)}, u32[]{:S(2)}) collective-permute-start(bf16[1280,128]{1,0:T(8,128)(2,1)} %refs_0_.3), channel_id=1, source_target_pairs={{0,4},{4,0},{8,12},{12,8},{1,5},{5,1},{9,13},{13,9},{2,6},{6,2},{1... | collective-permute-start | bytes 983048 | tf_op jit(solution)/shard_map/ppermute | solution.py:485
  3.0 2.4 %constant_dynamic-slice_fusion = bf16[4608,128]{1,0:T(8,128)(2,1)} fusion(bf16[6912,128]{1,0:T(8,128)(2,1)} %refs_1_.1, s32[]{:T(128)S(6)} %select_n.162), kind=kLoop, calls=%fused_computation.79 | loop fusion | bytes 2359300 | tf_op jit(solution)/shard_map/dynamic_slice | solution.py:484
  5.4 3.1 %collective-permute-start.4 = (bf16[4608,128]{1,0:T(8,128)(2,1)}, bf16[4608,128]{1,0:T(8,128)(2,1)S(1)}, u32[]{:S(2)}, u32[]{:S(2)}) collective-permute-start(bf16[4608,128]{1,0:T(8,128)(2,1)} %constant_dynamic-slice_fusion), channel_id=1, source_target_pairs={{0,4},{4,0},{8,12},{12,8},{1,5},{5,1},{9,13},{13,9},{2,6},{6,2},{1... | collective-permute-start | bytes 3538952 | tf_op jit(solution)/shard_map/ppermute | solution.py:487
  9.9 3.5 %divide_convert_fusion = bf16[64,32,512]{2,1,0:T(8,128)(2,1)} fusion(bf16[64,32,512]{2,1,0:T(8,128)(2,1)} %param.13, f32[32,512]{1,0:T(8,128)S(1)} %broadcast_add_fusion), kind=kLoop, calls=%fused_computation | loop fusion | flops 3145728 | bytes 4259840 | tf_op jit(solution)/shard_map/convert_element_type | solution.py:495
  13.5 3.0 %copy-done = bf16[512,6912]{1,0:T(8,128)(2,1)S(1)} copy-done((bf16[512,6912]{1,0:T(8,128)(2,1)S(1)}, bf16[512,6912]{1,0:T(8,128)(2,1)}, u32[]{:S(2)}) %copy-start) | copy-done | bytes 7077912
  21.8 3.0 %copy-done.1 = bf16[512,6912]{1,0:T(8,128)(2,1)S(1)} copy-done((bf16[512,6912]{1,0:T(8,128)(2,1)S(1)}, bf16[512,6912]{1,0:T(8,128)(2,1)}, u32[]{:S(2)}) %copy-start.1) | copy-done | bytes 7077912
  24.8 4.6 %shard_map.82 = (f32[64,512]{1,0:T(8,128)S(1)}, f32[64,512]{1,0:T(8,128)S(1)}) custom-call(s32[6]{0:T(128)S(1)} %stack.36.flags_ref, bf16[512,6912]{1,0:T(8,128)(2,1)S(1)} %copy-done.1, bf16[6912,128]{1,0:T(8,128)(2,1)S(1)} %copy-done.2), custom_call_target="tpu_custom_call" | custom-call | flops 1 | bytes 1 | tf_op jit(solution)/shard_map/pallas_call | solution.py:161
  29.7 5.2 %collective-permute-start.3 = (bf16[2560,128]{1,0:T(8,128)(2,1)S(1)}, bf16[2560,128]{1,0:T(8,128)(2,1)S(1)}, u32[]{:S(2)}, u32[]{:S(2)}) collective-permute-start(bf16[2560,128]{1,0:T(8,128)(2,1)S(1)} %maximum_select_fusion.1), channel_id=1, source_target_pairs={{0,4},{4,0},{8,12},{12,8},{1,5},{5,1},{9,13},{13,9},{2,6},{6,2},{1... | collective-permute-start | bytes 1966088 | tf_op jit(solution)/shard_map/ppermute | solution.py:467
  39.9 8.9 %collective-permute-start.9 = (bf16[4608,128]{1,0:T(8,128)(2,1)S(1)}, bf16[4608,128]{1,0:T(8,128)(2,1)S(1)}, u32[]{:S(2)}, u32[]{:S(2)}) collective-permute-start(bf16[4608,128]{1,0:T(8,128)(2,1)S(1)} %maximum_select_fusion), channel_id=1, source_target_pairs={{0,4},{4,0},{8,12},{12,8},{1,5},{5,1},{9,13},{13,9},{2,6},{6,2},{1... | collective-permute-start | bytes 3538952 | tf_op jit(solution)/shard_map/ppermute | solution.py:502
  51.3 3.9 %shard_map.83 = (f32[256,512]{1,0:T(8,128)S(1)}, f32[256,512]{1,0:T(8,128)S(1)}) custom-call(s32[6]{0:T(128)S(1)} %stack.36.flags_ref, bf16[512,1280]{1,0:T(8,128)(2,1)S(1)} %copy-done.9, bf16[1280,128]{1,0:T(8,128)(2,1)S(1)} %copy-done.20, bf16[1280,128]{1,0:T(8,128)(2,1)} %collective-permute-done.refs_1_, ...), custom_call_target="tpu_custom_call" | custom-call | flops 1 | bytes 1 | tf_op jit(solution)/shard_map/pallas_call | solution.py:438
  57.4 10.2 %collective-permute-start.13 = (bf16[2304,128]{1,0:T(8,128)(2,1)}, bf16[2304,128]{1,0:T(8,128)(2,1)}, u32[]{:S(2)}, u32[]{:S(2)}) collective-permute-start(bf16[2304,128]{1,0:T(8,128)(2,1)} %broadcast_select_fusion), channel_id=1, source_target_pairs={{0,4},{4,0},{8,12},{12,8},{1,5},{5,1},{9,13},{13,9},{2,6},{6,2},{1... | collective-permute-start | bytes 1769480 | tf_op jit(solution)/shard_map/ppermute | solution.py:467
  67.6 3.8 %shard_map.84 = (f32[64,512]{1,0:T(8,128)S(1)}, f32[64,512]{1,0:T(8,128)S(1)}) custom-call(s32[6]{0:T(128)S(1)} %stack.36.flags_ref, bf16[512,6912]{1,0:T(8,128)(2,1)S(1)} %bitcast.48, bf16[4608,128]{1,0:T(8,128)(2,1)S(1)} %copy-done.4, bf16[2560,128]{1,0:T(8,128)(2,1)S(1)} %collective-permute-done.3.refs_2_.refs_4_.refs_1_), custom_call_target="tpu_custom_call" | custom-call | flops 1 | bytes 1 | tf_op jit(solution)/shard_map/pallas_call | solution.py:161
  72.2 4.1 %collective-permute-done.9.end_ref.refs_3_.refs_4_ = bf16[4608,128]{1,0:T(8,128)(2,1)S(1)} collective-permute-done((bf16[4608,128]{1,0:T(8,128)(2,1)S(1)}, bf16[4608,128]{1,0:T(8,128)(2,1)S(1)}, u32[]{:S(2)}, u32[]{:S(2)}) %collective-permute-start.9) | collective-permute-done | bytes 1179680 | tf_op jit(solution)/shard_map/ppermute | solution.py:502
  77.3 5.2 %shard_map.86 = (f32[512,256]{1,0:T(8,128)S(1)}, bf16[512,2304]{1,0:T(8,128)(2,1)S(1)}, bf16[512,2304]{1,0:T(8,128)(2,1)S(1)}) custom-call(s32[6]{0:T(128)S(1)} %stack.36.flags_ref, bf16[512,6912]{1,0:T(8,128)(2,1)S(1)} %bitcast.48, bf16[4608,128]{1,0:T(8,128)(2,1)S(1)} %collective-permute-done.9.end_ref.refs_3_.refs_4_, ...), custom_call_target="tpu_custom_call" | custom-call | flops 1 | bytes 1 | tf_op jit(solution)/shard_map/pallas_call | solution.py:233
  86.3 2.3 %collective-permute-start.20 = (bf16[2304,128]{1,0:T(8,128)(2,1)}, bf16[2304,128]{1,0:T(8,128)(2,1)S(1)}, u32[]{:S(2)}, u32[]{:S(2)}) collective-permute-start(bf16[2304,128]{1,0:T(8,128)(2,1)} %broadcast_select_fusion.1), channel_id=1, source_target_pairs={{0,4},{4,0},{8,12},{12,8},{1,5},{5,1},{9,13},{13,9},{2,6},{6,2},{1... | collective-permute-start | bytes 1769480 | tf_op jit(solution)/shard_map/ppermute | solution.py:507
  91.3 3.7 %shard_map.87 = (f32[64,1664]{1,0:T(8,128)S(1)}, f32[64,1664]{1,0:T(8,128)S(1)}, f32[512,128]{1,0:T(8,128)S(1)}) custom-call(s32[6]{0:T(128)S(1)} %stack.36.flags_ref, bf16[2304,128]{1,0:T(8,128)(2,1)S(1)} %collective-permute-done.6.refs_0_.refs_2_, bf16[2304,128]{1,0:T(8,128)(2,1)} %collective-permute-done.12.refs_1_.refs_3_, ...), custom_call_target="tpu_custom_call" | custom-call | flops 1 | bytes 1 | tf_op jit(solution)/shard_map/pallas_call | solution.py:350
  99.3 3.5 %collective-permute-done.20.refs_0_.refs_4_ = bf16[2304,128]{1,0:T(8,128)(2,1)S(1)} collective-permute-done((bf16[2304,128]{1,0:T(8,128)(2,1)}, bf16[2304,128]{1,0:T(8,128)(2,1)S(1)}, u32[]{:S(2)}, u32[]{:S(2)}) %collective-permute-start.20) | collective-permute-done | bytes 589856 | tf_op jit(solution)/shard_map/ppermute | solution.py:507
  102.8 3.6 %shard_map.88 = (f32[64,896]{1,0:T(8,128)S(1)}, f32[64,896]{1,0:T(8,128)S(1)}) custom-call(s32[6]{0:T(128)S(1)} %stack.36.flags_ref, bf16[2304,128]{1,0:T(8,128)(2,1)S(1)} %collective-permute-done.20.refs_0_.refs_4_, bf16[6912,128]{1,0:T(8,128)(2,1)S(1)} %copy-done.2, bf16[2304,128]{1,0:T(8,128)(2,1)S(1)} %collective-permute-done.6.refs_0_.refs_2_, ...), custom_call_target="tpu_custom_call" | custom-call | flops 1 | bytes 1 | tf_op jit(solution)/shard_map/pallas_call | solution.py:350
  106.6 7.0 %collective-permute-start.19 = (bf16[32,1152]{1,0:T(8,128)(2,1)S(1)}, bf16[32,1152]{1,0:T(8,128)(2,1)S(1)}, u32[]{:S(2)}, u32[]{:S(2)}) collective-permute-start(bf16[32,1152]{1,0:T(8,128)(2,1)S(1)} %slice.85), channel_id=1, source_target_pairs={{0,4},{4,0},{8,12},{12,8},{1,5},{5,1},{9,13},{13,9},{2,6},{6,2},{1... | collective-permute-start | bytes 221192 | tf_op jit(solution)/shard_map/ppermute | solution.py:588
  115.4 2.5 %collective-permute-done.22 = bf16[32,896]{1,0:T(8,128)(2,1)S(1)} collective-permute-done((bf16[32,896]{1,0:T(8,128)(2,1)S(1)}, bf16[32,896]{1,0:T(8,128)(2,1)S(1)}, u32[]{:S(2)}, u32[]{:S(2)}) %collective-permute-start.22) | collective-permute-done | bytes 57376 | tf_op jit(solution)/shard_map/ppermute | solution.py:37
  122.3 2.8 %collective-permute-start.25 = (bf16[4,32,512]{2,1,0:T(8,128)(2,1)S(1)}, bf16[4,32,512]{2,1,0:T(8,128)(2,1)S(1)}, u32[]{:S(2)}, u32[]{:S(2)}) collective-permute-start(bf16[4,32,512]{2,1,0:T(8,128)(2,1)S(1)} %fusion.2), channel_id=1, source_target_pairs={{0,8},{8,0},{4,12},{12,4},{1,9},{9,1},{5,13},{13,5},{2,10},{10,2},... | collective-permute-start | bytes 393224 | tf_op jit(solution)/shard_map/ppermute | solution.py:600
  126.9 6.6 %collective-permute-done.26 = bf16[4,32,512]{2,1,0:T(8,128)(2,1)S(1)} collective-permute-done((bf16[4,32,512]{2,1,0:T(8,128)(2,1)S(1)}, bf16[4,32,512]{2,1,0:T(8,128)(2,1)S(1)}, u32[]{:S(2)}, u32[]{:S(2)}) %collective-permute-start.26) | collective-permute-done | bytes 131104 | tf_op jit(solution)/shard_map/ppermute | solution.py:601
  135.7 2.8 %fusion.3 = f32[16,64]{1,0:T(8,128)S(1)} fusion(bf16[64,32,512]{2,1,0:T(8,128)(2,1)S(1)} %copy-done.24, bf16[16,32,512]{2,1,0:T(8,128)(2,1)S(1)} %pad_maximum_fusion.1), kind=kOutput, calls=%fused_computation.10 | convolution fusion | flops 33554432 | bytes 2625536 | tf_op jit(solution)/shard_map/tea,jea->tj/dot_general | solution.py:577
  138.7 11.0 %all_to_all.5 = f32[16,2,16]{2,1,0:T(2,128)S(1)} all-to-all(f32[16,2,16]{2,1,0:T(2,128)S(1)} %copy.49), channel_id=1, replica_groups=mesh['groups'=2,'cand'=4,'eig'=2,'rep'=2] {'cand','eig','rep'}, dimensions={0} | all-to-all | bytes 4096 | tf_op jit(solution)/shard_map/all_to_all | solution.py:616
  (163 shorter events, 39.8 us)
Async XLA Ops:
  0.0 20.9 %collective-permute-start = (bf16[1280,128]{1,0:T(8,128)(2,1)}, bf16[1280,128]{1,0:T(8,128)(2,1)}, u32[]{:S(2)}, u32[]{:S(2)}) collective-permute-start(bf16[1280,128]{1,0:T(8,128)(2,1)} %refs_0_.3), channel_id=1, source_target_pairs={{0,4},{4,0},{8,12},{12,8},{1,5},{5,1},{9,13},{13,9},{2,6},{6,2},{1... | collective-permute-start | bytes 983048 | tf_op jit(solution)/shard_map/ppermute | solution.py:485
  3.0 17.9 %collective-permute-start.1 = (bf16[1280,128]{1,0:T(8,128)(2,1)}, bf16[1280,128]{1,0:T(8,128)(2,1)S(1)}, u32[]{:S(2)}, u32[]{:S(2)}) collective-permute-start(bf16[1280,128]{1,0:T(8,128)(2,1)} %refs_0_.3), channel_id=1, source_target_pairs={{0,1},{1,0},{2,3},{3,2},{4,8},{5,9},{6,10},{7,11},{8,4},{9,5},{10,... | collective-permute-start | bytes 983048 | tf_op jit(solution)/shard_map/ppermute | solution.py:477
  5.4 31.6 %collective-permute-start.4 = (bf16[4608,128]{1,0:T(8,128)(2,1)}, bf16[4608,128]{1,0:T(8,128)(2,1)S(1)}, u32[]{:S(2)}, u32[]{:S(2)}) collective-permute-start(bf16[4608,128]{1,0:T(8,128)(2,1)} %constant_dynamic-slice_fusion), channel_id=1, source_target_pairs={{0,4},{4,0},{8,12},{12,8},{1,5},{5,1},{9,13},{13,9},{2,6},{6,2},{1... | collective-permute-start | bytes 3538952 | tf_op jit(solution)/shard_map/ppermute | solution.py:487
  9.9 28.2 %collective-permute-start.7 = (bf16[2304,128]{1,0:T(8,128)(2,1)}, bf16[2304,128]{1,0:T(8,128)(2,1)}, u32[]{:S(2)}, u32[]{:S(2)}) collective-permute-start(bf16[2304,128]{1,0:T(8,128)(2,1)} %get-tuple-element.92), channel_id=1, source_target_pairs={{0,1},{1,0},{2,3},{3,2},{4,8},{5,9},{6,10},{7,11},{8,4},{9,5},{10,... | collective-permute-start | bytes 1769480 | tf_op jit(solution)/shard_map/ppermute | solution.py:477
  20.9 8.6 %collective-permute-start.2 = (bf16[1280,128]{1,0:T(8,128)(2,1)}, bf16[1280,128]{1,0:T(8,128)(2,1)S(1)}, u32[]{:S(2)}, u32[]{:S(2)}) collective-permute-start(bf16[1280,128]{1,0:T(8,128)(2,1)} %collective-permute-done.refs_1_), channel_id=1, source_target_pairs={{0,1},{1,0},{2,3},{3,2},{4,8},{5,9},{6,10},{7,11},{8,4},{9,5},{10,... | collective-permute-start | bytes 983048 | tf_op jit(solution)/shard_map/ppermute | solution.py:477
  29.4 8.6 %collective-permute-start.8 = (bf16[2304,128]{1,0:T(8,128)(2,1)S(1)}, bf16[2304,128]{1,0:T(8,128)(2,1)S(1)}, u32[]{:S(2)}, u32[]{:S(2)}) collective-permute-start(bf16[2304,128]{1,0:T(8,128)(2,1)S(1)} %copy-done.23), channel_id=1, source_target_pairs={{0,1},{1,0},{2,3},{3,2},{4,8},{5,9},{6,10},{7,11},{8,4},{9,5},{10,... | collective-permute-start | bytes 1769480 | tf_op jit(solution)/shard_map/ppermute | solution.py:477
  29.7 21.4 %collective-permute-start.3 = (bf16[2560,128]{1,0:T(8,128)(2,1)S(1)}, bf16[2560,128]{1,0:T(8,128)(2,1)S(1)}, u32[]{:S(2)}, u32[]{:S(2)}) collective-permute-start(bf16[2560,128]{1,0:T(8,128)(2,1)S(1)} %maximum_select_fusion.1), channel_id=1, source_target_pairs={{0,4},{4,0},{8,12},{12,8},{1,5},{5,1},{9,13},{13,9},{2,6},{6,2},{1... | collective-permute-start | bytes 1966088 | tf_op jit(solution)/shard_map/ppermute | solution.py:467
  38.0 13.2 %collective-permute-start.5 = (bf16[2304,128]{1,0:T(8,128)(2,1)S(1)}, bf16[2304,128]{1,0:T(8,128)(2,1)S(1)}, u32[]{:S(2)}, u32[]{:S(2)}) collective-permute-start(bf16[2304,128]{1,0:T(8,128)(2,1)S(1)} %get-tuple-element.94), channel_id=1, source_target_pairs={{0,1},{1,0},{2,3},{3,2},{4,8},{5,9},{6,10},{7,11},{8,4},{9,5},{10,... | collective-permute-start | bytes 1769480 | tf_op jit(solution)/shard_map/ppermute | solution.py:477
  39.9 36.5 %collective-permute-start.9 = (bf16[4608,128]{1,0:T(8,128)(2,1)S(1)}, bf16[4608,128]{1,0:T(8,128)(2,1)S(1)}, u32[]{:S(2)}, u32[]{:S(2)}) collective-permute-start(bf16[4608,128]{1,0:T(8,128)(2,1)S(1)} %maximum_select_fusion), channel_id=1, source_target_pairs={{0,4},{4,0},{8,12},{12,8},{1,5},{5,1},{9,13},{13,9},{2,6},{6,2},{1... | collective-permute-start | bytes 3538952 | tf_op jit(solution)/shard_map/ppermute | solution.py:502
  51.2 21.1 %collective-permute-start.10 = (bf16[2304,128]{1,0:T(8,128)(2,1)S(1)}, bf16[2304,128]{1,0:T(8,128)(2,1)S(1)}, u32[]{:S(2)}, u32[]{:S(2)}) collective-permute-start(bf16[2304,128]{1,0:T(8,128)(2,1)S(1)} %slice.81), channel_id=1, source_target_pairs={{0,1},{1,0},{2,3},{3,2},{4,8},{5,9},{6,10},{7,11},{8,4},{9,5},{10,... | collective-permute-start | bytes 1769480 | tf_op jit(solution)/shard_map/ppermute | solution.py:477
  56.0 30.2 %collective-permute-start.6 = (bf16[2304,128]{1,0:T(8,128)(2,1)S(1)}, bf16[2304,128]{1,0:T(8,128)(2,1)S(1)}, u32[]{:S(2)}, u32[]{:S(2)}) collective-permute-start(bf16[2304,128]{1,0:T(8,128)(2,1)S(1)} %copy-done.26), channel_id=1, source_target_pairs={{0,1},{1,0},{2,3},{3,2},{4,8},{5,9},{6,10},{7,11},{8,4},{9,5},{10,... | collective-permute-start | bytes 1769480 | tf_op jit(solution)/shard_map/ppermute | solution.py:477
  57.4 31.3 %collective-permute-start.13 = (bf16[2304,128]{1,0:T(8,128)(2,1)}, bf16[2304,128]{1,0:T(8,128)(2,1)}, u32[]{:S(2)}, u32[]{:S(2)}) collective-permute-start(bf16[2304,128]{1,0:T(8,128)(2,1)} %broadcast_select_fusion), channel_id=1, source_target_pairs={{0,4},{4,0},{8,12},{12,8},{1,5},{5,1},{9,13},{13,9},{2,6},{6,2},{1... | collective-permute-start | bytes 1769480 | tf_op jit(solution)/shard_map/ppermute | solution.py:467
  72.2 16.4 %collective-permute-start.12 = (bf16[2304,128]{1,0:T(8,128)(2,1)}, bf16[2304,128]{1,0:T(8,128)(2,1)}, u32[]{:S(2)}, u32[]{:S(2)}) collective-permute-start(bf16[2304,128]{1,0:T(8,128)(2,1)} %get-tuple-element.65), channel_id=1, source_target_pairs={{0,1},{1,0},{2,3},{3,2},{4,8},{5,9},{6,10},{7,11},{8,4},{9,5},{10,... | collective-permute-start | bytes 1769480 | tf_op jit(solution)/shard_map/ppermute | solution.py:477
  86.3 16.5 %collective-permute-start.20 = (bf16[2304,128]{1,0:T(8,128)(2,1)}, bf16[2304,128]{1,0:T(8,128)(2,1)S(1)}, u32[]{:S(2)}, u32[]{:S(2)}) collective-permute-start(bf16[2304,128]{1,0:T(8,128)(2,1)} %broadcast_select_fusion.1), channel_id=1, source_target_pairs={{0,4},{4,0},{8,12},{12,8},{1,5},{5,1},{9,13},{13,9},{2,6},{6,2},{1... | collective-permute-start | bytes 1769480 | tf_op jit(solution)/shard_map/ppermute | solution.py:507
  97.0 9.5 %collective-permute-start.15 = (bf16[32,2688]{1,0:T(8,128)(2,1)S(1)}, bf16[32,2688]{1,0:T(8,128)(2,1)S(1)}, u32[]{:S(2)}, u32[]{:S(2)}) collective-permute-start(bf16[32,2688]{1,0:T(8,128)(2,1)S(1)} %add_convert_fusion.1), channel_id=1, source_target_pairs={{0,2},{2,0},{1,3},{3,1},{4,6},{6,4},{5,7},{7,5},{8,10},{10,8},{9,1... | collective-permute-start | bytes 516104 | tf_op jit(solution)/shard_map/ppermute | solution.py:37
  98.7 16.5 %collective-permute-start.17 = (bf16[256,512]{1,0:T(8,128)(2,1)S(1)}, bf16[256,512]{1,0:T(8,128)(2,1)S(1)}, u32[]{:S(2)}, u32[]{:S(2)}) collective-permute-start(bf16[256,512]{1,0:T(8,128)(2,1)S(1)} %get-tuple-element.88), channel_id=1, source_target_pairs={{0,2},{2,0},{1,3},{3,1},{4,6},{6,4},{5,7},{7,5},{8,10},{10,8},{9,1... | collective-permute-start | bytes 786440 | tf_op jit(solution)/shard_map/ppermute | solution.py:37
  106.5 7.2 %collective-permute-start.21 = (f32[64,896]{1,0:T(8,128)S(1)}, f32[64,896]{1,0:T(8,128)S(1)}, u32[]{:S(2)}, u32[]{:S(2)}) collective-permute-start(f32[64,896]{1,0:T(8,128)S(1)} %get-tuple-element.76), channel_id=1, source_target_pairs={{0,1},{1,0},{2,3},{3,2},{4,5},{5,4},{6,7},{7,6},{8,9},{9,8},{10,11... | collective-permute-start | bytes 688136 | tf_op jit(solution)/shard_map/ppermute | solution.py:37
  106.6 15.2 %collective-permute-start.19 = (bf16[32,1152]{1,0:T(8,128)(2,1)S(1)}, bf16[32,1152]{1,0:T(8,128)(2,1)S(1)}, u32[]{:S(2)}, u32[]{:S(2)}) collective-permute-start(bf16[32,1152]{1,0:T(8,128)(2,1)S(1)} %slice.85), channel_id=1, source_target_pairs={{0,4},{4,0},{8,12},{12,8},{1,5},{5,1},{9,13},{13,9},{2,6},{6,2},{1... | collective-permute-start | bytes 221192 | tf_op jit(solution)/shard_map/ppermute | solution.py:588
  113.7 4.2 %collective-permute-start.22 = (bf16[32,896]{1,0:T(8,128)(2,1)S(1)}, bf16[32,896]{1,0:T(8,128)(2,1)S(1)}, u32[]{:S(2)}, u32[]{:S(2)}) collective-permute-start(bf16[32,896]{1,0:T(8,128)(2,1)S(1)} %add_convert_fusion.2), channel_id=1, source_target_pairs={{0,2},{2,0},{1,3},{3,1},{4,6},{6,4},{5,7},{7,5},{8,10},{10,8},{9,1... | collective-permute-start | bytes 172040 | tf_op jit(solution)/shard_map/ppermute | solution.py:37
  115.3 4.3 %collective-permute-start.18 = (bf16[256,512]{1,0:T(8,128)(2,1)S(1)}, bf16[256,512]{1,0:T(8,128)(2,1)S(1)}, u32[]{:S(2)}, u32[]{:S(2)}) collective-permute-start(bf16[256,512]{1,0:T(8,128)(2,1)S(1)} %add_convert_fusion), channel_id=1, source_target_pairs={{0,1},{1,0},{2,3},{3,2},{4,5},{5,4},{6,7},{7,6},{8,9},{9,8},{10,11... | collective-permute-start | bytes 786440 | tf_op jit(solution)/shard_map/ppermute | solution.py:37
  120.0 13.5 %collective-permute-start.27 = (bf16[4,32,512]{2,1,0:T(8,128)(2,1)S(1)}, bf16[4,32,512]{2,1,0:T(8,128)(2,1)S(1)}, u32[]{:S(2)}, u32[]{:S(2)}) collective-permute-start(bf16[4,32,512]{2,1,0:T(8,128)(2,1)S(1)} %convolution_convert_fusion.3), channel_id=1, source_target_pairs={{0,1},{1,0},{2,3},{3,2},{4,8},{5,9},{6,10},{7,11},{8,4},{9,5},{10,... | collective-permute-start | bytes 393224 | tf_op jit(solution)/shard_map/ppermute | solution.py:477
  122.3 12.1 %collective-permute-start.25 = (bf16[4,32,512]{2,1,0:T(8,128)(2,1)S(1)}, bf16[4,32,512]{2,1,0:T(8,128)(2,1)S(1)}, u32[]{:S(2)}, u32[]{:S(2)}) collective-permute-start(bf16[4,32,512]{2,1,0:T(8,128)(2,1)S(1)} %fusion.2), channel_id=1, source_target_pairs={{0,8},{8,0},{4,12},{12,4},{1,9},{9,1},{5,13},{13,5},{2,10},{10,2},... | collective-permute-start | bytes 393224 | tf_op jit(solution)/shard_map/ppermute | solution.py:600
  125.2 8.3 %collective-permute-start.26 = (bf16[4,32,512]{2,1,0:T(8,128)(2,1)S(1)}, bf16[4,32,512]{2,1,0:T(8,128)(2,1)S(1)}, u32[]{:S(2)}, u32[]{:S(2)}) collective-permute-start(bf16[4,32,512]{2,1,0:T(8,128)(2,1)S(1)} %convolution_convert_fusion), channel_id=1, source_target_pairs={{0,12},{1,13},{2,14},{3,15},{4,5},{5,4},{6,7},{7,6},{8,9},{9,8},{1... | collective-permute-start | bytes 393224 | tf_op jit(solution)/shard_map/ppermute | solution.py:601
  126.6 9.0 %collective-permute-start.24 = (bf16[4,32,512]{2,1,0:T(8,128)(2,1)S(1)}, bf16[4,32,512]{2,1,0:T(8,128)(2,1)S(1)}, u32[]{:S(2)}, u32[]{:S(2)}) collective-permute-start(bf16[4,32,512]{2,1,0:T(8,128)(2,1)S(1)} %convolution_convert_fusion.2), channel_id=1, source_target_pairs={{0,4},{4,0},{8,12},{12,8},{1,5},{5,1},{9,13},{13,9},{2,6},{6,2},{1... | collective-permute-start | bytes 393224 | tf_op jit(solution)/shard_map/ppermute | solution.py:602
  (37 other events, 254.4 us)

commit v21 on v20

--- a/solution.py
+++ b/solution.py
@@ -271,8 +271,11 @@
             specs.append(pl.BlockSpec((step, cols), at(row)))
     blocked = len(operands) - len(fetched)
     operands += [grads, start]
-    specs.append(pl.BlockSpec((tok, step), lambda i, flags_ref: (0, i)))
-    specs.append(pl.BlockSpec(start.shape, whole))
+    if two:
+        specs += [pl.BlockSpec(memory_space=pltpu.HBM)] * 2
+    else:
+        specs.append(pl.BlockSpec((tok, step), lambda i, flags_ref: (0, i)))
+        specs.append(pl.BlockSpec(start.shape, whole))
 
     def kernel(flags_ref, *refs):
         i = pl.program_id(0)
@@ -280,11 +283,15 @@
         grads_ref, start_ref = refs[len(fetched) + blocked : len(operands)]
         keep_ref, give_ref, *rest = refs[len(operands) :]
         if fetched:
-            *rest, held_ref, arrived = rest
+            *rest, held_ref, held_grads_ref, arrived = rest
+            pairs = [(far_ref, held_ref.at[k]) for k, far_ref in enumerate(far_refs)]
+            pairs += [(grads_ref, held_grads_ref), (start_ref, rest[1])]
             copies = [
-                pltpu.make_async_copy(far_ref, held_ref.at[k], arrived.at[k])
-                for k, far_ref in enumerate(far_refs)
+                pltpu.make_async_copy(source, target, arrived.at[k])
+                for k, (source, target) in enumerate(pairs)
             ]
+            columns_here = pl.ds(pl.multiple_of(i * step, step), step)
+            grads_ref = held_grads_ref.at[:, columns_here]
 
             @pl.when(i == 0)
             def fetch():
@@ -305,7 +312,8 @@
 
         @pl.when(i == 0)
         def begin():
-            total_ref[...] = start_ref[...]
+            if not two:
+                total_ref[...] = start_ref[...]
             sums_ref[...] = jnp.zeros_like(sums_ref)
 
         @pl.when(flags_ref[0] == 1)
@@ -363,7 +371,8 @@
             ]
             + [
                 pltpu.VMEM((len(fetched), STEPS * step, cols), grads.dtype),
-                pltpu.SemaphoreType.DMA((len(fetched),)),
+                pltpu.VMEM((tok, STEPS * step), grads.dtype),
+                pltpu.SemaphoreType.DMA((len(fetched) + 2,)),
             ]
             * bool(fetched),
         ),

time: 151 us -> 151 us (level)
  no operation moved by 1% of the time
where the time goes in v21:
time: 151 us; the launch traced here: 150 us
  starting transfers between devices  51.2 us (34%)
  Pallas kernels  25.9 us (17%)
  waiting for transfers between devices  25.4 us (17%)
  local copies, waits for them, and re-layouts  22.3 us (15%)
  blocking collectives  11 us (7%)
  other arithmetic  10 us (7%)
  matrix products  3.81 us (3%)
    unnamed x66, local copies, waits for them, and re-layouts  17.3 us
    ppermute x2, starting transfers between devices, side(): return lax.ppermute(pick(at_end, at_middle), 'cand', SIDE)  15.4 us
    all_to_all x1, blocking collectives, final_sum(): return jnp.sum(lax.all_to_all(blocks, ALL, 0, 0, tiled=True), axis=0)  11 us
    ppermute x1, starting transfers between devices, line_plan(): s45 = lax.ppermute(to_s45, 'cand', SIDE)  8.88 us
    pallas_call x2, Pallas kernels, feature_dots(): pl.pallas_call(kernel, out_shape=out_shape, grid_spec=pltpu.PrefetchScala...  8.38 us
    pallas_call x2, Pallas kernels, partner_dots(): pl.pallas_call(kernel, out_shape=out_shape, grid_spec=pltpu.PrefetchScala...  7.14 us
    ppermute x1, starting transfers between devices, line_plan(): back = after(lax.ppermute(sums, 'cand', SIDE), rows_there)  6.79 us
    ppermute x1, waiting for transfers between devices, line_plan(): from_far = lax.ppermute(after(prods_c, to_two), ALL, far)  6.59 us
  transfers between devices with their start and end apart: 28, of which 10 were waited for; matrix products, arithmetic and copies ran while one was open for 11% of the time, Pallas kernels for 17%

profile of v21, /device:TPU:0, one launch (start us, length us, event | category | flops | bytes accessed | tf_op | source)
XLA Modules:
  0.0 150.1 jit_solution(7540559800229930027)
XLA Ops:
  0.0 3.0 %collective-permute-start = (bf16[1280,128]{1,0:T(8,128)(2,1)}, bf16[1280,128]{1,0:T(8,128)(2,1)}, u32[]{:S(2)}, u32[]{:S(2)}) collective-permute-start(bf16[1280,128]{1,0:T(8,128)(2,1)} %refs_0_.3), channel_id=1, source_target_pairs={{0,4},{4,0},{8,12},{12,8},{1,5},{5,1},{9,13},{13,9},{2,6},{6,2},{1... | collective-permute-start | bytes 983048 | tf_op jit(solution)/shard_map/ppermute | solution.py:494
  3.0 2.4 %constant_dynamic-slice_fusion = bf16[4608,128]{1,0:T(8,128)(2,1)} fusion(bf16[6912,128]{1,0:T(8,128)(2,1)} %refs_1_.1, s32[]{:T(128)S(6)} %select_n.162), kind=kLoop, calls=%fused_computation.79 | loop fusion | bytes 2359300 | tf_op jit(solution)/shard_map/dynamic_slice | solution.py:493
  5.4 3.1 %collective-permute-start.4 = (bf16[4608,128]{1,0:T(8,128)(2,1)}, bf16[4608,128]{1,0:T(8,128)(2,1)S(1)}, u32[]{:S(2)}, u32[]{:S(2)}) collective-permute-start(bf16[4608,128]{1,0:T(8,128)(2,1)} %constant_dynamic-slice_fusion), channel_id=1, source_target_pairs={{0,4},{4,0},{8,12},{12,8},{1,5},{5,1},{9,13},{13,9},{2,6},{6,2},{1... | collective-permute-start | bytes 3538952 | tf_op jit(solution)/shard_map/ppermute | solution.py:496
  9.9 3.5 %divide_convert_fusion = bf16[64,32,512]{2,1,0:T(8,128)(2,1)} fusion(bf16[64,32,512]{2,1,0:T(8,128)(2,1)} %param.13, f32[32,512]{1,0:T(8,128)S(1)} %broadcast_add_fusion), kind=kLoop, calls=%fused_computation | loop fusion | flops 3145728 | bytes 4259840 | tf_op jit(solution)/shard_map/convert_element_type | solution.py:504
  13.5 3.0 %copy-done = bf16[512,6912]{1,0:T(8,128)(2,1)S(1)} copy-done((bf16[512,6912]{1,0:T(8,128)(2,1)S(1)}, bf16[512,6912]{1,0:T(8,128)(2,1)}, u32[]{:S(2)}) %copy-start) | copy-done | bytes 7077912
  21.8 3.0 %copy-done.1 = bf16[512,6912]{1,0:T(8,128)(2,1)S(1)} copy-done((bf16[512,6912]{1,0:T(8,128)(2,1)S(1)}, bf16[512,6912]{1,0:T(8,128)(2,1)}, u32[]{:S(2)}) %copy-start.1) | copy-done | bytes 7077912
  24.8 4.6 %shard_map.82 = (f32[64,512]{1,0:T(8,128)S(1)}, f32[64,512]{1,0:T(8,128)S(1)}) custom-call(s32[6]{0:T(128)S(1)} %stack.36.flags_ref, bf16[512,6912]{1,0:T(8,128)(2,1)S(1)} %copy-done.1, bf16[6912,128]{1,0:T(8,128)(2,1)S(1)} %copy-done.2), custom_call_target="tpu_custom_call" | custom-call | flops 1 | bytes 1 | tf_op jit(solution)/shard_map/pallas_call | solution.py:161
  29.7 5.2 %collective-permute-start.3 = (bf16[2560,128]{1,0:T(8,128)(2,1)S(1)}, bf16[2560,128]{1,0:T(8,128)(2,1)S(1)}, u32[]{:S(2)}, u32[]{:S(2)}) collective-permute-start(bf16[2560,128]{1,0:T(8,128)(2,1)S(1)} %maximum_select_fusion.1), channel_id=1, source_target_pairs={{0,4},{4,0},{8,12},{12,8},{1,5},{5,1},{9,13},{13,9},{2,6},{6,2},{1... | collective-permute-start | bytes 1966088 | tf_op jit(solution)/shard_map/ppermute | solution.py:476
  39.9 8.9 %collective-permute-start.9 = (bf16[4608,128]{1,0:T(8,128)(2,1)S(1)}, bf16[4608,128]{1,0:T(8,128)(2,1)S(1)}, u32[]{:S(2)}, u32[]{:S(2)}) collective-permute-start(bf16[4608,128]{1,0:T(8,128)(2,1)S(1)} %maximum_select_fusion), channel_id=1, source_target_pairs={{0,4},{4,0},{8,12},{12,8},{1,5},{5,1},{9,13},{13,9},{2,6},{6,2},{1... | collective-permute-start | bytes 3538952 | tf_op jit(solution)/shard_map/ppermute | solution.py:511
  51.3 3.9 %shard_map.83 = (f32[256,512]{1,0:T(8,128)S(1)}, f32[256,512]{1,0:T(8,128)S(1)}) custom-call(s32[6]{0:T(128)S(1)} %stack.36.flags_ref, bf16[512,1280]{1,0:T(8,128)(2,1)S(1)} %copy-done.9, bf16[1280,128]{1,0:T(8,128)(2,1)S(1)} %copy-done.20, bf16[1280,128]{1,0:T(8,128)(2,1)} %collective-permute-done.refs_1_, ...), custom_call_target="tpu_custom_call" | custom-call | flops 1 | bytes 1 | tf_op jit(solution)/shard_map/pallas_call | solution.py:447
  57.4 10.2 %collective-permute-start.13 = (bf16[2304,128]{1,0:T(8,128)(2,1)}, bf16[2304,128]{1,0:T(8,128)(2,1)}, u32[]{:S(2)}, u32[]{:S(2)}) collective-permute-start(bf16[2304,128]{1,0:T(8,128)(2,1)} %broadcast_select_fusion), channel_id=1, source_target_pairs={{0,4},{4,0},{8,12},{12,8},{1,5},{5,1},{9,13},{13,9},{2,6},{6,2},{1... | collective-permute-start | bytes 1769480 | tf_op jit(solution)/shard_map/ppermute | solution.py:476
  67.6 3.8 %shard_map.84 = (f32[64,512]{1,0:T(8,128)S(1)}, f32[64,512]{1,0:T(8,128)S(1)}) custom-call(s32[6]{0:T(128)S(1)} %stack.36.flags_ref, bf16[512,6912]{1,0:T(8,128)(2,1)S(1)} %bitcast.48, bf16[4608,128]{1,0:T(8,128)(2,1)S(1)} %copy-done.4, bf16[2560,128]{1,0:T(8,128)(2,1)S(1)} %collective-permute-done.3.refs_2_.refs_4_.refs_1_), custom_call_target="tpu_custom_call" | custom-call | flops 1 | bytes 1 | tf_op jit(solution)/shard_map/pallas_call | solution.py:161
  72.2 4.1 %collective-permute-done.9.end_ref.refs_3_.refs_4_ = bf16[4608,128]{1,0:T(8,128)(2,1)S(1)} collective-permute-done((bf16[4608,128]{1,0:T(8,128)(2,1)S(1)}, bf16[4608,128]{1,0:T(8,128)(2,1)S(1)}, u32[]{:S(2)}, u32[]{:S(2)}) %collective-permute-start.9) | collective-permute-done | bytes 1179680 | tf_op jit(solution)/shard_map/ppermute | solution.py:511
  77.3 5.2 %shard_map.86 = (f32[512,256]{1,0:T(8,128)S(1)}, bf16[512,2304]{1,0:T(8,128)(2,1)S(1)}, bf16[512,2304]{1,0:T(8,128)(2,1)S(1)}) custom-call(s32[6]{0:T(128)S(1)} %stack.36.flags_ref, bf16[512,6912]{1,0:T(8,128)(2,1)S(1)} %bitcast.48, bf16[4608,128]{1,0:T(8,128)(2,1)S(1)} %collective-permute-done.9.end_ref.refs_3_.refs_4_, ...), custom_call_target="tpu_custom_call" | custom-call | flops 1 | bytes 1 | tf_op jit(solution)/shard_map/pallas_call | solution.py:233
  86.3 2.3 %collective-permute-start.20 = (bf16[2304,128]{1,0:T(8,128)(2,1)}, bf16[2304,128]{1,0:T(8,128)(2,1)S(1)}, u32[]{:S(2)}, u32[]{:S(2)}) collective-permute-start(bf16[2304,128]{1,0:T(8,128)(2,1)} %broadcast_select_fusion.1), channel_id=1, source_target_pairs={{0,4},{4,0},{8,12},{12,8},{1,5},{5,1},{9,13},{13,9},{2,6},{6,2},{1... | collective-permute-start | bytes 1769480 | tf_op jit(solution)/shard_map/ppermute | solution.py:516
  91.3 3.5 %shard_map.87 = (f32[64,1664]{1,0:T(8,128)S(1)}, f32[64,1664]{1,0:T(8,128)S(1)}, f32[512,128]{1,0:T(8,128)S(1)}) custom-call(s32[6]{0:T(128)S(1)} %stack.36.flags_ref, bf16[2304,128]{1,0:T(8,128)(2,1)S(1)} %collective-permute-done.6.refs_0_.refs_2_, bf16[2304,128]{1,0:T(8,128)(2,1)} %collective-permute-done.12.refs_1_.refs_3_, ...), custom_call_target="tpu_custom_call" | custom-call | flops 1 | bytes 1 | tf_op jit(solution)/shard_map/pallas_call | solution.py:358
  99.1 3.7 %collective-permute-done.20.refs_0_.refs_4_ = bf16[2304,128]{1,0:T(8,128)(2,1)S(1)} collective-permute-done((bf16[2304,128]{1,0:T(8,128)(2,1)}, bf16[2304,128]{1,0:T(8,128)(2,1)S(1)}, u32[]{:S(2)}, u32[]{:S(2)}) %collective-permute-start.20) | collective-permute-done | bytes 589856 | tf_op jit(solution)/shard_map/ppermute | solution.py:516
  102.8 3.6 %shard_map.88 = (f32[64,896]{1,0:T(8,128)S(1)}, f32[64,896]{1,0:T(8,128)S(1)}) custom-call(s32[6]{0:T(128)S(1)} %stack.36.flags_ref, bf16[2304,128]{1,0:T(8,128)(2,1)S(1)} %collective-permute-done.20.refs_0_.refs_4_, bf16[6912,128]{1,0:T(8,128)(2,1)S(1)} %copy-done.2, bf16[2304,128]{1,0:T(8,128)(2,1)S(1)} %collective-permute-done.6.refs_0_.refs_2_, ...), custom_call_target="tpu_custom_call" | custom-call | flops 1 | bytes 1 | tf_op jit(solution)/shard_map/pallas_call | solution.py:358
  106.6 6.8 %collective-permute-start.19 = (bf16[32,1152]{1,0:T(8,128)(2,1)S(1)}, bf16[32,1152]{1,0:T(8,128)(2,1)S(1)}, u32[]{:S(2)}, u32[]{:S(2)}) collective-permute-start(bf16[32,1152]{1,0:T(8,128)(2,1)S(1)} %slice.85), channel_id=1, source_target_pairs={{0,4},{4,0},{8,12},{12,8},{1,5},{5,1},{9,13},{13,9},{2,6},{6,2},{1... | collective-permute-start | bytes 221192 | tf_op jit(solution)/shard_map/ppermute | solution.py:597
  115.2 2.5 %collective-permute-done.22 = bf16[32,896]{1,0:T(8,128)(2,1)S(1)} collective-permute-done((bf16[32,896]{1,0:T(8,128)(2,1)S(1)}, bf16[32,896]{1,0:T(8,128)(2,1)S(1)}, u32[]{:S(2)}, u32[]{:S(2)}) %collective-permute-start.22) | collective-permute-done | bytes 57376 | tf_op jit(solution)/shard_map/ppermute | solution.py:37
  122.1 2.8 %collective-permute-start.25 = (bf16[4,32,512]{2,1,0:T(8,128)(2,1)S(1)}, bf16[4,32,512]{2,1,0:T(8,128)(2,1)S(1)}, u32[]{:S(2)}, u32[]{:S(2)}) collective-permute-start(bf16[4,32,512]{2,1,0:T(8,128)(2,1)S(1)} %fusion.2), channel_id=1, source_target_pairs={{0,8},{8,0},{4,12},{12,4},{1,9},{9,1},{5,13},{13,5},{2,10},{10,2},... | collective-permute-start | bytes 393224 | tf_op jit(solution)/shard_map/ppermute | solution.py:609
  126.7 6.6 %collective-permute-done.26 = bf16[4,32,512]{2,1,0:T(8,128)(2,1)S(1)} collective-permute-done((bf16[4,32,512]{2,1,0:T(8,128)(2,1)S(1)}, bf16[4,32,512]{2,1,0:T(8,128)(2,1)S(1)}, u32[]{:S(2)}, u32[]{:S(2)}) %collective-permute-start.26) | collective-permute-done | bytes 131104 | tf_op jit(solution)/shard_map/ppermute | solution.py:610
  135.5 2.8 %fusion.3 = f32[16,64]{1,0:T(8,128)S(1)} fusion(bf16[64,32,512]{2,1,0:T(8,128)(2,1)S(1)} %copy-done.24, bf16[16,32,512]{2,1,0:T(8,128)(2,1)S(1)} %pad_maximum_fusion.1), kind=kOutput, calls=%fused_computation.10 | convolution fusion | flops 33554432 | bytes 2625536 | tf_op jit(solution)/shard_map/tea,jea->tj/dot_general | solution.py:586
  138.5 11.0 %all_to_all.5 = f32[16,2,16]{2,1,0:T(2,128)S(1)} all-to-all(f32[16,2,16]{2,1,0:T(2,128)S(1)} %copy.49), channel_id=1, replica_groups=mesh['groups'=2,'cand'=4,'eig'=2,'rep'=2] {'cand','eig','rep'}, dimensions={0} | all-to-all | bytes 4096 | tf_op jit(solution)/shard_map/all_to_all | solution.py:625
  (163 shorter events, 39.8 us)
Async XLA Ops:
  0.0 20.9 %collective-permute-start = (bf16[1280,128]{1,0:T(8,128)(2,1)}, bf16[1280,128]{1,0:T(8,128)(2,1)}, u32[]{:S(2)}, u32[]{:S(2)}) collective-permute-start(bf16[1280,128]{1,0:T(8,128)(2,1)} %refs_0_.3), channel_id=1, source_target_pairs={{0,4},{4,0},{8,12},{12,8},{1,5},{5,1},{9,13},{13,9},{2,6},{6,2},{1... | collective-permute-start | bytes 983048 | tf_op jit(solution)/shard_map/ppermute | solution.py:494
  3.0 17.9 %collective-permute-start.1 = (bf16[1280,128]{1,0:T(8,128)(2,1)}, bf16[1280,128]{1,0:T(8,128)(2,1)S(1)}, u32[]{:S(2)}, u32[]{:S(2)}) collective-permute-start(bf16[1280,128]{1,0:T(8,128)(2,1)} %refs_0_.3), channel_id=1, source_target_pairs={{0,1},{1,0},{2,3},{3,2},{4,8},{5,9},{6,10},{7,11},{8,4},{9,5},{10,... | collective-permute-start | bytes 983048 | tf_op jit(solution)/shard_map/ppermute | solution.py:486
  5.4 31.6 %collective-permute-start.4 = (bf16[4608,128]{1,0:T(8,128)(2,1)}, bf16[4608,128]{1,0:T(8,128)(2,1)S(1)}, u32[]{:S(2)}, u32[]{:S(2)}) collective-permute-start(bf16[4608,128]{1,0:T(8,128)(2,1)} %constant_dynamic-slice_fusion), channel_id=1, source_target_pairs={{0,4},{4,0},{8,12},{12,8},{1,5},{5,1},{9,13},{13,9},{2,6},{6,2},{1... | collective-permute-start | bytes 3538952 | tf_op jit(solution)/shard_map/ppermute | solution.py:496
  9.9 28.2 %collective-permute-start.7 = (bf16[2304,128]{1,0:T(8,128)(2,1)}, bf16[2304,128]{1,0:T(8,128)(2,1)}, u32[]{:S(2)}, u32[]{:S(2)}) collective-permute-start(bf16[2304,128]{1,0:T(8,128)(2,1)} %get-tuple-element.92), channel_id=1, source_target_pairs={{0,1},{1,0},{2,3},{3,2},{4,8},{5,9},{6,10},{7,11},{8,4},{9,5},{10,... | collective-permute-start | bytes 1769480 | tf_op jit(solution)/shard_map/ppermute | solution.py:486
  20.9 8.6 %collective-permute-start.2 = (bf16[1280,128]{1,0:T(8,128)(2,1)}, bf16[1280,128]{1,0:T(8,128)(2,1)S(1)}, u32[]{:S(2)}, u32[]{:S(2)}) collective-permute-start(bf16[1280,128]{1,0:T(8,128)(2,1)} %collective-permute-done.refs_1_), channel_id=1, source_target_pairs={{0,1},{1,0},{2,3},{3,2},{4,8},{5,9},{6,10},{7,11},{8,4},{9,5},{10,... | collective-permute-start | bytes 983048 | tf_op jit(solution)/shard_map/ppermute | solution.py:486
  29.4 8.6 %collective-permute-start.8 = (bf16[2304,128]{1,0:T(8,128)(2,1)S(1)}, bf16[2304,128]{1,0:T(8,128)(2,1)S(1)}, u32[]{:S(2)}, u32[]{:S(2)}) collective-permute-start(bf16[2304,128]{1,0:T(8,128)(2,1)S(1)} %copy-done.23), channel_id=1, source_target_pairs={{0,1},{1,0},{2,3},{3,2},{4,8},{5,9},{6,10},{7,11},{8,4},{9,5},{10,... | collective-permute-start | bytes 1769480 | tf_op jit(solution)/shard_map/ppermute | solution.py:486
  29.7 21.4 %collective-permute-start.3 = (bf16[2560,128]{1,0:T(8,128)(2,1)S(1)}, bf16[2560,128]{1,0:T(8,128)(2,1)S(1)}, u32[]{:S(2)}, u32[]{:S(2)}) collective-permute-start(bf16[2560,128]{1,0:T(8,128)(2,1)S(1)} %maximum_select_fusion.1), channel_id=1, source_target_pairs={{0,4},{4,0},{8,12},{12,8},{1,5},{5,1},{9,13},{13,9},{2,6},{6,2},{1... | collective-permute-start | bytes 1966088 | tf_op jit(solution)/shard_map/ppermute | solution.py:476
  38.0 13.2 %collective-permute-start.5 = (bf16[2304,128]{1,0:T(8,128)(2,1)S(1)}, bf16[2304,128]{1,0:T(8,128)(2,1)S(1)}, u32[]{:S(2)}, u32[]{:S(2)}) collective-permute-start(bf16[2304,128]{1,0:T(8,128)(2,1)S(1)} %get-tuple-element.94), channel_id=1, source_target_pairs={{0,1},{1,0},{2,3},{3,2},{4,8},{5,9},{6,10},{7,11},{8,4},{9,5},{10,... | collective-permute-start | bytes 1769480 | tf_op jit(solution)/shard_map/ppermute | solution.py:486
  39.9 36.5 %collective-permute-start.9 = (bf16[4608,128]{1,0:T(8,128)(2,1)S(1)}, bf16[4608,128]{1,0:T(8,128)(2,1)S(1)}, u32[]{:S(2)}, u32[]{:S(2)}) collective-permute-start(bf16[4608,128]{1,0:T(8,128)(2,1)S(1)} %maximum_select_fusion), channel_id=1, source_target_pairs={{0,4},{4,0},{8,12},{12,8},{1,5},{5,1},{9,13},{13,9},{2,6},{6,2},{1... | collective-permute-start | bytes 3538952 | tf_op jit(solution)/shard_map/ppermute | solution.py:511
  51.2 21.1 %collective-permute-start.10 = (bf16[2304,128]{1,0:T(8,128)(2,1)S(1)}, bf16[2304,128]{1,0:T(8,128)(2,1)S(1)}, u32[]{:S(2)}, u32[]{:S(2)}) collective-permute-start(bf16[2304,128]{1,0:T(8,128)(2,1)S(1)} %slice.81), channel_id=1, source_target_pairs={{0,1},{1,0},{2,3},{3,2},{4,8},{5,9},{6,10},{7,11},{8,4},{9,5},{10,... | collective-permute-start | bytes 1769480 | tf_op jit(solution)/shard_map/ppermute | solution.py:486
  56.0 30.2 %collective-permute-start.6 = (bf16[2304,128]{1,0:T(8,128)(2,1)S(1)}, bf16[2304,128]{1,0:T(8,128)(2,1)S(1)}, u32[]{:S(2)}, u32[]{:S(2)}) collective-permute-start(bf16[2304,128]{1,0:T(8,128)(2,1)S(1)} %copy-done.26), channel_id=1, source_target_pairs={{0,1},{1,0},{2,3},{3,2},{4,8},{5,9},{6,10},{7,11},{8,4},{9,5},{10,... | collective-permute-start | bytes 1769480 | tf_op jit(solution)/shard_map/ppermute | solution.py:486
  57.4 31.3 %collective-permute-start.13 = (bf16[2304,128]{1,0:T(8,128)(2,1)}, bf16[2304,128]{1,0:T(8,128)(2,1)}, u32[]{:S(2)}, u32[]{:S(2)}) collective-permute-start(bf16[2304,128]{1,0:T(8,128)(2,1)} %broadcast_select_fusion), channel_id=1, source_target_pairs={{0,4},{4,0},{8,12},{12,8},{1,5},{5,1},{9,13},{13,9},{2,6},{6,2},{1... | collective-permute-start | bytes 1769480 | tf_op jit(solution)/shard_map/ppermute | solution.py:476
  72.2 16.4 %collective-permute-start.12 = (bf16[2304,128]{1,0:T(8,128)(2,1)}, bf16[2304,128]{1,0:T(8,128)(2,1)}, u32[]{:S(2)}, u32[]{:S(2)}) collective-permute-start(bf16[2304,128]{1,0:T(8,128)(2,1)} %get-tuple-element.65), channel_id=1, source_target_pairs={{0,1},{1,0},{2,3},{3,2},{4,8},{5,9},{6,10},{7,11},{8,4},{9,5},{10,... | collective-permute-start | bytes 1769480 | tf_op jit(solution)/shard_map/ppermute | solution.py:486
  86.3 16.5 %collective-permute-start.20 = (bf16[2304,128]{1,0:T(8,128)(2,1)}, bf16[2304,128]{1,0:T(8,128)(2,1)S(1)}, u32[]{:S(2)}, u32[]{:S(2)}) collective-permute-start(bf16[2304,128]{1,0:T(8,128)(2,1)} %broadcast_select_fusion.1), channel_id=1, source_target_pairs={{0,4},{4,0},{8,12},{12,8},{1,5},{5,1},{9,13},{13,9},{2,6},{6,2},{1... | collective-permute-start | bytes 1769480 | tf_op jit(solution)/shard_map/ppermute | solution.py:516
  96.8 9.7 %collective-permute-start.15 = (bf16[32,2688]{1,0:T(8,128)(2,1)S(1)}, bf16[32,2688]{1,0:T(8,128)(2,1)S(1)}, u32[]{:S(2)}, u32[]{:S(2)}) collective-permute-start(bf16[32,2688]{1,0:T(8,128)(2,1)S(1)} %add_convert_fusion.1), channel_id=1, source_target_pairs={{0,2},{2,0},{1,3},{3,1},{4,6},{6,4},{5,7},{7,5},{8,10},{10,8},{9,1... | collective-permute-start | bytes 516104 | tf_op jit(solution)/shard_map/ppermute | solution.py:37
  98.5 16.5 %collective-permute-start.17 = (bf16[256,512]{1,0:T(8,128)(2,1)S(1)}, bf16[256,512]{1,0:T(8,128)(2,1)S(1)}, u32[]{:S(2)}, u32[]{:S(2)}) collective-permute-start(bf16[256,512]{1,0:T(8,128)(2,1)S(1)} %get-tuple-element.88), channel_id=1, source_target_pairs={{0,2},{2,0},{1,3},{3,1},{4,6},{6,4},{5,7},{7,5},{8,10},{10,8},{9,1... | collective-permute-start | bytes 786440 | tf_op jit(solution)/shard_map/ppermute | solution.py:37
  106.5 7.0 %collective-permute-start.21 = (f32[64,896]{1,0:T(8,128)S(1)}, f32[64,896]{1,0:T(8,128)S(1)}, u32[]{:S(2)}, u32[]{:S(2)}) collective-permute-start(f32[64,896]{1,0:T(8,128)S(1)} %get-tuple-element.76), channel_id=1, source_target_pairs={{0,1},{1,0},{2,3},{3,2},{4,5},{5,4},{6,7},{7,6},{8,9},{9,8},{10,11... | collective-permute-start | bytes 688136 | tf_op jit(solution)/shard_map/ppermute | solution.py:37
  106.6 15.0 %collective-permute-start.19 = (bf16[32,1152]{1,0:T(8,128)(2,1)S(1)}, bf16[32,1152]{1,0:T(8,128)(2,1)S(1)}, u32[]{:S(2)}, u32[]{:S(2)}) collective-permute-start(bf16[32,1152]{1,0:T(8,128)(2,1)S(1)} %slice.85), channel_id=1, source_target_pairs={{0,4},{4,0},{8,12},{12,8},{1,5},{5,1},{9,13},{13,9},{2,6},{6,2},{1... | collective-permute-start | bytes 221192 | tf_op jit(solution)/shard_map/ppermute | solution.py:597
  113.5 4.2 %collective-permute-start.22 = (bf16[32,896]{1,0:T(8,128)(2,1)S(1)}, bf16[32,896]{1,0:T(8,128)(2,1)S(1)}, u32[]{:S(2)}, u32[]{:S(2)}) collective-permute-start(bf16[32,896]{1,0:T(8,128)(2,1)S(1)} %add_convert_fusion.2), channel_id=1, source_target_pairs={{0,2},{2,0},{1,3},{3,1},{4,6},{6,4},{5,7},{7,5},{8,10},{10,8},{9,1... | collective-permute-start | bytes 172040 | tf_op jit(solution)/shard_map/ppermute | solution.py:37
  115.1 4.3 %collective-permute-start.18 = (bf16[256,512]{1,0:T(8,128)(2,1)S(1)}, bf16[256,512]{1,0:T(8,128)(2,1)S(1)}, u32[]{:S(2)}, u32[]{:S(2)}) collective-permute-start(bf16[256,512]{1,0:T(8,128)(2,1)S(1)} %add_convert_fusion), channel_id=1, source_target_pairs={{0,1},{1,0},{2,3},{3,2},{4,5},{5,4},{6,7},{7,6},{8,9},{9,8},{10,11... | collective-permute-start | bytes 786440 | tf_op jit(solution)/shard_map/ppermute | solution.py:37
  119.8 13.5 %collective-permute-start.27 = (bf16[4,32,512]{2,1,0:T(8,128)(2,1)S(1)}, bf16[4,32,512]{2,1,0:T(8,128)(2,1)S(1)}, u32[]{:S(2)}, u32[]{:S(2)}) collective-permute-start(bf16[4,32,512]{2,1,0:T(8,128)(2,1)S(1)} %convolution_convert_fusion.3), channel_id=1, source_target_pairs={{0,1},{1,0},{2,3},{3,2},{4,8},{5,9},{6,10},{7,11},{8,4},{9,5},{10,... | collective-permute-start | bytes 393224 | tf_op jit(solution)/shard_map/ppermute | solution.py:486
  122.1 12.1 %collective-permute-start.25 = (bf16[4,32,512]{2,1,0:T(8,128)(2,1)S(1)}, bf16[4,32,512]{2,1,0:T(8,128)(2,1)S(1)}, u32[]{:S(2)}, u32[]{:S(2)}) collective-permute-start(bf16[4,32,512]{2,1,0:T(8,128)(2,1)S(1)} %fusion.2), channel_id=1, source_target_pairs={{0,8},{8,0},{4,12},{12,4},{1,9},{9,1},{5,13},{13,5},{2,10},{10,2},... | collective-permute-start | bytes 393224 | tf_op jit(solution)/shard_map/ppermute | solution.py:609
  125.0 8.3 %collective-permute-start.26 = (bf16[4,32,512]{2,1,0:T(8,128)(2,1)S(1)}, bf16[4,32,512]{2,1,0:T(8,128)(2,1)S(1)}, u32[]{:S(2)}, u32[]{:S(2)}) collective-permute-start(bf16[4,32,512]{2,1,0:T(8,128)(2,1)S(1)} %convolution_convert_fusion), channel_id=1, source_target_pairs={{0,12},{1,13},{2,14},{3,15},{4,5},{5,4},{6,7},{7,6},{8,9},{9,8},{1... | collective-permute-start | bytes 393224 | tf_op jit(solution)/shard_map/ppermute | solution.py:610
  126.4 9.0 %collective-permute-start.24 = (bf16[4,32,512]{2,1,0:T(8,128)(2,1)S(1)}, bf16[4,32,512]{2,1,0:T(8,128)(2,1)S(1)}, u32[]{:S(2)}, u32[]{:S(2)}) collective-permute-start(bf16[4,32,512]{2,1,0:T(8,128)(2,1)S(1)} %convolution_convert_fusion.2), channel_id=1, source_target_pairs={{0,4},{4,0},{8,12},{12,8},{1,5},{5,1},{9,13},{13,9},{2,6},{6,2},{1... | collective-permute-start | bytes 393224 | tf_op jit(solution)/shard_map/ppermute | solution.py:611
  (37 other events, 254.2 us)

commit v22 on v21

--- a/solution.py
+++ b/solution.py
@@ -13,6 +13,7 @@
 SHORT = pl.CostEstimate(flops=1, bytes_accessed=1, transcendentals=0)
 SIDE = ((0, 1), (1, 0), (2, 3), (3, 2))
 TWO = ((0, 2), (2, 0), (1, 3), (3, 1))
+THREE = ((0, 3), (3, 0), (1, 2), (2, 1))
 
 damping = 0.01
 
@@ -592,7 +593,6 @@
 
     prods_own = tile_prods(sum_own)
     prods_middle = tile_prods(sum_b)
-    from_middle = middle(prods_middle)
     last = after(lax.ppermute(after(sum_last, rows_here), "cand", SIDE), prods_middle)
     back = after(lax.ppermute(sums, "cand", SIDE), rows_there)
     few = tok_rows - TILE
@@ -607,13 +607,14 @@
     prods_c = tile_prods(with_partner(sum_c, 2))
     to_two = pick(prods_b, prods_c)
     from_two = lax.ppermute(to_two, "cand", TWO)
-    from_far = lax.ppermute(after(prods_c, to_two), ALL, far)
+    to_three = after(pick(prods_c, prods_middle), to_two)
+    from_three = lax.ppermute(to_three, "cand", THREE)
     from_side = lax.ppermute(after(prods_a, to_two), "cand", SIDE)
     total = pair_scores(
         (prods_own, plane),
         (from_side, plane ^ 1),
         (from_two, plane ^ 2),
-        (pick(from_far, from_middle), plane ^ 3),
+        (from_three, plane ^ 3),
     )
     return final_sum(total)
 

time: 151 us -> 150 us (level)
    select_n x5 -> x4, other arithmetic: 3.51 us -> 3.5 us  [pick(): return jnp.where(end, at_end, at_middle)]
  transfers between devices with their start and end apart: 28 -> 27, of which waited for: 10 -> 10; matrix products, arithmetic and copies ran while one was open for 11% -> 10% of each run, Pallas kernels for 17% -> 17%
where the time goes in v22:
time: 150 us
  starting transfers between devices  51.1 us (34%)
  Pallas kernels  25.9 us (17%)
  waiting for transfers between devices  24.7 us (16%)
  local copies, waits for them, and re-layouts  22.3 us (15%)
  blocking collectives  11.5 us (8%)
  other arithmetic  10 us (7%)
  matrix products  3.81 us (3%)
    unnamed x66, local copies, waits for them, and re-layouts  17.3 us
    ppermute x2, starting transfers between devices, side(): return lax.ppermute(pick(at_end, at_middle), 'cand', SIDE)  15.4 us
    all_to_all x1, blocking collectives, final_sum(): return jnp.sum(lax.all_to_all(blocks, ALL, 0, 0, tiled=True), axis=0)  11.5 us
    ppermute x1, starting transfers between devices, line_plan(): s45 = lax.ppermute(to_s45, 'cand', SIDE)  8.88 us
    pallas_call x2, Pallas kernels, feature_dots(): pl.pallas_call(kernel, out_shape=out_shape, grid_spec=pltpu.PrefetchScala...  8.38 us
    pallas_call x2, Pallas kernels, partner_dots(): pl.pallas_call(kernel, out_shape=out_shape, grid_spec=pltpu.PrefetchScala...  7.14 us
    ppermute x1, starting transfers between devices, line_plan(): back = after(lax.ppermute(sums, 'cand', SIDE), rows_there)  6.79 us
    ppermute x1, waiting for transfers between devices, line_plan(): from_three = lax.ppermute(to_three, 'cand', THREE)  6.53 us
  transfers between devices with their start and end apart: 27, of which 10 were waited for; matrix products, arithmetic and copies ran while one was open for 10% of the time, Pallas kernels for 17%

profile of v22, /device:TPU:0, one launch (start us, length us, event | category | flops | bytes accessed | tf_op | source)
XLA Modules:
  0.0 149.7 jit_solution(10255500107864473012)
XLA Ops:
  0.0 3.0 %collective-permute-start = (bf16[1280,128]{1,0:T(8,128)(2,1)}, bf16[1280,128]{1,0:T(8,128)(2,1)}, u32[]{:S(2)}, u32[]{:S(2)}) collective-permute-start(bf16[1280,128]{1,0:T(8,128)(2,1)} %refs_0_.3), channel_id=1, source_target_pairs={{0,4},{4,0},{8,12},{12,8},{1,5},{5,1},{9,13},{13,9},{2,6},{6,2},{1... | collective-permute-start | bytes 983048 | tf_op jit(solution)/shard_map/ppermute | solution.py:495
  3.0 2.4 %constant_dynamic-slice_fusion = bf16[4608,128]{1,0:T(8,128)(2,1)} fusion(bf16[6912,128]{1,0:T(8,128)(2,1)} %refs_1_.1, s32[]{:T(128)S(6)} %select_n.162), kind=kLoop, calls=%fused_computation.79 | loop fusion | bytes 2359300 | tf_op jit(solution)/shard_map/dynamic_slice | solution.py:494
  5.4 3.1 %collective-permute-start.4 = (bf16[4608,128]{1,0:T(8,128)(2,1)}, bf16[4608,128]{1,0:T(8,128)(2,1)S(1)}, u32[]{:S(2)}, u32[]{:S(2)}) collective-permute-start(bf16[4608,128]{1,0:T(8,128)(2,1)} %constant_dynamic-slice_fusion), channel_id=1, source_target_pairs={{0,4},{4,0},{8,12},{12,8},{1,5},{5,1},{9,13},{13,9},{2,6},{6,2},{1... | collective-permute-start | bytes 3538952 | tf_op jit(solution)/shard_map/ppermute | solution.py:497
  9.9 3.5 %divide_convert_fusion = bf16[64,32,512]{2,1,0:T(8,128)(2,1)} fusion(bf16[64,32,512]{2,1,0:T(8,128)(2,1)} %param.13, f32[32,512]{1,0:T(8,128)S(1)} %broadcast_add_fusion), kind=kLoop, calls=%fused_computation | loop fusion | flops 3145728 | bytes 4259840 | tf_op jit(solution)/shard_map/convert_element_type | solution.py:505
  13.5 3.0 %copy-done = bf16[512,6912]{1,0:T(8,128)(2,1)S(1)} copy-done((bf16[512,6912]{1,0:T(8,128)(2,1)S(1)}, bf16[512,6912]{1,0:T(8,128)(2,1)}, u32[]{:S(2)}) %copy-start) | copy-done | bytes 7077912
  21.8 3.0 %copy-done.1 = bf16[512,6912]{1,0:T(8,128)(2,1)S(1)} copy-done((bf16[512,6912]{1,0:T(8,128)(2,1)S(1)}, bf16[512,6912]{1,0:T(8,128)(2,1)}, u32[]{:S(2)}) %copy-start.1) | copy-done | bytes 7077912
  24.8 4.6 %shard_map.82 = (f32[64,512]{1,0:T(8,128)S(1)}, f32[64,512]{1,0:T(8,128)S(1)}) custom-call(s32[6]{0:T(128)S(1)} %stack.36.flags_ref, bf16[512,6912]{1,0:T(8,128)(2,1)S(1)} %copy-done.1, bf16[6912,128]{1,0:T(8,128)(2,1)S(1)} %copy-done.2), custom_call_target="tpu_custom_call" | custom-call | flops 1 | bytes 1 | tf_op jit(solution)/shard_map/pallas_call | solution.py:162
  29.7 5.2 %collective-permute-start.3 = (bf16[2560,128]{1,0:T(8,128)(2,1)S(1)}, bf16[2560,128]{1,0:T(8,128)(2,1)S(1)}, u32[]{:S(2)}, u32[]{:S(2)}) collective-permute-start(bf16[2560,128]{1,0:T(8,128)(2,1)S(1)} %maximum_select_fusion.1), channel_id=1, source_target_pairs={{0,4},{4,0},{8,12},{12,8},{1,5},{5,1},{9,13},{13,9},{2,6},{6,2},{1... | collective-permute-start | bytes 1966088 | tf_op jit(solution)/shard_map/ppermute | solution.py:477
  39.9 8.9 %collective-permute-start.9 = (bf16[4608,128]{1,0:T(8,128)(2,1)S(1)}, bf16[4608,128]{1,0:T(8,128)(2,1)S(1)}, u32[]{:S(2)}, u32[]{:S(2)}) collective-permute-start(bf16[4608,128]{1,0:T(8,128)(2,1)S(1)} %maximum_select_fusion), channel_id=1, source_target_pairs={{0,4},{4,0},{8,12},{12,8},{1,5},{5,1},{9,13},{13,9},{2,6},{6,2},{1... | collective-permute-start | bytes 3538952 | tf_op jit(solution)/shard_map/ppermute | solution.py:512
  51.3 3.9 %shard_map.83 = (f32[256,512]{1,0:T(8,128)S(1)}, f32[256,512]{1,0:T(8,128)S(1)}) custom-call(s32[6]{0:T(128)S(1)} %stack.36.flags_ref, bf16[512,1280]{1,0:T(8,128)(2,1)S(1)} %copy-done.9, bf16[1280,128]{1,0:T(8,128)(2,1)S(1)} %copy-done.20, bf16[1280,128]{1,0:T(8,128)(2,1)} %collective-permute-done.refs_1_, ...), custom_call_target="tpu_custom_call" | custom-call | flops 1 | bytes 1 | tf_op jit(solution)/shard_map/pallas_call | solution.py:448
  57.4 10.2 %collective-permute-start.13 = (bf16[2304,128]{1,0:T(8,128)(2,1)}, bf16[2304,128]{1,0:T(8,128)(2,1)}, u32[]{:S(2)}, u32[]{:S(2)}) collective-permute-start(bf16[2304,128]{1,0:T(8,128)(2,1)} %broadcast_select_fusion), channel_id=1, source_target_pairs={{0,4},{4,0},{8,12},{12,8},{1,5},{5,1},{9,13},{13,9},{2,6},{6,2},{1... | collective-permute-start | bytes 1769480 | tf_op jit(solution)/shard_map/ppermute | solution.py:477
  67.6 3.8 %shard_map.84 = (f32[64,512]{1,0:T(8,128)S(1)}, f32[64,512]{1,0:T(8,128)S(1)}) custom-call(s32[6]{0:T(128)S(1)} %stack.36.flags_ref, bf16[512,6912]{1,0:T(8,128)(2,1)S(1)} %bitcast.50, bf16[4608,128]{1,0:T(8,128)(2,1)S(1)} %copy-done.4, bf16[2560,128]{1,0:T(8,128)(2,1)S(1)} %collective-permute-done.3.refs_2_.refs_4_.refs_1_), custom_call_target="tpu_custom_call" | custom-call | flops 1 | bytes 1 | tf_op jit(solution)/shard_map/pallas_call | solution.py:162
  72.2 4.1 %collective-permute-done.9.end_ref.refs_3_.refs_4_ = bf16[4608,128]{1,0:T(8,128)(2,1)S(1)} collective-permute-done((bf16[4608,128]{1,0:T(8,128)(2,1)S(1)}, bf16[4608,128]{1,0:T(8,128)(2,1)S(1)}, u32[]{:S(2)}, u32[]{:S(2)}) %collective-permute-start.9) | collective-permute-done | bytes 1179680 | tf_op jit(solution)/shard_map/ppermute | solution.py:512
  77.3 5.2 %shard_map.86 = (f32[512,256]{1,0:T(8,128)S(1)}, bf16[512,2304]{1,0:T(8,128)(2,1)S(1)}, bf16[512,2304]{1,0:T(8,128)(2,1)S(1)}) custom-call(s32[6]{0:T(128)S(1)} %stack.36.flags_ref, bf16[512,6912]{1,0:T(8,128)(2,1)S(1)} %bitcast.50, bf16[4608,128]{1,0:T(8,128)(2,1)S(1)} %collective-permute-done.9.end_ref.refs_3_.refs_4_, ...), custom_call_target="tpu_custom_call" | custom-call | flops 1 | bytes 1 | tf_op jit(solution)/shard_map/pallas_call | solution.py:234
  86.3 2.3 %collective-permute-start.20 = (bf16[2304,128]{1,0:T(8,128)(2,1)}, bf16[2304,128]{1,0:T(8,128)(2,1)S(1)}, u32[]{:S(2)}, u32[]{:S(2)}) collective-permute-start(bf16[2304,128]{1,0:T(8,128)(2,1)} %broadcast_select_fusion.1), channel_id=1, source_target_pairs={{0,4},{4,0},{8,12},{12,8},{1,5},{5,1},{9,13},{13,9},{2,6},{6,2},{1... | collective-permute-start | bytes 1769480 | tf_op jit(solution)/shard_map/ppermute | solution.py:517
  91.3 3.5 %shard_map.87 = (f32[64,1664]{1,0:T(8,128)S(1)}, f32[64,1664]{1,0:T(8,128)S(1)}, f32[512,128]{1,0:T(8,128)S(1)}) custom-call(s32[6]{0:T(128)S(1)} %stack.36.flags_ref, bf16[2304,128]{1,0:T(8,128)(2,1)S(1)} %collective-permute-done.6.refs_0_.refs_2_, bf16[2304,128]{1,0:T(8,128)(2,1)} %collective-permute-done.12.refs_1_.refs_3_, ...), custom_call_target="tpu_custom_call" | custom-call | flops 1 | bytes 1 | tf_op jit(solution)/shard_map/pallas_call | solution.py:359
  99.1 3.7 %collective-permute-done.20.refs_0_.refs_4_ = bf16[2304,128]{1,0:T(8,128)(2,1)S(1)} collective-permute-done((bf16[2304,128]{1,0:T(8,128)(2,1)}, bf16[2304,128]{1,0:T(8,128)(2,1)S(1)}, u32[]{:S(2)}, u32[]{:S(2)}) %collective-permute-start.20) | collective-permute-done | bytes 589856 | tf_op jit(solution)/shard_map/ppermute | solution.py:517
  102.8 3.6 %shard_map.88 = (f32[64,896]{1,0:T(8,128)S(1)}, f32[64,896]{1,0:T(8,128)S(1)}) custom-call(s32[6]{0:T(128)S(1)} %stack.36.flags_ref, bf16[2304,128]{1,0:T(8,128)(2,1)S(1)} %collective-permute-done.20.refs_0_.refs_4_, bf16[6912,128]{1,0:T(8,128)(2,1)S(1)} %copy-done.2, bf16[2304,128]{1,0:T(8,128)(2,1)S(1)} %collective-permute-done.6.refs_0_.refs_2_, ...), custom_call_target="tpu_custom_call" | custom-call | flops 1 | bytes 1 | tf_op jit(solution)/shard_map/pallas_call | solution.py:359
  106.6 6.8 %collective-permute-start.19 = (bf16[32,1152]{1,0:T(8,128)(2,1)S(1)}, bf16[32,1152]{1,0:T(8,128)(2,1)S(1)}, u32[]{:S(2)}, u32[]{:S(2)}) collective-permute-start(bf16[32,1152]{1,0:T(8,128)(2,1)S(1)} %slice.85), channel_id=1, source_target_pairs={{0,4},{4,0},{8,12},{12,8},{1,5},{5,1},{9,13},{13,9},{2,6},{6,2},{1... | collective-permute-start | bytes 221192 | tf_op jit(solution)/shard_map/ppermute | solution.py:597
  115.2 2.5 %collective-permute-done.22 = bf16[32,896]{1,0:T(8,128)(2,1)S(1)} collective-permute-done((bf16[32,896]{1,0:T(8,128)(2,1)S(1)}, bf16[32,896]{1,0:T(8,128)(2,1)S(1)}, u32[]{:S(2)}, u32[]{:S(2)}) %collective-permute-start.22) | collective-permute-done | bytes 57376 | tf_op jit(solution)/shard_map/ppermute | solution.py:38
  122.2 2.8 %collective-permute-start.25 = (bf16[4,32,512]{2,1,0:T(8,128)(2,1)S(1)}, bf16[4,32,512]{2,1,0:T(8,128)(2,1)S(1)}, u32[]{:S(2)}, u32[]{:S(2)}) collective-permute-start(bf16[4,32,512]{2,1,0:T(8,128)(2,1)S(1)} %fusion.2), channel_id=1, source_target_pairs={{0,8},{8,0},{4,12},{12,4},{1,9},{9,1},{5,13},{13,5},{2,10},{10,2},... | collective-permute-start | bytes 393224 | tf_op jit(solution)/shard_map/ppermute | solution.py:609
  126.7 6.5 %collective-permute-done.26 = bf16[4,32,512]{2,1,0:T(8,128)(2,1)S(1)} collective-permute-done((bf16[4,32,512]{2,1,0:T(8,128)(2,1)S(1)}, bf16[4,32,512]{2,1,0:T(8,128)(2,1)S(1)}, u32[]{:S(2)}, u32[]{:S(2)}) %collective-permute-start.26) | collective-permute-done | bytes 131104 | tf_op jit(solution)/shard_map/ppermute | solution.py:611
  134.7 2.8 %fusion.3 = f32[16,64]{1,0:T(8,128)S(1)} fusion(bf16[64,32,512]{2,1,0:T(8,128)(2,1)S(1)} %copy-done.24, bf16[16,32,512]{2,1,0:T(8,128)(2,1)S(1)} %pad_maximum_fusion.1), kind=kOutput, calls=%fused_computation.10 | convolution fusion | flops 33554432 | bytes 2625536 | tf_op jit(solution)/shard_map/tea,jea->tj/dot_general | solution.py:587
  137.7 11.5 %all_to_all.5 = f32[16,2,16]{2,1,0:T(2,128)S(1)} all-to-all(f32[16,2,16]{2,1,0:T(2,128)S(1)} %copy.49), channel_id=1, replica_groups=mesh['groups'=2,'cand'=4,'eig'=2,'rep'=2] {'cand','eig','rep'}, dimensions={0} | all-to-all | bytes 4096 | tf_op jit(solution)/shard_map/all_to_all | solution.py:626
  (160 shorter events, 39.0 us)
Async XLA Ops:
  0.0 20.9 %collective-permute-start = (bf16[1280,128]{1,0:T(8,128)(2,1)}, bf16[1280,128]{1,0:T(8,128)(2,1)}, u32[]{:S(2)}, u32[]{:S(2)}) collective-permute-start(bf16[1280,128]{1,0:T(8,128)(2,1)} %refs_0_.3), channel_id=1, source_target_pairs={{0,4},{4,0},{8,12},{12,8},{1,5},{5,1},{9,13},{13,9},{2,6},{6,2},{1... | collective-permute-start | bytes 983048 | tf_op jit(solution)/shard_map/ppermute | solution.py:495
  3.0 17.9 %collective-permute-start.1 = (bf16[1280,128]{1,0:T(8,128)(2,1)}, bf16[1280,128]{1,0:T(8,128)(2,1)S(1)}, u32[]{:S(2)}, u32[]{:S(2)}) collective-permute-start(bf16[1280,128]{1,0:T(8,128)(2,1)} %refs_0_.3), channel_id=1, source_target_pairs={{0,1},{1,0},{2,3},{3,2},{4,8},{5,9},{6,10},{7,11},{8,4},{9,5},{10,... | collective-permute-start | bytes 983048 | tf_op jit(solution)/shard_map/ppermute | solution.py:487
  5.4 31.6 %collective-permute-start.4 = (bf16[4608,128]{1,0:T(8,128)(2,1)}, bf16[4608,128]{1,0:T(8,128)(2,1)S(1)}, u32[]{:S(2)}, u32[]{:S(2)}) collective-permute-start(bf16[4608,128]{1,0:T(8,128)(2,1)} %constant_dynamic-slice_fusion), channel_id=1, source_target_pairs={{0,4},{4,0},{8,12},{12,8},{1,5},{5,1},{9,13},{13,9},{2,6},{6,2},{1... | collective-permute-start | bytes 3538952 | tf_op jit(solution)/shard_map/ppermute | solution.py:497
  9.9 28.2 %collective-permute-start.7 = (bf16[2304,128]{1,0:T(8,128)(2,1)}, bf16[2304,128]{1,0:T(8,128)(2,1)}, u32[]{:S(2)}, u32[]{:S(2)}) collective-permute-start(bf16[2304,128]{1,0:T(8,128)(2,1)} %get-tuple-element.92), channel_id=1, source_target_pairs={{0,1},{1,0},{2,3},{3,2},{4,8},{5,9},{6,10},{7,11},{8,4},{9,5},{10,... | collective-permute-start | bytes 1769480 | tf_op jit(solution)/shard_map/ppermute | solution.py:487
  20.9 8.6 %collective-permute-start.2 = (bf16[1280,128]{1,0:T(8,128)(2,1)}, bf16[1280,128]{1,0:T(8,128)(2,1)S(1)}, u32[]{:S(2)}, u32[]{:S(2)}) collective-permute-start(bf16[1280,128]{1,0:T(8,128)(2,1)} %collective-permute-done.refs_1_), channel_id=1, source_target_pairs={{0,1},{1,0},{2,3},{3,2},{4,8},{5,9},{6,10},{7,11},{8,4},{9,5},{10,... | collective-permute-start | bytes 983048 | tf_op jit(solution)/shard_map/ppermute | solution.py:487
  29.4 8.6 %collective-permute-start.8 = (bf16[2304,128]{1,0:T(8,128)(2,1)S(1)}, bf16[2304,128]{1,0:T(8,128)(2,1)S(1)}, u32[]{:S(2)}, u32[]{:S(2)}) collective-permute-start(bf16[2304,128]{1,0:T(8,128)(2,1)S(1)} %copy-done.23), channel_id=1, source_target_pairs={{0,1},{1,0},{2,3},{3,2},{4,8},{5,9},{6,10},{7,11},{8,4},{9,5},{10,... | collective-permute-start | bytes 1769480 | tf_op jit(solution)/shard_map/ppermute | solution.py:487
  29.7 21.4 %collective-permute-start.3 = (bf16[2560,128]{1,0:T(8,128)(2,1)S(1)}, bf16[2560,128]{1,0:T(8,128)(2,1)S(1)}, u32[]{:S(2)}, u32[]{:S(2)}) collective-permute-start(bf16[2560,128]{1,0:T(8,128)(2,1)S(1)} %maximum_select_fusion.1), channel_id=1, source_target_pairs={{0,4},{4,0},{8,12},{12,8},{1,5},{5,1},{9,13},{13,9},{2,6},{6,2},{1... | collective-permute-start | bytes 1966088 | tf_op jit(solution)/shard_map/ppermute | solution.py:477
  38.0 13.2 %collective-permute-start.5 = (bf16[2304,128]{1,0:T(8,128)(2,1)S(1)}, bf16[2304,128]{1,0:T(8,128)(2,1)S(1)}, u32[]{:S(2)}, u32[]{:S(2)}) collective-permute-start(bf16[2304,128]{1,0:T(8,128)(2,1)S(1)} %get-tuple-element.94), channel_id=1, source_target_pairs={{0,1},{1,0},{2,3},{3,2},{4,8},{5,9},{6,10},{7,11},{8,4},{9,5},{10,... | collective-permute-start | bytes 1769480 | tf_op jit(solution)/shard_map/ppermute | solution.py:487
  39.9 36.5 %collective-permute-start.9 = (bf16[4608,128]{1,0:T(8,128)(2,1)S(1)}, bf16[4608,128]{1,0:T(8,128)(2,1)S(1)}, u32[]{:S(2)}, u32[]{:S(2)}) collective-permute-start(bf16[4608,128]{1,0:T(8,128)(2,1)S(1)} %maximum_select_fusion), channel_id=1, source_target_pairs={{0,4},{4,0},{8,12},{12,8},{1,5},{5,1},{9,13},{13,9},{2,6},{6,2},{1... | collective-permute-start | bytes 3538952 | tf_op jit(solution)/shard_map/ppermute | solution.py:512
  51.2 21.1 %collective-permute-start.10 = (bf16[2304,128]{1,0:T(8,128)(2,1)S(1)}, bf16[2304,128]{1,0:T(8,128)(2,1)S(1)}, u32[]{:S(2)}, u32[]{:S(2)}) collective-permute-start(bf16[2304,128]{1,0:T(8,128)(2,1)S(1)} %slice.81), channel_id=1, source_target_pairs={{0,1},{1,0},{2,3},{3,2},{4,8},{5,9},{6,10},{7,11},{8,4},{9,5},{10,... | collective-permute-start | bytes 1769480 | tf_op jit(solution)/shard_map/ppermute | solution.py:487
  56.0 30.2 %collective-permute-start.6 = (bf16[2304,128]{1,0:T(8,128)(2,1)S(1)}, bf16[2304,128]{1,0:T(8,128)(2,1)S(1)}, u32[]{:S(2)}, u32[]{:S(2)}) collective-permute-start(bf16[2304,128]{1,0:T(8,128)(2,1)S(1)} %copy-done.26), channel_id=1, source_target_pairs={{0,1},{1,0},{2,3},{3,2},{4,8},{5,9},{6,10},{7,11},{8,4},{9,5},{10,... | collective-permute-start | bytes 1769480 | tf_op jit(solution)/shard_map/ppermute | solution.py:487
  57.4 31.3 %collective-permute-start.13 = (bf16[2304,128]{1,0:T(8,128)(2,1)}, bf16[2304,128]{1,0:T(8,128)(2,1)}, u32[]{:S(2)}, u32[]{:S(2)}) collective-permute-start(bf16[2304,128]{1,0:T(8,128)(2,1)} %broadcast_select_fusion), channel_id=1, source_target_pairs={{0,4},{4,0},{8,12},{12,8},{1,5},{5,1},{9,13},{13,9},{2,6},{6,2},{1... | collective-permute-start | bytes 1769480 | tf_op jit(solution)/shard_map/ppermute | solution.py:477
  72.2 16.4 %collective-permute-start.12 = (bf16[2304,128]{1,0:T(8,128)(2,1)}, bf16[2304,128]{1,0:T(8,128)(2,1)}, u32[]{:S(2)}, u32[]{:S(2)}) collective-permute-start(bf16[2304,128]{1,0:T(8,128)(2,1)} %get-tuple-element.65), channel_id=1, source_target_pairs={{0,1},{1,0},{2,3},{3,2},{4,8},{5,9},{6,10},{7,11},{8,4},{9,5},{10,... | collective-permute-start | bytes 1769480 | tf_op jit(solution)/shard_map/ppermute | solution.py:487
  86.3 16.5 %collective-permute-start.20 = (bf16[2304,128]{1,0:T(8,128)(2,1)}, bf16[2304,128]{1,0:T(8,128)(2,1)S(1)}, u32[]{:S(2)}, u32[]{:S(2)}) collective-permute-start(bf16[2304,128]{1,0:T(8,128)(2,1)} %broadcast_select_fusion.1), channel_id=1, source_target_pairs={{0,4},{4,0},{8,12},{12,8},{1,5},{5,1},{9,13},{13,9},{2,6},{6,2},{1... | collective-permute-start | bytes 1769480 | tf_op jit(solution)/shard_map/ppermute | solution.py:517
  96.8 9.7 %collective-permute-start.15 = (bf16[32,2688]{1,0:T(8,128)(2,1)S(1)}, bf16[32,2688]{1,0:T(8,128)(2,1)S(1)}, u32[]{:S(2)}, u32[]{:S(2)}) collective-permute-start(bf16[32,2688]{1,0:T(8,128)(2,1)S(1)} %add_convert_fusion.1), channel_id=1, source_target_pairs={{0,2},{2,0},{1,3},{3,1},{4,6},{6,4},{5,7},{7,5},{8,10},{10,8},{9,1... | collective-permute-start | bytes 516104 | tf_op jit(solution)/shard_map/ppermute | solution.py:38
  98.5 16.5 %collective-permute-start.17 = (bf16[256,512]{1,0:T(8,128)(2,1)S(1)}, bf16[256,512]{1,0:T(8,128)(2,1)S(1)}, u32[]{:S(2)}, u32[]{:S(2)}) collective-permute-start(bf16[256,512]{1,0:T(8,128)(2,1)S(1)} %get-tuple-element.88), channel_id=1, source_target_pairs={{0,2},{2,0},{1,3},{3,1},{4,6},{6,4},{5,7},{7,5},{8,10},{10,8},{9,1... | collective-permute-start | bytes 786440 | tf_op jit(solution)/shard_map/ppermute | solution.py:38
  106.5 7.0 %collective-permute-start.21 = (f32[64,896]{1,0:T(8,128)S(1)}, f32[64,896]{1,0:T(8,128)S(1)}, u32[]{:S(2)}, u32[]{:S(2)}) collective-permute-start(f32[64,896]{1,0:T(8,128)S(1)} %get-tuple-element.76), channel_id=1, source_target_pairs={{0,1},{1,0},{2,3},{3,2},{4,5},{5,4},{6,7},{7,6},{8,9},{9,8},{10,11... | collective-permute-start | bytes 688136 | tf_op jit(solution)/shard_map/ppermute | solution.py:38
  106.6 15.0 %collective-permute-start.19 = (bf16[32,1152]{1,0:T(8,128)(2,1)S(1)}, bf16[32,1152]{1,0:T(8,128)(2,1)S(1)}, u32[]{:S(2)}, u32[]{:S(2)}) collective-permute-start(bf16[32,1152]{1,0:T(8,128)(2,1)S(1)} %slice.85), channel_id=1, source_target_pairs={{0,4},{4,0},{8,12},{12,8},{1,5},{5,1},{9,13},{13,9},{2,6},{6,2},{1... | collective-permute-start | bytes 221192 | tf_op jit(solution)/shard_map/ppermute | solution.py:597
  113.5 4.2 %collective-permute-start.22 = (bf16[32,896]{1,0:T(8,128)(2,1)S(1)}, bf16[32,896]{1,0:T(8,128)(2,1)S(1)}, u32[]{:S(2)}, u32[]{:S(2)}) collective-permute-start(bf16[32,896]{1,0:T(8,128)(2,1)S(1)} %add_convert_fusion.2), channel_id=1, source_target_pairs={{0,2},{2,0},{1,3},{3,1},{4,6},{6,4},{5,7},{7,5},{8,10},{10,8},{9,1... | collective-permute-start | bytes 172040 | tf_op jit(solution)/shard_map/ppermute | solution.py:38
  115.1 4.3 %collective-permute-start.18 = (bf16[256,512]{1,0:T(8,128)(2,1)S(1)}, bf16[256,512]{1,0:T(8,128)(2,1)S(1)}, u32[]{:S(2)}, u32[]{:S(2)}) collective-permute-start(bf16[256,512]{1,0:T(8,128)(2,1)S(1)} %add_convert_fusion), channel_id=1, source_target_pairs={{0,1},{1,0},{2,3},{3,2},{4,5},{5,4},{6,7},{7,6},{8,9},{9,8},{10,11... | collective-permute-start | bytes 786440 | tf_op jit(solution)/shard_map/ppermute | solution.py:38
  117.8 3.9 %collective-permute-start.23 = (bf16[32,384]{1,0:T(8,128)(2,1)S(1)}, bf16[32,384]{1,0:T(8,128)(2,1)S(1)}, u32[]{:S(2)}, u32[]{:S(2)}) collective-permute-start(bf16[32,384]{1,0:T(8,128)(2,1)S(1)} %slice.117), channel_id=1, source_target_pairs={{0,4},{4,0},{8,12},{12,8},{1,5},{5,1},{9,13},{13,9},{2,6},{6,2},{1... | collective-permute-start | bytes 73736 | tf_op jit(solution)/shard_map/ppermute | solution.py:596
  122.2 12.1 %collective-permute-start.25 = (bf16[4,32,512]{2,1,0:T(8,128)(2,1)S(1)}, bf16[4,32,512]{2,1,0:T(8,128)(2,1)S(1)}, u32[]{:S(2)}, u32[]{:S(2)}) collective-permute-start(bf16[4,32,512]{2,1,0:T(8,128)(2,1)S(1)} %fusion.2), channel_id=1, source_target_pairs={{0,8},{8,0},{4,12},{12,4},{1,9},{9,1},{5,13},{13,5},{2,10},{10,2},... | collective-permute-start | bytes 393224 | tf_op jit(solution)/shard_map/ppermute | solution.py:609
  125.0 8.2 %collective-permute-start.26 = (bf16[4,32,512]{2,1,0:T(8,128)(2,1)S(1)}, bf16[4,32,512]{2,1,0:T(8,128)(2,1)S(1)}, u32[]{:S(2)}, u32[]{:S(2)}) collective-permute-start(bf16[4,32,512]{2,1,0:T(8,128)(2,1)S(1)} %get-tuple-element.80), channel_id=1, source_target_pairs={{0,12},{12,0},{4,8},{8,4},{1,13},{13,1},{5,9},{9,5},{2,14},{14,2},... | collective-permute-start | bytes 393224 | tf_op jit(solution)/shard_map/ppermute | solution.py:611
  126.4 8.2 %collective-permute-start.24 = (bf16[4,32,512]{2,1,0:T(8,128)(2,1)S(1)}, bf16[4,32,512]{2,1,0:T(8,128)(2,1)S(1)}, u32[]{:S(2)}, u32[]{:S(2)}) collective-permute-start(bf16[4,32,512]{2,1,0:T(8,128)(2,1)S(1)} %convolution_convert_fusion.2), channel_id=1, source_target_pairs={{0,4},{4,0},{8,12},{12,8},{1,5},{5,1},{9,13},{13,9},{2,6},{6,2},{1... | collective-permute-start | bytes 393224 | tf_op jit(solution)/shard_map/ppermute | solution.py:612
  (36 other events, 249.4 us)
